TPU v7x, 32 devices: a whole 2x2x4 slice. The times are simulated.
32 devices in a mesh: dp: 4 (over x, core), vocab: 8 (over z, y).
Axes of the slice: x: 2, y: 2, z: 4, core: 2. Of those that a mesh axis runs over, the one named last changes fastest.
Arguments:
- hidden: bfloat16 [512, 8192], P('dp', 'vocab'), may hold values from -500 to 500, as said below
- norm_gain: float32 [8192], replicated, may hold values from 0.5 to 1.5
- head_weight: bfloat16 [16384, 8192], P('vocab', 'dp'), may hold values from -1 to 1
- target_logits: bfloat16 [512, 16384], P('dp', 'vocab'), may hold values from -20 to 400
- valid_rows: int32 [512], P('dp'), may hold values from 0 to 1, as said below
- parents: int32 [512], P('dp'), may hold values from 0 to 62, as said below
- features: bfloat16 [512, 24576], P('dp', 'vocab'), may hold values from -0.29882812 to 0.29882812
Outputs:
- grad_hidden: bfloat16 [512, 8192], P('vocab', 'dp')
- grad_joining: float32 [8192, 24576], P('dp', 'vocab')
Inputs may be any that keep to these rules, and one draw needn't show every extreme that they name: hidden is finite; in some draws a few rows are far from the others. `valid_rows`: row 0 is always valid. `parents`: rows form trees of 64 rows aligned on multiples of 64; a tree's first row has parent 0, every other row a parent before it in its tree, and the last row of each tree has parent 64 - 2.
All inputs are finite; a program needn't handle non-finite values.
Results may differ from a plain program's by a relative error of at most 0.007.
Values may be sent and summed in bfloat16 or wider, within the bound.
No kernel may reach another device: no remote copies, remote signals or barrier semaphores. Data moves between devices by JAX's collectives and lax.ppermute only.
A program may use at most 128 MiB of HBM per device.

v0:
```python
import jax
import jax.numpy as jnp
from jax import lax
from jax.sharding import PartitionSpec as P

TREE = 64


def row_logits(normed_rows, head_weight):
    return lax.dot_general(
        normed_rows, head_weight, (((1,), (1,)), ((), ())), preferred_element_type=jnp.float32
    )


def body(hidden, norm_gain, head_weight, target_logits, valid_rows, parents, features):
    group_index = lax.axis_index("dp")
    vocab_index = lax.axis_index("vocab")
    group_rows = hidden.shape[0]
    whole_rows = lax.all_gather(hidden, "vocab", axis=1, tiled=True)
    model_width = whole_rows.shape[1]
    slice_rows = lax.all_to_all(whole_rows, "dp", split_axis=1, concat_axis=0, tiled=True)
    all_rows = slice_rows.shape[0]
    slice_width = slice_rows.shape[1]
    share_rows = all_rows // lax.axis_size("vocab")
    gain_slice = lax.dynamic_slice_in_dim(norm_gain, group_index * slice_width, slice_width)
    live_rows = (valid_rows == 1).astype(jnp.float32)
    square_part = jnp.sum(jnp.square(slice_rows.astype(jnp.float32)), axis=1)
    squares, valid_count = lax.psum((square_part, jnp.sum(live_rows)), "dp")
    row_factor = lax.rsqrt(squares / model_width + 1e-05)
    normed = (slice_rows.astype(jnp.float32) * row_factor[:, None] * gain_slice).astype(
        jnp.bfloat16
    )
    logits = lax.psum_scatter(
        row_logits(normed, head_weight), "dp", scatter_dimension=0, tiled=True
    )
    targets = target_logits.astype(jnp.float32)
    draft_max, target_max = lax.pmax((jnp.max(logits, axis=1), jnp.max(targets, axis=1)), "vocab")
    draft_total, target_total = lax.psum(
        (
            jnp.sum(jnp.exp(logits - draft_max[:, None]), axis=1),
            jnp.sum(jnp.exp(targets - target_max[:, None]), axis=1),
        ),
        "vocab",
    )
    row_weight = 1048576.0 * live_rows / valid_count
    draft_probs = jnp.exp(logits - draft_max[:, None]) / draft_total[:, None]
    target_probs = jnp.exp(targets - target_max[:, None]) / target_total[:, None]
    logit_grad = (row_weight[:, None] * (draft_probs - target_probs)).astype(jnp.bfloat16)
    partial_grad = jnp.dot(
        lax.all_gather(logit_grad, "dp", axis=0, tiled=True),
        head_weight,
        preferred_element_type=jnp.float32,
    )
    normed_grad = lax.psum(partial_grad, "vocab")
    values = slice_rows.astype(jnp.float32)
    row_dot = lax.psum(jnp.sum(gain_slice * values * normed_grad, axis=1), "dp")
    grad_all = (
        row_factor[:, None] * gain_slice * normed_grad
        - values * (row_factor**3 * row_dot / model_width)[:, None]
    ).astype(jnp.bfloat16)
    grad_share = lax.dynamic_slice_in_dim(grad_all, vocab_index * share_rows, share_rows, 0)
    tree_rows = jnp.arange(group_rows, dtype=jnp.int32) // TREE * TREE + parents
    chosen = jnp.take(features, tree_rows, axis=0)
    grad_joining = lax.dot_general(
        grad_all,
        lax.all_gather(chosen, "dp", axis=0, tiled=True),
        (((0,), (0,)), ((), ())),
        preferred_element_type=jnp.float32,
    )
    return (grad_share, grad_joining)


def solution(mesh):
    placed = (
        P("dp", "vocab"),
        P(),
        P("vocab", "dp"),
        P("dp", "vocab"),
        P("dp"),
        P("dp"),
        P("dp", "vocab"),
    )
    return jax.shard_map(
        body,
        mesh=mesh,
        in_specs=placed,
        out_specs=(P("vocab", "dp"), P("dp", "vocab")),
        check_vma=False,
    )
```

profile of v0, /device:TPU:0, one launch (start us, length us, event | category | flops | bytes accessed | tf_op | source)
XLA Modules:
  0.0 436.3 jit_solution(529619254047976136)
XLA Ops:
  7.2 0.0 copy-start
  7.2 0.0 all-gather.4.cloned.1.call-start
  7.2 0.7 all-gather.4.cloned.1.call-update
  7.9 54.3 %all-gather.4.cloned.1.call-done = bf16[128,8192]{1,0:T(8,128)(2,1)} async-done(((bf16[128,1024]{1,0:T(8,128)(2,1)}), bf16[128,8192]{1,0:T(8,128)(2,1)}) %all-gather.4.cloned.1.call-update) | async-done | bytes 2097168 | tf_op jit(solution)/shard_map/all_gather | solution.py:19
  62.2 0.0 copy-start.3
  62.2 3.2 copy.13
  65.4 3.6 all-to-all-start
  69.0 0.0 reduce-scatter.2.cloned.1.call-start
  69.0 0.7 dynamic_slice.6
  69.7 0.0 copy-done.3
  69.7 0.6 fusion.14
  70.3 24.3 %all-to-all-done = bf16[128,4,2048]{2,0,1:T(8,128)(2,1)S(1)} async-done(((bf16[128,4,2048]{2,0,1:T(8,128)(2,1)}), bf16[128,4,2048]{2,0,1:T(8,128)(2,1)S(1)}, u32[]{:S(2)}, u32[]{:S(2)}) %all-to-all-start) | async-done | bytes 2097184 | tf_op jit(solution)/shard_map/all_to_all | solution.py:21
  94.7 0.5 fusion
  95.1 6.4 %all-reduce.2 = (f32[512]{0:T(512)S(1)}, f32[]{:T(128)}) all-reduce(f32[512]{0:T(512)S(1)} %bitcast.33, f32[]{:T(128)} %fusion.14), channel_id=1, replica_groups=mesh['dp'=4,'vocab'=8] {'dp'}, use_global_device_ids=true, to_apply=%region_1.0 | all-reduce | flops 513 | bytes 4104 | tf_op jit(solution)/shard_map/psum | solution.py:28
  101.5 0.5 fusion.2
  102.1 9.5 %fusion.15 = f32[512,2048]{1,0:T(8,128)} fusion(bf16[512,2048]{1,0:T(8,128)(2,1)S(1)} %fusion.2, bf16[2048,2048]{1,0:T(8,128)(2,1)} %param.9), kind=kOutput, calls=%fused_computation.37 | convolution fusion | flops 4294967296 | bytes 14680064 | tf_op jit(solution)/shard_map/dot_general | solution.py:10
  111.6 0.0 copy-start.1
  111.6 0.0 reduce-scatter.2.cloned.1.call-update
  111.6 0.0 all-gather.6.cloned.1.call-start
  111.6 1.0 copy-done.1
  112.6 0.2 reduce_max.24
  112.8 0.6 fusion.13
  113.4 41.0 %reduce-scatter.2.cloned.1.call-done = f32[128,2048]{1,0:T(8,128)} async-done(((f32[512,2048]{1,0:T(8,128)}), f32[128,2048]{1,0:T(8,128)}) %reduce-scatter.2.cloned.1.call-update) | async-done | bytes 1048592 | tf_op jit(solution)/shard_map/reduce_scatter | solution.py:33
  154.4 1.4 reduce_max.23
  155.8 21.6 %all-reduce.1 = (f32[128]{0:T(128)S(1)}, f32[128]{0:T(128)S(1)}) all-reduce(bf16[128]{0:T(256)(128)(2,1)S(1)} %reduce_max.24, f32[128]{0:T(128)S(1)} %reduce_max.23), channel_id=1, replica_groups=mesh['dp'=4,'vocab'=8] {'vocab'}, use_global_device_ids=true, to_apply=%region_10.0 | all-reduce | flops 256 | bytes 1792 | tf_op jit(solution)/shard_map/pmax | solution.py:37
  177.4 1.7 fusion.7
  179.0 17.1 %all-reduce = (f32[128]{0:T(128)S(1)}, f32[128]{0:T(128)S(1)}) all-reduce(f32[128]{0:T(128)S(1)} %get-tuple-element.10, f32[128]{0:T(128)S(1)} %get-tuple-element.11), channel_id=1, replica_groups=mesh['dp'=4,'vocab'=8] {'vocab'}, use_global_device_ids=true, to_apply=%region_12.0 | all-reduce | flops 256 | bytes 2048 | tf_op jit(solution)/shard_map/psum | solution.py:38
  196.2 2.5 multiply_convert_fusion
  198.7 0.0 all-gather.6.cloned.1.call-update
  198.7 0.0 all-reduce.5.cloned.1.call-start
  198.8 20.5 %all-gather.6.cloned.1.call-done = bf16[512,2048]{1,0:T(8,128)(2,1)} async-done(((bf16[128,2048]{1,0:T(8,128)(2,1)}), bf16[512,2048]{1,0:T(8,128)(2,1)}) %all-gather.6.cloned.1.call-update) | async-done | bytes 2097168 | tf_op jit(solution)/shard_map/all_gather | solution.py:50
  219.2 10.5 %fusion.16 = f32[512,2048]{1,0:T(8,128)} fusion(bf16[512,2048]{1,0:T(8,128)(2,1)} %all-gather.6.cloned.1.call-done, bf16[2048,2048]{1,0:T(8,128)(2,1)} %param.9), kind=kOutput, calls=%fused_computation.38 | convolution fusion | flops 4294967296 | bytes 14680064 | tf_op jit(solution)/shard_map/dot_general | solution.py:49
  229.8 0.0 all-reduce.5.cloned.1.call-update
  229.8 0.0 all-gather.8.cloned.1.call-start
  229.8 0.6 copy-done.4
  230.4 0.0 copy-done
  230.4 1.9 gather_fusion
  232.4 2.1 broadcast_select_fusion
  234.5 0.0 all-gather.8.cloned.1.call-update
  234.5 151.7 %all-reduce.5.cloned.1.call-done = f32[512,2048]{1,0:T(8,128)} async-done(((f32[512,2048]{1,0:T(8,128)}), f32[512,2048]{1,0:T(8,128)}) %all-reduce.5.cloned.1.call-update) | async-done | bytes 4194320 | tf_op jit(solution)/shard_map/psum | solution.py:54
  386.3 2.8 fusion.4
  389.1 7.0 %psum.47 = f32[512]{0:T(512)S(1)} all-reduce(f32[512]{0:T(512)S(1)} %fusion.4), channel_id=1, replica_groups=mesh['dp'=4,'vocab'=8] {'dp'}, use_global_device_ids=true, to_apply=%region_15.0 | all-reduce | flops 512 | bytes 4096 | tf_op jit(solution)/shard_map/psum | solution.py:56
  396.1 3.0 fusion.6
  399.2 0.0 copy-start.2
  399.2 1.3 copy-done.2
  400.5 0.7 constant_dynamic-slice_fusion
  401.2 14.1 %all-gather.8.cloned.1.call-done = bf16[512,3072]{1,0:T(8,128)(2,1)} async-done(((bf16[128,3072]{1,0:T(8,128)(2,1)}), bf16[512,3072]{1,0:T(8,128)(2,1)}) %all-gather.8.cloned.1.call-update) | async-done | bytes 3145744 | tf_op jit(solution)/shard_map/all_gather | solution.py:66
  415.3 14.5 %fusion.17 = f32[2048,3072]{1,0:T(8,128)} fusion(bf16[512,2048]{1,0:T(8,128)(2,1)} %copy-done.2, bf16[512,3072]{1,0:T(8,128)(2,1)} %all-gather.8.cloned.1.call-done), kind=kOutput, calls=%fused_computation.39 | convolution fusion | flops 6442450944 | bytes 30408704 | tf_op jit(solution)/shard_map/dot_general | solution.py:64
  (5 shorter events, 0.0 us)
Async XLA Ops:
  7.2 223.3 %copy-start = (bf16[128,3072]{1,0:T(8,128)(2,1)S(1)}, bf16[128,3072]{1,0:T(8,128)(2,1)}, u32[]{:S(2)}) copy-start(bf16[128,3072]{1,0:T(8,128)(2,1)} %param.13) | copy-start | bytes 2359300
  7.2 55.0 %all-gather.4.cloned.1.call-start = ((), (), s32[]{:S(2)}) async-start(), calls=%async_computation.2 | async-start | bytes 2359296 | tf_op jit(solution)/shard_map/all_gather | solution.py:19
  62.2 7.6 %copy-start.3 = (s32[128]{0:T(128)S(1)}, s32[128]{0:T(128)}, u32[]{:S(2)}) copy-start(s32[128]{0:T(128)} %param.11) | copy-start | bytes 1540
  65.4 29.3 %all-to-all-start = ((bf16[128,4,2048]{2,0,1:T(8,128)(2,1)}), bf16[128,4,2048]{2,0,1:T(8,128)(2,1)S(1)}, u32[]{:S(2)}, u32[]{:S(2)}) async-start(bf16[128,4,2048]{2,0,1:T(8,128)(2,1)} %bitcast.31), calls=%async_computation | async-start | bytes 4194304 | tf_op jit(solution)/shard_map/all_to_all | solution.py:21
  69.0 85.4 %reduce-scatter.2.cloned.1.call-start = ((), (), s32[]{:S(2)}) async-start(), calls=%async_computation.3 | async-start | bytes 5242880 | tf_op jit(solution)/shard_map/reduce_scatter | solution.py:33
  111.6 1.0 copy-start.1
  111.6 107.7 %all-gather.6.cloned.1.call-start = ((), (), s32[]{:S(2)}) async-start(), calls=%async_computation.4 | async-start | bytes 2621440 | tf_op jit(solution)/shard_map/all_gather | solution.py:50
  198.7 187.6 %all-reduce.5.cloned.1.call-start = ((), (), s32[]{:S(2)}) async-start(), calls=%async_computation.5 | async-start | bytes 8388608 | tf_op jit(solution)/shard_map/psum | solution.py:54
  229.8 0.7 copy-start.4
  229.8 185.6 %all-gather.8.cloned.1.call-start = ((), (), s32[]{:S(2)}) async-start(), calls=%async_computation.6 | async-start | bytes 3932160 | tf_op jit(solution)/shard_map/all_gather | solution.py:66
  399.2 1.4 copy-start.2
Sparse Core Ops, SparseCore 0:
  10.2 51.9 all-gather.3
  111.7 42.6 reduce-scatter.1
  198.8 20.3 all-gather.5
  229.9 156.3 all-reduce.4
  387.8 27.5 all-gather.7
where the time goes:
time: 437 us; the launch traced here: 436 us
  waiting for transfers between devices  307 us (70%)
  blocking collectives  52.1 us (12%)
  matrix products  34.4 us (8%)
  other arithmetic  16 us (4%)
  between operations  13.9 us (3%)
  local copies, waits for them, and re-layouts  9.41 us (2%)
    psum x1, waiting for transfers between devices, body(): normed_grad = lax.psum(partial_grad, 'vocab')  152 us
    all_gather x1, waiting for transfers between devices, body(): whole_rows = lax.all_gather(hidden, 'vocab', axis=1, tiled=True)  54.3 us
    reduce_scatter x1, waiting for transfers between devices, body(): lax.psum_scatter(row_logits(normed, head_weight), 'dp', scatter_dimension...  41 us
    all_to_all x1, waiting for transfers between devices, body(): lax.all_to_all(whole_rows, 'dp', split_axis=1, concat_axis=0, tiled=True)  24.3 us
    pmax x1, blocking collectives, body(): lax.pmax((jnp.max(logits, axis=1), jnp.max(targets, axis=1)), 'vocab')  21.6 us
    all_gather x1, waiting for transfers between devices, body(): lax.all_gather(logit_grad, 'dp', axis=0, tiled=True)  20.5 us
    psum x1, blocking collectives, body(): lax.psum((jnp.sum(jnp.exp(logits - draft_max[:, None]), axis=1), jnp.sum(...  17.1 us
    dot_general x1, matrix products, body(): lax.dot_general(grad_all, lax.all_gather(chosen, 'dp', axis=0, tiled=True...  14.5 us
  transfers between devices with their start and end apart: 6, of which 6 were waited for; matrix products, arithmetic and copies ran while one was open for 3% of the time, Pallas kernels for 0%

commit v1 on v0

v1 whole, which is shorter than its diff:
```python
import jax
import jax.numpy as jnp
from jax import lax
from jax.sharding import PartitionSpec as P

TREE = 64
CORES = 2
F32 = jnp.float32
BF16 = jnp.bfloat16


def ring_order(rows, columns):
    if columns == 1 or rows == 1:
        return list(range(rows * columns))
    order = [r * columns for r in range(rows)]
    for step in range(rows):
        r = rows - 1 - step
        line = [r * columns + c for c in range(1, columns)]
        order += line if step % 2 == 0 else line[::-1]
    return order


class Ring:
    def __init__(self, size, columns):
        self.size = size
        self.order = ring_order(size // columns, columns)
        place = [0] * size
        for position, index in enumerate(self.order):
            place[index] = position
        self.place = place
        self.position = jnp.asarray(place, jnp.int32)[lax.axis_index("vocab")]

    def shift(self, x, step):
        size, order = self.size, self.order
        return lax.ppermute(
            x, "vocab", [(order[p], order[(p + step) % size]) for p in range(size)]
        )

    def gather(self, block):
        size = self.size
        half = size // 2
        ahead, behind = [block], [block]
        for _ in range((size - 1) // 2):
            ahead.append(self.shift(ahead[-1], 1))
            behind.append(self.shift(behind[-1], -1))
        far = []
        if size % 2 == 0:
            cut = block.shape[0] // 2
            far = [
                jnp.concatenate(
                    [self.shift(ahead[-1][:cut], 1), self.shift(behind[-1][cut:], -1)], axis=0
                )
            ]
        near = ahead[1:][::-1] + [block] + behind[1:]
        line = jnp.stack(far + near)
        start = half if size % 2 == 0 else (size - 1) // 2
        return jnp.roll(line, self.position - start, axis=0)

    def scatter_sum(self, part):
        size = self.size
        steps = (size - 1) // 2
        if size % 2 == 0:
            far = part(size // 2)
            cut = far.shape[0] // 2
            got = self.shift(far[:cut].astype(BF16), 1).astype(F32)
            ahead = part(steps)
            ahead = jnp.concatenate([ahead[:cut] + got, ahead[cut:]], axis=0)
            got = self.shift(far[cut:].astype(BF16), -1).astype(F32)
            behind = part(-steps)
            behind = jnp.concatenate([behind[:cut], behind[cut:] + got], axis=0)
        else:
            ahead, behind = part(steps), part(-steps)
        for step in range(steps - 1, -1, -1):
            got_ahead = self.shift(ahead.astype(BF16), 1).astype(F32)
            got_behind = self.shift(behind.astype(BF16), -1).astype(F32)
            if step > 0:
                ahead = part(step) + got_ahead
                behind = part(-step) + got_behind
            else:
                return part(0) + got_ahead + got_behind


def swap_core(x, size):
    return lax.ppermute(x, "dp", [(i, i ^ 1) for i in range(size)])


def shift_chip(x, size, step):
    return lax.ppermute(x, "dp", [(i, (i + CORES * step) % size) for i in range(size)])


def gather_groups(block, size):
    chips = size // CORES
    mine = [block] + [shift_chip(block, size, -d) for d in range(1, chips)]
    mine = jnp.stack(mine)
    return jnp.stack([mine, swap_core(mine, size)], axis=1)


def body(hidden, norm_gain, head_weight, target_logits, valid_rows, parents, features):
    groups = lax.axis_size("dp")
    parts = lax.axis_size("vocab")
    chips = groups // CORES
    group_index = lax.axis_index("dp")
    vocab_index = lax.axis_index("vocab")
    chip, core = group_index // CORES, group_index % CORES
    group_rows, block_width = hidden.shape
    all_rows = groups * group_rows
    model_width = block_width * parts
    slice_blocks = parts // groups
    slice_width = block_width * slice_blocks
    share_rows = all_rows // parts
    ring = Ring(parts, chips)

    tree_rows = jnp.arange(group_rows, dtype=jnp.int32) // TREE * TREE + parents
    chosen = jnp.take(features, tree_rows, axis=0)
    chosen_all = gather_groups(chosen, groups).reshape(all_rows, -1)

    live_rows = (valid_rows == 1).astype(F32)
    square_part = jnp.sum(jnp.square(hidden.astype(F32)), axis=1)
    small = lax.all_gather(jnp.stack([square_part, live_rows]), ("dp", "vocab"))
    small = small.reshape(groups, parts, 2, group_rows)
    squares = jnp.sum(small[:, :, 0], axis=1)
    valid_count = jnp.sum(small[:, 0, 1])
    row_factor = lax.rsqrt(squares / model_width + 1e-05).reshape(all_rows)

    turned = lax.ppermute(
        hidden,
        ("dp", "vocab"),
        [
            (g * parts + v, (v // slice_blocks) * parts + g * slice_blocks + v % slice_blocks)
            for g in range(groups)
            for v in range(parts)
        ],
    )
    by_position = ring.gather(turned)
    by_index = by_position[jnp.asarray(ring.place)]
    slice_rows = (
        by_index.reshape(groups, slice_blocks, group_rows, block_width)
        .transpose(0, 2, 1, 3)
        .reshape(all_rows, slice_width)
    )
    gain_slice = lax.dynamic_slice_in_dim(norm_gain, group_index * slice_width, slice_width)
    normed = (slice_rows.astype(F32) * row_factor[:, None] * gain_slice).astype(BF16)

    partial = lax.dot_general(
        normed, head_weight, (((1,), (1,)), ((), ())), preferred_element_type=F32
    )
    partial = partial.reshape(chips, CORES, group_rows, -1)
    sent = lax.dynamic_index_in_dim(partial, 1 - core, 1, keepdims=False)
    partial = lax.dynamic_index_in_dim(partial, core, 1, keepdims=False) + swap_core(sent, groups)
    logits = lax.dynamic_index_in_dim(partial, chip, 0, keepdims=False)
    for d in range(1, chips):
        out = lax.dynamic_index_in_dim(partial, (chip + d) % chips, 0, keepdims=False)
        logits = logits + shift_chip(out, groups, d)

    def part_stats(x):
        top = jnp.max(x, axis=1)
        return top, jnp.sum(jnp.exp(x - top[:, None]), axis=1)

    def scale_of(top, total):
        mine = jnp.stack([top, total])
        others = [mine] + [ring.shift(mine, d) for d in range(1, parts)]
        pairs = jnp.stack(others)
        whole_top = jnp.max(pairs[:, 0], axis=0)
        whole = jnp.sum(pairs[:, 1] * jnp.exp(pairs[:, 0] - whole_top), axis=0)
        return jnp.exp(top - whole_top) / whole

    targets = target_logits.astype(F32)
    target_top, target_total = part_stats(targets)
    target_scale = scale_of(target_top, target_total)
    draft_top, draft_total = part_stats(logits)
    draft_scale = scale_of(draft_top, draft_total)
    row_weight = 1048576.0 * live_rows / valid_count
    draft_probs = jnp.exp(logits - draft_top[:, None]) * draft_scale[:, None]
    target_probs = jnp.exp(targets - target_top[:, None]) * target_scale[:, None]
    logit_grad = (row_weight[:, None] * (draft_probs - target_probs)).astype(BF16)

    dot_part = jnp.sum(logit_grad.astype(F32) * logits, axis=1)
    dots = lax.all_gather(dot_part, ("dp", "vocab")).reshape(groups, parts, group_rows)
    row_dot = jnp.sum(dots, axis=1).reshape(all_rows) / row_factor

    grads = gather_groups(logit_grad, groups).reshape(all_rows, -1)
    normed_grad = jnp.dot(grads, head_weight, preferred_element_type=F32)

    def share_start(position):
        return position % parts * share_rows

    def share(t):
        return lax.dynamic_slice_in_dim(
            normed_grad, share_start(ring.position + t), share_rows, 0
        )

    def whole_row(start):
        entry = start // group_rows
        group = (chip + entry // CORES) % chips * CORES + (core ^ (entry % CORES))
        return group * group_rows + start % group_rows

    normed_share = ring.scatter_sum(share)
    first = whole_row(share_start(ring.position))
    values = lax.dynamic_slice_in_dim(slice_rows, first, share_rows, 0).astype(F32)
    factor = lax.dynamic_slice_in_dim(row_factor, first, share_rows, 0)
    dot = lax.dynamic_slice_in_dim(row_dot, first, share_rows, 0)
    grad_part = (
        factor[:, None] * gain_slice * normed_share
        - values * (factor**3 * dot / model_width)[:, None]
    ).astype(BF16)
    grad_all = ring.gather(grad_part).reshape(all_rows, slice_width)

    row_start = vocab_index * share_rows
    row_group = row_start // group_rows
    entry = (row_group // CORES - chip) % chips * CORES + (row_group % CORES ^ core)
    grad_share = lax.dynamic_slice_in_dim(
        grad_all, entry * group_rows + row_start % group_rows, share_rows, 0
    )
    grad_joining = lax.dot_general(
        grad_all, chosen_all, (((0,), (0,)), ((), ())), preferred_element_type=F32
    )
    return (grad_share, grad_joining)


def solution(mesh):
    placed = (
        P("dp", "vocab"),
        P(),
        P("vocab", "dp"),
        P("dp", "vocab"),
        P("dp"),
        P("dp"),
        P("dp", "vocab"),
    )
    return jax.shard_map(
        body,
        mesh=mesh,
        in_specs=placed,
        out_specs=(P("vocab", "dp"), P("dp", "vocab")),
        check_vma=False,
    )
```

time: 437 us -> 369 us (0.84)
  waiting for transfers between devices: 307 us -> 74.5 us
  blocking collectives: 52.1 us -> 133 us
  starting transfers between devices: 3.81 us -> 73.3 us
  other arithmetic: 16 us -> 31.8 us
  local copies, waits for them, and re-layouts: 9.41 us -> 19.2 us
  matrix products: 34.4 us -> 27.5 us
  between operations: 13.9 us -> 8.74 us
    psum x1 -> x0, waiting for transfers between devices: 152 us -> none  [body(): normed_grad = lax.psum(partial_grad, 'vocab')]
    all_gather x0 -> x2, blocking collectives: none -> 133 us  [the longest x1 67.4 us: body(): lax.all_gather(dot_part, ('dp', 'vocab')).reshape(groups, parts, group_rows)]
    all_gather x3 -> x0, waiting for transfers between devices: 88.9 us -> none  [the longest x1 54.3 us: body(): whole_rows = lax.all_gather(hidden, 'vocab', axis=1, tiled=True)]
    ppermute x0 -> x45, waiting for transfers between devices: none -> 74.5 us  [the longest x38 42.8 us: shift(): lax.ppermute(x, 'vocab', [(order[p], order[(p + step) % size]) for p in r...]
    ppermute x0 -> x45, starting transfers between devices: none -> 73.3 us  [the longest x38 64.4 us: shift(): lax.ppermute(x, 'vocab', [(order[p], order[(p + step) % size]) for p in r...]
    reduce_scatter x1 -> x0, waiting for transfers between devices: 41 us -> none  [body(): lax.psum_scatter(row_logits(normed, head_weight), 'dp', scatter_dimension...]
    psum x3 -> x0, blocking collectives: 30.5 us -> none  [the longest x1 17.1 us: body(): lax.psum((jnp.sum(jnp.exp(logits - draft_max[:, None]), axis=1), jnp.sum(...]
    all_to_all x1 -> x0, waiting for transfers between devices: 24.3 us -> none  [body(): lax.all_to_all(whole_rows, 'dp', split_axis=1, concat_axis=0, tiled=True)]
  transfers between devices with their start and end apart: 6 -> 45, of which waited for: 6 -> 21; matrix products, arithmetic and copies ran while one was open for 3% -> 6% of each run, Pallas kernels for 0% -> 0%
where the time goes in v1:
time: 369 us; the launch traced here: 368 us
  blocking collectives  133 us (36%)
  waiting for transfers between devices  74.5 us (20%)
  starting transfers between devices  73.3 us (20%)
  other arithmetic  31.8 us (9%)
  matrix products  27.5 us (7%)
  local copies, waits for them, and re-layouts  19.2 us (5%)
  between operations  8.74 us (2%)
    all_gather x1, blocking collectives, body(): lax.all_gather(dot_part, ('dp', 'vocab')).reshape(groups, parts, group_rows)  67.4 us
    all_gather x1, blocking collectives, body(): small = lax.all_gather(jnp.stack([square_part, live_rows]), ('dp', 'vocab'))  65.2 us
    ppermute x38, starting transfers between devices, shift(): lax.ppermute(x, 'vocab', [(order[p], order[(p + step) % size]) for p in r...  64.4 us
    ppermute x38, waiting for transfers between devices, shift(): lax.ppermute(x, 'vocab', [(order[p], order[(p + step) % size]) for p in r...  42.8 us
    ppermute x3, waiting for transfers between devices, shift_chip(): lax.ppermute(x, 'dp', [(i, (i + CORES * step) % size) for i in range(size)])  31.8 us
    dot_general x1, matrix products, body(): lax.dot_general(grad_all, chosen_all, (((0,), (0,)), ((), ())), preferred...  12.4 us
    dot_general x1, matrix products, body(): lax.dot_general(normed, head_weight, (((1,), (1,)), ((), ())), preferred_...  8.25 us
    reshape x1, other arithmetic, body(): by_index.reshape(groups, slice_blocks, group_rows, block_width)  7.58 us
  transfers between devices with their start and end apart: 45, of which 21 were waited for; matrix products, arithmetic and copies ran while one was open for 6% of the time, Pallas kernels for 0%

profile of v1, /device:TPU:0, one launch (start us, length us, event | category | flops | bytes accessed | tf_op | source)
XLA Modules:
  0.0 367.7 jit_solution(17310280674556288096)
XLA Ops:
  0.6 1.7 collective-permute-start
  2.4 9.3 %collective-permute-start.1 = (bf16[128,1024]{1,0:T(8,128)(2,1)S(1)}, bf16[128,1024]{1,0:T(8,128)(2,1)S(1)}, u32[]{:S(2)}, u32[]{:S(2)}) collective-permute-start(bf16[128,1024]{1,0:T(8,128)(2,1)S(1)} %collective-permute-done), channel_id=1, source_target_pairs={{0,2},{2,4},{4,6},{6,7},{7,5},{5,3},{3,1},{1,0},{8,10},{10,12},{12... | collective-permute-start | bytes 786440 | tf_op jit(solution)/shard_map/ppermute | solution.py:35
  11.7 4.4 %collective-permute-done.1 = bf16[128,1024]{1,0:T(8,128)(2,1)S(1)} collective-permute-done((bf16[128,1024]{1,0:T(8,128)(2,1)S(1)}, bf16[128,1024]{1,0:T(8,128)(2,1)S(1)}, u32[]{:S(2)}, u32[]{:S(2)}) %collective-permute-start.1) | collective-permute-done | bytes 262176 | tf_op jit(solution)/shard_map/ppermute | solution.py:35
  16.1 11.0 %collective-permute-start.2 = (bf16[128,1024]{1,0:T(8,128)(2,1)S(1)}, bf16[128,1024]{1,0:T(8,128)(2,1)S(1)}, u32[]{:S(2)}, u32[]{:S(2)}) collective-permute-start(bf16[128,1024]{1,0:T(8,128)(2,1)S(1)} %collective-permute-done.1), channel_id=1, source_target_pairs={{0,2},{2,4},{4,6},{6,7},{7,5},{5,3},{3,1},{1,0},{8,10},{10,12},{12... | collective-permute-start | bytes 786440 | tf_op jit(solution)/shard_map/ppermute | solution.py:35
  28.2 5.1 %collective-permute-done.2 = bf16[128,1024]{1,0:T(8,128)(2,1)S(1)} collective-permute-done((bf16[128,1024]{1,0:T(8,128)(2,1)S(1)}, bf16[128,1024]{1,0:T(8,128)(2,1)S(1)}, u32[]{:S(2)}, u32[]{:S(2)}) %collective-permute-start.2) | collective-permute-done | bytes 262176 | tf_op jit(solution)/shard_map/ppermute | solution.py:35
  33.3 2.5 collective-permute-start.3
  37.6 65.2 %all-gather.2 = f32[32,2,128]{2,1,0:T(2,128)S(1)} all-gather(f32[1,2,128]{2,1,0:T(2,128)S(1)} %maximum_bitcast_fusion.2), channel_id=2, replica_groups=mesh['dp'=4,'vocab'=8] {'dp','vocab'}, dimensions={0}, use_global_device_ids=true | all-gather | bytes 33792 | tf_op jit(solution)/shard_map/all_gather | solution.py:119
  102.9 2.1 collective-permute-start.8
  108.9 2.0 gather_fusion
  110.9 7.6 %fusion.22 = (bf16[4,2,128,1024]{3,1,2,0:T(2,128)(2,1)}, f32[4,128,2,1024]{3,2,1,0:T(2,128)}) fusion(bf16[4,2,128,1024]{3,2,1,0:T(8,128)(2,1)} %bitcast.157), kind=kLoop, calls=%fused_computation.126 | loop fusion | flops 1048576 | bytes 8388608 | tf_op jit(solution)/shard_map/reshape | solution.py:137
  118.5 6.6 %reshape.136 = f32[2,2,128,2048]{3,2,1,0:T(8,128)} reshape(f32[4,128,2,1024]{3,2,1,0:T(2,128)} %get-tuple-element.17) | data formatting | bytes 8388608 | tf_op jit(solution)/shard_map/convert_element_type | solution.py:142
  125.1 8.2 %fusion = f32[2,2,128,2048]{3,2,1,0:T(8,128)S(1)} fusion(bf16[2048,2048]{1,0:T(8,128)(2,1)} %param.11, f32[2,2,128,2048]{3,2,1,0:T(8,128)} %reshape.136, f32[2048]{0:T(1024)S(1)} %dynamic_slice.66, f32[2,2,128]{2,1,0:T(2,128)S(1)} %bitcast.182), kind=kOutput, calls=%fused_computation.2 | convolution fusion | flops 4298113024 | bytes 16787456 | tf_op jit(solution)/shard_map/dot_general | solution.py:144
  133.4 2.0 copy-done.7
  135.4 1.5 dynamic-slice_bitcast_fusion
  138.5 3.4 collective-permute-start.20
  143.6 2.9 collective-permute-start.22
  148.2 2.5 bitcast_add_fusion
  152.1 3.9 %collective-permute-start.10 = (f32[128,2048]{1,0:T(8,128)S(1)}, f32[128,2048]{1,0:T(8,128)S(1)}, u32[]{:S(2)}, u32[]{:S(2)}) collective-permute-start(f32[128,2048]{1,0:T(8,128)S(1)} %dynamic-slice_bitcast_fusion.1), channel_id=1, source_target_pairs={{0,16},{8,24},{16,0},{24,8},{1,17},{9,25},{17,1},{25,9},{2,18},{10... | collective-permute-start | bytes 3145736 | tf_op jit(solution)/shard_map/ppermute | solution.py:88
  156.8 21.2 %collective-permute-done.10 = f32[128,2048]{1,0:T(8,128)S(1)} collective-permute-done((f32[128,2048]{1,0:T(8,128)S(1)}, f32[128,2048]{1,0:T(8,128)S(1)}, u32[]{:S(2)}, u32[]{:S(2)}) %collective-permute-start.10) | collective-permute-done | bytes 1048608 | tf_op jit(solution)/shard_map/ppermute | solution.py:88
  179.7 1.5 collective-permute-start.11
  183.2 4.4 %collective-permute-start.14 = (f32[2,128]{1,0:T(2,128)S(1)}, f32[2,128]{1,0:T(2,128)S(1)}, u32[]{:S(2)}, u32[]{:S(2)}) collective-permute-start(f32[2,128]{1,0:T(2,128)S(1)} %pad_maximum_fusion.6), channel_id=1, source_target_pairs={{0,7},{2,5},{4,3},{6,1},{7,0},{5,2},{3,4},{1,6},{8,15},{10,13},{12... | collective-permute-start | bytes 3080 | tf_op jit(solution)/shard_map/ppermute | solution.py:35
  187.6 1.7 collective-permute-start.16
  189.4 3.5 collective-permute-done.15
  193.7 1.8 collective-permute-start.25
  195.5 7.7 %collective-permute-done.25 = bf16[128,2048]{1,0:T(8,128)(2,1)S(1)} collective-permute-done((bf16[128,2048]{1,0:T(8,128)(2,1)S(1)}, bf16[128,2048]{1,0:T(8,128)(2,1)S(1)}, u32[]{:S(2)}, u32[]{:S(2)}) %collective-permute-start.25) | collective-permute-done | bytes 524320 | tf_op jit(solution)/shard_map/ppermute | solution.py:88
  207.5 1.7 pad_maximum_fusion.1
  209.2 6.9 %fusion.26 = f32[512,2048]{1,0:T(8,128)S(1)} fusion(bf16[512,2048]{1,0:T(8,128)(2,1)S(1)} %bitcast.162, bf16[2048,2048]{1,0:T(8,128)(2,1)} %param.11), kind=kOutput, calls=%fused_computation.130 | convolution fusion | flops 4294967296 | bytes 14680064 | tf_op jit(solution)/shard_map/dot_general | solution.py:182
  218.2 3.9 %collective-permute-done.27 = bf16[32,2048]{1,0:T(8,128)(2,1)S(1)} collective-permute-done((bf16[32,2048]{1,0:T(8,128)(2,1)S(1)}, bf16[32,2048]{1,0:T(8,128)(2,1)S(1)}, u32[]{:S(2)}, u32[]{:S(2)}) %collective-permute-start.27) | collective-permute-done | bytes 131104 | tf_op jit(solution)/shard_map/ppermute | solution.py:35
  222.5 1.7 collective-permute-start.28
  227.8 2.4 collective-permute-done.28
  231.3 1.7 collective-permute-start.29
  239.8 1.5 collective-permute-start.33
  241.4 2.8 collective-permute-done.43
  244.2 3.0 fusion.20
  247.8 67.4 %all-gather.3 = f32[32,1,128]{2,1,0:T(1,128)S(1)} all-gather(f32[1,1,128]{2,1,0:T(1,128)S(1)} %bitcast.180), channel_id=3, replica_groups=mesh['dp'=4,'vocab'=8] {'dp','vocab'}, dimensions={0}, use_global_device_ids=true | all-gather | bytes 16896 | tf_op jit(solution)/shard_map/all_gather | solution.py:178
  316.4 2.1 collective-permute-start.34
  318.6 4.2 %collective-permute-done.30 = bf16[64,2048]{1,0:T(8,128)(2,1)S(1)} collective-permute-done((bf16[64,2048]{1,0:T(8,128)(2,1)S(1)}, bf16[64,2048]{1,0:T(8,128)(2,1)S(1)}, u32[]{:S(2)}, u32[]{:S(2)}) %collective-permute-start.30) | collective-permute-done | bytes 262176 | tf_op jit(solution)/shard_map/ppermute | solution.py:35
  324.7 2.5 collective-permute-start.39
  327.3 4.3 %collective-permute-done.35 = bf16[64,2048]{1,0:T(8,128)(2,1)S(1)} collective-permute-done((bf16[64,2048]{1,0:T(8,128)(2,1)S(1)}, bf16[64,2048]{1,0:T(8,128)(2,1)S(1)}, u32[]{:S(2)}, u32[]{:S(2)}) %collective-permute-start.35) | collective-permute-done | bytes 262176 | tf_op jit(solution)/shard_map/ppermute | solution.py:35
  331.6 1.5 collective-permute-done.39
  333.0 2.5 collective-permute-start.40
  335.5 4.9 %collective-permute-done.36 = bf16[64,2048]{1,0:T(8,128)(2,1)S(1)} collective-permute-done((bf16[64,2048]{1,0:T(8,128)(2,1)S(1)}, bf16[64,2048]{1,0:T(8,128)(2,1)S(1)}, u32[]{:S(2)}, u32[]{:S(2)}) %collective-permute-start.36) | collective-permute-done | bytes 262176 | tf_op jit(solution)/shard_map/ppermute | solution.py:35
  340.4 1.6 collective-permute-done.40
  342.0 2.5 collective-permute-start.41
  344.5 3.3 collective-permute-done.37
  348.9 2.4 collective-permute-start.42
  351.3 1.7 pad_maximum_fusion
  354.5 12.4 %fusion.27 = f32[2048,3072]{1,0:T(8,128)} fusion(bf16[512,2048]{1,0:T(8,128)(2,1)S(1)} %bitcast.159, bf16[512,3072]{1,0:T(8,128)(2,1)S(1)} %bitcast.158), kind=kOutput, calls=%fused_computation.131 | convolution fusion | flops 6442450944 | bytes 30408704 | tf_op jit(solution)/shard_map/dot_general | solution.py:214
  (179 shorter events, 36.3 us)
Async XLA Ops:
  0.6 205.8 %copy-start = (bf16[128,3072]{1,0:T(8,128)(2,1)S(1)}, bf16[128,3072]{1,0:T(8,128)(2,1)}, u32[]{:S(2)}) copy-start(bf16[128,3072]{1,0:T(8,128)(2,1)} %param.15) | copy-start | bytes 2359300
  0.6 1.7 collective-permute-start
  2.4 13.7 %collective-permute-start.1 = (bf16[128,1024]{1,0:T(8,128)(2,1)S(1)}, bf16[128,1024]{1,0:T(8,128)(2,1)S(1)}, u32[]{:S(2)}, u32[]{:S(2)}) collective-permute-start(bf16[128,1024]{1,0:T(8,128)(2,1)S(1)} %collective-permute-done), channel_id=1, source_target_pairs={{0,2},{2,4},{4,6},{6,7},{7,5},{5,3},{3,1},{1,0},{8,10},{10,12},{12... | collective-permute-start | bytes 786440 | tf_op jit(solution)/shard_map/ppermute | solution.py:35
  11.7 15.8 %collective-permute-start.5 = (bf16[128,1024]{1,0:T(8,128)(2,1)S(1)}, bf16[128,1024]{1,0:T(8,128)(2,1)S(1)}, u32[]{:S(2)}, u32[]{:S(2)}) collective-permute-start(bf16[128,1024]{1,0:T(8,128)(2,1)S(1)} %collective-permute-done), channel_id=1, source_target_pairs={{0,1},{2,0},{4,2},{6,4},{7,6},{5,7},{3,5},{1,3},{8,9},{10,8},{12,1... | collective-permute-start | bytes 786440 | tf_op jit(solution)/shard_map/ppermute | solution.py:35
  16.1 17.2 %collective-permute-start.2 = (bf16[128,1024]{1,0:T(8,128)(2,1)S(1)}, bf16[128,1024]{1,0:T(8,128)(2,1)S(1)}, u32[]{:S(2)}, u32[]{:S(2)}) collective-permute-start(bf16[128,1024]{1,0:T(8,128)(2,1)S(1)} %collective-permute-done.1), channel_id=1, source_target_pairs={{0,2},{2,4},{4,6},{6,7},{7,5},{5,3},{3,1},{1,0},{8,10},{10,12},{12... | collective-permute-start | bytes 786440 | tf_op jit(solution)/shard_map/ppermute | solution.py:35
  27.6 8.7 %collective-permute-start.6 = (bf16[128,1024]{1,0:T(8,128)(2,1)S(1)}, bf16[128,1024]{1,0:T(8,128)(2,1)S(1)}, u32[]{:S(2)}, u32[]{:S(2)}) collective-permute-start(bf16[128,1024]{1,0:T(8,128)(2,1)S(1)} %collective-permute-done.5), channel_id=1, source_target_pairs={{0,1},{2,0},{4,2},{6,4},{7,6},{5,7},{3,5},{1,3},{8,9},{10,8},{12,1... | collective-permute-start | bytes 786440 | tf_op jit(solution)/shard_map/ppermute | solution.py:35
  33.3 69.5 %collective-permute-start.3 = (bf16[128,1024]{1,0:T(8,128)(2,1)S(1)}, bf16[128,1024]{1,0:T(8,128)(2,1)S(1)}, u32[]{:S(2)}, u32[]{:S(2)}) collective-permute-start(bf16[128,1024]{1,0:T(8,128)(2,1)S(1)} %collective-permute-done.2), channel_id=1, source_target_pairs={{0,2},{2,4},{4,6},{6,7},{7,5},{5,3},{3,1},{1,0},{8,10},{10,12},{12... | collective-permute-start | bytes 786440 | tf_op jit(solution)/shard_map/ppermute | solution.py:35
  36.2 66.7 %collective-permute-start.7 = (bf16[128,1024]{1,0:T(8,128)(2,1)S(1)}, bf16[128,1024]{1,0:T(8,128)(2,1)S(1)}, u32[]{:S(2)}, u32[]{:S(2)}) collective-permute-start(bf16[128,1024]{1,0:T(8,128)(2,1)S(1)} %collective-permute-done.6), channel_id=1, source_target_pairs={{0,1},{2,0},{4,2},{6,4},{7,6},{5,7},{3,5},{1,3},{8,9},{10,8},{12,1... | collective-permute-start | bytes 786440 | tf_op jit(solution)/shard_map/ppermute | solution.py:35
  102.8 5.5 %collective-permute-start.4 = (bf16[64,1024]{1,0:T(8,128)(2,1)S(1)}, bf16[64,1024]{1,0:T(8,128)(2,1)S(1)}, u32[]{:S(2)}, u32[]{:S(2)}) collective-permute-start(bf16[64,1024]{1,0:T(8,128)(2,1)S(1)} %slice.76), channel_id=1, source_target_pairs={{0,2},{2,4},{4,6},{6,7},{7,5},{5,3},{3,1},{1,0},{8,10},{10,12},{12... | collective-permute-start | bytes 393224 | tf_op jit(solution)/shard_map/ppermute | solution.py:35
  102.9 5.4 %collective-permute-start.8 = (bf16[64,1024]{1,0:T(8,128)(2,1)S(1)}, bf16[64,1024]{1,0:T(8,128)(2,1)S(1)}, u32[]{:S(2)}, u32[]{:S(2)}) collective-permute-start(bf16[64,1024]{1,0:T(8,128)(2,1)S(1)} %slice.77), channel_id=1, source_target_pairs={{0,1},{2,0},{4,2},{6,4},{7,6},{5,7},{3,5},{1,3},{8,9},{10,8},{12,1... | collective-permute-start | bytes 393224 | tf_op jit(solution)/shard_map/ppermute | solution.py:35
  136.9 11.3 %collective-permute-start.9 = (f32[2,128,2048]{2,1,0:T(8,128)}, f32[2,128,2048]{2,1,0:T(8,128)}, u32[]{:S(2)}, u32[]{:S(2)}) collective-permute-start(f32[2,128,2048]{2,1,0:T(8,128)} %dynamic-slice_bitcast_fusion), channel_id=1, source_target_pairs={{0,8},{8,0},{16,24},{24,16},{1,9},{9,1},{17,25},{25,17},{2,10},{10... | collective-permute-start | bytes 6291464 | tf_op jit(solution)/shard_map/ppermute | solution.py:84
  137.4 6.2 %collective-permute-start.18 = (f32[2,128]{1,0:T(2,128)S(1)}, f32[2,128]{1,0:T(2,128)S(1)}, u32[]{:S(2)}, u32[]{:S(2)}) collective-permute-start(f32[2,128]{1,0:T(2,128)S(1)} %pad_maximum_fusion.7), channel_id=1, source_target_pairs={{0,2},{2,4},{4,6},{6,7},{7,5},{5,3},{3,1},{1,0},{8,10},{10,12},{12... | collective-permute-start | bytes 3080 | tf_op jit(solution)/shard_map/ppermute | solution.py:35
  137.4 9.1 %collective-permute-start.19 = (f32[2,128]{1,0:T(2,128)S(1)}, f32[2,128]{1,0:T(2,128)S(1)}, u32[]{:S(2)}, u32[]{:S(2)}) collective-permute-start(f32[2,128]{1,0:T(2,128)S(1)} %pad_maximum_fusion.7), channel_id=1, source_target_pairs={{0,4},{2,6},{4,7},{6,5},{7,3},{5,1},{3,0},{1,2},{8,12},{10,14},{12... | collective-permute-start | bytes 3080 | tf_op jit(solution)/shard_map/ppermute | solution.py:35
  138.5 8.8 %collective-permute-start.20 = (f32[2,128]{1,0:T(2,128)S(1)}, f32[2,128]{1,0:T(2,128)S(1)}, u32[]{:S(2)}, u32[]{:S(2)}) collective-permute-start(f32[2,128]{1,0:T(2,128)S(1)} %pad_maximum_fusion.7), channel_id=1, source_target_pairs={{0,6},{2,7},{4,5},{6,3},{7,1},{5,0},{3,2},{1,4},{8,14},{10,15},{12... | collective-permute-start | bytes 3080 | tf_op jit(solution)/shard_map/ppermute | solution.py:35
  141.9 6.3 %collective-permute-start.21 = (f32[2,128]{1,0:T(2,128)S(1)}, f32[2,128]{1,0:T(2,128)S(1)}, u32[]{:S(2)}, u32[]{:S(2)}) collective-permute-start(f32[2,128]{1,0:T(2,128)S(1)} %pad_maximum_fusion.7), channel_id=1, source_target_pairs={{0,7},{2,5},{4,3},{6,1},{7,0},{5,2},{3,4},{1,6},{8,15},{10,13},{12... | collective-permute-start | bytes 3080 | tf_op jit(solution)/shard_map/ppermute | solution.py:35
  143.6 12.4 %collective-permute-start.22 = (f32[2,128]{1,0:T(2,128)S(1)}, f32[2,128]{1,0:T(2,128)S(1)}, u32[]{:S(2)}, u32[]{:S(2)}) collective-permute-start(f32[2,128]{1,0:T(2,128)S(1)} %pad_maximum_fusion.7), channel_id=1, source_target_pairs={{0,5},{2,3},{4,1},{6,0},{7,2},{5,4},{3,6},{1,7},{8,13},{10,11},{12... | collective-permute-start | bytes 3080 | tf_op jit(solution)/shard_map/ppermute | solution.py:35
  146.5 9.5 %collective-permute-start.23 = (f32[2,128]{1,0:T(2,128)S(1)}, f32[2,128]{1,0:T(2,128)S(1)}, u32[]{:S(2)}, u32[]{:S(2)}) collective-permute-start(f32[2,128]{1,0:T(2,128)S(1)} %pad_maximum_fusion.7), channel_id=1, source_target_pairs={{0,3},{2,1},{4,0},{6,2},{7,4},{5,6},{3,7},{1,5},{8,11},{10,9},{12,... | collective-permute-start | bytes 3080 | tf_op jit(solution)/shard_map/ppermute | solution.py:35
  147.4 8.7 %collective-permute-start.24 = (f32[2,128]{1,0:T(2,128)S(1)}, f32[2,128]{1,0:T(2,128)S(1)}, u32[]{:S(2)}, u32[]{:S(2)}) collective-permute-start(f32[2,128]{1,0:T(2,128)S(1)} %pad_maximum_fusion.7), channel_id=1, source_target_pairs={{0,1},{2,0},{4,2},{6,4},{7,6},{5,7},{3,5},{1,3},{8,9},{10,8},{12,1... | collective-permute-start | bytes 3080 | tf_op jit(solution)/shard_map/ppermute | solution.py:35
  152.1 25.9 %collective-permute-start.10 = (f32[128,2048]{1,0:T(8,128)S(1)}, f32[128,2048]{1,0:T(8,128)S(1)}, u32[]{:S(2)}, u32[]{:S(2)}) collective-permute-start(f32[128,2048]{1,0:T(8,128)S(1)} %dynamic-slice_bitcast_fusion.1), channel_id=1, source_target_pairs={{0,16},{8,24},{16,0},{24,8},{1,17},{9,25},{17,1},{25,9},{2,18},{10... | collective-permute-start | bytes 3145736 | tf_op jit(solution)/shard_map/ppermute | solution.py:88
  156.7 49.6 %copy-start.10 = (s32[128]{0:T(128)S(1)}, s32[128]{0:T(128)}, u32[]{:S(2)}) copy-start(s32[128]{0:T(128)} %param.14) | copy-start | bytes 1540
  179.7 7.9 %collective-permute-start.11 = (f32[2,128]{1,0:T(2,128)S(1)}, f32[2,128]{1,0:T(2,128)S(1)}, u32[]{:S(2)}, u32[]{:S(2)}) collective-permute-start(f32[2,128]{1,0:T(2,128)S(1)} %pad_maximum_fusion.6), channel_id=1, source_target_pairs={{0,2},{2,4},{4,6},{6,7},{7,5},{5,3},{3,1},{1,0},{8,10},{10,12},{12... | collective-permute-start | bytes 3080 | tf_op jit(solution)/shard_map/ppermute | solution.py:35
  181.2 8.2 %collective-permute-start.12 = (f32[2,128]{1,0:T(2,128)S(1)}, f32[2,128]{1,0:T(2,128)S(1)}, u32[]{:S(2)}, u32[]{:S(2)}) collective-permute-start(f32[2,128]{1,0:T(2,128)S(1)} %pad_maximum_fusion.6), channel_id=1, source_target_pairs={{0,4},{2,6},{4,7},{6,5},{7,3},{5,1},{3,0},{1,2},{8,12},{10,14},{12... | collective-permute-start | bytes 3080 | tf_op jit(solution)/shard_map/ppermute | solution.py:35
  182.4 7.0 %collective-permute-start.13 = (f32[2,128]{1,0:T(2,128)S(1)}, f32[2,128]{1,0:T(2,128)S(1)}, u32[]{:S(2)}, u32[]{:S(2)}) collective-permute-start(f32[2,128]{1,0:T(2,128)S(1)} %pad_maximum_fusion.6), channel_id=1, source_target_pairs={{0,6},{2,7},{4,5},{6,3},{7,1},{5,0},{3,2},{1,4},{8,14},{10,15},{12... | collective-permute-start | bytes 3080 | tf_op jit(solution)/shard_map/ppermute | solution.py:35
  183.2 6.3 %collective-permute-start.14 = (f32[2,128]{1,0:T(2,128)S(1)}, f32[2,128]{1,0:T(2,128)S(1)}, u32[]{:S(2)}, u32[]{:S(2)}) collective-permute-start(f32[2,128]{1,0:T(2,128)S(1)} %pad_maximum_fusion.6), channel_id=1, source_target_pairs={{0,7},{2,5},{4,3},{6,1},{7,0},{5,2},{3,4},{1,6},{8,15},{10,13},{12... | collective-permute-start | bytes 3080 | tf_op jit(solution)/shard_map/ppermute | solution.py:35
  187.6 5.4 %collective-permute-start.15 = (f32[2,128]{1,0:T(2,128)S(1)}, f32[2,128]{1,0:T(2,128)S(1)}, u32[]{:S(2)}, u32[]{:S(2)}) collective-permute-start(f32[2,128]{1,0:T(2,128)S(1)} %pad_maximum_fusion.6), channel_id=1, source_target_pairs={{0,5},{2,3},{4,1},{6,0},{7,2},{5,4},{3,6},{1,7},{8,13},{10,11},{12... | collective-permute-start | bytes 3080 | tf_op jit(solution)/shard_map/ppermute | solution.py:35
  187.6 5.4 %collective-permute-start.16 = (f32[2,128]{1,0:T(2,128)S(1)}, f32[2,128]{1,0:T(2,128)S(1)}, u32[]{:S(2)}, u32[]{:S(2)}) collective-permute-start(f32[2,128]{1,0:T(2,128)S(1)} %pad_maximum_fusion.6), channel_id=1, source_target_pairs={{0,3},{2,1},{4,0},{6,2},{7,4},{5,6},{3,7},{1,5},{8,11},{10,9},{12,... | collective-permute-start | bytes 3080 | tf_op jit(solution)/shard_map/ppermute | solution.py:35
  189.4 3.6 collective-permute-start.17
  193.7 9.5 %collective-permute-start.25 = (bf16[128,2048]{1,0:T(8,128)(2,1)S(1)}, bf16[128,2048]{1,0:T(8,128)(2,1)S(1)}, u32[]{:S(2)}, u32[]{:S(2)}) collective-permute-start(bf16[128,2048]{1,0:T(8,128)(2,1)S(1)} %get-tuple-element.7), channel_id=1, source_target_pairs={{0,16},{8,24},{16,0},{24,8},{1,17},{9,25},{17,1},{25,9},{2,18},{10... | collective-permute-start | bytes 1572872 | tf_op jit(solution)/shard_map/ppermute | solution.py:88
  204.3 3.1 collective-permute-start.26
  216.1 6.0 %collective-permute-start.27 = (bf16[32,2048]{1,0:T(8,128)(2,1)S(1)}, bf16[32,2048]{1,0:T(8,128)(2,1)S(1)}, u32[]{:S(2)}, u32[]{:S(2)}) collective-permute-start(bf16[32,2048]{1,0:T(8,128)(2,1)S(1)} %get-tuple-element.22), channel_id=1, source_target_pairs={{0,2},{2,4},{4,6},{6,7},{7,5},{5,3},{3,1},{1,0},{8,10},{10,12},{12... | collective-permute-start | bytes 393224 | tf_op jit(solution)/shard_map/ppermute | solution.py:35
  216.8 5.6 %collective-permute-start.31 = (bf16[32,2048]{1,0:T(8,128)(2,1)S(1)}, bf16[32,2048]{1,0:T(8,128)(2,1)S(1)}, u32[]{:S(2)}, u32[]{:S(2)}) collective-permute-start(bf16[32,2048]{1,0:T(8,128)(2,1)S(1)} %get-tuple-element.23), channel_id=1, source_target_pairs={{0,1},{2,0},{4,2},{6,4},{7,6},{5,7},{3,5},{1,3},{8,9},{10,8},{12,1... | collective-permute-start | bytes 393224 | tf_op jit(solution)/shard_map/ppermute | solution.py:35
  222.5 7.7 %collective-permute-start.28 = (bf16[64,2048]{1,0:T(8,128)(2,1)S(1)}, bf16[64,2048]{1,0:T(8,128)(2,1)S(1)}, u32[]{:S(2)}, u32[]{:S(2)}) collective-permute-start(bf16[64,2048]{1,0:T(8,128)(2,1)S(1)} %pad_maximum_fusion.4), channel_id=1, source_target_pairs={{0,2},{2,4},{4,6},{6,7},{7,5},{5,3},{3,1},{1,0},{8,10},{10,12},{12... | collective-permute-start | bytes 786440 | tf_op jit(solution)/shard_map/ppermute | solution.py:35
  225.3 18.9 %collective-permute-start.43 = (bf16[128,3072]{1,0:T(8,128)(2,1)}, bf16[128,3072]{1,0:T(8,128)(2,1)}, u32[]{:S(2)}, u32[]{:S(2)}) collective-permute-start(bf16[128,3072]{1,0:T(8,128)(2,1)} %broadcast_select_fusion), channel_id=1, source_target_pairs={{0,16},{8,24},{16,0},{24,8},{1,17},{9,25},{17,1},{25,9},{2,18},{10... | collective-permute-start | bytes 2359304 | tf_op jit(solution)/shard_map/ppermute | solution.py:88
  227.5 10.9 %collective-permute-start.32 = (bf16[64,2048]{1,0:T(8,128)(2,1)S(1)}, bf16[64,2048]{1,0:T(8,128)(2,1)}, u32[]{:S(2)}, u32[]{:S(2)}) collective-permute-start(bf16[64,2048]{1,0:T(8,128)(2,1)S(1)} %pad_maximum_fusion.5), channel_id=1, source_target_pairs={{0,1},{2,0},{4,2},{6,4},{7,6},{5,7},{3,5},{1,3},{8,9},{10,8},{12,1... | collective-permute-start | bytes 786440 | tf_op jit(solution)/shard_map/ppermute | solution.py:35
  231.3 7.0 %collective-permute-start.29 = (bf16[64,2048]{1,0:T(8,128)(2,1)S(1)}, bf16[64,2048]{1,0:T(8,128)(2,1)}, u32[]{:S(2)}, u32[]{:S(2)}) collective-permute-start(bf16[64,2048]{1,0:T(8,128)(2,1)S(1)} %add_convert_fusion.3), channel_id=1, source_target_pairs={{0,2},{2,4},{4,6},{6,7},{7,5},{5,3},{3,1},{1,0},{8,10},{10,12},{12... | collective-permute-start | bytes 786440 | tf_op jit(solution)/shard_map/ppermute | solution.py:35
  239.8 75.5 %collective-permute-start.33 = (bf16[64,2048]{1,0:T(8,128)(2,1)S(1)}, bf16[64,2048]{1,0:T(8,128)(2,1)S(1)}, u32[]{:S(2)}, u32[]{:S(2)}) collective-permute-start(bf16[64,2048]{1,0:T(8,128)(2,1)S(1)} %get-tuple-element.11), channel_id=1, source_target_pairs={{0,1},{2,0},{4,2},{6,4},{7,6},{5,7},{3,5},{1,3},{8,9},{10,8},{12,1... | collective-permute-start | bytes 786440 | tf_op jit(solution)/shard_map/ppermute | solution.py:35
  247.2 104.1 %collective-permute-start.44 = (bf16[2,128,3072]{2,1,0:T(8,128)(2,1)}, bf16[2,128,3072]{2,1,0:T(8,128)(2,1)}, u32[]{:S(2)}, u32[]{:S(2)}) collective-permute-start(bf16[2,128,3072]{2,1,0:T(8,128)(2,1)} %get-tuple-element.19), channel_id=1, source_target_pairs={{0,8},{8,0},{16,24},{24,16},{1,9},{9,1},{17,25},{25,17},{2,10},{10... | collective-permute-start | bytes 4718600 | tf_op jit(solution)/shard_map/ppermute | solution.py:84
  247.8 103.5 %copy-start.5 = (bf16[2,1,128,3072]{3,2,0,1:T(8,128)(2,1)S(1)}, bf16[2,1,128,3072]{3,2,0,1:T(8,128)(2,1)}, u32[]{:S(2)}) copy-start(bf16[2,1,128,3072]{3,2,0,1:T(8,128)(2,1)} %get-tuple-element.18) | copy-start | bytes 4718596
  315.3 7.5 %collective-permute-start.30 = (bf16[64,2048]{1,0:T(8,128)(2,1)S(1)}, bf16[64,2048]{1,0:T(8,128)(2,1)S(1)}, u32[]{:S(2)}, u32[]{:S(2)}) collective-permute-start(bf16[64,2048]{1,0:T(8,128)(2,1)S(1)} %get-tuple-element.10), channel_id=1, source_target_pairs={{0,2},{2,4},{4,6},{6,7},{7,5},{5,3},{3,1},{1,0},{8,10},{10,12},{12... | collective-permute-start | bytes 786440 | tf_op jit(solution)/shard_map/ppermute | solution.py:35
  316.4 7.0 %collective-permute-start.34 = (bf16[64,2048]{1,0:T(8,128)(2,1)S(1)}, bf16[64,2048]{1,0:T(8,128)(2,1)S(1)}, u32[]{:S(2)}, u32[]{:S(2)}) collective-permute-start(bf16[64,2048]{1,0:T(8,128)(2,1)S(1)} %add_convert_fusion), channel_id=1, source_target_pairs={{0,1},{2,0},{4,2},{6,4},{7,6},{5,7},{3,5},{1,3},{8,9},{10,8},{12,1... | collective-permute-start | bytes 786440 | tf_op jit(solution)/shard_map/ppermute | solution.py:35
  324.7 6.9 %collective-permute-start.35 = (bf16[64,2048]{1,0:T(8,128)(2,1)S(1)}, bf16[64,2048]{1,0:T(8,128)(2,1)S(1)}, u32[]{:S(2)}, u32[]{:S(2)}) collective-permute-start(bf16[64,2048]{1,0:T(8,128)(2,1)S(1)} %subtract_convert_fusion), channel_id=1, source_target_pairs={{0,2},{2,4},{4,6},{6,7},{7,5},{5,3},{3,1},{1,0},{8,10},{10,12},{12... | collective-permute-start | bytes 786440 | tf_op jit(solution)/shard_map/ppermute | solution.py:35
  324.7 8.3 %collective-permute-start.39 = (bf16[64,2048]{1,0:T(8,128)(2,1)S(1)}, bf16[64,2048]{1,0:T(8,128)(2,1)S(1)}, u32[]{:S(2)}, u32[]{:S(2)}) collective-permute-start(bf16[64,2048]{1,0:T(8,128)(2,1)S(1)} %subtract_convert_fusion), channel_id=1, source_target_pairs={{0,1},{2,0},{4,2},{6,4},{7,6},{5,7},{3,5},{1,3},{8,9},{10,8},{12,1... | collective-permute-start | bytes 786440 | tf_op jit(solution)/shard_map/ppermute | solution.py:35
  331.6 8.9 %collective-permute-start.36 = (bf16[64,2048]{1,0:T(8,128)(2,1)S(1)}, bf16[64,2048]{1,0:T(8,128)(2,1)S(1)}, u32[]{:S(2)}, u32[]{:S(2)}) collective-permute-start(bf16[64,2048]{1,0:T(8,128)(2,1)S(1)} %collective-permute-done.35), channel_id=1, source_target_pairs={{0,2},{2,4},{4,6},{6,7},{7,5},{5,3},{3,1},{1,0},{8,10},{10,12},{12... | collective-permute-start | bytes 786440 | tf_op jit(solution)/shard_map/ppermute | solution.py:35
  333.0 9.0 %collective-permute-start.40 = (bf16[64,2048]{1,0:T(8,128)(2,1)S(1)}, bf16[64,2048]{1,0:T(8,128)(2,1)S(1)}, u32[]{:S(2)}, u32[]{:S(2)}) collective-permute-start(bf16[64,2048]{1,0:T(8,128)(2,1)S(1)} %collective-permute-done.39), channel_id=1, source_target_pairs={{0,1},{2,0},{4,2},{6,4},{7,6},{5,7},{3,5},{1,3},{8,9},{10,8},{12,1... | collective-permute-start | bytes 786440 | tf_op jit(solution)/shard_map/ppermute | solution.py:35
  340.4 7.4 %collective-permute-start.37 = (bf16[64,2048]{1,0:T(8,128)(2,1)S(1)}, bf16[64,2048]{1,0:T(8,128)(2,1)S(1)}, u32[]{:S(2)}, u32[]{:S(2)}) collective-permute-start(bf16[64,2048]{1,0:T(8,128)(2,1)S(1)} %collective-permute-done.36), channel_id=1, source_target_pairs={{0,2},{2,4},{4,6},{6,7},{7,5},{5,3},{3,1},{1,0},{8,10},{10,12},{12... | collective-permute-start | bytes 786440 | tf_op jit(solution)/shard_map/ppermute | solution.py:35
  342.0 6.9 %collective-permute-start.41 = (bf16[64,2048]{1,0:T(8,128)(2,1)S(1)}, bf16[64,2048]{1,0:T(8,128)(2,1)S(1)}, u32[]{:S(2)}, u32[]{:S(2)}) collective-permute-start(bf16[64,2048]{1,0:T(8,128)(2,1)S(1)} %collective-permute-done.40), channel_id=1, source_target_pairs={{0,1},{2,0},{4,2},{6,4},{7,6},{5,7},{3,5},{1,3},{8,9},{10,8},{12,1... | collective-permute-start | bytes 786440 | tf_op jit(solution)/shard_map/ppermute | solution.py:35
  347.8 5.4 %collective-permute-start.38 = (bf16[32,2048]{1,0:T(8,128)(2,1)S(1)}, bf16[32,2048]{1,0:T(8,128)(2,1)S(1)}, u32[]{:S(2)}, u32[]{:S(2)}) collective-permute-start(bf16[32,2048]{1,0:T(8,128)(2,1)S(1)} %slice.84), channel_id=1, source_target_pairs={{0,2},{2,4},{4,6},{6,7},{7,5},{5,3},{3,1},{1,0},{8,10},{10,12},{12... | collective-permute-start | bytes 393224 | tf_op jit(solution)/shard_map/ppermute | solution.py:35
  348.9 5.0 %collective-permute-start.42 = (bf16[32,2048]{1,0:T(8,128)(2,1)S(1)}, bf16[32,2048]{1,0:T(8,128)(2,1)S(1)}, u32[]{:S(2)}, u32[]{:S(2)}) collective-permute-start(bf16[32,2048]{1,0:T(8,128)(2,1)S(1)} %slice.85), channel_id=1, source_target_pairs={{0,1},{2,0},{4,2},{6,4},{7,6},{5,7},{3,5},{1,3},{8,9},{10,8},{12,1... | collective-permute-start | bytes 393224 | tf_op jit(solution)/shard_map/ppermute | solution.py:35
  (8 other events, 67.9 us)

commit v2 on v0

v2 whole, which is shorter than its diff:
```python
import functools

import jax
import jax.numpy as jnp
from jax import lax
from jax.experimental import pallas as pl
from jax.experimental.pallas import tpu as pltpu
from jax.sharding import PartitionSpec as P

TREE = 64
CORES = 2
LANES = 128
CHUNKS = 2
F32 = jnp.float32
BF16 = jnp.bfloat16


def ring_order(rows, columns):
    if columns == 1 or rows == 1:
        return list(range(rows * columns))
    order = [r * columns for r in range(rows)]
    for step in range(rows):
        r = rows - 1 - step
        line = [r * columns + c for c in range(1, columns)]
        order += line if step % 2 == 0 else line[::-1]
    return order


class Ring:
    def __init__(self, size, columns):
        self.size = size
        self.half = size // 2
        self.order = ring_order(size // columns, columns)
        place = [0] * size
        for position, index in enumerate(self.order):
            place[index] = position
        self.place = place
        self.position = jnp.asarray(place, jnp.int32)[lax.axis_index("vocab")]

    def shift(self, x, step):
        size, order = self.size, self.order
        return lax.ppermute(
            x, "vocab", [(order[p], order[(p + step) % size]) for p in range(size)]
        )

    def partner(self, x, bit):
        return lax.ppermute(x, "vocab", [(v, v ^ bit) for v in range(self.size)])

    def meet(self, x, merge):
        bit = 1
        while bit < self.size:
            x = merge(x, self.partner(x, bit))
            bit *= 2
        return x

    def entry(self, position):
        return (position - self.position + self.half + self.size) % self.size

    def gather(self, block):
        ahead, behind = [block], [block]
        for _ in range(self.half - 1):
            ahead.append(self.shift(ahead[-1], 1))
            behind.append(self.shift(behind[-1], -1))
        cut = block.shape[0] // 2
        far = jnp.concatenate(
            [self.shift(ahead[-1][:cut], 1), self.shift(behind[-1][cut:], -1)], axis=0
        )
        return jnp.stack([far] + ahead[1:][::-1] + [block] + behind[1:])

    def by_position(self, line):
        return jnp.roll(line, self.position - self.half, axis=0)

    def scatter_sum(self, part):
        steps = self.half - 1
        far = part(self.half).astype(BF16)
        cut = far.shape[0] // 2
        got = self.shift(far[:cut], 1).astype(F32)
        ahead = part(steps)
        ahead = jnp.concatenate([ahead[:cut] + got, ahead[cut:]], axis=0)
        got = self.shift(far[cut:], -1).astype(F32)
        behind = part(-steps)
        behind = jnp.concatenate([behind[:cut], behind[cut:] + got], axis=0)
        for step in range(steps - 1, -1, -1):
            got_ahead = self.shift(ahead.astype(BF16), 1).astype(F32)
            got_behind = self.shift(behind.astype(BF16), -1).astype(F32)
            if step > 0:
                ahead = part(step) + got_ahead
                behind = part(-step) + got_behind
        return part(0) + got_ahead + got_behind


class Groups:
    def __init__(self, size):
        self.size = size
        self.chips = size // CORES
        index = lax.axis_index("dp")
        self.chip, self.core = index // CORES, index % CORES
        self.order = [
            (self.chip + d) % self.chips * CORES + (self.core ^ e)
            for e in range(CORES)
            for d in range(self.chips)
        ]

    def entry(self, group):
        return (group % CORES ^ self.core) * self.chips + (
            group // CORES - self.chip + self.chips
        ) % self.chips

    def swap(self, x):
        return lax.ppermute(x, "dp", [(i, i ^ 1) for i in range(self.size)])

    def shift(self, x, step):
        size = self.size
        return lax.ppermute(x, "dp", [(i, (i + CORES * step) % size) for i in range(size)])

    def gather(self, block):
        mine = jnp.stack([block] + [self.shift(block, -d) for d in range(1, self.chips)])
        return jnp.concatenate([mine, self.swap(mine)], axis=0)


def project_kernel(slots, index_ref, blocks_ref, factor_ref, gain_ref, weight_ref, keep_ref, send_ref, normed_ref):
    rows, width = blocks_ref.shape[1:]
    groups = factor_ref.shape[0]
    half = groups // CORES * rows

    @pl.when(pl.program_id(0) == 0)
    def _():
        for g in range(groups):
            factor = factor_ref[g]
            for k in range(slots):
                columns = pl.ds(k * width, width)
                values = blocks_ref[index_ref[g * slots + k]].astype(F32)
                normed_ref[pl.ds(g * rows, rows), columns] = (
                    values * factor * gain_ref[:, columns]
                ).astype(BF16)

    for ref, start in ((keep_ref, 0), (send_ref, half)):
        ref[...] = lax.dot_general(
            normed_ref[pl.ds(start, half), :],
            weight_ref[...],
            (((1,), (1,)), ((), ())),
            preferred_element_type=F32,
        )


def project(index, blocks, factor, gain, weight):
    count, rows, width = blocks.shape
    groups = factor.shape[0]
    vocab, depth = weight.shape
    slots = depth // width
    tile = min(vocab, 256)
    all_rows = groups * rows
    half = all_rows // CORES
    out = jax.ShapeDtypeStruct((half, vocab), F32)
    whole = lambda shape: pl.BlockSpec(shape, lambda n, index: (0,) * len(shape))
    return pl.pallas_call(
        functools.partial(project_kernel, slots),
        grid_spec=pltpu.PrefetchScalarGridSpec(
            num_scalar_prefetch=1,
            grid=(vocab // tile,),
            in_specs=[
                whole(blocks.shape),
                whole(factor.shape),
                whole(gain.shape),
                pl.BlockSpec((tile, depth), lambda n, index: (n, 0)),
            ],
            out_specs=[pl.BlockSpec((half, tile), lambda n, index: (0, n))] * 2,
            scratch_shapes=[pltpu.VMEM((all_rows, depth), BF16)],
        ),
        out_shape=[out, out],
        compiler_params=pltpu.CompilerParams(vmem_limit_bytes=24 * 2**20),
        cost_estimate=pl.CostEstimate(
            flops=2 * all_rows * depth * vocab,
            bytes_accessed=vocab * depth * 2 + all_rows * (depth * 2 + vocab * 4),
            transcendentals=0,
        ),
    )(index, blocks, factor, gain, weight)


def body(hidden, norm_gain, head_weight, target_logits, valid_rows, parents, features):
    groups = Groups(lax.axis_size("dp"))
    parts = lax.axis_size("vocab")
    vocab_index = lax.axis_index("vocab")
    ring = Ring(parts, groups.chips)
    group_rows, block_width = hidden.shape
    chunk_rows = group_rows // CHUNKS
    step_rows = groups.size * chunk_rows
    piece_rows = step_rows // parts
    model_width = block_width * parts
    slots = parts // groups.size
    slice_width = block_width * slots
    vocab_width = target_logits.shape[1]

    def chunk(x, h):
        return x[h * chunk_rows : (h + 1) * chunk_rows]

    def column_owner(g, v):
        far = g % CORES * groups.chips + g // CORES
        return v // slots * parts + far * slots + v % slots

    turn = [
        (g * parts + v, column_owner(g, v)) for g in range(groups.size) for v in range(parts)
    ]
    turned = [lax.ppermute(chunk(hidden, h), ("dp", "vocab"), turn) for h in range(CHUNKS)]

    live_rows = (valid_rows == 1).astype(F32)
    targets = target_logits.astype(F32)
    target_top = jnp.max(targets, axis=1)
    target_total = jnp.sum(jnp.exp(targets - target_top[:, None]), axis=1)
    square_part = jnp.sum(jnp.square(hidden.astype(F32)), axis=1)

    def merge_totals(a, b):
        top = jnp.maximum(a[-2], b[-2])
        total = a[-1] * jnp.exp(a[-2] - top) + b[-1] * jnp.exp(b[-2] - top)
        return jnp.concatenate([a[:-2] + b[:-2], jnp.stack([top, total])])

    met = ring.meet(jnp.stack([square_part, target_top, target_total]), merge_totals)
    target_scale = jnp.exp(target_top - met[1]) / met[2]
    both = groups.gather(jnp.stack([met[0], live_rows]))
    valid_count = jnp.sum(both[:, 1])
    row_factor = lax.rsqrt(both[:, 0] / model_width + 1e-05)

    tree_rows = jnp.arange(group_rows, dtype=jnp.int32) // TREE * TREE + parents
    chosen = features.at[tree_rows].get(mode="promise_in_bounds")
    chosen = groups.gather(chosen.reshape(CHUNKS, chunk_rows, -1))
    chosen = chosen.transpose(1, 0, 2, 3).reshape(CHUNKS * step_rows, -1)

    gain = lax.dynamic_slice_in_dim(
        norm_gain, lax.axis_index("dp") * slice_width, slice_width
    ).reshape(1, slice_width)

    def slot_entry(group, k):
        far = group % CORES * groups.chips + group // CORES
        place = jnp.asarray(ring.place, jnp.int32)
        return ring.entry(place[far * slots + k])

    index = jnp.stack([slot_entry(g, k) for g in groups.order for k in range(slots)])

    row_weight = 1048576.0 * live_rows / valid_count
    lane = lax.broadcasted_iota(jnp.int32, (chunk_rows, LANES), 1)

    grads = []
    for h in range(CHUNKS):
        blocks = ring.gather(turned[h])
        factor = row_factor[:, h * chunk_rows : (h + 1) * chunk_rows]
        keep, send = project(index, blocks, factor[:, :, None], gain, head_weight)
        summed = (keep + groups.swap(send)).reshape(groups.chips, chunk_rows, vocab_width)
        logits = summed[0]
        for d in range(1, groups.chips):
            logits = logits + groups.shift(summed[d], d)

        top = jnp.max(logits, axis=1)
        total = jnp.sum(jnp.exp(logits - top[:, None]), axis=1)
        met = ring.meet(jnp.stack([top, total]), merge_totals)
        scale = jnp.exp(top - met[0]) / met[1]
        draft_probs = jnp.exp(logits - top[:, None]) * scale[:, None]
        target_probs = (
            jnp.exp(chunk(targets, h) - chunk(target_top, h)[:, None])
            * chunk(target_scale, h)[:, None]
        )
        logit_grad = chunk(row_weight, h)[:, None] * (draft_probs - target_probs)
        logit_grad = lax.reduce_precision(logit_grad, 8, 7)
        dot_part = jnp.sum(logit_grad * logits, axis=1)
        dot_high = lax.reduce_precision(dot_part, 8, 7)
        dot_low = dot_part - dot_high
        lanes = jnp.where(lane == 2 * ring.position, dot_high[:, None], 0.0) + jnp.where(
            lane == 2 * ring.position + 1, dot_low[:, None], 0.0
        )
        message = jnp.concatenate([logit_grad.astype(BF16), lanes.astype(BF16)], axis=1)
        everyone = groups.gather(message).reshape(step_rows, vocab_width + LANES)
        normed_grad = jnp.dot(
            everyone[:, :vocab_width], head_weight, preferred_element_type=F32
        )
        dots = everyone[:, vocab_width:]

        def part(t):
            start = (ring.position + t + parts) % parts * piece_rows
            return jnp.concatenate(
                [
                    lax.dynamic_slice_in_dim(normed_grad, start, piece_rows, 0),
                    lax.dynamic_slice_in_dim(dots, start, piece_rows, 0).astype(F32),
                ],
                axis=1,
            )

        piece = ring.scatter_sum(part)
        start = ring.position * piece_rows
        group, first = start // chunk_rows, start % chunk_rows
        values = jnp.concatenate(
            [
                lax.dynamic_slice(
                    blocks, (index[group * slots + k], first, 0), (1, piece_rows, block_width)
                )[0]
                for k in range(slots)
            ],
            axis=1,
        ).astype(F32)
        piece_factor = lax.dynamic_slice(factor, (group, first), (1, piece_rows))[0]
        row_dot = jnp.sum(piece[:, slice_width:], axis=1) / piece_factor
        grad_piece = (
            piece_factor[:, None] * gain * piece[:, :slice_width]
            - values * (piece_factor**3 * row_dot / model_width)[:, None]
        ).astype(BF16)
        line = ring.gather(grad_piece)
        grads.append(ring.by_position(line).reshape(step_rows, slice_width))

    grad_all = jnp.concatenate(grads, axis=0)
    grad_joining = lax.dot_general(
        grad_all, chosen, (((0,), (0,)), ((), ())), preferred_element_type=F32
    )
    share_rows = group_rows // slots
    first = vocab_index * share_rows
    entry = groups.entry(first // group_rows)
    first = first % group_rows
    start = first // chunk_rows * step_rows + entry * chunk_rows + first % chunk_rows
    grad_share = lax.dynamic_slice_in_dim(grad_all, start, share_rows, 0)
    return (grad_share, grad_joining)


def solution(mesh):
    placed = (
        P("dp", "vocab"),
        P(),
        P("vocab", "dp"),
        P("dp", "vocab"),
        P("dp"),
        P("dp"),
        P("dp", "vocab"),
    )
    return jax.shard_map(
        body,
        mesh=mesh,
        in_specs=placed,
        out_specs=(P("vocab", "dp"), P("dp", "vocab")),
        check_vma=False,
    )
```

time: 437 us -> 228 us (0.52)
  waiting for transfers between devices: 307 us -> 53.5 us
  starting transfers between devices: 3.81 us -> 77 us
  blocking collectives: 52.1 us -> 0 us
  matrix products: 34.4 us -> 17.1 us
  Pallas kernels: 0 us -> 16.6 us
  local copies, waits for them, and re-layouts: 9.41 us -> 22.7 us
  between operations: 13.9 us -> 21.8 us
    psum x1 -> x0, waiting for transfers between devices: 152 us -> none  [body(): normed_grad = lax.psum(partial_grad, 'vocab')]
    all_gather x3 -> x0, waiting for transfers between devices: 88.9 us -> none  [the longest x1 54.3 us: body(): whole_rows = lax.all_gather(hidden, 'vocab', axis=1, tiled=True)]
    ppermute x0 -> x71, starting transfers between devices: none -> 77 us  [the longest x48 49.5 us: shift(): lax.ppermute(x, 'vocab', [(order[p], order[(p + step) % size]) for p in r...]
    ppermute x0 -> x71, waiting for transfers between devices: none -> 53.5 us  [the longest x6 25.2 us: shift(): lax.ppermute(x, 'dp', [(i, (i + CORES * step) % size) for i in range(size)])]
    reduce_scatter x1 -> x0, waiting for transfers between devices: 41 us -> none  [body(): lax.psum_scatter(row_logits(normed, head_weight), 'dp', scatter_dimension...]
    psum x3 -> x0, blocking collectives: 30.5 us -> none  [the longest x1 17.1 us: body(): lax.psum((jnp.sum(jnp.exp(logits - draft_max[:, None]), axis=1), jnp.sum(...]
    all_to_all x1 -> x0, waiting for transfers between devices: 24.3 us -> none  [body(): lax.all_to_all(whole_rows, 'dp', split_axis=1, concat_axis=0, tiled=True)]
    pmax x1 -> x0, blocking collectives: 21.6 us -> none  [body(): lax.pmax((jnp.max(logits, axis=1), jnp.max(targets, axis=1)), 'vocab')]
  transfers between devices with their start and end apart: 6 -> 71, of which waited for: 6 -> 32; matrix products, arithmetic and copies ran while one was open for 3% -> 13% of each run, Pallas kernels for 0% -> 7%
where the time goes in v2:
time: 228 us; the launch traced here: 227 us
  starting transfers between devices  77 us (34%)
  waiting for transfers between devices  53.5 us (23%)
  local copies, waits for them, and re-layouts  22.7 us (10%)
  between operations  21.8 us (10%)
  other arithmetic  18 us (8%)
  matrix products  17.1 us (8%)
  Pallas kernels  16.6 us (7%)
    ppermute x48, starting transfers between devices, shift(): lax.ppermute(x, 'vocab', [(order[p], order[(p + step) % size]) for p in r...  49.5 us
    ppermute x6, waiting for transfers between devices, shift(): lax.ppermute(x, 'dp', [(i, (i + CORES * step) % size) for i in range(size)])  25.2 us
    ppermute x48, waiting for transfers between devices, shift(): lax.ppermute(x, 'vocab', [(order[p], order[(p + step) % size]) for p in r...  20.5 us
    ppermute x9, starting transfers between devices, partner(): return lax.ppermute(x, 'vocab', [(v, v ^ bit) for v in range(self.size)])  19.3 us
    pallas_call x2, Pallas kernels, project(): pl.pallas_call(functools.partial(project_kernel, slots), grid_spec=pltpu....  16.6 us
    unnamed x100, local copies, waits for them, and re-layouts  14.5 us
    dot_general x1, matrix products, body(): lax.dot_general(grad_all, chosen, (((0,), (0,)), ((), ())), preferred_ele...  12.5 us
    ppermute x9, waiting for transfers between devices, partner(): return lax.ppermute(x, 'vocab', [(v, v ^ bit) for v in range(self.size)])  7.36 us
  transfers between devices with their start and end apart: 71, of which 32 were waited for; matrix products, arithmetic and copies ran while one was open for 13% of the time, Pallas kernels for 7%

profile of v2, /device:TPU:0, one launch (start us, length us, event | category | flops | bytes accessed | tf_op | source)
XLA Modules:
  0.0 226.8 jit_solution(6698336257530972788)
XLA Ops:
  3.5 2.3 %fusion.138 = (f32[128,2048]{1,0:T(8,128)}, bf16[128]{0:T(256)(128)(2,1)S(1)}) fusion(bf16[128,2048]{1,0:T(8,128)(2,1)} %param.21), kind=kLoop, calls=%fused_computation.343 | loop fusion | flops 524160 | bytes 1573120 | tf_op jit(solution)/shard_map/convert_element_type | solution.py:207
  6.2 3.0 %collective-permute-start = (f32[3,128]{1,0:T(4,128)S(1)}, f32[3,128]{1,0:T(4,128)S(1)}, u32[]{:S(2)}, u32[]{:S(2)}) collective-permute-start(f32[3,128]{1,0:T(4,128)S(1)} %pad_maximum_fusion.21), channel_id=1, source_target_pairs={{0,1},{1,0},{2,3},{3,2},{4,5},{5,4},{6,7},{7,6},{8,9},{9,8},{10,11... | collective-permute-start | bytes 4616 | tf_op jit(solution)/shard_map/ppermute | solution.py:47
  15.1 6.6 %collective-permute-start.1 = (f32[3,128]{1,0:T(4,128)S(1)}, f32[3,128]{1,0:T(4,128)S(1)}, u32[]{:S(2)}, u32[]{:S(2)}) collective-permute-start(f32[3,128]{1,0:T(4,128)S(1)} %pad_maximum_fusion.22), channel_id=1, source_target_pairs={{0,2},{1,3},{2,0},{3,1},{4,6},{5,7},{6,4},{7,5},{8,10},{9,11},{10,... | collective-permute-start | bytes 4616 | tf_op jit(solution)/shard_map/ppermute | solution.py:47
  24.2 4.3 %collective-permute-start.2 = (f32[3,128]{1,0:T(4,128)S(1)}, f32[3,128]{1,0:T(4,128)S(1)}, u32[]{:S(2)}, u32[]{:S(2)}) collective-permute-start(f32[3,128]{1,0:T(4,128)S(1)} %pad_maximum_fusion.23), channel_id=1, source_target_pairs={{0,4},{1,5},{2,6},{3,7},{4,0},{5,1},{6,2},{7,3},{8,12},{9,13},{10,... | collective-permute-start | bytes 4616 | tf_op jit(solution)/shard_map/ppermute | solution.py:47
  31.6 1.5 collective-permute-start.6
  40.5 1.9 gather_fusion
  42.6 1.4 collective-permute-start.69
  46.6 1.5 collective-permute-start.8
  48.8 1.6 collective-permute-done.39
  52.5 1.4 collective-permute-done.12
  57.2 2.0 collective-permute-start.45
  59.5 3.4 %copy-done.2 = bf16[2048,2048]{1,0:T(8,128)(2,1)S(1)} copy-done((bf16[2048,2048]{1,0:T(8,128)(2,1)S(1)}, bf16[2048,2048]{1,0:T(8,128)(2,1)}, u32[]{:S(2)}) %copy-start.2) | copy-done | bytes 8388632
  62.9 8.3 %shard_map.167 = (f32[128,2048]{1,0:T(8,128)S(1)}, f32[128,2048]{1,0:T(8,128)}) custom-call(s32[8]{0:T(128)S(1)} %stack.234.index_ref, bf16[8,64,1024]{2,1,0:T(8,128)(2,1)S(1)} %bitcast_dynamic-update-slice_fusion.21.blocks_ref, f32[4,64,1]{2,1,0:T(8,128)S(1)} %copy.26.factor_ref, f32[1,2048]{1,0:T(1,128)S(1)} %bitcast.378, bf16[2048,2048]{1,0:T(8,128)(2,1)S(1)} %copy-done.2), custom_call_target="tpu_custom_call" | custom-call | flops 2147483648 | bytes 11534336 | tf_op jit(solution)/shard_map/pallas_call | solution.py:156
  71.4 3.4 %copy-done.3 = bf16[2048,2048]{1,0:T(8,128)(2,1)S(1)} copy-done((bf16[2048,2048]{1,0:T(8,128)(2,1)S(1)}, bf16[2048,2048]{1,0:T(8,128)(2,1)}, u32[]{:S(2)}) %copy-start.3) | copy-done | bytes 8388632
  74.8 8.3 %shard_map.168 = (f32[128,2048]{1,0:T(8,128)S(1)}, f32[128,2048]{1,0:T(8,128)}) custom-call(s32[8]{0:T(128)S(1)} %stack.234.index_ref, bf16[8,64,1024]{2,1,0:T(8,128)(2,1)S(1)} %bitcast_dynamic-update-slice_fusion.7.blocks_ref, f32[4,64,1]{2,1,0:T(8,128)S(1)} %copy.27.factor_ref, f32[1,2048]{1,0:T(1,128)S(1)} %bitcast.379, bf16[2048,2048]{1,0:T(8,128)(2,1)S(1)} %copy-done.3), custom_call_target="tpu_custom_call" | custom-call | flops 2147483648 | bytes 11534336 | tf_op jit(solution)/shard_map/pallas_call | solution.py:156
  94.2 1.4 add.686
  97.6 1.3 add.743
  100.1 10.4 %collective-permute-done.15 = f32[64,2048]{1,0:T(8,128)S(1)} collective-permute-done((f32[64,2048]{1,0:T(8,128)S(1)}, f32[64,2048]{1,0:T(8,128)S(1)}, u32[]{:S(2)}, u32[]{:S(2)}) %collective-permute-start.15) | collective-permute-done | bytes 524320 | tf_op jit(solution)/shard_map/ppermute | solution.py:114
  111.9 8.9 %collective-permute-done.47 = f32[64,2048]{1,0:T(8,128)S(1)} collective-permute-done((f32[64,2048]{1,0:T(8,128)S(1)}, f32[64,2048]{1,0:T(8,128)S(1)}, u32[]{:S(2)}, u32[]{:S(2)}) %collective-permute-start.47) | collective-permute-done | bytes 524320 | tf_op jit(solution)/shard_map/ppermute | solution.py:114
  122.9 2.0 collective-permute-done.48
  127.0 1.5 collective-permute-done.49
  129.2 1.3 collective-permute-done.18
  130.5 2.6 %collective-permute-done.50 = f32[2,64]{1,0:T(2,128)S(1)} collective-permute-done((f32[2,64]{1,0:T(2,128)S(1)}, f32[2,64]{1,0:T(2,128)S(1)}, u32[]{:S(2)}, u32[]{:S(2)}) %collective-permute-start.50) | collective-permute-done | bytes 544 | tf_op jit(solution)/shard_map/ppermute | solution.py:47
  136.4 5.1 %collective-permute-done.19 = bf16[64,2176]{1,0:T(8,128)(2,1)S(1)} collective-permute-done((bf16[64,2176]{1,0:T(8,128)(2,1)S(1)}, bf16[64,2176]{1,0:T(8,128)(2,1)S(1)}, u32[]{:S(2)}, u32[]{:S(2)}) %collective-permute-start.19) | collective-permute-done | bytes 278560 | tf_op jit(solution)/shard_map/ppermute | solution.py:114
  141.7 1.7 pad_maximum_fusion.3
  144.9 2.3 %fusion.5 = f32[256,2048]{1,0:T(8,128)S(1)} fusion(bf16[2048,2048]{1,0:T(8,128)(2,1)S(1)} %bitcast.377, bf16[256,2176]{1,0:T(8,128)(2,1)S(1)} %bitcast.386), kind=kOutput, calls=%fused_computation.17 | convolution fusion | flops 2147483648 | bytes 11534336 | tf_op jit(solution)/shard_map/dot_general | solution.py:271
  147.8 2.3 %fusion.3 = f32[256,2048]{1,0:T(8,128)S(1)} fusion(bf16[2048,2048]{1,0:T(8,128)(2,1)S(1)} %bitcast.377, bf16[256,2176]{1,0:T(8,128)(2,1)S(1)} %bitcast.387), kind=kOutput, calls=%fused_computation.15 | convolution fusion | flops 2147483648 | bytes 11534336 | tf_op jit(solution)/shard_map/dot_general | solution.py:271
  150.6 1.2 collective-permute-start.21
  152.7 1.2 collective-permute-start.53
  155.1 1.2 collective-permute-start.22
  157.3 1.2 collective-permute-start.54
  159.5 2.1 collective-permute-done.22
  161.6 1.2 collective-permute-start.23
  164.6 1.2 collective-permute-start.55
  174.9 1.4 collective-permute-done.56
  176.3 1.6 collective-permute-done.60
  180.3 1.6 collective-permute-start.65
  182.3 1.6 collective-permute-start.33
  184.0 2.3 %collective-permute-done.61 = bf16[32,2048]{1,0:T(8,128)(2,1)S(1)} collective-permute-done((bf16[32,2048]{1,0:T(8,128)(2,1)S(1)}, bf16[32,2048]{1,0:T(8,128)(2,1)S(1)}, u32[]{:S(2)}, u32[]{:S(2)}) %collective-permute-start.61) | collective-permute-done | bytes 131104 | tf_op jit(solution)/shard_map/ppermute | solution.py:42
  186.7 1.6 collective-permute-start.66
  189.4 1.6 collective-permute-start.34
  191.0 1.4 collective-permute-done.62
  193.2 1.6 collective-permute-start.67
  195.9 1.6 collective-permute-start.35
  199.8 1.6 collective-permute-start.68
  201.3 1.7 pad_maximum_fusion
  203.6 1.6 collective-permute-start.36
  213.5 12.5 %fusion = f32[2048,3072]{1,0:T(8,128)} fusion(bf16[512,3072]{1,0:T(8,128)(2,1)S(1)} %bitcast.384, bf16[256,2048]{1,0:T(8,128)(2,1)S(1)} %bitcast.380, bf16[256,2048]{1,0:T(8,128)(2,1)S(1)} %bitcast.382), kind=kOutput, calls=%fused_computation.5 | convolution fusion | flops 6446645248 | bytes 30408704 | tf_op jit(solution)/shard_map/dot_general | solution.py:308
  (323 shorter events, 70.0 us)
Async XLA Ops:
  1.8 29.2 %collective-permute-start.5 = (bf16[64,1024]{1,0:T(8,128)(2,1)S(1)}, bf16[64,1024]{1,0:T(8,128)(2,1)S(1)}, u32[]{:S(2)}, u32[]{:S(2)}) collective-permute-start(bf16[64,1024]{1,0:T(8,128)(2,1)S(1)} %get-tuple-element.56), channel_id=1, source_target_pairs={{0,0},{1,1},{2,8},{3,9},{4,16},{5,17},{6,24},{7,25},{8,4},{9,5},{1... | collective-permute-start | bytes 393224 | tf_op jit(solution)/shard_map/ppermute | solution.py:204
  6.2 8.8 %collective-permute-start = (f32[3,128]{1,0:T(4,128)S(1)}, f32[3,128]{1,0:T(4,128)S(1)}, u32[]{:S(2)}, u32[]{:S(2)}) collective-permute-start(f32[3,128]{1,0:T(4,128)S(1)} %pad_maximum_fusion.21), channel_id=1, source_target_pairs={{0,1},{1,0},{2,3},{3,2},{4,5},{5,4},{6,7},{7,6},{8,9},{9,8},{10,11... | collective-permute-start | bytes 4616 | tf_op jit(solution)/shard_map/ppermute | solution.py:47
  9.3 25.1 %collective-permute-start.37 = (bf16[64,1024]{1,0:T(8,128)(2,1)S(1)}, bf16[64,1024]{1,0:T(8,128)(2,1)S(1)}, u32[]{:S(2)}, u32[]{:S(2)}) collective-permute-start(bf16[64,1024]{1,0:T(8,128)(2,1)S(1)} %get-tuple-element.55), channel_id=1, source_target_pairs={{0,0},{1,1},{2,8},{3,9},{4,16},{5,17},{6,24},{7,25},{8,4},{9,5},{1... | collective-permute-start | bytes 393224 | tf_op jit(solution)/shard_map/ppermute | solution.py:204
  15.1 9.0 %collective-permute-start.1 = (f32[3,128]{1,0:T(4,128)S(1)}, f32[3,128]{1,0:T(4,128)S(1)}, u32[]{:S(2)}, u32[]{:S(2)}) collective-permute-start(f32[3,128]{1,0:T(4,128)S(1)} %pad_maximum_fusion.22), channel_id=1, source_target_pairs={{0,2},{1,3},{2,0},{3,1},{4,6},{5,7},{6,4},{7,5},{8,10},{9,11},{10,... | collective-permute-start | bytes 4616 | tf_op jit(solution)/shard_map/ppermute | solution.py:47
  24.2 8.9 %collective-permute-start.2 = (f32[3,128]{1,0:T(4,128)S(1)}, f32[3,128]{1,0:T(4,128)S(1)}, u32[]{:S(2)}, u32[]{:S(2)}) collective-permute-start(f32[3,128]{1,0:T(4,128)S(1)} %pad_maximum_fusion.23), channel_id=1, source_target_pairs={{0,4},{1,5},{2,6},{3,7},{4,0},{5,1},{6,2},{7,3},{8,12},{9,13},{10,... | collective-permute-start | bytes 4616 | tf_op jit(solution)/shard_map/ppermute | solution.py:47
  31.0 6.1 %collective-permute-start.10 = (bf16[64,1024]{1,0:T(8,128)(2,1)S(1)}, bf16[64,1024]{1,0:T(8,128)(2,1)S(1)}, u32[]{:S(2)}, u32[]{:S(2)}) collective-permute-start(bf16[64,1024]{1,0:T(8,128)(2,1)S(1)} %collective-permute-done.5), channel_id=1, source_target_pairs={{0,1},{2,0},{4,2},{6,4},{7,6},{5,7},{3,5},{1,3},{8,9},{10,8},{12,1... | collective-permute-start | bytes 393224 | tf_op jit(solution)/shard_map/ppermute | solution.py:42
  31.6 6.4 %collective-permute-start.6 = (bf16[64,1024]{1,0:T(8,128)(2,1)S(1)}, bf16[64,1024]{1,0:T(8,128)(2,1)S(1)}, u32[]{:S(2)}, u32[]{:S(2)}) collective-permute-start(bf16[64,1024]{1,0:T(8,128)(2,1)S(1)} %collective-permute-done.5), channel_id=1, source_target_pairs={{0,2},{2,4},{4,6},{6,7},{7,5},{5,3},{3,1},{1,0},{8,10},{10,12},{12... | collective-permute-start | bytes 393224 | tf_op jit(solution)/shard_map/ppermute | solution.py:42
  33.1 6.0 %collective-permute-start.3 = (f32[2,128]{1,0:T(2,128)S(1)}, f32[2,128]{1,0:T(2,128)S(1)}, u32[]{:S(2)}, u32[]{:S(2)}) collective-permute-start(f32[2,128]{1,0:T(2,128)S(1)} %get-tuple-element.96), channel_id=1, source_target_pairs={{0,16},{8,24},{16,0},{24,8},{1,17},{9,25},{17,1},{25,9},{2,18},{10... | collective-permute-start | bytes 3080 | tf_op jit(solution)/shard_map/ppermute | solution.py:114
  34.3 9.7 %collective-permute-start.38 = (bf16[64,1024]{1,0:T(8,128)(2,1)S(1)}, bf16[64,1024]{1,0:T(8,128)(2,1)S(1)}, u32[]{:S(2)}, u32[]{:S(2)}) collective-permute-start(bf16[64,1024]{1,0:T(8,128)(2,1)S(1)} %collective-permute-done.37), channel_id=1, source_target_pairs={{0,2},{2,4},{4,6},{6,7},{7,5},{5,3},{3,1},{1,0},{8,10},{10,12},{12... | collective-permute-start | bytes 393224 | tf_op jit(solution)/shard_map/ppermute | solution.py:42
  35.5 9.7 %collective-permute-start.42 = (bf16[64,1024]{1,0:T(8,128)(2,1)S(1)}, bf16[64,1024]{1,0:T(8,128)(2,1)S(1)}, u32[]{:S(2)}, u32[]{:S(2)}) collective-permute-start(bf16[64,1024]{1,0:T(8,128)(2,1)S(1)} %collective-permute-done.37), channel_id=1, source_target_pairs={{0,1},{2,0},{4,2},{6,4},{7,6},{5,7},{3,5},{1,3},{8,9},{10,8},{12,1... | collective-permute-start | bytes 393224 | tf_op jit(solution)/shard_map/ppermute | solution.py:42
  37.1 9.0 %collective-permute-start.11 = (bf16[64,1024]{1,0:T(8,128)(2,1)S(1)}, bf16[64,1024]{1,0:T(8,128)(2,1)S(1)}, u32[]{:S(2)}, u32[]{:S(2)}) collective-permute-start(bf16[64,1024]{1,0:T(8,128)(2,1)S(1)} %collective-permute-done.10), channel_id=1, source_target_pairs={{0,1},{2,0},{4,2},{6,4},{7,6},{5,7},{3,5},{1,3},{8,9},{10,8},{12,1... | collective-permute-start | bytes 393224 | tf_op jit(solution)/shard_map/ppermute | solution.py:42
  37.9 8.7 %collective-permute-start.7 = (bf16[64,1024]{1,0:T(8,128)(2,1)S(1)}, bf16[64,1024]{1,0:T(8,128)(2,1)S(1)}, u32[]{:S(2)}, u32[]{:S(2)}) collective-permute-start(bf16[64,1024]{1,0:T(8,128)(2,1)S(1)} %collective-permute-done.6), channel_id=1, source_target_pairs={{0,2},{2,4},{4,6},{6,7},{7,5},{5,3},{3,1},{1,0},{8,10},{10,12},{12... | collective-permute-start | bytes 393224 | tf_op jit(solution)/shard_map/ppermute | solution.py:42
  42.6 99.1 %collective-permute-start.69 = (bf16[2,64,3072]{2,1,0:T(8,128)(2,1)}, bf16[2,64,3072]{2,1,0:T(8,128)(2,1)}, u32[]{:S(2)}, u32[]{:S(2)}) collective-permute-start(bf16[2,64,3072]{2,1,0:T(8,128)(2,1)} %bitcast.109), channel_id=1, source_target_pairs={{0,16},{8,24},{16,0},{24,8},{1,17},{9,25},{17,1},{25,9},{2,18},{10... | collective-permute-start | bytes 2359304 | tf_op jit(solution)/shard_map/ppermute | solution.py:114
  44.0 6.4 %collective-permute-start.39 = (bf16[64,1024]{1,0:T(8,128)(2,1)S(1)}, bf16[64,1024]{1,0:T(8,128)(2,1)S(1)}, u32[]{:S(2)}, u32[]{:S(2)}) collective-permute-start(bf16[64,1024]{1,0:T(8,128)(2,1)S(1)} %collective-permute-done.38), channel_id=1, source_target_pairs={{0,2},{2,4},{4,6},{6,7},{7,5},{5,3},{3,1},{1,0},{8,10},{10,12},{12... | collective-permute-start | bytes 393224 | tf_op jit(solution)/shard_map/ppermute | solution.py:42
  45.2 6.4 %collective-permute-start.43 = (bf16[64,1024]{1,0:T(8,128)(2,1)S(1)}, bf16[64,1024]{1,0:T(8,128)(2,1)S(1)}, u32[]{:S(2)}, u32[]{:S(2)}) collective-permute-start(bf16[64,1024]{1,0:T(8,128)(2,1)S(1)} %collective-permute-done.42), channel_id=1, source_target_pairs={{0,1},{2,0},{4,2},{6,4},{7,6},{5,7},{3,5},{1,3},{8,9},{10,8},{12,1... | collective-permute-start | bytes 393224 | tf_op jit(solution)/shard_map/ppermute | solution.py:42
  46.1 7.8 %collective-permute-start.12 = (bf16[64,1024]{1,0:T(8,128)(2,1)S(1)}, bf16[64,1024]{1,0:T(8,128)(2,1)S(1)}, u32[]{:S(2)}, u32[]{:S(2)}) collective-permute-start(bf16[64,1024]{1,0:T(8,128)(2,1)S(1)} %collective-permute-done.11), channel_id=1, source_target_pairs={{0,1},{2,0},{4,2},{6,4},{7,6},{5,7},{3,5},{1,3},{8,9},{10,8},{12,1... | collective-permute-start | bytes 393224 | tf_op jit(solution)/shard_map/ppermute | solution.py:42
  46.6 8.2 %collective-permute-start.8 = (bf16[64,1024]{1,0:T(8,128)(2,1)S(1)}, bf16[64,1024]{1,0:T(8,128)(2,1)S(1)}, u32[]{:S(2)}, u32[]{:S(2)}) collective-permute-start(bf16[64,1024]{1,0:T(8,128)(2,1)S(1)} %collective-permute-done.7), channel_id=1, source_target_pairs={{0,2},{2,4},{4,6},{6,7},{7,5},{5,3},{3,1},{1,0},{8,10},{10,12},{12... | collective-permute-start | bytes 393224 | tf_op jit(solution)/shard_map/ppermute | solution.py:42
  50.4 6.5 %collective-permute-start.40 = (bf16[64,1024]{1,0:T(8,128)(2,1)S(1)}, bf16[64,1024]{1,0:T(8,128)(2,1)S(1)}, u32[]{:S(2)}, u32[]{:S(2)}) collective-permute-start(bf16[64,1024]{1,0:T(8,128)(2,1)S(1)} %collective-permute-done.39), channel_id=1, source_target_pairs={{0,2},{2,4},{4,6},{6,7},{7,5},{5,3},{3,1},{1,0},{8,10},{10,12},{12... | collective-permute-start | bytes 393224 | tf_op jit(solution)/shard_map/ppermute | solution.py:42
  57.0 14.2 %collective-permute-start.41 = (bf16[32,1024]{1,0:T(8,128)(2,1)S(1)}, bf16[32,1024]{1,0:T(8,128)(2,1)S(1)}, u32[]{:S(2)}, u32[]{:S(2)}) collective-permute-start(bf16[32,1024]{1,0:T(8,128)(2,1)S(1)} %slice.306), channel_id=1, source_target_pairs={{0,2},{2,4},{4,6},{6,7},{7,5},{5,3},{3,1},{1,0},{8,10},{10,12},{12... | collective-permute-start | bytes 196616 | tf_op jit(solution)/shard_map/ppermute | solution.py:42
  57.2 14.0 %collective-permute-start.45 = (bf16[32,1024]{1,0:T(8,128)(2,1)S(1)}, bf16[32,1024]{1,0:T(8,128)(2,1)S(1)}, u32[]{:S(2)}, u32[]{:S(2)}) collective-permute-start(bf16[32,1024]{1,0:T(8,128)(2,1)S(1)} %slice.307), channel_id=1, source_target_pairs={{0,1},{2,0},{4,2},{6,4},{7,6},{5,7},{3,5},{1,3},{8,9},{10,8},{12,1... | collective-permute-start | bytes 196616 | tf_op jit(solution)/shard_map/ppermute | solution.py:42
  71.2 23.0 %collective-permute-start.14 = (f32[128,2048]{1,0:T(8,128)}, f32[128,2048]{1,0:T(8,128)}, u32[]{:S(2)}, u32[]{:S(2)}) collective-permute-start(f32[128,2048]{1,0:T(8,128)} %get-tuple-element.8), channel_id=1, source_target_pairs={{0,8},{8,0},{16,24},{24,16},{1,9},{9,1},{17,25},{25,17},{2,10},{10... | collective-permute-start | bytes 3145736 | tf_op jit(solution)/shard_map/ppermute | solution.py:110
  84.1 13.4 %collective-permute-start.46 = (f32[128,2048]{1,0:T(8,128)}, f32[128,2048]{1,0:T(8,128)}, u32[]{:S(2)}, u32[]{:S(2)}) collective-permute-start(f32[128,2048]{1,0:T(8,128)} %get-tuple-element.10), channel_id=1, source_target_pairs={{0,8},{8,0},{16,24},{24,16},{1,9},{9,1},{17,25},{25,17},{2,10},{10... | collective-permute-start | bytes 3145736 | tf_op jit(solution)/shard_map/ppermute | solution.py:110
  95.7 14.9 %collective-permute-start.15 = (f32[64,2048]{1,0:T(8,128)S(1)}, f32[64,2048]{1,0:T(8,128)S(1)}, u32[]{:S(2)}, u32[]{:S(2)}) collective-permute-start(f32[64,2048]{1,0:T(8,128)S(1)} %slice.292), channel_id=1, source_target_pairs={{0,16},{8,24},{16,0},{24,8},{1,17},{9,25},{17,1},{25,9},{2,18},{10... | collective-permute-start | bytes 1572872 | tf_op jit(solution)/shard_map/ppermute | solution.py:114
  99.0 21.9 %collective-permute-start.47 = (f32[64,2048]{1,0:T(8,128)S(1)}, f32[64,2048]{1,0:T(8,128)S(1)}, u32[]{:S(2)}, u32[]{:S(2)}) collective-permute-start(f32[64,2048]{1,0:T(8,128)S(1)} %slice.309), channel_id=1, source_target_pairs={{0,16},{8,24},{16,0},{24,8},{1,17},{9,25},{17,1},{25,9},{2,18},{10... | collective-permute-start | bytes 1572872 | tf_op jit(solution)/shard_map/ppermute | solution.py:114
  111.0 11.3 %collective-permute-start.16 = (f32[2,64]{1,0:T(2,128)S(1)}, f32[2,64]{1,0:T(2,128)S(1)}, u32[]{:S(2)}, u32[]{:S(2)}) collective-permute-start(f32[2,64]{1,0:T(2,128)S(1)} %pad_maximum_fusion.26), channel_id=1, source_target_pairs={{0,1},{1,0},{2,3},{3,2},{4,5},{5,4},{6,7},{7,6},{8,9},{9,8},{10,11... | collective-permute-start | bytes 1544 | tf_op jit(solution)/shard_map/ppermute | solution.py:47
  134.2 7.3 %collective-permute-start.19 = (bf16[64,2176]{1,0:T(8,128)(2,1)S(1)}, bf16[64,2176]{1,0:T(8,128)(2,1)S(1)}, u32[]{:S(2)}, u32[]{:S(2)}) collective-permute-start(bf16[64,2176]{1,0:T(8,128)(2,1)S(1)} %get-tuple-element.54), channel_id=1, source_target_pairs={{0,16},{8,24},{16,0},{24,8},{1,17},{9,25},{17,1},{25,9},{2,18},{10... | collective-permute-start | bytes 835592 | tf_op jit(solution)/shard_map/ppermute | solution.py:114
  135.3 9.2 %collective-permute-start.51 = (bf16[64,2176]{1,0:T(8,128)(2,1)S(1)}, bf16[64,2176]{1,0:T(8,128)(2,1)S(1)}, u32[]{:S(2)}, u32[]{:S(2)}) collective-permute-start(bf16[64,2176]{1,0:T(8,128)(2,1)S(1)} %get-tuple-element.52), channel_id=1, source_target_pairs={{0,16},{8,24},{16,0},{24,8},{1,17},{9,25},{17,1},{25,9},{2,18},{10... | collective-permute-start | bytes 835592 | tf_op jit(solution)/shard_map/ppermute | solution.py:114
  143.4 57.9 %collective-permute-start.70 = (bf16[2,2,64,3072]{3,2,0,1:T(8,128)(2,1)S(1)}, bf16[2,2,64,3072]{3,2,0,1:T(8,128)(2,1)S(1)}, u32[]{:S(2)}, u32[]{:S(2)}) collective-permute-start(bf16[2,2,64,3072]{3,2,0,1:T(8,128)(2,1)S(1)} %pad_maximum_fusion.3), channel_id=1, source_target_pairs={{0,8},{8,0},{16,24},{24,16},{1,9},{9,1},{17,25},{25,17},{2,10},{10... | collective-permute-start | bytes 4718600 | tf_op jit(solution)/shard_map/ppermute | solution.py:110
  155.1 6.5 %collective-permute-start.22 = (bf16[32,2176]{1,0:T(8,128)(2,1)S(1)}, bf16[32,2176]{1,0:T(8,128)(2,1)S(1)}, u32[]{:S(2)}, u32[]{:S(2)}) collective-permute-start(bf16[32,2176]{1,0:T(8,128)(2,1)S(1)} %pad_maximum_fusion.14), channel_id=1, source_target_pairs={{0,2},{2,4},{4,6},{6,7},{7,5},{5,3},{3,1},{1,0},{8,10},{10,12},{12... | collective-permute-start | bytes 417800 | tf_op jit(solution)/shard_map/ppermute | solution.py:42
  156.4 6.6 %collective-permute-start.26 = (bf16[32,2176]{1,0:T(8,128)(2,1)S(1)}, bf16[32,2176]{1,0:T(8,128)(2,1)S(1)}, u32[]{:S(2)}, u32[]{:S(2)}) collective-permute-start(bf16[32,2176]{1,0:T(8,128)(2,1)S(1)} %pad_maximum_fusion.15), channel_id=1, source_target_pairs={{0,1},{2,0},{4,2},{6,4},{7,6},{5,7},{3,5},{1,3},{8,9},{10,8},{12,1... | collective-permute-start | bytes 417800 | tf_op jit(solution)/shard_map/ppermute | solution.py:42
  157.3 7.3 %collective-permute-start.54 = (bf16[32,2176]{1,0:T(8,128)(2,1)S(1)}, bf16[32,2176]{1,0:T(8,128)(2,1)S(1)}, u32[]{:S(2)}, u32[]{:S(2)}) collective-permute-start(bf16[32,2176]{1,0:T(8,128)(2,1)S(1)} %pad_maximum_fusion.16), channel_id=1, source_target_pairs={{0,2},{2,4},{4,6},{6,7},{7,5},{5,3},{3,1},{1,0},{8,10},{10,12},{12... | collective-permute-start | bytes 417800 | tf_op jit(solution)/shard_map/ppermute | solution.py:42
  158.6 7.4 %collective-permute-start.58 = (bf16[32,2176]{1,0:T(8,128)(2,1)S(1)}, bf16[32,2176]{1,0:T(8,128)(2,1)S(1)}, u32[]{:S(2)}, u32[]{:S(2)}) collective-permute-start(bf16[32,2176]{1,0:T(8,128)(2,1)S(1)} %pad_maximum_fusion.17), channel_id=1, source_target_pairs={{0,1},{2,0},{4,2},{6,4},{7,6},{5,7},{3,5},{1,3},{8,9},{10,8},{12,1... | collective-permute-start | bytes 417800 | tf_op jit(solution)/shard_map/ppermute | solution.py:42
  161.6 6.2 %collective-permute-start.23 = (bf16[32,2176]{1,0:T(8,128)(2,1)S(1)}, bf16[32,2176]{1,0:T(8,128)(2,1)S(1)}, u32[]{:S(2)}, u32[]{:S(2)}) collective-permute-start(bf16[32,2176]{1,0:T(8,128)(2,1)S(1)} %fusion.21), channel_id=1, source_target_pairs={{0,2},{2,4},{4,6},{6,7},{7,5},{5,3},{3,1},{1,0},{8,10},{10,12},{12... | collective-permute-start | bytes 417800 | tf_op jit(solution)/shard_map/ppermute | solution.py:42
  163.0 6.1 %collective-permute-start.27 = (bf16[32,2176]{1,0:T(8,128)(2,1)S(1)}, bf16[32,2176]{1,0:T(8,128)(2,1)S(1)}, u32[]{:S(2)}, u32[]{:S(2)}) collective-permute-start(bf16[32,2176]{1,0:T(8,128)(2,1)S(1)} %fusion.23), channel_id=1, source_target_pairs={{0,1},{2,0},{4,2},{6,4},{7,6},{5,7},{3,5},{1,3},{8,9},{10,8},{12,1... | collective-permute-start | bytes 417800 | tf_op jit(solution)/shard_map/ppermute | solution.py:42
  164.6 6.5 %collective-permute-start.55 = (bf16[32,2176]{1,0:T(8,128)(2,1)S(1)}, bf16[32,2176]{1,0:T(8,128)(2,1)S(1)}, u32[]{:S(2)}, u32[]{:S(2)}) collective-permute-start(bf16[32,2176]{1,0:T(8,128)(2,1)S(1)} %fusion.26), channel_id=1, source_target_pairs={{0,2},{2,4},{4,6},{6,7},{7,5},{5,3},{3,1},{1,0},{8,10},{10,12},{12... | collective-permute-start | bytes 417800 | tf_op jit(solution)/shard_map/ppermute | solution.py:42
  166.0 6.5 %collective-permute-start.59 = (bf16[32,2176]{1,0:T(8,128)(2,1)S(1)}, bf16[32,2176]{1,0:T(8,128)(2,1)S(1)}, u32[]{:S(2)}, u32[]{:S(2)}) collective-permute-start(bf16[32,2176]{1,0:T(8,128)(2,1)S(1)} %fusion.28), channel_id=1, source_target_pairs={{0,1},{2,0},{4,2},{6,4},{7,6},{5,7},{3,5},{1,3},{8,9},{10,8},{12,1... | collective-permute-start | bytes 417800 | tf_op jit(solution)/shard_map/ppermute | solution.py:42
  179.8 6.4 %collective-permute-start.61 = (bf16[32,2048]{1,0:T(8,128)(2,1)S(1)}, bf16[32,2048]{1,0:T(8,128)(2,1)S(1)}, u32[]{:S(2)}, u32[]{:S(2)}) collective-permute-start(bf16[32,2048]{1,0:T(8,128)(2,1)S(1)} %get-tuple-element.77), channel_id=1, source_target_pairs={{0,2},{2,4},{4,6},{6,7},{7,5},{5,3},{3,1},{1,0},{8,10},{10,12},{12... | collective-permute-start | bytes 393224 | tf_op jit(solution)/shard_map/ppermute | solution.py:42
  180.3 6.4 %collective-permute-start.65 = (bf16[32,2048]{1,0:T(8,128)(2,1)S(1)}, bf16[32,2048]{1,0:T(8,128)(2,1)S(1)}, u32[]{:S(2)}, u32[]{:S(2)}) collective-permute-start(bf16[32,2048]{1,0:T(8,128)(2,1)S(1)} %get-tuple-element.77), channel_id=1, source_target_pairs={{0,1},{2,0},{4,2},{6,4},{7,6},{5,7},{3,5},{1,3},{8,9},{10,8},{12,1... | collective-permute-start | bytes 393224 | tf_op jit(solution)/shard_map/ppermute | solution.py:42
  181.9 7.1 %collective-permute-start.29 = (bf16[32,2048]{1,0:T(8,128)(2,1)S(1)}, bf16[32,2048]{1,0:T(8,128)(2,1)}, u32[]{:S(2)}, u32[]{:S(2)}) collective-permute-start(bf16[32,2048]{1,0:T(8,128)(2,1)S(1)} %get-tuple-element.78), channel_id=1, source_target_pairs={{0,2},{2,4},{4,6},{6,7},{7,5},{5,3},{3,1},{1,0},{8,10},{10,12},{12... | collective-permute-start | bytes 393224 | tf_op jit(solution)/shard_map/ppermute | solution.py:42
  182.3 7.1 %collective-permute-start.33 = (bf16[32,2048]{1,0:T(8,128)(2,1)S(1)}, bf16[32,2048]{1,0:T(8,128)(2,1)}, u32[]{:S(2)}, u32[]{:S(2)}) collective-permute-start(bf16[32,2048]{1,0:T(8,128)(2,1)S(1)} %get-tuple-element.78), channel_id=1, source_target_pairs={{0,1},{2,0},{4,2},{6,4},{7,6},{5,7},{3,5},{1,3},{8,9},{10,8},{12,1... | collective-permute-start | bytes 393224 | tf_op jit(solution)/shard_map/ppermute | solution.py:42
  186.3 6.2 %collective-permute-start.62 = (bf16[32,2048]{1,0:T(8,128)(2,1)S(1)}, bf16[32,2048]{1,0:T(8,128)(2,1)}, u32[]{:S(2)}, u32[]{:S(2)}) collective-permute-start(bf16[32,2048]{1,0:T(8,128)(2,1)S(1)} %collective-permute-done.61), channel_id=1, source_target_pairs={{0,2},{2,4},{4,6},{6,7},{7,5},{5,3},{3,1},{1,0},{8,10},{10,12},{12... | collective-permute-start | bytes 393224 | tf_op jit(solution)/shard_map/ppermute | solution.py:42
  186.7 6.5 %collective-permute-start.66 = (bf16[32,2048]{1,0:T(8,128)(2,1)S(1)}, bf16[32,2048]{1,0:T(8,128)(2,1)}, u32[]{:S(2)}, u32[]{:S(2)}) collective-permute-start(bf16[32,2048]{1,0:T(8,128)(2,1)S(1)} %collective-permute-done.65), channel_id=1, source_target_pairs={{0,1},{2,0},{4,2},{6,4},{7,6},{5,7},{3,5},{1,3},{8,9},{10,8},{12,1... | collective-permute-start | bytes 393224 | tf_op jit(solution)/shard_map/ppermute | solution.py:42
  189.0 6.5 %collective-permute-start.30 = (bf16[32,2048]{1,0:T(8,128)(2,1)}, bf16[32,2048]{1,0:T(8,128)(2,1)}, u32[]{:S(2)}, u32[]{:S(2)}) collective-permute-start(bf16[32,2048]{1,0:T(8,128)(2,1)} %collective-permute-done.29), channel_id=1, source_target_pairs={{0,2},{2,4},{4,6},{6,7},{7,5},{5,3},{3,1},{1,0},{8,10},{10,12},{12... | collective-permute-start | bytes 393224 | tf_op jit(solution)/shard_map/ppermute | solution.py:42
  189.4 6.5 %collective-permute-start.34 = (bf16[32,2048]{1,0:T(8,128)(2,1)}, bf16[32,2048]{1,0:T(8,128)(2,1)}, u32[]{:S(2)}, u32[]{:S(2)}) collective-permute-start(bf16[32,2048]{1,0:T(8,128)(2,1)} %collective-permute-done.33), channel_id=1, source_target_pairs={{0,1},{2,0},{4,2},{6,4},{7,6},{5,7},{3,5},{1,3},{8,9},{10,8},{12,1... | collective-permute-start | bytes 393224 | tf_op jit(solution)/shard_map/ppermute | solution.py:42
  193.2 6.6 %collective-permute-start.67 = (bf16[32,2048]{1,0:T(8,128)(2,1)}, bf16[32,2048]{1,0:T(8,128)(2,1)S(1)}, u32[]{:S(2)}, u32[]{:S(2)}) collective-permute-start(bf16[32,2048]{1,0:T(8,128)(2,1)} %collective-permute-done.66), channel_id=1, source_target_pairs={{0,1},{2,0},{4,2},{6,4},{7,6},{5,7},{3,5},{1,3},{8,9},{10,8},{12,1... | collective-permute-start | bytes 393224 | tf_op jit(solution)/shard_map/ppermute | solution.py:42
  195.5 7.6 %collective-permute-start.31 = (bf16[32,2048]{1,0:T(8,128)(2,1)}, bf16[32,2048]{1,0:T(8,128)(2,1)S(1)}, u32[]{:S(2)}, u32[]{:S(2)}) collective-permute-start(bf16[32,2048]{1,0:T(8,128)(2,1)} %collective-permute-done.30), channel_id=1, source_target_pairs={{0,2},{2,4},{4,6},{6,7},{7,5},{5,3},{3,1},{1,0},{8,10},{10,12},{12... | collective-permute-start | bytes 393224 | tf_op jit(solution)/shard_map/ppermute | solution.py:42
  195.9 7.7 %collective-permute-start.35 = (bf16[32,2048]{1,0:T(8,128)(2,1)}, bf16[32,2048]{1,0:T(8,128)(2,1)S(1)}, u32[]{:S(2)}, u32[]{:S(2)}) collective-permute-start(bf16[32,2048]{1,0:T(8,128)(2,1)} %collective-permute-done.34), channel_id=1, source_target_pairs={{0,1},{2,0},{4,2},{6,4},{7,6},{5,7},{3,5},{1,3},{8,9},{10,8},{12,1... | collective-permute-start | bytes 393224 | tf_op jit(solution)/shard_map/ppermute | solution.py:42
  199.2 6.0 %collective-permute-start.64 = (bf16[16,2048]{1,0:T(8,128)(2,1)S(1)}, bf16[16,2048]{1,0:T(8,128)(2,1)S(1)}, u32[]{:S(2)}, u32[]{:S(2)}) collective-permute-start(bf16[16,2048]{1,0:T(8,128)(2,1)S(1)} %slice.321), channel_id=1, source_target_pairs={{0,2},{2,4},{4,6},{6,7},{7,5},{5,3},{3,1},{1,0},{8,10},{10,12},{12... | collective-permute-start | bytes 196616 | tf_op jit(solution)/shard_map/ppermute | solution.py:42
  (61 other events, 602.7 us)

commit v3 on v2

--- a/solution.py
+++ b/solution.py
@@ -56,9 +56,12 @@
     def entry(self, position):
         return (position - self.position + self.half + self.size) % self.size
 
-    def gather(self, block):
+    def gather(self, block, waits=None):
         ahead, behind = [block], [block]
-        for _ in range(self.half - 1):
+        for step in range(self.half - 1):
+            if waits and step in waits:
+                others = waits[step]()
+                ahead[-1], behind[-1] = after(ahead[-1], others), after(behind[-1], others)
             ahead.append(self.shift(ahead[-1], 1))
             behind.append(self.shift(behind[-1], -1))
         cut = block.shape[0] // 2
@@ -118,63 +121,39 @@
         return jnp.concatenate([mine, self.swap(mine)], axis=0)
 
 
-def project_kernel(slots, index_ref, blocks_ref, factor_ref, gain_ref, weight_ref, keep_ref, send_ref, normed_ref):
+def normalise_kernel(slots, index_ref, blocks_ref, factor_ref, gain_ref, normed_ref):
     rows, width = blocks_ref.shape[1:]
-    groups = factor_ref.shape[0]
-    half = groups // CORES * rows
-
-    @pl.when(pl.program_id(0) == 0)
-    def _():
-        for g in range(groups):
-            factor = factor_ref[g]
-            for k in range(slots):
-                columns = pl.ds(k * width, width)
-                values = blocks_ref[index_ref[g * slots + k]].astype(F32)
-                normed_ref[pl.ds(g * rows, rows), columns] = (
-                    values * factor * gain_ref[:, columns]
-                ).astype(BF16)
-
-    for ref, start in ((keep_ref, 0), (send_ref, half)):
-        ref[...] = lax.dot_general(
-            normed_ref[pl.ds(start, half), :],
-            weight_ref[...],
-            (((1,), (1,)), ((), ())),
-            preferred_element_type=F32,
-        )
-
-
-def project(index, blocks, factor, gain, weight):
-    count, rows, width = blocks.shape
+    for g in range(factor_ref.shape[0]):
+        factor = factor_ref[g]
+        for k in range(slots):
+            columns = pl.ds(k * width, width)
+            values = blocks_ref[index_ref[g * slots + k]].astype(F32)
+            normed_ref[pl.ds(g * rows, rows), columns] = (
+                values * factor * gain_ref[:, columns]
+            ).astype(BF16)
+
+
+def normalise(index, blocks, factor, gain):
+    rows = blocks.shape[1]
     groups = factor.shape[0]
-    vocab, depth = weight.shape
-    slots = depth // width
-    tile = min(vocab, 256)
-    all_rows = groups * rows
-    half = all_rows // CORES
-    out = jax.ShapeDtypeStruct((half, vocab), F32)
-    whole = lambda shape: pl.BlockSpec(shape, lambda n, index: (0,) * len(shape))
+    depth = gain.shape[1]
+    whole = pl.BlockSpec(memory_space=pltpu.VMEM)
     return pl.pallas_call(
-        functools.partial(project_kernel, slots),
-        grid_spec=pltpu.PrefetchScalarGridSpec(
-            num_scalar_prefetch=1,
-            grid=(vocab // tile,),
-            in_specs=[
-                whole(blocks.shape),
-                whole(factor.shape),
-                whole(gain.shape),
-                pl.BlockSpec((tile, depth), lambda n, index: (n, 0)),
-            ],
-            out_specs=[pl.BlockSpec((half, tile), lambda n, index: (0, n))] * 2,
-            scratch_shapes=[pltpu.VMEM((all_rows, depth), BF16)],
-        ),
-        out_shape=[out, out],
-        compiler_params=pltpu.CompilerParams(vmem_limit_bytes=24 * 2**20),
+        functools.partial(normalise_kernel, depth // blocks.shape[2]),
+        in_specs=[pl.BlockSpec(memory_space=pltpu.SMEM), whole, whole, whole],
+        out_specs=whole,
+        out_shape=jax.ShapeDtypeStruct((groups * rows, depth), BF16),
+        compiler_params=pltpu.CompilerParams(vmem_limit_bytes=12 * 2**20),
         cost_estimate=pl.CostEstimate(
-            flops=2 * all_rows * depth * vocab,
-            bytes_accessed=vocab * depth * 2 + all_rows * (depth * 2 + vocab * 4),
+            flops=3 * groups * rows * depth,
+            bytes_accessed=4 * groups * rows * depth,
             transcendentals=0,
         ),
-    )(index, blocks, factor, gain, weight)
+    )(index, blocks, factor, gain)
+
+
+def after(x, *others):
+    return lax.optimization_barrier((x, others))[0]
 
 
 def body(hidden, norm_gain, head_weight, target_logits, valid_rows, parents, features):
@@ -239,16 +218,41 @@
     row_weight = 1048576.0 * live_rows / valid_count
     lane = lax.broadcasted_iota(jnp.int32, (chunk_rows, LANES), 1)
 
-    grads = []
-    for h in range(CHUNKS):
-        blocks = ring.gather(turned[h])
+    def group_logits(h, blocks):
         factor = row_factor[:, h * chunk_rows : (h + 1) * chunk_rows]
-        keep, send = project(index, blocks, factor[:, :, None], gain, head_weight)
-        summed = (keep + groups.swap(send)).reshape(groups.chips, chunk_rows, vocab_width)
+        normed = normalise(index, blocks, factor[:, :, None], gain)
+        own = lax.dot_general(
+            normed, head_weight, (((1,), (1,)), ((), ())), preferred_element_type=F32
+        )
+        yield own
+        half = step_rows // CORES
+        summed = own[:half] + groups.swap(own[half:])
+        yield summed
+        summed = summed.reshape(groups.chips, chunk_rows, vocab_width)
         logits = summed[0]
         for d in range(1, groups.chips):
             logits = logits + groups.shift(summed[d], d)
-
+        yield logits
+
+    gathered, logits_of = [], []
+    for h in range(CHUNKS):
+        waits = None
+        if h > 0:
+            stages = group_logits(h - 1, gathered[-1])
+            waits = {
+                0: lambda: (gathered[-1],),
+                1: lambda: (next(stages),),
+                2: lambda: (next(stages),),
+            }
+        gathered.append(ring.gather(turned[h], waits))
+        if h > 0:
+            logits_of.append(list(stages)[-1])
+    logits_of.append(list(group_logits(CHUNKS - 1, gathered[-1]))[-1])
+
+    grads = []
+    for h in range(CHUNKS):
+        blocks, logits = gathered[h], logits_of[h]
+        factor = row_factor[:, h * chunk_rows : (h + 1) * chunk_rows]
         top = jnp.max(logits, axis=1)
         total = jnp.sum(jnp.exp(logits - top[:, None]), axis=1)
         met = ring.meet(jnp.stack([top, total]), merge_totals)

time: 228 us -> 227 us (level)
  Pallas kernels: 16.6 us -> 1.7 us
  matrix products: 17.1 us -> 28.8 us
  starting transfers between devices: 77 us -> 84.7 us
  waiting for transfers between devices: 53.5 us -> 50.2 us
  local copies, waits for them, and re-layouts: 22.7 us -> 19.6 us
    pallas_call x2, Pallas kernels: 16.6 us -> 1.7 us  [normalise(): pl.pallas_call(functools.partial(normalise_kernel, depth // blocks.shape[...]
    dot_general x0 -> x2, matrix products: none -> 11.5 us  [group_logits(): lax.dot_general(normed, head_weight, (((1,), (1,)), ((), ())), preferred_...]
    ppermute x48, starting transfers between devices: 49.5 us -> 58.3 us  [shift(): lax.ppermute(x, 'vocab', [(order[p], order[(p + step) % size]) for p in r...]
    ppermute x6, waiting for transfers between devices: 25.2 us -> 16.6 us  [shift(): lax.ppermute(x, 'dp', [(i, (i + CORES * step) % size) for i in range(size)])]
    unnamed x100 -> x76, local copies, waits for them, and re-layouts: 14.5 us -> 8.09 us
    ppermute x9, starting transfers between devices: 19.3 us -> 15.2 us  [partner(): return lax.ppermute(x, 'vocab', [(v, v ^ bit) for v in range(self.size)])]
    ppermute x6, starting transfers between devices: 5.81 us -> 9.16 us  [shift(): lax.ppermute(x, 'dp', [(i, (i + CORES * step) % size) for i in range(size)])]
    ppermute x9, waiting for transfers between devices: 7.36 us -> 9.84 us  [partner(): return lax.ppermute(x, 'vocab', [(v, v ^ bit) for v in range(self.size)])]
  transfers between devices with their start and end apart: 71 -> 71, of which waited for: 32 -> 34; matrix products, arithmetic and copies ran while one was open for 13% -> 18% of each run, Pallas kernels for 7% -> 0%
where the time goes in v3:
time: 227 us; the launch traced here: 225 us
  starting transfers between devices  84.7 us (37%)
  waiting for transfers between devices  50.2 us (22%)
  matrix products  28.8 us (13%)
  between operations  21.1 us (9%)
  local copies, waits for them, and re-layouts  19.6 us (9%)
  other arithmetic  19.2 us (8%)
    ppermute x48, starting transfers between devices, shift(): lax.ppermute(x, 'vocab', [(order[p], order[(p + step) % size]) for p in r...  58.3 us
    ppermute x48, waiting for transfers between devices, shift(): lax.ppermute(x, 'vocab', [(order[p], order[(p + step) % size]) for p in r...  22.9 us
    ppermute x6, waiting for transfers between devices, shift(): lax.ppermute(x, 'dp', [(i, (i + CORES * step) % size) for i in range(size)])  16.6 us
    ppermute x9, starting transfers between devices, partner(): return lax.ppermute(x, 'vocab', [(v, v ^ bit) for v in range(self.size)])  15.2 us
    dot_general x1, matrix products, body(): lax.dot_general(grad_all, chosen, (((0,), (0,)), ((), ())), preferred_ele...  12.5 us
    dot_general x2, matrix products, group_logits(): lax.dot_general(normed, head_weight, (((1,), (1,)), ((), ())), preferred_...  11.5 us
    ppermute x9, waiting for transfers between devices, partner(): return lax.ppermute(x, 'vocab', [(v, v ^ bit) for v in range(self.size)])  9.84 us
    ppermute x6, starting transfers between devices, shift(): lax.ppermute(x, 'dp', [(i, (i + CORES * step) % size) for i in range(size)])  9.16 us
  transfers between devices with their start and end apart: 71, of which 34 were waited for; matrix products, arithmetic and copies ran while one was open for 18% of the time, Pallas kernels for 0%

profile of v3, /device:TPU:0, one launch (start us, length us, event | category | flops | bytes accessed | tf_op | source)
XLA Modules:
  0.0 225.4 jit_solution(15975684111145500739)
XLA Ops:
  3.5 2.3 %fusion.138 = (f32[128,2048]{1,0:T(8,128)}, bf16[128]{0:T(256)(128)(2,1)S(1)}) fusion(bf16[128,2048]{1,0:T(8,128)(2,1)} %param.21), kind=kLoop, calls=%fused_computation.345 | loop fusion | flops 524160 | bytes 1573120 | tf_op jit(solution)/shard_map/convert_element_type | solution.py:186
  6.2 3.0 %collective-permute-start = (f32[3,128]{1,0:T(4,128)S(1)}, f32[3,128]{1,0:T(4,128)S(1)}, u32[]{:S(2)}, u32[]{:S(2)}) collective-permute-start(f32[3,128]{1,0:T(4,128)S(1)} %pad_maximum_fusion.21), channel_id=1, source_target_pairs={{0,1},{1,0},{2,3},{3,2},{4,5},{5,4},{6,7},{7,6},{8,9},{9,8},{10,11... | collective-permute-start | bytes 4616 | tf_op jit(solution)/shard_map/ppermute | solution.py:47
  12.4 2.9 %collective-permute-start.1 = (f32[3,128]{1,0:T(4,128)S(1)}, f32[3,128]{1,0:T(4,128)S(1)}, u32[]{:S(2)}, u32[]{:S(2)}) collective-permute-start(f32[3,128]{1,0:T(4,128)S(1)} %pad_maximum_fusion.22), channel_id=1, source_target_pairs={{0,2},{1,3},{2,0},{3,1},{4,6},{5,7},{6,4},{7,5},{8,10},{9,11},{10,... | collective-permute-start | bytes 4616 | tf_op jit(solution)/shard_map/ppermute | solution.py:47
  17.7 3.5 %collective-permute-start.2 = (f32[3,128]{1,0:T(4,128)S(1)}, f32[3,128]{1,0:T(4,128)S(1)}, u32[]{:S(2)}, u32[]{:S(2)}) collective-permute-start(f32[3,128]{1,0:T(4,128)S(1)} %pad_maximum_fusion.23), channel_id=1, source_target_pairs={{0,4},{1,5},{2,6},{3,7},{4,0},{5,1},{6,2},{7,3},{8,12},{9,13},{10,... | collective-permute-start | bytes 4616 | tf_op jit(solution)/shard_map/ppermute | solution.py:47
  25.4 1.5 collective-permute-start.6
  30.4 1.5 collective-permute-start.7
  33.1 1.8 collective-permute-done.11
  35.3 1.5 collective-permute-start.8
  37.5 2.4 %collective-permute-done.12 = bf16[64,1024]{1,0:T(8,128)(2,1)S(1)} collective-permute-done((bf16[64,1024]{1,0:T(8,128)(2,1)S(1)}, bf16[64,1024]{1,0:T(8,128)(2,1)S(1)}, u32[]{:S(2)}, u32[]{:S(2)}) %collective-permute-start.12) | collective-permute-done | bytes 131104 | tf_op jit(solution)/shard_map/ppermute | solution.py:42
  40.6 1.5 collective-permute-start.9
  45.9 5.7 %fusion.148 = f32[256,2048]{1,0:T(8,128)S(1)} fusion(bf16[256,2048]{1,0:T(8,128)(2,1)S(1)} %shard_map.167, bf16[2048,2048]{1,0:T(8,128)(2,1)} %param.20), kind=kOutput, calls=%fused_computation.355 | convolution fusion | flops 2147483648 | bytes 11534336 | tf_op jit(solution)/shard_map/dot_general | solution.py:224
  53.5 9.6 %collective-permute-start.38 = (bf16[64,1024]{1,0:T(8,128)(2,1)S(1)}, bf16[64,1024]{1,0:T(8,128)(2,1)S(1)}, u32[]{:S(2)}, u32[]{:S(2)}) collective-permute-start(bf16[64,1024]{1,0:T(8,128)(2,1)S(1)} %collective-permute-done.37), channel_id=1, source_target_pairs={{0,2},{2,4},{4,6},{6,7},{7,5},{5,3},{3,1},{1,0},{8,10},{10,12},{12... | collective-permute-start | bytes 393224 | tf_op jit(solution)/shard_map/ppermute | solution.py:42
  64.2 2.0 collective-permute-start.69
  66.2 1.9 collective-permute-start.39
  68.9 2.7 %slice_add_fusion.1 = f32[128,2048]{1,0:T(8,128)} fusion(f32[128,2048]{1,0:T(8,128)} %collective-permute-done.14, f32[256,2048]{1,0:T(8,128)} %copy-done.4), kind=kLoop, calls=%fused_computation.20 | loop fusion | flops 262144 | bytes 3145728 | tf_op jit(solution)/shard_map/add | solution.py:229
  71.7 1.4 collective-permute-start.40
  87.9 1.4 fusion.88
  91.2 3.1 %collective-permute-start.15 = (f32[64,2048]{1,0:T(8,128)S(1)}, f32[64,2048]{1,0:T(8,128)S(1)}, u32[]{:S(2)}, u32[]{:S(2)}) collective-permute-start(f32[64,2048]{1,0:T(8,128)S(1)} %slice.312), channel_id=1, source_target_pairs={{0,16},{8,24},{16,0},{24,8},{1,17},{9,25},{17,1},{25,9},{2,18},{10... | collective-permute-start | bytes 1572872 | tf_op jit(solution)/shard_map/ppermute | solution.py:117
  97.0 5.7 %fusion.149 = f32[256,2048]{1,0:T(8,128)S(1)} fusion(bf16[256,2048]{1,0:T(8,128)(2,1)S(1)} %shard_map.168, bf16[2048,2048]{1,0:T(8,128)(2,1)} %param.20), kind=kOutput, calls=%fused_computation.356 | convolution fusion | flops 2147483648 | bytes 11534336 | tf_op jit(solution)/shard_map/dot_general | solution.py:224
  107.0 1.7 collective-permute-start.16
  108.8 1.8 collective-permute-done.16
  111.0 8.9 %collective-permute-done.47 = f32[64,2048]{1,0:T(8,128)S(1)} collective-permute-done((f32[64,2048]{1,0:T(8,128)S(1)}, f32[64,2048]{1,0:T(8,128)S(1)}, u32[]{:S(2)}, u32[]{:S(2)}) %collective-permute-start.47) | collective-permute-done | bytes 524320 | tf_op jit(solution)/shard_map/ppermute | solution.py:117
  120.3 1.3 collective-permute-start.48
  121.6 2.3 %collective-permute-done.48 = f32[2,64]{1,0:T(2,128)S(1)} collective-permute-done((f32[2,64]{1,0:T(2,128)S(1)}, f32[2,64]{1,0:T(2,128)S(1)}, u32[]{:S(2)}, u32[]{:S(2)}) %collective-permute-start.48) | collective-permute-done | bytes 544 | tf_op jit(solution)/shard_map/ppermute | solution.py:47
  124.3 1.8 collective-permute-start.18
  126.1 1.4 collective-permute-done.49
  128.8 3.3 %collective-permute-done.50 = f32[2,64]{1,0:T(2,128)S(1)} collective-permute-done((f32[2,64]{1,0:T(2,128)S(1)}, f32[2,64]{1,0:T(2,128)S(1)}, u32[]{:S(2)}, u32[]{:S(2)}) %collective-permute-start.50) | collective-permute-done | bytes 544 | tf_op jit(solution)/shard_map/ppermute | solution.py:47
  133.7 1.8 collective-permute-start.51
  135.5 5.3 %collective-permute-done.19 = bf16[64,2176]{1,0:T(8,128)(2,1)S(1)} collective-permute-done((bf16[64,2176]{1,0:T(8,128)(2,1)S(1)}, bf16[64,2176]{1,0:T(8,128)(2,1)S(1)}, u32[]{:S(2)}, u32[]{:S(2)}) %collective-permute-start.19) | collective-permute-done | bytes 278560 | tf_op jit(solution)/shard_map/ppermute | solution.py:117
  141.7 2.1 collective-permute-done.51
  144.1 2.4 %fusion.5 = f32[256,2048]{1,0:T(8,128)S(1)} fusion(bf16[2048,2048]{1,0:T(8,128)(2,1)S(1)} %bitcast.410, bf16[256,2176]{1,0:T(8,128)(2,1)S(1)} %bitcast.393), kind=kOutput, calls=%fused_computation.18 | convolution fusion | flops 2147483648 | bytes 11534336 | tf_op jit(solution)/shard_map/dot_general | solution.py:275
  146.7 2.4 %fusion.3 = f32[256,2048]{1,0:T(8,128)S(1)} fusion(bf16[2048,2048]{1,0:T(8,128)(2,1)S(1)} %bitcast.410, bf16[256,2176]{1,0:T(8,128)(2,1)S(1)} %bitcast.394), kind=kOutput, calls=%fused_computation.15 | convolution fusion | flops 2147483648 | bytes 11534336 | tf_op jit(solution)/shard_map/dot_general | solution.py:275
  150.0 1.7 collective-permute-start.25
  152.1 1.7 collective-permute-start.57
  154.7 1.8 collective-permute-start.26
  156.9 1.8 collective-permute-start.58
  158.7 2.2 collective-permute-done.22
  161.3 1.8 collective-permute-start.27
  164.3 1.8 collective-permute-start.59
  167.8 1.8 collective-permute-start.28
  170.9 1.8 collective-permute-start.60
  173.3 2.3 %collective-permute-done.56 = bf16[32,2176]{1,0:T(8,128)(2,1)S(1)} collective-permute-done((bf16[32,2176]{1,0:T(8,128)(2,1)S(1)}, bf16[32,2176]{1,0:T(8,128)(2,1)S(1)}, u32[]{:S(2)}, u32[]{:S(2)}) %collective-permute-start.56) | collective-permute-done | bytes 139296 | tf_op jit(solution)/shard_map/ppermute | solution.py:42
  182.1 2.3 %collective-permute-done.61 = bf16[32,2048]{1,0:T(8,128)(2,1)S(1)} collective-permute-done((bf16[32,2048]{1,0:T(8,128)(2,1)S(1)}, bf16[32,2048]{1,0:T(8,128)(2,1)S(1)}, u32[]{:S(2)}, u32[]{:S(2)}) %collective-permute-start.61) | collective-permute-done | bytes 131104 | tf_op jit(solution)/shard_map/ppermute | solution.py:42
  193.3 1.3 collective-permute-start.31
  199.3 1.7 pad_maximum_fusion
  201.0 1.2 collective-permute-start.32
  205.3 1.3 collective-permute-done.36
  212.1 12.5 %fusion = f32[2048,3072]{1,0:T(8,128)} fusion(bf16[512,3072]{1,0:T(8,128)(2,1)S(1)} %bitcast.389, bf16[256,2048]{1,0:T(8,128)(2,1)S(1)} %bitcast.385, bf16[256,2048]{1,0:T(8,128)(2,1)S(1)} %bitcast.387), kind=kOutput, calls=%fused_computation.5 | convolution fusion | flops 6446645248 | bytes 30408704 | tf_op jit(solution)/shard_map/dot_general | solution.py:312
  (303 shorter events, 73.2 us)
Async XLA Ops:
  1.8 23.0 %collective-permute-start.5 = (bf16[64,1024]{1,0:T(8,128)(2,1)S(1)}, bf16[64,1024]{1,0:T(8,128)(2,1)S(1)}, u32[]{:S(2)}, u32[]{:S(2)}) collective-permute-start(bf16[64,1024]{1,0:T(8,128)(2,1)S(1)} %get-tuple-element.58), channel_id=1, source_target_pairs={{0,0},{1,1},{2,8},{3,9},{4,16},{5,17},{6,24},{7,25},{8,4},{9,5},{1... | collective-permute-start | bytes 393224 | tf_op jit(solution)/shard_map/ppermute | solution.py:183
  6.2 6.1 %collective-permute-start = (f32[3,128]{1,0:T(4,128)S(1)}, f32[3,128]{1,0:T(4,128)S(1)}, u32[]{:S(2)}, u32[]{:S(2)}) collective-permute-start(f32[3,128]{1,0:T(4,128)S(1)} %pad_maximum_fusion.21), channel_id=1, source_target_pairs={{0,1},{1,0},{2,3},{3,2},{4,5},{5,4},{6,7},{7,6},{8,9},{9,8},{10,11... | collective-permute-start | bytes 4616 | tf_op jit(solution)/shard_map/ppermute | solution.py:47
  12.4 5.3 %collective-permute-start.1 = (f32[3,128]{1,0:T(4,128)S(1)}, f32[3,128]{1,0:T(4,128)S(1)}, u32[]{:S(2)}, u32[]{:S(2)}) collective-permute-start(f32[3,128]{1,0:T(4,128)S(1)} %pad_maximum_fusion.22), channel_id=1, source_target_pairs={{0,2},{1,3},{2,0},{3,1},{4,6},{5,7},{6,4},{7,5},{8,10},{9,11},{10,... | collective-permute-start | bytes 4616 | tf_op jit(solution)/shard_map/ppermute | solution.py:47
  17.7 9.2 %collective-permute-start.2 = (f32[3,128]{1,0:T(4,128)S(1)}, f32[3,128]{1,0:T(4,128)S(1)}, u32[]{:S(2)}, u32[]{:S(2)}) collective-permute-start(f32[3,128]{1,0:T(4,128)S(1)} %pad_maximum_fusion.23), channel_id=1, source_target_pairs={{0,4},{1,5},{2,6},{3,7},{4,0},{5,1},{6,2},{7,3},{8,12},{9,13},{10,... | collective-permute-start | bytes 4616 | tf_op jit(solution)/shard_map/ppermute | solution.py:47
  24.8 5.0 %collective-permute-start.10 = (bf16[64,1024]{1,0:T(8,128)(2,1)S(1)}, bf16[64,1024]{1,0:T(8,128)(2,1)S(1)}, u32[]{:S(2)}, u32[]{:S(2)}) collective-permute-start(bf16[64,1024]{1,0:T(8,128)(2,1)S(1)} %collective-permute-done.5), channel_id=1, source_target_pairs={{0,1},{2,0},{4,2},{6,4},{7,6},{5,7},{3,5},{1,3},{8,9},{10,8},{12,1... | collective-permute-start | bytes 393224 | tf_op jit(solution)/shard_map/ppermute | solution.py:42
  25.4 5.0 %collective-permute-start.6 = (bf16[64,1024]{1,0:T(8,128)(2,1)S(1)}, bf16[64,1024]{1,0:T(8,128)(2,1)S(1)}, u32[]{:S(2)}, u32[]{:S(2)}) collective-permute-start(bf16[64,1024]{1,0:T(8,128)(2,1)S(1)} %collective-permute-done.5), channel_id=1, source_target_pairs={{0,2},{2,4},{4,6},{6,7},{7,5},{5,3},{3,1},{1,0},{8,10},{10,12},{12... | collective-permute-start | bytes 393224 | tf_op jit(solution)/shard_map/ppermute | solution.py:42
  34.8 5.0 %collective-permute-start.12 = (bf16[64,1024]{1,0:T(8,128)(2,1)S(1)}, bf16[64,1024]{1,0:T(8,128)(2,1)S(1)}, u32[]{:S(2)}, u32[]{:S(2)}) collective-permute-start(bf16[64,1024]{1,0:T(8,128)(2,1)S(1)} %collective-permute-done.11), channel_id=1, source_target_pairs={{0,1},{2,0},{4,2},{6,4},{7,6},{5,7},{3,5},{1,3},{8,9},{10,8},{12,1... | collective-permute-start | bytes 393224 | tf_op jit(solution)/shard_map/ppermute | solution.py:42
  35.3 5.3 %collective-permute-start.8 = (bf16[64,1024]{1,0:T(8,128)(2,1)S(1)}, bf16[64,1024]{1,0:T(8,128)(2,1)S(1)}, u32[]{:S(2)}, u32[]{:S(2)}) collective-permute-start(bf16[64,1024]{1,0:T(8,128)(2,1)S(1)} %collective-permute-done.7), channel_id=1, source_target_pairs={{0,2},{2,4},{4,6},{6,7},{7,5},{5,3},{3,1},{1,0},{8,10},{10,12},{12... | collective-permute-start | bytes 393224 | tf_op jit(solution)/shard_map/ppermute | solution.py:42
  52.9 16.0 %collective-permute-start.14 = (f32[128,2048]{1,0:T(8,128)}, f32[128,2048]{1,0:T(8,128)}, u32[]{:S(2)}, u32[]{:S(2)}) collective-permute-start(f32[128,2048]{1,0:T(8,128)} %slice.310), channel_id=1, source_target_pairs={{0,8},{8,0},{16,24},{24,16},{1,9},{9,1},{17,25},{25,17},{2,10},{10... | collective-permute-start | bytes 3145736 | tf_op jit(solution)/shard_map/ppermute | solution.py:113
  53.5 12.7 %collective-permute-start.38 = (bf16[64,1024]{1,0:T(8,128)(2,1)S(1)}, bf16[64,1024]{1,0:T(8,128)(2,1)S(1)}, u32[]{:S(2)}, u32[]{:S(2)}) collective-permute-start(bf16[64,1024]{1,0:T(8,128)(2,1)S(1)} %collective-permute-done.37), channel_id=1, source_target_pairs={{0,2},{2,4},{4,6},{6,7},{7,5},{5,3},{3,1},{1,0},{8,10},{10,12},{12... | collective-permute-start | bytes 393224 | tf_op jit(solution)/shard_map/ppermute | solution.py:42
  63.1 5.0 %collective-permute-start.42 = (bf16[64,1024]{1,0:T(8,128)(2,1)S(1)}, bf16[64,1024]{1,0:T(8,128)(2,1)S(1)}, u32[]{:S(2)}, u32[]{:S(2)}) collective-permute-start(bf16[64,1024]{1,0:T(8,128)(2,1)S(1)} %collective-permute-done.37), channel_id=1, source_target_pairs={{0,1},{2,0},{4,2},{6,4},{7,6},{5,7},{3,5},{1,3},{8,9},{10,8},{12,1... | collective-permute-start | bytes 393224 | tf_op jit(solution)/shard_map/ppermute | solution.py:42
  64.2 76.8 %collective-permute-start.69 = (bf16[2,64,3072]{2,1,0:T(8,128)(2,1)S(1)}, bf16[2,64,3072]{2,1,0:T(8,128)(2,1)S(1)}, u32[]{:S(2)}, u32[]{:S(2)}) collective-permute-start(bf16[2,64,3072]{2,1,0:T(8,128)(2,1)S(1)} %bitcast.382), channel_id=1, source_target_pairs={{0,16},{8,24},{16,0},{24,8},{1,17},{9,25},{17,1},{25,9},{2,18},{10... | collective-permute-start | bytes 2359304 | tf_op jit(solution)/shard_map/ppermute | solution.py:117
  66.2 5.5 %collective-permute-start.39 = (bf16[64,1024]{1,0:T(8,128)(2,1)S(1)}, bf16[64,1024]{1,0:T(8,128)(2,1)S(1)}, u32[]{:S(2)}, u32[]{:S(2)}) collective-permute-start(bf16[64,1024]{1,0:T(8,128)(2,1)S(1)} %collective-permute-done.38), channel_id=1, source_target_pairs={{0,2},{2,4},{4,6},{6,7},{7,5},{5,3},{3,1},{1,0},{8,10},{10,12},{12... | collective-permute-start | bytes 393224 | tf_op jit(solution)/shard_map/ppermute | solution.py:42
  71.7 13.0 %collective-permute-start.40 = (bf16[64,1024]{1,0:T(8,128)(2,1)S(1)}, bf16[64,1024]{1,0:T(8,128)(2,1)S(1)}, u32[]{:S(2)}, u32[]{:S(2)}) collective-permute-start(bf16[64,1024]{1,0:T(8,128)(2,1)S(1)} %collective-permute-done.39), channel_id=1, source_target_pairs={{0,2},{2,4},{4,6},{6,7},{7,5},{5,3},{3,1},{1,0},{8,10},{10,12},{12... | collective-permute-start | bytes 393224 | tf_op jit(solution)/shard_map/ppermute | solution.py:42
  73.0 13.4 %collective-permute-start.44 = (bf16[64,1024]{1,0:T(8,128)(2,1)S(1)}, bf16[64,1024]{1,0:T(8,128)(2,1)S(1)}, u32[]{:S(2)}, u32[]{:S(2)}) collective-permute-start(bf16[64,1024]{1,0:T(8,128)(2,1)S(1)} %collective-permute-done.43), channel_id=1, source_target_pairs={{0,1},{2,0},{4,2},{6,4},{7,6},{5,7},{3,5},{1,3},{8,9},{10,8},{12,1... | collective-permute-start | bytes 393224 | tf_op jit(solution)/shard_map/ppermute | solution.py:42
  85.3 9.0 %collective-permute-start.41 = (bf16[32,1024]{1,0:T(8,128)(2,1)}, bf16[32,1024]{1,0:T(8,128)(2,1)}, u32[]{:S(2)}, u32[]{:S(2)}) collective-permute-start(bf16[32,1024]{1,0:T(8,128)(2,1)} %slice.326), channel_id=1, source_target_pairs={{0,2},{2,4},{4,6},{6,7},{7,5},{5,3},{3,1},{1,0},{8,10},{10,12},{12... | collective-permute-start | bytes 196616 | tf_op jit(solution)/shard_map/ppermute | solution.py:42
  87.1 7.1 %collective-permute-start.45 = (bf16[32,1024]{1,0:T(8,128)(2,1)}, bf16[32,1024]{1,0:T(8,128)(2,1)}, u32[]{:S(2)}, u32[]{:S(2)}) collective-permute-start(bf16[32,1024]{1,0:T(8,128)(2,1)} %slice.327), channel_id=1, source_target_pairs={{0,1},{2,0},{4,2},{6,4},{7,6},{5,7},{3,5},{1,3},{8,9},{10,8},{12,1... | collective-permute-start | bytes 196616 | tf_op jit(solution)/shard_map/ppermute | solution.py:42
  91.2 13.4 %collective-permute-start.15 = (f32[64,2048]{1,0:T(8,128)S(1)}, f32[64,2048]{1,0:T(8,128)S(1)}, u32[]{:S(2)}, u32[]{:S(2)}) collective-permute-start(f32[64,2048]{1,0:T(8,128)S(1)} %slice.312), channel_id=1, source_target_pairs={{0,16},{8,24},{16,0},{24,8},{1,17},{9,25},{17,1},{25,9},{2,18},{10... | collective-permute-start | bytes 1572872 | tf_op jit(solution)/shard_map/ppermute | solution.py:117
  105.8 14.0 %collective-permute-start.47 = (f32[64,2048]{1,0:T(8,128)S(1)}, f32[64,2048]{1,0:T(8,128)S(1)}, u32[]{:S(2)}, u32[]{:S(2)}) collective-permute-start(f32[64,2048]{1,0:T(8,128)S(1)} %slice.331), channel_id=1, source_target_pairs={{0,16},{8,24},{16,0},{24,8},{1,17},{9,25},{17,1},{25,9},{2,18},{10... | collective-permute-start | bytes 1572872 | tf_op jit(solution)/shard_map/ppermute | solution.py:117
  110.6 11.0 %collective-permute-start.17 = (f32[2,64]{1,0:T(2,128)S(1)}, f32[2,64]{1,0:T(2,128)S(1)}, u32[]{:S(2)}, u32[]{:S(2)}) collective-permute-start(f32[2,64]{1,0:T(2,128)S(1)} %pad_maximum_fusion.27), channel_id=1, source_target_pairs={{0,2},{1,3},{2,0},{3,1},{4,6},{5,7},{6,4},{7,5},{8,10},{9,11},{10,... | collective-permute-start | bytes 1544 | tf_op jit(solution)/shard_map/ppermute | solution.py:47
  133.3 7.5 %collective-permute-start.19 = (bf16[64,2176]{1,0:T(8,128)(2,1)S(1)}, bf16[64,2176]{1,0:T(8,128)(2,1)S(1)}, u32[]{:S(2)}, u32[]{:S(2)}) collective-permute-start(bf16[64,2176]{1,0:T(8,128)(2,1)S(1)} %get-tuple-element.56), channel_id=1, source_target_pairs={{0,16},{8,24},{16,0},{24,8},{1,17},{9,25},{17,1},{25,9},{2,18},{10... | collective-permute-start | bytes 835592 | tf_op jit(solution)/shard_map/ppermute | solution.py:117
  133.7 10.1 %collective-permute-start.51 = (bf16[64,2176]{1,0:T(8,128)(2,1)S(1)}, bf16[64,2176]{1,0:T(8,128)(2,1)S(1)}, u32[]{:S(2)}, u32[]{:S(2)}) collective-permute-start(bf16[64,2176]{1,0:T(8,128)(2,1)S(1)} %get-tuple-element.54), channel_id=1, source_target_pairs={{0,16},{8,24},{16,0},{24,8},{1,17},{9,25},{17,1},{25,9},{2,18},{10... | collective-permute-start | bytes 835592 | tf_op jit(solution)/shard_map/ppermute | solution.py:117
  141.1 58.1 %collective-permute-start.70 = (bf16[2,2,64,3072]{3,2,0,1:T(8,128)(2,1)S(1)}, bf16[2,2,64,3072]{3,2,0,1:T(8,128)(2,1)}, u32[]{:S(2)}, u32[]{:S(2)}) collective-permute-start(bf16[2,2,64,3072]{3,2,0,1:T(8,128)(2,1)S(1)} %pad_maximum_fusion.3), channel_id=1, source_target_pairs={{0,8},{8,0},{16,24},{24,16},{1,9},{9,1},{17,25},{25,17},{2,10},{10... | collective-permute-start | bytes 4718600 | tf_op jit(solution)/shard_map/ppermute | solution.py:113
  154.3 6.6 %collective-permute-start.22 = (bf16[32,2176]{1,0:T(8,128)(2,1)S(1)}, bf16[32,2176]{1,0:T(8,128)(2,1)S(1)}, u32[]{:S(2)}, u32[]{:S(2)}) collective-permute-start(bf16[32,2176]{1,0:T(8,128)(2,1)S(1)} %pad_maximum_fusion.14), channel_id=1, source_target_pairs={{0,2},{2,4},{4,6},{6,7},{7,5},{5,3},{3,1},{1,0},{8,10},{10,12},{12... | collective-permute-start | bytes 417800 | tf_op jit(solution)/shard_map/ppermute | solution.py:42
  154.7 6.6 %collective-permute-start.26 = (bf16[32,2176]{1,0:T(8,128)(2,1)S(1)}, bf16[32,2176]{1,0:T(8,128)(2,1)S(1)}, u32[]{:S(2)}, u32[]{:S(2)}) collective-permute-start(bf16[32,2176]{1,0:T(8,128)(2,1)S(1)} %pad_maximum_fusion.15), channel_id=1, source_target_pairs={{0,1},{2,0},{4,2},{6,4},{7,6},{5,7},{3,5},{1,3},{8,9},{10,8},{12,1... | collective-permute-start | bytes 417800 | tf_op jit(solution)/shard_map/ppermute | solution.py:42
  156.5 7.4 %collective-permute-start.54 = (bf16[32,2176]{1,0:T(8,128)(2,1)S(1)}, bf16[32,2176]{1,0:T(8,128)(2,1)S(1)}, u32[]{:S(2)}, u32[]{:S(2)}) collective-permute-start(bf16[32,2176]{1,0:T(8,128)(2,1)S(1)} %pad_maximum_fusion.16), channel_id=1, source_target_pairs={{0,2},{2,4},{4,6},{6,7},{7,5},{5,3},{3,1},{1,0},{8,10},{10,12},{12... | collective-permute-start | bytes 417800 | tf_op jit(solution)/shard_map/ppermute | solution.py:42
  156.9 7.4 %collective-permute-start.58 = (bf16[32,2176]{1,0:T(8,128)(2,1)S(1)}, bf16[32,2176]{1,0:T(8,128)(2,1)S(1)}, u32[]{:S(2)}, u32[]{:S(2)}) collective-permute-start(bf16[32,2176]{1,0:T(8,128)(2,1)S(1)} %pad_maximum_fusion.17), channel_id=1, source_target_pairs={{0,1},{2,0},{4,2},{6,4},{7,6},{5,7},{3,5},{1,3},{8,9},{10,8},{12,1... | collective-permute-start | bytes 417800 | tf_op jit(solution)/shard_map/ppermute | solution.py:42
  161.0 6.1 %collective-permute-start.23 = (bf16[32,2176]{1,0:T(8,128)(2,1)S(1)}, bf16[32,2176]{1,0:T(8,128)(2,1)S(1)}, u32[]{:S(2)}, u32[]{:S(2)}) collective-permute-start(bf16[32,2176]{1,0:T(8,128)(2,1)S(1)} %fusion.21), channel_id=1, source_target_pairs={{0,2},{2,4},{4,6},{6,7},{7,5},{5,3},{3,1},{1,0},{8,10},{10,12},{12... | collective-permute-start | bytes 417800 | tf_op jit(solution)/shard_map/ppermute | solution.py:42
  161.3 6.4 %collective-permute-start.27 = (bf16[32,2176]{1,0:T(8,128)(2,1)S(1)}, bf16[32,2176]{1,0:T(8,128)(2,1)S(1)}, u32[]{:S(2)}, u32[]{:S(2)}) collective-permute-start(bf16[32,2176]{1,0:T(8,128)(2,1)S(1)} %fusion.23), channel_id=1, source_target_pairs={{0,1},{2,0},{4,2},{6,4},{7,6},{5,7},{3,5},{1,3},{8,9},{10,8},{12,1... | collective-permute-start | bytes 417800 | tf_op jit(solution)/shard_map/ppermute | solution.py:42
  164.0 6.5 %collective-permute-start.55 = (bf16[32,2176]{1,0:T(8,128)(2,1)S(1)}, bf16[32,2176]{1,0:T(8,128)(2,1)S(1)}, u32[]{:S(2)}, u32[]{:S(2)}) collective-permute-start(bf16[32,2176]{1,0:T(8,128)(2,1)S(1)} %fusion.26), channel_id=1, source_target_pairs={{0,2},{2,4},{4,6},{6,7},{7,5},{5,3},{3,1},{1,0},{8,10},{10,12},{12... | collective-permute-start | bytes 417800 | tf_op jit(solution)/shard_map/ppermute | solution.py:42
  164.3 6.5 %collective-permute-start.59 = (bf16[32,2176]{1,0:T(8,128)(2,1)S(1)}, bf16[32,2176]{1,0:T(8,128)(2,1)S(1)}, u32[]{:S(2)}, u32[]{:S(2)}) collective-permute-start(bf16[32,2176]{1,0:T(8,128)(2,1)S(1)} %fusion.28), channel_id=1, source_target_pairs={{0,1},{2,0},{4,2},{6,4},{7,6},{5,7},{3,5},{1,3},{8,9},{10,8},{12,1... | collective-permute-start | bytes 417800 | tf_op jit(solution)/shard_map/ppermute | solution.py:42
  167.1 6.0 %collective-permute-start.24 = (bf16[32,2176]{1,0:T(8,128)(2,1)S(1)}, bf16[32,2176]{1,0:T(8,128)(2,1)S(1)}, u32[]{:S(2)}, u32[]{:S(2)}) collective-permute-start(bf16[32,2176]{1,0:T(8,128)(2,1)S(1)} %fusion.20), channel_id=1, source_target_pairs={{0,2},{2,4},{4,6},{6,7},{7,5},{5,3},{3,1},{1,0},{8,10},{10,12},{12... | collective-permute-start | bytes 417800 | tf_op jit(solution)/shard_map/ppermute | solution.py:42
  167.8 5.5 %collective-permute-start.28 = (bf16[32,2176]{1,0:T(8,128)(2,1)S(1)}, bf16[32,2176]{1,0:T(8,128)(2,1)S(1)}, u32[]{:S(2)}, u32[]{:S(2)}) collective-permute-start(bf16[32,2176]{1,0:T(8,128)(2,1)S(1)} %fusion.22), channel_id=1, source_target_pairs={{0,1},{2,0},{4,2},{6,4},{7,6},{5,7},{3,5},{1,3},{8,9},{10,8},{12,1... | collective-permute-start | bytes 417800 | tf_op jit(solution)/shard_map/ppermute | solution.py:42
  170.5 5.1 %collective-permute-start.56 = (bf16[32,2176]{1,0:T(8,128)(2,1)S(1)}, bf16[32,2176]{1,0:T(8,128)(2,1)S(1)}, u32[]{:S(2)}, u32[]{:S(2)}) collective-permute-start(bf16[32,2176]{1,0:T(8,128)(2,1)S(1)} %fusion.25), channel_id=1, source_target_pairs={{0,2},{2,4},{4,6},{6,7},{7,5},{5,3},{3,1},{1,0},{8,10},{10,12},{12... | collective-permute-start | bytes 417800 | tf_op jit(solution)/shard_map/ppermute | solution.py:42
  170.9 5.1 %collective-permute-start.60 = (bf16[32,2176]{1,0:T(8,128)(2,1)S(1)}, bf16[32,2176]{1,0:T(8,128)(2,1)S(1)}, u32[]{:S(2)}, u32[]{:S(2)}) collective-permute-start(bf16[32,2176]{1,0:T(8,128)(2,1)S(1)} %fusion.27), channel_id=1, source_target_pairs={{0,1},{2,0},{4,2},{6,4},{7,6},{5,7},{3,5},{1,3},{8,9},{10,8},{12,1... | collective-permute-start | bytes 417800 | tf_op jit(solution)/shard_map/ppermute | solution.py:42
  178.0 6.4 %collective-permute-start.61 = (bf16[32,2048]{1,0:T(8,128)(2,1)S(1)}, bf16[32,2048]{1,0:T(8,128)(2,1)S(1)}, u32[]{:S(2)}, u32[]{:S(2)}) collective-permute-start(bf16[32,2048]{1,0:T(8,128)(2,1)S(1)} %get-tuple-element.79), channel_id=1, source_target_pairs={{0,2},{2,4},{4,6},{6,7},{7,5},{5,3},{3,1},{1,0},{8,10},{10,12},{12... | collective-permute-start | bytes 393224 | tf_op jit(solution)/shard_map/ppermute | solution.py:42
  179.0 6.4 %collective-permute-start.65 = (bf16[32,2048]{1,0:T(8,128)(2,1)S(1)}, bf16[32,2048]{1,0:T(8,128)(2,1)S(1)}, u32[]{:S(2)}, u32[]{:S(2)}) collective-permute-start(bf16[32,2048]{1,0:T(8,128)(2,1)S(1)} %get-tuple-element.79), channel_id=1, source_target_pairs={{0,1},{2,0},{4,2},{6,4},{7,6},{5,7},{3,5},{1,3},{8,9},{10,8},{12,1... | collective-permute-start | bytes 393224 | tf_op jit(solution)/shard_map/ppermute | solution.py:42
  180.1 7.1 %collective-permute-start.29 = (bf16[32,2048]{1,0:T(8,128)(2,1)S(1)}, bf16[32,2048]{1,0:T(8,128)(2,1)}, u32[]{:S(2)}, u32[]{:S(2)}) collective-permute-start(bf16[32,2048]{1,0:T(8,128)(2,1)S(1)} %get-tuple-element.80), channel_id=1, source_target_pairs={{0,2},{2,4},{4,6},{6,7},{7,5},{5,3},{3,1},{1,0},{8,10},{10,12},{12... | collective-permute-start | bytes 393224 | tf_op jit(solution)/shard_map/ppermute | solution.py:42
  181.0 7.1 %collective-permute-start.33 = (bf16[32,2048]{1,0:T(8,128)(2,1)S(1)}, bf16[32,2048]{1,0:T(8,128)(2,1)}, u32[]{:S(2)}, u32[]{:S(2)}) collective-permute-start(bf16[32,2048]{1,0:T(8,128)(2,1)S(1)} %get-tuple-element.80), channel_id=1, source_target_pairs={{0,1},{2,0},{4,2},{6,4},{7,6},{5,7},{3,5},{1,3},{8,9},{10,8},{12,1... | collective-permute-start | bytes 393224 | tf_op jit(solution)/shard_map/ppermute | solution.py:42
  184.4 5.9 %collective-permute-start.62 = (bf16[32,2048]{1,0:T(8,128)(2,1)S(1)}, bf16[32,2048]{1,0:T(8,128)(2,1)}, u32[]{:S(2)}, u32[]{:S(2)}) collective-permute-start(bf16[32,2048]{1,0:T(8,128)(2,1)S(1)} %collective-permute-done.61), channel_id=1, source_target_pairs={{0,2},{2,4},{4,6},{6,7},{7,5},{5,3},{3,1},{1,0},{8,10},{10,12},{12... | collective-permute-start | bytes 393224 | tf_op jit(solution)/shard_map/ppermute | solution.py:42
  185.3 6.5 %collective-permute-start.66 = (bf16[32,2048]{1,0:T(8,128)(2,1)S(1)}, bf16[32,2048]{1,0:T(8,128)(2,1)}, u32[]{:S(2)}, u32[]{:S(2)}) collective-permute-start(bf16[32,2048]{1,0:T(8,128)(2,1)S(1)} %collective-permute-done.65), channel_id=1, source_target_pairs={{0,1},{2,0},{4,2},{6,4},{7,6},{5,7},{3,5},{1,3},{8,9},{10,8},{12,1... | collective-permute-start | bytes 393224 | tf_op jit(solution)/shard_map/ppermute | solution.py:42
  187.1 6.1 %collective-permute-start.30 = (bf16[32,2048]{1,0:T(8,128)(2,1)}, bf16[32,2048]{1,0:T(8,128)(2,1)}, u32[]{:S(2)}, u32[]{:S(2)}) collective-permute-start(bf16[32,2048]{1,0:T(8,128)(2,1)} %collective-permute-done.29), channel_id=1, source_target_pairs={{0,2},{2,4},{4,6},{6,7},{7,5},{5,3},{3,1},{1,0},{8,10},{10,12},{12... | collective-permute-start | bytes 393224 | tf_op jit(solution)/shard_map/ppermute | solution.py:42
  188.1 6.5 %collective-permute-start.34 = (bf16[32,2048]{1,0:T(8,128)(2,1)}, bf16[32,2048]{1,0:T(8,128)(2,1)}, u32[]{:S(2)}, u32[]{:S(2)}) collective-permute-start(bf16[32,2048]{1,0:T(8,128)(2,1)} %collective-permute-done.33), channel_id=1, source_target_pairs={{0,1},{2,0},{4,2},{6,4},{7,6},{5,7},{3,5},{1,3},{8,9},{10,8},{12,1... | collective-permute-start | bytes 393224 | tf_op jit(solution)/shard_map/ppermute | solution.py:42
  190.3 6.0 %collective-permute-start.63 = (bf16[32,2048]{1,0:T(8,128)(2,1)}, bf16[32,2048]{1,0:T(8,128)(2,1)}, u32[]{:S(2)}, u32[]{:S(2)}) collective-permute-start(bf16[32,2048]{1,0:T(8,128)(2,1)} %collective-permute-done.62), channel_id=1, source_target_pairs={{0,2},{2,4},{4,6},{6,7},{7,5},{5,3},{3,1},{1,0},{8,10},{10,12},{12... | collective-permute-start | bytes 393224 | tf_op jit(solution)/shard_map/ppermute | solution.py:42
  191.8 6.5 %collective-permute-start.67 = (bf16[32,2048]{1,0:T(8,128)(2,1)}, bf16[32,2048]{1,0:T(8,128)(2,1)S(1)}, u32[]{:S(2)}, u32[]{:S(2)}) collective-permute-start(bf16[32,2048]{1,0:T(8,128)(2,1)} %collective-permute-done.66), channel_id=1, source_target_pairs={{0,1},{2,0},{4,2},{6,4},{7,6},{5,7},{3,5},{1,3},{8,9},{10,8},{12,1... | collective-permute-start | bytes 393224 | tf_op jit(solution)/shard_map/ppermute | solution.py:42
  193.3 7.7 %collective-permute-start.31 = (bf16[32,2048]{1,0:T(8,128)(2,1)}, bf16[32,2048]{1,0:T(8,128)(2,1)S(1)}, u32[]{:S(2)}, u32[]{:S(2)}) collective-permute-start(bf16[32,2048]{1,0:T(8,128)(2,1)} %collective-permute-done.30), channel_id=1, source_target_pairs={{0,2},{2,4},{4,6},{6,7},{7,5},{5,3},{3,1},{1,0},{8,10},{10,12},{12... | collective-permute-start | bytes 393224 | tf_op jit(solution)/shard_map/ppermute | solution.py:42
  194.6 7.7 %collective-permute-start.35 = (bf16[32,2048]{1,0:T(8,128)(2,1)}, bf16[32,2048]{1,0:T(8,128)(2,1)S(1)}, u32[]{:S(2)}, u32[]{:S(2)}) collective-permute-start(bf16[32,2048]{1,0:T(8,128)(2,1)} %collective-permute-done.34), channel_id=1, source_target_pairs={{0,1},{2,0},{4,2},{6,4},{7,6},{5,7},{3,5},{1,3},{8,9},{10,8},{12,1... | collective-permute-start | bytes 393224 | tf_op jit(solution)/shard_map/ppermute | solution.py:42
  197.2 6.0 %collective-permute-start.64 = (bf16[16,2048]{1,0:T(8,128)(2,1)S(1)}, bf16[16,2048]{1,0:T(8,128)(2,1)S(1)}, u32[]{:S(2)}, u32[]{:S(2)}) collective-permute-start(bf16[16,2048]{1,0:T(8,128)(2,1)S(1)} %slice.343), channel_id=1, source_target_pairs={{0,2},{2,4},{4,6},{6,7},{7,5},{5,3},{3,1},{1,0},{8,10},{10,12},{12... | collective-permute-start | bytes 196616 | tf_op jit(solution)/shard_map/ppermute | solution.py:42
  (49 other events, 397.2 us)

commit v4 on v3

v4 whole, which is shorter than its diff:
```python
import functools

import jax
import jax.numpy as jnp
import numpy as np
from jax import lax
from jax.experimental import pallas as pl
from jax.experimental.pallas import tpu as pltpu
from jax.sharding import PartitionSpec as P

TREE = 64
CORES = 2
LANES = 128
CHUNKS = 2
F32 = jnp.float32
BF16 = jnp.bfloat16


def ring_order(rows, columns):
    if columns == 1 or rows == 1:
        return list(range(rows * columns))
    order = [r * columns for r in range(rows)]
    for step in range(rows):
        r = rows - 1 - step
        line = [r * columns + c for c in range(1, columns)]
        order += line if step % 2 == 0 else line[::-1]
    return order


def half_width(x):
    return x.shape[1] // 2 // LANES * LANES


class Ring:
    def __init__(self, size, columns):
        self.size = size
        self.half = size // 2
        self.order = ring_order(size // columns, columns)
        self.place = [0] * size
        for position, index in enumerate(self.order):
            self.place[index] = position

    def shift(self, x, step):
        size, order = self.size, self.order
        return lax.ppermute(
            x, "vocab", [(order[p], order[(p + step) % size]) for p in range(size)]
        )

    def partner(self, x, bit):
        return lax.ppermute(x, "vocab", [(v, v ^ bit) for v in range(self.size)])

    def meet(self, x, merge):
        bit = 1
        while bit < self.size:
            x = merge(x, self.partner(x, bit))
            bit *= 2
        return x

    def gather(self, block, waits=None):
        ahead, behind = [block], [block]
        for step in range(self.half - 1):
            if waits and step in waits:
                others = waits[step]()
                ahead[-1], behind[-1] = after(ahead[-1], others), after(behind[-1], others)
            ahead.append(self.shift(ahead[-1], 1))
            behind.append(self.shift(behind[-1], -1))
        cut = half_width(block)
        far = [self.shift(ahead[-1][:, :cut], 1), self.shift(behind[-1][:, cut:], -1)]
        return far + ahead[1:][::-1] + [block] + behind[1:]

    def sources(self, vocab):
        p = self.place[vocab]
        return [(p + k - self.half) % self.size for k in range(self.size)]

    def scatter_sum(self, part):
        steps = self.half - 1
        far = part(self.half).astype(BF16)
        cut = half_width(far)
        got = self.shift(far[:, :cut], 1).astype(F32)
        ahead = part(steps)
        ahead = jnp.concatenate([ahead[:, :cut] + got, ahead[:, cut:]], axis=1)
        got = self.shift(far[:, cut:], -1).astype(F32)
        behind = part(-steps)
        behind = jnp.concatenate([behind[:, :cut], behind[:, cut:] + got], axis=1)
        for step in range(steps - 1, -1, -1):
            got_ahead = self.shift(ahead.astype(BF16), 1).astype(F32)
            got_behind = self.shift(behind.astype(BF16), -1).astype(F32)
            if step > 0:
                ahead = part(step) + got_ahead
                behind = part(-step) + got_behind
        return part(0) + got_ahead + got_behind


class Groups:
    def __init__(self, size):
        self.size = size
        self.chips = size // CORES

    def entry(self, index, group):
        chip = (group // CORES - index // CORES) % self.chips
        return (group % CORES ^ index % CORES) * self.chips + chip

    def swap(self, x):
        return lax.ppermute(x, "dp", [(i, i ^ 1) for i in range(self.size)])

    def shift(self, x, step):
        size = self.size
        return lax.ppermute(x, "dp", [(i, (i + CORES * step) % size) for i in range(size)])

    def gather(self, block):
        mine = jnp.stack([block] + [self.shift(block, -d) for d in range(1, self.chips)])
        return jnp.concatenate([mine, self.swap(mine)], axis=0)


def place_pieces(refs, put):
    put(0, refs[0], 0)
    put(0, refs[1], refs[0].shape[1])
    for k, ref in enumerate(refs[2:]):
        put(k + 1, ref, 0)


def normalise_kernel(count, index_ref, factor_ref, gain_ref, *refs):
    blocks, (normed_ref, piece_ref, raw_ref) = refs[: count + 1], refs[count + 1 :]
    rows, width = blocks[2].shape
    piece = piece_ref.shape[0]

    def put(k, ref, first):
        start = pl.multiple_of(index_ref[k] * rows, rows)
        column = pl.multiple_of(index_ref[count + k] * width + first, LANES)
        raw_ref[pl.ds(start, rows), pl.ds(column, ref.shape[1])] = ref[...]

    place_pieces(blocks, put)
    for g in range(factor_ref.shape[0]):
        group = pl.ds(g * rows, rows)
        normed_ref[group, :] = (
            raw_ref[group, :].astype(F32) * factor_ref[g] * gain_ref[...]
        ).astype(BF16)
    start = pl.multiple_of(index_ref[2 * count] * piece, piece)
    piece_ref[...] = raw_ref[pl.ds(start, piece), :]


def normalise(index, blocks, factor, gain, piece_rows):
    count = len(blocks) - 1
    rows = blocks[2].shape[0]
    groups = factor.shape[0]
    depth = gain.shape[1]
    whole = pl.BlockSpec(memory_space=pltpu.VMEM)
    return pl.pallas_call(
        functools.partial(normalise_kernel, count),
        in_specs=[pl.BlockSpec(memory_space=pltpu.SMEM)] + [whole] * (count + 3),
        out_specs=[whole, whole],
        out_shape=[
            jax.ShapeDtypeStruct((groups * rows, depth), BF16),
            jax.ShapeDtypeStruct((piece_rows, depth), BF16),
        ],
        scratch_shapes=[pltpu.VMEM((groups * rows, depth), BF16)],
        compiler_params=pltpu.CompilerParams(vmem_limit_bytes=16 * 2**20),
        cost_estimate=pl.CostEstimate(
            flops=3 * groups * rows * depth,
            bytes_accessed=4 * groups * rows * depth,
            transcendentals=0,
        ),
    )(index, factor, gain, *blocks)


def outer_kernel(count, chunks, tile, index_ref, chosen_ref, *refs):
    split = chunks * (count + 1)
    pieces, (out_ref, share_ref, grad_ref) = refs[:split], refs[split:]
    rows = pieces[2].shape[0]
    share = share_ref.shape[0]
    step = pl.program_id(0)

    @pl.when(step == 0)
    def _():
        for h in range(chunks):

            def put(k, ref, first):
                start = pl.multiple_of((h * count + index_ref[k]) * rows, rows)
                grad_ref[pl.ds(start, rows), pl.ds(first, ref.shape[1])] = ref[...]

            place_pieces(pieces[h * (count + 1) : (h + 1) * (count + 1)], put)
        start = pl.multiple_of(index_ref[count] * share, share)
        share_ref[...] = grad_ref[pl.ds(start, share), :]

    columns = pl.ds(pl.multiple_of(step * tile, tile), tile)
    out_ref[...] = lax.dot_general(
        grad_ref[:, columns], chosen_ref[...], (((0,), (0,)), ((), ())), preferred_element_type=F32
    )


def outer(index, chosen, chunks, share_rows):
    count = len(chunks[0]) - 1
    depth = chunks[0][2].shape[1]
    all_rows, joined = chosen.shape
    tile = min(depth, 256)
    whole = pl.BlockSpec(memory_space=pltpu.VMEM)
    return pl.pallas_call(
        functools.partial(outer_kernel, count, len(chunks), tile),
        grid=(depth // tile,),
        in_specs=[pl.BlockSpec(memory_space=pltpu.SMEM), whole]
        + [whole] * (len(chunks) * (count + 1)),
        out_specs=[
            pl.BlockSpec((tile, joined), lambda n: (n, 0)),
            pl.BlockSpec((share_rows, depth), lambda n: (0, 0)),
        ],
        out_shape=[
            jax.ShapeDtypeStruct((depth, joined), F32),
            jax.ShapeDtypeStruct((share_rows, depth), BF16),
        ],
        scratch_shapes=[pltpu.VMEM((all_rows, depth), BF16)],
        compiler_params=pltpu.CompilerParams(vmem_limit_bytes=40 * 2**20),
        cost_estimate=pl.CostEstimate(
            flops=2 * all_rows * depth * joined,
            bytes_accessed=4 * depth * joined + 2 * all_rows * (depth + joined),
            transcendentals=0,
        ),
    )(index, chosen, *[x for pieces in chunks for x in pieces])


def device_table(groups, ring, slots, widths):
    group_rows, chunk_rows, piece_rows, slice_width = widths
    parts = ring.size
    step_rows = piece_rows * parts
    share_rows = group_rows // slots
    rows = []
    for g in range(groups.size):
        for v in range(parts):
            p = ring.place[v]
            sources = ring.sources(v)
            held = [ring.order[q] for q in sources]
            group = [(i // slots % groups.chips) * CORES + i // slots // groups.chips for i in held]
            row = [groups.entry(g, i) for i in group] + [i % slots for i in held] + [p]
            row += sources
            entry = groups.entry(g, v * share_rows // group_rows)
            first = v * share_rows % group_rows
            start = first // chunk_rows * step_rows + entry * chunk_rows + first % chunk_rows
            row += [start // share_rows]
            row += [(p + t) % parts * piece_rows for t in range(parts)]
            row += [
                g * slice_width,
                p * piece_rows // chunk_rows,
                p * piece_rows % chunk_rows,
                2 * p,
            ]
            rows.append(row)
    return np.asarray(rows, np.int32).reshape(groups.size, parts, -1)


def after(x, *others):
    return lax.optimization_barrier((x, others))[0]


def body(hidden, norm_gain, head_weight, target_logits, valid_rows, parents, features):
    groups = Groups(lax.axis_size("dp"))
    parts = lax.axis_size("vocab")
    ring = Ring(parts, groups.chips)
    group_rows, block_width = hidden.shape
    chunk_rows = group_rows // CHUNKS
    step_rows = groups.size * chunk_rows
    piece_rows = step_rows // parts
    model_width = block_width * parts
    slots = parts // groups.size
    slice_width = block_width * slots
    vocab_width = target_logits.shape[1]

    table = device_table(
        groups, ring, slots, (group_rows, chunk_rows, piece_rows, slice_width)
    )
    table = lax.dynamic_slice(
        jnp.asarray(table),
        (lax.axis_index("dp"), lax.axis_index("vocab"), 0),
        (1, 1, table.shape[2]),
    ).reshape(-1)
    place_index = table[: 2 * parts + 1]
    piece_index = table[2 * parts + 1 : 3 * parts + 2]
    starts = table[3 * parts + 2 :].astype(jnp.uint32)
    gain_start, own_entry, own_first, own_lane = [starts[parts + k] for k in range(4)]

    def chunk(x, h):
        return x[h * chunk_rows : (h + 1) * chunk_rows]

    def column_owner(g, v):
        far = g % CORES * groups.chips + g // CORES
        return v // slots * parts + far * slots + v % slots

    turn = [
        (g * parts + v, column_owner(g, v)) for g in range(groups.size) for v in range(parts)
    ]
    turned = [lax.ppermute(chunk(hidden, h), ("dp", "vocab"), turn) for h in range(CHUNKS)]

    live_rows = (valid_rows == 1).astype(F32)
    targets = target_logits.astype(F32)
    target_top = jnp.max(targets, axis=1)
    target_total = jnp.sum(jnp.exp(targets - target_top[:, None]), axis=1)
    square_part = jnp.sum(jnp.square(hidden.astype(F32)), axis=1)

    def merge_totals(a, b):
        top = jnp.maximum(a[-2], b[-2])
        total = a[-1] * jnp.exp(a[-2] - top) + b[-1] * jnp.exp(b[-2] - top)
        return jnp.concatenate([a[:-2] + b[:-2], jnp.stack([top, total])])

    met = ring.meet(jnp.stack([square_part, target_top, target_total]), merge_totals)
    target_scale = jnp.exp(target_top - met[1]) / met[2]
    both = groups.gather(jnp.stack([met[0], live_rows]))
    valid_count = jnp.sum(both[:, 1])
    row_factor = lax.rsqrt(both[:, 0] / model_width + 1e-05)

    tree_rows = jnp.arange(group_rows, dtype=jnp.int32) // TREE * TREE + parents
    own_chosen = features.at[tree_rows].get(mode="promise_in_bounds")

    gain = lax.dynamic_slice(norm_gain, (gain_start,), (slice_width,)).reshape(1, slice_width)
    row_weight = 1048576.0 * live_rows / valid_count
    lane = lax.broadcasted_iota(jnp.uint32, (chunk_rows, LANES), 1)

    def group_logits(h, blocks):
        factor = row_factor[:, h * chunk_rows : (h + 1) * chunk_rows]
        normed, piece = normalise(place_index, blocks, factor[:, :, None], gain, piece_rows)
        pieces.append(piece)
        own = lax.dot_general(
            normed, head_weight, (((1,), (1,)), ((), ())), preferred_element_type=F32
        )
        yield own
        half = step_rows // CORES
        summed = own[:half] + groups.swap(own[half:])
        yield summed
        summed = summed.reshape(groups.chips, chunk_rows, vocab_width)
        logits = summed[0]
        for d in range(1, groups.chips):
            logits = logits + groups.shift(summed[d], d)
        yield logits

    gathered, logits_of, pieces = [], [], []
    for h in range(CHUNKS):
        waits = None
        if h > 0:
            stages = group_logits(h - 1, gathered[-1])
            waits = {
                0: lambda: (gathered[-1],),
                1: lambda: (next(stages),),
                2: lambda: (next(stages),),
            }
        gathered.append(ring.gather(turned[h], waits))
        if h > 0:
            logits_of.append(list(stages)[-1])
    logits_of.append(list(group_logits(CHUNKS - 1, gathered[-1]))[-1])

    grads = []
    for h in range(CHUNKS):
        logits = logits_of[h]
        factor = row_factor[:, h * chunk_rows : (h + 1) * chunk_rows]
        top = jnp.max(logits, axis=1)
        total = jnp.sum(jnp.exp(logits - top[:, None]), axis=1)
        met = ring.meet(jnp.stack([top, total]), merge_totals)
        scale = jnp.exp(top - met[0]) / met[1]
        draft_probs = jnp.exp(logits - top[:, None]) * scale[:, None]
        target_probs = (
            jnp.exp(chunk(targets, h) - chunk(target_top, h)[:, None])
            * chunk(target_scale, h)[:, None]
        )
        logit_grad = chunk(row_weight, h)[:, None] * (draft_probs - target_probs)
        logit_grad = lax.reduce_precision(logit_grad, 8, 7)
        dot_part = jnp.sum(logit_grad * logits, axis=1)
        dot_high = lax.reduce_precision(dot_part, 8, 7)
        dot_low = dot_part - dot_high
        lanes = jnp.where(lane == own_lane, dot_high[:, None], 0.0) + jnp.where(
            lane == own_lane + 1, dot_low[:, None], 0.0
        )
        message = jnp.concatenate([logit_grad.astype(BF16), lanes.astype(BF16)], axis=1)
        everyone = groups.gather(message).reshape(step_rows, vocab_width + LANES)
        if h == CHUNKS - 1:
            chosen = groups.gather(after(own_chosen, everyone).reshape(CHUNKS, chunk_rows, -1))
            chosen = chosen.transpose(1, 0, 2, 3).reshape(CHUNKS * step_rows, -1)
        normed_grad = jnp.dot(
            everyone[:, :vocab_width], head_weight, preferred_element_type=F32
        )
        dots = everyone[:, vocab_width:]

        def part(t):
            start = (starts[t % parts], jnp.uint32(0))
            return jnp.concatenate(
                [
                    lax.dynamic_slice(normed_grad, start, (piece_rows, slice_width)),
                    lax.dynamic_slice(dots, start, (piece_rows, LANES)).astype(F32),
                ],
                axis=1,
            )

        summed = ring.scatter_sum(part)
        own_factor = lax.dynamic_slice(factor, (own_entry, own_first), (1, piece_rows))[0]
        row_dot = jnp.sum(summed[:, slice_width:], axis=1) / own_factor
        grad_piece = (
            own_factor[:, None] * gain * summed[:, :slice_width]
            - pieces[h].astype(F32) * (own_factor**3 * row_dot / model_width)[:, None]
        ).astype(BF16)
        grads.append(ring.gather(grad_piece))

    grad_joining, grad_share = outer(piece_index, chosen, grads, group_rows // slots)
    return (grad_share, grad_joining)


def solution(mesh):
    placed = (
        P("dp", "vocab"),
        P(),
        P("vocab", "dp"),
        P("dp", "vocab"),
        P("dp"),
        P("dp"),
        P("dp", "vocab"),
    )
    return jax.shard_map(
        body,
        mesh=mesh,
        in_specs=placed,
        out_specs=(P("vocab", "dp"), P("dp", "vocab")),
        check_vma=False,
    )
```

time: 227 us -> 236 us (1.040)
  between operations: 21.1 us -> 2.02 us
  waiting for transfers between devices: 50.2 us -> 65.9 us
  Pallas kernels: 1.7 us -> 14.3 us
  matrix products: 28.8 us -> 19.8 us
  other arithmetic: 19.2 us -> 26.7 us
  starting transfers between devices: 84.7 us -> 87.2 us
    ppermute x48, waiting for transfers between devices: 22.9 us -> 39.3 us  [shift(): lax.ppermute(x, 'vocab', [(order[p], order[(p + step) % size]) for p in r...]
    pallas_call x2 -> x3, Pallas kernels: 1.7 us -> 14.3 us  [the longest x1 12.6 us: outer(): pl.pallas_call(functools.partial(outer_kernel, count, len(chunks), tile),...]
    dot_general x1 -> x0, matrix products: 12.5 us -> none  [body(): lax.dot_general(grad_all, chosen, (((0,), (0,)), ((), ())), preferred_ele...]
    dynamic_slice x0 -> x2, other arithmetic: none -> 9.69 us  [part(): lax.dynamic_slice(dots, start, (piece_rows, LANES)).astype(F32)]
    unnamed x76 -> x18, local copies, waits for them, and re-layouts: 8.09 us -> 0.06 us
    dynamic_slice x5 -> x4, local copies, waits for them, and re-layouts: 2.3 us -> 9.82 us  [the longest x2 7.7 us: part(): lax.dynamic_slice(normed_grad, start, (piece_rows, slice_width))]
    ppermute x9, starting transfers between devices: 15.2 us -> 19.5 us  [partner(): return lax.ppermute(x, 'vocab', [(v, v ^ bit) for v in range(self.size)])]
    another operation x7 -> x4, local copies, waits for them, and re-layouts: 0.18 us -> 3.63 us  [the longest x1 0.08 us: body(): jnp.stack([slot_entry(g, k) for g in groups.order for k in range(slots)])]
  transfers between devices with their start and end apart: 71 -> 71, of which waited for: 34 -> 38; matrix products, arithmetic and copies ran while one was open for 18% -> 14% of each run, Pallas kernels for 0% -> 0%
where the time goes in v4:
time: 236 us; the launch traced here: 235 us
  starting transfers between devices  87.2 us (37%)
  waiting for transfers between devices  65.9 us (28%)
  other arithmetic  26.7 us (11%)
  matrix products  19.8 us (8%)
  local copies, waits for them, and re-layouts  19.4 us (8%)
  Pallas kernels  14.3 us (6%)
    ppermute x48, starting transfers between devices, shift(): lax.ppermute(x, 'vocab', [(order[p], order[(p + step) % size]) for p in r...  57.4 us
    ppermute x48, waiting for transfers between devices, shift(): lax.ppermute(x, 'vocab', [(order[p], order[(p + step) % size]) for p in r...  39.3 us
    ppermute x9, starting transfers between devices, partner(): return lax.ppermute(x, 'vocab', [(v, v ^ bit) for v in range(self.size)])  19.5 us
    ppermute x6, waiting for transfers between devices, shift(): lax.ppermute(x, 'dp', [(i, (i + CORES * step) % size) for i in range(size)])  17.5 us
    pallas_call x1, Pallas kernels, outer(): pl.pallas_call(functools.partial(outer_kernel, count, len(chunks), tile),...  12.6 us
    dot_general x2, matrix products, group_logits(): lax.dot_general(normed, head_weight, (((1,), (1,)), ((), ())), preferred_...  11.5 us
    dynamic_slice x2, other arithmetic, part(): lax.dynamic_slice(dots, start, (piece_rows, LANES)).astype(F32)  9.69 us
    ppermute x9, waiting for transfers between devices, partner(): return lax.ppermute(x, 'vocab', [(v, v ^ bit) for v in range(self.size)])  9.18 us
  transfers between devices with their start and end apart: 71, of which 38 were waited for; matrix products, arithmetic and copies ran while one was open for 14% of the time, Pallas kernels for 0%

profile of v4, /device:TPU:0, one launch (start us, length us, event | category | flops | bytes accessed | tf_op | source)
XLA Modules:
  0.0 235.3 jit_solution(7208722948362238334)
XLA Ops:
  5.4 3.0 %collective-permute-start = (f32[3,128]{1,0:T(4,128)S(1)}, f32[3,128]{1,0:T(4,128)S(1)}, u32[]{:S(2)}, u32[]{:S(2)}) collective-permute-start(f32[3,128]{1,0:T(4,128)S(1)} %pad_maximum_fusion.15), channel_id=1, source_target_pairs={{0,1},{1,0},{2,3},{3,2},{4,5},{5,4},{6,7},{7,6},{8,9},{9,8},{10,11... | collective-permute-start | bytes 4616 | tf_op jit(solution)/shard_map/ppermute | solution.py:50
  10.0 3.4 %collective-permute-start.1 = (f32[3,128]{1,0:T(4,128)S(1)}, f32[3,128]{1,0:T(4,128)S(1)}, u32[]{:S(2)}, u32[]{:S(2)}) collective-permute-start(f32[3,128]{1,0:T(4,128)S(1)} %pad_maximum_fusion.16), channel_id=1, source_target_pairs={{0,2},{1,3},{2,0},{3,1},{4,6},{5,7},{6,4},{7,5},{8,10},{9,11},{10,... | collective-permute-start | bytes 4616 | tf_op jit(solution)/shard_map/ppermute | solution.py:50
  13.4 1.6 collective-permute-done.1
  15.0 4.3 %collective-permute-start.2 = (f32[3,128]{1,0:T(4,128)S(1)}, f32[3,128]{1,0:T(4,128)S(1)}, u32[]{:S(2)}, u32[]{:S(2)}) collective-permute-start(f32[3,128]{1,0:T(4,128)S(1)} %pad_maximum_fusion.17), channel_id=1, source_target_pairs={{0,4},{1,5},{2,6},{3,7},{4,0},{5,1},{6,2},{7,3},{8,12},{9,13},{10,... | collective-permute-start | bytes 4616 | tf_op jit(solution)/shard_map/ppermute | solution.py:50
  19.3 1.6 collective-permute-done.2
  20.9 2.2 collective-permute-start.3
  23.1 1.5 collective-permute-start.11
  25.2 2.8 %collective-permute-done.11.refs_6_ = bf16[64,1024]{1,0:T(8,128)(2,1)S(1)} collective-permute-done((bf16[64,1024]{1,0:T(8,128)(2,1)S(1)}, bf16[64,1024]{1,0:T(8,128)(2,1)S(1)}, u32[]{:S(2)}, u32[]{:S(2)}) %collective-permute-start.11) | collective-permute-done | bytes 131104 | tf_op jit(solution)/shard_map/ppermute | solution.py:45
  32.2 1.6 collective-permute-done.12.refs_7_
  33.8 1.7 collective-permute-start.13
  36.7 2.5 %collective-permute-done.13.refs_8_ = bf16[64,1024]{1,0:T(8,128)(2,1)S(1)} collective-permute-done((bf16[64,1024]{1,0:T(8,128)(2,1)S(1)}, bf16[64,1024]{1,0:T(8,128)(2,1)S(1)}, u32[]{:S(2)}, u32[]{:S(2)}) %collective-permute-start.13) | collective-permute-done | bytes 131104 | tf_op jit(solution)/shard_map/ppermute | solution.py:45
  41.5 2.0 collective-permute-done.14.refs_1_
  45.7 5.7 %fusion.130 = f32[256,2048]{1,0:T(8,128)S(1)} fusion(bf16[256,2048]{1,0:T(8,128)(2,1)S(1)} %get-tuple-element.15, bf16[2048,2048]{1,0:T(8,128)(2,1)} %param.10), kind=kOutput, calls=%fused_computation.287 | convolution fusion | flops 2147483648 | bytes 11534336 | tf_op jit(solution)/shard_map/dot_general | solution.py:319
  53.7 8.9 %collective-permute-start.15 = (bf16[64,1024]{1,0:T(8,128)(2,1)S(1)}, bf16[64,1024]{1,0:T(8,128)(2,1)S(1)}, u32[]{:S(2)}, u32[]{:S(2)}) collective-permute-start(bf16[64,1024]{1,0:T(8,128)(2,1)S(1)} %collective-permute-done.5.refs_5_), channel_id=1, source_target_pairs={{0,2},{2,4},{4,6},{6,7},{7,5},{5,3},{3,1},{1,0},{8,10},{10,12},{12... | collective-permute-start | bytes 393224 | tf_op jit(solution)/shard_map/ppermute | solution.py:45
  63.3 3.1 %collective-permute-done.20.refs_6_ = bf16[64,1024]{1,0:T(8,128)(2,1)S(1)} collective-permute-done((bf16[64,1024]{1,0:T(8,128)(2,1)S(1)}, bf16[64,1024]{1,0:T(8,128)(2,1)S(1)}, u32[]{:S(2)}, u32[]{:S(2)}) %collective-permute-start.20) | collective-permute-done | bytes 131104 | tf_op jit(solution)/shard_map/ppermute | solution.py:45
  69.6 2.7 %slice_add_fusion.1 = f32[128,2048]{1,0:T(8,128)} fusion(f32[128,2048]{1,0:T(8,128)} %collective-permute-done.17, f32[256,2048]{1,0:T(8,128)} %copy-done.3), kind=kLoop, calls=%fused_computation.10 | loop fusion | flops 262144 | bytes 3145728 | tf_op jit(solution)/shard_map/add | solution.py:324
  72.3 1.7 collective-permute-done.21.refs_7_
  76.0 2.9 %collective-permute-done.18.refs_2_ = bf16[64,1024]{1,0:T(8,128)(2,1)S(1)} collective-permute-done((bf16[64,1024]{1,0:T(8,128)(2,1)S(1)}, bf16[64,1024]{1,0:T(8,128)(2,1)S(1)}, u32[]{:S(2)}, u32[]{:S(2)}) %collective-permute-start.18) | collective-permute-done | bytes 131104 | tf_op jit(solution)/shard_map/ppermute | solution.py:45
  79.6 1.6 collective-permute-start.23
  85.3 5.7 %fusion.131 = f32[256,2048]{1,0:T(8,128)S(1)} fusion(bf16[256,2048]{1,0:T(8,128)(2,1)S(1)} %get-tuple-element.20, bf16[2048,2048]{1,0:T(8,128)(2,1)} %param.10), kind=kOutput, calls=%fused_computation.288 | convolution fusion | flops 2147483648 | bytes 11534336 | tf_op jit(solution)/shard_map/dot_general | solution.py:319
  92.0 2.3 collective-permute-done.33
  96.2 1.8 collective-permute-start.25
  99.0 9.6 %collective-permute-done.25 = f32[64,2048]{1,0:T(8,128)S(1)} collective-permute-done((f32[64,2048]{1,0:T(8,128)S(1)}, f32[64,2048]{1,0:T(8,128)S(1)}, u32[]{:S(2)}, u32[]{:S(2)}) %collective-permute-start.25) | collective-permute-done | bytes 524320 | tf_op jit(solution)/shard_map/ppermute | solution.py:108
  110.4 2.3 collective-permute-done.26
  116.3 2.5 %collective-permute-start.28 = (f32[2,64]{1,0:T(2,128)S(1)}, f32[2,64]{1,0:T(2,128)S(1)}, u32[]{:S(2)}, u32[]{:S(2)}) collective-permute-start(f32[2,64]{1,0:T(2,128)S(1)} %pad_maximum_fusion.22), channel_id=1, source_target_pairs={{0,4},{1,5},{2,6},{3,7},{4,0},{5,1},{6,2},{7,3},{8,12},{9,13},{10,... | collective-permute-start | bytes 1544 | tf_op jit(solution)/shard_map/ppermute | solution.py:50
  118.9 2.0 collective-permute-done.28
  124.9 4.6 %collective-permute-done.29 = bf16[64,2176]{1,0:T(8,128)(2,1)S(1)} collective-permute-done((bf16[64,2176]{1,0:T(8,128)(2,1)S(1)}, bf16[64,2176]{1,0:T(8,128)(2,1)S(1)}, u32[]{:S(2)}, u32[]{:S(2)}) %collective-permute-start.29) | collective-permute-done | bytes 278560 | tf_op jit(solution)/shard_map/ppermute | solution.py:108
  132.8 6.0 %fusion = f32[256,2048]{1,0:T(8,128)S(1)} fusion(bf16[2048,2048]{1,0:T(8,128)(2,1)} %param.10, bf16[256,2176]{1,0:T(8,128)(2,1)S(1)} %bitcast.293), kind=kOutput, calls=%fused_computation.5 | convolution fusion | flops 2147483648 | bytes 11534336 | tf_op jit(solution)/shard_map/dot_general | solution.py:373
  138.9 2.3 fusion.2
  144.2 3.8 %constant_dynamic-slice_fusion.9 = (f32[32,2048]{1,0:T(8,128)S(1)}, f32[32,2048]{1,0:T(8,128)S(1)}, f32[32,2048]{1,0:T(8,128)S(1)}, f32[32,2048]{1,0:T(8,128)S(1...) fusion(f32[256,2048]{1,0:T(8,128)S(1)} %fusion, u32[]{:T(128)} %bitcast.54, u32[]{:T(128)} %bitcast.59, u32[]{:T(128)} %bitcast.58, ...), kind=kLoop, calls=%fused_computation.103 | loop fusion | bytes 3145752 | tf_op jit(solution)/shard_map/dynamic_slice | solution.py:382
  148.1 3.8 %constant_dynamic-slice_fusion.23 = (f32[32,2048]{1,0:T(8,128)S(1)}, f32[32,2048]{1,0:T(8,128)S(1)}, f32[32,2048]{1,0:T(8,128)S(1)}, f32[32,2048]{1,0:T(8,128)S(...) fusion(f32[256,2048]{1,0:T(8,128)S(1)} %fusion.2, u32[]{:T(128)} %bitcast.54, u32[]{:T(128)} %bitcast.59, ...), kind=kLoop, calls=%fused_computation.117 | loop fusion | bytes 3145752 | tf_op jit(solution)/shard_map/dynamic_slice | solution.py:382
  152.0 4.8 %constant_dynamic-slice_fusion.21 = (bf16[32,128]{1,0:T(8,128)(2,1)S(1)}, bf16[32,128]{1,0:T(8,128)(2,1)S(1)}, f32[32,128]{1,0:T(8,128)S(1)}, f32[32,128]{1,0:T(...) fusion(bf16[256,128]{1,0:T(8,128)(2,1)S(1)} %slice.413, ...), kind=kLoop, calls=%fused_computation.115 | loop fusion | flops 24576 | bytes 180256 | tf_op jit(solution)/shard_map/dynamic_slice | solution.py:383
  156.8 4.8 %constant_dynamic-slice_fusion.7 = (bf16[32,128]{1,0:T(8,128)(2,1)S(1)}, bf16[32,128]{1,0:T(8,128)(2,1)S(1)}, f32[32,128]{1,0:T(8,128)S(1)}, f32[32,128]{1,0:T(8...) fusion(bf16[256,128]{1,0:T(8,128)(2,1)S(1)} %slice.420, ...), kind=kLoop, calls=%fused_computation.101 | loop fusion | flops 24576 | bytes 180256 | tf_op jit(solution)/shard_map/dynamic_slice | solution.py:383
  175.7 2.1 collective-permute-done.40
  182.4 2.2 collective-permute-done.41
  187.5 1.8 collective-permute-start.46
  190.6 2.0 collective-permute-done.46
  196.0 1.8 collective-permute-start.67
  198.1 1.7 collective-permute-start.51
  200.1 2.2 collective-permute-done.67.refs_15_
  202.3 1.7 collective-permute-start.68
  205.1 1.7 collective-permute-start.52
  208.0 1.7 collective-permute-start.69
  211.6 1.7 collective-permute-start.53
  214.5 1.7 collective-permute-start.70
  216.7 1.7 collective-permute-start.54
  221.0 1.8 collective-permute-done.50.refs_0_
  222.8 12.6 %shard_map.97 = (f32[2048,3072]{1,0:T(8,128)}, bf16[64,2048]{1,0:T(8,128)(2,1)}) custom-call(s32[9]{0:T(128)S(1)} %slice_bitcast_fusion.1.index_ref, bf16[512,3072]{1,0:T(8,128)(2,1)S(1)} %bitcast.284, bf16[32,1024]{1,0:T(8,128)(2,1)S(1)} %collective-permute-done.50.refs_0_, bf16[32,1024]{1,0:T(8,128)(2,1)S(1)} %collective-permute-done.54.refs_1_, ...), custom_call_target="tpu_custom_call" | custom-call | flops 6442450944 | bytes 30408704 | tf_op jit(solution)/shard_map/pallas_call | solution.py:197
  (234 shorter events, 83.7 us)
Async XLA Ops:
  1.8 21.3 %collective-permute-start.6 = (bf16[64,1024]{1,0:T(8,128)(2,1)S(1)}, bf16[64,1024]{1,0:T(8,128)(2,1)S(1)}, u32[]{:S(2)}, u32[]{:S(2)}) collective-permute-start(bf16[64,1024]{1,0:T(8,128)(2,1)S(1)} %get-tuple-element.68), channel_id=1, source_target_pairs={{0,0},{1,1},{2,8},{3,9},{4,16},{5,17},{6,24},{7,25},{8,4},{9,5},{1... | collective-permute-start | bytes 393224 | tf_op jit(solution)/shard_map/ppermute | solution.py:289
  15.0 5.9 %collective-permute-start.2 = (f32[3,128]{1,0:T(4,128)S(1)}, f32[3,128]{1,0:T(4,128)S(1)}, u32[]{:S(2)}, u32[]{:S(2)}) collective-permute-start(f32[3,128]{1,0:T(4,128)S(1)} %pad_maximum_fusion.17), channel_id=1, source_target_pairs={{0,4},{1,5},{2,6},{3,7},{4,0},{5,1},{6,2},{7,3},{8,12},{9,13},{10,... | collective-permute-start | bytes 4616 | tf_op jit(solution)/shard_map/ppermute | solution.py:50
  24.6 5.0 %collective-permute-start.7 = (bf16[64,1024]{1,0:T(8,128)(2,1)S(1)}, bf16[64,1024]{1,0:T(8,128)(2,1)S(1)}, u32[]{:S(2)}, u32[]{:S(2)}) collective-permute-start(bf16[64,1024]{1,0:T(8,128)(2,1)S(1)} %collective-permute-done.6.refs_5_), channel_id=1, source_target_pairs={{0,2},{2,4},{4,6},{6,7},{7,5},{5,3},{3,1},{1,0},{8,10},{10,12},{12... | collective-permute-start | bytes 393224 | tf_op jit(solution)/shard_map/ppermute | solution.py:45
  25.2 7.0 %collective-permute-start.4 = (f32[2,2,128]{2,1,0:T(2,128)S(1)}, f32[2,2,128]{2,1,0:T(2,128)S(1)}, u32[]{:S(2)}, u32[]{:S(2)}) collective-permute-start(f32[2,2,128]{2,1,0:T(2,128)S(1)} %pad_maximum_fusion.18), channel_id=1, source_target_pairs={{0,8},{8,0},{16,24},{24,16},{1,9},{9,1},{17,25},{25,17},{2,10},{10... | collective-permute-start | bytes 6152 | tf_op jit(solution)/shard_map/ppermute | solution.py:104
  28.1 5.8 %collective-permute-start.12 = (bf16[64,1024]{1,0:T(8,128)(2,1)S(1)}, bf16[64,1024]{1,0:T(8,128)(2,1)S(1)}, u32[]{:S(2)}, u32[]{:S(2)}) collective-permute-start(bf16[64,1024]{1,0:T(8,128)(2,1)S(1)} %collective-permute-done.11.refs_6_), channel_id=1, source_target_pairs={{0,1},{2,0},{4,2},{6,4},{7,6},{5,7},{3,5},{1,3},{8,9},{10,8},{12,1... | collective-permute-start | bytes 393224 | tf_op jit(solution)/shard_map/ppermute | solution.py:45
  29.6 6.1 %collective-permute-start.8 = (bf16[64,1024]{1,0:T(8,128)(2,1)S(1)}, bf16[64,1024]{1,0:T(8,128)(2,1)S(1)}, u32[]{:S(2)}, u32[]{:S(2)}) collective-permute-start(bf16[64,1024]{1,0:T(8,128)(2,1)S(1)} %collective-permute-done.7.refs_4_), channel_id=1, source_target_pairs={{0,2},{2,4},{4,6},{6,7},{7,5},{5,3},{3,1},{1,0},{8,10},{10,12},{12... | collective-permute-start | bytes 393224 | tf_op jit(solution)/shard_map/ppermute | solution.py:45
  33.8 5.4 %collective-permute-start.13 = (bf16[64,1024]{1,0:T(8,128)(2,1)S(1)}, bf16[64,1024]{1,0:T(8,128)(2,1)S(1)}, u32[]{:S(2)}, u32[]{:S(2)}) collective-permute-start(bf16[64,1024]{1,0:T(8,128)(2,1)S(1)} %collective-permute-done.12.refs_7_), channel_id=1, source_target_pairs={{0,1},{2,0},{4,2},{6,4},{7,6},{5,7},{3,5},{1,3},{8,9},{10,8},{12,1... | collective-permute-start | bytes 393224 | tf_op jit(solution)/shard_map/ppermute | solution.py:45
  52.7 16.9 %collective-permute-start.17 = (f32[128,2048]{1,0:T(8,128)}, f32[128,2048]{1,0:T(8,128)}, u32[]{:S(2)}, u32[]{:S(2)}) collective-permute-start(f32[128,2048]{1,0:T(8,128)} %slice.401), channel_id=1, source_target_pairs={{0,8},{8,0},{16,24},{24,16},{1,9},{9,1},{17,25},{25,17},{2,10},{10... | collective-permute-start | bytes 3145736 | tf_op jit(solution)/shard_map/ppermute | solution.py:104
  53.4 13.0 %collective-permute-start.20 = (bf16[64,1024]{1,0:T(8,128)(2,1)S(1)}, bf16[64,1024]{1,0:T(8,128)(2,1)S(1)}, u32[]{:S(2)}, u32[]{:S(2)}) collective-permute-start(bf16[64,1024]{1,0:T(8,128)(2,1)S(1)} %collective-permute-done.5.refs_5_), channel_id=1, source_target_pairs={{0,1},{2,0},{4,2},{6,4},{7,6},{5,7},{3,5},{1,3},{8,9},{10,8},{12,1... | collective-permute-start | bytes 393224 | tf_op jit(solution)/shard_map/ppermute | solution.py:45
  53.7 13.8 %collective-permute-start.15 = (bf16[64,1024]{1,0:T(8,128)(2,1)S(1)}, bf16[64,1024]{1,0:T(8,128)(2,1)S(1)}, u32[]{:S(2)}, u32[]{:S(2)}) collective-permute-start(bf16[64,1024]{1,0:T(8,128)(2,1)S(1)} %collective-permute-done.5.refs_5_), channel_id=1, source_target_pairs={{0,2},{2,4},{4,6},{6,7},{7,5},{5,3},{3,1},{1,0},{8,10},{10,12},{12... | collective-permute-start | bytes 393224 | tf_op jit(solution)/shard_map/ppermute | solution.py:45
  67.6 6.4 %collective-permute-start.16 = (bf16[64,1024]{1,0:T(8,128)(2,1)S(1)}, bf16[64,1024]{1,0:T(8,128)(2,1)S(1)}, u32[]{:S(2)}, u32[]{:S(2)}) collective-permute-start(bf16[64,1024]{1,0:T(8,128)(2,1)S(1)} %collective-permute-done.15.refs_4_), channel_id=1, source_target_pairs={{0,2},{2,4},{4,6},{6,7},{7,5},{5,3},{3,1},{1,0},{8,10},{10,12},{12... | collective-permute-start | bytes 393224 | tf_op jit(solution)/shard_map/ppermute | solution.py:45
  68.7 5.2 %collective-permute-start.21 = (bf16[64,1024]{1,0:T(8,128)(2,1)S(1)}, bf16[64,1024]{1,0:T(8,128)(2,1)S(1)}, u32[]{:S(2)}, u32[]{:S(2)}) collective-permute-start(bf16[64,1024]{1,0:T(8,128)(2,1)S(1)} %collective-permute-done.20.refs_6_), channel_id=1, source_target_pairs={{0,1},{2,0},{4,2},{6,4},{7,6},{5,7},{3,5},{1,3},{8,9},{10,8},{12,1... | collective-permute-start | bytes 393224 | tf_op jit(solution)/shard_map/ppermute | solution.py:45
  74.6 5.0 %collective-permute-start.22 = (bf16[64,1024]{1,0:T(8,128)(2,1)S(1)}, bf16[64,1024]{1,0:T(8,128)(2,1)S(1)}, u32[]{:S(2)}, u32[]{:S(2)}) collective-permute-start(bf16[64,1024]{1,0:T(8,128)(2,1)S(1)} %collective-permute-done.21.refs_7_), channel_id=1, source_target_pairs={{0,1},{2,0},{4,2},{6,4},{7,6},{5,7},{3,5},{1,3},{8,9},{10,8},{12,1... | collective-permute-start | bytes 393224 | tf_op jit(solution)/shard_map/ppermute | solution.py:45
  78.9 5.5 %collective-permute-start.19 = (bf16[64,512]{1,0:T(8,128)(2,1)S(1)}, bf16[64,512]{1,0:T(8,128)(2,1)S(1)}, u32[]{:S(2)}, u32[]{:S(2)}) collective-permute-start(bf16[64,512]{1,0:T(8,128)(2,1)S(1)} %slice.402), channel_id=1, source_target_pairs={{0,2},{2,4},{4,6},{6,7},{7,5},{5,3},{3,1},{1,0},{8,10},{10,12},{12... | collective-permute-start | bytes 196616 | tf_op jit(solution)/shard_map/ppermute | solution.py:45
  83.1 11.2 %collective-permute-start.33 = (f32[64,2048]{1,0:T(8,128)S(1)}, f32[64,2048]{1,0:T(8,128)S(1)}, u32[]{:S(2)}, u32[]{:S(2)}) collective-permute-start(f32[64,2048]{1,0:T(8,128)S(1)} %slice.410), channel_id=1, source_target_pairs={{0,16},{8,24},{16,0},{24,8},{1,17},{9,25},{17,1},{25,9},{2,18},{10... | collective-permute-start | bytes 1572872 | tf_op jit(solution)/shard_map/ppermute | solution.py:108
  96.2 12.4 %collective-permute-start.25 = (f32[64,2048]{1,0:T(8,128)S(1)}, f32[64,2048]{1,0:T(8,128)S(1)}, u32[]{:S(2)}, u32[]{:S(2)}) collective-permute-start(f32[64,2048]{1,0:T(8,128)S(1)} %slice.407), channel_id=1, source_target_pairs={{0,16},{8,24},{16,0},{24,8},{1,17},{9,25},{17,1},{25,9},{2,18},{10... | collective-permute-start | bytes 1572872 | tf_op jit(solution)/shard_map/ppermute | solution.py:108
  98.4 12.0 %collective-permute-start.35 = (f32[2,64]{1,0:T(2,128)S(1)}, f32[2,64]{1,0:T(2,128)S(1)}, u32[]{:S(2)}, u32[]{:S(2)}) collective-permute-start(f32[2,64]{1,0:T(2,128)S(1)} %pad_maximum_fusion.24), channel_id=1, source_target_pairs={{0,2},{1,3},{2,0},{3,1},{4,6},{5,7},{6,4},{7,5},{8,10},{9,11},{10,... | collective-permute-start | bytes 1544 | tf_op jit(solution)/shard_map/ppermute | solution.py:50
  122.0 7.4 %collective-permute-start.29 = (bf16[64,2176]{1,0:T(8,128)(2,1)S(1)}, bf16[64,2176]{1,0:T(8,128)(2,1)S(1)}, u32[]{:S(2)}, u32[]{:S(2)}) collective-permute-start(bf16[64,2176]{1,0:T(8,128)(2,1)S(1)} %get-tuple-element.67), channel_id=1, source_target_pairs={{0,16},{8,24},{16,0},{24,8},{1,17},{9,25},{17,1},{25,9},{2,18},{10... | collective-permute-start | bytes 835592 | tf_op jit(solution)/shard_map/ppermute | solution.py:108
  123.5 8.9 %collective-permute-start.37 = (bf16[64,2176]{1,0:T(8,128)(2,1)}, bf16[64,2176]{1,0:T(8,128)(2,1)S(1)}, u32[]{:S(2)}, u32[]{:S(2)}) collective-permute-start(bf16[64,2176]{1,0:T(8,128)(2,1)} %get-tuple-element.65), channel_id=1, source_target_pairs={{0,16},{8,24},{16,0},{24,8},{1,17},{9,25},{17,1},{25,9},{2,18},{10... | collective-permute-start | bytes 835592 | tf_op jit(solution)/shard_map/ppermute | solution.py:108
  132.5 6.2 %collective-permute-start.38 = (bf16[2,64,2176]{2,1,0:T(8,128)(2,1)S(1)}, bf16[2,64,2176]{2,1,0:T(8,128)(2,1)S(1)}, u32[]{:S(2)}, u32[]{:S(2)}) collective-permute-start(bf16[2,64,2176]{2,1,0:T(8,128)(2,1)S(1)} %pad_maximum_fusion.5), channel_id=1, source_target_pairs={{0,8},{8,0},{16,24},{24,16},{1,9},{9,1},{17,25},{25,17},{2,10},{10... | collective-permute-start | bytes 1671176 | tf_op jit(solution)/shard_map/ppermute | solution.py:104
  161.7 31.0 %collective-permute-start.31 = (bf16[2,64,3072]{2,1,0:T(8,128)(2,1)S(1)}, bf16[2,64,3072]{2,1,0:T(8,128)(2,1)S(1)}, u32[]{:S(2)}, u32[]{:S(2)}) collective-permute-start(bf16[2,64,3072]{2,1,0:T(8,128)(2,1)S(1)} %bitcast.287), channel_id=1, source_target_pairs={{0,16},{8,24},{16,0},{24,8},{1,17},{9,25},{17,1},{25,9},{2,18},{10... | collective-permute-start | bytes 2359304 | tf_op jit(solution)/shard_map/ppermute | solution.py:108
  163.7 7.6 %collective-permute-start.59 = (bf16[32,1152]{1,0:T(8,128)(2,1)S(1)}, bf16[32,1152]{1,0:T(8,128)(2,1)S(1)}, u32[]{:S(2)}, u32[]{:S(2)}) collective-permute-start(bf16[32,1152]{1,0:T(8,128)(2,1)S(1)} %pad_maximum_fusion.12), channel_id=1, source_target_pairs={{0,1},{2,0},{4,2},{6,4},{7,6},{5,7},{3,5},{1,3},{8,9},{10,8},{12,1... | collective-permute-start | bytes 221192 | tf_op jit(solution)/shard_map/ppermute | solution.py:45
  165.8 6.5 %collective-permute-start.43 = (bf16[32,1152]{1,0:T(8,128)(2,1)S(1)}, bf16[32,1152]{1,0:T(8,128)(2,1)S(1)}, u32[]{:S(2)}, u32[]{:S(2)}) collective-permute-start(bf16[32,1152]{1,0:T(8,128)(2,1)S(1)} %pad_maximum_fusion.13), channel_id=1, source_target_pairs={{0,1},{2,0},{4,2},{6,4},{7,6},{5,7},{3,5},{1,3},{8,9},{10,8},{12,1... | collective-permute-start | bytes 221192 | tf_op jit(solution)/shard_map/ppermute | solution.py:45
  168.5 6.3 %collective-permute-start.56 = (bf16[32,2176]{1,0:T(8,128)(2,1)S(1)}, bf16[32,2176]{1,0:T(8,128)(2,1)S(1)}, u32[]{:S(2)}, u32[]{:S(2)}) collective-permute-start(bf16[32,2176]{1,0:T(8,128)(2,1)S(1)} %fusion.39), channel_id=1, source_target_pairs={{0,2},{2,4},{4,6},{6,7},{7,5},{5,3},{3,1},{1,0},{8,10},{10,12},{12... | collective-permute-start | bytes 417800 | tf_op jit(solution)/shard_map/ppermute | solution.py:45
  170.1 7.7 %collective-permute-start.40 = (bf16[32,2176]{1,0:T(8,128)(2,1)S(1)}, bf16[32,2176]{1,0:T(8,128)(2,1)S(1)}, u32[]{:S(2)}, u32[]{:S(2)}) collective-permute-start(bf16[32,2176]{1,0:T(8,128)(2,1)S(1)} %fusion.37), channel_id=1, source_target_pairs={{0,2},{2,4},{4,6},{6,7},{7,5},{5,3},{3,1},{1,0},{8,10},{10,12},{12... | collective-permute-start | bytes 417800 | tf_op jit(solution)/shard_map/ppermute | solution.py:45
  171.3 7.6 %collective-permute-start.60 = (bf16[32,2176]{1,0:T(8,128)(2,1)S(1)}, bf16[32,2176]{1,0:T(8,128)(2,1)S(1)}, u32[]{:S(2)}, u32[]{:S(2)}) collective-permute-start(bf16[32,2176]{1,0:T(8,128)(2,1)S(1)} %pad_maximum_fusion.11), channel_id=1, source_target_pairs={{0,1},{2,0},{4,2},{6,4},{7,6},{5,7},{3,5},{1,3},{8,9},{10,8},{12,1... | collective-permute-start | bytes 417800 | tf_op jit(solution)/shard_map/ppermute | solution.py:45
  172.3 7.9 %collective-permute-start.44 = (bf16[32,2176]{1,0:T(8,128)(2,1)S(1)}, bf16[32,2176]{1,0:T(8,128)(2,1)S(1)}, u32[]{:S(2)}, u32[]{:S(2)}) collective-permute-start(bf16[32,2176]{1,0:T(8,128)(2,1)S(1)} %pad_maximum_fusion.10), channel_id=1, source_target_pairs={{0,1},{2,0},{4,2},{6,4},{7,6},{5,7},{3,5},{1,3},{8,9},{10,8},{12,1... | collective-permute-start | bytes 417800 | tf_op jit(solution)/shard_map/ppermute | solution.py:45
  174.8 6.3 %collective-permute-start.57 = (bf16[32,2176]{1,0:T(8,128)(2,1)S(1)}, bf16[32,2176]{1,0:T(8,128)(2,1)S(1)}, u32[]{:S(2)}, u32[]{:S(2)}) collective-permute-start(bf16[32,2176]{1,0:T(8,128)(2,1)S(1)} %fusion.25), channel_id=1, source_target_pairs={{0,2},{2,4},{4,6},{6,7},{7,5},{5,3},{3,1},{1,0},{8,10},{10,12},{12... | collective-permute-start | bytes 417800 | tf_op jit(solution)/shard_map/ppermute | solution.py:45
  177.8 6.9 %collective-permute-start.41 = (bf16[32,2176]{1,0:T(8,128)(2,1)S(1)}, bf16[32,2176]{1,0:T(8,128)(2,1)S(1)}, u32[]{:S(2)}, u32[]{:S(2)}) collective-permute-start(bf16[32,2176]{1,0:T(8,128)(2,1)S(1)} %fusion.20), channel_id=1, source_target_pairs={{0,2},{2,4},{4,6},{6,7},{7,5},{5,3},{3,1},{1,0},{8,10},{10,12},{12... | collective-permute-start | bytes 417800 | tf_op jit(solution)/shard_map/ppermute | solution.py:45
  179.0 6.5 %collective-permute-start.61 = (bf16[32,2176]{1,0:T(8,128)(2,1)S(1)}, bf16[32,2176]{1,0:T(8,128)(2,1)S(1)}, u32[]{:S(2)}, u32[]{:S(2)}) collective-permute-start(bf16[32,2176]{1,0:T(8,128)(2,1)S(1)} %fusion.27), channel_id=1, source_target_pairs={{0,1},{2,0},{4,2},{6,4},{7,6},{5,7},{3,5},{1,3},{8,9},{10,8},{12,1... | collective-permute-start | bytes 417800 | tf_op jit(solution)/shard_map/ppermute | solution.py:45
  180.3 7.2 %collective-permute-start.45 = (bf16[32,2176]{1,0:T(8,128)(2,1)S(1)}, bf16[32,2176]{1,0:T(8,128)(2,1)S(1)}, u32[]{:S(2)}, u32[]{:S(2)}) collective-permute-start(bf16[32,2176]{1,0:T(8,128)(2,1)S(1)} %fusion.22), channel_id=1, source_target_pairs={{0,1},{2,0},{4,2},{6,4},{7,6},{5,7},{3,5},{1,3},{8,9},{10,8},{12,1... | collective-permute-start | bytes 417800 | tf_op jit(solution)/shard_map/ppermute | solution.py:45
  181.1 8.1 %collective-permute-start.58 = (bf16[32,2176]{1,0:T(8,128)(2,1)S(1)}, bf16[32,2176]{1,0:T(8,128)(2,1)S(1)}, u32[]{:S(2)}, u32[]{:S(2)}) collective-permute-start(bf16[32,2176]{1,0:T(8,128)(2,1)S(1)} %fusion.24), channel_id=1, source_target_pairs={{0,2},{2,4},{4,6},{6,7},{7,5},{5,3},{3,1},{1,0},{8,10},{10,12},{12... | collective-permute-start | bytes 417800 | tf_op jit(solution)/shard_map/ppermute | solution.py:45
  184.7 5.9 %collective-permute-start.42 = (bf16[32,2176]{1,0:T(8,128)(2,1)S(1)}, bf16[32,2176]{1,0:T(8,128)(2,1)S(1)}, u32[]{:S(2)}, u32[]{:S(2)}) collective-permute-start(bf16[32,2176]{1,0:T(8,128)(2,1)S(1)} %fusion.19), channel_id=1, source_target_pairs={{0,2},{2,4},{4,6},{6,7},{7,5},{5,3},{3,1},{1,0},{8,10},{10,12},{12... | collective-permute-start | bytes 417800 | tf_op jit(solution)/shard_map/ppermute | solution.py:45
  185.5 5.1 %collective-permute-start.62 = (bf16[32,2176]{1,0:T(8,128)(2,1)S(1)}, bf16[32,2176]{1,0:T(8,128)(2,1)S(1)}, u32[]{:S(2)}, u32[]{:S(2)}) collective-permute-start(bf16[32,2176]{1,0:T(8,128)(2,1)S(1)} %fusion.26), channel_id=1, source_target_pairs={{0,1},{2,0},{4,2},{6,4},{7,6},{5,7},{3,5},{1,3},{8,9},{10,8},{12,1... | collective-permute-start | bytes 417800 | tf_op jit(solution)/shard_map/ppermute | solution.py:45
  187.5 5.1 %collective-permute-start.46 = (bf16[32,2176]{1,0:T(8,128)(2,1)S(1)}, bf16[32,2176]{1,0:T(8,128)(2,1)S(1)}, u32[]{:S(2)}, u32[]{:S(2)}) collective-permute-start(bf16[32,2176]{1,0:T(8,128)(2,1)S(1)} %fusion.21), channel_id=1, source_target_pairs={{0,1},{2,0},{4,2},{6,4},{7,6},{5,7},{3,5},{1,3},{8,9},{10,8},{12,1... | collective-permute-start | bytes 417800 | tf_op jit(solution)/shard_map/ppermute | solution.py:45
  192.8 26.0 %collective-permute-start.32 = (bf16[2,2,64,3072]{3,2,0,1:T(8,128)(2,1)S(1)}, bf16[2,2,64,3072]{3,2,0,1:T(8,128)(2,1)S(1)}, u32[]{:S(2)}, u32[]{:S(2)}) collective-permute-start(bf16[2,2,64,3072]{3,2,0,1:T(8,128)(2,1)S(1)} %pad_maximum_fusion.1), channel_id=1, source_target_pairs={{0,8},{8,0},{16,24},{24,16},{1,9},{9,1},{17,25},{25,17},{2,10},{10... | collective-permute-start | bytes 4718600 | tf_op jit(solution)/shard_map/ppermute | solution.py:104
  196.0 6.3 %collective-permute-start.67 = (bf16[32,2048]{1,0:T(8,128)(2,1)S(1)}, bf16[32,2048]{1,0:T(8,128)(2,1)S(1)}, u32[]{:S(2)}, u32[]{:S(2)}) collective-permute-start(bf16[32,2048]{1,0:T(8,128)(2,1)S(1)} %get-tuple-element.86.refs_14_), channel_id=1, source_target_pairs={{0,1},{2,0},{4,2},{6,4},{7,6},{5,7},{3,5},{1,3},{8,9},{10,8},{12,1... | collective-permute-start | bytes 393224 | tf_op jit(solution)/shard_map/ppermute | solution.py:45
  197.8 6.3 %collective-permute-start.63 = (bf16[32,2048]{1,0:T(8,128)(2,1)S(1)}, bf16[32,2048]{1,0:T(8,128)(2,1)S(1)}, u32[]{:S(2)}, u32[]{:S(2)}) collective-permute-start(bf16[32,2048]{1,0:T(8,128)(2,1)S(1)} %get-tuple-element.86.refs_14_), channel_id=1, source_target_pairs={{0,2},{2,4},{4,6},{6,7},{7,5},{5,3},{3,1},{1,0},{8,10},{10,12},{12... | collective-permute-start | bytes 393224 | tf_op jit(solution)/shard_map/ppermute | solution.py:45
  198.1 7.1 %collective-permute-start.51 = (bf16[32,2048]{1,0:T(8,128)(2,1)S(1)}, bf16[32,2048]{1,0:T(8,128)(2,1)S(1)}, u32[]{:S(2)}, u32[]{:S(2)}) collective-permute-start(bf16[32,2048]{1,0:T(8,128)(2,1)S(1)} %get-tuple-element.87.refs_5_), channel_id=1, source_target_pairs={{0,1},{2,0},{4,2},{6,4},{7,6},{5,7},{3,5},{1,3},{8,9},{10,8},{12,1... | collective-permute-start | bytes 393224 | tf_op jit(solution)/shard_map/ppermute | solution.py:45
  199.8 7.1 %collective-permute-start.47 = (bf16[32,2048]{1,0:T(8,128)(2,1)S(1)}, bf16[32,2048]{1,0:T(8,128)(2,1)S(1)}, u32[]{:S(2)}, u32[]{:S(2)}) collective-permute-start(bf16[32,2048]{1,0:T(8,128)(2,1)S(1)} %get-tuple-element.87.refs_5_), channel_id=1, source_target_pairs={{0,2},{2,4},{4,6},{6,7},{7,5},{5,3},{3,1},{1,0},{8,10},{10,12},{12... | collective-permute-start | bytes 393224 | tf_op jit(solution)/shard_map/ppermute | solution.py:45
  202.3 5.7 %collective-permute-start.68 = (bf16[32,2048]{1,0:T(8,128)(2,1)S(1)}, bf16[32,2048]{1,0:T(8,128)(2,1)S(1)}, u32[]{:S(2)}, u32[]{:S(2)}) collective-permute-start(bf16[32,2048]{1,0:T(8,128)(2,1)S(1)} %collective-permute-done.67.refs_15_), channel_id=1, source_target_pairs={{0,1},{2,0},{4,2},{6,4},{7,6},{5,7},{3,5},{1,3},{8,9},{10,8},{12,1... | collective-permute-start | bytes 393224 | tf_op jit(solution)/shard_map/ppermute | solution.py:45
  204.1 5.7 %collective-permute-start.64 = (bf16[32,2048]{1,0:T(8,128)(2,1)S(1)}, bf16[32,2048]{1,0:T(8,128)(2,1)S(1)}, u32[]{:S(2)}, u32[]{:S(2)}) collective-permute-start(bf16[32,2048]{1,0:T(8,128)(2,1)S(1)} %collective-permute-done.63.refs_13_), channel_id=1, source_target_pairs={{0,2},{2,4},{4,6},{6,7},{7,5},{5,3},{3,1},{1,0},{8,10},{10,12},{12... | collective-permute-start | bytes 393224 | tf_op jit(solution)/shard_map/ppermute | solution.py:45
  205.1 6.4 %collective-permute-start.52 = (bf16[32,2048]{1,0:T(8,128)(2,1)S(1)}, bf16[32,2048]{1,0:T(8,128)(2,1)S(1)}, u32[]{:S(2)}, u32[]{:S(2)}) collective-permute-start(bf16[32,2048]{1,0:T(8,128)(2,1)S(1)} %collective-permute-done.51.refs_6_), channel_id=1, source_target_pairs={{0,1},{2,0},{4,2},{6,4},{7,6},{5,7},{3,5},{1,3},{8,9},{10,8},{12,1... | collective-permute-start | bytes 393224 | tf_op jit(solution)/shard_map/ppermute | solution.py:45
  206.9 6.4 %collective-permute-start.48 = (bf16[32,2048]{1,0:T(8,128)(2,1)S(1)}, bf16[32,2048]{1,0:T(8,128)(2,1)S(1)}, u32[]{:S(2)}, u32[]{:S(2)}) collective-permute-start(bf16[32,2048]{1,0:T(8,128)(2,1)S(1)} %collective-permute-done.47.refs_4_), channel_id=1, source_target_pairs={{0,2},{2,4},{4,6},{6,7},{7,5},{5,3},{3,1},{1,0},{8,10},{10,12},{12... | collective-permute-start | bytes 393224 | tf_op jit(solution)/shard_map/ppermute | solution.py:45
  208.0 6.4 %collective-permute-start.69 = (bf16[32,2048]{1,0:T(8,128)(2,1)S(1)}, bf16[32,2048]{1,0:T(8,128)(2,1)S(1)}, u32[]{:S(2)}, u32[]{:S(2)}) collective-permute-start(bf16[32,2048]{1,0:T(8,128)(2,1)S(1)} %collective-permute-done.68.refs_16_), channel_id=1, source_target_pairs={{0,1},{2,0},{4,2},{6,4},{7,6},{5,7},{3,5},{1,3},{8,9},{10,8},{12,1... | collective-permute-start | bytes 393224 | tf_op jit(solution)/shard_map/ppermute | solution.py:45
  209.8 6.4 %collective-permute-start.65 = (bf16[32,2048]{1,0:T(8,128)(2,1)S(1)}, bf16[32,2048]{1,0:T(8,128)(2,1)S(1)}, u32[]{:S(2)}, u32[]{:S(2)}) collective-permute-start(bf16[32,2048]{1,0:T(8,128)(2,1)S(1)} %collective-permute-done.64.refs_12_), channel_id=1, source_target_pairs={{0,2},{2,4},{4,6},{6,7},{7,5},{5,3},{3,1},{1,0},{8,10},{10,12},{12... | collective-permute-start | bytes 393224 | tf_op jit(solution)/shard_map/ppermute | solution.py:45
  211.6 5.1 %collective-permute-start.53 = (bf16[32,2048]{1,0:T(8,128)(2,1)S(1)}, bf16[32,2048]{1,0:T(8,128)(2,1)S(1)}, u32[]{:S(2)}, u32[]{:S(2)}) collective-permute-start(bf16[32,2048]{1,0:T(8,128)(2,1)S(1)} %collective-permute-done.52.refs_7_), channel_id=1, source_target_pairs={{0,1},{2,0},{4,2},{6,4},{7,6},{5,7},{3,5},{1,3},{8,9},{10,8},{12,1... | collective-permute-start | bytes 393224 | tf_op jit(solution)/shard_map/ppermute | solution.py:45
  213.3 5.1 %collective-permute-start.49 = (bf16[32,2048]{1,0:T(8,128)(2,1)S(1)}, bf16[32,2048]{1,0:T(8,128)(2,1)S(1)}, u32[]{:S(2)}, u32[]{:S(2)}) collective-permute-start(bf16[32,2048]{1,0:T(8,128)(2,1)S(1)} %collective-permute-done.48.refs_3_), channel_id=1, source_target_pairs={{0,2},{2,4},{4,6},{6,7},{7,5},{5,3},{3,1},{1,0},{8,10},{10,12},{12... | collective-permute-start | bytes 393224 | tf_op jit(solution)/shard_map/ppermute | solution.py:45
  (32 other events, 288.3 us)

commit v5 on v4

v5 whole, which is shorter than its diff:
```python
import functools

import jax
import jax.numpy as jnp
import numpy as np
from jax import lax
from jax.experimental import pallas as pl
from jax.experimental.pallas import tpu as pltpu
from jax.sharding import PartitionSpec as P

TREE = 64
CORES = 2
LANES = 128
CHUNKS = 2
F32 = jnp.float32
BF16 = jnp.bfloat16


def ring_order(rows, columns):
    if columns == 1 or rows == 1:
        return list(range(rows * columns))
    order = [r * columns for r in range(rows)]
    for step in range(rows):
        r = rows - 1 - step
        line = [r * columns + c for c in range(1, columns)]
        order += line if step % 2 == 0 else line[::-1]
    return order


class Ring:
    def __init__(self, size, columns):
        self.size = size
        self.half = size // 2
        self.order = ring_order(size // columns, columns)
        self.place = [0] * size
        for position, index in enumerate(self.order):
            self.place[index] = position

    def shift(self, x, step):
        size, order = self.size, self.order
        return lax.ppermute(
            x, "vocab", [(order[p], order[(p + step) % size]) for p in range(size)]
        )

    def partner(self, x, bit):
        return lax.ppermute(x, "vocab", [(v, v ^ bit) for v in range(self.size)])

    def meet(self, x, merge, waits=None):
        bit = 1
        while bit < self.size:
            if waits and bit in waits:
                x = after(x, waits[bit]())
            x = merge(x, self.partner(x, bit))
            bit *= 2
        return x

    def reach(self, h):
        return (self.half, self.half - 1) if h % 2 == 0 else (self.half - 1, self.half)

    def gather(self, block, h, waits=None):
        far_ahead, far_behind = self.reach(h)
        ahead, behind = [block], [block]
        for step in range(self.half):
            if waits and step in waits:
                others = waits[step]()
                ahead[-1], behind[-1] = after(ahead[-1], others), after(behind[-1], others)
            if step < far_ahead:
                ahead.append(self.shift(ahead[-1], 1))
            if step < far_behind:
                behind.append(self.shift(behind[-1], -1))
        return ahead[1:][::-1] + [block] + behind[1:]

    def sources(self, vocab, h):
        p, far_ahead = self.place[vocab], self.reach(h)[0]
        return [(p + k - far_ahead) % self.size for k in range(self.size)]

    def scatter_sum(self, part, h):
        far_ahead, far_behind = self.reach(h)
        got_ahead = got_behind = None
        for step in range(self.half, 0, -1):
            if step <= far_ahead:
                ahead = part(step) if got_ahead is None else part(step) + got_ahead
                got_ahead = self.shift(ahead.astype(BF16), 1).astype(F32)
            if step <= far_behind:
                behind = part(-step) if got_behind is None else part(-step) + got_behind
                got_behind = self.shift(behind.astype(BF16), -1).astype(F32)
        return part(0) + got_ahead + got_behind


class Groups:
    def __init__(self, size):
        self.size = size
        self.chips = size // CORES

    def entry(self, index, group):
        chip = (group // CORES - index // CORES) % self.chips
        return (group % CORES ^ index % CORES) * self.chips + chip

    def swap(self, x):
        return lax.ppermute(x, "dp", [(i, i ^ 1) for i in range(self.size)])

    def shift(self, x, step):
        size = self.size
        return lax.ppermute(x, "dp", [(i, (i + CORES * step) % size) for i in range(size)])

    def gather_halves(self, block):
        mine = jnp.stack([block] + [self.shift(block, -d) for d in range(1, self.chips)])
        return mine, self.swap(mine)

    def gather(self, block):
        return jnp.concatenate(self.gather_halves(block), axis=0)


VMEM = pl.BlockSpec(memory_space=pltpu.VMEM)
SMEM = pl.BlockSpec(memory_space=pltpu.SMEM)


def transpose_into(out_ref, ref):
    tile = min(ref.shape[1], 256)
    for start in range(0, ref.shape[1], tile):
        block = ref[:, pl.ds(start, tile)].astype(F32)
        out_ref[pl.ds(start, tile), :] = block.T.astype(BF16)


def project_kernel(count, index_ref, factor_ref, gain_ref, weight_ref, *refs):
    blocks = refs[:count]
    keep_ref, send_ref, piece_ref, raw_ref, normed_ref, turned_ref = refs[count:]
    rows, width = blocks[0].shape
    piece = piece_ref.shape[0]
    half = keep_ref.shape[0]

    @pl.when(pl.program_id(0) == 0)
    def _():
        for k, ref in enumerate(blocks):
            start = pl.multiple_of(index_ref[k] * rows, rows)
            column = pl.multiple_of(index_ref[count + k] * width, width)
            raw_ref[pl.ds(start, rows), pl.ds(column, width)] = ref[...]
        for g in range(factor_ref.shape[0]):
            group = pl.ds(g * rows, rows)
            normed_ref[group, :] = (
                raw_ref[group, :].astype(F32) * factor_ref[g] * gain_ref[...]
            ).astype(BF16)
        transpose_into(turned_ref, normed_ref)
        start = pl.multiple_of(index_ref[2 * count] * piece, piece)
        piece_ref[...] = raw_ref[pl.ds(start, piece), :]

    logits = jnp.dot(weight_ref[...], turned_ref[...], preferred_element_type=F32).T
    keep_ref[...] = logits[:half]
    send_ref[...] = logits[half:]


def project(index, blocks, factor, gain, weight, piece_rows):
    rows = blocks[0].shape[0]
    vocab, depth = weight.shape
    all_rows = factor.shape[0] * rows
    half = all_rows // CORES
    tile = min(vocab, 512)
    out = jax.ShapeDtypeStruct((half, vocab), F32)
    return pl.pallas_call(
        functools.partial(project_kernel, len(blocks)),
        grid=(vocab // tile,),
        in_specs=[SMEM, VMEM, VMEM, pl.BlockSpec((tile, depth), lambda n: (n, 0))]
        + [VMEM] * len(blocks),
        out_specs=[pl.BlockSpec((half, tile), lambda n: (0, n))] * 2
        + [pl.BlockSpec((piece_rows, depth), lambda n: (0, 0))],
        out_shape=[out, out, jax.ShapeDtypeStruct((piece_rows, depth), BF16)],
        scratch_shapes=[
            pltpu.VMEM((all_rows, depth), BF16),
            pltpu.VMEM((all_rows, depth), BF16),
            pltpu.VMEM((depth, all_rows), BF16),
        ],
        compiler_params=pltpu.CompilerParams(vmem_limit_bytes=24 * 2**20),
        cost_estimate=pl.CostEstimate(
            flops=2 * all_rows * depth * vocab,
            bytes_accessed=2 * vocab * depth + all_rows * (2 * depth + 4 * vocab),
            transcendentals=0,
        ),
    )(index, factor, gain, weight, *blocks)


def back_kernel(piece, index_ref, mine_ref, other_ref, weight_ref, out_ref, grad_ref):
    vocab = weight_ref.shape[0]
    tile = weight_ref.shape[1]
    half = mine_ref.shape[0]
    depth = out_ref.shape[1] - LANES
    step = pl.program_id(0)

    @pl.when(step == 0)
    def _():
        for k in range(2 * half // piece):
            ref, first = (mine_ref, k * piece) if k * piece < half else (other_ref, k * piece - half)
            rows = pl.ds(pl.multiple_of(index_ref[k] * piece, piece), piece)
            grad_ref[rows, :] = ref[pl.ds(first, piece), :vocab]
            out_ref[rows, pl.ds(depth, LANES)] = ref[pl.ds(first, piece), vocab:].astype(F32)

    columns = pl.ds(pl.multiple_of(step * tile, tile), tile)
    out_ref[:, columns] = jnp.dot(grad_ref[...], weight_ref[...], preferred_element_type=F32)


def back(index, mine, other, weight, piece_rows):
    vocab, depth = weight.shape
    all_rows = mine.shape[0] + other.shape[0]
    tile = min(depth, 512)
    return pl.pallas_call(
        functools.partial(back_kernel, piece_rows),
        grid=(depth // tile,),
        in_specs=[SMEM, VMEM, VMEM, pl.BlockSpec((vocab, tile), lambda n: (0, n))],
        out_specs=pl.BlockSpec((all_rows, depth + LANES), lambda n: (0, 0)),
        out_shape=jax.ShapeDtypeStruct((all_rows, depth + LANES), F32),
        scratch_shapes=[pltpu.VMEM((all_rows, vocab), BF16)],
        compiler_params=pltpu.CompilerParams(vmem_limit_bytes=24 * 2**20),
        cost_estimate=pl.CostEstimate(
            flops=2 * all_rows * depth * vocab,
            bytes_accessed=2 * vocab * depth + all_rows * (2 * vocab + 4 * depth),
            transcendentals=0,
        ),
    )(index, mine, other, weight)


def outer_kernel(count, index_ref, chosen_ref, *refs):
    pieces, (out_ref, share_ref, grad_ref, turned_ref) = refs[:-4], refs[-4:]
    rows = pieces[0].shape[0]
    share = share_ref.shape[0]

    @pl.when(pl.program_id(0) == 0)
    def _():
        for k, ref in enumerate(pieces):
            start = pl.multiple_of((k // count * count + index_ref[k]) * rows, rows)
            grad_ref[pl.ds(start, rows), :] = ref[...]
        transpose_into(turned_ref, grad_ref)
        start = pl.multiple_of(index_ref[len(pieces)] * share, share)
        share_ref[...] = grad_ref[pl.ds(start, share), :]

    out_ref[...] = jnp.dot(turned_ref[...], chosen_ref[...], preferred_element_type=F32)


def outer(index, chosen, chunks, share_rows):
    depth = chunks[0][0].shape[1]
    all_rows, joined = chosen.shape
    tile = min(joined, 256)
    pieces = [x for chunk in chunks for x in chunk]
    return pl.pallas_call(
        functools.partial(outer_kernel, len(chunks[0])),
        grid=(joined // tile,),
        in_specs=[SMEM, pl.BlockSpec((all_rows, tile), lambda n: (0, n))] + [VMEM] * len(pieces),
        out_specs=[
            pl.BlockSpec((depth, tile), lambda n: (0, n)),
            pl.BlockSpec((share_rows, depth), lambda n: (0, 0)),
        ],
        out_shape=[
            jax.ShapeDtypeStruct((depth, joined), F32),
            jax.ShapeDtypeStruct((share_rows, depth), BF16),
        ],
        scratch_shapes=[
            pltpu.VMEM((all_rows, depth), BF16),
            pltpu.VMEM((depth, all_rows), BF16),
        ],
        compiler_params=pltpu.CompilerParams(vmem_limit_bytes=32 * 2**20),
        cost_estimate=pl.CostEstimate(
            flops=2 * all_rows * depth * joined,
            bytes_accessed=4 * depth * joined + 2 * all_rows * (depth + joined),
            transcendentals=0,
        ),
    )(index, chosen, *pieces)


def device_table(groups, ring, slots, widths):
    group_rows, chunk_rows, piece_rows, slice_width = widths
    parts = ring.size
    step_rows = piece_rows * parts
    share_rows = group_rows // slots
    table = {}

    def add(name, values):
        table.setdefault(name, []).append(values)

    for g in range(groups.size):
        for v in range(parts):
            p = ring.place[v]
            for h in range(CHUNKS):
                held = [ring.order[q] for q in ring.sources(v, h)]
                group = [
                    i // slots % groups.chips * CORES + i // slots // groups.chips for i in held
                ]
                add(f"place{h}", [groups.entry(g, i) for i in group] + [i % slots for i in held] + [p])
            entry = groups.entry(g, v * share_rows // group_rows)
            first = v * share_rows % group_rows
            start = first // chunk_rows * step_rows + entry * chunk_rows + first % chunk_rows
            pieces = [q for h in range(CHUNKS) for q in ring.sources(v, h)]
            add("pieces", pieces + [start // share_rows])
            add("turn", [(k - p) % parts for k in range(parts)])
            start = p * piece_rows
            add("starts", [g * slice_width, start // chunk_rows, start % chunk_rows, 2 * p])
    return {
        name: np.asarray(rows, np.int32).reshape(groups.size, parts, -1)
        for name, rows in table.items()
    }


def after(x, *others):
    return lax.optimization_barrier((x, others))[0]


def body(hidden, norm_gain, head_weight, target_logits, valid_rows, parents, features):
    groups = Groups(lax.axis_size("dp"))
    parts = lax.axis_size("vocab")
    ring = Ring(parts, groups.chips)
    group_rows, block_width = hidden.shape
    chunk_rows = group_rows // CHUNKS
    step_rows = groups.size * chunk_rows
    piece_rows = step_rows // parts
    model_width = block_width * parts
    slots = parts // groups.size
    slice_width = block_width * slots
    vocab_width = target_logits.shape[1]

    table = device_table(
        groups, ring, slots, (group_rows, chunk_rows, piece_rows, slice_width)
    )
    own = lax.dynamic_slice(
        jnp.asarray(np.concatenate(list(table.values()), axis=2)),
        (lax.axis_index("dp"), lax.axis_index("vocab"), 0),
        (1, 1, sum(rows.shape[2] for rows in table.values())),
    ).reshape(-1)
    index, first = {}, 0
    for name, rows in table.items():
        index[name] = own[first : first + rows.shape[2]]
        first += rows.shape[2]
    gain_start, own_entry, own_first, own_lane = [
        index["starts"].astype(jnp.uint32)[k] for k in range(4)
    ]

    def chunk(x, h):
        return x[h * chunk_rows : (h + 1) * chunk_rows]

    def column_owner(g, v):
        far = g % CORES * groups.chips + g // CORES
        return v // slots * parts + far * slots + v % slots

    turn = [
        (g * parts + v, column_owner(g, v)) for g in range(groups.size) for v in range(parts)
    ]
    turned = [lax.ppermute(chunk(hidden, h), ("dp", "vocab"), turn) for h in range(CHUNKS)]

    live_rows = (valid_rows == 1).astype(F32)
    squares = jnp.sum(jnp.square(hidden.astype(F32)), axis=1)[None]
    squares = ring.meet(squares, lambda a, b: a + b, {2: lambda: (turned[0],)})
    both = groups.gather(jnp.concatenate([squares, live_rows[None]]))
    valid_count = jnp.sum(both[:, 1])
    row_factor = lax.rsqrt(both[:, 0] / model_width + 1e-05)

    targets = target_logits.astype(F32)
    target_top = jnp.max(targets, axis=1)
    target_total = jnp.sum(jnp.exp(targets - target_top[:, None]), axis=1)

    def merge_totals(a, b):
        top = jnp.maximum(a[0], b[0])
        total = a[1] * jnp.exp(a[0] - top) + b[1] * jnp.exp(b[0] - top)
        return jnp.stack([top, total])

    tree_rows = jnp.arange(group_rows, dtype=jnp.int32) // TREE * TREE + parents
    own_chosen = features.at[tree_rows].get(mode="promise_in_bounds")

    gain = lax.dynamic_slice(norm_gain, (gain_start,), (slice_width,)).reshape(1, slice_width)
    row_weight = 1048576.0 * live_rows / valid_count
    lane = lax.broadcasted_iota(jnp.uint32, (chunk_rows, LANES), 1)

    def group_logits(h, blocks):
        factor = row_factor[:, h * chunk_rows : (h + 1) * chunk_rows]
        keep, send, piece = project(
            index[f"place{h}"], blocks, factor[:, :, None], gain, head_weight, piece_rows
        )
        pieces.append(piece)
        yield keep
        summed = keep + groups.swap(send)
        yield summed
        summed = summed.reshape(groups.chips, chunk_rows, vocab_width)
        logits = summed[0]
        for d in range(1, groups.chips):
            logits = logits + groups.shift(summed[d], d)
        yield logits

    gathered, logits_of, pieces = [], [], []
    for h in range(CHUNKS):
        waits = {1: lambda: tuple(turned[1:])}
        if h > 0:
            stages = group_logits(h - 1, gathered[-1])
            waits = {
                0: lambda: (gathered[-1],),
                1: lambda: (next(stages),),
                2: lambda: (next(stages),),
                3: lambda: (logits_of.append(next(stages)), logits_of[-1])[1:],
            }
        gathered.append(ring.gather(turned[h], h, waits))
    logits_of.append(list(group_logits(CHUNKS - 1, gathered[-1]))[-1])

    grads = []
    for h in range(CHUNKS):
        logits = logits_of[h]
        factor = row_factor[:, h * chunk_rows : (h + 1) * chunk_rows]
        top = jnp.max(logits, axis=1)
        total = jnp.sum(jnp.exp(logits - top[:, None]), axis=1)
        mine = jnp.stack([top, total])
        if h == 0:
            mine = jnp.concatenate([mine, jnp.stack([target_top, target_total])], axis=1)
        met = ring.meet(mine, merge_totals)
        scale = jnp.exp(top - met[0, :chunk_rows]) / met[1, :chunk_rows]
        if h == 0:
            target_scale = jnp.exp(target_top - met[0, chunk_rows:]) / met[1, chunk_rows:]
        draft_probs = jnp.exp(logits - top[:, None]) * scale[:, None]
        target_probs = (
            jnp.exp(chunk(targets, h) - chunk(target_top, h)[:, None])
            * chunk(target_scale, h)[:, None]
        )
        logit_grad = chunk(row_weight, h)[:, None] * (draft_probs - target_probs)
        logit_grad = lax.reduce_precision(logit_grad, 8, 7)
        dot_part = jnp.sum(logit_grad * logits, axis=1)
        dot_high = lax.reduce_precision(dot_part, 8, 7)
        dot_low = dot_part - dot_high
        lanes = jnp.where(lane == own_lane, dot_high[:, None], 0.0) + jnp.where(
            lane == own_lane + 1, dot_low[:, None], 0.0
        )
        message = jnp.concatenate([logit_grad.astype(BF16), lanes.astype(BF16)], axis=1)
        everyone = groups.gather_halves(message)
        if h == CHUNKS - 1:
            chosen = groups.gather(after(own_chosen, everyone).reshape(CHUNKS, chunk_rows, -1))
            chosen = chosen.transpose(1, 0, 2, 3).reshape(CHUNKS * step_rows, -1)
        mine, other = [x.reshape(step_rows // CORES, -1) for x in everyone]
        normed_grad = back(index["turn"], mine, other, head_weight, piece_rows)

        def part(t):
            first = t % parts * piece_rows
            return normed_grad[first : first + piece_rows]

        summed = ring.scatter_sum(part, h)
        own_factor = lax.dynamic_slice(factor, (own_entry, own_first), (1, piece_rows))[0]
        row_dot = jnp.sum(summed[:, slice_width:], axis=1) / own_factor
        grad_piece = (
            own_factor[:, None] * gain * summed[:, :slice_width]
            - pieces[h].astype(F32) * (own_factor**3 * row_dot / model_width)[:, None]
        ).astype(BF16)
        grads.append(ring.gather(grad_piece, h))

    grad_joining, grad_share = outer(index["pieces"], chosen, grads, group_rows // slots)
    return (grad_share, grad_joining)


def solution(mesh):
    placed = (
        P("dp", "vocab"),
        P(),
        P("vocab", "dp"),
        P("dp", "vocab"),
        P("dp"),
        P("dp"),
        P("dp", "vocab"),
    )
    return jax.shard_map(
        body,
        mesh=mesh,
        in_specs=placed,
        out_specs=(P("vocab", "dp"), P("dp", "vocab")),
        check_vma=False,
    )
```

time: 236 us -> 222 us (0.941)
  matrix products: 19.8 us -> 0 us
  Pallas kernels: 14.3 us -> 32.1 us
  waiting for transfers between devices: 65.9 us -> 79 us
  other arithmetic: 26.7 us -> 14.2 us
  local copies, waits for them, and re-layouts: 19.4 us -> 12.4 us
  starting transfers between devices: 87.2 us -> 82.6 us
    dot_general x4 -> x0, matrix products: 19.8 us -> none  [the longest x2 11.5 us: group_logits(): lax.dot_general(normed, head_weight, (((1,), (1,)), ((), ())), preferred_...]
    pallas_call x3 -> x5, Pallas kernels: 14.3 us -> 32.1 us  [the longest x1 14.5 us: outer(): pl.pallas_call(functools.partial(outer_kernel, len(chunks[0])), grid=(joi...]
    ppermute x48 -> x42, starting transfers between devices: 57.4 us -> 43.7 us  [shift(): lax.ppermute(x, 'vocab', [(order[p], order[(p + step) % size]) for p in r...]
    ppermute x48 -> x42, waiting for transfers between devices: 39.3 us -> 50.9 us  [shift(): lax.ppermute(x, 'vocab', [(order[p], order[(p + step) % size]) for p in r...]
    ppermute x9, starting transfers between devices: 19.5 us -> 29.6 us  [partner(): return lax.ppermute(x, 'vocab', [(v, v ^ bit) for v in range(self.size)])]
    dynamic_slice x2 -> x0, other arithmetic: 9.69 us -> none  [part(): lax.dynamic_slice(dots, start, (piece_rows, LANES)).astype(F32)]
    dynamic_slice x3 -> x1, local copies, waits for them, and re-layouts: 8.39 us -> 0.7 us  [body(): lax.dynamic_slice(jnp.asarray(np.concatenate(list(table.values()), axis=2...]
    unnamed x18 -> x24, local copies, waits for them, and re-layouts: 0.06 us -> 6.82 us
  transfers between devices with their start and end apart: 71 -> 65, of which waited for: 38 -> 38; matrix products, arithmetic and copies ran while one was open for 14% -> 7% of each run, Pallas kernels for 0% -> 4%
where the time goes in v5:
time: 222 us
  starting transfers between devices  82.6 us (37%)
  waiting for transfers between devices  79 us (36%)
  Pallas kernels  32.1 us (14%)
  other arithmetic  14.2 us (6%)
  local copies, waits for them, and re-layouts  12.4 us (6%)
    ppermute x42, waiting for transfers between devices, shift(): lax.ppermute(x, 'vocab', [(order[p], order[(p + step) % size]) for p in r...  50.9 us
    ppermute x42, starting transfers between devices, shift(): lax.ppermute(x, 'vocab', [(order[p], order[(p + step) % size]) for p in r...  43.7 us
    ppermute x9, starting transfers between devices, partner(): return lax.ppermute(x, 'vocab', [(v, v ^ bit) for v in range(self.size)])  29.6 us
    ppermute x6, waiting for transfers between devices, shift(): lax.ppermute(x, 'dp', [(i, (i + CORES * step) % size) for i in range(size)])  16.2 us
    pallas_call x1, Pallas kernels, outer(): pl.pallas_call(functools.partial(outer_kernel, len(chunks[0])), grid=(joi...  14.5 us
    ppermute x9, waiting for transfers between devices, partner(): return lax.ppermute(x, 'vocab', [(v, v ^ bit) for v in range(self.size)])  10.5 us
    pallas_call x2, Pallas kernels, project(): pl.pallas_call(functools.partial(project_kernel, len(blocks)), grid=(voca...  9.62 us
    pallas_call x2, Pallas kernels, back(): pl.pallas_call(functools.partial(back_kernel, piece_rows), grid=(depth //...  8.03 us
  transfers between devices with their start and end apart: 65, of which 38 were waited for; matrix products, arithmetic and copies ran while one was open for 7% of the time, Pallas kernels for 4%

profile of v5, /device:TPU:0, one launch (start us, length us, event | category | flops | bytes accessed | tf_op | source)
XLA Modules:
  0.0 222.1 jit_solution(4686339193051765899)
XLA Ops:
  1.8 3.0 %collective-permute-start = (f32[1,128]{1,0:T(1,128)S(1)}, f32[1,128]{1,0:T(1,128)S(1)}, u32[]{:S(2)}, u32[]{:S(2)}) collective-permute-start(f32[1,128]{1,0:T(1,128)S(1)} %bitcast.177), channel_id=1, source_target_pairs={{0,1},{1,0},{2,3},{3,2},{4,5},{5,4},{6,7},{7,6},{8,9},{9,8},{10,11... | collective-permute-start | bytes 1544 | tf_op jit(solution)/shard_map/ppermute | solution.py:46
  7.9 10.5 %collective-permute-start.2 = (f32[1,128]{1,0:T(1,128)S(1)}, f32[1,128]{1,0:T(1,128)S(1)}, u32[]{:S(2)}, u32[]{:S(2)}) collective-permute-start(f32[1,128]{1,0:T(1,128)S(1)} %bitcast_add_fusion), channel_id=1, source_target_pairs={{0,2},{1,3},{2,0},{3,1},{4,6},{5,7},{6,4},{7,5},{8,10},{9,11},{10,... | collective-permute-start | bytes 1544 | tf_op jit(solution)/shard_map/ppermute | solution.py:46
  20.0 3.5 %collective-permute-start.3 = (f32[1,128]{1,0:T(1,128)S(1)}, f32[1,128]{1,0:T(1,128)S(1)}, u32[]{:S(2)}, u32[]{:S(2)}) collective-permute-start(f32[1,128]{1,0:T(1,128)S(1)} %add.145), channel_id=1, source_target_pairs={{0,4},{1,5},{2,6},{3,7},{4,0},{5,1},{6,2},{7,3},{8,12},{9,13},{10,... | collective-permute-start | bytes 1544 | tf_op jit(solution)/shard_map/ppermute | solution.py:46
  24.1 2.0 collective-permute-start.7
  26.1 2.9 %collective-permute-start.4 = (f32[2,128]{1,0:T(2,128)S(1)}, f32[2,128]{1,0:T(2,128)S(1)}, u32[]{:S(2)}, u32[]{:S(2)}) collective-permute-start(f32[2,128]{1,0:T(2,128)S(1)} %get-tuple-element.91), channel_id=1, source_target_pairs={{0,16},{8,24},{16,0},{24,8},{1,17},{9,25},{17,1},{25,9},{2,18},{10... | collective-permute-start | bytes 3080 | tf_op jit(solution)/shard_map/ppermute | solution.py:104
  34.8 1.7 collective-permute-done.8.refs_2_
  42.7 1.7 collective-permute-done.13.refs_7_
  44.3 2.2 %collective-permute-done.10.refs_0_ = bf16[64,1024]{1,0:T(8,128)(2,1)S(1)} collective-permute-done((bf16[64,1024]{1,0:T(8,128)(2,1)S(1)}, bf16[64,1024]{1,0:T(8,128)(2,1)S(1)}, u32[]{:S(2)}, u32[]{:S(2)}) %collective-permute-start.10) | collective-permute-done | bytes 131104 | tf_op jit(solution)/shard_map/ppermute | solution.py:41
  46.6 3.4 %copy-done.2 = bf16[2048,2048]{1,0:T(8,128)(2,1)S(1)} copy-done((bf16[2048,2048]{1,0:T(8,128)(2,1)S(1)}, bf16[2048,2048]{1,0:T(8,128)(2,1)}, u32[]{:S(2)}) %copy-start.2) | copy-done | bytes 8388632
  50.0 4.5 %shard_map.95 = (f32[128,2048]{1,0:T(8,128)S(1)}, f32[128,2048]{1,0:T(8,128)S(1)}, bf16[32,2048]{1,0:T(8,128)(2,1)S(1)}) custom-call(s32[17]{0:T(128)S(1)} %get-tuple-element.107.index_ref, f32[4,64,1]{2,1,0:T(8,128)S(1)} %copy.20.factor_ref, f32[1,2048]{1,0:T(1,128)S(1)} %bitcast.160, bf16[2048,2048]{1,0:T(8,128)(2,1)S(1)} %copy-done.2, ...), custom_call_target="tpu_custom_call" | custom-call | flops 2147483648 | bytes 11534336 | tf_op jit(solution)/shard_map/pallas_call | solution.py:159
  57.4 2.1 collective-permute-start.18
  59.5 2.0 collective-permute-start.14
  61.6 3.2 %collective-permute-done.19.refs_4_ = bf16[64,1024]{1,0:T(8,128)(2,1)S(1)} collective-permute-done((bf16[64,1024]{1,0:T(8,128)(2,1)S(1)}, bf16[64,1024]{1,0:T(8,128)(2,1)S(1)}, u32[]{:S(2)}, u32[]{:S(2)}) %collective-permute-start.19) | collective-permute-done | bytes 131104 | tf_op jit(solution)/shard_map/ppermute | solution.py:41
  64.8 1.7 collective-permute-start.15
  66.8 4.7 %collective-permute-done.20.refs_5_ = bf16[64,1024]{1,0:T(8,128)(2,1)S(1)} collective-permute-done((bf16[64,1024]{1,0:T(8,128)(2,1)S(1)}, bf16[64,1024]{1,0:T(8,128)(2,1)S(1)}, u32[]{:S(2)}, u32[]{:S(2)}) %collective-permute-start.20) | collective-permute-done | bytes 131104 | tf_op jit(solution)/shard_map/ppermute | solution.py:41
  74.5 3.5 %collective-permute-done.21.refs_6_ = bf16[64,1024]{1,0:T(8,128)(2,1)S(1)} collective-permute-done((bf16[64,1024]{1,0:T(8,128)(2,1)S(1)}, bf16[64,1024]{1,0:T(8,128)(2,1)S(1)}, u32[]{:S(2)}, u32[]{:S(2)}) %collective-permute-start.21) | collective-permute-done | bytes 131104 | tf_op jit(solution)/shard_map/ppermute | solution.py:41
  78.1 1.7 collective-permute-start.22
  80.9 2.2 %collective-permute-done.22.refs_7_ = bf16[64,1024]{1,0:T(8,128)(2,1)S(1)} collective-permute-done((bf16[64,1024]{1,0:T(8,128)(2,1)S(1)}, bf16[64,1024]{1,0:T(8,128)(2,1)S(1)}, u32[]{:S(2)}, u32[]{:S(2)}) %collective-permute-start.22) | collective-permute-done | bytes 131104 | tf_op jit(solution)/shard_map/ppermute | solution.py:41
  83.1 3.4 %copy-done.3 = bf16[2048,2048]{1,0:T(8,128)(2,1)S(1)} copy-done((bf16[2048,2048]{1,0:T(8,128)(2,1)S(1)}, bf16[2048,2048]{1,0:T(8,128)(2,1)}, u32[]{:S(2)}) %copy-start.3) | copy-done | bytes 8388632
  86.5 5.1 %shard_map.96 = (f32[128,2048]{1,0:T(8,128)S(1)}, f32[128,2048]{1,0:T(8,128)}, bf16[32,2048]{1,0:T(8,128)(2,1)S(1)}) custom-call(s32[17]{0:T(128)S(1)} %get-tuple-element.106.index_ref, f32[4,64,1]{2,1,0:T(8,128)S(1)} %copy.21.factor_ref, f32[1,2048]{1,0:T(1,128)S(1)} %bitcast.161, bf16[2048,2048]{1,0:T(8,128)(2,1)S(1)} %copy-done.3, ...), custom_call_target="tpu_custom_call" | custom-call | flops 2147483648 | bytes 11534336 | tf_op jit(solution)/shard_map/pallas_call | solution.py:159
  92.0 1.6 collective-permute-start.28
  95.6 2.1 collective-permute-start.29
  100.9 3.5 %collective-permute-start.30 = (f32[2,192]{1,0:T(2,128)S(1)}, f32[2,192]{1,0:T(2,128)S(1)}, u32[]{:S(2)}, u32[]{:S(2)}) collective-permute-start(f32[2,192]{1,0:T(2,128)S(1)} %pad_maximum_fusion.9), channel_id=1, source_target_pairs={{0,4},{1,5},{2,6},{3,7},{4,0},{5,1},{6,2},{7,3},{8,12},{9,13},{10,... | collective-permute-start | bytes 4616 | tf_op jit(solution)/shard_map/ppermute | solution.py:46
  106.1 7.5 %collective-permute-done.24 = f32[64,2048]{1,0:T(8,128)S(1)} collective-permute-done((f32[64,2048]{1,0:T(8,128)S(1)}, f32[64,2048]{1,0:T(8,128)S(1)}, u32[]{:S(2)}, u32[]{:S(2)}) %collective-permute-start.24) | collective-permute-done | bytes 524320 | tf_op jit(solution)/shard_map/ppermute | solution.py:104
  115.1 2.5 %collective-permute-done.25 = f32[2,64]{1,0:T(2,128)S(1)} collective-permute-done((f32[2,64]{1,0:T(2,128)S(1)}, f32[2,64]{1,0:T(2,128)S(1)}, u32[]{:S(2)}, u32[]{:S(2)}) %collective-permute-start.25) | collective-permute-done | bytes 544 | tf_op jit(solution)/shard_map/ppermute | solution.py:46
  119.1 2.2 collective-permute-done.26
  121.3 2.8 %collective-permute-start.27 = (f32[2,64]{1,0:T(2,128)S(1)}, f32[2,64]{1,0:T(2,128)S(1)}, u32[]{:S(2)}, u32[]{:S(2)}) collective-permute-start(f32[2,64]{1,0:T(2,128)S(1)} %pad_maximum_fusion.13), channel_id=1, source_target_pairs={{0,4},{1,5},{2,6},{3,7},{4,0},{5,1},{6,2},{7,3},{8,12},{9,13},{10,... | collective-permute-start | bytes 1544 | tf_op jit(solution)/shard_map/ppermute | solution.py:46
  124.2 1.6 collective-permute-done.27
  127.4 1.8 collective-permute-start.35
  129.2 4.4 %collective-permute-done.31 = bf16[64,2176]{1,0:T(8,128)(2,1)S(1)} collective-permute-done((bf16[64,2176]{1,0:T(8,128)(2,1)S(1)}, bf16[64,2176]{1,0:T(8,128)(2,1)S(1)}, u32[]{:S(2)}, u32[]{:S(2)}) %collective-permute-start.31) | collective-permute-done | bytes 278560 | tf_op jit(solution)/shard_map/ppermute | solution.py:104
  133.8 2.8 %collective-permute-done.35 = bf16[64,2176]{1,0:T(8,128)(2,1)S(1)} collective-permute-done((bf16[64,2176]{1,0:T(8,128)(2,1)S(1)}, bf16[64,2176]{1,0:T(8,128)(2,1)S(1)}, u32[]{:S(2)}, u32[]{:S(2)}) %collective-permute-start.35) | collective-permute-done | bytes 278560 | tf_op jit(solution)/shard_map/ppermute | solution.py:104
  137.1 4.0 %shard_map.98 = f32[256,2176]{1,0:T(8,128)S(1)} custom-call(s32[8]{0:T(128)S(1)} %slice_bitcast_fusion.4.index_ref, bf16[128,2176]{1,0:T(8,128)(2,1)S(1)} %bitcast.157, bf16[128,2176]{1,0:T(8,128)(2,1)S(1)} %bitcast.159, bf16[2048,2048]{1,0:T(8,128)(2,1)S(1)} %bitcast.154), custom_call_target="tpu_custom_call" | custom-call | flops 2147483648 | bytes 11534336 | tf_op jit(solution)/shard_map/pallas_call | solution.py:204
  143.3 4.0 %shard_map.97 = f32[256,2176]{1,0:T(8,128)S(1)} custom-call(s32[8]{0:T(128)S(1)} %slice_bitcast_fusion.4.index_ref, bf16[128,2176]{1,0:T(8,128)(2,1)S(1)} %bitcast.156, bf16[128,2176]{1,0:T(8,128)(2,1)S(1)} %bitcast.158, bf16[2048,2048]{1,0:T(8,128)(2,1)S(1)} %bitcast.154), custom_call_target="tpu_custom_call" | custom-call | flops 2147483648 | bytes 11534336 | tf_op jit(solution)/shard_map/pallas_call | solution.py:204
  151.1 3.1 %collective-permute-done.37 = bf16[32,2176]{1,0:T(8,128)(2,1)S(1)} collective-permute-done((bf16[32,2176]{1,0:T(8,128)(2,1)S(1)}, bf16[32,2176]{1,0:T(8,128)(2,1)S(1)}, u32[]{:S(2)}, u32[]{:S(2)}) %collective-permute-start.37) | collective-permute-done | bytes 139296 | tf_op jit(solution)/shard_map/ppermute | solution.py:41
  160.5 1.8 collective-permute-start.39
  162.3 2.0 collective-permute-done.55
  165.7 1.7 collective-permute-start.40
  167.8 3.8 %collective-permute-done.56 = bf16[32,2176]{1,0:T(8,128)(2,1)S(1)} collective-permute-done((bf16[32,2176]{1,0:T(8,128)(2,1)S(1)}, bf16[32,2176]{1,0:T(8,128)(2,1)S(1)}, u32[]{:S(2)}, u32[]{:S(2)}) %collective-permute-start.56) | collective-permute-done | bytes 139296 | tf_op jit(solution)/shard_map/ppermute | solution.py:41
  172.0 2.5 %collective-permute-done.42 = bf16[32,2176]{1,0:T(8,128)(2,1)S(1)} collective-permute-done((bf16[32,2176]{1,0:T(8,128)(2,1)S(1)}, bf16[32,2176]{1,0:T(8,128)(2,1)S(1)}, u32[]{:S(2)}, u32[]{:S(2)}) %collective-permute-start.42) | collective-permute-done | bytes 139296 | tf_op jit(solution)/shard_map/ppermute | solution.py:41
  175.0 1.7 collective-permute-done.57
  177.0 2.7 %collective-permute-done.43 = bf16[32,2176]{1,0:T(8,128)(2,1)S(1)} collective-permute-done((bf16[32,2176]{1,0:T(8,128)(2,1)S(1)}, bf16[32,2176]{1,0:T(8,128)(2,1)S(1)}, u32[]{:S(2)}, u32[]{:S(2)}) %collective-permute-start.43) | collective-permute-done | bytes 139296 | tf_op jit(solution)/shard_map/ppermute | solution.py:41
  183.2 1.7 collective-permute-start.44
  186.9 2.3 %collective-permute-done.61.refs_12_ = bf16[32,2048]{1,0:T(8,128)(2,1)S(1)} collective-permute-done((bf16[32,2048]{1,0:T(8,128)(2,1)S(1)}, bf16[32,2048]{1,0:T(8,128)(2,1)S(1)}, u32[]{:S(2)}, u32[]{:S(2)}) %collective-permute-start.61) | collective-permute-done | bytes 131104 | tf_op jit(solution)/shard_map/ppermute | solution.py:41
  189.6 1.7 collective-permute-start.45
  196.0 1.6 collective-permute-start.46
  200.5 1.6 collective-permute-done.63.refs_14_
  205.0 2.1 collective-permute-done.64.refs_15_
  207.6 14.5 %shard_map.99 = (f32[2048,3072]{1,0:T(8,128)}, bf16[64,2048]{1,0:T(8,128)(2,1)}) custom-call(s32[17]{0:T(128)S(1)} %get-tuple-element.108.index_ref, bf16[512,3072]{1,0:T(8,128)(2,1)S(1)} %bitcast.155, bf16[32,2048]{1,0:T(8,128)(2,1)S(1)} %collective-permute-done.47.refs_0_, bf16[32,2048]{1,0:T(8,128)(2,1)S(1)} %collective-permute-done.46.refs_1_, ...), custom_call_target="tpu_custom_call" | custom-call | flops 6442450944 | bytes 30408704 | tf_op jit(solution)/shard_map/pallas_call | solution.py:242
  (194 shorter events, 69.4 us)
Async XLA Ops:
  1.8 6.1 %collective-permute-start = (f32[1,128]{1,0:T(1,128)S(1)}, f32[1,128]{1,0:T(1,128)S(1)}, u32[]{:S(2)}, u32[]{:S(2)}) collective-permute-start(f32[1,128]{1,0:T(1,128)S(1)} %bitcast.177), channel_id=1, source_target_pairs={{0,1},{1,0},{2,3},{3,2},{4,5},{5,4},{6,7},{7,6},{8,9},{9,8},{10,11... | collective-permute-start | bytes 1544 | tf_op jit(solution)/shard_map/ppermute | solution.py:46
  5.8 24.8 %collective-permute-start.6 = (bf16[64,1024]{1,0:T(8,128)(2,1)S(1)}, bf16[64,1024]{1,0:T(8,128)(2,1)S(1)}, u32[]{:S(2)}, u32[]{:S(2)}) collective-permute-start(bf16[64,1024]{1,0:T(8,128)(2,1)S(1)} %get-tuple-element.74), channel_id=1, source_target_pairs={{0,0},{1,1},{2,8},{3,9},{4,16},{5,17},{6,24},{7,25},{8,4},{9,5},{1... | collective-permute-start | bytes 393224 | tf_op jit(solution)/shard_map/ppermute | solution.py:343
  7.9 12.1 %collective-permute-start.2 = (f32[1,128]{1,0:T(1,128)S(1)}, f32[1,128]{1,0:T(1,128)S(1)}, u32[]{:S(2)}, u32[]{:S(2)}) collective-permute-start(f32[1,128]{1,0:T(1,128)S(1)} %bitcast_add_fusion), channel_id=1, source_target_pairs={{0,2},{1,3},{2,0},{3,1},{4,6},{5,7},{6,4},{7,5},{8,10},{9,11},{10,... | collective-permute-start | bytes 1544 | tf_op jit(solution)/shard_map/ppermute | solution.py:46
  20.0 6.1 %collective-permute-start.3 = (f32[1,128]{1,0:T(1,128)S(1)}, f32[1,128]{1,0:T(1,128)S(1)}, u32[]{:S(2)}, u32[]{:S(2)}) collective-permute-start(f32[1,128]{1,0:T(1,128)S(1)} %add.145), channel_id=1, source_target_pairs={{0,4},{1,5},{2,6},{3,7},{4,0},{5,1},{6,2},{7,3},{8,12},{9,13},{10,... | collective-permute-start | bytes 1544 | tf_op jit(solution)/shard_map/ppermute | solution.py:46
  24.1 6.5 %collective-permute-start.7 = (bf16[64,1024]{1,0:T(8,128)(2,1)S(1)}, bf16[64,1024]{1,0:T(8,128)(2,1)S(1)}, u32[]{:S(2)}, u32[]{:S(2)}) collective-permute-start(bf16[64,1024]{1,0:T(8,128)(2,1)S(1)} %collective-permute-done.1.refs_4_), channel_id=1, source_target_pairs={{0,2},{2,4},{4,6},{6,7},{7,5},{5,3},{3,1},{1,0},{8,10},{10,12},{12... | collective-permute-start | bytes 393224 | tf_op jit(solution)/shard_map/ppermute | solution.py:41
  30.6 5.9 %collective-permute-start.8 = (bf16[64,1024]{1,0:T(8,128)(2,1)S(1)}, bf16[64,1024]{1,0:T(8,128)(2,1)S(1)}, u32[]{:S(2)}, u32[]{:S(2)}) collective-permute-start(bf16[64,1024]{1,0:T(8,128)(2,1)S(1)} %collective-permute-done.7.refs_3_), channel_id=1, source_target_pairs={{0,2},{2,4},{4,6},{6,7},{7,5},{5,3},{3,1},{1,0},{8,10},{10,12},{12... | collective-permute-start | bytes 393224 | tf_op jit(solution)/shard_map/ppermute | solution.py:41
  34.1 5.1 %collective-permute-start.12 = (bf16[64,1024]{1,0:T(8,128)(2,1)S(1)}, bf16[64,1024]{1,0:T(8,128)(2,1)S(1)}, u32[]{:S(2)}, u32[]{:S(2)}) collective-permute-start(bf16[64,1024]{1,0:T(8,128)(2,1)S(1)} %collective-permute-done.11.refs_5_), channel_id=1, source_target_pairs={{0,1},{2,0},{4,2},{6,4},{7,6},{5,7},{3,5},{1,3},{8,9},{10,8},{12,1... | collective-permute-start | bytes 393224 | tf_op jit(solution)/shard_map/ppermute | solution.py:41
  36.5 5.1 %collective-permute-start.9 = (bf16[64,1024]{1,0:T(8,128)(2,1)S(1)}, bf16[64,1024]{1,0:T(8,128)(2,1)S(1)}, u32[]{:S(2)}, u32[]{:S(2)}) collective-permute-start(bf16[64,1024]{1,0:T(8,128)(2,1)S(1)} %collective-permute-done.8.refs_2_), channel_id=1, source_target_pairs={{0,2},{2,4},{4,6},{6,7},{7,5},{5,3},{3,1},{1,0},{8,10},{10,12},{12... | collective-permute-start | bytes 393224 | tf_op jit(solution)/shard_map/ppermute | solution.py:41
  39.2 5.1 %collective-permute-start.13 = (bf16[64,1024]{1,0:T(8,128)(2,1)S(1)}, bf16[64,1024]{1,0:T(8,128)(2,1)S(1)}, u32[]{:S(2)}, u32[]{:S(2)}) collective-permute-start(bf16[64,1024]{1,0:T(8,128)(2,1)S(1)} %collective-permute-done.12.refs_6_), channel_id=1, source_target_pairs={{0,1},{2,0},{4,2},{6,4},{7,6},{5,7},{3,5},{1,3},{8,9},{10,8},{12,1... | collective-permute-start | bytes 393224 | tf_op jit(solution)/shard_map/ppermute | solution.py:41
  57.4 16.2 %collective-permute-start.18 = (f32[64,2048]{1,0:T(8,128)S(1)}, f32[64,2048]{1,0:T(8,128)S(1)}, u32[]{:S(2)}, u32[]{:S(2)}) collective-permute-start(f32[64,2048]{1,0:T(8,128)S(1)} %slice.303), channel_id=1, source_target_pairs={{0,16},{8,24},{16,0},{24,8},{1,17},{9,25},{17,1},{25,9},{2,18},{10... | collective-permute-start | bytes 1572872 | tf_op jit(solution)/shard_map/ppermute | solution.py:104
  59.5 5.3 %collective-permute-start.19 = (bf16[64,1024]{1,0:T(8,128)(2,1)S(1)}, bf16[64,1024]{1,0:T(8,128)(2,1)S(1)}, u32[]{:S(2)}, u32[]{:S(2)}) collective-permute-start(bf16[64,1024]{1,0:T(8,128)(2,1)S(1)} %collective-permute-done.6.refs_3_), channel_id=1, source_target_pairs={{0,1},{2,0},{4,2},{6,4},{7,6},{5,7},{3,5},{1,3},{8,9},{10,8},{12,1... | collective-permute-start | bytes 393224 | tf_op jit(solution)/shard_map/ppermute | solution.py:41
  59.5 5.3 %collective-permute-start.14 = (bf16[64,1024]{1,0:T(8,128)(2,1)S(1)}, bf16[64,1024]{1,0:T(8,128)(2,1)S(1)}, u32[]{:S(2)}, u32[]{:S(2)}) collective-permute-start(bf16[64,1024]{1,0:T(8,128)(2,1)S(1)} %collective-permute-done.6.refs_3_), channel_id=1, source_target_pairs={{0,2},{2,4},{4,6},{6,7},{7,5},{5,3},{3,1},{1,0},{8,10},{10,12},{12... | collective-permute-start | bytes 393224 | tf_op jit(solution)/shard_map/ppermute | solution.py:41
  64.8 6.7 %collective-permute-start.15 = (bf16[64,1024]{1,0:T(8,128)(2,1)S(1)}, bf16[64,1024]{1,0:T(8,128)(2,1)S(1)}, u32[]{:S(2)}, u32[]{:S(2)}) collective-permute-start(bf16[64,1024]{1,0:T(8,128)(2,1)S(1)} %collective-permute-done.14.refs_2_), channel_id=1, source_target_pairs={{0,2},{2,4},{4,6},{6,7},{7,5},{5,3},{3,1},{1,0},{8,10},{10,12},{12... | collective-permute-start | bytes 393224 | tf_op jit(solution)/shard_map/ppermute | solution.py:41
  71.5 9.4 %collective-permute-start.17 = (bf16[64,1024]{1,0:T(8,128)(2,1)S(1)}, bf16[64,1024]{1,0:T(8,128)(2,1)S(1)}, u32[]{:S(2)}, u32[]{:S(2)}) collective-permute-start(bf16[64,1024]{1,0:T(8,128)(2,1)S(1)} %collective-permute-done.15.refs_1_), channel_id=1, source_target_pairs={{0,2},{2,4},{4,6},{6,7},{7,5},{5,3},{3,1},{1,0},{8,10},{10,12},{12... | collective-permute-start | bytes 393224 | tf_op jit(solution)/shard_map/ppermute | solution.py:41
  72.4 5.7 %collective-permute-start.21 = (bf16[64,1024]{1,0:T(8,128)(2,1)S(1)}, bf16[64,1024]{1,0:T(8,128)(2,1)S(1)}, u32[]{:S(2)}, u32[]{:S(2)}) collective-permute-start(bf16[64,1024]{1,0:T(8,128)(2,1)S(1)} %collective-permute-done.20.refs_5_), channel_id=1, source_target_pairs={{0,1},{2,0},{4,2},{6,4},{7,6},{5,7},{3,5},{1,3},{8,9},{10,8},{12,1... | collective-permute-start | bytes 393224 | tf_op jit(solution)/shard_map/ppermute | solution.py:41
  91.6 7.6 %collective-permute-start.23 = (f32[128,2048]{1,0:T(8,128)}, f32[128,2048]{1,0:T(8,128)}, u32[]{:S(2)}, u32[]{:S(2)}) collective-permute-start(f32[128,2048]{1,0:T(8,128)} %get-tuple-element.34), channel_id=1, source_target_pairs={{0,8},{8,0},{16,24},{24,16},{1,9},{9,1},{17,25},{25,17},{2,10},{10... | collective-permute-start | bytes 3145736 | tf_op jit(solution)/shard_map/ppermute | solution.py:100
  100.8 12.7 %collective-permute-start.24 = (f32[64,2048]{1,0:T(8,128)S(1)}, f32[64,2048]{1,0:T(8,128)S(1)}, u32[]{:S(2)}, u32[]{:S(2)}) collective-permute-start(f32[64,2048]{1,0:T(8,128)S(1)} %slice.305), channel_id=1, source_target_pairs={{0,16},{8,24},{16,0},{24,8},{1,17},{9,25},{17,1},{25,9},{2,18},{10... | collective-permute-start | bytes 1572872 | tf_op jit(solution)/shard_map/ppermute | solution.py:104
  100.9 5.1 %collective-permute-start.30 = (f32[2,192]{1,0:T(2,128)S(1)}, f32[2,192]{1,0:T(2,128)S(1)}, u32[]{:S(2)}, u32[]{:S(2)}) collective-permute-start(f32[2,192]{1,0:T(2,128)S(1)} %pad_maximum_fusion.9), channel_id=1, source_target_pairs={{0,4},{1,5},{2,6},{3,7},{4,0},{5,1},{6,2},{7,3},{8,12},{9,13},{10,... | collective-permute-start | bytes 4616 | tf_op jit(solution)/shard_map/ppermute | solution.py:46
  127.0 6.6 %collective-permute-start.31 = (bf16[64,2176]{1,0:T(8,128)(2,1)S(1)}, bf16[64,2176]{1,0:T(8,128)(2,1)S(1)}, u32[]{:S(2)}, u32[]{:S(2)}) collective-permute-start(bf16[64,2176]{1,0:T(8,128)(2,1)S(1)} %get-tuple-element.73), channel_id=1, source_target_pairs={{0,16},{8,24},{16,0},{24,8},{1,17},{9,25},{17,1},{25,9},{2,18},{10... | collective-permute-start | bytes 835592 | tf_op jit(solution)/shard_map/ppermute | solution.py:104
  127.4 9.2 %collective-permute-start.35 = (bf16[64,2176]{1,0:T(8,128)(2,1)S(1)}, bf16[64,2176]{1,0:T(8,128)(2,1)S(1)}, u32[]{:S(2)}, u32[]{:S(2)}) collective-permute-start(bf16[64,2176]{1,0:T(8,128)(2,1)S(1)} %get-tuple-element.71), channel_id=1, source_target_pairs={{0,16},{8,24},{16,0},{24,8},{1,17},{9,25},{17,1},{25,9},{2,18},{10... | collective-permute-start | bytes 835592 | tf_op jit(solution)/shard_map/ppermute | solution.py:104
  136.6 6.7 %collective-permute-start.36 = (bf16[2,64,2176]{2,1,0:T(8,128)(2,1)S(1)}, bf16[2,64,2176]{2,1,0:T(8,128)(2,1)S(1)}, u32[]{:S(2)}, u32[]{:S(2)}) collective-permute-start(bf16[2,64,2176]{2,1,0:T(8,128)(2,1)S(1)} %pad_maximum_fusion.3), channel_id=1, source_target_pairs={{0,8},{8,0},{16,24},{24,16},{1,9},{9,1},{17,25},{25,17},{2,10},{10... | collective-permute-start | bytes 1671176 | tf_op jit(solution)/shard_map/ppermute | solution.py:100
  136.7 40.0 %collective-permute-start.33 = (bf16[2,64,3072]{2,1,0:T(8,128)(2,1)S(1)}, bf16[2,64,3072]{2,1,0:T(8,128)(2,1)S(1)}, u32[]{:S(2)}, u32[]{:S(2)}) collective-permute-start(bf16[2,64,3072]{2,1,0:T(8,128)(2,1)S(1)} %bitcast.162), channel_id=1, source_target_pairs={{0,16},{8,24},{16,0},{24,8},{1,17},{9,25},{17,1},{25,9},{2,18},{10... | collective-permute-start | bytes 2359304 | tf_op jit(solution)/shard_map/ppermute | solution.py:104
  141.3 8.3 %collective-permute-start.51 = (bf16[32,2176]{1,0:T(8,128)(2,1)S(1)}, bf16[32,2176]{1,0:T(8,128)(2,1)S(1)}, u32[]{:S(2)}, u32[]{:S(2)}) collective-permute-start(bf16[32,2176]{1,0:T(8,128)(2,1)S(1)} %get-tuple-element.62), channel_id=1, source_target_pairs={{0,2},{2,4},{4,6},{6,7},{7,5},{5,3},{3,1},{1,0},{8,10},{10,12},{12... | collective-permute-start | bytes 417800 | tf_op jit(solution)/shard_map/ppermute | solution.py:41
  142.7 12.9 %collective-permute-start.54 = (bf16[32,2176]{1,0:T(8,128)(2,1)S(1)}, bf16[32,2176]{1,0:T(8,128)(2,1)S(1)}, u32[]{:S(2)}, u32[]{:S(2)}) collective-permute-start(bf16[32,2176]{1,0:T(8,128)(2,1)S(1)} %get-tuple-element.63), channel_id=1, source_target_pairs={{0,1},{2,0},{4,2},{6,4},{7,6},{5,7},{3,5},{1,3},{8,9},{10,8},{12,1... | collective-permute-start | bytes 417800 | tf_op jit(solution)/shard_map/ppermute | solution.py:41
  147.5 6.6 %collective-permute-start.37 = (bf16[32,2176]{1,0:T(8,128)(2,1)S(1)}, bf16[32,2176]{1,0:T(8,128)(2,1)S(1)}, u32[]{:S(2)}, u32[]{:S(2)}) collective-permute-start(bf16[32,2176]{1,0:T(8,128)(2,1)S(1)} %get-tuple-element.64), channel_id=1, source_target_pairs={{0,2},{2,4},{4,6},{6,7},{7,5},{5,3},{3,1},{1,0},{8,10},{10,12},{12... | collective-permute-start | bytes 417800 | tf_op jit(solution)/shard_map/ppermute | solution.py:41
  149.0 16.6 %collective-permute-start.41 = (bf16[32,2176]{1,0:T(8,128)(2,1)S(1)}, bf16[32,2176]{1,0:T(8,128)(2,1)S(1)}, u32[]{:S(2)}, u32[]{:S(2)}) collective-permute-start(bf16[32,2176]{1,0:T(8,128)(2,1)S(1)} %get-tuple-element.65), channel_id=1, source_target_pairs={{0,1},{2,0},{4,2},{6,4},{7,6},{5,7},{3,5},{1,3},{8,9},{10,8},{12,1... | collective-permute-start | bytes 417800 | tf_op jit(solution)/shard_map/ppermute | solution.py:41
  149.6 7.5 %collective-permute-start.52 = (bf16[32,2176]{1,0:T(8,128)(2,1)S(1)}, bf16[32,2176]{1,0:T(8,128)(2,1)S(1)}, u32[]{:S(2)}, u32[]{:S(2)}) collective-permute-start(bf16[32,2176]{1,0:T(8,128)(2,1)S(1)} %fusion.15), channel_id=1, source_target_pairs={{0,2},{2,4},{4,6},{6,7},{7,5},{5,3},{3,1},{1,0},{8,10},{10,12},{12... | collective-permute-start | bytes 417800 | tf_op jit(solution)/shard_map/ppermute | solution.py:41
  154.2 6.2 %collective-permute-start.38 = (bf16[32,2176]{1,0:T(8,128)(2,1)S(1)}, bf16[32,2176]{1,0:T(8,128)(2,1)S(1)}, u32[]{:S(2)}, u32[]{:S(2)}) collective-permute-start(bf16[32,2176]{1,0:T(8,128)(2,1)S(1)} %fusion.20), channel_id=1, source_target_pairs={{0,2},{2,4},{4,6},{6,7},{7,5},{5,3},{3,1},{1,0},{8,10},{10,12},{12... | collective-permute-start | bytes 417800 | tf_op jit(solution)/shard_map/ppermute | solution.py:41
  157.2 17.8 %collective-permute-start.53 = (bf16[32,2176]{1,0:T(8,128)(2,1)S(1)}, bf16[32,2176]{1,0:T(8,128)(2,1)S(1)}, u32[]{:S(2)}, u32[]{:S(2)}) collective-permute-start(bf16[32,2176]{1,0:T(8,128)(2,1)S(1)} %get-tuple-element.58), channel_id=1, source_target_pairs={{0,2},{2,4},{4,6},{6,7},{7,5},{5,3},{3,1},{1,0},{8,10},{10,12},{12... | collective-permute-start | bytes 417800 | tf_op jit(solution)/shard_map/ppermute | solution.py:41
  158.6 5.6 %collective-permute-start.55 = (bf16[32,2176]{1,0:T(8,128)(2,1)S(1)}, bf16[32,2176]{1,0:T(8,128)(2,1)S(1)}, u32[]{:S(2)}, u32[]{:S(2)}) collective-permute-start(bf16[32,2176]{1,0:T(8,128)(2,1)S(1)} %get-tuple-element.59), channel_id=1, source_target_pairs={{0,1},{2,0},{4,2},{6,4},{7,6},{5,7},{3,5},{1,3},{8,9},{10,8},{12,1... | collective-permute-start | bytes 417800 | tf_op jit(solution)/shard_map/ppermute | solution.py:41
  160.5 5.2 %collective-permute-start.39 = (bf16[32,2176]{1,0:T(8,128)(2,1)S(1)}, bf16[32,2176]{1,0:T(8,128)(2,1)S(1)}, u32[]{:S(2)}, u32[]{:S(2)}) collective-permute-start(bf16[32,2176]{1,0:T(8,128)(2,1)S(1)} %fusion.21), channel_id=1, source_target_pairs={{0,2},{2,4},{4,6},{6,7},{7,5},{5,3},{3,1},{1,0},{8,10},{10,12},{12... | collective-permute-start | bytes 417800 | tf_op jit(solution)/shard_map/ppermute | solution.py:41
  164.3 7.3 %collective-permute-start.56 = (bf16[32,2176]{1,0:T(8,128)(2,1)S(1)}, bf16[32,2176]{1,0:T(8,128)(2,1)S(1)}, u32[]{:S(2)}, u32[]{:S(2)}) collective-permute-start(bf16[32,2176]{1,0:T(8,128)(2,1)S(1)} %fusion.13), channel_id=1, source_target_pairs={{0,1},{2,0},{4,2},{6,4},{7,6},{5,7},{3,5},{1,3},{8,9},{10,8},{12,1... | collective-permute-start | bytes 417800 | tf_op jit(solution)/shard_map/ppermute | solution.py:41
  165.7 11.3 %collective-permute-start.40 = (bf16[32,2176]{1,0:T(8,128)(2,1)S(1)}, bf16[32,2176]{1,0:T(8,128)(2,1)S(1)}, u32[]{:S(2)}, u32[]{:S(2)}) collective-permute-start(bf16[32,2176]{1,0:T(8,128)(2,1)S(1)} %get-tuple-element.60), channel_id=1, source_target_pairs={{0,2},{2,4},{4,6},{6,7},{7,5},{5,3},{3,1},{1,0},{8,10},{10,12},{12... | collective-permute-start | bytes 417800 | tf_op jit(solution)/shard_map/ppermute | solution.py:41
  167.4 7.1 %collective-permute-start.42 = (bf16[32,2176]{1,0:T(8,128)(2,1)S(1)}, bf16[32,2176]{1,0:T(8,128)(2,1)S(1)}, u32[]{:S(2)}, u32[]{:S(2)}) collective-permute-start(bf16[32,2176]{1,0:T(8,128)(2,1)S(1)} %get-tuple-element.61), channel_id=1, source_target_pairs={{0,1},{2,0},{4,2},{6,4},{7,6},{5,7},{3,5},{1,3},{8,9},{10,8},{12,1... | collective-permute-start | bytes 417800 | tf_op jit(solution)/shard_map/ppermute | solution.py:41
  171.6 5.1 %collective-permute-start.57 = (bf16[32,2176]{1,0:T(8,128)(2,1)S(1)}, bf16[32,2176]{1,0:T(8,128)(2,1)S(1)}, u32[]{:S(2)}, u32[]{:S(2)}) collective-permute-start(bf16[32,2176]{1,0:T(8,128)(2,1)S(1)} %fusion.14), channel_id=1, source_target_pairs={{0,1},{2,0},{4,2},{6,4},{7,6},{5,7},{3,5},{1,3},{8,9},{10,8},{12,1... | collective-permute-start | bytes 417800 | tf_op jit(solution)/shard_map/ppermute | solution.py:41
  174.6 5.1 %collective-permute-start.43 = (bf16[32,2176]{1,0:T(8,128)(2,1)S(1)}, bf16[32,2176]{1,0:T(8,128)(2,1)S(1)}, u32[]{:S(2)}, u32[]{:S(2)}) collective-permute-start(bf16[32,2176]{1,0:T(8,128)(2,1)S(1)} %fusion.19), channel_id=1, source_target_pairs={{0,1},{2,0},{4,2},{6,4},{7,6},{5,7},{3,5},{1,3},{8,9},{10,8},{12,1... | collective-permute-start | bytes 417800 | tf_op jit(solution)/shard_map/ppermute | solution.py:41
  176.9 27.2 %collective-permute-start.34 = (bf16[2,2,64,3072]{3,2,0,1:T(8,128)(2,1)S(1)}, bf16[2,2,64,3072]{3,2,0,1:T(8,128)(2,1)S(1)}, u32[]{:S(2)}, u32[]{:S(2)}) collective-permute-start(bf16[2,2,64,3072]{3,2,0,1:T(8,128)(2,1)S(1)} %pad_maximum_fusion.1), channel_id=1, source_target_pairs={{0,8},{8,0},{16,24},{24,16},{1,9},{9,1},{17,25},{25,17},{2,10},{10... | collective-permute-start | bytes 4718600 | tf_op jit(solution)/shard_map/ppermute | solution.py:100
  182.8 6.4 %collective-permute-start.61 = (bf16[32,2048]{1,0:T(8,128)(2,1)S(1)}, bf16[32,2048]{1,0:T(8,128)(2,1)S(1)}, u32[]{:S(2)}, u32[]{:S(2)}) collective-permute-start(bf16[32,2048]{1,0:T(8,128)(2,1)S(1)} %get-tuple-element.76.refs_11_), channel_id=1, source_target_pairs={{0,1},{2,0},{4,2},{6,4},{7,6},{5,7},{3,5},{1,3},{8,9},{10,8},{12,1... | collective-permute-start | bytes 393224 | tf_op jit(solution)/shard_map/ppermute | solution.py:41
  183.2 6.4 %collective-permute-start.44 = (bf16[32,2048]{1,0:T(8,128)(2,1)S(1)}, bf16[32,2048]{1,0:T(8,128)(2,1)S(1)}, u32[]{:S(2)}, u32[]{:S(2)}) collective-permute-start(bf16[32,2048]{1,0:T(8,128)(2,1)S(1)} %get-tuple-element.77.refs_4_), channel_id=1, source_target_pairs={{0,2},{2,4},{4,6},{6,7},{7,5},{5,3},{3,1},{1,0},{8,10},{10,12},{12... | collective-permute-start | bytes 393224 | tf_op jit(solution)/shard_map/ppermute | solution.py:41
  184.9 7.2 %collective-permute-start.58 = (bf16[32,2048]{1,0:T(8,128)(2,1)S(1)}, bf16[32,2048]{1,0:T(8,128)(2,1)S(1)}, u32[]{:S(2)}, u32[]{:S(2)}) collective-permute-start(bf16[32,2048]{1,0:T(8,128)(2,1)S(1)} %get-tuple-element.76.refs_11_), channel_id=1, source_target_pairs={{0,2},{2,4},{4,6},{6,7},{7,5},{5,3},{3,1},{1,0},{8,10},{10,12},{12... | collective-permute-start | bytes 393224 | tf_op jit(solution)/shard_map/ppermute | solution.py:41
  186.3 7.3 %collective-permute-start.48 = (bf16[32,2048]{1,0:T(8,128)(2,1)S(1)}, bf16[32,2048]{1,0:T(8,128)(2,1)S(1)}, u32[]{:S(2)}, u32[]{:S(2)}) collective-permute-start(bf16[32,2048]{1,0:T(8,128)(2,1)S(1)} %get-tuple-element.77.refs_4_), channel_id=1, source_target_pairs={{0,1},{2,0},{4,2},{6,4},{7,6},{5,7},{3,5},{1,3},{8,9},{10,8},{12,1... | collective-permute-start | bytes 393224 | tf_op jit(solution)/shard_map/ppermute | solution.py:41
  189.2 6.4 %collective-permute-start.62 = (bf16[32,2048]{1,0:T(8,128)(2,1)S(1)}, bf16[32,2048]{1,0:T(8,128)(2,1)S(1)}, u32[]{:S(2)}, u32[]{:S(2)}) collective-permute-start(bf16[32,2048]{1,0:T(8,128)(2,1)S(1)} %collective-permute-done.61.refs_12_), channel_id=1, source_target_pairs={{0,1},{2,0},{4,2},{6,4},{7,6},{5,7},{3,5},{1,3},{8,9},{10,8},{12,1... | collective-permute-start | bytes 393224 | tf_op jit(solution)/shard_map/ppermute | solution.py:41
  189.6 6.4 %collective-permute-start.45 = (bf16[32,2048]{1,0:T(8,128)(2,1)S(1)}, bf16[32,2048]{1,0:T(8,128)(2,1)S(1)}, u32[]{:S(2)}, u32[]{:S(2)}) collective-permute-start(bf16[32,2048]{1,0:T(8,128)(2,1)S(1)} %collective-permute-done.44.refs_3_), channel_id=1, source_target_pairs={{0,2},{2,4},{4,6},{6,7},{7,5},{5,3},{3,1},{1,0},{8,10},{10,12},{12... | collective-permute-start | bytes 393224 | tf_op jit(solution)/shard_map/ppermute | solution.py:41
  192.1 6.4 %collective-permute-start.59 = (bf16[32,2048]{1,0:T(8,128)(2,1)S(1)}, bf16[32,2048]{1,0:T(8,128)(2,1)S(1)}, u32[]{:S(2)}, u32[]{:S(2)}) collective-permute-start(bf16[32,2048]{1,0:T(8,128)(2,1)S(1)} %collective-permute-done.58.refs_10_), channel_id=1, source_target_pairs={{0,2},{2,4},{4,6},{6,7},{7,5},{5,3},{3,1},{1,0},{8,10},{10,12},{12... | collective-permute-start | bytes 393224 | tf_op jit(solution)/shard_map/ppermute | solution.py:41
  193.6 6.4 %collective-permute-start.49 = (bf16[32,2048]{1,0:T(8,128)(2,1)S(1)}, bf16[32,2048]{1,0:T(8,128)(2,1)S(1)}, u32[]{:S(2)}, u32[]{:S(2)}) collective-permute-start(bf16[32,2048]{1,0:T(8,128)(2,1)S(1)} %collective-permute-done.48.refs_5_), channel_id=1, source_target_pairs={{0,1},{2,0},{4,2},{6,4},{7,6},{5,7},{3,5},{1,3},{8,9},{10,8},{12,1... | collective-permute-start | bytes 393224 | tf_op jit(solution)/shard_map/ppermute | solution.py:41
  195.6 6.5 %collective-permute-start.63 = (bf16[32,2048]{1,0:T(8,128)(2,1)S(1)}, bf16[32,2048]{1,0:T(8,128)(2,1)S(1)}, u32[]{:S(2)}, u32[]{:S(2)}) collective-permute-start(bf16[32,2048]{1,0:T(8,128)(2,1)S(1)} %collective-permute-done.62.refs_13_), channel_id=1, source_target_pairs={{0,1},{2,0},{4,2},{6,4},{7,6},{5,7},{3,5},{1,3},{8,9},{10,8},{12,1... | collective-permute-start | bytes 393224 | tf_op jit(solution)/shard_map/ppermute | solution.py:41
  196.0 6.6 %collective-permute-start.46 = (bf16[32,2048]{1,0:T(8,128)(2,1)S(1)}, bf16[32,2048]{1,0:T(8,128)(2,1)S(1)}, u32[]{:S(2)}, u32[]{:S(2)}) collective-permute-start(bf16[32,2048]{1,0:T(8,128)(2,1)S(1)} %collective-permute-done.45.refs_2_), channel_id=1, source_target_pairs={{0,2},{2,4},{4,6},{6,7},{7,5},{5,3},{3,1},{1,0},{8,10},{10,12},{12... | collective-permute-start | bytes 393224 | tf_op jit(solution)/shard_map/ppermute | solution.py:41
  198.5 6.0 %collective-permute-start.60 = (bf16[32,2048]{1,0:T(8,128)(2,1)S(1)}, bf16[32,2048]{1,0:T(8,128)(2,1)S(1)}, u32[]{:S(2)}, u32[]{:S(2)}) collective-permute-start(bf16[32,2048]{1,0:T(8,128)(2,1)S(1)} %collective-permute-done.59.refs_9_), channel_id=1, source_target_pairs={{0,2},{2,4},{4,6},{6,7},{7,5},{5,3},{3,1},{1,0},{8,10},{10,12},{12... | collective-permute-start | bytes 393224 | tf_op jit(solution)/shard_map/ppermute | solution.py:41
  (29 other events, 306.9 us)

commit v6 on v5

--- a/solution.py
+++ b/solution.py
@@ -30,6 +30,7 @@
 class Ring:
     def __init__(self, size, columns):
         self.size = size
+        self.columns = columns
         self.half = size // 2
         self.order = ring_order(size // columns, columns)
         self.place = [0] * size
@@ -45,36 +46,39 @@
     def partner(self, x, bit):
         return lax.ppermute(x, "vocab", [(v, v ^ bit) for v in range(self.size)])
 
-    def meet(self, x, merge, waits=None):
-        bit = 1
-        while bit < self.size:
-            if waits and bit in waits:
-                x = after(x, waits[bit]())
-            x = merge(x, self.partner(x, bit))
-            bit *= 2
+    def meetings(self, merge):
+        near = [bit for bit in range(1, self.columns)]
+        far = [bit for bit in range(self.columns, self.size, self.columns)]
+        return [
+            lambda x, bits=bits: merge([x] + [self.partner(x, bit) for bit in bits])
+            for bits in (near, far)
+        ]
+
+    def meet(self, x, merge):
+        for round in self.meetings(merge):
+            x = round(x)
         return x
 
     def reach(self, h):
         return (self.half, self.half - 1) if h % 2 == 0 else (self.half - 1, self.half)
 
-    def gather(self, block, h, waits=None):
+    def gather(self, block, h, seen=None):
         far_ahead, far_behind = self.reach(h)
         ahead, behind = [block], [block]
         for step in range(self.half):
-            if waits and step in waits:
-                others = waits[step]()
-                ahead[-1], behind[-1] = after(ahead[-1], others), after(behind[-1], others)
             if step < far_ahead:
                 ahead.append(self.shift(ahead[-1], 1))
             if step < far_behind:
                 behind.append(self.shift(behind[-1], -1))
+            if seen:
+                seen(step, (ahead[-1], behind[-1]))
         return ahead[1:][::-1] + [block] + behind[1:]
 
     def sources(self, vocab, h):
         p, far_ahead = self.place[vocab], self.reach(h)[0]
         return [(p + k - far_ahead) % self.size for k in range(self.size)]
 
-    def scatter_sum(self, part, h):
+    def scatter_sum(self, part, h, seen=None):
         far_ahead, far_behind = self.reach(h)
         got_ahead = got_behind = None
         for step in range(self.half, 0, -1):
@@ -84,6 +88,8 @@
             if step <= far_behind:
                 behind = part(-step) if got_behind is None else part(-step) + got_behind
                 got_behind = self.shift(behind.astype(BF16), -1).astype(F32)
+            if seen:
+                seen(self.half - step, (got_ahead, got_behind))
         return part(0) + got_ahead + got_behind
 
 
@@ -103,8 +109,11 @@
         size = self.size
         return lax.ppermute(x, "dp", [(i, (i + CORES * step) % size) for i in range(size)])
 
+    def gather_chips(self, block):
+        return jnp.stack([block] + [self.shift(block, -d) for d in range(1, self.chips)])
+
     def gather_halves(self, block):
-        mine = jnp.stack([block] + [self.shift(block, -d) for d in range(1, self.chips)])
+        mine = self.gather_chips(block)
         return mine, self.swap(mine)
 
     def gather(self, block):
@@ -123,14 +132,24 @@
 
 
 def project_kernel(count, index_ref, factor_ref, gain_ref, weight_ref, *refs):
-    blocks = refs[:count]
-    keep_ref, send_ref, piece_ref, raw_ref, normed_ref, turned_ref = refs[count:]
+    blocks, refs = refs[:count], refs[count:]
+    logits_refs, piece_refs = refs[:CORES], refs[CORES:-5]
+    raw_ref, normed_ref, turned_ref, held_ref, sems = refs[-5:]
     rows, width = blocks[0].shape
-    piece = piece_ref.shape[0]
-    half = keep_ref.shape[0]
-
-    @pl.when(pl.program_id(0) == 0)
+    step = pl.program_id(0)
+    tiles, tile = held_ref.shape[:2]
+    piece = piece_refs[0].shape[0]
+    half = logits_refs[0].shape[0]
+
+    def fetch(n):
+        return pltpu.make_async_copy(
+            weight_ref.at[pl.ds(n * tile, tile), :], held_ref.at[n], sems.at[n]
+        )
+
+    @pl.when(step == 0)
     def _():
+        for n in range(tiles):
+            fetch(n).start()
         for k, ref in enumerate(blocks):
             start = pl.multiple_of(index_ref[k] * rows, rows)
             column = pl.multiple_of(index_ref[count + k] * width, width)
@@ -140,36 +159,40 @@
             normed_ref[group, :] = (
                 raw_ref[group, :].astype(F32) * factor_ref[g] * gain_ref[...]
             ).astype(BF16)
+        for h, ref in enumerate(piece_refs):
+            start = pl.multiple_of(index_ref[2 * count + h] * piece, piece)
+            ref[...] = raw_ref[pl.ds(start, piece), :]
         transpose_into(turned_ref, normed_ref)
-        start = pl.multiple_of(index_ref[2 * count] * piece, piece)
-        piece_ref[...] = raw_ref[pl.ds(start, piece), :]
-
-    logits = jnp.dot(weight_ref[...], turned_ref[...], preferred_element_type=F32).T
-    keep_ref[...] = logits[:half]
-    send_ref[...] = logits[half:]
+
+    fetch(step).wait()
+    logits = jnp.dot(held_ref[step], turned_ref[...], preferred_element_type=F32).T
+    for k, ref in enumerate(logits_refs):
+        ref[...] = logits[k * half : (k + 1) * half]
 
 
 def project(index, blocks, factor, gain, weight, piece_rows):
-    rows = blocks[0].shape[0]
     vocab, depth = weight.shape
-    all_rows = factor.shape[0] * rows
+    all_rows = factor.shape[0] * blocks[0].shape[0]
     half = all_rows // CORES
     tile = min(vocab, 512)
     out = jax.ShapeDtypeStruct((half, vocab), F32)
+    piece = jax.ShapeDtypeStruct((piece_rows, depth), BF16)
     return pl.pallas_call(
         functools.partial(project_kernel, len(blocks)),
         grid=(vocab // tile,),
-        in_specs=[SMEM, VMEM, VMEM, pl.BlockSpec((tile, depth), lambda n: (n, 0))]
+        in_specs=[SMEM, VMEM, VMEM, pl.BlockSpec(memory_space=pltpu.HBM)]
         + [VMEM] * len(blocks),
-        out_specs=[pl.BlockSpec((half, tile), lambda n: (0, n))] * 2
-        + [pl.BlockSpec((piece_rows, depth), lambda n: (0, 0))],
-        out_shape=[out, out, jax.ShapeDtypeStruct((piece_rows, depth), BF16)],
+        out_specs=[pl.BlockSpec((half, tile), lambda n: (0, n))] * CORES
+        + [pl.BlockSpec((piece_rows, depth), lambda n: (0, 0))] * CHUNKS,
+        out_shape=[out] * CORES + [piece] * CHUNKS,
         scratch_shapes=[
             pltpu.VMEM((all_rows, depth), BF16),
             pltpu.VMEM((all_rows, depth), BF16),
             pltpu.VMEM((depth, all_rows), BF16),
+            pltpu.VMEM((vocab // tile, tile, depth), BF16),
+            pltpu.SemaphoreType.DMA((vocab // tile,)),
         ],
-        compiler_params=pltpu.CompilerParams(vmem_limit_bytes=24 * 2**20),
+        compiler_params=pltpu.CompilerParams(vmem_limit_bytes=48 * 2**20),
         cost_estimate=pl.CostEstimate(
             flops=2 * all_rows * depth * vocab,
             bytes_accessed=2 * vocab * depth + all_rows * (2 * depth + 4 * vocab),
@@ -217,45 +240,45 @@
     )(index, mine, other, weight)
 
 
-def outer_kernel(count, index_ref, chosen_ref, *refs):
-    pieces, (out_ref, share_ref, grad_ref, turned_ref) = refs[:-4], refs[-4:]
+def outer_kernel(count, tile, index_ref, chosen_ref, *refs):
+    pieces, (out_ref, share_ref, grad_ref) = refs[:-3], refs[-3:]
     rows = pieces[0].shape[0]
     share = share_ref.shape[0]
-
-    @pl.when(pl.program_id(0) == 0)
+    step = pl.program_id(0)
+
+    @pl.when(step == 0)
     def _():
         for k, ref in enumerate(pieces):
             start = pl.multiple_of((k // count * count + index_ref[k]) * rows, rows)
             grad_ref[pl.ds(start, rows), :] = ref[...]
-        transpose_into(turned_ref, grad_ref)
         start = pl.multiple_of(index_ref[len(pieces)] * share, share)
         share_ref[...] = grad_ref[pl.ds(start, share), :]
 
-    out_ref[...] = jnp.dot(turned_ref[...], chosen_ref[...], preferred_element_type=F32)
+    columns = pl.ds(pl.multiple_of(step * tile, tile), tile)
+    out_ref[...] = lax.dot_general(
+        grad_ref[:, columns], chosen_ref[...], (((0,), (0,)), ((), ())), preferred_element_type=F32
+    )
 
 
 def outer(index, chosen, chunks, share_rows):
     depth = chunks[0][0].shape[1]
     all_rows, joined = chosen.shape
-    tile = min(joined, 256)
+    tile = min(depth, 256)
     pieces = [x for chunk in chunks for x in chunk]
     return pl.pallas_call(
-        functools.partial(outer_kernel, len(chunks[0])),
-        grid=(joined // tile,),
-        in_specs=[SMEM, pl.BlockSpec((all_rows, tile), lambda n: (0, n))] + [VMEM] * len(pieces),
+        functools.partial(outer_kernel, len(chunks[0]), tile),
+        grid=(depth // tile,),
+        in_specs=[SMEM, VMEM] + [VMEM] * len(pieces),
         out_specs=[
-            pl.BlockSpec((depth, tile), lambda n: (0, n)),
+            pl.BlockSpec((tile, joined), lambda n: (n, 0)),
             pl.BlockSpec((share_rows, depth), lambda n: (0, 0)),
         ],
         out_shape=[
             jax.ShapeDtypeStruct((depth, joined), F32),
             jax.ShapeDtypeStruct((share_rows, depth), BF16),
         ],
-        scratch_shapes=[
-            pltpu.VMEM((all_rows, depth), BF16),
-            pltpu.VMEM((depth, all_rows), BF16),
-        ],
-        compiler_params=pltpu.CompilerParams(vmem_limit_bytes=32 * 2**20),
+        scratch_shapes=[pltpu.VMEM((all_rows, depth), BF16)],
+        compiler_params=pltpu.CompilerParams(vmem_limit_bytes=40 * 2**20),
         cost_estimate=pl.CostEstimate(
             flops=2 * all_rows * depth * joined,
             bytes_accessed=4 * depth * joined + 2 * all_rows * (depth + joined),
@@ -277,12 +300,13 @@
     for g in range(groups.size):
         for v in range(parts):
             p = ring.place[v]
+            held = [ring.order[q] for q in ring.sources(v, 0)]
+            group = [i // slots % groups.chips * CORES + i // slots // groups.chips for i in held]
+            add("place", [groups.entry(g, i) for i in group] + [i % slots for i in held])
             for h in range(CHUNKS):
-                held = [ring.order[q] for q in ring.sources(v, h)]
-                group = [
-                    i // slots % groups.chips * CORES + i // slots // groups.chips for i in held
-                ]
-                add(f"place{h}", [groups.entry(g, i) for i in group] + [i % slots for i in held] + [p])
+                start = p * piece_rows
+                start = start // chunk_rows * group_rows + h * chunk_rows + start % chunk_rows
+                table["place"][-1].append(start // piece_rows)
             entry = groups.entry(g, v * share_rows // group_rows)
             first = v * share_rows % group_rows
             start = first // chunk_rows * step_rows + entry * chunk_rows + first % chunk_rows
@@ -340,12 +364,22 @@
     turn = [
         (g * parts + v, column_owner(g, v)) for g in range(groups.size) for v in range(parts)
     ]
-    turned = [lax.ppermute(chunk(hidden, h), ("dp", "vocab"), turn) for h in range(CHUNKS)]
+    turned = lax.ppermute(hidden, ("dp", "vocab"), turn)
 
     live_rows = (valid_rows == 1).astype(F32)
     squares = jnp.sum(jnp.square(hidden.astype(F32)), axis=1)[None]
-    squares = ring.meet(squares, lambda a, b: a + b, {2: lambda: (turned[0],)})
-    both = groups.gather(jnp.concatenate([squares, live_rows[None]]))
+    rounds = ring.meetings(lambda terms: sum(terms[1:], terms[0]))
+    rounds.append(lambda x: groups.gather_chips(jnp.concatenate([x, live_rows[None]])))
+    rounds.append(lambda x: jnp.concatenate([x, groups.swap(x)], axis=0))
+    exchanged = [rounds[0](squares)]
+    late = rounds[1:]
+
+    def seen(step, arrivals):
+        if step < len(late):
+            exchanged.append(late[step](after(exchanged[-1], arrivals)))
+
+    blocks = ring.gather(turned, 0, seen)
+    both = exchanged[-1]
     valid_count = jnp.sum(both[:, 1])
     row_factor = lax.rsqrt(both[:, 0] / model_width + 1e-05)
 
@@ -353,10 +387,9 @@
     target_top = jnp.max(targets, axis=1)
     target_total = jnp.sum(jnp.exp(targets - target_top[:, None]), axis=1)
 
-    def merge_totals(a, b):
-        top = jnp.maximum(a[0], b[0])
-        total = a[1] * jnp.exp(a[0] - top) + b[1] * jnp.exp(b[0] - top)
-        return jnp.stack([top, total])
+    def merge_totals(terms):
+        top = functools.reduce(jnp.maximum, [x[0] for x in terms])
+        return jnp.stack([top, sum(x[1] * jnp.exp(x[0] - top) for x in terms)])
 
     tree_rows = jnp.arange(group_rows, dtype=jnp.int32) // TREE * TREE + parents
     own_chosen = features.at[tree_rows].get(mode="promise_in_bounds")
@@ -365,56 +398,33 @@
     row_weight = 1048576.0 * live_rows / valid_count
     lane = lax.broadcasted_iota(jnp.uint32, (chunk_rows, LANES), 1)
 
-    def group_logits(h, blocks):
-        factor = row_factor[:, h * chunk_rows : (h + 1) * chunk_rows]
-        keep, send, piece = project(
-            index[f"place{h}"], blocks, factor[:, :, None], gain, head_weight, piece_rows
-        )
-        pieces.append(piece)
-        yield keep
-        summed = keep + groups.swap(send)
-        yield summed
-        summed = summed.reshape(groups.chips, chunk_rows, vocab_width)
-        logits = summed[0]
-        for d in range(1, groups.chips):
-            logits = logits + groups.shift(summed[d], d)
-        yield logits
-
-    gathered, logits_of, pieces = [], [], []
-    for h in range(CHUNKS):
-        waits = {1: lambda: tuple(turned[1:])}
-        if h > 0:
-            stages = group_logits(h - 1, gathered[-1])
-            waits = {
-                0: lambda: (gathered[-1],),
-                1: lambda: (next(stages),),
-                2: lambda: (next(stages),),
-                3: lambda: (logits_of.append(next(stages)), logits_of[-1])[1:],
-            }
-        gathered.append(ring.gather(turned[h], h, waits))
-    logits_of.append(list(group_logits(CHUNKS - 1, gathered[-1]))[-1])
+    keep, send, *pieces = project(
+        index["place"], blocks, row_factor[:, :, None], gain, head_weight, piece_rows
+    )
+    summed = (keep + groups.swap(send)).reshape(groups.chips, group_rows, vocab_width)
+    logits = summed[0]
+    for d in range(1, groups.chips):
+        logits = logits + groups.shift(summed[d], d)
+
+    top = jnp.max(logits, axis=1)
+    total = jnp.sum(jnp.exp(logits - top[:, None]), axis=1)
+    mine = jnp.stack([jnp.concatenate([top, target_top]), jnp.concatenate([total, target_total])])
+    met = ring.meet(mine, merge_totals)
+    scale = jnp.exp(mine[0] - met[0]) / met[1]
+    draft_scale, target_scale = scale[:group_rows], scale[group_rows:]
 
     grads = []
     for h in range(CHUNKS):
-        logits = logits_of[h]
         factor = row_factor[:, h * chunk_rows : (h + 1) * chunk_rows]
-        top = jnp.max(logits, axis=1)
-        total = jnp.sum(jnp.exp(logits - top[:, None]), axis=1)
-        mine = jnp.stack([top, total])
-        if h == 0:
-            mine = jnp.concatenate([mine, jnp.stack([target_top, target_total])], axis=1)
-        met = ring.meet(mine, merge_totals)
-        scale = jnp.exp(top - met[0, :chunk_rows]) / met[1, :chunk_rows]
-        if h == 0:
-            target_scale = jnp.exp(target_top - met[0, chunk_rows:]) / met[1, chunk_rows:]
-        draft_probs = jnp.exp(logits - top[:, None]) * scale[:, None]
+        own = chunk(logits, h)
+        draft_probs = jnp.exp(own - chunk(top, h)[:, None]) * chunk(draft_scale, h)[:, None]
         target_probs = (
             jnp.exp(chunk(targets, h) - chunk(target_top, h)[:, None])
             * chunk(target_scale, h)[:, None]
         )
         logit_grad = chunk(row_weight, h)[:, None] * (draft_probs - target_probs)
         logit_grad = lax.reduce_precision(logit_grad, 8, 7)
-        dot_part = jnp.sum(logit_grad * logits, axis=1)
+        dot_part = jnp.sum(logit_grad * own, axis=1)
         dot_high = lax.reduce_precision(dot_part, 8, 7)
         dot_low = dot_part - dot_high
         lanes = jnp.where(lane == own_lane, dot_high[:, None], 0.0) + jnp.where(

time: 222 us -> 202 us (0.910)
  starting transfers between devices: 82.6 us -> 66.1 us
  local copies, waits for them, and re-layouts: 12.4 us -> 6.41 us
  waiting for transfers between devices: 79 us -> 84.9 us
  Pallas kernels: 32.1 us -> 29.6 us
    ppermute x9 -> x8, starting transfers between devices: 29.6 us -> 12.5 us  [partner(): return lax.ppermute(x, 'vocab', [(v, v ^ bit) for v in range(self.size)])]
    ppermute x6 -> x5, waiting for transfers between devices: 16.2 us -> 27 us  [shift(): lax.ppermute(x, 'dp', [(i, (i + CORES * step) % size) for i in range(size)])]
    unnamed x24 -> x17, local copies, waits for them, and re-layouts: 6.82 us -> 0.04 us
    ppermute x9 -> x8, waiting for transfers between devices: 10.5 us -> 5.29 us  [partner(): return lax.ppermute(x, 'vocab', [(v, v ^ bit) for v in range(self.size)])]
    ppermute x6 -> x5, waiting for transfers between devices: 1.52 us -> 4.33 us  [swap(): return lax.ppermute(x, 'dp', [(i, i ^ 1) for i in range(self.size)])]
    ppermute x42 -> x35, waiting for transfers between devices: 50.9 us -> 48.3 us  [shift(): lax.ppermute(x, 'vocab', [(order[p], order[(p + step) % size]) for p in r...]
    ppermute x6 -> x5, starting transfers between devices: 7.59 us -> 8.68 us  [shift(): lax.ppermute(x, 'dp', [(i, (i + CORES * step) % size) for i in range(size)])]
    ppermute x42 -> x35, starting transfers between devices: 43.7 us -> 42.9 us  [shift(): lax.ppermute(x, 'vocab', [(order[p], order[(p + step) % size]) for p in r...]
  transfers between devices with their start and end apart: 65 -> 54, of which waited for: 38 -> 32; matrix products, arithmetic and copies ran while one was open for 7% -> 7% of each run, Pallas kernels for 4% -> 4%
where the time goes in v6:
time: 202 us
  waiting for transfers between devices  84.9 us (42%)
  starting transfers between devices  66.1 us (33%)
  Pallas kernels  29.6 us (15%)
  other arithmetic  13 us (6%)
  local copies, waits for them, and re-layouts  6.41 us (3%)
    ppermute x35, waiting for transfers between devices, shift(): lax.ppermute(x, 'vocab', [(order[p], order[(p + step) % size]) for p in r...  48.3 us
    ppermute x35, starting transfers between devices, shift(): lax.ppermute(x, 'vocab', [(order[p], order[(p + step) % size]) for p in r...  42.9 us
    ppermute x5, waiting for transfers between devices, shift(): lax.ppermute(x, 'dp', [(i, (i + CORES * step) % size) for i in range(size)])  27 us
    pallas_call x1, Pallas kernels, outer(): pl.pallas_call(functools.partial(outer_kernel, len(chunks[0]), tile), gri...  12.6 us
    ppermute x8, starting transfers between devices, partner(): return lax.ppermute(x, 'vocab', [(v, v ^ bit) for v in range(self.size)])  12.5 us
    pallas_call x1, Pallas kernels, project(): pl.pallas_call(functools.partial(project_kernel, len(blocks)), grid=(voca...  8.97 us
    ppermute x5, starting transfers between devices, shift(): lax.ppermute(x, 'dp', [(i, (i + CORES * step) % size) for i in range(size)])  8.68 us
    pallas_call x2, Pallas kernels, back(): pl.pallas_call(functools.partial(back_kernel, piece_rows), grid=(depth //...  8.03 us
  transfers between devices with their start and end apart: 54, of which 32 were waited for; matrix products, arithmetic and copies ran while one was open for 7% of the time, Pallas kernels for 4%

profile of v6, /device:TPU:0, one launch (start us, length us, event | category | flops | bytes accessed | tf_op | source)
XLA Modules:
  0.0 201.6 jit_solution(8499555977560528939)
XLA Ops:
  0.6 1.7 collective-permute-start.1
  3.5 3.0 %collective-permute-start = (f32[1,128]{1,0:T(1,128)S(1)}, f32[1,128]{1,0:T(1,128)S(1)}, u32[]{:S(2)}, u32[]{:S(2)}) collective-permute-start(f32[1,128]{1,0:T(1,128)S(1)} %bitcast.90), channel_id=1, source_target_pairs={{0,1},{1,0},{2,3},{3,2},{4,5},{5,4},{6,7},{7,6},{8,9},{9,8},{10,11... | collective-permute-start | bytes 1544 | tf_op jit(solution)/shard_map/ppermute | solution.py:47
  7.3 8.3 %collective-permute-start.2 = (bf16[128,1024]{1,0:T(8,128)(2,1)S(1)}, bf16[128,1024]{1,0:T(8,128)(2,1)S(1)}, u32[]{:S(2)}, u32[]{:S(2)}) collective-permute-start(bf16[128,1024]{1,0:T(8,128)(2,1)S(1)} %collective-permute-done.1.refs_4_), channel_id=1, source_target_pairs={{0,2},{2,4},{4,6},{6,7},{7,5},{5,3},{3,1},{1,0},{8,10},{10,12},{12... | collective-permute-start | bytes 786440 | tf_op jit(solution)/shard_map/ppermute | solution.py:42
  15.6 5.9 %collective-permute-done.3.refs_5_ = bf16[128,1024]{1,0:T(8,128)(2,1)S(1)} collective-permute-done((bf16[128,1024]{1,0:T(8,128)(2,1)S(1)}, bf16[128,1024]{1,0:T(8,128)(2,1)S(1)}, u32[]{:S(2)}, u32[]{:S(2)}) %collective-permute-start.3) | collective-permute-done | bytes 262176 | tf_op jit(solution)/shard_map/ppermute | solution.py:42
  21.5 1.8 collective-permute-done.2.refs_3_
  23.3 1.3 collective-permute-start.6
  25.4 2.3 %collective-permute-start.4 = (f32[1,128]{1,0:T(1,128)S(1)}, f32[1,128]{1,0:T(1,128)S(1)}, u32[]{:S(2)}, u32[]{:S(2)}) collective-permute-start(f32[1,128]{1,0:T(1,128)S(1)} %bitcast_add_fusion), channel_id=1, source_target_pairs={{0,2},{1,3},{2,0},{3,1},{4,6},{5,7},{6,4},{7,5},{8,10},{9,11},{10,... | collective-permute-start | bytes 1544 | tf_op jit(solution)/shard_map/ppermute | solution.py:47
  27.7 2.1 %collective-permute-start.8 = (bf16[128,1024]{1,0:T(8,128)(2,1)S(1)}, bf16[128,1024]{1,0:T(8,128)(2,1)S(1)}, u32[]{:S(2)}, u32[]{:S(2)}) collective-permute-start(bf16[128,1024]{1,0:T(8,128)(2,1)S(1)} %collective-permute-done.3.refs_5_), channel_id=1, source_target_pairs={{0,1},{2,0},{4,2},{6,4},{7,6},{5,7},{3,5},{1,3},{8,9},{10,8},{12,1... | collective-permute-start | bytes 786440 | tf_op jit(solution)/shard_map/ppermute | solution.py:42
  30.5 5.3 %collective-permute-done.8.refs_6_ = bf16[128,1024]{1,0:T(8,128)(2,1)S(1)} collective-permute-done((bf16[128,1024]{1,0:T(8,128)(2,1)S(1)}, bf16[128,1024]{1,0:T(8,128)(2,1)S(1)}, u32[]{:S(2)}, u32[]{:S(2)}) %collective-permute-start.8) | collective-permute-done | bytes 262176 | tf_op jit(solution)/shard_map/ppermute | solution.py:42
  36.5 1.7 collective-permute-start.10
  38.3 2.6 %collective-permute-start.9 = (f32[2,128]{1,0:T(2,128)S(1)}, f32[2,128]{1,0:T(2,128)S(1)}, u32[]{:S(2)}, u32[]{:S(2)}) collective-permute-start(f32[2,128]{1,0:T(2,128)S(1)} %get-tuple-element.73), channel_id=1, source_target_pairs={{0,16},{8,24},{16,0},{24,8},{1,17},{9,25},{17,1},{25,9},{2,18},{10... | collective-permute-start | bytes 3080 | tf_op jit(solution)/shard_map/ppermute | solution.py:110
  41.5 1.4 dynamic_slice.13
  43.1 1.7 collective-permute-start.13
  45.6 6.2 %collective-permute-done.13.refs_0_ = bf16[128,1024]{1,0:T(8,128)(2,1)S(1)} collective-permute-done((bf16[128,1024]{1,0:T(8,128)(2,1)S(1)}, bf16[128,1024]{1,0:T(8,128)(2,1)S(1)}, u32[]{:S(2)}, u32[]{:S(2)}) %collective-permute-start.13) | collective-permute-done | bytes 262176 | tf_op jit(solution)/shard_map/ppermute | solution.py:42
  51.8 9.0 %shard_map.95 = (f32[256,2048]{1,0:T(8,128)S(1)}, f32[256,2048]{1,0:T(8,128)}, bf16[32,2048]{1,0:T(8,128)(2,1)S(1)}, bf16[32,2048]{1,0:T(8,128)(2,1)S(1)}) custom-call(s32[18]{0:T(128)S(1)} %slice_bitcast_fusion.1.index_ref, f32[4,128,1]{2,1,0:T(8,128)S(1)} %copy.13.factor_ref, f32[1,2048]{1,0:T(1,128)S(1)} %bitcast.66, bf16[2048,2048]{1,0:T(8,128)(2,1)} %weight_ref.5, ...), custom_call_target="tpu_custom_call" | custom-call | flops 4294967296 | bytes 14680064 | tf_op jit(solution)/shard_map/pallas_call | solution.py:180
  60.9 4.3 %collective-permute-done.14 = f32[256,2048]{1,0:T(8,128)S(1)} collective-permute-done((f32[256,2048]{1,0:T(8,128)}, f32[256,2048]{1,0:T(8,128)S(1)}, u32[]{:S(2)}, u32[]{:S(2)}) %collective-permute-start.14) | collective-permute-done | bytes 2097184 | tf_op jit(solution)/shard_map/ppermute | solution.py:106
  66.5 2.5 %collective-permute-start.15 = (f32[128,2048]{1,0:T(8,128)}, f32[128,2048]{1,0:T(8,128)}, u32[]{:S(2)}, u32[]{:S(2)}) collective-permute-start(f32[128,2048]{1,0:T(8,128)} %slice.262), channel_id=1, source_target_pairs={{0,16},{8,24},{16,0},{24,8},{1,17},{9,25},{17,1},{25,9},{2,18},{10... | collective-permute-start | bytes 3145736 | tf_op jit(solution)/shard_map/ppermute | solution.py:110
  69.6 1.9 gather_fusion
  72.3 1.6 fusion.51
  74.7 18.1 %collective-permute-done.15 = f32[128,2048]{1,0:T(8,128)} collective-permute-done((f32[128,2048]{1,0:T(8,128)}, f32[128,2048]{1,0:T(8,128)}, u32[]{:S(2)}, u32[]{:S(2)}) %collective-permute-start.15) | collective-permute-done | bytes 1048608 | tf_op jit(solution)/shard_map/ppermute | solution.py:110
  92.7 1.4 fusion.48
  95.4 2.9 %collective-permute-done.16 = f32[2,256]{1,0:T(2,128)S(1)} collective-permute-done((f32[2,256]{1,0:T(2,128)S(1)}, f32[2,256]{1,0:T(2,128)S(1)}, u32[]{:S(2)}, u32[]{:S(2)}) %collective-permute-start.16) | collective-permute-done | bytes 2080 | tf_op jit(solution)/shard_map/ppermute | solution.py:47
  98.3 2.0 collective-permute-start.19
  106.4 1.8 collective-permute-start.20
  108.6 6.2 %collective-permute-done.20 = bf16[64,2176]{1,0:T(8,128)(2,1)S(1)} collective-permute-done((bf16[64,2176]{1,0:T(8,128)(2,1)S(1)}, bf16[64,2176]{1,0:T(8,128)(2,1)S(1)}, u32[]{:S(2)}, u32[]{:S(2)}) %collective-permute-start.20) | collective-permute-done | bytes 278560 | tf_op jit(solution)/shard_map/ppermute | solution.py:110
  115.0 2.8 %collective-permute-done.24 = bf16[64,2176]{1,0:T(8,128)(2,1)S(1)} collective-permute-done((bf16[64,2176]{1,0:T(8,128)(2,1)S(1)}, bf16[64,2176]{1,0:T(8,128)(2,1)S(1)}, u32[]{:S(2)}, u32[]{:S(2)}) %collective-permute-start.24) | collective-permute-done | bytes 278560 | tf_op jit(solution)/shard_map/ppermute | solution.py:110
  118.0 1.5 collective-permute-start.22
  119.5 4.0 %shard_map.97 = f32[256,2176]{1,0:T(8,128)S(1)} custom-call(s32[8]{0:T(128)S(1)} %slice_bitcast_fusion.index_ref, bf16[128,2176]{1,0:T(8,128)(2,1)S(1)} %bitcast.63, bf16[128,2176]{1,0:T(8,128)(2,1)S(1)} %bitcast.65, bf16[2048,2048]{1,0:T(8,128)(2,1)S(1)} %bitcast.60), custom_call_target="tpu_custom_call" | custom-call | flops 2147483648 | bytes 11534336 | tf_op jit(solution)/shard_map/pallas_call | solution.py:227
  125.7 4.0 %shard_map.96 = f32[256,2176]{1,0:T(8,128)S(1)} custom-call(s32[8]{0:T(128)S(1)} %slice_bitcast_fusion.index_ref, bf16[128,2176]{1,0:T(8,128)(2,1)S(1)} %bitcast.62, bf16[128,2176]{1,0:T(8,128)(2,1)S(1)} %bitcast.64, bf16[2048,2048]{1,0:T(8,128)(2,1)S(1)} %bitcast.60), custom_call_target="tpu_custom_call" | custom-call | flops 2147483648 | bytes 11534336 | tf_op jit(solution)/shard_map/pallas_call | solution.py:227
  133.3 3.3 %collective-permute-done.26 = bf16[32,2176]{1,0:T(8,128)(2,1)S(1)} collective-permute-done((bf16[32,2176]{1,0:T(8,128)(2,1)S(1)}, bf16[32,2176]{1,0:T(8,128)(2,1)S(1)}, u32[]{:S(2)}, u32[]{:S(2)}) %collective-permute-start.26) | collective-permute-done | bytes 139296 | tf_op jit(solution)/shard_map/ppermute | solution.py:42
  136.6 1.3 collective-permute-start.27
  137.9 1.7 collective-permute-done.41
  139.6 1.3 collective-permute-start.42
  142.8 1.3 collective-permute-start.28
  144.1 3.0 %collective-permute-done.44 = bf16[32,2176]{1,0:T(8,128)(2,1)S(1)} collective-permute-done((bf16[32,2176]{1,0:T(8,128)(2,1)S(1)}, bf16[32,2176]{1,0:T(8,128)(2,1)S(1)}, u32[]{:S(2)}, u32[]{:S(2)}) %collective-permute-start.44) | collective-permute-done | bytes 139296 | tf_op jit(solution)/shard_map/ppermute | solution.py:42
  148.1 1.3 collective-permute-start.29
  150.2 3.5 %collective-permute-done.45 = bf16[32,2176]{1,0:T(8,128)(2,1)S(1)} collective-permute-done((bf16[32,2176]{1,0:T(8,128)(2,1)S(1)}, bf16[32,2176]{1,0:T(8,128)(2,1)S(1)}, u32[]{:S(2)}, u32[]{:S(2)}) %collective-permute-start.45) | collective-permute-done | bytes 139296 | tf_op jit(solution)/shard_map/ppermute | solution.py:42
  154.6 1.6 collective-permute-done.31
  157.1 1.7 collective-permute-done.46
  158.9 2.4 %collective-permute-done.32 = bf16[32,2176]{1,0:T(8,128)(2,1)S(1)} collective-permute-done((bf16[32,2176]{1,0:T(8,128)(2,1)S(1)}, bf16[32,2176]{1,0:T(8,128)(2,1)S(1)}, u32[]{:S(2)}, u32[]{:S(2)}) %collective-permute-start.32) | collective-permute-done | bytes 139296 | tf_op jit(solution)/shard_map/ppermute | solution.py:42
  161.9 1.3 fusion.38
  163.2 1.3 fusion.39
  167.2 1.5 collective-permute-start.37
  168.7 2.2 %collective-permute-done.50.refs_12_ = bf16[32,2048]{1,0:T(8,128)(2,1)S(1)} collective-permute-done((bf16[32,2048]{1,0:T(8,128)(2,1)S(1)}, bf16[32,2048]{1,0:T(8,128)(2,1)S(1)}, u32[]{:S(2)}, u32[]{:S(2)}) %collective-permute-start.50) | collective-permute-done | bytes 131104 | tf_op jit(solution)/shard_map/ppermute | solution.py:42
  173.0 1.3 collective-permute-done.47.refs_10_
  179.0 1.7 collective-permute-done.48.refs_9_
  187.0 1.4 collective-permute-done.53.refs_15_
  189.1 12.6 %shard_map.98 = (f32[2048,3072]{1,0:T(8,128)}, bf16[64,2048]{1,0:T(8,128)(2,1)}) custom-call(s32[17]{0:T(128)S(1)} %slice_bitcast_fusion.2.index_ref, bf16[512,3072]{1,0:T(8,128)(2,1)S(1)} %bitcast.61, bf16[32,2048]{1,0:T(8,128)(2,1)S(1)} %collective-permute-done.36.refs_0_, bf16[32,2048]{1,0:T(8,128)(2,1)S(1)} %collective-permute-done.35.refs_1_, ...), custom_call_target="tpu_custom_call" | custom-call | flops 6442450944 | bytes 30408704 | tf_op jit(solution)/shard_map/pallas_call | solution.py:268
  (152 shorter events, 44.7 us)
Async XLA Ops:
  0.6 6.6 %collective-permute-start.1 = (bf16[128,1024]{1,0:T(8,128)(2,1)}, bf16[128,1024]{1,0:T(8,128)(2,1)S(1)}, u32[]{:S(2)}, u32[]{:S(2)}) collective-permute-start(bf16[128,1024]{1,0:T(8,128)(2,1)} %param.8), channel_id=1, source_target_pairs={{0,0},{1,1},{2,8},{3,9},{4,16},{5,17},{6,24},{7,25},{8,4},{9,5},{1... | collective-permute-start | bytes 786440 | tf_op jit(solution)/shard_map/ppermute | solution.py:367
  3.5 12.1 %collective-permute-start = (f32[1,128]{1,0:T(1,128)S(1)}, f32[1,128]{1,0:T(1,128)S(1)}, u32[]{:S(2)}, u32[]{:S(2)}) collective-permute-start(f32[1,128]{1,0:T(1,128)S(1)} %bitcast.90), channel_id=1, source_target_pairs={{0,1},{1,0},{2,3},{3,2},{4,5},{5,4},{6,7},{7,6},{8,9},{9,8},{10,11... | collective-permute-start | bytes 1544 | tf_op jit(solution)/shard_map/ppermute | solution.py:47
  7.3 14.2 %collective-permute-start.3 = (bf16[128,1024]{1,0:T(8,128)(2,1)S(1)}, bf16[128,1024]{1,0:T(8,128)(2,1)S(1)}, u32[]{:S(2)}, u32[]{:S(2)}) collective-permute-start(bf16[128,1024]{1,0:T(8,128)(2,1)S(1)} %collective-permute-done.1.refs_4_), channel_id=1, source_target_pairs={{0,1},{2,0},{4,2},{6,4},{7,6},{5,7},{3,5},{1,3},{8,9},{10,8},{12,1... | collective-permute-start | bytes 786440 | tf_op jit(solution)/shard_map/ppermute | solution.py:42
  7.3 16.1 %collective-permute-start.2 = (bf16[128,1024]{1,0:T(8,128)(2,1)S(1)}, bf16[128,1024]{1,0:T(8,128)(2,1)S(1)}, u32[]{:S(2)}, u32[]{:S(2)}) collective-permute-start(bf16[128,1024]{1,0:T(8,128)(2,1)S(1)} %collective-permute-done.1.refs_4_), channel_id=1, source_target_pairs={{0,2},{2,4},{4,6},{6,7},{7,5},{5,3},{3,1},{1,0},{8,10},{10,12},{12... | collective-permute-start | bytes 786440 | tf_op jit(solution)/shard_map/ppermute | solution.py:42
  23.3 7.1 %collective-permute-start.6 = (f32[1,128]{1,0:T(1,128)S(1)}, f32[1,128]{1,0:T(1,128)S(1)}, u32[]{:S(2)}, u32[]{:S(2)}) collective-permute-start(f32[1,128]{1,0:T(1,128)S(1)} %bitcast_add_fusion), channel_id=1, source_target_pairs={{0,6},{1,7},{2,4},{3,5},{4,2},{5,3},{6,0},{7,1},{8,14},{9,15},{10,... | collective-permute-start | bytes 1544 | tf_op jit(solution)/shard_map/ppermute | solution.py:47
  24.7 5.8 %collective-permute-start.5 = (f32[1,128]{1,0:T(1,128)S(1)}, f32[1,128]{1,0:T(1,128)S(1)}, u32[]{:S(2)}, u32[]{:S(2)}) collective-permute-start(f32[1,128]{1,0:T(1,128)S(1)} %bitcast_add_fusion), channel_id=1, source_target_pairs={{0,4},{1,5},{2,6},{3,7},{4,0},{5,1},{6,2},{7,3},{8,12},{9,13},{10,... | collective-permute-start | bytes 1544 | tf_op jit(solution)/shard_map/ppermute | solution.py:47
  25.4 5.1 %collective-permute-start.4 = (f32[1,128]{1,0:T(1,128)S(1)}, f32[1,128]{1,0:T(1,128)S(1)}, u32[]{:S(2)}, u32[]{:S(2)}) collective-permute-start(f32[1,128]{1,0:T(1,128)S(1)} %bitcast_add_fusion), channel_id=1, source_target_pairs={{0,2},{1,3},{2,0},{3,1},{4,6},{5,7},{6,4},{7,5},{8,10},{9,11},{10,... | collective-permute-start | bytes 1544 | tf_op jit(solution)/shard_map/ppermute | solution.py:47
  27.7 8.1 %collective-permute-start.8 = (bf16[128,1024]{1,0:T(8,128)(2,1)S(1)}, bf16[128,1024]{1,0:T(8,128)(2,1)S(1)}, u32[]{:S(2)}, u32[]{:S(2)}) collective-permute-start(bf16[128,1024]{1,0:T(8,128)(2,1)S(1)} %collective-permute-done.3.refs_5_), channel_id=1, source_target_pairs={{0,1},{2,0},{4,2},{6,4},{7,6},{5,7},{3,5},{1,3},{8,9},{10,8},{12,1... | collective-permute-start | bytes 786440 | tf_op jit(solution)/shard_map/ppermute | solution.py:42
  29.8 6.4 %collective-permute-start.7 = (bf16[128,1024]{1,0:T(8,128)(2,1)S(1)}, bf16[128,1024]{1,0:T(8,128)(2,1)S(1)}, u32[]{:S(2)}, u32[]{:S(2)}) collective-permute-start(bf16[128,1024]{1,0:T(8,128)(2,1)S(1)} %collective-permute-done.2.refs_3_), channel_id=1, source_target_pairs={{0,2},{2,4},{4,6},{6,7},{7,5},{5,3},{3,1},{1,0},{8,10},{10,12},{12... | collective-permute-start | bytes 786440 | tf_op jit(solution)/shard_map/ppermute | solution.py:42
  36.2 6.8 %collective-permute-start.11 = (bf16[128,1024]{1,0:T(8,128)(2,1)S(1)}, bf16[128,1024]{1,0:T(8,128)(2,1)S(1)}, u32[]{:S(2)}, u32[]{:S(2)}) collective-permute-start(bf16[128,1024]{1,0:T(8,128)(2,1)S(1)} %collective-permute-done.8.refs_6_), channel_id=1, source_target_pairs={{0,1},{2,0},{4,2},{6,4},{7,6},{5,7},{3,5},{1,3},{8,9},{10,8},{12,1... | collective-permute-start | bytes 786440 | tf_op jit(solution)/shard_map/ppermute | solution.py:42
  36.5 6.5 %collective-permute-start.10 = (bf16[128,1024]{1,0:T(8,128)(2,1)S(1)}, bf16[128,1024]{1,0:T(8,128)(2,1)S(1)}, u32[]{:S(2)}, u32[]{:S(2)}) collective-permute-start(bf16[128,1024]{1,0:T(8,128)(2,1)S(1)} %collective-permute-done.7.refs_2_), channel_id=1, source_target_pairs={{0,2},{2,4},{4,6},{6,7},{7,5},{5,3},{3,1},{1,0},{8,10},{10,12},{12... | collective-permute-start | bytes 786440 | tf_op jit(solution)/shard_map/ppermute | solution.py:42
  38.3 4.6 %collective-permute-start.9 = (f32[2,128]{1,0:T(2,128)S(1)}, f32[2,128]{1,0:T(2,128)S(1)}, u32[]{:S(2)}, u32[]{:S(2)}) collective-permute-start(f32[2,128]{1,0:T(2,128)S(1)} %get-tuple-element.73), channel_id=1, source_target_pairs={{0,16},{8,24},{16,0},{24,8},{1,17},{9,25},{17,1},{25,9},{2,18},{10... | collective-permute-start | bytes 3080 | tf_op jit(solution)/shard_map/ppermute | solution.py:110
  43.1 8.7 %collective-permute-start.13 = (bf16[128,1024]{1,0:T(8,128)(2,1)S(1)}, bf16[128,1024]{1,0:T(8,128)(2,1)S(1)}, u32[]{:S(2)}, u32[]{:S(2)}) collective-permute-start(bf16[128,1024]{1,0:T(8,128)(2,1)S(1)} %collective-permute-done.10.refs_1_), channel_id=1, source_target_pairs={{0,2},{2,4},{4,6},{6,7},{7,5},{5,3},{3,1},{1,0},{8,10},{10,12},{12... | collective-permute-start | bytes 786440 | tf_op jit(solution)/shard_map/ppermute | solution.py:42
  66.5 26.2 %collective-permute-start.15 = (f32[128,2048]{1,0:T(8,128)}, f32[128,2048]{1,0:T(8,128)}, u32[]{:S(2)}, u32[]{:S(2)}) collective-permute-start(f32[128,2048]{1,0:T(8,128)} %slice.262), channel_id=1, source_target_pairs={{0,16},{8,24},{16,0},{24,8},{1,17},{9,25},{17,1},{25,9},{2,18},{10... | collective-permute-start | bytes 3145736 | tf_op jit(solution)/shard_map/ppermute | solution.py:110
  98.3 5.4 %collective-permute-start.19 = (f32[2,256]{1,0:T(2,128)S(1)}, f32[2,256]{1,0:T(2,128)S(1)}, u32[]{:S(2)}, u32[]{:S(2)}) collective-permute-start(f32[2,256]{1,0:T(2,128)S(1)} %pad_maximum_fusion.8), channel_id=1, source_target_pairs={{0,6},{1,7},{2,4},{3,5},{4,2},{5,3},{6,0},{7,1},{8,14},{9,15},{10,... | collective-permute-start | bytes 6152 | tf_op jit(solution)/shard_map/ppermute | solution.py:47
  106.4 8.4 %collective-permute-start.20 = (bf16[64,2176]{1,0:T(8,128)(2,1)S(1)}, bf16[64,2176]{1,0:T(8,128)(2,1)S(1)}, u32[]{:S(2)}, u32[]{:S(2)}) collective-permute-start(bf16[64,2176]{1,0:T(8,128)(2,1)S(1)} %get-tuple-element.49), channel_id=1, source_target_pairs={{0,16},{8,24},{16,0},{24,8},{1,17},{9,25},{17,1},{25,9},{2,18},{10... | collective-permute-start | bytes 835592 | tf_op jit(solution)/shard_map/ppermute | solution.py:110
  108.3 9.5 %collective-permute-start.24 = (bf16[64,2176]{1,0:T(8,128)(2,1)S(1)}, bf16[64,2176]{1,0:T(8,128)(2,1)S(1)}, u32[]{:S(2)}, u32[]{:S(2)}) collective-permute-start(bf16[64,2176]{1,0:T(8,128)(2,1)S(1)} %get-tuple-element.47), channel_id=1, source_target_pairs={{0,16},{8,24},{16,0},{24,8},{1,17},{9,25},{17,1},{25,9},{2,18},{10... | collective-permute-start | bytes 835592 | tf_op jit(solution)/shard_map/ppermute | solution.py:110
  117.9 7.9 %collective-permute-start.25 = (bf16[2,64,2176]{2,1,0:T(8,128)(2,1)S(1)}, bf16[2,64,2176]{2,1,0:T(8,128)(2,1)S(1)}, u32[]{:S(2)}, u32[]{:S(2)}) collective-permute-start(bf16[2,64,2176]{2,1,0:T(8,128)(2,1)S(1)} %pad_maximum_fusion.3), channel_id=1, source_target_pairs={{0,8},{8,0},{16,24},{24,16},{1,9},{9,1},{17,25},{25,17},{2,10},{10... | collective-permute-start | bytes 1671176 | tf_op jit(solution)/shard_map/ppermute | solution.py:106
  118.0 43.4 %collective-permute-start.22 = (bf16[2,64,3072]{2,1,0:T(8,128)(2,1)S(1)}, bf16[2,64,3072]{2,1,0:T(8,128)(2,1)S(1)}, u32[]{:S(2)}, u32[]{:S(2)}) collective-permute-start(bf16[2,64,3072]{2,1,0:T(8,128)(2,1)S(1)} %bitcast.67), channel_id=1, source_target_pairs={{0,16},{8,24},{16,0},{24,8},{1,17},{9,25},{17,1},{25,9},{2,18},{10... | collective-permute-start | bytes 2359304 | tf_op jit(solution)/shard_map/ppermute | solution.py:110
  123.6 8.3 %collective-permute-start.40 = (bf16[32,2176]{1,0:T(8,128)(2,1)S(1)}, bf16[32,2176]{1,0:T(8,128)(2,1)S(1)}, u32[]{:S(2)}, u32[]{:S(2)}) collective-permute-start(bf16[32,2176]{1,0:T(8,128)(2,1)S(1)} %get-tuple-element.40), channel_id=1, source_target_pairs={{0,2},{2,4},{4,6},{6,7},{7,5},{5,3},{3,1},{1,0},{8,10},{10,12},{12... | collective-permute-start | bytes 417800 | tf_op jit(solution)/shard_map/ppermute | solution.py:42
  124.9 12.9 %collective-permute-start.43 = (bf16[32,2176]{1,0:T(8,128)(2,1)S(1)}, bf16[32,2176]{1,0:T(8,128)(2,1)S(1)}, u32[]{:S(2)}, u32[]{:S(2)}) collective-permute-start(bf16[32,2176]{1,0:T(8,128)(2,1)S(1)} %get-tuple-element.41), channel_id=1, source_target_pairs={{0,1},{2,0},{4,2},{6,4},{7,6},{5,7},{3,5},{1,3},{8,9},{10,8},{12,1... | collective-permute-start | bytes 417800 | tf_op jit(solution)/shard_map/ppermute | solution.py:42
  129.9 6.6 %collective-permute-start.26 = (bf16[32,2176]{1,0:T(8,128)(2,1)S(1)}, bf16[32,2176]{1,0:T(8,128)(2,1)S(1)}, u32[]{:S(2)}, u32[]{:S(2)}) collective-permute-start(bf16[32,2176]{1,0:T(8,128)(2,1)S(1)} %get-tuple-element.42), channel_id=1, source_target_pairs={{0,2},{2,4},{4,6},{6,7},{7,5},{5,3},{3,1},{1,0},{8,10},{10,12},{12... | collective-permute-start | bytes 417800 | tf_op jit(solution)/shard_map/ppermute | solution.py:42
  131.2 16.8 %collective-permute-start.30 = (bf16[32,2176]{1,0:T(8,128)(2,1)S(1)}, bf16[32,2176]{1,0:T(8,128)(2,1)S(1)}, u32[]{:S(2)}, u32[]{:S(2)}) collective-permute-start(bf16[32,2176]{1,0:T(8,128)(2,1)S(1)} %get-tuple-element.43), channel_id=1, source_target_pairs={{0,1},{2,0},{4,2},{6,4},{7,6},{5,7},{3,5},{1,3},{8,9},{10,8},{12,1... | collective-permute-start | bytes 417800 | tf_op jit(solution)/shard_map/ppermute | solution.py:42
  132.0 7.5 %collective-permute-start.41 = (bf16[32,2176]{1,0:T(8,128)(2,1)S(1)}, bf16[32,2176]{1,0:T(8,128)(2,1)S(1)}, u32[]{:S(2)}, u32[]{:S(2)}) collective-permute-start(bf16[32,2176]{1,0:T(8,128)(2,1)S(1)} %fusion.13), channel_id=1, source_target_pairs={{0,2},{2,4},{4,6},{6,7},{7,5},{5,3},{3,1},{1,0},{8,10},{10,12},{12... | collective-permute-start | bytes 417800 | tf_op jit(solution)/shard_map/ppermute | solution.py:42
  136.6 6.2 %collective-permute-start.27 = (bf16[32,2176]{1,0:T(8,128)(2,1)S(1)}, bf16[32,2176]{1,0:T(8,128)(2,1)S(1)}, u32[]{:S(2)}, u32[]{:S(2)}) collective-permute-start(bf16[32,2176]{1,0:T(8,128)(2,1)S(1)} %fusion.18), channel_id=1, source_target_pairs={{0,2},{2,4},{4,6},{6,7},{7,5},{5,3},{3,1},{1,0},{8,10},{10,12},{12... | collective-permute-start | bytes 417800 | tf_op jit(solution)/shard_map/ppermute | solution.py:42
  139.6 17.5 %collective-permute-start.42 = (bf16[32,2176]{1,0:T(8,128)(2,1)S(1)}, bf16[32,2176]{1,0:T(8,128)(2,1)S(1)}, u32[]{:S(2)}, u32[]{:S(2)}) collective-permute-start(bf16[32,2176]{1,0:T(8,128)(2,1)S(1)} %get-tuple-element.34), channel_id=1, source_target_pairs={{0,2},{2,4},{4,6},{6,7},{7,5},{5,3},{3,1},{1,0},{8,10},{10,12},{12... | collective-permute-start | bytes 417800 | tf_op jit(solution)/shard_map/ppermute | solution.py:42
  140.9 6.2 %collective-permute-start.44 = (bf16[32,2176]{1,0:T(8,128)(2,1)S(1)}, bf16[32,2176]{1,0:T(8,128)(2,1)S(1)}, u32[]{:S(2)}, u32[]{:S(2)}) collective-permute-start(bf16[32,2176]{1,0:T(8,128)(2,1)S(1)} %get-tuple-element.35), channel_id=1, source_target_pairs={{0,1},{2,0},{4,2},{6,4},{7,6},{5,7},{3,5},{1,3},{8,9},{10,8},{12,1... | collective-permute-start | bytes 417800 | tf_op jit(solution)/shard_map/ppermute | solution.py:42
  142.8 5.2 %collective-permute-start.28 = (bf16[32,2176]{1,0:T(8,128)(2,1)S(1)}, bf16[32,2176]{1,0:T(8,128)(2,1)S(1)}, u32[]{:S(2)}, u32[]{:S(2)}) collective-permute-start(bf16[32,2176]{1,0:T(8,128)(2,1)S(1)} %fusion.19), channel_id=1, source_target_pairs={{0,2},{2,4},{4,6},{6,7},{7,5},{5,3},{3,1},{1,0},{8,10},{10,12},{12... | collective-permute-start | bytes 417800 | tf_op jit(solution)/shard_map/ppermute | solution.py:42
  147.2 6.5 %collective-permute-start.45 = (bf16[32,2176]{1,0:T(8,128)(2,1)S(1)}, bf16[32,2176]{1,0:T(8,128)(2,1)S(1)}, u32[]{:S(2)}, u32[]{:S(2)}) collective-permute-start(bf16[32,2176]{1,0:T(8,128)(2,1)S(1)} %fusion.11), channel_id=1, source_target_pairs={{0,1},{2,0},{4,2},{6,4},{7,6},{5,7},{3,5},{1,3},{8,9},{10,8},{12,1... | collective-permute-start | bytes 417800 | tf_op jit(solution)/shard_map/ppermute | solution.py:42
  148.1 10.8 %collective-permute-start.29 = (bf16[32,2176]{1,0:T(8,128)(2,1)S(1)}, bf16[32,2176]{1,0:T(8,128)(2,1)S(1)}, u32[]{:S(2)}, u32[]{:S(2)}) collective-permute-start(bf16[32,2176]{1,0:T(8,128)(2,1)S(1)} %get-tuple-element.36), channel_id=1, source_target_pairs={{0,2},{2,4},{4,6},{6,7},{7,5},{5,3},{3,1},{1,0},{8,10},{10,12},{12... | collective-permute-start | bytes 417800 | tf_op jit(solution)/shard_map/ppermute | solution.py:42
  149.4 6.8 %collective-permute-start.31 = (bf16[32,2176]{1,0:T(8,128)(2,1)S(1)}, bf16[32,2176]{1,0:T(8,128)(2,1)S(1)}, u32[]{:S(2)}, u32[]{:S(2)}) collective-permute-start(bf16[32,2176]{1,0:T(8,128)(2,1)S(1)} %get-tuple-element.37), channel_id=1, source_target_pairs={{0,1},{2,0},{4,2},{6,4},{7,6},{5,7},{3,5},{1,3},{8,9},{10,8},{12,1... | collective-permute-start | bytes 417800 | tf_op jit(solution)/shard_map/ppermute | solution.py:42
  153.7 5.1 %collective-permute-start.46 = (bf16[32,2176]{1,0:T(8,128)(2,1)S(1)}, bf16[32,2176]{1,0:T(8,128)(2,1)S(1)}, u32[]{:S(2)}, u32[]{:S(2)}) collective-permute-start(bf16[32,2176]{1,0:T(8,128)(2,1)S(1)} %fusion.12), channel_id=1, source_target_pairs={{0,1},{2,0},{4,2},{6,4},{7,6},{5,7},{3,5},{1,3},{8,9},{10,8},{12,1... | collective-permute-start | bytes 417800 | tf_op jit(solution)/shard_map/ppermute | solution.py:42
  156.3 5.1 %collective-permute-start.32 = (bf16[32,2176]{1,0:T(8,128)(2,1)S(1)}, bf16[32,2176]{1,0:T(8,128)(2,1)S(1)}, u32[]{:S(2)}, u32[]{:S(2)}) collective-permute-start(bf16[32,2176]{1,0:T(8,128)(2,1)S(1)} %fusion.17), channel_id=1, source_target_pairs={{0,1},{2,0},{4,2},{6,4},{7,6},{5,7},{3,5},{1,3},{8,9},{10,8},{12,1... | collective-permute-start | bytes 417800 | tf_op jit(solution)/shard_map/ppermute | solution.py:42
  161.6 23.7 %collective-permute-start.23 = (bf16[2,2,64,3072]{3,2,0,1:T(8,128)(2,1)S(1)}, bf16[2,2,64,3072]{3,2,0,1:T(8,128)(2,1)S(1)}, u32[]{:S(2)}, u32[]{:S(2)}) collective-permute-start(bf16[2,2,64,3072]{3,2,0,1:T(8,128)(2,1)S(1)} %pad_maximum_fusion.1), channel_id=1, source_target_pairs={{0,8},{8,0},{16,24},{24,16},{1,9},{9,1},{17,25},{25,17},{2,10},{10... | collective-permute-start | bytes 4718600 | tf_op jit(solution)/shard_map/ppermute | solution.py:106
  164.6 6.3 %collective-permute-start.50 = (bf16[32,2048]{1,0:T(8,128)(2,1)S(1)}, bf16[32,2048]{1,0:T(8,128)(2,1)S(1)}, u32[]{:S(2)}, u32[]{:S(2)}) collective-permute-start(bf16[32,2048]{1,0:T(8,128)(2,1)S(1)} %get-tuple-element.50.refs_11_), channel_id=1, source_target_pairs={{0,1},{2,0},{4,2},{6,4},{7,6},{5,7},{3,5},{1,3},{8,9},{10,8},{12,1... | collective-permute-start | bytes 393224 | tf_op jit(solution)/shard_map/ppermute | solution.py:42
  165.5 6.3 %collective-permute-start.33 = (bf16[32,2048]{1,0:T(8,128)(2,1)S(1)}, bf16[32,2048]{1,0:T(8,128)(2,1)S(1)}, u32[]{:S(2)}, u32[]{:S(2)}) collective-permute-start(bf16[32,2048]{1,0:T(8,128)(2,1)S(1)} %get-tuple-element.51.refs_4_), channel_id=1, source_target_pairs={{0,2},{2,4},{4,6},{6,7},{7,5},{5,3},{3,1},{1,0},{8,10},{10,12},{12... | collective-permute-start | bytes 393224 | tf_op jit(solution)/shard_map/ppermute | solution.py:42
  166.7 7.6 %collective-permute-start.47 = (bf16[32,2048]{1,0:T(8,128)(2,1)S(1)}, bf16[32,2048]{1,0:T(8,128)(2,1)S(1)}, u32[]{:S(2)}, u32[]{:S(2)}) collective-permute-start(bf16[32,2048]{1,0:T(8,128)(2,1)S(1)} %get-tuple-element.50.refs_11_), channel_id=1, source_target_pairs={{0,2},{2,4},{4,6},{6,7},{7,5},{5,3},{3,1},{1,0},{8,10},{10,12},{12... | collective-permute-start | bytes 393224 | tf_op jit(solution)/shard_map/ppermute | solution.py:42
  167.2 8.3 %collective-permute-start.37 = (bf16[32,2048]{1,0:T(8,128)(2,1)S(1)}, bf16[32,2048]{1,0:T(8,128)(2,1)S(1)}, u32[]{:S(2)}, u32[]{:S(2)}) collective-permute-start(bf16[32,2048]{1,0:T(8,128)(2,1)S(1)} %get-tuple-element.51.refs_4_), channel_id=1, source_target_pairs={{0,1},{2,0},{4,2},{6,4},{7,6},{5,7},{3,5},{1,3},{8,9},{10,8},{12,1... | collective-permute-start | bytes 393224 | tf_op jit(solution)/shard_map/ppermute | solution.py:42
  171.0 5.4 %collective-permute-start.51 = (bf16[32,2048]{1,0:T(8,128)(2,1)S(1)}, bf16[32,2048]{1,0:T(8,128)(2,1)S(1)}, u32[]{:S(2)}, u32[]{:S(2)}) collective-permute-start(bf16[32,2048]{1,0:T(8,128)(2,1)S(1)} %collective-permute-done.50.refs_12_), channel_id=1, source_target_pairs={{0,1},{2,0},{4,2},{6,4},{7,6},{5,7},{3,5},{1,3},{8,9},{10,8},{12,1... | collective-permute-start | bytes 393224 | tf_op jit(solution)/shard_map/ppermute | solution.py:42
  171.8 5.9 %collective-permute-start.34 = (bf16[32,2048]{1,0:T(8,128)(2,1)S(1)}, bf16[32,2048]{1,0:T(8,128)(2,1)S(1)}, u32[]{:S(2)}, u32[]{:S(2)}) collective-permute-start(bf16[32,2048]{1,0:T(8,128)(2,1)S(1)} %collective-permute-done.33.refs_3_), channel_id=1, source_target_pairs={{0,2},{2,4},{4,6},{6,7},{7,5},{5,3},{3,1},{1,0},{8,10},{10,12},{12... | collective-permute-start | bytes 393224 | tf_op jit(solution)/shard_map/ppermute | solution.py:42
  174.3 6.4 %collective-permute-start.48 = (bf16[32,2048]{1,0:T(8,128)(2,1)S(1)}, bf16[32,2048]{1,0:T(8,128)(2,1)S(1)}, u32[]{:S(2)}, u32[]{:S(2)}) collective-permute-start(bf16[32,2048]{1,0:T(8,128)(2,1)S(1)} %collective-permute-done.47.refs_10_), channel_id=1, source_target_pairs={{0,2},{2,4},{4,6},{6,7},{7,5},{5,3},{3,1},{1,0},{8,10},{10,12},{12... | collective-permute-start | bytes 393224 | tf_op jit(solution)/shard_map/ppermute | solution.py:42
  175.6 6.4 %collective-permute-start.38 = (bf16[32,2048]{1,0:T(8,128)(2,1)S(1)}, bf16[32,2048]{1,0:T(8,128)(2,1)S(1)}, u32[]{:S(2)}, u32[]{:S(2)}) collective-permute-start(bf16[32,2048]{1,0:T(8,128)(2,1)S(1)} %collective-permute-done.37.refs_5_), channel_id=1, source_target_pairs={{0,1},{2,0},{4,2},{6,4},{7,6},{5,7},{3,5},{1,3},{8,9},{10,8},{12,1... | collective-permute-start | bytes 393224 | tf_op jit(solution)/shard_map/ppermute | solution.py:42
  176.4 6.4 %collective-permute-start.52 = (bf16[32,2048]{1,0:T(8,128)(2,1)S(1)}, bf16[32,2048]{1,0:T(8,128)(2,1)S(1)}, u32[]{:S(2)}, u32[]{:S(2)}) collective-permute-start(bf16[32,2048]{1,0:T(8,128)(2,1)S(1)} %collective-permute-done.51.refs_13_), channel_id=1, source_target_pairs={{0,1},{2,0},{4,2},{6,4},{7,6},{5,7},{3,5},{1,3},{8,9},{10,8},{12,1... | collective-permute-start | bytes 393224 | tf_op jit(solution)/shard_map/ppermute | solution.py:42
  177.7 6.4 %collective-permute-start.35 = (bf16[32,2048]{1,0:T(8,128)(2,1)S(1)}, bf16[32,2048]{1,0:T(8,128)(2,1)S(1)}, u32[]{:S(2)}, u32[]{:S(2)}) collective-permute-start(bf16[32,2048]{1,0:T(8,128)(2,1)S(1)} %collective-permute-done.34.refs_2_), channel_id=1, source_target_pairs={{0,2},{2,4},{4,6},{6,7},{7,5},{5,3},{3,1},{1,0},{8,10},{10,12},{12... | collective-permute-start | bytes 393224 | tf_op jit(solution)/shard_map/ppermute | solution.py:42
  180.8 6.0 %collective-permute-start.49 = (bf16[32,2048]{1,0:T(8,128)(2,1)S(1)}, bf16[32,2048]{1,0:T(8,128)(2,1)S(1)}, u32[]{:S(2)}, u32[]{:S(2)}) collective-permute-start(bf16[32,2048]{1,0:T(8,128)(2,1)S(1)} %collective-permute-done.48.refs_9_), channel_id=1, source_target_pairs={{0,2},{2,4},{4,6},{6,7},{7,5},{5,3},{3,1},{1,0},{8,10},{10,12},{12... | collective-permute-start | bytes 393224 | tf_op jit(solution)/shard_map/ppermute | solution.py:42
  182.0 5.0 %collective-permute-start.39 = (bf16[32,2048]{1,0:T(8,128)(2,1)S(1)}, bf16[32,2048]{1,0:T(8,128)(2,1)S(1)}, u32[]{:S(2)}, u32[]{:S(2)}) collective-permute-start(bf16[32,2048]{1,0:T(8,128)(2,1)S(1)} %collective-permute-done.38.refs_6_), channel_id=1, source_target_pairs={{0,1},{2,0},{4,2},{6,4},{7,6},{5,7},{3,5},{1,3},{8,9},{10,8},{12,1... | collective-permute-start | bytes 393224 | tf_op jit(solution)/shard_map/ppermute | solution.py:42
  182.8 5.6 %collective-permute-start.53 = (bf16[32,2048]{1,0:T(8,128)(2,1)S(1)}, bf16[32,2048]{1,0:T(8,128)(2,1)S(1)}, u32[]{:S(2)}, u32[]{:S(2)}) collective-permute-start(bf16[32,2048]{1,0:T(8,128)(2,1)S(1)} %collective-permute-done.52.refs_14_), channel_id=1, source_target_pairs={{0,1},{2,0},{4,2},{6,4},{7,6},{5,7},{3,5},{1,3},{8,9},{10,8},{12,1... | collective-permute-start | bytes 393224 | tf_op jit(solution)/shard_map/ppermute | solution.py:42
  184.1 5.0 %collective-permute-start.36 = (bf16[32,2048]{1,0:T(8,128)(2,1)S(1)}, bf16[32,2048]{1,0:T(8,128)(2,1)S(1)}, u32[]{:S(2)}, u32[]{:S(2)}) collective-permute-start(bf16[32,2048]{1,0:T(8,128)(2,1)S(1)} %collective-permute-done.35.refs_1_), channel_id=1, source_target_pairs={{0,2},{2,4},{4,6},{6,7},{7,5},{5,3},{3,1},{1,0},{8,10},{10,12},{12... | collective-permute-start | bytes 393224 | tf_op jit(solution)/shard_map/ppermute | solution.py:42
  (14 other events, 210.8 us)

commit v7 on v6

--- a/solution.py
+++ b/solution.py
@@ -131,74 +131,105 @@
         out_ref[pl.ds(start, tile), :] = block.T.astype(BF16)
 
 
+def fetch_tiles(weight_ref, first, held_ref, sems):
+    tile = held_ref.shape[1]
+    return lambda n: pltpu.make_async_copy(
+        weight_ref.at[pl.ds(first + n * tile, tile), :], held_ref.at[n], sems.at[n]
+    )
+
+
+def tile_logits(fetch, held_ref, turned_ref, keep_ref, send_ref):
+    step = pl.program_id(0)
+    half = keep_ref.shape[0]
+    fetch(step).wait()
+    logits = jnp.dot(held_ref[step], turned_ref[...], preferred_element_type=F32).T
+    keep_ref[...] = logits[:half]
+    send_ref[...] = logits[half:]
+
+
 def project_kernel(count, index_ref, factor_ref, gain_ref, weight_ref, *refs):
-    blocks, refs = refs[:count], refs[count:]
-    logits_refs, piece_refs = refs[:CORES], refs[CORES:-5]
-    raw_ref, normed_ref, turned_ref, held_ref, sems = refs[-5:]
+    blocks, refs = refs[: CHUNKS * count], refs[CHUNKS * count :]
+    keep_ref, send_ref, turned_ref = refs[:3]
+    piece_refs = refs[3 : 3 + CHUNKS]
+    raw_ref, normed_ref, held_ref, sems = refs[3 + CHUNKS :]
     rows, width = blocks[0].shape
-    step = pl.program_id(0)
-    tiles, tile = held_ref.shape[:2]
+    group_rows = CHUNKS * rows
     piece = piece_refs[0].shape[0]
-    half = logits_refs[0].shape[0]
-
-    def fetch(n):
-        return pltpu.make_async_copy(
-            weight_ref.at[pl.ds(n * tile, tile), :], held_ref.at[n], sems.at[n]
-        )
-
-    @pl.when(step == 0)
+    fetch = fetch_tiles(weight_ref, 0, held_ref, sems)
+
+    @pl.when(pl.program_id(0) == 0)
     def _():
-        for n in range(tiles):
+        for n in range(held_ref.shape[0]):
             fetch(n).start()
         for k, ref in enumerate(blocks):
-            start = pl.multiple_of(index_ref[k] * rows, rows)
-            column = pl.multiple_of(index_ref[count + k] * width, width)
+            h, at = k // count, k + k // count * count
+            start = pl.multiple_of(index_ref[at] * group_rows + h * rows, rows)
+            column = pl.multiple_of(index_ref[at + count] * width, width)
             raw_ref[pl.ds(start, rows), pl.ds(column, width)] = ref[...]
         for g in range(factor_ref.shape[0]):
-            group = pl.ds(g * rows, rows)
+            group = pl.ds(g * group_rows, group_rows)
             normed_ref[group, :] = (
                 raw_ref[group, :].astype(F32) * factor_ref[g] * gain_ref[...]
             ).astype(BF16)
+        transpose_into(turned_ref, normed_ref)
         for h, ref in enumerate(piece_refs):
-            start = pl.multiple_of(index_ref[2 * count + h] * piece, piece)
+            start = pl.multiple_of(index_ref[2 * CHUNKS * count + h] * piece, piece)
             ref[...] = raw_ref[pl.ds(start, piece), :]
-        transpose_into(turned_ref, normed_ref)
-
-    fetch(step).wait()
-    logits = jnp.dot(held_ref[step], turned_ref[...], preferred_element_type=F32).T
-    for k, ref in enumerate(logits_refs):
-        ref[...] = logits[k * half : (k + 1) * half]
+
+    tile_logits(fetch, held_ref, turned_ref, keep_ref, send_ref)
+
+
+def project_rest_kernel(weight_ref, turned_ref, keep_ref, send_ref, held_ref, sems):
+    fetch = fetch_tiles(weight_ref, weight_ref.shape[0] // 2, held_ref, sems)
+
+    @pl.when(pl.program_id(0) == 0)
+    def _():
+        for n in range(held_ref.shape[0]):
+            fetch(n).start()
+
+    tile_logits(fetch, held_ref, turned_ref, keep_ref, send_ref)
 
 
 def project(index, blocks, factor, gain, weight, piece_rows):
     vocab, depth = weight.shape
-    all_rows = factor.shape[0] * blocks[0].shape[0]
+    all_rows = factor.shape[0] * factor.shape[1]
     half = all_rows // CORES
-    tile = min(vocab, 512)
-    out = jax.ShapeDtypeStruct((half, vocab), F32)
-    piece = jax.ShapeDtypeStruct((piece_rows, depth), BF16)
-    return pl.pallas_call(
-        functools.partial(project_kernel, len(blocks)),
-        grid=(vocab // tile,),
-        in_specs=[SMEM, VMEM, VMEM, pl.BlockSpec(memory_space=pltpu.HBM)]
-        + [VMEM] * len(blocks),
-        out_specs=[pl.BlockSpec((half, tile), lambda n: (0, n))] * CORES
-        + [pl.BlockSpec((piece_rows, depth), lambda n: (0, 0))] * CHUNKS,
-        out_shape=[out] * CORES + [piece] * CHUNKS,
-        scratch_shapes=[
-            pltpu.VMEM((all_rows, depth), BF16),
-            pltpu.VMEM((all_rows, depth), BF16),
-            pltpu.VMEM((depth, all_rows), BF16),
-            pltpu.VMEM((vocab // tile, tile, depth), BF16),
-            pltpu.SemaphoreType.DMA((vocab // tile,)),
-        ],
-        compiler_params=pltpu.CompilerParams(vmem_limit_bytes=48 * 2**20),
-        cost_estimate=pl.CostEstimate(
-            flops=2 * all_rows * depth * vocab,
-            bytes_accessed=2 * vocab * depth + all_rows * (2 * depth + 4 * vocab),
-            transcendentals=0,
-        ),
-    )(index, factor, gain, weight, *blocks)
+    tile = min(vocab // 2, 512)
+    tiles = vocab // 2 // tile
+    out = [jax.ShapeDtypeStruct((half, vocab // 2), F32)] * CORES
+    out_specs = [pl.BlockSpec((half, tile), lambda n: (0, n))] * CORES
+    whole = lambda rows, columns: pl.BlockSpec((rows, columns), lambda n: (0, 0))
+    held = [pltpu.VMEM((tiles, tile, depth), BF16), pltpu.SemaphoreType.DMA((tiles,))]
+    hbm = pl.BlockSpec(memory_space=pltpu.HBM)
+    params = pltpu.CompilerParams(vmem_limit_bytes=48 * 2**20)
+    cost = pl.CostEstimate(
+        flops=all_rows * depth * vocab,
+        bytes_accessed=vocab * depth + all_rows * (2 * depth + 2 * vocab),
+        transcendentals=0,
+    )
+    keep, send, turned, *pieces = pl.pallas_call(
+        functools.partial(project_kernel, len(blocks[0])),
+        grid=(tiles,),
+        in_specs=[SMEM, VMEM, VMEM, hbm] + [VMEM] * (CHUNKS * len(blocks[0])),
+        out_specs=out_specs + [whole(depth, all_rows)] + [whole(piece_rows, depth)] * CHUNKS,
+        out_shape=out
+        + [jax.ShapeDtypeStruct((depth, all_rows), BF16)]
+        + [jax.ShapeDtypeStruct((piece_rows, depth), BF16)] * CHUNKS,
+        scratch_shapes=[pltpu.VMEM((all_rows, depth), BF16)] * 2 + held,
+        compiler_params=params,
+        cost_estimate=cost,
+    )(index, factor, gain, weight, *[x for chunk in blocks for x in chunk])
+    rest = pl.pallas_call(
+        project_rest_kernel,
+        grid=(tiles,),
+        in_specs=[hbm, VMEM],
+        out_specs=out_specs,
+        out_shape=out,
+        scratch_shapes=held,
+        compiler_params=params,
+        cost_estimate=cost,
+    )(weight, turned)
+    return [(keep, send), rest], pieces
 
 
 def back_kernel(piece, index_ref, mine_ref, other_ref, weight_ref, out_ref, grad_ref):
@@ -300,13 +331,18 @@
     for g in range(groups.size):
         for v in range(parts):
             p = ring.place[v]
-            held = [ring.order[q] for q in ring.sources(v, 0)]
-            group = [i // slots % groups.chips * CORES + i // slots // groups.chips for i in held]
-            add("place", [groups.entry(g, i) for i in group] + [i % slots for i in held])
+            place = []
+            for h in range(CHUNKS):
+                held = [ring.order[q] for q in ring.sources(v, h)]
+                for i in held:
+                    group = i // slots % groups.chips * CORES + i // slots // groups.chips
+                    place.append(groups.entry(g, group))
+                place += [i % slots for i in held]
             for h in range(CHUNKS):
                 start = p * piece_rows
                 start = start // chunk_rows * group_rows + h * chunk_rows + start % chunk_rows
-                table["place"][-1].append(start // piece_rows)
+                place.append(start // piece_rows)
+            add("place", place)
             entry = groups.entry(g, v * share_rows // group_rows)
             first = v * share_rows % group_rows
             start = first // chunk_rows * step_rows + entry * chunk_rows + first % chunk_rows
@@ -371,14 +407,17 @@
     rounds = ring.meetings(lambda terms: sum(terms[1:], terms[0]))
     rounds.append(lambda x: groups.gather_chips(jnp.concatenate([x, live_rows[None]])))
     rounds.append(lambda x: jnp.concatenate([x, groups.swap(x)], axis=0))
-    exchanged = [rounds[0](squares)]
-    late = rounds[1:]
+    for round in rounds[:2]:
+        squares = round(squares)
+    turned = after(turned, squares)
+    late = rounds[2:]
+    exchanged = [squares]
 
     def seen(step, arrivals):
         if step < len(late):
             exchanged.append(late[step](after(exchanged[-1], arrivals)))
 
-    blocks = ring.gather(turned, 0, seen)
+    blocks = [ring.gather(chunk(turned, h), h, seen if h == 0 else None) for h in range(CHUNKS)]
     both = exchanged[-1]
     valid_count = jnp.sum(both[:, 1])
     row_factor = lax.rsqrt(both[:, 0] / model_width + 1e-05)
@@ -398,45 +437,54 @@
     row_weight = 1048576.0 * live_rows / valid_count
     lane = lax.broadcasted_iota(jnp.uint32, (chunk_rows, LANES), 1)
 
-    keep, send, *pieces = project(
+    halves, pieces = project(
         index["place"], blocks, row_factor[:, :, None], gain, head_weight, piece_rows
     )
-    summed = (keep + groups.swap(send)).reshape(groups.chips, group_rows, vocab_width)
-    logits = summed[0]
-    for d in range(1, groups.chips):
-        logits = logits + groups.shift(summed[d], d)
-
-    top = jnp.max(logits, axis=1)
-    total = jnp.sum(jnp.exp(logits - top[:, None]), axis=1)
-    mine = jnp.stack([jnp.concatenate([top, target_top]), jnp.concatenate([total, target_total])])
+    logits, totals = [], []
+    for keep, send in halves:
+        summed = (keep + groups.swap(send)).reshape(groups.chips, group_rows, -1)
+        half = summed[0]
+        for d in range(1, groups.chips):
+            half = half + groups.shift(summed[d], d)
+        top = jnp.max(half, axis=1)
+        logits.append(half)
+        totals.append(jnp.stack([top, jnp.sum(jnp.exp(half - top[:, None]), axis=1)]))
+
+    mine = jnp.concatenate([merge_totals(totals), jnp.stack([target_top, target_total])], axis=1)
     met = ring.meet(mine, merge_totals)
     scale = jnp.exp(mine[0] - met[0]) / met[1]
-    draft_scale, target_scale = scale[:group_rows], scale[group_rows:]
+    top, draft_scale, target_scale = mine[0], scale[:group_rows], scale[group_rows:]
 
     grads = []
     for h in range(CHUNKS):
         factor = row_factor[:, h * chunk_rows : (h + 1) * chunk_rows]
-        own = chunk(logits, h)
-        draft_probs = jnp.exp(own - chunk(top, h)[:, None]) * chunk(draft_scale, h)[:, None]
-        target_probs = (
-            jnp.exp(chunk(targets, h) - chunk(target_top, h)[:, None])
-            * chunk(target_scale, h)[:, None]
-        )
-        logit_grad = chunk(row_weight, h)[:, None] * (draft_probs - target_probs)
-        logit_grad = lax.reduce_precision(logit_grad, 8, 7)
-        dot_part = jnp.sum(logit_grad * own, axis=1)
+        parts_of, dot_part = [], 0.0
+        for k, half in enumerate(logits):
+            own = chunk(half, h)
+            columns = slice(k * own.shape[1], (k + 1) * own.shape[1])
+            draft_probs = jnp.exp(own - chunk(top, h)[:, None]) * chunk(draft_scale, h)[:, None]
+            target_probs = (
+                jnp.exp(chunk(targets, h)[:, columns] - chunk(target_top, h)[:, None])
+                * chunk(target_scale, h)[:, None]
+            )
+            logit_grad = chunk(row_weight, h)[:, None] * (draft_probs - target_probs)
+            logit_grad = lax.reduce_precision(logit_grad, 8, 7)
+            dot_part = dot_part + jnp.sum(logit_grad * own, axis=1)
+            parts_of.append(logit_grad.astype(BF16))
         dot_high = lax.reduce_precision(dot_part, 8, 7)
         dot_low = dot_part - dot_high
         lanes = jnp.where(lane == own_lane, dot_high[:, None], 0.0) + jnp.where(
             lane == own_lane + 1, dot_low[:, None], 0.0
         )
-        message = jnp.concatenate([logit_grad.astype(BF16), lanes.astype(BF16)], axis=1)
-        everyone = groups.gather_halves(message)
+        message = jnp.concatenate(parts_of + [lanes.astype(BF16)], axis=1)
+        if h > 0:
+            message = after(message, mine)
+        mine = groups.gather_chips(message)
+        mine, other = [x.reshape(step_rows // CORES, -1) for x in (mine, groups.swap(mine))]
+        normed_grad = back(index["turn"], mine, other, head_weight, piece_rows)
         if h == CHUNKS - 1:
-            chosen = groups.gather(after(own_chosen, everyone).reshape(CHUNKS, chunk_rows, -1))
-            chosen = chosen.transpose(1, 0, 2, 3).reshape(CHUNKS * step_rows, -1)
-        mine, other = [x.reshape(step_rows // CORES, -1) for x in everyone]
-        normed_grad = back(index["turn"], mine, other, head_weight, piece_rows)
+            chosen = after(own_chosen, normed_grad).reshape(CHUNKS, chunk_rows, -1)
+            chosen = groups.gather(chosen).transpose(1, 0, 2, 3).reshape(CHUNKS * step_rows, -1)
 
         def part(t):
             first = t % parts * piece_rows

time: 202 us -> 207 us (1.025)
  waiting for transfers between devices: 84.9 us -> 74.2 us
  local copies, waits for them, and re-layouts: 6.41 us -> 16.8 us
  Pallas kernels: 29.6 us -> 32.7 us
    unnamed x17 -> x53, local copies, waits for them, and re-layouts: 0.04 us -> 12.2 us
    ppermute x35 -> x42, waiting for transfers between devices: 48.3 us -> 39.1 us  [shift(): lax.ppermute(x, 'vocab', [(order[p], order[(p + step) % size]) for p in r...]
    ppermute x5 -> x6, starting transfers between devices: 8.68 us -> 4.95 us  [shift(): lax.ppermute(x, 'dp', [(i, (i + CORES * step) % size) for i in range(size)])]
    ppermute x8, waiting for transfers between devices: 5.29 us -> 8.65 us  [partner(): return lax.ppermute(x, 'vocab', [(v, v ^ bit) for v in range(self.size)])]
    pallas_call x1 -> x2, Pallas kernels: 8.97 us -> 12.1 us  [the longest x1 6.73 us: project(): pl.pallas_call(functools.partial(project_kernel, len(blocks[0])), grid=(t...]
    ppermute x5 -> x6, waiting for transfers between devices: 4.33 us -> 1.5 us  [swap(): return lax.ppermute(x, 'dp', [(i, i ^ 1) for i in range(self.size)])]
    add x1 -> x2, other arithmetic: 0.25 us -> 2.73 us  [body(): summed = (keep + groups.swap(send)).reshape(groups.chips, group_rows, -1)]
    ppermute x5 -> x6, waiting for transfers between devices: 27 us -> 25 us  [shift(): lax.ppermute(x, 'dp', [(i, (i + CORES * step) % size) for i in range(size)])]
  transfers between devices with their start and end apart: 54 -> 63, of which waited for: 32 -> 37; matrix products, arithmetic and copies ran while one was open for 7% -> 8% of each run, Pallas kernels for 4% -> 7%
where the time goes in v7:
time: 207 us; the launch traced here: 206 us
  waiting for transfers between devices  74.2 us (36%)
  starting transfers between devices  65.9 us (32%)
  Pallas kernels  32.7 us (16%)
  local copies, waits for them, and re-layouts  16.8 us (8%)
  other arithmetic  14.7 us (7%)
    ppermute x42, starting transfers between devices, shift(): lax.ppermute(x, 'vocab', [(order[p], order[(p + step) % size]) for p in r...  44.1 us
    ppermute x42, waiting for transfers between devices, shift(): lax.ppermute(x, 'vocab', [(order[p], order[(p + step) % size]) for p in r...  39.1 us
    ppermute x6, waiting for transfers between devices, shift(): lax.ppermute(x, 'dp', [(i, (i + CORES * step) % size) for i in range(size)])  25 us
    ppermute x8, starting transfers between devices, partner(): return lax.ppermute(x, 'vocab', [(v, v ^ bit) for v in range(self.size)])  14.3 us
    pallas_call x1, Pallas kernels, outer(): pl.pallas_call(functools.partial(outer_kernel, len(chunks[0]), tile), gri...  12.6 us
    unnamed x53, local copies, waits for them, and re-layouts  12.2 us
    ppermute x8, waiting for transfers between devices, partner(): return lax.ppermute(x, 'vocab', [(v, v ^ bit) for v in range(self.size)])  8.65 us
    pallas_call x2, Pallas kernels, back(): pl.pallas_call(functools.partial(back_kernel, piece_rows), grid=(depth //...  8.03 us
  transfers between devices with their start and end apart: 63, of which 37 were waited for; matrix products, arithmetic and copies ran while one was open for 8% of the time, Pallas kernels for 7%

profile of v7, /device:TPU:0, one launch (start us, length us, event | category | flops | bytes accessed | tf_op | source)
XLA Modules:
  0.0 206.1 jit_solution(6336832394994258305)
XLA Ops:
  0.6 1.7 collective-permute-start.4
  3.5 3.0 %collective-permute-start = (f32[1,128]{1,0:T(1,128)S(1)}, f32[1,128]{1,0:T(1,128)S(1)}, u32[]{:S(2)}, u32[]{:S(2)}) collective-permute-start(f32[1,128]{1,0:T(1,128)S(1)} %bitcast.114), channel_id=1, source_target_pairs={{0,1},{1,0},{2,3},{3,2},{4,5},{5,4},{6,7},{7,6},{8,9},{9,8},{10,11... | collective-permute-start | bytes 1544 | tf_op jit(solution)/shard_map/ppermute | solution.py:47
  8.0 5.0 %collective-permute-start.3 = (f32[1,128]{1,0:T(1,128)S(1)}, f32[1,128]{1,0:T(1,128)S(1)}, u32[]{:S(2)}, u32[]{:S(2)}) collective-permute-start(f32[1,128]{1,0:T(1,128)S(1)} %bitcast_add_fusion), channel_id=1, source_target_pairs={{0,6},{1,7},{2,4},{3,5},{4,2},{5,3},{6,0},{7,1},{8,14},{9,15},{10,... | collective-permute-start | bytes 1544 | tf_op jit(solution)/shard_map/ppermute | solution.py:47
  13.6 1.8 collective-permute-done.3
  15.4 2.1 %collective-permute-done.2 = f32[1,128]{1,0:T(1,128)S(1)} collective-permute-done((f32[1,128]{1,0:T(1,128)S(1)}, f32[1,128]{1,0:T(1,128)S(1)}, u32[]{:S(2)}, u32[]{:S(2)}) %collective-permute-start.2) | collective-permute-done | bytes 544 | tf_op jit(solution)/shard_map/ppermute | solution.py:47
  17.5 1.6 collective-permute-start.6
  19.6 1.5 collective-permute-start.17
  22.7 1.9 collective-permute-done.5.refs_3_
  24.6 1.7 collective-permute-start.7
  30.1 1.4 dynamic_slice.13
  33.5 1.8 collective-permute-start.19
  36.6 1.5 collective-permute-start.16
  38.2 1.7 collective-permute-done.19.refs_14_
  39.9 1.8 collective-permute-start.20
  51.8 6.7 %shard_map.95 = (f32[256,1024]{1,0:T(8,128)S(1)}, f32[256,1024]{1,0:T(8,128)}, bf16[2048,512]{1,0:T(8,128)(2,1)}, bf16[32,2048]{1,0:T(8,128)(2,1)S(1)}, bf16[32,2048]{1,0:T(8,128)(2,1)S(1)}) custom-call(s32[34]{0:T(128)S(1)} %slice_bitcast_fusion.2.index_ref, f32[4,128,1]{2,1,0:T(8,128)S(1)} %copy.13.factor_ref, f32[1,2048]{1,0:T(1,128)S(1)} %bitcast.91, ...), custom_call_target="tpu_custom_call" | custom-call | flops 2147483648 | bytes 8388608 | tf_op jit(solution)/shard_map/pallas_call | solution.py:210
  58.6 1.6 copy-done.3
  60.2 5.4 %shard_map.96 = (f32[256,1024]{1,0:T(8,128)S(1)}, f32[256,1024]{1,0:T(8,128)}) custom-call(bf16[2048,2048]{1,0:T(8,128)(2,1)} %weight_ref.7, bf16[2048,512]{1,0:T(8,128)(2,1)S(1)} %copy-done.3), custom_call_target="tpu_custom_call" | custom-call | flops 2147483648 | bytes 8388608 | tf_op jit(solution)/shard_map/pallas_call | solution.py:222
  68.4 1.4 add.163
  71.0 1.4 add.165
  72.4 1.8 collective-permute-start.24
  74.8 9.9 %collective-permute-done.22 = f32[128,1024]{1,0:T(8,128)S(1)} collective-permute-done((f32[128,1024]{1,0:T(8,128)S(1)}, f32[128,1024]{1,0:T(8,128)S(1)}, u32[]{:S(2)}, u32[]{:S(2)}) %collective-permute-start.22) | collective-permute-done | bytes 524320 | tf_op jit(solution)/shard_map/ppermute | solution.py:110
  85.1 9.9 %collective-permute-done.24 = f32[128,1024]{1,0:T(8,128)S(1)} collective-permute-done((f32[128,1024]{1,0:T(8,128)S(1)}, f32[128,1024]{1,0:T(8,128)S(1)}, u32[]{:S(2)}, u32[]{:S(2)}) %collective-permute-start.24) | collective-permute-done | bytes 524320 | tf_op jit(solution)/shard_map/ppermute | solution.py:110
  96.7 2.3 %collective-permute-done.25 = f32[2,256]{1,0:T(2,128)S(1)} collective-permute-done((f32[2,256]{1,0:T(2,128)S(1)}, f32[2,256]{1,0:T(2,128)S(1)}, u32[]{:S(2)}, u32[]{:S(2)}) %collective-permute-start.25) | collective-permute-done | bytes 2080 | tf_op jit(solution)/shard_map/ppermute | solution.py:47
  99.1 1.7 collective-permute-start.28
  101.0 2.6 %collective-permute-start.26 = (f32[2,256]{1,0:T(2,128)S(1)}, f32[2,256]{1,0:T(2,128)S(1)}, u32[]{:S(2)}, u32[]{:S(2)}) collective-permute-start(f32[2,256]{1,0:T(2,128)S(1)} %pad_maximum_fusion.7), channel_id=1, source_target_pairs={{0,2},{1,3},{2,0},{3,1},{4,6},{5,7},{6,4},{7,5},{8,10},{9,11},{10,... | collective-permute-start | bytes 6152 | tf_op jit(solution)/shard_map/ppermute | solution.py:47
  108.6 5.1 %collective-permute-done.29 = bf16[64,2176]{1,0:T(8,128)(2,1)S(1)} collective-permute-done((bf16[64,2176]{1,0:T(8,128)(2,1)S(1)}, bf16[64,2176]{1,0:T(8,128)(2,1)S(1)}, u32[]{:S(2)}, u32[]{:S(2)}) %collective-permute-start.29) | collective-permute-done | bytes 278560 | tf_op jit(solution)/shard_map/ppermute | solution.py:110
  114.3 1.5 collective-permute-done.34
  115.8 3.4 %copy-done.2 = bf16[2048,2048]{1,0:T(8,128)(2,1)S(1)} copy-done((bf16[2048,2048]{1,0:T(8,128)(2,1)S(1)}, bf16[2048,2048]{1,0:T(8,128)(2,1)}, u32[]{:S(2)}) %copy-start.2) | copy-done | bytes 8388632
  119.2 4.0 %shard_map.98 = f32[256,2176]{1,0:T(8,128)S(1)} custom-call(s32[8]{0:T(128)S(1)} %slice_bitcast_fusion.3.index_ref, bf16[128,2176]{1,0:T(8,128)(2,1)S(1)} %bitcast.88, bf16[128,2176]{1,0:T(8,128)(2,1)S(1)} %bitcast.90, bf16[2048,2048]{1,0:T(8,128)(2,1)S(1)} %copy-done.2), custom_call_target="tpu_custom_call" | custom-call | flops 2147483648 | bytes 11534336 | tf_op jit(solution)/shard_map/pallas_call | solution.py:258
  123.4 1.9 collective-permute-start.35
  125.6 3.5 %collective-permute-done.35 = bf16[32,2176]{1,0:T(8,128)(2,1)S(1)} collective-permute-done((bf16[32,2176]{1,0:T(8,128)(2,1)S(1)}, bf16[32,2176]{1,0:T(8,128)(2,1)S(1)}, u32[]{:S(2)}, u32[]{:S(2)}) %collective-permute-start.35) | collective-permute-done | bytes 139296 | tf_op jit(solution)/shard_map/ppermute | solution.py:42
  129.2 1.9 collective-permute-start.36
  131.1 4.0 %shard_map.97 = f32[256,2176]{1,0:T(8,128)S(1)} custom-call(s32[8]{0:T(128)S(1)} %slice_bitcast_fusion.3.index_ref, bf16[128,2176]{1,0:T(8,128)(2,1)S(1)} %bitcast.87, bf16[128,2176]{1,0:T(8,128)(2,1)S(1)} %bitcast.89, bf16[2048,2048]{1,0:T(8,128)(2,1)S(1)} %copy-done.2), custom_call_target="tpu_custom_call" | custom-call | flops 2147483648 | bytes 11534336 | tf_op jit(solution)/shard_map/pallas_call | solution.py:258
  138.5 3.4 %collective-permute-done.37 = bf16[32,2176]{1,0:T(8,128)(2,1)S(1)} collective-permute-done((bf16[32,2176]{1,0:T(8,128)(2,1)S(1)}, bf16[32,2176]{1,0:T(8,128)(2,1)S(1)}, u32[]{:S(2)}, u32[]{:S(2)}) %collective-permute-start.37) | collective-permute-done | bytes 139296 | tf_op jit(solution)/shard_map/ppermute | solution.py:42
  145.7 3.3 %collective-permute-done.40 = bf16[32,2176]{1,0:T(8,128)(2,1)S(1)} collective-permute-done((bf16[32,2176]{1,0:T(8,128)(2,1)S(1)}, bf16[32,2176]{1,0:T(8,128)(2,1)S(1)}, u32[]{:S(2)}, u32[]{:S(2)}) %collective-permute-start.40) | collective-permute-done | bytes 139296 | tf_op jit(solution)/shard_map/ppermute | solution.py:42
  149.1 1.4 collective-permute-start.41
  154.6 2.6 %collective-permute-done.53 = bf16[32,2176]{1,0:T(8,128)(2,1)S(1)} collective-permute-done((bf16[32,2176]{1,0:T(8,128)(2,1)S(1)}, bf16[32,2176]{1,0:T(8,128)(2,1)S(1)}, u32[]{:S(2)}, u32[]{:S(2)}) %collective-permute-start.53) | collective-permute-done | bytes 139296 | tf_op jit(solution)/shard_map/ppermute | solution.py:42
  157.2 1.4 collective-permute-start.54
  160.0 2.4 %collective-permute-done.54 = bf16[32,2176]{1,0:T(8,128)(2,1)S(1)} collective-permute-done((bf16[32,2176]{1,0:T(8,128)(2,1)S(1)}, bf16[32,2176]{1,0:T(8,128)(2,1)S(1)}, u32[]{:S(2)}, u32[]{:S(2)}) %collective-permute-start.54) | collective-permute-done | bytes 139296 | tf_op jit(solution)/shard_map/ppermute | solution.py:42
  162.4 1.4 collective-permute-start.55
  164.0 3.5 %collective-permute-done.55 = bf16[32,2176]{1,0:T(8,128)(2,1)S(1)} collective-permute-done((bf16[32,2176]{1,0:T(8,128)(2,1)S(1)}, bf16[32,2176]{1,0:T(8,128)(2,1)S(1)}, u32[]{:S(2)}, u32[]{:S(2)}) %collective-permute-start.55) | collective-permute-done | bytes 139296 | tf_op jit(solution)/shard_map/ppermute | solution.py:42
  169.2 1.4 collective-permute-start.59
  171.7 1.6 collective-permute-start.46
  173.3 2.2 %collective-permute-done.59.refs_12_ = bf16[32,2048]{1,0:T(8,128)(2,1)S(1)} collective-permute-done((bf16[32,2048]{1,0:T(8,128)(2,1)S(1)}, bf16[32,2048]{1,0:T(8,128)(2,1)S(1)}, u32[]{:S(2)}, u32[]{:S(2)}) %collective-permute-start.59) | collective-permute-done | bytes 131104 | tf_op jit(solution)/shard_map/ppermute | solution.py:42
  178.5 1.8 collective-permute-start.57
  183.3 2.0 collective-permute-done.57.refs_9_
  191.5 1.4 collective-permute-done.62.refs_15_
  193.5 12.6 %shard_map.99 = (f32[2048,3072]{1,0:T(8,128)}, bf16[64,2048]{1,0:T(8,128)(2,1)}) custom-call(s32[17]{0:T(128)S(1)} %slice_bitcast_fusion.4.index_ref, bf16[512,3072]{1,0:T(8,128)(2,1)S(1)} %bitcast.86, bf16[32,2048]{1,0:T(8,128)(2,1)S(1)} %collective-permute-done.45.refs_0_, bf16[32,2048]{1,0:T(8,128)(2,1)S(1)} %collective-permute-done.44.refs_1_, ...), custom_call_target="tpu_custom_call" | custom-call | flops 6442450944 | bytes 30408704 | tf_op jit(solution)/shard_map/pallas_call | solution.py:299
  (212 shorter events, 63.6 us)
Async XLA Ops:
  0.6 16.8 %collective-permute-start.4 = (bf16[128,1024]{1,0:T(8,128)(2,1)}, bf16[128,1024]{1,0:T(8,128)(2,1)S(1)}, u32[]{:S(2)}, u32[]{:S(2)}) collective-permute-start(bf16[128,1024]{1,0:T(8,128)(2,1)} %param.8), channel_id=1, source_target_pairs={{0,0},{1,1},{2,8},{3,9},{4,16},{5,17},{6,24},{7,25},{8,4},{9,5},{1... | collective-permute-start | bytes 786440 | tf_op jit(solution)/shard_map/ppermute | solution.py:403
  8.0 7.3 %collective-permute-start.3 = (f32[1,128]{1,0:T(1,128)S(1)}, f32[1,128]{1,0:T(1,128)S(1)}, u32[]{:S(2)}, u32[]{:S(2)}) collective-permute-start(f32[1,128]{1,0:T(1,128)S(1)} %bitcast_add_fusion), channel_id=1, source_target_pairs={{0,6},{1,7},{2,4},{3,5},{4,2},{5,3},{6,0},{7,1},{8,14},{9,15},{10,... | collective-permute-start | bytes 1544 | tf_op jit(solution)/shard_map/ppermute | solution.py:47
  17.5 5.1 %collective-permute-start.6 = (bf16[64,1024]{1,0:T(8,128)(2,1)S(1)}, bf16[64,1024]{1,0:T(8,128)(2,1)S(1)}, u32[]{:S(2)}, u32[]{:S(2)}) collective-permute-start(bf16[64,1024]{1,0:T(8,128)(2,1)S(1)} %get-tuple-element.71.refs_4_), channel_id=1, source_target_pairs={{0,1},{2,0},{4,2},{6,4},{7,6},{5,7},{3,5},{1,3},{8,9},{10,8},{12,1... | collective-permute-start | bytes 393224 | tf_op jit(solution)/shard_map/ppermute | solution.py:42
  19.1 5.5 %collective-permute-start.5 = (bf16[64,1024]{1,0:T(8,128)(2,1)S(1)}, bf16[64,1024]{1,0:T(8,128)(2,1)S(1)}, u32[]{:S(2)}, u32[]{:S(2)}) collective-permute-start(bf16[64,1024]{1,0:T(8,128)(2,1)S(1)} %get-tuple-element.71.refs_4_), channel_id=1, source_target_pairs={{0,2},{2,4},{4,6},{6,7},{7,5},{5,3},{3,1},{1,0},{8,10},{10,12},{12... | collective-permute-start | bytes 393224 | tf_op jit(solution)/shard_map/ppermute | solution.py:42
  19.6 8.7 %collective-permute-start.17 = (bf16[64,1024]{1,0:T(8,128)(2,1)S(1)}, bf16[64,1024]{1,0:T(8,128)(2,1)S(1)}, u32[]{:S(2)}, u32[]{:S(2)}) collective-permute-start(bf16[64,1024]{1,0:T(8,128)(2,1)S(1)} %get-tuple-element.70.refs_11_), channel_id=1, source_target_pairs={{0,1},{2,0},{4,2},{6,4},{7,6},{5,7},{3,5},{1,3},{8,9},{10,8},{12,1... | collective-permute-start | bytes 393224 | tf_op jit(solution)/shard_map/ppermute | solution.py:42
  21.8 9.8 %collective-permute-start.14 = (bf16[64,1024]{1,0:T(8,128)(2,1)S(1)}, bf16[64,1024]{1,0:T(8,128)(2,1)S(1)}, u32[]{:S(2)}, u32[]{:S(2)}) collective-permute-start(bf16[64,1024]{1,0:T(8,128)(2,1)S(1)} %get-tuple-element.70.refs_11_), channel_id=1, source_target_pairs={{0,2},{2,4},{4,6},{6,7},{7,5},{5,3},{3,1},{1,0},{8,10},{10,12},{12... | collective-permute-start | bytes 393224 | tf_op jit(solution)/shard_map/ppermute | solution.py:42
  24.6 7.9 %collective-permute-start.7 = (f32[2,128]{1,0:T(2,128)S(1)}, f32[2,128]{1,0:T(2,128)S(1)}, u32[]{:S(2)}, u32[]{:S(2)}) collective-permute-start(f32[2,128]{1,0:T(2,128)S(1)} %get-tuple-element.103), channel_id=1, source_target_pairs={{0,16},{8,24},{16,0},{24,8},{1,17},{9,25},{17,1},{25,9},{2,18},{10... | collective-permute-start | bytes 3080 | tf_op jit(solution)/shard_map/ppermute | solution.py:110
  26.3 6.2 %collective-permute-start.9 = (bf16[64,1024]{1,0:T(8,128)(2,1)S(1)}, bf16[64,1024]{1,0:T(8,128)(2,1)S(1)}, u32[]{:S(2)}, u32[]{:S(2)}) collective-permute-start(bf16[64,1024]{1,0:T(8,128)(2,1)S(1)} %collective-permute-done.6.refs_5_), channel_id=1, source_target_pairs={{0,1},{2,0},{4,2},{6,4},{7,6},{5,7},{3,5},{1,3},{8,9},{10,8},{12,1... | collective-permute-start | bytes 393224 | tf_op jit(solution)/shard_map/ppermute | solution.py:42
  27.4 5.8 %collective-permute-start.8 = (bf16[64,1024]{1,0:T(8,128)(2,1)S(1)}, bf16[64,1024]{1,0:T(8,128)(2,1)S(1)}, u32[]{:S(2)}, u32[]{:S(2)}) collective-permute-start(bf16[64,1024]{1,0:T(8,128)(2,1)S(1)} %collective-permute-done.5.refs_3_), channel_id=1, source_target_pairs={{0,2},{2,4},{4,6},{6,7},{7,5},{5,3},{3,1},{1,0},{8,10},{10,12},{12... | collective-permute-start | bytes 393224 | tf_op jit(solution)/shard_map/ppermute | solution.py:42
  28.3 5.2 %collective-permute-start.18 = (bf16[64,1024]{1,0:T(8,128)(2,1)S(1)}, bf16[64,1024]{1,0:T(8,128)(2,1)S(1)}, u32[]{:S(2)}, u32[]{:S(2)}) collective-permute-start(bf16[64,1024]{1,0:T(8,128)(2,1)S(1)} %collective-permute-done.17.refs_12_), channel_id=1, source_target_pairs={{0,1},{2,0},{4,2},{6,4},{7,6},{5,7},{3,5},{1,3},{8,9},{10,8},{12,1... | collective-permute-start | bytes 393224 | tf_op jit(solution)/shard_map/ppermute | solution.py:42
  33.3 8.4 %collective-permute-start.11 = (bf16[64,1024]{1,0:T(8,128)(2,1)S(1)}, bf16[64,1024]{1,0:T(8,128)(2,1)S(1)}, u32[]{:S(2)}, u32[]{:S(2)}) collective-permute-start(bf16[64,1024]{1,0:T(8,128)(2,1)S(1)} %collective-permute-done.8.refs_2_), channel_id=1, source_target_pairs={{0,2},{2,4},{4,6},{6,7},{7,5},{5,3},{3,1},{1,0},{8,10},{10,12},{12... | collective-permute-start | bytes 393224 | tf_op jit(solution)/shard_map/ppermute | solution.py:42
  33.5 6.3 %collective-permute-start.19 = (bf16[64,1024]{1,0:T(8,128)(2,1)S(1)}, bf16[64,1024]{1,0:T(8,128)(2,1)S(1)}, u32[]{:S(2)}, u32[]{:S(2)}) collective-permute-start(bf16[64,1024]{1,0:T(8,128)(2,1)S(1)} %collective-permute-done.18.refs_13_), channel_id=1, source_target_pairs={{0,1},{2,0},{4,2},{6,4},{7,6},{5,7},{3,5},{1,3},{8,9},{10,8},{12,1... | collective-permute-start | bytes 393224 | tf_op jit(solution)/shard_map/ppermute | solution.py:42
  35.3 8.0 %collective-permute-start.13 = (bf16[64,1024]{1,0:T(8,128)(2,1)S(1)}, bf16[64,1024]{1,0:T(8,128)(2,1)S(1)}, u32[]{:S(2)}, u32[]{:S(2)}) collective-permute-start(bf16[64,1024]{1,0:T(8,128)(2,1)S(1)} %collective-permute-done.9.refs_6_), channel_id=1, source_target_pairs={{0,1},{2,0},{4,2},{6,4},{7,6},{5,7},{3,5},{1,3},{8,9},{10,8},{12,1... | collective-permute-start | bytes 393224 | tf_op jit(solution)/shard_map/ppermute | solution.py:42
  36.6 6.0 %collective-permute-start.16 = (bf16[64,1024]{1,0:T(8,128)(2,1)S(1)}, bf16[64,1024]{1,0:T(8,128)(2,1)S(1)}, u32[]{:S(2)}, u32[]{:S(2)}) collective-permute-start(bf16[64,1024]{1,0:T(8,128)(2,1)S(1)} %collective-permute-done.15.refs_9_), channel_id=1, source_target_pairs={{0,2},{2,4},{4,6},{6,7},{7,5},{5,3},{3,1},{1,0},{8,10},{10,12},{12... | collective-permute-start | bytes 393224 | tf_op jit(solution)/shard_map/ppermute | solution.py:42
  58.5 9.9 %collective-permute-start.21 = (f32[256,1024]{1,0:T(8,128)}, f32[256,1024]{1,0:T(8,128)}, u32[]{:S(2)}, u32[]{:S(2)}) collective-permute-start(f32[256,1024]{1,0:T(8,128)} %get-tuple-element.20), channel_id=1, source_target_pairs={{0,8},{8,0},{16,24},{24,16},{1,9},{9,1},{17,25},{25,17},{2,10},{10... | collective-permute-start | bytes 3145736 | tf_op jit(solution)/shard_map/ppermute | solution.py:106
  65.7 5.3 %collective-permute-start.23 = (f32[256,1024]{1,0:T(8,128)}, f32[256,1024]{1,0:T(8,128)}, u32[]{:S(2)}, u32[]{:S(2)}) collective-permute-start(f32[256,1024]{1,0:T(8,128)} %get-tuple-element.23), channel_id=1, source_target_pairs={{0,8},{8,0},{16,24},{24,16},{1,9},{9,1},{17,25},{25,17},{2,10},{10... | collective-permute-start | bytes 3145736 | tf_op jit(solution)/shard_map/ppermute | solution.py:106
  69.8 14.9 %collective-permute-start.22 = (f32[128,1024]{1,0:T(8,128)S(1)}, f32[128,1024]{1,0:T(8,128)S(1)}, u32[]{:S(2)}, u32[]{:S(2)}) collective-permute-start(f32[128,1024]{1,0:T(8,128)S(1)} %slice.333), channel_id=1, source_target_pairs={{0,16},{8,24},{16,0},{24,8},{1,17},{9,25},{17,1},{25,9},{2,18},{10... | collective-permute-start | bytes 1572872 | tf_op jit(solution)/shard_map/ppermute | solution.py:110
  72.4 22.6 %collective-permute-start.24 = (f32[128,1024]{1,0:T(8,128)S(1)}, f32[128,1024]{1,0:T(8,128)S(1)}, u32[]{:S(2)}, u32[]{:S(2)}) collective-permute-start(f32[128,1024]{1,0:T(8,128)S(1)} %slice.336), channel_id=1, source_target_pairs={{0,16},{8,24},{16,0},{24,8},{1,17},{9,25},{17,1},{25,9},{2,18},{10... | collective-permute-start | bytes 1572872 | tf_op jit(solution)/shard_map/ppermute | solution.py:110
  99.1 5.4 %collective-permute-start.28 = (f32[2,256]{1,0:T(2,128)S(1)}, f32[2,256]{1,0:T(2,128)S(1)}, u32[]{:S(2)}, u32[]{:S(2)}) collective-permute-start(f32[2,256]{1,0:T(2,128)S(1)} %pad_maximum_fusion.7), channel_id=1, source_target_pairs={{0,6},{1,7},{2,4},{3,5},{4,2},{5,3},{6,0},{7,1},{8,14},{9,15},{10,... | collective-permute-start | bytes 6152 | tf_op jit(solution)/shard_map/ppermute | solution.py:47
  107.1 6.6 %collective-permute-start.29 = (bf16[64,2176]{1,0:T(8,128)(2,1)S(1)}, bf16[64,2176]{1,0:T(8,128)(2,1)S(1)}, u32[]{:S(2)}, u32[]{:S(2)}) collective-permute-start(bf16[64,2176]{1,0:T(8,128)(2,1)S(1)} %get-tuple-element.69), channel_id=1, source_target_pairs={{0,16},{8,24},{16,0},{24,8},{1,17},{9,25},{17,1},{25,9},{2,18},{10... | collective-permute-start | bytes 835592 | tf_op jit(solution)/shard_map/ppermute | solution.py:110
  114.0 11.3 %collective-permute-start.30 = (bf16[64,2176]{1,0:T(8,128)(2,1)S(1)}, bf16[64,2176]{1,0:T(8,128)(2,1)S(1)}, u32[]{:S(2)}, u32[]{:S(2)}) collective-permute-start(bf16[64,2176]{1,0:T(8,128)(2,1)S(1)} %pad_maximum_fusion.4), channel_id=1, source_target_pairs={{0,16},{8,24},{16,0},{24,8},{1,17},{9,25},{17,1},{25,9},{2,18},{10... | collective-permute-start | bytes 835592 | tf_op jit(solution)/shard_map/ppermute | solution.py:110
  123.4 5.8 %collective-permute-start.35 = (bf16[32,2176]{1,0:T(8,128)(2,1)S(1)}, bf16[32,2176]{1,0:T(8,128)(2,1)S(1)}, u32[]{:S(2)}, u32[]{:S(2)}) collective-permute-start(bf16[32,2176]{1,0:T(8,128)(2,1)S(1)} %get-tuple-element.60), channel_id=1, source_target_pairs={{0,2},{2,4},{4,6},{6,7},{7,5},{5,3},{3,1},{1,0},{8,10},{10,12},{12... | collective-permute-start | bytes 417800 | tf_op jit(solution)/shard_map/ppermute | solution.py:42
  125.3 5.7 %collective-permute-start.31 = (bf16[2,64,2176]{2,1,0:T(8,128)(2,1)S(1)}, bf16[2,64,2176]{2,1,0:T(8,128)(2,1)S(1)}, u32[]{:S(2)}, u32[]{:S(2)}) collective-permute-start(bf16[2,64,2176]{2,1,0:T(8,128)(2,1)S(1)} %pad_maximum_fusion.3), channel_id=1, source_target_pairs={{0,8},{8,0},{16,24},{24,16},{1,9},{9,1},{17,25},{25,17},{2,10},{10... | collective-permute-start | bytes 1671176 | tf_op jit(solution)/shard_map/ppermute | solution.py:106
  125.4 13.1 %collective-permute-start.39 = (bf16[32,2176]{1,0:T(8,128)(2,1)S(1)}, bf16[32,2176]{1,0:T(8,128)(2,1)S(1)}, u32[]{:S(2)}, u32[]{:S(2)}) collective-permute-start(bf16[32,2176]{1,0:T(8,128)(2,1)S(1)} %get-tuple-element.61), channel_id=1, source_target_pairs={{0,1},{2,0},{4,2},{6,4},{7,6},{5,7},{3,5},{1,3},{8,9},{10,8},{12,1... | collective-permute-start | bytes 417800 | tf_op jit(solution)/shard_map/ppermute | solution.py:42
  129.2 6.5 %collective-permute-start.36 = (bf16[32,2176]{1,0:T(8,128)(2,1)S(1)}, bf16[32,2176]{1,0:T(8,128)(2,1)S(1)}, u32[]{:S(2)}, u32[]{:S(2)}) collective-permute-start(bf16[32,2176]{1,0:T(8,128)(2,1)S(1)} %fusion.8), channel_id=1, source_target_pairs={{0,2},{2,4},{4,6},{6,7},{7,5},{5,3},{3,1},{1,0},{8,10},{10,12},{12... | collective-permute-start | bytes 417800 | tf_op jit(solution)/shard_map/ppermute | solution.py:42
  135.2 28.5 %collective-permute-start.32 = (bf16[2,64,3072]{2,1,0:T(8,128)(2,1)S(1)}, bf16[2,64,3072]{2,1,0:T(8,128)(2,1)S(1)}, u32[]{:S(2)}, u32[]{:S(2)}) collective-permute-start(bf16[2,64,3072]{2,1,0:T(8,128)(2,1)S(1)} %bitcast.92), channel_id=1, source_target_pairs={{0,16},{8,24},{16,0},{24,8},{1,17},{9,25},{17,1},{25,9},{2,18},{10... | collective-permute-start | bytes 2359304 | tf_op jit(solution)/shard_map/ppermute | solution.py:110
  135.7 6.3 %collective-permute-start.37 = (bf16[32,2176]{1,0:T(8,128)(2,1)S(1)}, bf16[32,2176]{1,0:T(8,128)(2,1)S(1)}, u32[]{:S(2)}, u32[]{:S(2)}) collective-permute-start(bf16[32,2176]{1,0:T(8,128)(2,1)S(1)} %fusion.9), channel_id=1, source_target_pairs={{0,2},{2,4},{4,6},{6,7},{7,5},{5,3},{3,1},{1,0},{8,10},{10,12},{12... | collective-permute-start | bytes 417800 | tf_op jit(solution)/shard_map/ppermute | solution.py:42
  136.4 8.5 %collective-permute-start.49 = (bf16[32,2176]{1,0:T(8,128)(2,1)S(1)}, bf16[32,2176]{1,0:T(8,128)(2,1)S(1)}, u32[]{:S(2)}, u32[]{:S(2)}) collective-permute-start(bf16[32,2176]{1,0:T(8,128)(2,1)S(1)} %get-tuple-element.58), channel_id=1, source_target_pairs={{0,2},{2,4},{4,6},{6,7},{7,5},{5,3},{3,1},{1,0},{8,10},{10,12},{12... | collective-permute-start | bytes 417800 | tf_op jit(solution)/shard_map/ppermute | solution.py:42
  137.3 13.2 %collective-permute-start.52 = (bf16[32,2176]{1,0:T(8,128)(2,1)S(1)}, bf16[32,2176]{1,0:T(8,128)(2,1)S(1)}, u32[]{:S(2)}, u32[]{:S(2)}) collective-permute-start(bf16[32,2176]{1,0:T(8,128)(2,1)S(1)} %get-tuple-element.59), channel_id=1, source_target_pairs={{0,1},{2,0},{4,2},{6,4},{7,6},{5,7},{3,5},{1,3},{8,9},{10,8},{12,1... | collective-permute-start | bytes 417800 | tf_op jit(solution)/shard_map/ppermute | solution.py:42
  142.0 11.1 %collective-permute-start.38 = (bf16[32,2176]{1,0:T(8,128)(2,1)S(1)}, bf16[32,2176]{1,0:T(8,128)(2,1)S(1)}, u32[]{:S(2)}, u32[]{:S(2)}) collective-permute-start(bf16[32,2176]{1,0:T(8,128)(2,1)S(1)} %get-tuple-element.52), channel_id=1, source_target_pairs={{0,2},{2,4},{4,6},{6,7},{7,5},{5,3},{3,1},{1,0},{8,10},{10,12},{12... | collective-permute-start | bytes 417800 | tf_op jit(solution)/shard_map/ppermute | solution.py:42
  142.8 6.3 %collective-permute-start.40 = (bf16[32,2176]{1,0:T(8,128)(2,1)S(1)}, bf16[32,2176]{1,0:T(8,128)(2,1)S(1)}, u32[]{:S(2)}, u32[]{:S(2)}) collective-permute-start(bf16[32,2176]{1,0:T(8,128)(2,1)S(1)} %get-tuple-element.53), channel_id=1, source_target_pairs={{0,1},{2,0},{4,2},{6,4},{7,6},{5,7},{3,5},{1,3},{8,9},{10,8},{12,1... | collective-permute-start | bytes 417800 | tf_op jit(solution)/shard_map/ppermute | solution.py:42
  144.9 6.0 %collective-permute-start.50 = (bf16[32,2176]{1,0:T(8,128)(2,1)S(1)}, bf16[32,2176]{1,0:T(8,128)(2,1)S(1)}, u32[]{:S(2)}, u32[]{:S(2)}) collective-permute-start(bf16[32,2176]{1,0:T(8,128)(2,1)S(1)} %fusion.3), channel_id=1, source_target_pairs={{0,2},{2,4},{4,6},{6,7},{7,5},{5,3},{3,1},{1,0},{8,10},{10,12},{12... | collective-permute-start | bytes 417800 | tf_op jit(solution)/shard_map/ppermute | solution.py:42
  149.1 5.4 %collective-permute-start.41 = (bf16[32,2176]{1,0:T(8,128)(2,1)S(1)}, bf16[32,2176]{1,0:T(8,128)(2,1)S(1)}, u32[]{:S(2)}, u32[]{:S(2)}) collective-permute-start(bf16[32,2176]{1,0:T(8,128)(2,1)S(1)} %fusion.7), channel_id=1, source_target_pairs={{0,1},{2,0},{4,2},{6,4},{7,6},{5,7},{3,5},{1,3},{8,9},{10,8},{12,1... | collective-permute-start | bytes 417800 | tf_op jit(solution)/shard_map/ppermute | solution.py:42
  151.0 12.9 %collective-permute-start.51 = (bf16[32,2176]{1,0:T(8,128)(2,1)S(1)}, bf16[32,2176]{1,0:T(8,128)(2,1)S(1)}, u32[]{:S(2)}, u32[]{:S(2)}) collective-permute-start(bf16[32,2176]{1,0:T(8,128)(2,1)S(1)} %get-tuple-element.50), channel_id=1, source_target_pairs={{0,2},{2,4},{4,6},{6,7},{7,5},{5,3},{3,1},{1,0},{8,10},{10,12},{12... | collective-permute-start | bytes 417800 | tf_op jit(solution)/shard_map/ppermute | solution.py:42
  151.8 5.4 %collective-permute-start.53 = (bf16[32,2176]{1,0:T(8,128)(2,1)S(1)}, bf16[32,2176]{1,0:T(8,128)(2,1)S(1)}, u32[]{:S(2)}, u32[]{:S(2)}) collective-permute-start(bf16[32,2176]{1,0:T(8,128)(2,1)S(1)} %get-tuple-element.51), channel_id=1, source_target_pairs={{0,1},{2,0},{4,2},{6,4},{7,6},{5,7},{3,5},{1,3},{8,9},{10,8},{12,1... | collective-permute-start | bytes 417800 | tf_op jit(solution)/shard_map/ppermute | solution.py:42
  162.4 5.1 %collective-permute-start.55 = (bf16[32,2176]{1,0:T(8,128)(2,1)S(1)}, bf16[32,2176]{1,0:T(8,128)(2,1)S(1)}, u32[]{:S(2)}, u32[]{:S(2)}) collective-permute-start(bf16[32,2176]{1,0:T(8,128)(2,1)S(1)} %fusion.2), channel_id=1, source_target_pairs={{0,1},{2,0},{4,2},{6,4},{7,6},{5,7},{3,5},{1,3},{8,9},{10,8},{12,1... | collective-permute-start | bytes 417800 | tf_op jit(solution)/shard_map/ppermute | solution.py:42
  163.9 25.8 %collective-permute-start.33 = (bf16[2,2,64,3072]{3,2,0,1:T(8,128)(2,1)S(1)}, bf16[2,2,64,3072]{3,2,0,1:T(8,128)(2,1)S(1)}, u32[]{:S(2)}, u32[]{:S(2)}) collective-permute-start(bf16[2,2,64,3072]{3,2,0,1:T(8,128)(2,1)S(1)} %pad_maximum_fusion.1), channel_id=1, source_target_pairs={{0,8},{8,0},{16,24},{24,16},{1,9},{9,1},{17,25},{25,17},{2,10},{10... | collective-permute-start | bytes 4718600 | tf_op jit(solution)/shard_map/ppermute | solution.py:106
  169.2 6.3 %collective-permute-start.59 = (bf16[32,2048]{1,0:T(8,128)(2,1)S(1)}, bf16[32,2048]{1,0:T(8,128)(2,1)S(1)}, u32[]{:S(2)}, u32[]{:S(2)}) collective-permute-start(bf16[32,2048]{1,0:T(8,128)(2,1)S(1)} %get-tuple-element.72.refs_11_), channel_id=1, source_target_pairs={{0,1},{2,0},{4,2},{6,4},{7,6},{5,7},{3,5},{1,3},{8,9},{10,8},{12,1... | collective-permute-start | bytes 393224 | tf_op jit(solution)/shard_map/ppermute | solution.py:42
  170.6 6.4 %collective-permute-start.42 = (bf16[32,2048]{1,0:T(8,128)(2,1)S(1)}, bf16[32,2048]{1,0:T(8,128)(2,1)S(1)}, u32[]{:S(2)}, u32[]{:S(2)}) collective-permute-start(bf16[32,2048]{1,0:T(8,128)(2,1)S(1)} %get-tuple-element.73.refs_4_), channel_id=1, source_target_pairs={{0,2},{2,4},{4,6},{6,7},{7,5},{5,3},{3,1},{1,0},{8,10},{10,12},{12... | collective-permute-start | bytes 393224 | tf_op jit(solution)/shard_map/ppermute | solution.py:42
  171.3 7.2 %collective-permute-start.56 = (bf16[32,2048]{1,0:T(8,128)(2,1)S(1)}, bf16[32,2048]{1,0:T(8,128)(2,1)S(1)}, u32[]{:S(2)}, u32[]{:S(2)}) collective-permute-start(bf16[32,2048]{1,0:T(8,128)(2,1)S(1)} %get-tuple-element.72.refs_11_), channel_id=1, source_target_pairs={{0,2},{2,4},{4,6},{6,7},{7,5},{5,3},{3,1},{1,0},{8,10},{10,12},{12... | collective-permute-start | bytes 393224 | tf_op jit(solution)/shard_map/ppermute | solution.py:42
  171.7 8.5 %collective-permute-start.46 = (bf16[32,2048]{1,0:T(8,128)(2,1)S(1)}, bf16[32,2048]{1,0:T(8,128)(2,1)S(1)}, u32[]{:S(2)}, u32[]{:S(2)}) collective-permute-start(bf16[32,2048]{1,0:T(8,128)(2,1)S(1)} %get-tuple-element.73.refs_4_), channel_id=1, source_target_pairs={{0,1},{2,0},{4,2},{6,4},{7,6},{5,7},{3,5},{1,3},{8,9},{10,8},{12,1... | collective-permute-start | bytes 393224 | tf_op jit(solution)/shard_map/ppermute | solution.py:42
  175.5 5.6 %collective-permute-start.60 = (bf16[32,2048]{1,0:T(8,128)(2,1)S(1)}, bf16[32,2048]{1,0:T(8,128)(2,1)S(1)}, u32[]{:S(2)}, u32[]{:S(2)}) collective-permute-start(bf16[32,2048]{1,0:T(8,128)(2,1)S(1)} %collective-permute-done.59.refs_12_), channel_id=1, source_target_pairs={{0,1},{2,0},{4,2},{6,4},{7,6},{5,7},{3,5},{1,3},{8,9},{10,8},{12,1... | collective-permute-start | bytes 393224 | tf_op jit(solution)/shard_map/ppermute | solution.py:42
  177.0 5.8 %collective-permute-start.43 = (bf16[32,2048]{1,0:T(8,128)(2,1)S(1)}, bf16[32,2048]{1,0:T(8,128)(2,1)S(1)}, u32[]{:S(2)}, u32[]{:S(2)}) collective-permute-start(bf16[32,2048]{1,0:T(8,128)(2,1)S(1)} %collective-permute-done.42.refs_3_), channel_id=1, source_target_pairs={{0,2},{2,4},{4,6},{6,7},{7,5},{5,3},{3,1},{1,0},{8,10},{10,12},{12... | collective-permute-start | bytes 393224 | tf_op jit(solution)/shard_map/ppermute | solution.py:42
  178.5 6.9 %collective-permute-start.57 = (bf16[32,2048]{1,0:T(8,128)(2,1)S(1)}, bf16[32,2048]{1,0:T(8,128)(2,1)S(1)}, u32[]{:S(2)}, u32[]{:S(2)}) collective-permute-start(bf16[32,2048]{1,0:T(8,128)(2,1)S(1)} %collective-permute-done.56.refs_10_), channel_id=1, source_target_pairs={{0,2},{2,4},{4,6},{6,7},{7,5},{5,3},{3,1},{1,0},{8,10},{10,12},{12... | collective-permute-start | bytes 393224 | tf_op jit(solution)/shard_map/ppermute | solution.py:42
  180.2 6.3 %collective-permute-start.47 = (bf16[32,2048]{1,0:T(8,128)(2,1)S(1)}, bf16[32,2048]{1,0:T(8,128)(2,1)S(1)}, u32[]{:S(2)}, u32[]{:S(2)}) collective-permute-start(bf16[32,2048]{1,0:T(8,128)(2,1)S(1)} %collective-permute-done.46.refs_5_), channel_id=1, source_target_pairs={{0,1},{2,0},{4,2},{6,4},{7,6},{5,7},{3,5},{1,3},{8,9},{10,8},{12,1... | collective-permute-start | bytes 393224 | tf_op jit(solution)/shard_map/ppermute | solution.py:42
  181.1 6.6 %collective-permute-start.61 = (bf16[32,2048]{1,0:T(8,128)(2,1)S(1)}, bf16[32,2048]{1,0:T(8,128)(2,1)S(1)}, u32[]{:S(2)}, u32[]{:S(2)}) collective-permute-start(bf16[32,2048]{1,0:T(8,128)(2,1)S(1)} %collective-permute-done.60.refs_13_), channel_id=1, source_target_pairs={{0,1},{2,0},{4,2},{6,4},{7,6},{5,7},{3,5},{1,3},{8,9},{10,8},{12,1... | collective-permute-start | bytes 393224 | tf_op jit(solution)/shard_map/ppermute | solution.py:42
  182.8 5.8 %collective-permute-start.44 = (bf16[32,2048]{1,0:T(8,128)(2,1)S(1)}, bf16[32,2048]{1,0:T(8,128)(2,1)S(1)}, u32[]{:S(2)}, u32[]{:S(2)}) collective-permute-start(bf16[32,2048]{1,0:T(8,128)(2,1)S(1)} %collective-permute-done.43.refs_2_), channel_id=1, source_target_pairs={{0,2},{2,4},{4,6},{6,7},{7,5},{5,3},{3,1},{1,0},{8,10},{10,12},{12... | collective-permute-start | bytes 393224 | tf_op jit(solution)/shard_map/ppermute | solution.py:42
  187.7 5.2 %collective-permute-start.62 = (bf16[32,2048]{1,0:T(8,128)(2,1)S(1)}, bf16[32,2048]{1,0:T(8,128)(2,1)S(1)}, u32[]{:S(2)}, u32[]{:S(2)}) collective-permute-start(bf16[32,2048]{1,0:T(8,128)(2,1)S(1)} %collective-permute-done.61.refs_14_), channel_id=1, source_target_pairs={{0,1},{2,0},{4,2},{6,4},{7,6},{5,7},{3,5},{1,3},{8,9},{10,8},{12,1... | collective-permute-start | bytes 393224 | tf_op jit(solution)/shard_map/ppermute | solution.py:42
  (41 other events, 327.4 us)

commit v8 on v6

--- a/solution.py
+++ b/solution.py
@@ -131,79 +131,93 @@
         out_ref[pl.ds(start, tile), :] = block.T.astype(BF16)
 
 
-def project_kernel(count, index_ref, factor_ref, gain_ref, weight_ref, *refs):
-    blocks, refs = refs[:count], refs[count:]
-    logits_refs, piece_refs = refs[:CORES], refs[CORES:-5]
-    raw_ref, normed_ref, turned_ref, held_ref, sems = refs[-5:]
+def hold_kernel(weight_ref, held_ref, sems):
+    tile = weight_ref.shape[0] // sems.shape[0]
+    copies = [
+        pltpu.make_async_copy(
+            weight_ref.at[pl.ds(n * tile, tile), :], held_ref.at[pl.ds(n * tile, tile), :], sems.at[n]
+        )
+        for n in range(sems.shape[0])
+    ]
+    for copy in copies:
+        copy.start()
+    for copy in copies:
+        copy.wait()
+
+
+def hold(weight):
+    return pl.pallas_call(
+        hold_kernel,
+        in_specs=[pl.BlockSpec(memory_space=pltpu.HBM)],
+        out_specs=VMEM,
+        out_shape=jax.ShapeDtypeStruct(weight.shape, weight.dtype),
+        scratch_shapes=[pltpu.SemaphoreType.DMA((4,))],
+        compiler_params=pltpu.CompilerParams(vmem_limit_bytes=12 * 2**20),
+        cost_estimate=pl.CostEstimate(flops=0, bytes_accessed=2 * weight.size, transcendentals=0),
+    )(weight)
+
+
+def project_kernel(count, tile, index_ref, factor_ref, gain_ref, weight_ref, *refs):
+    blocks, refs = refs[: CHUNKS * count], refs[CHUNKS * count :]
+    keep_ref, send_ref = refs[:CORES]
+    piece_refs = refs[CORES : CORES + CHUNKS]
+    raw_ref, normed_ref, turned_ref = refs[CORES + CHUNKS :]
     rows, width = blocks[0].shape
+    group_rows = CHUNKS * rows
+    piece = piece_refs[0].shape[0]
+    half = keep_ref.shape[0]
     step = pl.program_id(0)
-    tiles, tile = held_ref.shape[:2]
-    piece = piece_refs[0].shape[0]
-    half = logits_refs[0].shape[0]
-
-    def fetch(n):
-        return pltpu.make_async_copy(
-            weight_ref.at[pl.ds(n * tile, tile), :], held_ref.at[n], sems.at[n]
-        )
 
     @pl.when(step == 0)
     def _():
-        for n in range(tiles):
-            fetch(n).start()
         for k, ref in enumerate(blocks):
-            start = pl.multiple_of(index_ref[k] * rows, rows)
-            column = pl.multiple_of(index_ref[count + k] * width, width)
+            h, at = k // count, k + k // count * count
+            start = pl.multiple_of(index_ref[at] * group_rows + h * rows, rows)
+            column = pl.multiple_of(index_ref[at + count] * width, width)
             raw_ref[pl.ds(start, rows), pl.ds(column, width)] = ref[...]
         for g in range(factor_ref.shape[0]):
-            group = pl.ds(g * rows, rows)
+            group = pl.ds(g * group_rows, group_rows)
             normed_ref[group, :] = (
                 raw_ref[group, :].astype(F32) * factor_ref[g] * gain_ref[...]
             ).astype(BF16)
+        transpose_into(turned_ref, normed_ref)
         for h, ref in enumerate(piece_refs):
-            start = pl.multiple_of(index_ref[2 * count + h] * piece, piece)
+            start = pl.multiple_of(index_ref[2 * CHUNKS * count + h] * piece, piece)
             ref[...] = raw_ref[pl.ds(start, piece), :]
-        transpose_into(turned_ref, normed_ref)
-
-    fetch(step).wait()
-    logits = jnp.dot(held_ref[step], turned_ref[...], preferred_element_type=F32).T
-    for k, ref in enumerate(logits_refs):
-        ref[...] = logits[k * half : (k + 1) * half]
+
+    rows = pl.ds(pl.multiple_of(step * tile, tile), tile)
+    logits = jnp.dot(weight_ref[rows, :], turned_ref[...], preferred_element_type=F32).T
+    keep_ref[...] = logits[:half]
+    send_ref[...] = logits[half:]
 
 
 def project(index, blocks, factor, gain, weight, piece_rows):
     vocab, depth = weight.shape
-    all_rows = factor.shape[0] * blocks[0].shape[0]
+    all_rows = factor.shape[0] * factor.shape[1]
     half = all_rows // CORES
     tile = min(vocab, 512)
     out = jax.ShapeDtypeStruct((half, vocab), F32)
     piece = jax.ShapeDtypeStruct((piece_rows, depth), BF16)
     return pl.pallas_call(
-        functools.partial(project_kernel, len(blocks)),
+        functools.partial(project_kernel, len(blocks[0]), tile),
         grid=(vocab // tile,),
-        in_specs=[SMEM, VMEM, VMEM, pl.BlockSpec(memory_space=pltpu.HBM)]
-        + [VMEM] * len(blocks),
+        in_specs=[SMEM] + [VMEM] * (3 + CHUNKS * len(blocks[0])),
         out_specs=[pl.BlockSpec((half, tile), lambda n: (0, n))] * CORES
         + [pl.BlockSpec((piece_rows, depth), lambda n: (0, 0))] * CHUNKS,
         out_shape=[out] * CORES + [piece] * CHUNKS,
-        scratch_shapes=[
-            pltpu.VMEM((all_rows, depth), BF16),
-            pltpu.VMEM((all_rows, depth), BF16),
-            pltpu.VMEM((depth, all_rows), BF16),
-            pltpu.VMEM((vocab // tile, tile, depth), BF16),
-            pltpu.SemaphoreType.DMA((vocab // tile,)),
-        ],
-        compiler_params=pltpu.CompilerParams(vmem_limit_bytes=48 * 2**20),
+        scratch_shapes=[pltpu.VMEM((all_rows, depth), BF16)] * 2
+        + [pltpu.VMEM((depth, all_rows), BF16)],
+        compiler_params=pltpu.CompilerParams(vmem_limit_bytes=28 * 2**20),
         cost_estimate=pl.CostEstimate(
             flops=2 * all_rows * depth * vocab,
             bytes_accessed=2 * vocab * depth + all_rows * (2 * depth + 4 * vocab),
             transcendentals=0,
         ),
-    )(index, factor, gain, weight, *blocks)
-
-
-def back_kernel(piece, index_ref, mine_ref, other_ref, weight_ref, out_ref, grad_ref):
+    )(index, factor, gain, weight, *[x for chunk in blocks for x in chunk])
+
+
+def back_kernel(piece, tile, index_ref, mine_ref, other_ref, weight_ref, out_ref, grad_ref):
     vocab = weight_ref.shape[0]
-    tile = weight_ref.shape[1]
     half = mine_ref.shape[0]
     depth = out_ref.shape[1] - LANES
     step = pl.program_id(0)
@@ -217,7 +231,9 @@
             out_ref[rows, pl.ds(depth, LANES)] = ref[pl.ds(first, piece), vocab:].astype(F32)
 
     columns = pl.ds(pl.multiple_of(step * tile, tile), tile)
-    out_ref[:, columns] = jnp.dot(grad_ref[...], weight_ref[...], preferred_element_type=F32)
+    out_ref[:, columns] = jnp.dot(
+        grad_ref[...], weight_ref[:, columns], preferred_element_type=F32
+    )
 
 
 def back(index, mine, other, weight, piece_rows):
@@ -225,9 +241,9 @@
     all_rows = mine.shape[0] + other.shape[0]
     tile = min(depth, 512)
     return pl.pallas_call(
-        functools.partial(back_kernel, piece_rows),
+        functools.partial(back_kernel, piece_rows, tile),
         grid=(depth // tile,),
-        in_specs=[SMEM, VMEM, VMEM, pl.BlockSpec((vocab, tile), lambda n: (0, n))],
+        in_specs=[SMEM, VMEM, VMEM, VMEM],
         out_specs=pl.BlockSpec((all_rows, depth + LANES), lambda n: (0, 0)),
         out_shape=jax.ShapeDtypeStruct((all_rows, depth + LANES), F32),
         scratch_shapes=[pltpu.VMEM((all_rows, vocab), BF16)],
@@ -300,13 +316,18 @@
     for g in range(groups.size):
         for v in range(parts):
             p = ring.place[v]
-            held = [ring.order[q] for q in ring.sources(v, 0)]
-            group = [i // slots % groups.chips * CORES + i // slots // groups.chips for i in held]
-            add("place", [groups.entry(g, i) for i in group] + [i % slots for i in held])
+            place = []
+            for h in range(CHUNKS):
+                held = [ring.order[q] for q in ring.sources(v, h)]
+                for i in held:
+                    group = i // slots % groups.chips * CORES + i // slots // groups.chips
+                    place.append(groups.entry(g, group))
+                place += [i % slots for i in held]
             for h in range(CHUNKS):
                 start = p * piece_rows
                 start = start // chunk_rows * group_rows + h * chunk_rows + start % chunk_rows
-                table["place"][-1].append(start // piece_rows)
+                place.append(start // piece_rows)
+            add("place", place)
             entry = groups.entry(g, v * share_rows // group_rows)
             first = v * share_rows % group_rows
             start = first // chunk_rows * step_rows + entry * chunk_rows + first % chunk_rows
@@ -366,19 +387,24 @@
     ]
     turned = lax.ppermute(hidden, ("dp", "vocab"), turn)
 
+    weight = hold(head_weight)
+
     live_rows = (valid_rows == 1).astype(F32)
     squares = jnp.sum(jnp.square(hidden.astype(F32)), axis=1)[None]
     rounds = ring.meetings(lambda terms: sum(terms[1:], terms[0]))
     rounds.append(lambda x: groups.gather_chips(jnp.concatenate([x, live_rows[None]])))
     rounds.append(lambda x: jnp.concatenate([x, groups.swap(x)], axis=0))
-    exchanged = [rounds[0](squares)]
-    late = rounds[1:]
+    for round in rounds[:2]:
+        squares = round(squares)
+    turned = after(turned, squares, weight)
+    late = rounds[2:]
+    exchanged = [squares]
 
     def seen(step, arrivals):
         if step < len(late):
             exchanged.append(late[step](after(exchanged[-1], arrivals)))
 
-    blocks = ring.gather(turned, 0, seen)
+    blocks = [ring.gather(chunk(turned, h), h, seen if h == 0 else None) for h in range(CHUNKS)]
     both = exchanged[-1]
     valid_count = jnp.sum(both[:, 1])
     row_factor = lax.rsqrt(both[:, 0] / model_width + 1e-05)
@@ -399,13 +425,16 @@
     lane = lax.broadcasted_iota(jnp.uint32, (chunk_rows, LANES), 1)
 
     keep, send, *pieces = project(
-        index["place"], blocks, row_factor[:, :, None], gain, head_weight, piece_rows
+        index["place"], blocks, row_factor[:, :, None], gain, weight, piece_rows
     )
-    summed = (keep + groups.swap(send)).reshape(groups.chips, group_rows, vocab_width)
-    logits = summed[0]
-    for d in range(1, groups.chips):
-        logits = logits + groups.shift(summed[d], d)
-
+    other = groups.swap(send)
+
+    def chip_sum(d):
+        rows = slice(d * group_rows, (d + 1) * group_rows)
+        return keep[rows] + other[rows]
+
+    came = [groups.shift(chip_sum(d), d) for d in range(1, groups.chips)]
+    logits = sum(came, chip_sum(0))
     top = jnp.max(logits, axis=1)
     total = jnp.sum(jnp.exp(logits - top[:, None]), axis=1)
     mine = jnp.stack([jnp.concatenate([top, target_top]), jnp.concatenate([total, target_total])])
@@ -431,12 +460,14 @@
             lane == own_lane + 1, dot_low[:, None], 0.0
         )
         message = jnp.concatenate([logit_grad.astype(BF16), lanes.astype(BF16)], axis=1)
-        everyone = groups.gather_halves(message)
+        if h > 0:
+            message = after(message, mine)
+        mine = groups.gather_chips(message)
+        mine, other = [x.reshape(step_rows // CORES, -1) for x in (mine, groups.swap(mine))]
+        normed_grad = back(index["turn"], mine, other, weight, piece_rows)
         if h == CHUNKS - 1:
-            chosen = groups.gather(after(own_chosen, everyone).reshape(CHUNKS, chunk_rows, -1))
-            chosen = chosen.transpose(1, 0, 2, 3).reshape(CHUNKS * step_rows, -1)
-        mine, other = [x.reshape(step_rows // CORES, -1) for x in everyone]
-        normed_grad = back(index["turn"], mine, other, head_weight, piece_rows)
+            chosen = after(own_chosen, normed_grad).reshape(CHUNKS, chunk_rows, -1)
+            chosen = groups.gather(chosen).transpose(1, 0, 2, 3).reshape(CHUNKS * step_rows, -1)
 
         def part(t):
             first = t % parts * piece_rows

time: 202 us -> 223 us (1.10)
  local copies, waits for them, and re-layouts: 6.41 us -> 40.5 us
  waiting for transfers between devices: 84.9 us -> 75.1 us
  starting transfers between devices: 66.1 us -> 63.4 us
    unnamed x17 -> x87, local copies, waits for them, and re-layouts: 0.04 us -> 36 us
    ppermute x35 -> x42, waiting for transfers between devices: 48.3 us -> 37 us  [shift(): lax.ppermute(x, 'vocab', [(order[p], order[(p + step) % size]) for p in r...]
    ppermute x5, starting transfers between devices: 8.68 us -> 3.88 us  [shift(): lax.ppermute(x, 'dp', [(i, (i + CORES * step) % size) for i in range(size)])]
    pallas_call x3 -> x4, Pallas kernels: 17 us -> 15.2 us  [the longest x1 7.55 us: project(): pl.pallas_call(functools.partial(project_kernel, len(blocks[0]), tile), g...]
    ppermute x35 -> x42, starting transfers between devices: 42.9 us -> 43.9 us  [shift(): lax.ppermute(x, 'vocab', [(order[p], order[(p + step) % size]) for p in r...]
  transfers between devices with their start and end apart: 54 -> 61, of which waited for: 32 -> 31; matrix products, arithmetic and copies ran while one was open for 7% -> 6% of each run, Pallas kernels for 4% -> 3%
where the time goes in v8:
time: 223 us; the launch traced here: 222 us
  waiting for transfers between devices  75.1 us (34%)
  starting transfers between devices  63.4 us (28%)
  local copies, waits for them, and re-layouts  40.5 us (18%)
  Pallas kernels  27.8 us (12%)
  other arithmetic  13.4 us (6%)
    ppermute x42, starting transfers between devices, shift(): lax.ppermute(x, 'vocab', [(order[p], order[(p + step) % size]) for p in r...  43.9 us
    ppermute x42, waiting for transfers between devices, shift(): lax.ppermute(x, 'vocab', [(order[p], order[(p + step) % size]) for p in r...  37 us
    unnamed x87, local copies, waits for them, and re-layouts  36 us
    ppermute x5, waiting for transfers between devices, shift(): lax.ppermute(x, 'dp', [(i, (i + CORES * step) % size) for i in range(size)])  27.1 us
    ppermute x8, starting transfers between devices, partner(): return lax.ppermute(x, 'vocab', [(v, v ^ bit) for v in range(self.size)])  13.6 us
    pallas_call x1, Pallas kernels, outer(): pl.pallas_call(functools.partial(outer_kernel, len(chunks[0]), tile), gri...  12.6 us
    pallas_call x1, Pallas kernels, project(): pl.pallas_call(functools.partial(project_kernel, len(blocks[0]), tile), g...  7.55 us
    pallas_call x2, Pallas kernels, back(): pl.pallas_call(functools.partial(back_kernel, piece_rows, tile), grid=(de...  7.09 us
  transfers between devices with their start and end apart: 61, of which 31 were waited for; matrix products, arithmetic and copies ran while one was open for 6% of the time, Pallas kernels for 3%

profile of v8, /device:TPU:0, one launch (start us, length us, event | category | flops | bytes accessed | tf_op | source)
XLA Modules:
  0.0 222.0 jit_solution(15135659505864102886)
XLA Ops:
  0.6 1.7 collective-permute-start.4
  3.5 3.0 %collective-permute-start = (f32[1,128]{1,0:T(1,128)S(1)}, f32[1,128]{1,0:T(1,128)S(1)}, u32[]{:S(2)}, u32[]{:S(2)}) collective-permute-start(f32[1,128]{1,0:T(1,128)S(1)} %bitcast.88), channel_id=1, source_target_pairs={{0,1},{1,0},{2,3},{3,2},{4,5},{5,4},{6,7},{7,6},{8,9},{9,8},{10,11... | collective-permute-start | bytes 1544 | tf_op jit(solution)/shard_map/ppermute | solution.py:47
  8.0 5.0 %collective-permute-start.3 = (f32[1,128]{1,0:T(1,128)S(1)}, f32[1,128]{1,0:T(1,128)S(1)}, u32[]{:S(2)}, u32[]{:S(2)}) collective-permute-start(f32[1,128]{1,0:T(1,128)S(1)} %bitcast_add_fusion), channel_id=1, source_target_pairs={{0,6},{1,7},{2,4},{3,5},{4,2},{5,3},{6,0},{7,1},{8,14},{9,15},{10,... | collective-permute-start | bytes 1544 | tf_op jit(solution)/shard_map/ppermute | solution.py:47
  13.6 3.4 %copy-done.5 = bf16[2048,2048]{1,0:T(8,128)(2,1)S(1)} copy-done((bf16[2048,2048]{1,0:T(8,128)(2,1)S(1)}, bf16[2048,2048]{1,0:T(8,128)(2,1)}, u32[]{:S(2)}) %copy-start.5) | copy-done | bytes 8388632
  17.6 3.4 %copy-done.2 = bf16[2048,2048]{1,0:T(8,128)(2,1)} copy-done((bf16[2048,2048]{1,0:T(8,128)(2,1)}, bf16[2048,2048]{1,0:T(8,128)(2,1)S(1)}, u32[]{:S(2)}) %copy-start.2) | copy-done | bytes 8388632
  21.1 1.6 collective-permute-start.6
  23.1 1.5 collective-permute-start.17
  25.2 2.3 %collective-permute-done.6.refs_5_ = bf16[64,1024]{1,0:T(8,128)(2,1)S(1)} collective-permute-done((bf16[64,1024]{1,0:T(8,128)(2,1)S(1)}, bf16[64,1024]{1,0:T(8,128)(2,1)S(1)}, u32[]{:S(2)}, u32[]{:S(2)}) %collective-permute-start.6) | collective-permute-done | bytes 131104 | tf_op jit(solution)/shard_map/ppermute | solution.py:42
  27.4 1.6 collective-permute-done.5.refs_3_
  29.0 2.7 %collective-permute-start.7 = (f32[2,128]{1,0:T(2,128)S(1)}, f32[2,128]{1,0:T(2,128)S(1)}, u32[]{:S(2)}, u32[]{:S(2)}) collective-permute-start(f32[2,128]{1,0:T(2,128)S(1)} %get-tuple-element.75), channel_id=1, source_target_pairs={{0,16},{8,24},{16,0},{24,8},{1,17},{9,25},{17,1},{25,9},{2,18},{10... | collective-permute-start | bytes 3080 | tf_op jit(solution)/shard_map/ppermute | solution.py:110
  31.7 2.0 collective-permute-start.8
  35.1 1.4 dynamic_slice.13
  36.5 2.0 collective-permute-start.15
  40.5 1.5 collective-permute-start.19
  43.4 2.0 collective-permute-start.16
  46.9 1.5 collective-permute-start.20
  54.7 3.4 %copy-done.3 = bf16[2048,2048]{1,0:T(8,128)(2,1)S(1)} copy-done((bf16[2048,2048]{1,0:T(8,128)(2,1)S(1)}, bf16[2048,2048]{1,0:T(8,128)(2,1)}, u32[]{:S(2)}) %copy-start.3) | copy-done | bytes 8388632
  70.7 7.5 %shard_map.96 = (f32[256,2048]{1,0:T(8,128)S(1)}, f32[256,2048]{1,0:T(8,128)S(1)}, bf16[32,2048]{1,0:T(8,128)(2,1)S(1)}, bf16[32,2048]{1,0:T(8,128)(2,1)S(1)}) custom-call(s32[34]{0:T(128)S(1)} %slice_bitcast_fusion.index_ref, f32[4,128,1]{2,1,0:T(8,128)S(1)} %copy.13.factor_ref, f32[1,2048]{1,0:T(1,128)S(1)} %bitcast.63, bf16[2048,2048]{1,0:T(8,128)(2,1)S(1)} %copy-done.3, ...), custom_call_target="tpu_custom_call" | custom-call | flops 4294967296 | bytes 14680064 | tf_op jit(solution)/shard_map/pallas_call | solution.py:201
  78.9 4.2 %collective-permute-done.21 = f32[256,2048]{1,0:T(8,128)S(1)} collective-permute-done((f32[256,2048]{1,0:T(8,128)S(1)}, f32[256,2048]{1,0:T(8,128)S(1)}, u32[]{:S(2)}, u32[]{:S(2)}) %collective-permute-start.21) | collective-permute-done | bytes 2097184 | tf_op jit(solution)/shard_map/ppermute | solution.py:106
  86.9 1.5 fusion.52
  89.1 22.0 %collective-permute-done.22 = f32[128,2048]{1,0:T(8,128)} collective-permute-done((f32[128,2048]{1,0:T(8,128)}, f32[128,2048]{1,0:T(8,128)}, u32[]{:S(2)}, u32[]{:S(2)}) %collective-permute-start.22) | collective-permute-done | bytes 1048608 | tf_op jit(solution)/shard_map/ppermute | solution.py:110
  111.1 1.8 fusion.48
  114.0 3.0 %collective-permute-done.23 = f32[2,256]{1,0:T(2,128)S(1)} collective-permute-done((f32[2,256]{1,0:T(2,128)S(1)}, f32[2,256]{1,0:T(2,128)S(1)}, u32[]{:S(2)}, u32[]{:S(2)}) %collective-permute-start.23) | collective-permute-done | bytes 2080 | tf_op jit(solution)/shard_map/ppermute | solution.py:47
  119.2 2.4 %collective-permute-start.24 = (f32[2,256]{1,0:T(2,128)S(1)}, f32[2,256]{1,0:T(2,128)S(1)}, u32[]{:S(2)}, u32[]{:S(2)}) collective-permute-start(f32[2,256]{1,0:T(2,128)S(1)} %pad_maximum_fusion.8), channel_id=1, source_target_pairs={{0,2},{1,3},{2,0},{3,1},{4,6},{5,7},{6,4},{7,5},{8,10},{9,11},{10,... | collective-permute-start | bytes 6152 | tf_op jit(solution)/shard_map/ppermute | solution.py:47
  125.8 5.1 %collective-permute-done.27 = bf16[64,2176]{1,0:T(8,128)(2,1)S(1)} collective-permute-done((bf16[64,2176]{1,0:T(8,128)(2,1)S(1)}, bf16[64,2176]{1,0:T(8,128)(2,1)S(1)}, u32[]{:S(2)}, u32[]{:S(2)}) %collective-permute-start.27) | collective-permute-done | bytes 278560 | tf_op jit(solution)/shard_map/ppermute | solution.py:110
  131.5 1.5 collective-permute-done.32
  133.0 3.4 %copy-done.4 = bf16[2048,2048]{1,0:T(8,128)(2,1)S(1)} copy-done((bf16[2048,2048]{1,0:T(8,128)(2,1)S(1)}, bf16[2048,2048]{1,0:T(8,128)(2,1)}, u32[]{:S(2)}) %copy-start.4) | copy-done | bytes 8388632
  136.4 3.5 %shard_map.98 = f32[256,2176]{1,0:T(8,128)S(1)} custom-call(s32[8]{0:T(128)S(1)} %slice_bitcast_fusion.1.index_ref, bf16[128,2176]{1,0:T(8,128)(2,1)S(1)} %bitcast.60, bf16[128,2176]{1,0:T(8,128)(2,1)S(1)} %bitcast.62, bf16[2048,2048]{1,0:T(8,128)(2,1)S(1)} %copy-done.4), custom_call_target="tpu_custom_call" | custom-call | flops 2147483648 | bytes 11534336 | tf_op jit(solution)/shard_map/pallas_call | solution.py:243
  140.1 2.1 collective-permute-start.33
  142.4 3.5 %collective-permute-done.33 = bf16[32,2176]{1,0:T(8,128)(2,1)S(1)} collective-permute-done((bf16[32,2176]{1,0:T(8,128)(2,1)S(1)}, bf16[32,2176]{1,0:T(8,128)(2,1)S(1)}, u32[]{:S(2)}, u32[]{:S(2)}) %collective-permute-start.33) | collective-permute-done | bytes 139296 | tf_op jit(solution)/shard_map/ppermute | solution.py:42
  145.9 2.1 collective-permute-start.34
  148.0 3.5 %shard_map.97 = f32[256,2176]{1,0:T(8,128)S(1)} custom-call(s32[8]{0:T(128)S(1)} %slice_bitcast_fusion.1.index_ref, bf16[128,2176]{1,0:T(8,128)(2,1)S(1)} %bitcast.59, bf16[128,2176]{1,0:T(8,128)(2,1)S(1)} %bitcast.61, bf16[2048,2048]{1,0:T(8,128)(2,1)S(1)} %copy-done.4), custom_call_target="tpu_custom_call" | custom-call | flops 2147483648 | bytes 11534336 | tf_op jit(solution)/shard_map/pallas_call | solution.py:243
  153.7 1.5 collective-permute-start.50
  155.2 3.2 %collective-permute-done.35 = bf16[32,2176]{1,0:T(8,128)(2,1)S(1)} collective-permute-done((bf16[32,2176]{1,0:T(8,128)(2,1)S(1)}, bf16[32,2176]{1,0:T(8,128)(2,1)S(1)}, u32[]{:S(2)}, u32[]{:S(2)}) %collective-permute-start.35) | collective-permute-done | bytes 139296 | tf_op jit(solution)/shard_map/ppermute | solution.py:42
  159.1 1.4 collective-permute-start.38
  162.1 3.3 %collective-permute-done.38 = bf16[32,2176]{1,0:T(8,128)(2,1)S(1)} collective-permute-done((bf16[32,2176]{1,0:T(8,128)(2,1)S(1)}, bf16[32,2176]{1,0:T(8,128)(2,1)S(1)}, u32[]{:S(2)}, u32[]{:S(2)}) %collective-permute-start.38) | collective-permute-done | bytes 139296 | tf_op jit(solution)/shard_map/ppermute | solution.py:42
  168.2 1.4 collective-permute-start.51
  171.0 2.6 %collective-permute-done.51 = bf16[32,2176]{1,0:T(8,128)(2,1)S(1)} collective-permute-done((bf16[32,2176]{1,0:T(8,128)(2,1)S(1)}, bf16[32,2176]{1,0:T(8,128)(2,1)S(1)}, u32[]{:S(2)}, u32[]{:S(2)}) %collective-permute-start.51) | collective-permute-done | bytes 139296 | tf_op jit(solution)/shard_map/ppermute | solution.py:42
  176.3 2.4 %collective-permute-done.52 = bf16[32,2176]{1,0:T(8,128)(2,1)S(1)} collective-permute-done((bf16[32,2176]{1,0:T(8,128)(2,1)S(1)}, bf16[32,2176]{1,0:T(8,128)(2,1)S(1)}, u32[]{:S(2)}, u32[]{:S(2)}) %collective-permute-start.52) | collective-permute-done | bytes 139296 | tf_op jit(solution)/shard_map/ppermute | solution.py:42
  178.7 1.5 collective-permute-start.53
  180.5 3.5 %collective-permute-done.53 = bf16[32,2176]{1,0:T(8,128)(2,1)S(1)} collective-permute-done((bf16[32,2176]{1,0:T(8,128)(2,1)S(1)}, bf16[32,2176]{1,0:T(8,128)(2,1)S(1)}, u32[]{:S(2)}, u32[]{:S(2)}) %collective-permute-start.53) | collective-permute-done | bytes 139296 | tf_op jit(solution)/shard_map/ppermute | solution.py:42
  189.8 2.2 collective-permute-done.57.refs_12_
  195.1 1.6 collective-permute-start.55
  199.8 1.6 collective-permute-done.55.refs_9_
  201.4 1.5 collective-permute-start.56
  204.5 1.7 collective-permute-start.43
  207.9 1.4 collective-permute-done.60.refs_15_
  209.5 12.6 %shard_map.99 = (f32[2048,3072]{1,0:T(8,128)}, bf16[64,2048]{1,0:T(8,128)(2,1)}) custom-call(s32[17]{0:T(128)S(1)} %slice_bitcast_fusion.2.index_ref, bf16[512,3072]{1,0:T(8,128)(2,1)S(1)} %bitcast.58, bf16[32,2048]{1,0:T(8,128)(2,1)S(1)} %collective-permute-done.43.refs_0_, bf16[32,2048]{1,0:T(8,128)(2,1)S(1)} %collective-permute-done.42.refs_1_, ...), custom_call_target="tpu_custom_call" | custom-call | flops 6442450944 | bytes 30408704 | tf_op jit(solution)/shard_map/pallas_call | solution.py:284
  (236 shorter events, 69.7 us)
Async XLA Ops:
  0.6 20.4 %collective-permute-start.4 = (bf16[128,1024]{1,0:T(8,128)(2,1)}, bf16[128,1024]{1,0:T(8,128)(2,1)S(1)}, u32[]{:S(2)}, u32[]{:S(2)}) collective-permute-start(bf16[128,1024]{1,0:T(8,128)(2,1)} %param.8), channel_id=1, source_target_pairs={{0,0},{1,1},{2,8},{3,9},{4,16},{5,17},{6,24},{7,25},{8,4},{9,5},{1... | collective-permute-start | bytes 786440 | tf_op jit(solution)/shard_map/ppermute | solution.py:388
  8.0 13.0 %collective-permute-start.3 = (f32[1,128]{1,0:T(1,128)S(1)}, f32[1,128]{1,0:T(1,128)S(1)}, u32[]{:S(2)}, u32[]{:S(2)}) collective-permute-start(f32[1,128]{1,0:T(1,128)S(1)} %bitcast_add_fusion), channel_id=1, source_target_pairs={{0,6},{1,7},{2,4},{3,5},{4,2},{5,3},{6,0},{7,1},{8,14},{9,15},{10,... | collective-permute-start | bytes 1544 | tf_op jit(solution)/shard_map/ppermute | solution.py:47
  13.0 8.0 %collective-permute-start.2 = (f32[1,128]{1,0:T(1,128)S(1)}, f32[1,128]{1,0:T(1,128)S(1)}, u32[]{:S(2)}, u32[]{:S(2)}) collective-permute-start(f32[1,128]{1,0:T(1,128)S(1)} %bitcast_add_fusion), channel_id=1, source_target_pairs={{0,4},{1,5},{2,6},{3,7},{4,0},{5,1},{6,2},{7,3},{8,12},{9,13},{10,... | collective-permute-start | bytes 1544 | tf_op jit(solution)/shard_map/ppermute | solution.py:47
  13.0 8.0 %collective-permute-start.1 = (f32[1,128]{1,0:T(1,128)S(1)}, f32[1,128]{1,0:T(1,128)S(1)}, u32[]{:S(2)}, u32[]{:S(2)}) collective-permute-start(f32[1,128]{1,0:T(1,128)S(1)} %bitcast_add_fusion), channel_id=1, source_target_pairs={{0,2},{1,3},{2,0},{3,1},{4,6},{5,7},{6,4},{7,5},{8,10},{9,11},{10,... | collective-permute-start | bytes 1544 | tf_op jit(solution)/shard_map/ppermute | solution.py:47
  21.1 6.4 %collective-permute-start.6 = (bf16[64,1024]{1,0:T(8,128)(2,1)S(1)}, bf16[64,1024]{1,0:T(8,128)(2,1)S(1)}, u32[]{:S(2)}, u32[]{:S(2)}) collective-permute-start(bf16[64,1024]{1,0:T(8,128)(2,1)S(1)} %get-tuple-element.51.refs_4_), channel_id=1, source_target_pairs={{0,1},{2,0},{4,2},{6,4},{7,6},{5,7},{3,5},{1,3},{8,9},{10,8},{12,1... | collective-permute-start | bytes 393224 | tf_op jit(solution)/shard_map/ppermute | solution.py:42
  22.6 6.4 %collective-permute-start.5 = (bf16[64,1024]{1,0:T(8,128)(2,1)S(1)}, bf16[64,1024]{1,0:T(8,128)(2,1)S(1)}, u32[]{:S(2)}, u32[]{:S(2)}) collective-permute-start(bf16[64,1024]{1,0:T(8,128)(2,1)S(1)} %get-tuple-element.51.refs_4_), channel_id=1, source_target_pairs={{0,2},{2,4},{4,6},{6,7},{7,5},{5,3},{3,1},{1,0},{8,10},{10,12},{12... | collective-permute-start | bytes 393224 | tf_op jit(solution)/shard_map/ppermute | solution.py:42
  23.1 10.6 %collective-permute-start.17 = (bf16[64,1024]{1,0:T(8,128)(2,1)S(1)}, bf16[64,1024]{1,0:T(8,128)(2,1)S(1)}, u32[]{:S(2)}, u32[]{:S(2)}) collective-permute-start(bf16[64,1024]{1,0:T(8,128)(2,1)S(1)} %get-tuple-element.50.refs_11_), channel_id=1, source_target_pairs={{0,1},{2,0},{4,2},{6,4},{7,6},{5,7},{3,5},{1,3},{8,9},{10,8},{12,1... | collective-permute-start | bytes 393224 | tf_op jit(solution)/shard_map/ppermute | solution.py:42
  24.7 11.9 %collective-permute-start.14 = (bf16[64,1024]{1,0:T(8,128)(2,1)S(1)}, bf16[64,1024]{1,0:T(8,128)(2,1)S(1)}, u32[]{:S(2)}, u32[]{:S(2)}) collective-permute-start(bf16[64,1024]{1,0:T(8,128)(2,1)S(1)} %get-tuple-element.50.refs_11_), channel_id=1, source_target_pairs={{0,2},{2,4},{4,6},{6,7},{7,5},{5,3},{3,1},{1,0},{8,10},{10,12},{12... | collective-permute-start | bytes 393224 | tf_op jit(solution)/shard_map/ppermute | solution.py:42
  29.0 10.2 %collective-permute-start.7 = (f32[2,128]{1,0:T(2,128)S(1)}, f32[2,128]{1,0:T(2,128)S(1)}, u32[]{:S(2)}, u32[]{:S(2)}) collective-permute-start(f32[2,128]{1,0:T(2,128)S(1)} %get-tuple-element.75), channel_id=1, source_target_pairs={{0,16},{8,24},{16,0},{24,8},{1,17},{9,25},{17,1},{25,9},{2,18},{10... | collective-permute-start | bytes 3080 | tf_op jit(solution)/shard_map/ppermute | solution.py:110
  31.7 7.5 %collective-permute-start.9 = (bf16[64,1024]{1,0:T(8,128)(2,1)S(1)}, bf16[64,1024]{1,0:T(8,128)(2,1)S(1)}, u32[]{:S(2)}, u32[]{:S(2)}) collective-permute-start(bf16[64,1024]{1,0:T(8,128)(2,1)S(1)} %collective-permute-done.6.refs_5_), channel_id=1, source_target_pairs={{0,1},{2,0},{4,2},{6,4},{7,6},{5,7},{3,5},{1,3},{8,9},{10,8},{12,1... | collective-permute-start | bytes 393224 | tf_op jit(solution)/shard_map/ppermute | solution.py:42
  31.7 7.5 %collective-permute-start.8 = (bf16[64,1024]{1,0:T(8,128)(2,1)S(1)}, bf16[64,1024]{1,0:T(8,128)(2,1)S(1)}, u32[]{:S(2)}, u32[]{:S(2)}) collective-permute-start(bf16[64,1024]{1,0:T(8,128)(2,1)S(1)} %collective-permute-done.5.refs_3_), channel_id=1, source_target_pairs={{0,2},{2,4},{4,6},{6,7},{7,5},{5,3},{3,1},{1,0},{8,10},{10,12},{12... | collective-permute-start | bytes 393224 | tf_op jit(solution)/shard_map/ppermute | solution.py:42
  33.8 6.8 %collective-permute-start.18 = (bf16[64,1024]{1,0:T(8,128)(2,1)S(1)}, bf16[64,1024]{1,0:T(8,128)(2,1)S(1)}, u32[]{:S(2)}, u32[]{:S(2)}) collective-permute-start(bf16[64,1024]{1,0:T(8,128)(2,1)S(1)} %collective-permute-done.17.refs_12_), channel_id=1, source_target_pairs={{0,1},{2,0},{4,2},{6,4},{7,6},{5,7},{3,5},{1,3},{8,9},{10,8},{12,1... | collective-permute-start | bytes 393224 | tf_op jit(solution)/shard_map/ppermute | solution.py:42
  36.5 6.8 %collective-permute-start.15 = (bf16[64,1024]{1,0:T(8,128)(2,1)S(1)}, bf16[64,1024]{1,0:T(8,128)(2,1)S(1)}, u32[]{:S(2)}, u32[]{:S(2)}) collective-permute-start(bf16[64,1024]{1,0:T(8,128)(2,1)S(1)} %collective-permute-done.14.refs_10_), channel_id=1, source_target_pairs={{0,2},{2,4},{4,6},{6,7},{7,5},{5,3},{3,1},{1,0},{8,10},{10,12},{12... | collective-permute-start | bytes 393224 | tf_op jit(solution)/shard_map/ppermute | solution.py:42
  39.2 6.8 %collective-permute-start.10 = (f32[2,2,128]{2,1,0:T(2,128)S(1)}, f32[2,2,128]{2,1,0:T(2,128)S(1)}, u32[]{:S(2)}, u32[]{:S(2)}) collective-permute-start(f32[2,2,128]{2,1,0:T(2,128)S(1)} %pad_maximum_fusion.6), channel_id=1, source_target_pairs={{0,8},{8,0},{16,24},{24,16},{1,9},{9,1},{17,25},{25,17},{2,10},{10... | collective-permute-start | bytes 6152 | tf_op jit(solution)/shard_map/ppermute | solution.py:106
  39.3 9.7 %collective-permute-start.11 = (bf16[64,1024]{1,0:T(8,128)(2,1)S(1)}, bf16[64,1024]{1,0:T(8,128)(2,1)S(1)}, u32[]{:S(2)}, u32[]{:S(2)}) collective-permute-start(bf16[64,1024]{1,0:T(8,128)(2,1)S(1)} %collective-permute-done.8.refs_2_), channel_id=1, source_target_pairs={{0,2},{2,4},{4,6},{6,7},{7,5},{5,3},{3,1},{1,0},{8,10},{10,12},{12... | collective-permute-start | bytes 393224 | tf_op jit(solution)/shard_map/ppermute | solution.py:42
  40.5 6.3 %collective-permute-start.19 = (bf16[64,1024]{1,0:T(8,128)(2,1)S(1)}, bf16[64,1024]{1,0:T(8,128)(2,1)S(1)}, u32[]{:S(2)}, u32[]{:S(2)}) collective-permute-start(bf16[64,1024]{1,0:T(8,128)(2,1)S(1)} %collective-permute-done.18.refs_13_), channel_id=1, source_target_pairs={{0,1},{2,0},{4,2},{6,4},{7,6},{5,7},{3,5},{1,3},{8,9},{10,8},{12,1... | collective-permute-start | bytes 393224 | tf_op jit(solution)/shard_map/ppermute | solution.py:42
  42.7 9.0 %collective-permute-start.13 = (bf16[64,1024]{1,0:T(8,128)(2,1)S(1)}, bf16[64,1024]{1,0:T(8,128)(2,1)S(1)}, u32[]{:S(2)}, u32[]{:S(2)}) collective-permute-start(bf16[64,1024]{1,0:T(8,128)(2,1)S(1)} %collective-permute-done.9.refs_6_), channel_id=1, source_target_pairs={{0,1},{2,0},{4,2},{6,4},{7,6},{5,7},{3,5},{1,3},{8,9},{10,8},{12,1... | collective-permute-start | bytes 393224 | tf_op jit(solution)/shard_map/ppermute | solution.py:42
  43.4 7.6 %collective-permute-start.16 = (bf16[64,1024]{1,0:T(8,128)(2,1)S(1)}, bf16[64,1024]{1,0:T(8,128)(2,1)S(1)}, u32[]{:S(2)}, u32[]{:S(2)}) collective-permute-start(bf16[64,1024]{1,0:T(8,128)(2,1)S(1)} %collective-permute-done.15.refs_9_), channel_id=1, source_target_pairs={{0,2},{2,4},{4,6},{6,7},{7,5},{5,3},{3,1},{1,0},{8,10},{10,12},{12... | collective-permute-start | bytes 393224 | tf_op jit(solution)/shard_map/ppermute | solution.py:42
  46.9 5.4 %collective-permute-start.20 = (bf16[64,1024]{1,0:T(8,128)(2,1)S(1)}, bf16[64,1024]{1,0:T(8,128)(2,1)S(1)}, u32[]{:S(2)}, u32[]{:S(2)}) collective-permute-start(bf16[64,1024]{1,0:T(8,128)(2,1)S(1)} %collective-permute-done.19.refs_14_), channel_id=1, source_target_pairs={{0,1},{2,0},{4,2},{6,4},{7,6},{5,7},{3,5},{1,3},{8,9},{10,8},{12,1... | collective-permute-start | bytes 393224 | tf_op jit(solution)/shard_map/ppermute | solution.py:42
  85.6 25.5 %collective-permute-start.22 = (f32[128,2048]{1,0:T(8,128)}, f32[128,2048]{1,0:T(8,128)}, u32[]{:S(2)}, u32[]{:S(2)}) collective-permute-start(f32[128,2048]{1,0:T(8,128)} %slice_add_fusion), channel_id=1, source_target_pairs={{0,16},{8,24},{16,0},{24,8},{1,17},{9,25},{17,1},{25,9},{2,18},{10... | collective-permute-start | bytes 3145736 | tf_op jit(solution)/shard_map/ppermute | solution.py:110
  117.1 5.4 %collective-permute-start.26 = (f32[2,256]{1,0:T(2,128)S(1)}, f32[2,256]{1,0:T(2,128)S(1)}, u32[]{:S(2)}, u32[]{:S(2)}) collective-permute-start(f32[2,256]{1,0:T(2,128)S(1)} %pad_maximum_fusion.8), channel_id=1, source_target_pairs={{0,6},{1,7},{2,4},{3,5},{4,2},{5,3},{6,0},{7,1},{8,14},{9,15},{10,... | collective-permute-start | bytes 6152 | tf_op jit(solution)/shard_map/ppermute | solution.py:47
  124.3 6.6 %collective-permute-start.27 = (bf16[64,2176]{1,0:T(8,128)(2,1)S(1)}, bf16[64,2176]{1,0:T(8,128)(2,1)S(1)}, u32[]{:S(2)}, u32[]{:S(2)}) collective-permute-start(bf16[64,2176]{1,0:T(8,128)(2,1)S(1)} %get-tuple-element.49), channel_id=1, source_target_pairs={{0,16},{8,24},{16,0},{24,8},{1,17},{9,25},{17,1},{25,9},{2,18},{10... | collective-permute-start | bytes 835592 | tf_op jit(solution)/shard_map/ppermute | solution.py:110
  131.2 11.0 %collective-permute-start.28 = (bf16[64,2176]{1,0:T(8,128)(2,1)S(1)}, bf16[64,2176]{1,0:T(8,128)(2,1)S(1)}, u32[]{:S(2)}, u32[]{:S(2)}) collective-permute-start(bf16[64,2176]{1,0:T(8,128)(2,1)S(1)} %pad_maximum_fusion.4), channel_id=1, source_target_pairs={{0,16},{8,24},{16,0},{24,8},{1,17},{9,25},{17,1},{25,9},{2,18},{10... | collective-permute-start | bytes 835592 | tf_op jit(solution)/shard_map/ppermute | solution.py:110
  140.1 5.8 %collective-permute-start.33 = (bf16[32,2176]{1,0:T(8,128)(2,1)S(1)}, bf16[32,2176]{1,0:T(8,128)(2,1)S(1)}, u32[]{:S(2)}, u32[]{:S(2)}) collective-permute-start(bf16[32,2176]{1,0:T(8,128)(2,1)S(1)} %get-tuple-element.44), channel_id=1, source_target_pairs={{0,2},{2,4},{4,6},{6,7},{7,5},{5,3},{3,1},{1,0},{8,10},{10,12},{12... | collective-permute-start | bytes 417800 | tf_op jit(solution)/shard_map/ppermute | solution.py:42
  142.3 5.7 %collective-permute-start.29 = (bf16[2,64,2176]{2,1,0:T(8,128)(2,1)S(1)}, bf16[2,64,2176]{2,1,0:T(8,128)(2,1)S(1)}, u32[]{:S(2)}, u32[]{:S(2)}) collective-permute-start(bf16[2,64,2176]{2,1,0:T(8,128)(2,1)S(1)} %pad_maximum_fusion.3), channel_id=1, source_target_pairs={{0,8},{8,0},{16,24},{24,16},{1,9},{9,1},{17,25},{25,17},{2,10},{10... | collective-permute-start | bytes 1671176 | tf_op jit(solution)/shard_map/ppermute | solution.py:106
  142.3 12.9 %collective-permute-start.37 = (bf16[32,2176]{1,0:T(8,128)(2,1)S(1)}, bf16[32,2176]{1,0:T(8,128)(2,1)S(1)}, u32[]{:S(2)}, u32[]{:S(2)}) collective-permute-start(bf16[32,2176]{1,0:T(8,128)(2,1)S(1)} %get-tuple-element.45), channel_id=1, source_target_pairs={{0,1},{2,0},{4,2},{6,4},{7,6},{5,7},{3,5},{1,3},{8,9},{10,8},{12,1... | collective-permute-start | bytes 417800 | tf_op jit(solution)/shard_map/ppermute | solution.py:42
  145.9 6.2 %collective-permute-start.34 = (bf16[32,2176]{1,0:T(8,128)(2,1)S(1)}, bf16[32,2176]{1,0:T(8,128)(2,1)S(1)}, u32[]{:S(2)}, u32[]{:S(2)}) collective-permute-start(bf16[32,2176]{1,0:T(8,128)(2,1)S(1)} %fusion.19), channel_id=1, source_target_pairs={{0,2},{2,4},{4,6},{6,7},{7,5},{5,3},{3,1},{1,0},{8,10},{10,12},{12... | collective-permute-start | bytes 417800 | tf_op jit(solution)/shard_map/ppermute | solution.py:42
  151.7 28.6 %collective-permute-start.30 = (bf16[2,64,3072]{2,1,0:T(8,128)(2,1)S(1)}, bf16[2,64,3072]{2,1,0:T(8,128)(2,1)S(1)}, u32[]{:S(2)}, u32[]{:S(2)}) collective-permute-start(bf16[2,64,3072]{2,1,0:T(8,128)(2,1)S(1)} %bitcast.64), channel_id=1, source_target_pairs={{0,16},{8,24},{16,0},{24,8},{1,17},{9,25},{17,1},{25,9},{2,18},{10... | collective-permute-start | bytes 2359304 | tf_op jit(solution)/shard_map/ppermute | solution.py:110
  152.1 6.3 %collective-permute-start.35 = (bf16[32,2176]{1,0:T(8,128)(2,1)S(1)}, bf16[32,2176]{1,0:T(8,128)(2,1)S(1)}, u32[]{:S(2)}, u32[]{:S(2)}) collective-permute-start(bf16[32,2176]{1,0:T(8,128)(2,1)S(1)} %fusion.20), channel_id=1, source_target_pairs={{0,2},{2,4},{4,6},{6,7},{7,5},{5,3},{3,1},{1,0},{8,10},{10,12},{12... | collective-permute-start | bytes 417800 | tf_op jit(solution)/shard_map/ppermute | solution.py:42
  153.2 8.2 %collective-permute-start.47 = (bf16[32,2176]{1,0:T(8,128)(2,1)S(1)}, bf16[32,2176]{1,0:T(8,128)(2,1)S(1)}, u32[]{:S(2)}, u32[]{:S(2)}) collective-permute-start(bf16[32,2176]{1,0:T(8,128)(2,1)S(1)} %get-tuple-element.42), channel_id=1, source_target_pairs={{0,2},{2,4},{4,6},{6,7},{7,5},{5,3},{3,1},{1,0},{8,10},{10,12},{12... | collective-permute-start | bytes 417800 | tf_op jit(solution)/shard_map/ppermute | solution.py:42
  153.7 13.1 %collective-permute-start.50 = (bf16[32,2176]{1,0:T(8,128)(2,1)S(1)}, bf16[32,2176]{1,0:T(8,128)(2,1)S(1)}, u32[]{:S(2)}, u32[]{:S(2)}) collective-permute-start(bf16[32,2176]{1,0:T(8,128)(2,1)S(1)} %get-tuple-element.43), channel_id=1, source_target_pairs={{0,1},{2,0},{4,2},{6,4},{7,6},{5,7},{3,5},{1,3},{8,9},{10,8},{12,1... | collective-permute-start | bytes 417800 | tf_op jit(solution)/shard_map/ppermute | solution.py:42
  158.5 11.1 %collective-permute-start.36 = (bf16[32,2176]{1,0:T(8,128)(2,1)S(1)}, bf16[32,2176]{1,0:T(8,128)(2,1)S(1)}, u32[]{:S(2)}, u32[]{:S(2)}) collective-permute-start(bf16[32,2176]{1,0:T(8,128)(2,1)S(1)} %get-tuple-element.38), channel_id=1, source_target_pairs={{0,2},{2,4},{4,6},{6,7},{7,5},{5,3},{3,1},{1,0},{8,10},{10,12},{12... | collective-permute-start | bytes 417800 | tf_op jit(solution)/shard_map/ppermute | solution.py:42
  159.1 6.3 %collective-permute-start.38 = (bf16[32,2176]{1,0:T(8,128)(2,1)S(1)}, bf16[32,2176]{1,0:T(8,128)(2,1)S(1)}, u32[]{:S(2)}, u32[]{:S(2)}) collective-permute-start(bf16[32,2176]{1,0:T(8,128)(2,1)S(1)} %get-tuple-element.39), channel_id=1, source_target_pairs={{0,1},{2,0},{4,2},{6,4},{7,6},{5,7},{3,5},{1,3},{8,9},{10,8},{12,1... | collective-permute-start | bytes 417800 | tf_op jit(solution)/shard_map/ppermute | solution.py:42
  161.4 6.0 %collective-permute-start.48 = (bf16[32,2176]{1,0:T(8,128)(2,1)S(1)}, bf16[32,2176]{1,0:T(8,128)(2,1)S(1)}, u32[]{:S(2)}, u32[]{:S(2)}) collective-permute-start(bf16[32,2176]{1,0:T(8,128)(2,1)S(1)} %fusion.14), channel_id=1, source_target_pairs={{0,2},{2,4},{4,6},{6,7},{7,5},{5,3},{3,1},{1,0},{8,10},{10,12},{12... | collective-permute-start | bytes 417800 | tf_op jit(solution)/shard_map/ppermute | solution.py:42
  165.4 5.3 %collective-permute-start.39 = (bf16[32,2176]{1,0:T(8,128)(2,1)S(1)}, bf16[32,2176]{1,0:T(8,128)(2,1)S(1)}, u32[]{:S(2)}, u32[]{:S(2)}) collective-permute-start(bf16[32,2176]{1,0:T(8,128)(2,1)S(1)} %fusion.18), channel_id=1, source_target_pairs={{0,1},{2,0},{4,2},{6,4},{7,6},{5,7},{3,5},{1,3},{8,9},{10,8},{12,1... | collective-permute-start | bytes 417800 | tf_op jit(solution)/shard_map/ppermute | solution.py:42
  167.5 13.0 %collective-permute-start.49 = (bf16[32,2176]{1,0:T(8,128)(2,1)S(1)}, bf16[32,2176]{1,0:T(8,128)(2,1)S(1)}, u32[]{:S(2)}, u32[]{:S(2)}) collective-permute-start(bf16[32,2176]{1,0:T(8,128)(2,1)S(1)} %get-tuple-element.36), channel_id=1, source_target_pairs={{0,2},{2,4},{4,6},{6,7},{7,5},{5,3},{3,1},{1,0},{8,10},{10,12},{12... | collective-permute-start | bytes 417800 | tf_op jit(solution)/shard_map/ppermute | solution.py:42
  168.2 5.4 %collective-permute-start.51 = (bf16[32,2176]{1,0:T(8,128)(2,1)S(1)}, bf16[32,2176]{1,0:T(8,128)(2,1)S(1)}, u32[]{:S(2)}, u32[]{:S(2)}) collective-permute-start(bf16[32,2176]{1,0:T(8,128)(2,1)S(1)} %get-tuple-element.37), channel_id=1, source_target_pairs={{0,1},{2,0},{4,2},{6,4},{7,6},{5,7},{3,5},{1,3},{8,9},{10,8},{12,1... | collective-permute-start | bytes 417800 | tf_op jit(solution)/shard_map/ppermute | solution.py:42
  180.4 25.8 %collective-permute-start.31 = (bf16[2,2,64,3072]{3,2,0,1:T(8,128)(2,1)S(1)}, bf16[2,2,64,3072]{3,2,0,1:T(8,128)(2,1)S(1)}, u32[]{:S(2)}, u32[]{:S(2)}) collective-permute-start(bf16[2,2,64,3072]{3,2,0,1:T(8,128)(2,1)S(1)} %pad_maximum_fusion.1), channel_id=1, source_target_pairs={{0,8},{8,0},{16,24},{24,16},{1,9},{9,1},{17,25},{25,17},{2,10},{10... | collective-permute-start | bytes 4718600 | tf_op jit(solution)/shard_map/ppermute | solution.py:106
  185.7 6.3 %collective-permute-start.57 = (bf16[32,2048]{1,0:T(8,128)(2,1)S(1)}, bf16[32,2048]{1,0:T(8,128)(2,1)S(1)}, u32[]{:S(2)}, u32[]{:S(2)}) collective-permute-start(bf16[32,2048]{1,0:T(8,128)(2,1)S(1)} %get-tuple-element.52.refs_11_), channel_id=1, source_target_pairs={{0,1},{2,0},{4,2},{6,4},{7,6},{5,7},{3,5},{1,3},{8,9},{10,8},{12,1... | collective-permute-start | bytes 393224 | tf_op jit(solution)/shard_map/ppermute | solution.py:42
  187.1 6.4 %collective-permute-start.40 = (bf16[32,2048]{1,0:T(8,128)(2,1)S(1)}, bf16[32,2048]{1,0:T(8,128)(2,1)S(1)}, u32[]{:S(2)}, u32[]{:S(2)}) collective-permute-start(bf16[32,2048]{1,0:T(8,128)(2,1)S(1)} %get-tuple-element.53.refs_4_), channel_id=1, source_target_pairs={{0,2},{2,4},{4,6},{6,7},{7,5},{5,3},{3,1},{1,0},{8,10},{10,12},{12... | collective-permute-start | bytes 393224 | tf_op jit(solution)/shard_map/ppermute | solution.py:42
  187.8 7.3 %collective-permute-start.54 = (bf16[32,2048]{1,0:T(8,128)(2,1)S(1)}, bf16[32,2048]{1,0:T(8,128)(2,1)S(1)}, u32[]{:S(2)}, u32[]{:S(2)}) collective-permute-start(bf16[32,2048]{1,0:T(8,128)(2,1)S(1)} %get-tuple-element.52.refs_11_), channel_id=1, source_target_pairs={{0,2},{2,4},{4,6},{6,7},{7,5},{5,3},{3,1},{1,0},{8,10},{10,12},{12... | collective-permute-start | bytes 393224 | tf_op jit(solution)/shard_map/ppermute | solution.py:42
  188.5 8.2 %collective-permute-start.44 = (bf16[32,2048]{1,0:T(8,128)(2,1)S(1)}, bf16[32,2048]{1,0:T(8,128)(2,1)S(1)}, u32[]{:S(2)}, u32[]{:S(2)}) collective-permute-start(bf16[32,2048]{1,0:T(8,128)(2,1)S(1)} %get-tuple-element.53.refs_4_), channel_id=1, source_target_pairs={{0,1},{2,0},{4,2},{6,4},{7,6},{5,7},{3,5},{1,3},{8,9},{10,8},{12,1... | collective-permute-start | bytes 393224 | tf_op jit(solution)/shard_map/ppermute | solution.py:42
  192.0 5.7 %collective-permute-start.58 = (bf16[32,2048]{1,0:T(8,128)(2,1)S(1)}, bf16[32,2048]{1,0:T(8,128)(2,1)S(1)}, u32[]{:S(2)}, u32[]{:S(2)}) collective-permute-start(bf16[32,2048]{1,0:T(8,128)(2,1)S(1)} %collective-permute-done.57.refs_12_), channel_id=1, source_target_pairs={{0,1},{2,0},{4,2},{6,4},{7,6},{5,7},{3,5},{1,3},{8,9},{10,8},{12,1... | collective-permute-start | bytes 393224 | tf_op jit(solution)/shard_map/ppermute | solution.py:42
  193.4 5.8 %collective-permute-start.41 = (bf16[32,2048]{1,0:T(8,128)(2,1)S(1)}, bf16[32,2048]{1,0:T(8,128)(2,1)S(1)}, u32[]{:S(2)}, u32[]{:S(2)}) collective-permute-start(bf16[32,2048]{1,0:T(8,128)(2,1)S(1)} %collective-permute-done.40.refs_3_), channel_id=1, source_target_pairs={{0,2},{2,4},{4,6},{6,7},{7,5},{5,3},{3,1},{1,0},{8,10},{10,12},{12... | collective-permute-start | bytes 393224 | tf_op jit(solution)/shard_map/ppermute | solution.py:42
  195.1 6.4 %collective-permute-start.55 = (bf16[32,2048]{1,0:T(8,128)(2,1)S(1)}, bf16[32,2048]{1,0:T(8,128)(2,1)S(1)}, u32[]{:S(2)}, u32[]{:S(2)}) collective-permute-start(bf16[32,2048]{1,0:T(8,128)(2,1)S(1)} %collective-permute-done.54.refs_10_), channel_id=1, source_target_pairs={{0,2},{2,4},{4,6},{6,7},{7,5},{5,3},{3,1},{1,0},{8,10},{10,12},{12... | collective-permute-start | bytes 393224 | tf_op jit(solution)/shard_map/ppermute | solution.py:42
  196.7 6.2 %collective-permute-start.45 = (bf16[32,2048]{1,0:T(8,128)(2,1)S(1)}, bf16[32,2048]{1,0:T(8,128)(2,1)S(1)}, u32[]{:S(2)}, u32[]{:S(2)}) collective-permute-start(bf16[32,2048]{1,0:T(8,128)(2,1)S(1)} %collective-permute-done.44.refs_5_), channel_id=1, source_target_pairs={{0,1},{2,0},{4,2},{6,4},{7,6},{5,7},{3,5},{1,3},{8,9},{10,8},{12,1... | collective-permute-start | bytes 393224 | tf_op jit(solution)/shard_map/ppermute | solution.py:42
  197.6 6.6 %collective-permute-start.59 = (bf16[32,2048]{1,0:T(8,128)(2,1)S(1)}, bf16[32,2048]{1,0:T(8,128)(2,1)S(1)}, u32[]{:S(2)}, u32[]{:S(2)}) collective-permute-start(bf16[32,2048]{1,0:T(8,128)(2,1)S(1)} %collective-permute-done.58.refs_13_), channel_id=1, source_target_pairs={{0,1},{2,0},{4,2},{6,4},{7,6},{5,7},{3,5},{1,3},{8,9},{10,8},{12,1... | collective-permute-start | bytes 393224 | tf_op jit(solution)/shard_map/ppermute | solution.py:42
  199.2 5.3 %collective-permute-start.42 = (bf16[32,2048]{1,0:T(8,128)(2,1)S(1)}, bf16[32,2048]{1,0:T(8,128)(2,1)S(1)}, u32[]{:S(2)}, u32[]{:S(2)}) collective-permute-start(bf16[32,2048]{1,0:T(8,128)(2,1)S(1)} %collective-permute-done.41.refs_2_), channel_id=1, source_target_pairs={{0,2},{2,4},{4,6},{6,7},{7,5},{5,3},{3,1},{1,0},{8,10},{10,12},{12... | collective-permute-start | bytes 393224 | tf_op jit(solution)/shard_map/ppermute | solution.py:42
  (56 other events, 347.6 us)

commit v9 on v8

--- a/solution.py
+++ b/solution.py
@@ -78,7 +78,7 @@
         p, far_ahead = self.place[vocab], self.reach(h)[0]
         return [(p + k - far_ahead) % self.size for k in range(self.size)]
 
-    def scatter_sum(self, part, h, seen=None):
+    def scatter_sum(self, part, h, wait):
         far_ahead, far_behind = self.reach(h)
         got_ahead = got_behind = None
         for step in range(self.half, 0, -1):
@@ -88,8 +88,10 @@
             if step <= far_behind:
                 behind = part(-step) if got_behind is None else part(-step) + got_behind
                 got_behind = self.shift(behind.astype(BF16), -1).astype(F32)
-            if seen:
-                seen(self.half - step, (got_ahead, got_behind))
+            if step == self.half:
+                got_ahead, got_behind = [
+                    x if x is None else after(x, wait) for x in (got_ahead, got_behind)
+                ]
         return part(0) + got_ahead + got_behind
 
 
@@ -124,11 +126,32 @@
 SMEM = pl.BlockSpec(memory_space=pltpu.SMEM)
 
 
-def transpose_into(out_ref, ref):
-    tile = min(ref.shape[1], 256)
-    for start in range(0, ref.shape[1], tile):
-        block = ref[:, pl.ds(start, tile)].astype(F32)
-        out_ref[pl.ds(start, tile), :] = block.T.astype(BF16)
+def choose_kernel(parents_ref, features_ref, out_ref):
+    rows = features_ref.shape[0]
+    from_row = lax.broadcasted_iota(jnp.int32, (rows, rows), 0)
+    row = lax.broadcasted_iota(jnp.int32, (rows, rows), 1)
+    chosen = from_row == row // TREE * TREE + parents_ref[...]
+    out_ref[...] = lax.dot_general(
+        chosen.astype(BF16),
+        features_ref[...],
+        (((0,), (0,)), ((), ())),
+        preferred_element_type=F32,
+    ).astype(BF16)
+
+
+def choose(parents, features):
+    return pl.pallas_call(
+        choose_kernel,
+        in_specs=[VMEM, VMEM],
+        out_specs=VMEM,
+        out_shape=jax.ShapeDtypeStruct(features.shape, BF16),
+        compiler_params=pltpu.CompilerParams(vmem_limit_bytes=12 * 2**20),
+        cost_estimate=pl.CostEstimate(
+            flops=2 * features.shape[0] * features.size,
+            bytes_accessed=4 * features.size,
+            transcendentals=0,
+        ),
+    )(parents.reshape(1, -1), features)
 
 
 def hold_kernel(weight_ref, held_ref, sems):
@@ -161,7 +184,7 @@
     blocks, refs = refs[: CHUNKS * count], refs[CHUNKS * count :]
     keep_ref, send_ref = refs[:CORES]
     piece_refs = refs[CORES : CORES + CHUNKS]
-    raw_ref, normed_ref, turned_ref = refs[CORES + CHUNKS :]
+    raw_ref, turned_ref = refs[CORES + CHUNKS :]
     rows, width = blocks[0].shape
     group_rows = CHUNKS * rows
     piece = piece_refs[0].shape[0]
@@ -175,12 +198,13 @@
             start = pl.multiple_of(index_ref[at] * group_rows + h * rows, rows)
             column = pl.multiple_of(index_ref[at + count] * width, width)
             raw_ref[pl.ds(start, rows), pl.ds(column, width)] = ref[...]
+        slab = min(raw_ref.shape[1], 256)
         for g in range(factor_ref.shape[0]):
             group = pl.ds(g * group_rows, group_rows)
-            normed_ref[group, :] = (
-                raw_ref[group, :].astype(F32) * factor_ref[g] * gain_ref[...]
-            ).astype(BF16)
-        transpose_into(turned_ref, normed_ref)
+            for first in range(0, raw_ref.shape[1], slab):
+                columns = pl.ds(first, slab)
+                values = raw_ref[group, columns].astype(F32) * gain_ref[:, columns]
+                turned_ref[columns, group] = (values.T * factor_ref[g : g + 1, :]).astype(BF16)
         for h, ref in enumerate(piece_refs):
             start = pl.multiple_of(index_ref[2 * CHUNKS * count + h] * piece, piece)
             ref[...] = raw_ref[pl.ds(start, piece), :]
@@ -205,8 +229,10 @@
         out_specs=[pl.BlockSpec((half, tile), lambda n: (0, n))] * CORES
         + [pl.BlockSpec((piece_rows, depth), lambda n: (0, 0))] * CHUNKS,
         out_shape=[out] * CORES + [piece] * CHUNKS,
-        scratch_shapes=[pltpu.VMEM((all_rows, depth), BF16)] * 2
-        + [pltpu.VMEM((depth, all_rows), BF16)],
+        scratch_shapes=[
+            pltpu.VMEM((all_rows, depth), BF16),
+            pltpu.VMEM((depth, all_rows), BF16),
+        ],
         compiler_params=pltpu.CompilerParams(vmem_limit_bytes=28 * 2**20),
         cost_estimate=pl.CostEstimate(
             flops=2 * all_rows * depth * vocab,
@@ -335,7 +361,7 @@
             add("pieces", pieces + [start // share_rows])
             add("turn", [(k - p) % parts for k in range(parts)])
             start = p * piece_rows
-            add("starts", [g * slice_width, start // chunk_rows, start % chunk_rows, 2 * p])
+            add("starts", [g * slice_width, start // chunk_rows, start % chunk_rows, 2 * p, 2 * p + 1])
     return {
         name: np.asarray(rows, np.int32).reshape(groups.size, parts, -1)
         for name, rows in table.items()
@@ -371,8 +397,8 @@
     for name, rows in table.items():
         index[name] = own[first : first + rows.shape[2]]
         first += rows.shape[2]
-    gain_start, own_entry, own_first, own_lane = [
-        index["starts"].astype(jnp.uint32)[k] for k in range(4)
+    gain_start, own_entry, own_first, high_lane, low_lane = [
+        index["starts"].astype(jnp.uint32)[k] for k in range(5)
     ]
 
     def chunk(x, h):
@@ -417,15 +443,14 @@
         top = functools.reduce(jnp.maximum, [x[0] for x in terms])
         return jnp.stack([top, sum(x[1] * jnp.exp(x[0] - top) for x in terms)])
 
-    tree_rows = jnp.arange(group_rows, dtype=jnp.int32) // TREE * TREE + parents
-    own_chosen = features.at[tree_rows].get(mode="promise_in_bounds")
+    own_chosen = choose(parents, features)
 
     gain = lax.dynamic_slice(norm_gain, (gain_start,), (slice_width,)).reshape(1, slice_width)
     row_weight = 1048576.0 * live_rows / valid_count
     lane = lax.broadcasted_iota(jnp.uint32, (chunk_rows, LANES), 1)
 
     keep, send, *pieces = project(
-        index["place"], blocks, row_factor[:, :, None], gain, weight, piece_rows
+        index["place"], blocks, row_factor, gain, weight, piece_rows
     )
     other = groups.swap(send)
 
@@ -442,9 +467,8 @@
     scale = jnp.exp(mine[0] - met[0]) / met[1]
     draft_scale, target_scale = scale[:group_rows], scale[group_rows:]
 
-    grads = []
+    products = []
     for h in range(CHUNKS):
-        factor = row_factor[:, h * chunk_rows : (h + 1) * chunk_rows]
         own = chunk(logits, h)
         draft_probs = jnp.exp(own - chunk(top, h)[:, None]) * chunk(draft_scale, h)[:, None]
         target_probs = (
@@ -456,24 +480,27 @@
         dot_part = jnp.sum(logit_grad * own, axis=1)
         dot_high = lax.reduce_precision(dot_part, 8, 7)
         dot_low = dot_part - dot_high
-        lanes = jnp.where(lane == own_lane, dot_high[:, None], 0.0) + jnp.where(
-            lane == own_lane + 1, dot_low[:, None], 0.0
+        lanes = jnp.where(lane == high_lane, dot_high[:, None], 0.0) + jnp.where(
+            lane == low_lane, dot_low[:, None], 0.0
         )
         message = jnp.concatenate([logit_grad.astype(BF16), lanes.astype(BF16)], axis=1)
         if h > 0:
             message = after(message, mine)
         mine = groups.gather_chips(message)
         mine, other = [x.reshape(step_rows // CORES, -1) for x in (mine, groups.swap(mine))]
-        normed_grad = back(index["turn"], mine, other, weight, piece_rows)
-        if h == CHUNKS - 1:
-            chosen = after(own_chosen, normed_grad).reshape(CHUNKS, chunk_rows, -1)
-            chosen = groups.gather(chosen).transpose(1, 0, 2, 3).reshape(CHUNKS * step_rows, -1)
+        products.append(back(index["turn"], mine, other, weight, piece_rows))
+    chosen = after(own_chosen, products[-1]).reshape(CHUNKS, chunk_rows, -1)
+    chosen = groups.gather(chosen).transpose(1, 0, 2, 3).reshape(CHUNKS * step_rows, -1)
+
+    grads = []
+    for h, normed_grad in enumerate(products):
 
         def part(t):
             first = t % parts * piece_rows
             return normed_grad[first : first + piece_rows]
 
-        summed = ring.scatter_sum(part, h)
+        summed = ring.scatter_sum(part, h, products)
+        factor = row_factor[:, h * chunk_rows : (h + 1) * chunk_rows]
         own_factor = lax.dynamic_slice(factor, (own_entry, own_first), (1, piece_rows))[0]
         row_dot = jnp.sum(summed[:, slice_width:], axis=1) / own_factor
         grad_piece = (

time: 223 us -> 195 us (0.87)
  local copies, waits for them, and re-layouts: 40.5 us -> 6.7 us
  waiting for transfers between devices: 75.1 us -> 81.5 us
  other arithmetic: 13.4 us -> 10.2 us
  starting transfers between devices: 63.4 us -> 66.6 us
    unnamed x87 -> x10, local copies, waits for them, and re-layouts: 36 us -> 3.4 us
    ppermute x5, waiting for transfers between devices: 27.1 us -> 34.4 us  [shift(): lax.ppermute(x, 'dp', [(i, (i + CORES * step) % size) for i in range(size)])]
    ppermute x5, starting transfers between devices: 3.88 us -> 6.65 us  [shift(): lax.ppermute(x, 'dp', [(i, (i + CORES * step) % size) for i in range(size)])]
  transfers between devices with their start and end apart: 61 -> 61, of which waited for: 31 -> 33; matrix products, arithmetic and copies ran while one was open for 6% -> 6% of each run, Pallas kernels for 3% -> 4%
where the time goes in v9:
time: 195 us
  waiting for transfers between devices  81.5 us (42%)
  starting transfers between devices  66.6 us (34%)
  Pallas kernels  28.6 us (15%)
  other arithmetic  10.2 us (5%)
  local copies, waits for them, and re-layouts  6.7 us (3%)
    ppermute x42, starting transfers between devices, shift(): lax.ppermute(x, 'vocab', [(order[p], order[(p + step) % size]) for p in r...  44.2 us
    ppermute x42, waiting for transfers between devices, shift(): lax.ppermute(x, 'vocab', [(order[p], order[(p + step) % size]) for p in r...  36.6 us
    ppermute x5, waiting for transfers between devices, shift(): lax.ppermute(x, 'dp', [(i, (i + CORES * step) % size) for i in range(size)])  34.4 us
    ppermute x8, starting transfers between devices, partner(): return lax.ppermute(x, 'vocab', [(v, v ^ bit) for v in range(self.size)])  13.8 us
    pallas_call x1, Pallas kernels, outer(): pl.pallas_call(functools.partial(outer_kernel, len(chunks[0]), tile), gri...  12.6 us
    pallas_call x1, Pallas kernels, project(): pl.pallas_call(functools.partial(project_kernel, len(blocks[0]), tile), g...  7.94 us
    pallas_call x2, Pallas kernels, back(): pl.pallas_call(functools.partial(back_kernel, piece_rows, tile), grid=(de...  7.13 us
    ppermute x5, starting transfers between devices, shift(): lax.ppermute(x, 'dp', [(i, (i + CORES * step) % size) for i in range(size)])  6.65 us
  transfers between devices with their start and end apart: 61, of which 33 were waited for; matrix products, arithmetic and copies ran while one was open for 6% of the time, Pallas kernels for 4%

profile of v9, /device:TPU:0, one launch (start us, length us, event | category | flops | bytes accessed | tf_op | source)
XLA Modules:
  0.0 194.7 jit_solution(3672545861572835776)
XLA Ops:
  0.6 1.6 collective-permute-start.4
  3.3 3.0 %collective-permute-start = (f32[1,128]{1,0:T(1,128)S(1)}, f32[1,128]{1,0:T(1,128)S(1)}, u32[]{:S(2)}, u32[]{:S(2)}) collective-permute-start(f32[1,128]{1,0:T(1,128)S(1)} %bitcast.91), channel_id=1, source_target_pairs={{0,1},{1,0},{2,3},{3,2},{4,5},{5,4},{6,7},{7,6},{8,9},{9,8},{10,11... | collective-permute-start | bytes 1544 | tf_op jit(solution)/shard_map/ppermute | solution.py:47
  6.3 1.5 collective-permute-done
  7.9 5.0 %collective-permute-start.3 = (f32[1,128]{1,0:T(1,128)S(1)}, f32[1,128]{1,0:T(1,128)S(1)}, u32[]{:S(2)}, u32[]{:S(2)}) collective-permute-start(f32[1,128]{1,0:T(1,128)S(1)} %bitcast_add_fusion), channel_id=1, source_target_pairs={{0,6},{1,7},{2,4},{3,5},{4,2},{5,3},{6,0},{7,1},{8,14},{9,15},{10,... | collective-permute-start | bytes 1544 | tf_op jit(solution)/shard_map/ppermute | solution.py:47
  14.1 3.4 %copy-done = bf16[2048,2048]{1,0:T(8,128)(2,1)S(1)} copy-done((bf16[2048,2048]{1,0:T(8,128)(2,1)S(1)}, bf16[2048,2048]{1,0:T(8,128)(2,1)}, u32[]{:S(2)}) %copy-start) | copy-done | bytes 8388632
  18.2 1.6 collective-permute-start.17
  20.4 1.5 collective-permute-start.14
  22.4 2.2 %collective-permute-done.17.refs_12_ = bf16[64,1024]{1,0:T(8,128)(2,1)S(1)} collective-permute-done((bf16[64,1024]{1,0:T(8,128)(2,1)S(1)}, bf16[64,1024]{1,0:T(8,128)(2,1)S(1)}, u32[]{:S(2)}, u32[]{:S(2)}) %collective-permute-start.17) | collective-permute-done | bytes 131104 | tf_op jit(solution)/shard_map/ppermute | solution.py:42
  24.6 1.5 collective-permute-start.18
  27.5 2.5 %collective-permute-start.7 = (f32[2,128]{1,0:T(2,128)S(1)}, f32[2,128]{1,0:T(2,128)S(1)}, u32[]{:S(2)}, u32[]{:S(2)}) collective-permute-start(f32[2,128]{1,0:T(2,128)S(1)} %pad_maximum_fusion.10), channel_id=1, source_target_pairs={{0,16},{8,24},{16,0},{24,8},{1,17},{9,25},{17,1},{25,9},{2,18},{10... | collective-permute-start | bytes 3080 | tf_op jit(solution)/shard_map/ppermute | solution.py:112
  30.1 1.5 collective-permute-start.9
  32.1 1.5 collective-permute-start.19
  34.1 3.1 %collective-permute-done.15.refs_9_ = bf16[64,1024]{1,0:T(8,128)(2,1)S(1)} collective-permute-done((bf16[64,1024]{1,0:T(8,128)(2,1)S(1)}, bf16[64,1024]{1,0:T(8,128)(2,1)S(1)}, u32[]{:S(2)}, u32[]{:S(2)}) %collective-permute-start.15) | collective-permute-done | bytes 131104 | tf_op jit(solution)/shard_map/ppermute | solution.py:42
  37.8 1.5 collective-permute-start.13
  42.1 1.4 dynamic_slice.13
  45.0 7.9 %shard_map.97 = (f32[256,2048]{1,0:T(8,128)S(1)}, f32[256,2048]{1,0:T(8,128)S(1)}, bf16[32,2048]{1,0:T(8,128)(2,1)S(1)}, bf16[32,2048]{1,0:T(8,128)(2,1)S(1)}) custom-call(s32[34]{0:T(128)S(1)} %slice_bitcast_fusion.index_ref, f32[4,128]{1,0:T(4,128)S(1)} %get-tuple-element.59.factor_ref, f32[1,2048]{1,0:T(1,128)S(1)} %bitcast.69, ...), custom_call_target="tpu_custom_call" | custom-call | flops 4294967296 | bytes 14680064 | tf_op jit(solution)/shard_map/pallas_call | solution.py:225
  53.1 4.1 %collective-permute-done.21 = f32[256,2048]{1,0:T(8,128)S(1)} collective-permute-done((f32[256,2048]{1,0:T(8,128)S(1)}, f32[256,2048]{1,0:T(8,128)S(1)}, u32[]{:S(2)}, u32[]{:S(2)}) %collective-permute-start.21) | collective-permute-done | bytes 2097184 | tf_op jit(solution)/shard_map/ppermute | solution.py:108
  60.5 22.2 %collective-permute-done.22 = f32[128,2048]{1,0:T(8,128)S(1)} collective-permute-done((f32[128,2048]{1,0:T(8,128)S(1)}, f32[128,2048]{1,0:T(8,128)S(1)}, u32[]{:S(2)}, u32[]{:S(2)}) %collective-permute-start.22) | collective-permute-done | bytes 1048608 | tf_op jit(solution)/shard_map/ppermute | solution.py:112
  84.2 2.8 %collective-permute-done.23 = f32[2,256]{1,0:T(2,128)S(1)} collective-permute-done((f32[2,256]{1,0:T(2,128)S(1)}, f32[2,256]{1,0:T(2,128)S(1)}, u32[]{:S(2)}, u32[]{:S(2)}) %collective-permute-start.23) | collective-permute-done | bytes 2080 | tf_op jit(solution)/shard_map/ppermute | solution.py:47
  87.1 1.9 collective-permute-start.26
  89.9 1.7 collective-permute-start.24
  95.6 7.4 %collective-permute-done.27 = bf16[64,2176]{1,0:T(8,128)(2,1)S(1)} collective-permute-done((bf16[64,2176]{1,0:T(8,128)(2,1)S(1)}, bf16[64,2176]{1,0:T(8,128)(2,1)S(1)}, u32[]{:S(2)}, u32[]{:S(2)}) %collective-permute-start.27) | collective-permute-done | bytes 278560 | tf_op jit(solution)/shard_map/ppermute | solution.py:112
  104.8 4.9 %collective-permute-done.28 = bf16[64,2176]{1,0:T(8,128)(2,1)S(1)} collective-permute-done((bf16[64,2176]{1,0:T(8,128)(2,1)S(1)}, bf16[64,2176]{1,0:T(8,128)(2,1)S(1)}, u32[]{:S(2)}, u32[]{:S(2)}) %collective-permute-start.28) | collective-permute-done | bytes 278560 | tf_op jit(solution)/shard_map/ppermute | solution.py:112
  109.8 3.6 %shard_map.99 = f32[256,2176]{1,0:T(8,128)S(1)} custom-call(s32[8]{0:T(128)S(1)} %slice_bitcast_fusion.1.index_ref, bf16[128,2176]{1,0:T(8,128)(2,1)S(1)} %bitcast.66, bf16[128,2176]{1,0:T(8,128)(2,1)S(1)} %bitcast.68, bf16[2048,2048]{1,0:T(8,128)(2,1)S(1)} %shard_map.96.weight_ref), custom_call_target="tpu_custom_call" | custom-call | flops 2147483648 | bytes 11534336 | tf_op jit(solution)/shard_map/pallas_call | solution.py:269
  113.6 2.0 %collective-permute-start.33 = (bf16[32,2176]{1,0:T(8,128)(2,1)S(1)}, bf16[32,2176]{1,0:T(8,128)(2,1)S(1)}, u32[]{:S(2)}, u32[]{:S(2)}) collective-permute-start(bf16[32,2176]{1,0:T(8,128)(2,1)S(1)} %get-tuple-element.48), channel_id=1, source_target_pairs={{0,2},{2,4},{4,6},{6,7},{7,5},{5,3},{3,1},{1,0},{8,10},{10,12},{12... | collective-permute-start | bytes 417800 | tf_op jit(solution)/shard_map/ppermute | solution.py:42
  115.7 3.9 %collective-permute-done.33 = bf16[32,2176]{1,0:T(8,128)(2,1)S(1)} collective-permute-done((bf16[32,2176]{1,0:T(8,128)(2,1)S(1)}, bf16[32,2176]{1,0:T(8,128)(2,1)S(1)}, u32[]{:S(2)}, u32[]{:S(2)}) %collective-permute-start.33) | collective-permute-done | bytes 139296 | tf_op jit(solution)/shard_map/ppermute | solution.py:42
  119.7 3.6 %shard_map.98 = f32[256,2176]{1,0:T(8,128)S(1)} custom-call(s32[8]{0:T(128)S(1)} %slice_bitcast_fusion.1.index_ref, bf16[128,2176]{1,0:T(8,128)(2,1)S(1)} %bitcast.65, bf16[128,2176]{1,0:T(8,128)(2,1)S(1)} %bitcast.67, bf16[2048,2048]{1,0:T(8,128)(2,1)S(1)} %shard_map.96.weight_ref), custom_call_target="tpu_custom_call" | custom-call | flops 2147483648 | bytes 11534336 | tf_op jit(solution)/shard_map/pallas_call | solution.py:269
  124.6 1.7 collective-permute-start.47
  126.7 1.7 collective-permute-start.50
  128.5 2.8 %collective-permute-done.47 = bf16[32,2176]{1,0:T(8,128)(2,1)S(1)} collective-permute-done((bf16[32,2176]{1,0:T(8,128)(2,1)S(1)}, bf16[32,2176]{1,0:T(8,128)(2,1)S(1)}, u32[]{:S(2)}, u32[]{:S(2)}) %collective-permute-start.47) | collective-permute-done | bytes 139296 | tf_op jit(solution)/shard_map/ppermute | solution.py:42
  131.3 1.7 collective-permute-start.48
  134.3 1.7 collective-permute-start.35
  138.0 1.8 collective-permute-done.35
  139.8 1.7 collective-permute-start.36
  141.9 1.7 collective-permute-start.49
  144.5 2.8 %collective-permute-done.38 = bf16[32,2176]{1,0:T(8,128)(2,1)S(1)} collective-permute-done((bf16[32,2176]{1,0:T(8,128)(2,1)S(1)}, bf16[32,2176]{1,0:T(8,128)(2,1)S(1)}, u32[]{:S(2)}, u32[]{:S(2)}) %collective-permute-start.38) | collective-permute-done | bytes 139296 | tf_op jit(solution)/shard_map/ppermute | solution.py:42
  147.8 2.7 %collective-permute-done.52 = bf16[32,2176]{1,0:T(8,128)(2,1)S(1)} collective-permute-done((bf16[32,2176]{1,0:T(8,128)(2,1)S(1)}, bf16[32,2176]{1,0:T(8,128)(2,1)S(1)}, u32[]{:S(2)}, u32[]{:S(2)}) %collective-permute-start.52) | collective-permute-done | bytes 139296 | tf_op jit(solution)/shard_map/ppermute | solution.py:42
  154.3 1.3 collective-permute-done.53
  158.0 1.3 collective-permute-start.40
  161.3 2.0 %collective-permute-done.57.refs_12_ = bf16[32,2048]{1,0:T(8,128)(2,1)S(1)} collective-permute-done((bf16[32,2048]{1,0:T(8,128)(2,1)S(1)}, bf16[32,2048]{1,0:T(8,128)(2,1)S(1)}, u32[]{:S(2)}, u32[]{:S(2)}) %collective-permute-start.57) | collective-permute-done | bytes 131104 | tf_op jit(solution)/shard_map/ppermute | solution.py:42
  163.7 1.7 collective-permute-start.41
  166.5 1.4 collective-permute-start.55
  170.1 1.7 collective-permute-start.42
  172.8 1.4 collective-permute-start.56
  174.9 1.7 collective-permute-done.59.refs_14_
  177.2 1.4 collective-permute-start.43
  179.1 2.4 %collective-permute-done.60.refs_15_ = bf16[32,2048]{1,0:T(8,128)(2,1)S(1)} collective-permute-done((bf16[32,2048]{1,0:T(8,128)(2,1)S(1)}, bf16[32,2048]{1,0:T(8,128)(2,1)S(1)}, u32[]{:S(2)}, u32[]{:S(2)}) %collective-permute-start.60) | collective-permute-done | bytes 131104 | tf_op jit(solution)/shard_map/ppermute | solution.py:42
  182.1 12.6 %shard_map.100 = (f32[2048,3072]{1,0:T(8,128)}, bf16[64,2048]{1,0:T(8,128)(2,1)}) custom-call(s32[17]{0:T(128)S(1)} %slice_bitcast_fusion.2.index_ref, bf16[512,3072]{1,0:T(8,128)(2,1)S(1)} %bitcast.64, bf16[32,2048]{1,0:T(8,128)(2,1)S(1)} %collective-permute-done.43.refs_0_, bf16[32,2048]{1,0:T(8,128)(2,1)S(1)} %collective-permute-done.42.refs_1_, ...), custom_call_target="tpu_custom_call" | custom-call | flops 6442450944 | bytes 30408704 | tf_op jit(solution)/shard_map/pallas_call | solution.py:310
  (157 shorter events, 45.5 us)
Async XLA Ops:
  0.6 17.6 %collective-permute-start.4 = (bf16[128,1024]{1,0:T(8,128)(2,1)}, bf16[128,1024]{1,0:T(8,128)(2,1)S(1)}, u32[]{:S(2)}, u32[]{:S(2)}) collective-permute-start(bf16[128,1024]{1,0:T(8,128)(2,1)} %param.8), channel_id=1, source_target_pairs={{0,0},{1,1},{2,8},{3,9},{4,16},{5,17},{6,24},{7,25},{8,4},{9,5},{1... | collective-permute-start | bytes 786440 | tf_op jit(solution)/shard_map/ppermute | solution.py:414
  7.9 10.3 %collective-permute-start.3 = (f32[1,128]{1,0:T(1,128)S(1)}, f32[1,128]{1,0:T(1,128)S(1)}, u32[]{:S(2)}, u32[]{:S(2)}) collective-permute-start(f32[1,128]{1,0:T(1,128)S(1)} %bitcast_add_fusion), channel_id=1, source_target_pairs={{0,6},{1,7},{2,4},{3,5},{4,2},{5,3},{6,0},{7,1},{8,14},{9,15},{10,... | collective-permute-start | bytes 1544 | tf_op jit(solution)/shard_map/ppermute | solution.py:47
  12.9 5.3 %collective-permute-start.2 = (f32[1,128]{1,0:T(1,128)S(1)}, f32[1,128]{1,0:T(1,128)S(1)}, u32[]{:S(2)}, u32[]{:S(2)}) collective-permute-start(f32[1,128]{1,0:T(1,128)S(1)} %bitcast_add_fusion), channel_id=1, source_target_pairs={{0,4},{1,5},{2,6},{3,7},{4,0},{5,1},{6,2},{7,3},{8,12},{9,13},{10,... | collective-permute-start | bytes 1544 | tf_op jit(solution)/shard_map/ppermute | solution.py:47
  12.9 5.3 %collective-permute-start.1 = (f32[1,128]{1,0:T(1,128)S(1)}, f32[1,128]{1,0:T(1,128)S(1)}, u32[]{:S(2)}, u32[]{:S(2)}) collective-permute-start(f32[1,128]{1,0:T(1,128)S(1)} %bitcast_add_fusion), channel_id=1, source_target_pairs={{0,2},{1,3},{2,0},{3,1},{4,6},{5,7},{6,4},{7,5},{8,10},{9,11},{10,... | collective-permute-start | bytes 1544 | tf_op jit(solution)/shard_map/ppermute | solution.py:47
  18.2 6.4 %collective-permute-start.17 = (bf16[64,1024]{1,0:T(8,128)(2,1)S(1)}, bf16[64,1024]{1,0:T(8,128)(2,1)S(1)}, u32[]{:S(2)}, u32[]{:S(2)}) collective-permute-start(bf16[64,1024]{1,0:T(8,128)(2,1)S(1)} %get-tuple-element.54.refs_11_), channel_id=1, source_target_pairs={{0,1},{2,0},{4,2},{6,4},{7,6},{5,7},{3,5},{1,3},{8,9},{10,8},{12,1... | collective-permute-start | bytes 393224 | tf_op jit(solution)/shard_map/ppermute | solution.py:42
  19.8 6.4 %collective-permute-start.5 = (bf16[64,1024]{1,0:T(8,128)(2,1)S(1)}, bf16[64,1024]{1,0:T(8,128)(2,1)S(1)}, u32[]{:S(2)}, u32[]{:S(2)}) collective-permute-start(bf16[64,1024]{1,0:T(8,128)(2,1)S(1)} %get-tuple-element.55.refs_4_), channel_id=1, source_target_pairs={{0,2},{2,4},{4,6},{6,7},{7,5},{5,3},{3,1},{1,0},{8,10},{10,12},{12... | collective-permute-start | bytes 393224 | tf_op jit(solution)/shard_map/ppermute | solution.py:42
  20.4 11.2 %collective-permute-start.14 = (bf16[64,1024]{1,0:T(8,128)(2,1)S(1)}, bf16[64,1024]{1,0:T(8,128)(2,1)S(1)}, u32[]{:S(2)}, u32[]{:S(2)}) collective-permute-start(bf16[64,1024]{1,0:T(8,128)(2,1)S(1)} %get-tuple-element.54.refs_11_), channel_id=1, source_target_pairs={{0,2},{2,4},{4,6},{6,7},{7,5},{5,3},{3,1},{1,0},{8,10},{10,12},{12... | collective-permute-start | bytes 393224 | tf_op jit(solution)/shard_map/ppermute | solution.py:42
  21.8 5.7 %collective-permute-start.6 = (bf16[64,1024]{1,0:T(8,128)(2,1)S(1)}, bf16[64,1024]{1,0:T(8,128)(2,1)S(1)}, u32[]{:S(2)}, u32[]{:S(2)}) collective-permute-start(bf16[64,1024]{1,0:T(8,128)(2,1)S(1)} %get-tuple-element.55.refs_4_), channel_id=1, source_target_pairs={{0,1},{2,0},{4,2},{6,4},{7,6},{5,7},{3,5},{1,3},{8,9},{10,8},{12,1... | collective-permute-start | bytes 393224 | tf_op jit(solution)/shard_map/ppermute | solution.py:42
  24.6 7.5 %collective-permute-start.18 = (bf16[64,1024]{1,0:T(8,128)(2,1)S(1)}, bf16[64,1024]{1,0:T(8,128)(2,1)S(1)}, u32[]{:S(2)}, u32[]{:S(2)}) collective-permute-start(bf16[64,1024]{1,0:T(8,128)(2,1)S(1)} %collective-permute-done.17.refs_12_), channel_id=1, source_target_pairs={{0,1},{2,0},{4,2},{6,4},{7,6},{5,7},{3,5},{1,3},{8,9},{10,8},{12,1... | collective-permute-start | bytes 393224 | tf_op jit(solution)/shard_map/ppermute | solution.py:42
  26.2 7.4 %collective-permute-start.8 = (bf16[64,1024]{1,0:T(8,128)(2,1)S(1)}, bf16[64,1024]{1,0:T(8,128)(2,1)S(1)}, u32[]{:S(2)}, u32[]{:S(2)}) collective-permute-start(bf16[64,1024]{1,0:T(8,128)(2,1)S(1)} %collective-permute-done.5.refs_3_), channel_id=1, source_target_pairs={{0,2},{2,4},{4,6},{6,7},{7,5},{5,3},{3,1},{1,0},{8,10},{10,12},{12... | collective-permute-start | bytes 393224 | tf_op jit(solution)/shard_map/ppermute | solution.py:42
  27.5 13.8 %collective-permute-start.7 = (f32[2,128]{1,0:T(2,128)S(1)}, f32[2,128]{1,0:T(2,128)S(1)}, u32[]{:S(2)}, u32[]{:S(2)}) collective-permute-start(f32[2,128]{1,0:T(2,128)S(1)} %pad_maximum_fusion.10), channel_id=1, source_target_pairs={{0,16},{8,24},{16,0},{24,8},{1,17},{9,25},{17,1},{25,9},{2,18},{10... | collective-permute-start | bytes 3080 | tf_op jit(solution)/shard_map/ppermute | solution.py:112
  30.1 7.7 %collective-permute-start.9 = (bf16[64,1024]{1,0:T(8,128)(2,1)S(1)}, bf16[64,1024]{1,0:T(8,128)(2,1)S(1)}, u32[]{:S(2)}, u32[]{:S(2)}) collective-permute-start(bf16[64,1024]{1,0:T(8,128)(2,1)S(1)} %collective-permute-done.6.refs_5_), channel_id=1, source_target_pairs={{0,1},{2,0},{4,2},{6,4},{7,6},{5,7},{3,5},{1,3},{8,9},{10,8},{12,1... | collective-permute-start | bytes 393224 | tf_op jit(solution)/shard_map/ppermute | solution.py:42
  31.6 5.7 %collective-permute-start.15 = (bf16[64,1024]{1,0:T(8,128)(2,1)S(1)}, bf16[64,1024]{1,0:T(8,128)(2,1)S(1)}, u32[]{:S(2)}, u32[]{:S(2)}) collective-permute-start(bf16[64,1024]{1,0:T(8,128)(2,1)S(1)} %collective-permute-done.14.refs_10_), channel_id=1, source_target_pairs={{0,2},{2,4},{4,6},{6,7},{7,5},{5,3},{3,1},{1,0},{8,10},{10,12},{12... | collective-permute-start | bytes 393224 | tf_op jit(solution)/shard_map/ppermute | solution.py:42
  32.1 7.2 %collective-permute-start.19 = (bf16[64,1024]{1,0:T(8,128)(2,1)S(1)}, bf16[64,1024]{1,0:T(8,128)(2,1)S(1)}, u32[]{:S(2)}, u32[]{:S(2)}) collective-permute-start(bf16[64,1024]{1,0:T(8,128)(2,1)S(1)} %collective-permute-done.18.refs_13_), channel_id=1, source_target_pairs={{0,1},{2,0},{4,2},{6,4},{7,6},{5,7},{3,5},{1,3},{8,9},{10,8},{12,1... | collective-permute-start | bytes 393224 | tf_op jit(solution)/shard_map/ppermute | solution.py:42
  33.6 6.5 %collective-permute-start.11 = (bf16[64,1024]{1,0:T(8,128)(2,1)S(1)}, bf16[64,1024]{1,0:T(8,128)(2,1)S(1)}, u32[]{:S(2)}, u32[]{:S(2)}) collective-permute-start(bf16[64,1024]{1,0:T(8,128)(2,1)S(1)} %collective-permute-done.8.refs_2_), channel_id=1, source_target_pairs={{0,2},{2,4},{4,6},{6,7},{7,5},{5,3},{3,1},{1,0},{8,10},{10,12},{12... | collective-permute-start | bytes 393224 | tf_op jit(solution)/shard_map/ppermute | solution.py:42
  37.3 6.9 %collective-permute-start.16 = (bf16[64,1024]{1,0:T(8,128)(2,1)S(1)}, bf16[64,1024]{1,0:T(8,128)(2,1)S(1)}, u32[]{:S(2)}, u32[]{:S(2)}) collective-permute-start(bf16[64,1024]{1,0:T(8,128)(2,1)S(1)} %collective-permute-done.15.refs_9_), channel_id=1, source_target_pairs={{0,2},{2,4},{4,6},{6,7},{7,5},{5,3},{3,1},{1,0},{8,10},{10,12},{12... | collective-permute-start | bytes 393224 | tf_op jit(solution)/shard_map/ppermute | solution.py:42
  37.8 6.4 %collective-permute-start.13 = (bf16[64,1024]{1,0:T(8,128)(2,1)S(1)}, bf16[64,1024]{1,0:T(8,128)(2,1)S(1)}, u32[]{:S(2)}, u32[]{:S(2)}) collective-permute-start(bf16[64,1024]{1,0:T(8,128)(2,1)S(1)} %collective-permute-done.9.refs_6_), channel_id=1, source_target_pairs={{0,1},{2,0},{4,2},{6,4},{7,6},{5,7},{3,5},{1,3},{8,9},{10,8},{12,1... | collective-permute-start | bytes 393224 | tf_op jit(solution)/shard_map/ppermute | solution.py:42
  57.4 25.3 %collective-permute-start.22 = (f32[128,2048]{1,0:T(8,128)S(1)}, f32[128,2048]{1,0:T(8,128)S(1)}, u32[]{:S(2)}, u32[]{:S(2)}) collective-permute-start(f32[128,2048]{1,0:T(8,128)S(1)} %slice_add_fusion), channel_id=1, source_target_pairs={{0,16},{8,24},{16,0},{24,8},{1,17},{9,25},{17,1},{25,9},{2,18},{10... | collective-permute-start | bytes 3145736 | tf_op jit(solution)/shard_map/ppermute | solution.py:112
  87.1 5.4 %collective-permute-start.26 = (f32[2,256]{1,0:T(2,128)S(1)}, f32[2,256]{1,0:T(2,128)S(1)}, u32[]{:S(2)}, u32[]{:S(2)}) collective-permute-start(f32[2,256]{1,0:T(2,128)S(1)} %pad_maximum_fusion.9), channel_id=1, source_target_pairs={{0,6},{1,7},{2,4},{3,5},{4,2},{5,3},{6,0},{7,1},{8,14},{9,15},{10,... | collective-permute-start | bytes 6152 | tf_op jit(solution)/shard_map/ppermute | solution.py:47
  94.7 8.3 %collective-permute-start.27 = (bf16[64,2176]{1,0:T(8,128)(2,1)S(1)}, bf16[64,2176]{1,0:T(8,128)(2,1)S(1)}, u32[]{:S(2)}, u32[]{:S(2)}) collective-permute-start(bf16[64,2176]{1,0:T(8,128)(2,1)S(1)} %get-tuple-element.53), channel_id=1, source_target_pairs={{0,16},{8,24},{16,0},{24,8},{1,17},{9,25},{17,1},{25,9},{2,18},{10... | collective-permute-start | bytes 835592 | tf_op jit(solution)/shard_map/ppermute | solution.py:112
  103.1 6.6 %collective-permute-start.28 = (bf16[64,2176]{1,0:T(8,128)(2,1)S(1)}, bf16[64,2176]{1,0:T(8,128)(2,1)S(1)}, u32[]{:S(2)}, u32[]{:S(2)}) collective-permute-start(bf16[64,2176]{1,0:T(8,128)(2,1)S(1)} %pad_maximum_fusion.4), channel_id=1, source_target_pairs={{0,16},{8,24},{16,0},{24,8},{1,17},{9,25},{17,1},{25,9},{2,18},{10... | collective-permute-start | bytes 835592 | tf_op jit(solution)/shard_map/ppermute | solution.py:112
  109.8 9.9 %collective-permute-start.29 = (bf16[2,64,2176]{2,1,0:T(8,128)(2,1)S(1)}, bf16[2,64,2176]{2,1,0:T(8,128)(2,1)S(1)}, u32[]{:S(2)}, u32[]{:S(2)}) collective-permute-start(bf16[2,64,2176]{2,1,0:T(8,128)(2,1)S(1)} %pad_maximum_fusion.3), channel_id=1, source_target_pairs={{0,8},{8,0},{16,24},{24,16},{1,9},{9,1},{17,25},{25,17},{2,10},{10... | collective-permute-start | bytes 1671176 | tf_op jit(solution)/shard_map/ppermute | solution.py:108
  113.6 6.1 %collective-permute-start.33 = (bf16[32,2176]{1,0:T(8,128)(2,1)S(1)}, bf16[32,2176]{1,0:T(8,128)(2,1)S(1)}, u32[]{:S(2)}, u32[]{:S(2)}) collective-permute-start(bf16[32,2176]{1,0:T(8,128)(2,1)S(1)} %get-tuple-element.48), channel_id=1, source_target_pairs={{0,2},{2,4},{4,6},{6,7},{7,5},{5,3},{3,1},{1,0},{8,10},{10,12},{12... | collective-permute-start | bytes 417800 | tf_op jit(solution)/shard_map/ppermute | solution.py:42
  115.7 22.3 %collective-permute-start.37 = (bf16[32,2176]{1,0:T(8,128)(2,1)S(1)}, bf16[32,2176]{1,0:T(8,128)(2,1)S(1)}, u32[]{:S(2)}, u32[]{:S(2)}) collective-permute-start(bf16[32,2176]{1,0:T(8,128)(2,1)S(1)} %get-tuple-element.49), channel_id=1, source_target_pairs={{0,1},{2,0},{4,2},{6,4},{7,6},{5,7},{3,5},{1,3},{8,9},{10,8},{12,1... | collective-permute-start | bytes 417800 | tf_op jit(solution)/shard_map/ppermute | solution.py:42
  123.4 30.6 %collective-permute-start.30 = (bf16[2,64,3072]{2,1,0:T(8,128)(2,1)S(1)}, bf16[2,64,3072]{2,1,0:T(8,128)(2,1)S(1)}, u32[]{:S(2)}, u32[]{:S(2)}) collective-permute-start(bf16[2,64,3072]{2,1,0:T(8,128)(2,1)S(1)} %bitcast.61), channel_id=1, source_target_pairs={{0,16},{8,24},{16,0},{24,8},{1,17},{9,25},{17,1},{25,9},{2,18},{10... | collective-permute-start | bytes 2359304 | tf_op jit(solution)/shard_map/ppermute | solution.py:112
  124.6 6.7 %collective-permute-start.47 = (bf16[32,2176]{1,0:T(8,128)(2,1)S(1)}, bf16[32,2176]{1,0:T(8,128)(2,1)S(1)}, u32[]{:S(2)}, u32[]{:S(2)}) collective-permute-start(bf16[32,2176]{1,0:T(8,128)(2,1)S(1)} %get-tuple-element.46), channel_id=1, source_target_pairs={{0,2},{2,4},{4,6},{6,7},{7,5},{5,3},{3,1},{1,0},{8,10},{10,12},{12... | collective-permute-start | bytes 417800 | tf_op jit(solution)/shard_map/ppermute | solution.py:42
  126.4 7.9 %collective-permute-start.34 = (bf16[32,2176]{1,0:T(8,128)(2,1)S(1)}, bf16[32,2176]{1,0:T(8,128)(2,1)S(1)}, u32[]{:S(2)}, u32[]{:S(2)}) collective-permute-start(bf16[32,2176]{1,0:T(8,128)(2,1)S(1)} %fusion.19), channel_id=1, source_target_pairs={{0,2},{2,4},{4,6},{6,7},{7,5},{5,3},{3,1},{1,0},{8,10},{10,12},{12... | collective-permute-start | bytes 417800 | tf_op jit(solution)/shard_map/ppermute | solution.py:42
  126.7 9.3 %collective-permute-start.50 = (bf16[32,2176]{1,0:T(8,128)(2,1)S(1)}, bf16[32,2176]{1,0:T(8,128)(2,1)S(1)}, u32[]{:S(2)}, u32[]{:S(2)}) collective-permute-start(bf16[32,2176]{1,0:T(8,128)(2,1)S(1)} %get-tuple-element.47), channel_id=1, source_target_pairs={{0,1},{2,0},{4,2},{6,4},{7,6},{5,7},{3,5},{1,3},{8,9},{10,8},{12,1... | collective-permute-start | bytes 417800 | tf_op jit(solution)/shard_map/ppermute | solution.py:42
  131.3 5.8 %collective-permute-start.48 = (bf16[32,2176]{1,0:T(8,128)(2,1)S(1)}, bf16[32,2176]{1,0:T(8,128)(2,1)S(1)}, u32[]{:S(2)}, u32[]{:S(2)}) collective-permute-start(bf16[32,2176]{1,0:T(8,128)(2,1)S(1)} %fusion.14), channel_id=1, source_target_pairs={{0,2},{2,4},{4,6},{6,7},{7,5},{5,3},{3,1},{1,0},{8,10},{10,12},{12... | collective-permute-start | bytes 417800 | tf_op jit(solution)/shard_map/ppermute | solution.py:42
  134.3 5.4 %collective-permute-start.35 = (bf16[32,2176]{1,0:T(8,128)(2,1)S(1)}, bf16[32,2176]{1,0:T(8,128)(2,1)S(1)}, u32[]{:S(2)}, u32[]{:S(2)}) collective-permute-start(bf16[32,2176]{1,0:T(8,128)(2,1)S(1)} %fusion.20), channel_id=1, source_target_pairs={{0,2},{2,4},{4,6},{6,7},{7,5},{5,3},{3,1},{1,0},{8,10},{10,12},{12... | collective-permute-start | bytes 417800 | tf_op jit(solution)/shard_map/ppermute | solution.py:42
  137.2 6.6 %collective-permute-start.51 = (bf16[32,2176]{1,0:T(8,128)(2,1)S(1)}, bf16[32,2176]{1,0:T(8,128)(2,1)S(1)}, u32[]{:S(2)}, u32[]{:S(2)}) collective-permute-start(bf16[32,2176]{1,0:T(8,128)(2,1)S(1)} %get-tuple-element.41), channel_id=1, source_target_pairs={{0,1},{2,0},{4,2},{6,4},{7,6},{5,7},{3,5},{1,3},{8,9},{10,8},{12,1... | collective-permute-start | bytes 417800 | tf_op jit(solution)/shard_map/ppermute | solution.py:42
  139.8 11.4 %collective-permute-start.36 = (bf16[32,2176]{1,0:T(8,128)(2,1)S(1)}, bf16[32,2176]{1,0:T(8,128)(2,1)S(1)}, u32[]{:S(2)}, u32[]{:S(2)}) collective-permute-start(bf16[32,2176]{1,0:T(8,128)(2,1)S(1)} %get-tuple-element.42), channel_id=1, source_target_pairs={{0,2},{2,4},{4,6},{6,7},{7,5},{5,3},{3,1},{1,0},{8,10},{10,12},{12... | collective-permute-start | bytes 417800 | tf_op jit(solution)/shard_map/ppermute | solution.py:42
  141.5 5.8 %collective-permute-start.38 = (bf16[32,2176]{1,0:T(8,128)(2,1)S(1)}, bf16[32,2176]{1,0:T(8,128)(2,1)S(1)}, u32[]{:S(2)}, u32[]{:S(2)}) collective-permute-start(bf16[32,2176]{1,0:T(8,128)(2,1)S(1)} %get-tuple-element.43), channel_id=1, source_target_pairs={{0,1},{2,0},{4,2},{6,4},{7,6},{5,7},{3,5},{1,3},{8,9},{10,8},{12,1... | collective-permute-start | bytes 417800 | tf_op jit(solution)/shard_map/ppermute | solution.py:42
  141.9 12.4 %collective-permute-start.49 = (bf16[32,2176]{1,0:T(8,128)(2,1)S(1)}, bf16[32,2176]{1,0:T(8,128)(2,1)S(1)}, u32[]{:S(2)}, u32[]{:S(2)}) collective-permute-start(bf16[32,2176]{1,0:T(8,128)(2,1)S(1)} %get-tuple-element.40), channel_id=1, source_target_pairs={{0,2},{2,4},{4,6},{6,7},{7,5},{5,3},{3,1},{1,0},{8,10},{10,12},{12... | collective-permute-start | bytes 417800 | tf_op jit(solution)/shard_map/ppermute | solution.py:42
  143.8 6.7 %collective-permute-start.52 = (bf16[32,2176]{1,0:T(8,128)(2,1)S(1)}, bf16[32,2176]{1,0:T(8,128)(2,1)S(1)}, u32[]{:S(2)}, u32[]{:S(2)}) collective-permute-start(bf16[32,2176]{1,0:T(8,128)(2,1)S(1)} %fusion.12), channel_id=1, source_target_pairs={{0,1},{2,0},{4,2},{6,4},{7,6},{5,7},{3,5},{1,3},{8,9},{10,8},{12,1... | collective-permute-start | bytes 417800 | tf_op jit(solution)/shard_map/ppermute | solution.py:42
  147.3 5.2 %collective-permute-start.39 = (bf16[32,2176]{1,0:T(8,128)(2,1)S(1)}, bf16[32,2176]{1,0:T(8,128)(2,1)S(1)}, u32[]{:S(2)}, u32[]{:S(2)}) collective-permute-start(bf16[32,2176]{1,0:T(8,128)(2,1)S(1)} %fusion.18), channel_id=1, source_target_pairs={{0,1},{2,0},{4,2},{6,4},{7,6},{5,7},{3,5},{1,3},{8,9},{10,8},{12,1... | collective-permute-start | bytes 417800 | tf_op jit(solution)/shard_map/ppermute | solution.py:42
  154.2 24.4 %collective-permute-start.31 = (bf16[2,2,64,3072]{3,2,0,1:T(8,128)(2,1)S(1)}, bf16[2,2,64,3072]{3,2,0,1:T(8,128)(2,1)S(1)}, u32[]{:S(2)}, u32[]{:S(2)}) collective-permute-start(bf16[2,2,64,3072]{3,2,0,1:T(8,128)(2,1)S(1)} %pad_maximum_fusion.1), channel_id=1, source_target_pairs={{0,8},{8,0},{16,24},{24,16},{1,9},{9,1},{17,25},{25,17},{2,10},{10... | collective-permute-start | bytes 4718600 | tf_op jit(solution)/shard_map/ppermute | solution.py:108
  157.2 6.1 %collective-permute-start.57 = (bf16[32,2048]{1,0:T(8,128)(2,1)S(1)}, bf16[32,2048]{1,0:T(8,128)(2,1)S(1)}, u32[]{:S(2)}, u32[]{:S(2)}) collective-permute-start(bf16[32,2048]{1,0:T(8,128)(2,1)S(1)} %get-tuple-element.56.refs_11_), channel_id=1, source_target_pairs={{0,1},{2,0},{4,2},{6,4},{7,6},{5,7},{3,5},{1,3},{8,9},{10,8},{12,1... | collective-permute-start | bytes 393224 | tf_op jit(solution)/shard_map/ppermute | solution.py:42
  158.0 5.7 %collective-permute-start.40 = (bf16[32,2048]{1,0:T(8,128)(2,1)S(1)}, bf16[32,2048]{1,0:T(8,128)(2,1)S(1)}, u32[]{:S(2)}, u32[]{:S(2)}) collective-permute-start(bf16[32,2048]{1,0:T(8,128)(2,1)S(1)} %get-tuple-element.57.refs_4_), channel_id=1, source_target_pairs={{0,2},{2,4},{4,6},{6,7},{7,5},{5,3},{3,1},{1,0},{8,10},{10,12},{12... | collective-permute-start | bytes 393224 | tf_op jit(solution)/shard_map/ppermute | solution.py:42
  159.3 7.1 %collective-permute-start.54 = (bf16[32,2048]{1,0:T(8,128)(2,1)S(1)}, bf16[32,2048]{1,0:T(8,128)(2,1)S(1)}, u32[]{:S(2)}, u32[]{:S(2)}) collective-permute-start(bf16[32,2048]{1,0:T(8,128)(2,1)S(1)} %get-tuple-element.56.refs_11_), channel_id=1, source_target_pairs={{0,2},{2,4},{4,6},{6,7},{7,5},{5,3},{3,1},{1,0},{8,10},{10,12},{12... | collective-permute-start | bytes 393224 | tf_op jit(solution)/shard_map/ppermute | solution.py:42
  160.3 7.6 %collective-permute-start.44 = (bf16[32,2048]{1,0:T(8,128)(2,1)S(1)}, bf16[32,2048]{1,0:T(8,128)(2,1)S(1)}, u32[]{:S(2)}, u32[]{:S(2)}) collective-permute-start(bf16[32,2048]{1,0:T(8,128)(2,1)S(1)} %get-tuple-element.57.refs_4_), channel_id=1, source_target_pairs={{0,1},{2,0},{4,2},{6,4},{7,6},{5,7},{3,5},{1,3},{8,9},{10,8},{12,1... | collective-permute-start | bytes 393224 | tf_op jit(solution)/shard_map/ppermute | solution.py:42
  163.4 6.4 %collective-permute-start.58 = (bf16[32,2048]{1,0:T(8,128)(2,1)S(1)}, bf16[32,2048]{1,0:T(8,128)(2,1)S(1)}, u32[]{:S(2)}, u32[]{:S(2)}) collective-permute-start(bf16[32,2048]{1,0:T(8,128)(2,1)S(1)} %collective-permute-done.57.refs_12_), channel_id=1, source_target_pairs={{0,1},{2,0},{4,2},{6,4},{7,6},{5,7},{3,5},{1,3},{8,9},{10,8},{12,1... | collective-permute-start | bytes 393224 | tf_op jit(solution)/shard_map/ppermute | solution.py:42
  163.7 6.4 %collective-permute-start.41 = (bf16[32,2048]{1,0:T(8,128)(2,1)S(1)}, bf16[32,2048]{1,0:T(8,128)(2,1)S(1)}, u32[]{:S(2)}, u32[]{:S(2)}) collective-permute-start(bf16[32,2048]{1,0:T(8,128)(2,1)S(1)} %collective-permute-done.40.refs_3_), channel_id=1, source_target_pairs={{0,2},{2,4},{4,6},{6,7},{7,5},{5,3},{3,1},{1,0},{8,10},{10,12},{12... | collective-permute-start | bytes 393224 | tf_op jit(solution)/shard_map/ppermute | solution.py:42
  166.5 6.4 %collective-permute-start.55 = (bf16[32,2048]{1,0:T(8,128)(2,1)S(1)}, bf16[32,2048]{1,0:T(8,128)(2,1)S(1)}, u32[]{:S(2)}, u32[]{:S(2)}) collective-permute-start(bf16[32,2048]{1,0:T(8,128)(2,1)S(1)} %collective-permute-done.54.refs_10_), channel_id=1, source_target_pairs={{0,2},{2,4},{4,6},{6,7},{7,5},{5,3},{3,1},{1,0},{8,10},{10,12},{12... | collective-permute-start | bytes 393224 | tf_op jit(solution)/shard_map/ppermute | solution.py:42
  167.8 6.3 %collective-permute-start.45 = (bf16[32,2048]{1,0:T(8,128)(2,1)S(1)}, bf16[32,2048]{1,0:T(8,128)(2,1)S(1)}, u32[]{:S(2)}, u32[]{:S(2)}) collective-permute-start(bf16[32,2048]{1,0:T(8,128)(2,1)S(1)} %collective-permute-done.44.refs_5_), channel_id=1, source_target_pairs={{0,1},{2,0},{4,2},{6,4},{7,6},{5,7},{3,5},{1,3},{8,9},{10,8},{12,1... | collective-permute-start | bytes 393224 | tf_op jit(solution)/shard_map/ppermute | solution.py:42
  169.7 6.8 %collective-permute-start.59 = (bf16[32,2048]{1,0:T(8,128)(2,1)S(1)}, bf16[32,2048]{1,0:T(8,128)(2,1)S(1)}, u32[]{:S(2)}, u32[]{:S(2)}) collective-permute-start(bf16[32,2048]{1,0:T(8,128)(2,1)S(1)} %collective-permute-done.58.refs_13_), channel_id=1, source_target_pairs={{0,1},{2,0},{4,2},{6,4},{7,6},{5,7},{3,5},{1,3},{8,9},{10,8},{12,1... | collective-permute-start | bytes 393224 | tf_op jit(solution)/shard_map/ppermute | solution.py:42
  170.1 7.1 %collective-permute-start.42 = (bf16[32,2048]{1,0:T(8,128)(2,1)S(1)}, bf16[32,2048]{1,0:T(8,128)(2,1)S(1)}, u32[]{:S(2)}, u32[]{:S(2)}) collective-permute-start(bf16[32,2048]{1,0:T(8,128)(2,1)S(1)} %collective-permute-done.41.refs_2_), channel_id=1, source_target_pairs={{0,2},{2,4},{4,6},{6,7},{7,5},{5,3},{3,1},{1,0},{8,10},{10,12},{12... | collective-permute-start | bytes 393224 | tf_op jit(solution)/shard_map/ppermute | solution.py:42
  172.8 6.1 %collective-permute-start.56 = (bf16[32,2048]{1,0:T(8,128)(2,1)S(1)}, bf16[32,2048]{1,0:T(8,128)(2,1)S(1)}, u32[]{:S(2)}, u32[]{:S(2)}) collective-permute-start(bf16[32,2048]{1,0:T(8,128)(2,1)S(1)} %collective-permute-done.55.refs_9_), channel_id=1, source_target_pairs={{0,2},{2,4},{4,6},{6,7},{7,5},{5,3},{3,1},{1,0},{8,10},{10,12},{12... | collective-permute-start | bytes 393224 | tf_op jit(solution)/shard_map/ppermute | solution.py:42
  (18 other events, 96.8 us)

commit v10 on v9

--- a/solution.py
+++ b/solution.py
@@ -78,7 +78,7 @@
         p, far_ahead = self.place[vocab], self.reach(h)[0]
         return [(p + k - far_ahead) % self.size for k in range(self.size)]
 
-    def scatter_sum(self, part, h, wait):
+    def scatter_sum(self, part, h):
         far_ahead, far_behind = self.reach(h)
         got_ahead = got_behind = None
         for step in range(self.half, 0, -1):
@@ -88,10 +88,6 @@
             if step <= far_behind:
                 behind = part(-step) if got_behind is None else part(-step) + got_behind
                 got_behind = self.shift(behind.astype(BF16), -1).astype(F32)
-            if step == self.half:
-                got_ahead, got_behind = [
-                    x if x is None else after(x, wait) for x in (got_ahead, got_behind)
-                ]
         return part(0) + got_ahead + got_behind
 
 
@@ -242,38 +238,45 @@
     )(index, factor, gain, weight, *[x for chunk in blocks for x in chunk])
 
 
-def back_kernel(piece, tile, index_ref, mine_ref, other_ref, weight_ref, out_ref, grad_ref):
+def back_kernel(piece, tile, index_ref, mine_ref, other_ref, weight_ref, *refs):
+    out_refs, grad_ref = refs[:-1], refs[-1]
     vocab = weight_ref.shape[0]
-    half = mine_ref.shape[0]
-    depth = out_ref.shape[1] - LANES
+    rows, depth = out_refs[0].shape[0], out_refs[0].shape[1] - LANES
     step = pl.program_id(0)
+    groups, group_rows = mine_ref.shape[:2]
+    chunk_rows = group_rows // CHUNKS
 
     @pl.when(step == 0)
     def _():
-        for k in range(2 * half // piece):
-            ref, first = (mine_ref, k * piece) if k * piece < half else (other_ref, k * piece - half)
-            rows = pl.ds(pl.multiple_of(index_ref[k] * piece, piece), piece)
-            grad_ref[rows, :] = ref[pl.ds(first, piece), :vocab]
-            out_ref[rows, pl.ds(depth, LANES)] = ref[pl.ds(first, piece), vocab:].astype(F32)
+        for h, out_ref in enumerate(out_refs):
+            for k in range(rows // piece):
+                entry, first = k * piece // chunk_rows, k * piece % chunk_rows
+                ref = mine_ref if entry < groups else other_ref
+                source = (entry % groups, pl.ds(h * chunk_rows + first, piece))
+                start = pl.multiple_of(index_ref[k] * piece, piece)
+                grad_ref[pl.ds(h * rows + start, piece), :] = ref[source + (slice(0, vocab),)]
+                lanes = ref[source + (slice(vocab, vocab + LANES),)]
+                out_ref[pl.ds(start, piece), pl.ds(depth, LANES)] = lanes.astype(F32)
 
     columns = pl.ds(pl.multiple_of(step * tile, tile), tile)
-    out_ref[:, columns] = jnp.dot(
-        grad_ref[...], weight_ref[:, columns], preferred_element_type=F32
-    )
+    product = jnp.dot(grad_ref[...], weight_ref[:, columns], preferred_element_type=F32)
+    for h, out_ref in enumerate(out_refs):
+        out_ref[:, columns] = product[h * rows : (h + 1) * rows]
 
 
 def back(index, mine, other, weight, piece_rows):
     vocab, depth = weight.shape
-    all_rows = mine.shape[0] + other.shape[0]
+    all_rows = 2 * mine.shape[0] * mine.shape[1]
     tile = min(depth, 512)
+    shape = (all_rows // CHUNKS, depth + LANES)
     return pl.pallas_call(
         functools.partial(back_kernel, piece_rows, tile),
         grid=(depth // tile,),
         in_specs=[SMEM, VMEM, VMEM, VMEM],
-        out_specs=pl.BlockSpec((all_rows, depth + LANES), lambda n: (0, 0)),
-        out_shape=jax.ShapeDtypeStruct((all_rows, depth + LANES), F32),
+        out_specs=[pl.BlockSpec(shape, lambda n: (0, 0))] * CHUNKS,
+        out_shape=[jax.ShapeDtypeStruct(shape, F32)] * CHUNKS,
         scratch_shapes=[pltpu.VMEM((all_rows, vocab), BF16)],
-        compiler_params=pltpu.CompilerParams(vmem_limit_bytes=24 * 2**20),
+        compiler_params=pltpu.CompilerParams(vmem_limit_bytes=28 * 2**20),
         cost_estimate=pl.CostEstimate(
             flops=2 * all_rows * depth * vocab,
             bytes_accessed=2 * vocab * depth + all_rows * (2 * vocab + 4 * depth),
@@ -282,11 +285,23 @@
     )(index, mine, other, weight)
 
 
-def outer_kernel(count, tile, index_ref, chosen_ref, *refs):
-    pieces, (out_ref, share_ref, grad_ref) = refs[:-3], refs[-3:]
+def outer_kernel(count, copies, index_ref, chosen_ref, *refs):
+    pieces, (out_ref, share_ref, grad_ref, held_ref, sems) = refs[:-5], refs[-5:]
     rows = pieces[0].shape[0]
     share = share_ref.shape[0]
     step = pl.program_id(0)
+    steps = pl.num_programs(0)
+    slots, tile = held_ref.shape[:2]
+    part = tile // copies
+
+    def copy(step, k):
+        slot = lax.rem(step, slots)
+        start = pl.multiple_of(step * tile + k * part, part)
+        return pltpu.make_async_copy(
+            held_ref.at[slot, pl.ds(k * part, part), :],
+            out_ref.at[pl.ds(start, part), :],
+            sems.at[slot, k],
+        )
 
     @pl.when(step == 0)
     def _():
@@ -296,31 +311,49 @@
         start = pl.multiple_of(index_ref[len(pieces)] * share, share)
         share_ref[...] = grad_ref[pl.ds(start, share), :]
 
+    @pl.when(step >= slots)
+    def _():
+        for k in range(copies):
+            copy(step - slots, k).wait()
+
     columns = pl.ds(pl.multiple_of(step * tile, tile), tile)
-    out_ref[...] = lax.dot_general(
+    held_ref[lax.rem(step, slots)] = lax.dot_general(
         grad_ref[:, columns], chosen_ref[...], (((0,), (0,)), ((), ())), preferred_element_type=F32
     )
+    for k in range(copies):
+        copy(step, k).start()
+
+    @pl.when(step == steps - 1)
+    def _():
+        for back in range(slots - 1, -1, -1):
+            for k in range(copies):
+                copy(step - back, k).wait()
 
 
 def outer(index, chosen, chunks, share_rows):
     depth = chunks[0][0].shape[1]
     all_rows, joined = chosen.shape
-    tile = min(depth, 256)
+    tile = min(depth // 4, 256)
+    slots, copies = 3, 4
     pieces = [x for chunk in chunks for x in chunk]
     return pl.pallas_call(
-        functools.partial(outer_kernel, len(chunks[0]), tile),
+        functools.partial(outer_kernel, len(chunks[0]), copies),
         grid=(depth // tile,),
         in_specs=[SMEM, VMEM] + [VMEM] * len(pieces),
         out_specs=[
-            pl.BlockSpec((tile, joined), lambda n: (n, 0)),
+            pl.BlockSpec(memory_space=pl.ANY),
             pl.BlockSpec((share_rows, depth), lambda n: (0, 0)),
         ],
         out_shape=[
             jax.ShapeDtypeStruct((depth, joined), F32),
             jax.ShapeDtypeStruct((share_rows, depth), BF16),
         ],
-        scratch_shapes=[pltpu.VMEM((all_rows, depth), BF16)],
-        compiler_params=pltpu.CompilerParams(vmem_limit_bytes=40 * 2**20),
+        scratch_shapes=[
+            pltpu.VMEM((all_rows, depth), BF16),
+            pltpu.VMEM((slots, tile, joined), F32),
+            pltpu.SemaphoreType.DMA((slots, copies)),
+        ],
+        compiler_params=pltpu.CompilerParams(vmem_limit_bytes=32 * 2**20),
         cost_estimate=pl.CostEstimate(
             flops=2 * all_rows * depth * joined,
             bytes_accessed=4 * depth * joined + 2 * all_rows * (depth + joined),
@@ -435,7 +468,7 @@
     valid_count = jnp.sum(both[:, 1])
     row_factor = lax.rsqrt(both[:, 0] / model_width + 1e-05)
 
-    targets = target_logits.astype(F32)
+    targets = lax.optimization_barrier(target_logits.astype(F32))
     target_top = jnp.max(targets, axis=1)
     target_total = jnp.sum(jnp.exp(targets - target_top[:, None]), axis=1)
 
@@ -447,7 +480,7 @@
 
     gain = lax.dynamic_slice(norm_gain, (gain_start,), (slice_width,)).reshape(1, slice_width)
     row_weight = 1048576.0 * live_rows / valid_count
-    lane = lax.broadcasted_iota(jnp.uint32, (chunk_rows, LANES), 1)
+    lane = lax.broadcasted_iota(jnp.uint32, (group_rows, LANES), 1)
 
     keep, send, *pieces = project(
         index["place"], blocks, row_factor, gain, weight, piece_rows
@@ -467,29 +500,21 @@
     scale = jnp.exp(mine[0] - met[0]) / met[1]
     draft_scale, target_scale = scale[:group_rows], scale[group_rows:]
 
-    products = []
-    for h in range(CHUNKS):
-        own = chunk(logits, h)
-        draft_probs = jnp.exp(own - chunk(top, h)[:, None]) * chunk(draft_scale, h)[:, None]
-        target_probs = (
-            jnp.exp(chunk(targets, h) - chunk(target_top, h)[:, None])
-            * chunk(target_scale, h)[:, None]
-        )
-        logit_grad = chunk(row_weight, h)[:, None] * (draft_probs - target_probs)
-        logit_grad = lax.reduce_precision(logit_grad, 8, 7)
-        dot_part = jnp.sum(logit_grad * own, axis=1)
-        dot_high = lax.reduce_precision(dot_part, 8, 7)
-        dot_low = dot_part - dot_high
-        lanes = jnp.where(lane == high_lane, dot_high[:, None], 0.0) + jnp.where(
-            lane == low_lane, dot_low[:, None], 0.0
-        )
-        message = jnp.concatenate([logit_grad.astype(BF16), lanes.astype(BF16)], axis=1)
-        if h > 0:
-            message = after(message, mine)
-        mine = groups.gather_chips(message)
-        mine, other = [x.reshape(step_rows // CORES, -1) for x in (mine, groups.swap(mine))]
-        products.append(back(index["turn"], mine, other, weight, piece_rows))
-    chosen = after(own_chosen, products[-1]).reshape(CHUNKS, chunk_rows, -1)
+    draft_probs = jnp.exp(logits - top[:, None]) * draft_scale[:, None]
+    target_probs = jnp.exp(targets - target_top[:, None]) * target_scale[:, None]
+    logit_grad = row_weight[:, None] * (draft_probs - target_probs)
+    logit_grad = lax.reduce_precision(logit_grad, 8, 7)
+    dot_part = jnp.sum(logit_grad * logits, axis=1)
+    dot_high = lax.reduce_precision(dot_part, 8, 7)
+    dot_low = dot_part - dot_high
+    lanes = jnp.where(lane == high_lane, dot_high[:, None], 0.0) + jnp.where(
+        lane == low_lane, dot_low[:, None], 0.0
+    )
+    mine, other = groups.gather_halves(
+        jnp.concatenate([logit_grad.astype(BF16), lanes.astype(BF16)], axis=1)
+    )
+    products = back(index["turn"], mine, other, weight, piece_rows)
+    chosen = after(own_chosen, products).reshape(CHUNKS, chunk_rows, -1)
     chosen = groups.gather(chosen).transpose(1, 0, 2, 3).reshape(CHUNKS * step_rows, -1)
 
     grads = []
@@ -499,7 +524,7 @@
             first = t % parts * piece_rows
             return normed_grad[first : first + piece_rows]
 
-        summed = ring.scatter_sum(part, h, products)
+        summed = ring.scatter_sum(part, h)
         factor = row_factor[:, h * chunk_rows : (h + 1) * chunk_rows]
         own_factor = lax.dynamic_slice(factor, (own_entry, own_first), (1, piece_rows))[0]
         row_dot = jnp.sum(summed[:, slice_width:], axis=1) / own_factor

time: 195 us -> 195 us (level)
  other arithmetic: 10.2 us -> 12.8 us
  Pallas kernels: 28.6 us -> 26.5 us
  starting transfers between devices: 66.6 us -> 64.5 us
    ppermute x5 -> x4, waiting for transfers between devices: 4.16 us -> 6.33 us  [swap(): return lax.ppermute(x, 'dp', [(i, i ^ 1) for i in range(self.size)])]
    ppermute x5 -> x4, starting transfers between devices: 6.65 us -> 4.8 us  [shift(): lax.ppermute(x, 'dp', [(i, (i + CORES * step) % size) for i in range(size)])]
    pallas_call x2 -> x1, Pallas kernels: 7.13 us -> 5.86 us  [back(): pl.pallas_call(functools.partial(back_kernel, piece_rows, tile), grid=(de...]
    ppermute x5 -> x4, waiting for transfers between devices: 34.4 us -> 34.9 us  [shift(): lax.ppermute(x, 'dp', [(i, (i + CORES * step) % size) for i in range(size)])]
  transfers between devices with their start and end apart: 61 -> 59, of which waited for: 33 -> 35; matrix products, arithmetic and copies ran while one was open for 6% -> 5% of each run, Pallas kernels for 4% -> 1%
where the time goes in v10:
time: 195 us
  waiting for transfers between devices  82.8 us (42%)
  starting transfers between devices  64.5 us (33%)
  Pallas kernels  26.5 us (14%)
  other arithmetic  12.8 us (7%)
  local copies, waits for them, and re-layouts  6.92 us (4%)
    ppermute x42, starting transfers between devices, shift(): lax.ppermute(x, 'vocab', [(order[p], order[(p + step) % size]) for p in r...  43.9 us
    ppermute x42, waiting for transfers between devices, shift(): lax.ppermute(x, 'vocab', [(order[p], order[(p + step) % size]) for p in r...  36.4 us
    ppermute x4, waiting for transfers between devices, shift(): lax.ppermute(x, 'dp', [(i, (i + CORES * step) % size) for i in range(size)])  34.9 us
    ppermute x8, starting transfers between devices, partner(): return lax.ppermute(x, 'vocab', [(v, v ^ bit) for v in range(self.size)])  13.9 us
    pallas_call x1, Pallas kernels, outer(): pl.pallas_call(functools.partial(outer_kernel, len(chunks[0]), copies), g...  11.7 us
    pallas_call x1, Pallas kernels, project(): pl.pallas_call(functools.partial(project_kernel, len(blocks[0]), tile), g...  7.95 us
    ppermute x4, waiting for transfers between devices, swap(): return lax.ppermute(x, 'dp', [(i, i ^ 1) for i in range(self.size)])  6.33 us
    pallas_call x1, Pallas kernels, back(): pl.pallas_call(functools.partial(back_kernel, piece_rows, tile), grid=(de...  5.86 us
  transfers between devices with their start and end apart: 59, of which 35 were waited for; matrix products, arithmetic and copies ran while one was open for 5% of the time, Pallas kernels for 1%

profile of v10, /device:TPU:0, one launch (start us, length us, event | category | flops | bytes accessed | tf_op | source)
XLA Modules:
  0.0 194.6 jit_solution(13832107836596921895)
XLA Ops:
  0.6 1.6 collective-permute-start.4
  3.3 3.0 %collective-permute-start = (f32[1,128]{1,0:T(1,128)S(1)}, f32[1,128]{1,0:T(1,128)S(1)}, u32[]{:S(2)}, u32[]{:S(2)}) collective-permute-start(f32[1,128]{1,0:T(1,128)S(1)} %bitcast.81), channel_id=1, source_target_pairs={{0,1},{1,0},{2,3},{3,2},{4,5},{5,4},{6,7},{7,6},{8,9},{9,8},{10,11... | collective-permute-start | bytes 1544 | tf_op jit(solution)/shard_map/ppermute | solution.py:47
  6.3 1.5 collective-permute-done
  7.9 5.0 %collective-permute-start.3 = (f32[1,128]{1,0:T(1,128)S(1)}, f32[1,128]{1,0:T(1,128)S(1)}, u32[]{:S(2)}, u32[]{:S(2)}) collective-permute-start(f32[1,128]{1,0:T(1,128)S(1)} %bitcast_add_fusion), channel_id=1, source_target_pairs={{0,6},{1,7},{2,4},{3,5},{4,2},{5,3},{6,0},{7,1},{8,14},{9,15},{10,... | collective-permute-start | bytes 1544 | tf_op jit(solution)/shard_map/ppermute | solution.py:47
  14.1 3.4 %copy-done = bf16[2048,2048]{1,0:T(8,128)(2,1)S(1)} copy-done((bf16[2048,2048]{1,0:T(8,128)(2,1)S(1)}, bf16[2048,2048]{1,0:T(8,128)(2,1)}, u32[]{:S(2)}) %copy-start) | copy-done | bytes 8388632
  18.2 1.6 collective-permute-start.17
  20.4 1.5 collective-permute-start.14
  22.4 2.2 %collective-permute-done.17.refs_12_ = bf16[64,1024]{1,0:T(8,128)(2,1)S(1)} collective-permute-done((bf16[64,1024]{1,0:T(8,128)(2,1)S(1)}, bf16[64,1024]{1,0:T(8,128)(2,1)S(1)}, u32[]{:S(2)}, u32[]{:S(2)}) %collective-permute-start.17) | collective-permute-done | bytes 131104 | tf_op jit(solution)/shard_map/ppermute | solution.py:42
  24.6 1.5 collective-permute-start.18
  27.6 2.5 %collective-permute-start.7 = (f32[2,128]{1,0:T(2,128)S(1)}, f32[2,128]{1,0:T(2,128)S(1)}, u32[]{:S(2)}, u32[]{:S(2)}) collective-permute-start(f32[2,128]{1,0:T(2,128)S(1)} %pad_maximum_fusion.8), channel_id=1, source_target_pairs={{0,16},{8,24},{16,0},{24,8},{1,17},{9,25},{17,1},{25,9},{2,18},{10... | collective-permute-start | bytes 3080 | tf_op jit(solution)/shard_map/ppermute | solution.py:108
  30.1 1.5 collective-permute-start.9
  32.1 1.5 collective-permute-start.19
  34.1 3.1 %collective-permute-done.15.refs_9_ = bf16[64,1024]{1,0:T(8,128)(2,1)S(1)} collective-permute-done((bf16[64,1024]{1,0:T(8,128)(2,1)S(1)}, bf16[64,1024]{1,0:T(8,128)(2,1)S(1)}, u32[]{:S(2)}, u32[]{:S(2)}) %collective-permute-start.15) | collective-permute-done | bytes 131104 | tf_op jit(solution)/shard_map/ppermute | solution.py:42
  37.8 1.5 collective-permute-start.13
  45.0 7.9 %shard_map.97 = (f32[256,2048]{1,0:T(8,128)S(1)}, f32[256,2048]{1,0:T(8,128)S(1)}, bf16[32,2048]{1,0:T(8,128)(2,1)S(1)}, bf16[32,2048]{1,0:T(8,128)(2,1)S(1)}) custom-call(s32[34]{0:T(128)S(1)} %slice_bitcast_fusion.index_ref, f32[4,128]{1,0:T(4,128)S(1)} %get-tuple-element.49.factor_ref, f32[1,2048]{1,0:T(1,128)S(1)} %bitcast.60, ...), custom_call_target="tpu_custom_call" | custom-call | flops 4294967296 | bytes 14680064 | tf_op jit(solution)/shard_map/pallas_call | solution.py:221
  53.1 4.1 %collective-permute-done.21 = f32[256,2048]{1,0:T(8,128)S(1)} collective-permute-done((f32[256,2048]{1,0:T(8,128)S(1)}, f32[256,2048]{1,0:T(8,128)S(1)}, u32[]{:S(2)}, u32[]{:S(2)}) %collective-permute-start.21) | collective-permute-done | bytes 2097184 | tf_op jit(solution)/shard_map/ppermute | solution.py:104
  60.0 24.5 %collective-permute-done.22 = f32[128,2048]{1,0:T(8,128)} collective-permute-done((f32[128,2048]{1,0:T(8,128)}, f32[128,2048]{1,0:T(8,128)}, u32[]{:S(2)}, u32[]{:S(2)}) %collective-permute-start.22) | collective-permute-done | bytes 1048608 | tf_op jit(solution)/shard_map/ppermute | solution.py:108
  84.5 1.9 fusion.26
  88.9 1.6 collective-permute-done.23
  90.6 1.9 collective-permute-start.26
  94.1 1.7 collective-permute-start.24
  96.0 1.6 collective-permute-done.25
  99.7 10.4 %collective-permute-done.27 = bf16[128,2176]{1,0:T(8,128)(2,1)S(1)} collective-permute-done((bf16[128,2176]{1,0:T(8,128)(2,1)S(1)}, bf16[128,2176]{1,0:T(8,128)(2,1)S(1)}, u32[]{:S(2)}, u32[]{:S(2)}) %collective-permute-start.27) | collective-permute-done | bytes 557088 | tf_op jit(solution)/shard_map/ppermute | solution.py:108
  110.9 2.2 %collective-permute-done.28.other_ref = bf16[2,128,2176]{2,1,0:T(8,128)(2,1)S(1)} collective-permute-done((bf16[2,128,2176]{2,1,0:T(8,128)(2,1)S(1)}, bf16[2,128,2176]{2,1,0:T(8,128)(2,1)S(1)}, u32[]{:S(2)}, u32[]{:S(2)}) %collective-permute-start.28) | collective-permute-done | bytes 1114144 | tf_op jit(solution)/shard_map/ppermute | solution.py:104
  113.1 5.9 %shard_map.98 = (f32[256,2176]{1,0:T(8,128)S(1)}, f32[256,2176]{1,0:T(8,128)S(1)}) custom-call(s32[8]{0:T(128)S(1)} %slice_bitcast_fusion.1.index_ref, bf16[2,128,2176]{2,1,0:T(8,128)(2,1)S(1)} %pad_maximum_fusion.2.mine_ref, bf16[2,128,2176]{2,1,0:T(8,128)(2,1)S(1)} %collective-permute-done.28.other_ref, bf16[2048,2048]{1,0:T(8,128)(2,1)S(1)} %bitcast.55), custom_call_target="tpu_custom_call" | custom-call | flops 4294967296 | bytes 14680064 | tf_op jit(solution)/shard_map/pallas_call | solution.py:272
  119.8 1.7 collective-permute-start.31
  121.9 1.7 collective-permute-start.45
  124.0 2.4 %collective-permute-done.31 = bf16[32,2176]{1,0:T(8,128)(2,1)S(1)} collective-permute-done((bf16[32,2176]{1,0:T(8,128)(2,1)S(1)}, bf16[32,2176]{1,0:T(8,128)(2,1)S(1)}, u32[]{:S(2)}, u32[]{:S(2)}) %collective-permute-start.31) | collective-permute-done | bytes 139296 | tf_op jit(solution)/shard_map/ppermute | solution.py:42
  126.5 1.7 collective-permute-start.32
  129.5 1.7 collective-permute-start.46
  131.2 1.9 collective-permute-done.32
  133.1 1.7 collective-permute-start.33
  136.2 1.7 collective-permute-start.47
  139.3 1.7 collective-permute-start.34
  141.3 3.2 %collective-permute-done.49 = bf16[32,2176]{1,0:T(8,128)(2,1)S(1)} collective-permute-done((bf16[32,2176]{1,0:T(8,128)(2,1)S(1)}, bf16[32,2176]{1,0:T(8,128)(2,1)S(1)}, u32[]{:S(2)}, u32[]{:S(2)}) %collective-permute-start.49) | collective-permute-done | bytes 139296 | tf_op jit(solution)/shard_map/ppermute | solution.py:42
  145.0 2.6 %collective-permute-done.36 = bf16[32,2176]{1,0:T(8,128)(2,1)S(1)} collective-permute-done((bf16[32,2176]{1,0:T(8,128)(2,1)S(1)}, bf16[32,2176]{1,0:T(8,128)(2,1)S(1)}, u32[]{:S(2)}, u32[]{:S(2)}) %collective-permute-start.36) | collective-permute-done | bytes 139296 | tf_op jit(solution)/shard_map/ppermute | solution.py:42
  148.0 2.3 %collective-permute-done.50 = bf16[32,2176]{1,0:T(8,128)(2,1)S(1)} collective-permute-done((bf16[32,2176]{1,0:T(8,128)(2,1)S(1)}, bf16[32,2176]{1,0:T(8,128)(2,1)S(1)}, u32[]{:S(2)}, u32[]{:S(2)}) %collective-permute-start.50) | collective-permute-done | bytes 139296 | tf_op jit(solution)/shard_map/ppermute | solution.py:42
  150.9 1.9 collective-permute-done.37
  152.8 2.7 %collective-permute-done.51 = bf16[32,2176]{1,0:T(8,128)(2,1)S(1)} collective-permute-done((bf16[32,2176]{1,0:T(8,128)(2,1)S(1)}, bf16[32,2176]{1,0:T(8,128)(2,1)S(1)}, u32[]{:S(2)}, u32[]{:S(2)}) %collective-permute-start.51) | collective-permute-done | bytes 139296 | tf_op jit(solution)/shard_map/ppermute | solution.py:42
  159.2 1.6 collective-permute-start.38
  161.4 1.5 collective-permute-start.42
  162.9 2.2 %collective-permute-done.55.refs_12_ = bf16[32,2048]{1,0:T(8,128)(2,1)S(1)} collective-permute-done((bf16[32,2048]{1,0:T(8,128)(2,1)S(1)}, bf16[32,2048]{1,0:T(8,128)(2,1)S(1)}, u32[]{:S(2)}, u32[]{:S(2)}) %collective-permute-start.55) | collective-permute-done | bytes 131104 | tf_op jit(solution)/shard_map/ppermute | solution.py:42
  165.5 1.6 collective-permute-start.39
  168.1 1.6 collective-permute-start.53
  171.5 1.6 collective-permute-start.40
  174.3 1.9 collective-permute-start.54
  177.9 1.6 collective-permute-start.41
  182.8 11.7 %shard_map.99 = (f32[2048,3072]{1,0:T(8,128)}, bf16[64,2048]{1,0:T(8,128)(2,1)}) custom-call(s32[17]{0:T(128)S(1)} %slice_bitcast_fusion.2.index_ref, bf16[512,3072]{1,0:T(8,128)(2,1)S(1)} %bitcast.59, bf16[32,2048]{1,0:T(8,128)(2,1)S(1)} %collective-permute-done.41.refs_0_, bf16[32,2048]{1,0:T(8,128)(2,1)S(1)} %collective-permute-done.40.refs_1_, ...), custom_call_target="tpu_custom_call" | custom-call | flops 6442450944 | bytes 30408704 | tf_op jit(solution)/shard_map/pallas_call | solution.py:339
  (154 shorter events, 43.6 us)
Async XLA Ops:
  0.6 17.6 %collective-permute-start.4 = (bf16[128,1024]{1,0:T(8,128)(2,1)}, bf16[128,1024]{1,0:T(8,128)(2,1)S(1)}, u32[]{:S(2)}, u32[]{:S(2)}) collective-permute-start(bf16[128,1024]{1,0:T(8,128)(2,1)} %param.8), channel_id=1, source_target_pairs={{0,0},{1,1},{2,8},{3,9},{4,16},{5,17},{6,24},{7,25},{8,4},{9,5},{1... | collective-permute-start | bytes 786440 | tf_op jit(solution)/shard_map/ppermute | solution.py:447
  7.9 10.3 %collective-permute-start.3 = (f32[1,128]{1,0:T(1,128)S(1)}, f32[1,128]{1,0:T(1,128)S(1)}, u32[]{:S(2)}, u32[]{:S(2)}) collective-permute-start(f32[1,128]{1,0:T(1,128)S(1)} %bitcast_add_fusion), channel_id=1, source_target_pairs={{0,6},{1,7},{2,4},{3,5},{4,2},{5,3},{6,0},{7,1},{8,14},{9,15},{10,... | collective-permute-start | bytes 1544 | tf_op jit(solution)/shard_map/ppermute | solution.py:47
  12.9 5.3 %collective-permute-start.2 = (f32[1,128]{1,0:T(1,128)S(1)}, f32[1,128]{1,0:T(1,128)S(1)}, u32[]{:S(2)}, u32[]{:S(2)}) collective-permute-start(f32[1,128]{1,0:T(1,128)S(1)} %bitcast_add_fusion), channel_id=1, source_target_pairs={{0,4},{1,5},{2,6},{3,7},{4,0},{5,1},{6,2},{7,3},{8,12},{9,13},{10,... | collective-permute-start | bytes 1544 | tf_op jit(solution)/shard_map/ppermute | solution.py:47
  12.9 5.3 %collective-permute-start.1 = (f32[1,128]{1,0:T(1,128)S(1)}, f32[1,128]{1,0:T(1,128)S(1)}, u32[]{:S(2)}, u32[]{:S(2)}) collective-permute-start(f32[1,128]{1,0:T(1,128)S(1)} %bitcast_add_fusion), channel_id=1, source_target_pairs={{0,2},{1,3},{2,0},{3,1},{4,6},{5,7},{6,4},{7,5},{8,10},{9,11},{10,... | collective-permute-start | bytes 1544 | tf_op jit(solution)/shard_map/ppermute | solution.py:47
  18.2 6.4 %collective-permute-start.17 = (bf16[64,1024]{1,0:T(8,128)(2,1)S(1)}, bf16[64,1024]{1,0:T(8,128)(2,1)S(1)}, u32[]{:S(2)}, u32[]{:S(2)}) collective-permute-start(bf16[64,1024]{1,0:T(8,128)(2,1)S(1)} %get-tuple-element.44.refs_11_), channel_id=1, source_target_pairs={{0,1},{2,0},{4,2},{6,4},{7,6},{5,7},{3,5},{1,3},{8,9},{10,8},{12,1... | collective-permute-start | bytes 393224 | tf_op jit(solution)/shard_map/ppermute | solution.py:42
  19.8 6.4 %collective-permute-start.5 = (bf16[64,1024]{1,0:T(8,128)(2,1)S(1)}, bf16[64,1024]{1,0:T(8,128)(2,1)S(1)}, u32[]{:S(2)}, u32[]{:S(2)}) collective-permute-start(bf16[64,1024]{1,0:T(8,128)(2,1)S(1)} %get-tuple-element.45.refs_4_), channel_id=1, source_target_pairs={{0,2},{2,4},{4,6},{6,7},{7,5},{5,3},{3,1},{1,0},{8,10},{10,12},{12... | collective-permute-start | bytes 393224 | tf_op jit(solution)/shard_map/ppermute | solution.py:42
  20.4 11.2 %collective-permute-start.14 = (bf16[64,1024]{1,0:T(8,128)(2,1)S(1)}, bf16[64,1024]{1,0:T(8,128)(2,1)S(1)}, u32[]{:S(2)}, u32[]{:S(2)}) collective-permute-start(bf16[64,1024]{1,0:T(8,128)(2,1)S(1)} %get-tuple-element.44.refs_11_), channel_id=1, source_target_pairs={{0,2},{2,4},{4,6},{6,7},{7,5},{5,3},{3,1},{1,0},{8,10},{10,12},{12... | collective-permute-start | bytes 393224 | tf_op jit(solution)/shard_map/ppermute | solution.py:42
  21.8 5.7 %collective-permute-start.6 = (bf16[64,1024]{1,0:T(8,128)(2,1)S(1)}, bf16[64,1024]{1,0:T(8,128)(2,1)S(1)}, u32[]{:S(2)}, u32[]{:S(2)}) collective-permute-start(bf16[64,1024]{1,0:T(8,128)(2,1)S(1)} %get-tuple-element.45.refs_4_), channel_id=1, source_target_pairs={{0,1},{2,0},{4,2},{6,4},{7,6},{5,7},{3,5},{1,3},{8,9},{10,8},{12,1... | collective-permute-start | bytes 393224 | tf_op jit(solution)/shard_map/ppermute | solution.py:42
  24.6 7.5 %collective-permute-start.18 = (bf16[64,1024]{1,0:T(8,128)(2,1)S(1)}, bf16[64,1024]{1,0:T(8,128)(2,1)S(1)}, u32[]{:S(2)}, u32[]{:S(2)}) collective-permute-start(bf16[64,1024]{1,0:T(8,128)(2,1)S(1)} %collective-permute-done.17.refs_12_), channel_id=1, source_target_pairs={{0,1},{2,0},{4,2},{6,4},{7,6},{5,7},{3,5},{1,3},{8,9},{10,8},{12,1... | collective-permute-start | bytes 393224 | tf_op jit(solution)/shard_map/ppermute | solution.py:42
  26.2 7.4 %collective-permute-start.8 = (bf16[64,1024]{1,0:T(8,128)(2,1)S(1)}, bf16[64,1024]{1,0:T(8,128)(2,1)S(1)}, u32[]{:S(2)}, u32[]{:S(2)}) collective-permute-start(bf16[64,1024]{1,0:T(8,128)(2,1)S(1)} %collective-permute-done.5.refs_3_), channel_id=1, source_target_pairs={{0,2},{2,4},{4,6},{6,7},{7,5},{5,3},{3,1},{1,0},{8,10},{10,12},{12... | collective-permute-start | bytes 393224 | tf_op jit(solution)/shard_map/ppermute | solution.py:42
  27.6 13.8 %collective-permute-start.7 = (f32[2,128]{1,0:T(2,128)S(1)}, f32[2,128]{1,0:T(2,128)S(1)}, u32[]{:S(2)}, u32[]{:S(2)}) collective-permute-start(f32[2,128]{1,0:T(2,128)S(1)} %pad_maximum_fusion.8), channel_id=1, source_target_pairs={{0,16},{8,24},{16,0},{24,8},{1,17},{9,25},{17,1},{25,9},{2,18},{10... | collective-permute-start | bytes 3080 | tf_op jit(solution)/shard_map/ppermute | solution.py:108
  30.1 7.7 %collective-permute-start.9 = (bf16[64,1024]{1,0:T(8,128)(2,1)S(1)}, bf16[64,1024]{1,0:T(8,128)(2,1)S(1)}, u32[]{:S(2)}, u32[]{:S(2)}) collective-permute-start(bf16[64,1024]{1,0:T(8,128)(2,1)S(1)} %collective-permute-done.6.refs_5_), channel_id=1, source_target_pairs={{0,1},{2,0},{4,2},{6,4},{7,6},{5,7},{3,5},{1,3},{8,9},{10,8},{12,1... | collective-permute-start | bytes 393224 | tf_op jit(solution)/shard_map/ppermute | solution.py:42
  31.6 5.7 %collective-permute-start.15 = (bf16[64,1024]{1,0:T(8,128)(2,1)S(1)}, bf16[64,1024]{1,0:T(8,128)(2,1)S(1)}, u32[]{:S(2)}, u32[]{:S(2)}) collective-permute-start(bf16[64,1024]{1,0:T(8,128)(2,1)S(1)} %collective-permute-done.14.refs_10_), channel_id=1, source_target_pairs={{0,2},{2,4},{4,6},{6,7},{7,5},{5,3},{3,1},{1,0},{8,10},{10,12},{12... | collective-permute-start | bytes 393224 | tf_op jit(solution)/shard_map/ppermute | solution.py:42
  32.1 7.2 %collective-permute-start.19 = (bf16[64,1024]{1,0:T(8,128)(2,1)S(1)}, bf16[64,1024]{1,0:T(8,128)(2,1)S(1)}, u32[]{:S(2)}, u32[]{:S(2)}) collective-permute-start(bf16[64,1024]{1,0:T(8,128)(2,1)S(1)} %collective-permute-done.18.refs_13_), channel_id=1, source_target_pairs={{0,1},{2,0},{4,2},{6,4},{7,6},{5,7},{3,5},{1,3},{8,9},{10,8},{12,1... | collective-permute-start | bytes 393224 | tf_op jit(solution)/shard_map/ppermute | solution.py:42
  33.6 6.5 %collective-permute-start.11 = (bf16[64,1024]{1,0:T(8,128)(2,1)S(1)}, bf16[64,1024]{1,0:T(8,128)(2,1)S(1)}, u32[]{:S(2)}, u32[]{:S(2)}) collective-permute-start(bf16[64,1024]{1,0:T(8,128)(2,1)S(1)} %collective-permute-done.8.refs_2_), channel_id=1, source_target_pairs={{0,2},{2,4},{4,6},{6,7},{7,5},{5,3},{3,1},{1,0},{8,10},{10,12},{12... | collective-permute-start | bytes 393224 | tf_op jit(solution)/shard_map/ppermute | solution.py:42
  37.3 6.9 %collective-permute-start.16 = (bf16[64,1024]{1,0:T(8,128)(2,1)S(1)}, bf16[64,1024]{1,0:T(8,128)(2,1)S(1)}, u32[]{:S(2)}, u32[]{:S(2)}) collective-permute-start(bf16[64,1024]{1,0:T(8,128)(2,1)S(1)} %collective-permute-done.15.refs_9_), channel_id=1, source_target_pairs={{0,2},{2,4},{4,6},{6,7},{7,5},{5,3},{3,1},{1,0},{8,10},{10,12},{12... | collective-permute-start | bytes 393224 | tf_op jit(solution)/shard_map/ppermute | solution.py:42
  37.8 6.4 %collective-permute-start.13 = (bf16[64,1024]{1,0:T(8,128)(2,1)S(1)}, bf16[64,1024]{1,0:T(8,128)(2,1)S(1)}, u32[]{:S(2)}, u32[]{:S(2)}) collective-permute-start(bf16[64,1024]{1,0:T(8,128)(2,1)S(1)} %collective-permute-done.9.refs_6_), channel_id=1, source_target_pairs={{0,1},{2,0},{4,2},{6,4},{7,6},{5,7},{3,5},{1,3},{8,9},{10,8},{12,1... | collective-permute-start | bytes 393224 | tf_op jit(solution)/shard_map/ppermute | solution.py:42
  59.0 25.5 %collective-permute-start.22 = (f32[128,2048]{1,0:T(8,128)}, f32[128,2048]{1,0:T(8,128)}, u32[]{:S(2)}, u32[]{:S(2)}) collective-permute-start(f32[128,2048]{1,0:T(8,128)} %slice_add_fusion), channel_id=1, source_target_pairs={{0,16},{8,24},{16,0},{24,8},{1,17},{9,25},{17,1},{25,9},{2,18},{10... | collective-permute-start | bytes 3145736 | tf_op jit(solution)/shard_map/ppermute | solution.py:108
  90.6 5.4 %collective-permute-start.26 = (f32[2,256]{1,0:T(2,128)S(1)}, f32[2,256]{1,0:T(2,128)S(1)}, u32[]{:S(2)}, u32[]{:S(2)}) collective-permute-start(f32[2,256]{1,0:T(2,128)S(1)} %pad_maximum_fusion.7), channel_id=1, source_target_pairs={{0,6},{1,7},{2,4},{3,5},{4,2},{5,3},{6,0},{7,1},{8,14},{9,15},{10,... | collective-permute-start | bytes 6152 | tf_op jit(solution)/shard_map/ppermute | solution.py:47
  98.8 11.3 %collective-permute-start.27 = (bf16[128,2176]{1,0:T(8,128)(2,1)S(1)}, bf16[128,2176]{1,0:T(8,128)(2,1)S(1)}, u32[]{:S(2)}, u32[]{:S(2)}) collective-permute-start(bf16[128,2176]{1,0:T(8,128)(2,1)S(1)} %get-tuple-element.43), channel_id=1, source_target_pairs={{0,16},{8,24},{16,0},{24,8},{1,17},{9,25},{17,1},{25,9},{2,18},{10... | collective-permute-start | bytes 1671176 | tf_op jit(solution)/shard_map/ppermute | solution.py:108
  119.2 36.4 %collective-permute-start.29 = (bf16[2,64,3072]{2,1,0:T(8,128)(2,1)S(1)}, bf16[2,64,3072]{2,1,0:T(8,128)(2,1)S(1)}, u32[]{:S(2)}, u32[]{:S(2)}) collective-permute-start(bf16[2,64,3072]{2,1,0:T(8,128)(2,1)S(1)} %bitcast.56), channel_id=1, source_target_pairs={{0,16},{8,24},{16,0},{24,8},{1,17},{9,25},{17,1},{25,9},{2,18},{10... | collective-permute-start | bytes 2359304 | tf_op jit(solution)/shard_map/ppermute | solution.py:108
  119.8 6.6 %collective-permute-start.31 = (bf16[32,2176]{1,0:T(8,128)(2,1)S(1)}, bf16[32,2176]{1,0:T(8,128)(2,1)S(1)}, u32[]{:S(2)}, u32[]{:S(2)}) collective-permute-start(bf16[32,2176]{1,0:T(8,128)(2,1)S(1)} %get-tuple-element.40), channel_id=1, source_target_pairs={{0,2},{2,4},{4,6},{6,7},{7,5},{5,3},{3,1},{1,0},{8,10},{10,12},{12... | collective-permute-start | bytes 417800 | tf_op jit(solution)/shard_map/ppermute | solution.py:42
  121.5 16.7 %collective-permute-start.35 = (bf16[32,2176]{1,0:T(8,128)(2,1)S(1)}, bf16[32,2176]{1,0:T(8,128)(2,1)S(1)}, u32[]{:S(2)}, u32[]{:S(2)}) collective-permute-start(bf16[32,2176]{1,0:T(8,128)(2,1)S(1)} %get-tuple-element.41), channel_id=1, source_target_pairs={{0,1},{2,0},{4,2},{6,4},{7,6},{5,7},{3,5},{1,3},{8,9},{10,8},{12,1... | collective-permute-start | bytes 417800 | tf_op jit(solution)/shard_map/ppermute | solution.py:42
  121.9 7.5 %collective-permute-start.45 = (bf16[32,2176]{1,0:T(8,128)(2,1)S(1)}, bf16[32,2176]{1,0:T(8,128)(2,1)S(1)}, u32[]{:S(2)}, u32[]{:S(2)}) collective-permute-start(bf16[32,2176]{1,0:T(8,128)(2,1)S(1)} %get-tuple-element.38), channel_id=1, source_target_pairs={{0,2},{2,4},{4,6},{6,7},{7,5},{5,3},{3,1},{1,0},{8,10},{10,12},{12... | collective-permute-start | bytes 417800 | tf_op jit(solution)/shard_map/ppermute | solution.py:42
  123.7 11.2 %collective-permute-start.48 = (bf16[32,2176]{1,0:T(8,128)(2,1)S(1)}, bf16[32,2176]{1,0:T(8,128)(2,1)S(1)}, u32[]{:S(2)}, u32[]{:S(2)}) collective-permute-start(bf16[32,2176]{1,0:T(8,128)(2,1)S(1)} %get-tuple-element.39), channel_id=1, source_target_pairs={{0,1},{2,0},{4,2},{6,4},{7,6},{5,7},{3,5},{1,3},{8,9},{10,8},{12,1... | collective-permute-start | bytes 417800 | tf_op jit(solution)/shard_map/ppermute | solution.py:42
  126.5 6.6 %collective-permute-start.32 = (bf16[32,2176]{1,0:T(8,128)(2,1)S(1)}, bf16[32,2176]{1,0:T(8,128)(2,1)S(1)}, u32[]{:S(2)}, u32[]{:S(2)}) collective-permute-start(bf16[32,2176]{1,0:T(8,128)(2,1)S(1)} %add_convert_fusion.9), channel_id=1, source_target_pairs={{0,2},{2,4},{4,6},{6,7},{7,5},{5,3},{3,1},{1,0},{8,10},{10,12},{12... | collective-permute-start | bytes 417800 | tf_op jit(solution)/shard_map/ppermute | solution.py:42
  129.5 6.7 %collective-permute-start.46 = (bf16[32,2176]{1,0:T(8,128)(2,1)S(1)}, bf16[32,2176]{1,0:T(8,128)(2,1)S(1)}, u32[]{:S(2)}, u32[]{:S(2)}) collective-permute-start(bf16[32,2176]{1,0:T(8,128)(2,1)S(1)} %add_convert_fusion.4), channel_id=1, source_target_pairs={{0,2},{2,4},{4,6},{6,7},{7,5},{5,3},{3,1},{1,0},{8,10},{10,12},{12... | collective-permute-start | bytes 417800 | tf_op jit(solution)/shard_map/ppermute | solution.py:42
  133.1 6.1 %collective-permute-start.33 = (bf16[32,2176]{1,0:T(8,128)(2,1)S(1)}, bf16[32,2176]{1,0:T(8,128)(2,1)S(1)}, u32[]{:S(2)}, u32[]{:S(2)}) collective-permute-start(bf16[32,2176]{1,0:T(8,128)(2,1)S(1)} %add_convert_fusion.8), channel_id=1, source_target_pairs={{0,2},{2,4},{4,6},{6,7},{7,5},{5,3},{3,1},{1,0},{8,10},{10,12},{12... | collective-permute-start | bytes 417800 | tf_op jit(solution)/shard_map/ppermute | solution.py:42
  136.2 16.6 %collective-permute-start.47 = (bf16[32,2176]{1,0:T(8,128)(2,1)S(1)}, bf16[32,2176]{1,0:T(8,128)(2,1)S(1)}, u32[]{:S(2)}, u32[]{:S(2)}) collective-permute-start(bf16[32,2176]{1,0:T(8,128)(2,1)S(1)} %get-tuple-element.34), channel_id=1, source_target_pairs={{0,2},{2,4},{4,6},{6,7},{7,5},{5,3},{3,1},{1,0},{8,10},{10,12},{12... | collective-permute-start | bytes 417800 | tf_op jit(solution)/shard_map/ppermute | solution.py:42
  137.9 6.6 %collective-permute-start.49 = (bf16[32,2176]{1,0:T(8,128)(2,1)S(1)}, bf16[32,2176]{1,0:T(8,128)(2,1)S(1)}, u32[]{:S(2)}, u32[]{:S(2)}) collective-permute-start(bf16[32,2176]{1,0:T(8,128)(2,1)S(1)} %get-tuple-element.35), channel_id=1, source_target_pairs={{0,1},{2,0},{4,2},{6,4},{7,6},{5,7},{3,5},{1,3},{8,9},{10,8},{12,1... | collective-permute-start | bytes 417800 | tf_op jit(solution)/shard_map/ppermute | solution.py:42
  139.3 11.6 %collective-permute-start.34 = (bf16[32,2176]{1,0:T(8,128)(2,1)S(1)}, bf16[32,2176]{1,0:T(8,128)(2,1)S(1)}, u32[]{:S(2)}, u32[]{:S(2)}) collective-permute-start(bf16[32,2176]{1,0:T(8,128)(2,1)S(1)} %get-tuple-element.36), channel_id=1, source_target_pairs={{0,2},{2,4},{4,6},{6,7},{7,5},{5,3},{3,1},{1,0},{8,10},{10,12},{12... | collective-permute-start | bytes 417800 | tf_op jit(solution)/shard_map/ppermute | solution.py:42
  141.0 6.6 %collective-permute-start.36 = (bf16[32,2176]{1,0:T(8,128)(2,1)S(1)}, bf16[32,2176]{1,0:T(8,128)(2,1)S(1)}, u32[]{:S(2)}, u32[]{:S(2)}) collective-permute-start(bf16[32,2176]{1,0:T(8,128)(2,1)S(1)} %get-tuple-element.37), channel_id=1, source_target_pairs={{0,1},{2,0},{4,2},{6,4},{7,6},{5,7},{3,5},{1,3},{8,9},{10,8},{12,1... | collective-permute-start | bytes 417800 | tf_op jit(solution)/shard_map/ppermute | solution.py:42
  144.6 5.8 %collective-permute-start.50 = (bf16[32,2176]{1,0:T(8,128)(2,1)S(1)}, bf16[32,2176]{1,0:T(8,128)(2,1)S(1)}, u32[]{:S(2)}, u32[]{:S(2)}) collective-permute-start(bf16[32,2176]{1,0:T(8,128)(2,1)S(1)} %add_convert_fusion.1), channel_id=1, source_target_pairs={{0,1},{2,0},{4,2},{6,4},{7,6},{5,7},{3,5},{1,3},{8,9},{10,8},{12,1... | collective-permute-start | bytes 417800 | tf_op jit(solution)/shard_map/ppermute | solution.py:42
  147.6 5.1 %collective-permute-start.37 = (bf16[32,2176]{1,0:T(8,128)(2,1)S(1)}, bf16[32,2176]{1,0:T(8,128)(2,1)S(1)}, u32[]{:S(2)}, u32[]{:S(2)}) collective-permute-start(bf16[32,2176]{1,0:T(8,128)(2,1)S(1)} %add_convert_fusion.5), channel_id=1, source_target_pairs={{0,1},{2,0},{4,2},{6,4},{7,6},{5,7},{3,5},{1,3},{8,9},{10,8},{12,1... | collective-permute-start | bytes 417800 | tf_op jit(solution)/shard_map/ppermute | solution.py:42
  150.4 5.1 %collective-permute-start.51 = (bf16[32,2176]{1,0:T(8,128)(2,1)S(1)}, bf16[32,2176]{1,0:T(8,128)(2,1)S(1)}, u32[]{:S(2)}, u32[]{:S(2)}) collective-permute-start(bf16[32,2176]{1,0:T(8,128)(2,1)S(1)} %add_convert_fusion), channel_id=1, source_target_pairs={{0,1},{2,0},{4,2},{6,4},{7,6},{5,7},{3,5},{1,3},{8,9},{10,8},{12,1... | collective-permute-start | bytes 417800 | tf_op jit(solution)/shard_map/ppermute | solution.py:42
  155.7 23.7 %collective-permute-start.30 = (bf16[2,2,64,3072]{3,2,0,1:T(8,128)(2,1)S(1)}, bf16[2,2,64,3072]{3,2,0,1:T(8,128)(2,1)S(1)}, u32[]{:S(2)}, u32[]{:S(2)}) collective-permute-start(bf16[2,2,64,3072]{3,2,0,1:T(8,128)(2,1)S(1)} %pad_maximum_fusion.1), channel_id=1, source_target_pairs={{0,8},{8,0},{16,24},{24,16},{1,9},{9,1},{17,25},{25,17},{2,10},{10... | collective-permute-start | bytes 4718600 | tf_op jit(solution)/shard_map/ppermute | solution.py:104
  158.8 6.3 %collective-permute-start.55 = (bf16[32,2048]{1,0:T(8,128)(2,1)S(1)}, bf16[32,2048]{1,0:T(8,128)(2,1)S(1)}, u32[]{:S(2)}, u32[]{:S(2)}) collective-permute-start(bf16[32,2048]{1,0:T(8,128)(2,1)S(1)} %get-tuple-element.46.refs_11_), channel_id=1, source_target_pairs={{0,1},{2,0},{4,2},{6,4},{7,6},{5,7},{3,5},{1,3},{8,9},{10,8},{12,1... | collective-permute-start | bytes 393224 | tf_op jit(solution)/shard_map/ppermute | solution.py:42
  159.2 6.3 %collective-permute-start.38 = (bf16[32,2048]{1,0:T(8,128)(2,1)S(1)}, bf16[32,2048]{1,0:T(8,128)(2,1)S(1)}, u32[]{:S(2)}, u32[]{:S(2)}) collective-permute-start(bf16[32,2048]{1,0:T(8,128)(2,1)S(1)} %get-tuple-element.47.refs_4_), channel_id=1, source_target_pairs={{0,2},{2,4},{4,6},{6,7},{7,5},{5,3},{3,1},{1,0},{8,10},{10,12},{12... | collective-permute-start | bytes 393224 | tf_op jit(solution)/shard_map/ppermute | solution.py:42
  160.8 7.2 %collective-permute-start.52 = (bf16[32,2048]{1,0:T(8,128)(2,1)S(1)}, bf16[32,2048]{1,0:T(8,128)(2,1)S(1)}, u32[]{:S(2)}, u32[]{:S(2)}) collective-permute-start(bf16[32,2048]{1,0:T(8,128)(2,1)S(1)} %get-tuple-element.46.refs_11_), channel_id=1, source_target_pairs={{0,2},{2,4},{4,6},{6,7},{7,5},{5,3},{3,1},{1,0},{8,10},{10,12},{12... | collective-permute-start | bytes 393224 | tf_op jit(solution)/shard_map/ppermute | solution.py:42
  161.4 8.3 %collective-permute-start.42 = (bf16[32,2048]{1,0:T(8,128)(2,1)S(1)}, bf16[32,2048]{1,0:T(8,128)(2,1)S(1)}, u32[]{:S(2)}, u32[]{:S(2)}) collective-permute-start(bf16[32,2048]{1,0:T(8,128)(2,1)S(1)} %get-tuple-element.47.refs_4_), channel_id=1, source_target_pairs={{0,1},{2,0},{4,2},{6,4},{7,6},{5,7},{3,5},{1,3},{8,9},{10,8},{12,1... | collective-permute-start | bytes 393224 | tf_op jit(solution)/shard_map/ppermute | solution.py:42
  165.1 5.2 %collective-permute-start.56 = (bf16[32,2048]{1,0:T(8,128)(2,1)S(1)}, bf16[32,2048]{1,0:T(8,128)(2,1)S(1)}, u32[]{:S(2)}, u32[]{:S(2)}) collective-permute-start(bf16[32,2048]{1,0:T(8,128)(2,1)S(1)} %collective-permute-done.55.refs_12_), channel_id=1, source_target_pairs={{0,1},{2,0},{4,2},{6,4},{7,6},{5,7},{3,5},{1,3},{8,9},{10,8},{12,1... | collective-permute-start | bytes 393224 | tf_op jit(solution)/shard_map/ppermute | solution.py:42
  165.5 5.9 %collective-permute-start.39 = (bf16[32,2048]{1,0:T(8,128)(2,1)S(1)}, bf16[32,2048]{1,0:T(8,128)(2,1)S(1)}, u32[]{:S(2)}, u32[]{:S(2)}) collective-permute-start(bf16[32,2048]{1,0:T(8,128)(2,1)S(1)} %collective-permute-done.38.refs_3_), channel_id=1, source_target_pairs={{0,2},{2,4},{4,6},{6,7},{7,5},{5,3},{3,1},{1,0},{8,10},{10,12},{12... | collective-permute-start | bytes 393224 | tf_op jit(solution)/shard_map/ppermute | solution.py:42
  168.1 6.2 %collective-permute-start.53 = (bf16[32,2048]{1,0:T(8,128)(2,1)S(1)}, bf16[32,2048]{1,0:T(8,128)(2,1)S(1)}, u32[]{:S(2)}, u32[]{:S(2)}) collective-permute-start(bf16[32,2048]{1,0:T(8,128)(2,1)S(1)} %collective-permute-done.52.refs_10_), channel_id=1, source_target_pairs={{0,2},{2,4},{4,6},{6,7},{7,5},{5,3},{3,1},{1,0},{8,10},{10,12},{12... | collective-permute-start | bytes 393224 | tf_op jit(solution)/shard_map/ppermute | solution.py:42
  169.7 6.4 %collective-permute-start.43 = (bf16[32,2048]{1,0:T(8,128)(2,1)S(1)}, bf16[32,2048]{1,0:T(8,128)(2,1)S(1)}, u32[]{:S(2)}, u32[]{:S(2)}) collective-permute-start(bf16[32,2048]{1,0:T(8,128)(2,1)S(1)} %collective-permute-done.42.refs_5_), channel_id=1, source_target_pairs={{0,1},{2,0},{4,2},{6,4},{7,6},{5,7},{3,5},{1,3},{8,9},{10,8},{12,1... | collective-permute-start | bytes 393224 | tf_op jit(solution)/shard_map/ppermute | solution.py:42
  170.3 6.6 %collective-permute-start.57 = (bf16[32,2048]{1,0:T(8,128)(2,1)S(1)}, bf16[32,2048]{1,0:T(8,128)(2,1)S(1)}, u32[]{:S(2)}, u32[]{:S(2)}) collective-permute-start(bf16[32,2048]{1,0:T(8,128)(2,1)S(1)} %collective-permute-done.56.refs_13_), channel_id=1, source_target_pairs={{0,1},{2,0},{4,2},{6,4},{7,6},{5,7},{3,5},{1,3},{8,9},{10,8},{12,1... | collective-permute-start | bytes 393224 | tf_op jit(solution)/shard_map/ppermute | solution.py:42
  171.5 6.4 %collective-permute-start.40 = (bf16[32,2048]{1,0:T(8,128)(2,1)S(1)}, bf16[32,2048]{1,0:T(8,128)(2,1)S(1)}, u32[]{:S(2)}, u32[]{:S(2)}) collective-permute-start(bf16[32,2048]{1,0:T(8,128)(2,1)S(1)} %collective-permute-done.39.refs_2_), channel_id=1, source_target_pairs={{0,2},{2,4},{4,6},{6,7},{7,5},{5,3},{3,1},{1,0},{8,10},{10,12},{12... | collective-permute-start | bytes 393224 | tf_op jit(solution)/shard_map/ppermute | solution.py:42
  174.3 6.2 %collective-permute-start.54 = (bf16[32,2048]{1,0:T(8,128)(2,1)S(1)}, bf16[32,2048]{1,0:T(8,128)(2,1)S(1)}, u32[]{:S(2)}, u32[]{:S(2)}) collective-permute-start(bf16[32,2048]{1,0:T(8,128)(2,1)S(1)} %collective-permute-done.53.refs_9_), channel_id=1, source_target_pairs={{0,2},{2,4},{4,6},{6,7},{7,5},{5,3},{3,1},{1,0},{8,10},{10,12},{12... | collective-permute-start | bytes 393224 | tf_op jit(solution)/shard_map/ppermute | solution.py:42
  176.9 5.6 %collective-permute-start.58 = (bf16[32,2048]{1,0:T(8,128)(2,1)S(1)}, bf16[32,2048]{1,0:T(8,128)(2,1)S(1)}, u32[]{:S(2)}, u32[]{:S(2)}) collective-permute-start(bf16[32,2048]{1,0:T(8,128)(2,1)S(1)} %collective-permute-done.57.refs_14_), channel_id=1, source_target_pairs={{0,1},{2,0},{4,2},{6,4},{7,6},{5,7},{3,5},{1,3},{8,9},{10,8},{12,1... | collective-permute-start | bytes 393224 | tf_op jit(solution)/shard_map/ppermute | solution.py:42
  (20 other events, 168.8 us)

commit v11 on v10

--- a/solution.py
+++ b/solution.py
@@ -78,17 +78,25 @@
         p, far_ahead = self.place[vocab], self.reach(h)[0]
         return [(p + k - far_ahead) % self.size for k in range(self.size)]
 
-    def scatter_sum(self, part, h):
-        far_ahead, far_behind = self.reach(h)
-        got_ahead = got_behind = None
+    def scatter_sums(self, parts):
+        got = [[None, None] for _ in parts]
+        sent = []
         for step in range(self.half, 0, -1):
-            if step <= far_ahead:
-                ahead = part(step) if got_ahead is None else part(step) + got_ahead
-                got_ahead = self.shift(ahead.astype(BF16), 1).astype(F32)
-            if step <= far_behind:
-                behind = part(-step) if got_behind is None else part(-step) + got_behind
-                got_behind = self.shift(behind.astype(BF16), -1).astype(F32)
-        return part(0) + got_ahead + got_behind
+            for h, part in enumerate(parts):
+                for way, reach in enumerate(self.reach(h)):
+                    if step > reach:
+                        continue
+                    share = part(step if way == 0 else -step)
+                    if got[h][way] is not None:
+                        share = share + got[h][way].astype(F32)
+                    share = share.astype(BF16)
+                    if len(sent) >= len(parts):
+                        share = after(share, sent[-len(parts)])
+                    got[h][way] = self.shift(share, 1 if way == 0 else -1)
+                sent.append([x for x in got[h] if x is not None])
+        return [
+            part(0) + got[h][0].astype(F32) + got[h][1].astype(F32) for h, part in enumerate(parts)
+        ]
 
 
 class Groups:
@@ -468,7 +476,7 @@
     valid_count = jnp.sum(both[:, 1])
     row_factor = lax.rsqrt(both[:, 0] / model_width + 1e-05)
 
-    targets = lax.optimization_barrier(target_logits.astype(F32))
+    targets = target_logits.astype(F32)
     target_top = jnp.max(targets, axis=1)
     target_total = jnp.sum(jnp.exp(targets - target_top[:, None]), axis=1)
 
@@ -491,8 +499,13 @@
         rows = slice(d * group_rows, (d + 1) * group_rows)
         return keep[rows] + other[rows]
 
-    came = [groups.shift(chip_sum(d), d) for d in range(1, groups.chips)]
-    logits = sum(came, chip_sum(0))
+    def cross(x, d):
+        largest = jnp.maximum(jnp.max(jnp.abs(x), axis=1), 1e-30)
+        code = jnp.round(x * (32767.0 / largest)[:, None]).astype(jnp.int16)
+        scale = groups.shift(largest, d) / 32767.0
+        return groups.shift(code, d).astype(F32) * scale[:, None]
+
+    logits = sum([cross(chip_sum(d), d) for d in range(1, groups.chips)], chip_sum(0))
     top = jnp.max(logits, axis=1)
     total = jnp.sum(jnp.exp(logits - top[:, None]), axis=1)
     mine = jnp.stack([jnp.concatenate([top, target_top]), jnp.concatenate([total, target_total])])
@@ -517,14 +530,11 @@
     chosen = after(own_chosen, products).reshape(CHUNKS, chunk_rows, -1)
     chosen = groups.gather(chosen).transpose(1, 0, 2, 3).reshape(CHUNKS * step_rows, -1)
 
+    def shares(product):
+        return lambda t: product[t % parts * piece_rows :][:piece_rows]
+
     grads = []
-    for h, normed_grad in enumerate(products):
-
-        def part(t):
-            first = t % parts * piece_rows
-            return normed_grad[first : first + piece_rows]
-
-        summed = ring.scatter_sum(part, h)
+    for h, summed in enumerate(ring.scatter_sums([shares(x) for x in products])):
         factor = row_factor[:, h * chunk_rows : (h + 1) * chunk_rows]
         own_factor = lax.dynamic_slice(factor, (own_entry, own_first), (1, piece_rows))[0]
         row_dot = jnp.sum(summed[:, slice_width:], axis=1) / own_factor

time: 195 us -> 181 us (0.928)
  waiting for transfers between devices: 82.8 us -> 64.6 us
  local copies, waits for them, and re-layouts: 6.92 us -> 9.87 us
    ppermute x4 -> x5, waiting for transfers between devices: 34.9 us -> 22.4 us  [shift(): lax.ppermute(x, 'dp', [(i, (i + CORES * step) % size) for i in range(size)])]
    ppermute x42, waiting for transfers between devices: 36.4 us -> 30.7 us  [shift(): lax.ppermute(x, 'vocab', [(order[p], order[(p + step) % size]) for p in r...]
    unnamed x18 -> x16, local copies, waits for them, and re-layouts: 3.83 us -> 6.79 us
    ppermute x4 -> x5, starting transfers between devices: 4.8 us -> 6.08 us  [shift(): lax.ppermute(x, 'dp', [(i, (i + CORES * step) % size) for i in range(size)])]
  transfers between devices with their start and end apart: 59 -> 60, of which waited for: 35 -> 36; matrix products, arithmetic and copies ran while one was open for 5% -> 6% of each run, Pallas kernels for 1% -> 1%
where the time goes in v11:
time: 181 us; the launch traced here: 180 us
  starting transfers between devices  65.6 us (36%)
  waiting for transfers between devices  64.6 us (36%)
  Pallas kernels  26.5 us (15%)
  other arithmetic  12.5 us (7%)
  local copies, waits for them, and re-layouts  9.87 us (5%)
    ppermute x42, starting transfers between devices, shift(): lax.ppermute(x, 'vocab', [(order[p], order[(p + step) % size]) for p in r...  43.7 us
    ppermute x42, waiting for transfers between devices, shift(): lax.ppermute(x, 'vocab', [(order[p], order[(p + step) % size]) for p in r...  30.7 us
    ppermute x5, waiting for transfers between devices, shift(): lax.ppermute(x, 'dp', [(i, (i + CORES * step) % size) for i in range(size)])  22.4 us
    ppermute x8, starting transfers between devices, partner(): return lax.ppermute(x, 'vocab', [(v, v ^ bit) for v in range(self.size)])  13.9 us
    pallas_call x1, Pallas kernels, outer(): pl.pallas_call(functools.partial(outer_kernel, len(chunks[0]), copies), g...  11.7 us
    pallas_call x1, Pallas kernels, project(): pl.pallas_call(functools.partial(project_kernel, len(blocks[0]), tile), g...  7.95 us
    unnamed x16, local copies, waits for them, and re-layouts  6.79 us
    ppermute x4, waiting for transfers between devices, swap(): return lax.ppermute(x, 'dp', [(i, i ^ 1) for i in range(self.size)])  6.33 us
  transfers between devices with their start and end apart: 60, of which 36 were waited for; matrix products, arithmetic and copies ran while one was open for 6% of the time, Pallas kernels for 1%

profile of v11, /device:TPU:0, one launch (start us, length us, event | category | flops | bytes accessed | tf_op | source)
XLA Modules:
  0.0 180.1 jit_solution(3263466876544016377)
XLA Ops:
  0.6 1.6 collective-permute-start.4
  3.3 3.0 %collective-permute-start = (f32[1,128]{1,0:T(1,128)S(1)}, f32[1,128]{1,0:T(1,128)S(1)}, u32[]{:S(2)}, u32[]{:S(2)}) collective-permute-start(f32[1,128]{1,0:T(1,128)S(1)} %bitcast.79), channel_id=1, source_target_pairs={{0,1},{1,0},{2,3},{3,2},{4,5},{5,4},{6,7},{7,6},{8,9},{9,8},{10,11... | collective-permute-start | bytes 1544 | tf_op jit(solution)/shard_map/ppermute | solution.py:47
  6.3 1.5 collective-permute-done
  7.9 5.0 %collective-permute-start.3 = (f32[1,128]{1,0:T(1,128)S(1)}, f32[1,128]{1,0:T(1,128)S(1)}, u32[]{:S(2)}, u32[]{:S(2)}) collective-permute-start(f32[1,128]{1,0:T(1,128)S(1)} %bitcast_add_fusion), channel_id=1, source_target_pairs={{0,6},{1,7},{2,4},{3,5},{4,2},{5,3},{6,0},{7,1},{8,14},{9,15},{10,... | collective-permute-start | bytes 1544 | tf_op jit(solution)/shard_map/ppermute | solution.py:47
  14.1 3.4 %copy-done = bf16[2048,2048]{1,0:T(8,128)(2,1)S(1)} copy-done((bf16[2048,2048]{1,0:T(8,128)(2,1)S(1)}, bf16[2048,2048]{1,0:T(8,128)(2,1)}, u32[]{:S(2)}) %copy-start) | copy-done | bytes 8388632
  18.2 1.6 collective-permute-start.17
  20.4 1.5 collective-permute-start.14
  22.4 2.2 %collective-permute-done.17.refs_12_ = bf16[64,1024]{1,0:T(8,128)(2,1)S(1)} collective-permute-done((bf16[64,1024]{1,0:T(8,128)(2,1)S(1)}, bf16[64,1024]{1,0:T(8,128)(2,1)S(1)}, u32[]{:S(2)}, u32[]{:S(2)}) %collective-permute-start.17) | collective-permute-done | bytes 131104 | tf_op jit(solution)/shard_map/ppermute | solution.py:42
  24.6 1.5 collective-permute-start.18
  27.6 2.5 %collective-permute-start.7 = (f32[2,128]{1,0:T(2,128)S(1)}, f32[2,128]{1,0:T(2,128)S(1)}, u32[]{:S(2)}, u32[]{:S(2)}) collective-permute-start(f32[2,128]{1,0:T(2,128)S(1)} %pad_maximum_fusion.8), channel_id=1, source_target_pairs={{0,16},{8,24},{16,0},{24,8},{1,17},{9,25},{17,1},{25,9},{2,18},{10... | collective-permute-start | bytes 3080 | tf_op jit(solution)/shard_map/ppermute | solution.py:116
  30.1 1.5 collective-permute-start.9
  32.1 1.5 collective-permute-start.19
  34.1 3.1 %collective-permute-done.15.refs_9_ = bf16[64,1024]{1,0:T(8,128)(2,1)S(1)} collective-permute-done((bf16[64,1024]{1,0:T(8,128)(2,1)S(1)}, bf16[64,1024]{1,0:T(8,128)(2,1)S(1)}, u32[]{:S(2)}, u32[]{:S(2)}) %collective-permute-start.15) | collective-permute-done | bytes 131104 | tf_op jit(solution)/shard_map/ppermute | solution.py:42
  37.8 1.5 collective-permute-start.13
  42.1 1.4 dynamic_slice.13
  45.0 7.9 %shard_map.97 = (f32[256,2048]{1,0:T(8,128)S(1)}, f32[256,2048]{1,0:T(8,128)S(1)}, bf16[32,2048]{1,0:T(8,128)(2,1)S(1)}, bf16[32,2048]{1,0:T(8,128)(2,1)S(1)}) custom-call(s32[34]{0:T(128)S(1)} %slice_bitcast_fusion.index_ref, f32[4,128]{1,0:T(4,128)S(1)} %get-tuple-element.77.factor_ref, f32[1,2048]{1,0:T(1,128)S(1)} %bitcast.59, ...), custom_call_target="tpu_custom_call" | custom-call | flops 4294967296 | bytes 14680064 | tf_op jit(solution)/shard_map/pallas_call | solution.py:229
  53.1 4.1 %collective-permute-done.21 = f32[256,2048]{1,0:T(8,128)S(1)} collective-permute-done((f32[256,2048]{1,0:T(8,128)S(1)}, f32[256,2048]{1,0:T(8,128)S(1)}, u32[]{:S(2)}, u32[]{:S(2)}) %collective-permute-start.21) | collective-permute-done | bytes 2097184 | tf_op jit(solution)/shard_map/ppermute | solution.py:112
  60.9 12.0 %collective-permute-done.23 = f32[128]{0:T(128)S(1)} collective-permute-done((f32[128]{0:T(128)S(1)}, f32[128]{0:T(128)S(1)}, u32[]{:S(2)}, u32[]{:S(2)}) %collective-permute-start.23) | collective-permute-done | bytes 544 | tf_op jit(solution)/shard_map/ppermute | solution.py:116
  72.9 1.6 fusion.26
  76.9 1.8 collective-permute-done.24
  78.8 1.9 %collective-permute-start.27 = (f32[2,256]{1,0:T(2,128)S(1)}, f32[2,256]{1,0:T(2,128)S(1)}, u32[]{:S(2)}, u32[]{:S(2)}) collective-permute-start(f32[2,256]{1,0:T(2,128)S(1)} %pad_maximum_fusion.7), channel_id=1, source_target_pairs={{0,6},{1,7},{2,4},{3,5},{4,2},{5,3},{6,0},{7,1},{8,14},{9,15},{10,... | collective-permute-start | bytes 6152 | tf_op jit(solution)/shard_map/ppermute | solution.py:47
  82.3 1.7 collective-permute-start.25
  84.2 1.6 collective-permute-done.26
  87.6 10.4 %collective-permute-done.28 = bf16[128,2176]{1,0:T(8,128)(2,1)S(1)} collective-permute-done((bf16[128,2176]{1,0:T(8,128)(2,1)S(1)}, bf16[128,2176]{1,0:T(8,128)(2,1)S(1)}, u32[]{:S(2)}, u32[]{:S(2)}) %collective-permute-start.28) | collective-permute-done | bytes 557088 | tf_op jit(solution)/shard_map/ppermute | solution.py:116
  98.8 2.2 %collective-permute-done.29.other_ref = bf16[2,128,2176]{2,1,0:T(8,128)(2,1)S(1)} collective-permute-done((bf16[2,128,2176]{2,1,0:T(8,128)(2,1)S(1)}, bf16[2,128,2176]{2,1,0:T(8,128)(2,1)S(1)}, u32[]{:S(2)}, u32[]{:S(2)}) %collective-permute-start.29) | collective-permute-done | bytes 1114144 | tf_op jit(solution)/shard_map/ppermute | solution.py:112
  100.9 3.4 %copy-done.2 = bf16[2048,2048]{1,0:T(8,128)(2,1)S(1)} copy-done((bf16[2048,2048]{1,0:T(8,128)(2,1)S(1)}, bf16[2048,2048]{1,0:T(8,128)(2,1)}, u32[]{:S(2)}) %copy-start.2) | copy-done | bytes 8388632
  104.3 5.9 %shard_map.98 = (f32[256,2176]{1,0:T(8,128)S(1)}, f32[256,2176]{1,0:T(8,128)S(1)}) custom-call(s32[8]{0:T(128)S(1)} %slice_bitcast_fusion.1.index_ref, bf16[2,128,2176]{2,1,0:T(8,128)(2,1)S(1)} %pad_maximum_fusion.2.mine_ref, bf16[2,128,2176]{2,1,0:T(8,128)(2,1)S(1)} %collective-permute-done.29.other_ref, bf16[2048,2048]{1,0:T(8,128)(2,1)S(1)} %copy-done.2), custom_call_target="tpu_custom_call" | custom-call | flops 4294967296 | bytes 14680064 | tf_op jit(solution)/shard_map/pallas_call | solution.py:280
  111.1 1.7 collective-permute-start.32
  113.2 3.3 %collective-permute-done.32 = bf16[32,2176]{1,0:T(8,128)(2,1)S(1)} collective-permute-done((bf16[32,2176]{1,0:T(8,128)(2,1)S(1)}, bf16[32,2176]{1,0:T(8,128)(2,1)S(1)}, u32[]{:S(2)}, u32[]{:S(2)}) %collective-permute-start.32) | collective-permute-done | bytes 139296 | tf_op jit(solution)/shard_map/ppermute | solution.py:42
  116.6 1.7 collective-permute-start.33
  120.8 1.8 %collective-permute-done.33 = bf16[32,2176]{1,0:T(8,128)(2,1)S(1)} collective-permute-done((bf16[32,2176]{1,0:T(8,128)(2,1)S(1)}, bf16[32,2176]{1,0:T(8,128)(2,1)S(1)}, u32[]{:S(2)}, u32[]{:S(2)}) %collective-permute-start.33) | collective-permute-done | bytes 139296 | tf_op jit(solution)/shard_map/ppermute | solution.py:42
  122.6 1.6 collective-permute-done.34
  124.7 1.7 collective-permute-start.35
  127.6 1.7 collective-permute-start.49
  132.4 1.4 collective-permute-done.50
  134.2 1.5 collective-permute-start.52
  136.4 2.9 %collective-permute-done.52 = bf16[32,2176]{1,0:T(8,128)(2,1)S(1)} collective-permute-done((bf16[32,2176]{1,0:T(8,128)(2,1)S(1)}, bf16[32,2176]{1,0:T(8,128)(2,1)S(1)}, u32[]{:S(2)}, u32[]{:S(2)}) %collective-permute-start.52) | collective-permute-done | bytes 139296 | tf_op jit(solution)/shard_map/ppermute | solution.py:42
  139.3 1.4 collective-permute-done.51
  144.8 1.5 collective-permute-start.39
  146.9 1.4 collective-permute-start.43
  148.3 2.2 %collective-permute-done.56.refs_12_ = bf16[32,2048]{1,0:T(8,128)(2,1)S(1)} collective-permute-done((bf16[32,2048]{1,0:T(8,128)(2,1)S(1)}, bf16[32,2048]{1,0:T(8,128)(2,1)S(1)}, u32[]{:S(2)}, u32[]{:S(2)}) %collective-permute-start.56) | collective-permute-done | bytes 131104 | tf_op jit(solution)/shard_map/ppermute | solution.py:42
  151.2 1.5 collective-permute-start.40
  153.7 1.5 collective-permute-start.54
  157.1 1.5 collective-permute-start.41
  158.6 1.4 collective-permute-done.54.refs_9_
  160.0 1.6 collective-permute-start.55
  163.4 1.5 collective-permute-start.42
  168.4 11.7 %shard_map.99 = (f32[2048,3072]{1,0:T(8,128)}, bf16[64,2048]{1,0:T(8,128)(2,1)}) custom-call(s32[17]{0:T(128)S(1)} %slice_bitcast_fusion.2.index_ref, bf16[512,3072]{1,0:T(8,128)(2,1)S(1)} %bitcast.58, bf16[32,2048]{1,0:T(8,128)(2,1)S(1)} %collective-permute-done.42.refs_0_, bf16[32,2048]{1,0:T(8,128)(2,1)S(1)} %collective-permute-done.41.refs_1_, ...), custom_call_target="tpu_custom_call" | custom-call | flops 6442450944 | bytes 30408704 | tf_op jit(solution)/shard_map/pallas_call | solution.py:347
  (153 shorter events, 45.3 us)
Async XLA Ops:
  0.6 17.6 %collective-permute-start.4 = (bf16[128,1024]{1,0:T(8,128)(2,1)}, bf16[128,1024]{1,0:T(8,128)(2,1)S(1)}, u32[]{:S(2)}, u32[]{:S(2)}) collective-permute-start(bf16[128,1024]{1,0:T(8,128)(2,1)} %param.8), channel_id=1, source_target_pairs={{0,0},{1,1},{2,8},{3,9},{4,16},{5,17},{6,24},{7,25},{8,4},{9,5},{1... | collective-permute-start | bytes 786440 | tf_op jit(solution)/shard_map/ppermute | solution.py:455
  7.9 10.3 %collective-permute-start.3 = (f32[1,128]{1,0:T(1,128)S(1)}, f32[1,128]{1,0:T(1,128)S(1)}, u32[]{:S(2)}, u32[]{:S(2)}) collective-permute-start(f32[1,128]{1,0:T(1,128)S(1)} %bitcast_add_fusion), channel_id=1, source_target_pairs={{0,6},{1,7},{2,4},{3,5},{4,2},{5,3},{6,0},{7,1},{8,14},{9,15},{10,... | collective-permute-start | bytes 1544 | tf_op jit(solution)/shard_map/ppermute | solution.py:47
  12.9 5.3 %collective-permute-start.2 = (f32[1,128]{1,0:T(1,128)S(1)}, f32[1,128]{1,0:T(1,128)S(1)}, u32[]{:S(2)}, u32[]{:S(2)}) collective-permute-start(f32[1,128]{1,0:T(1,128)S(1)} %bitcast_add_fusion), channel_id=1, source_target_pairs={{0,4},{1,5},{2,6},{3,7},{4,0},{5,1},{6,2},{7,3},{8,12},{9,13},{10,... | collective-permute-start | bytes 1544 | tf_op jit(solution)/shard_map/ppermute | solution.py:47
  12.9 5.3 %collective-permute-start.1 = (f32[1,128]{1,0:T(1,128)S(1)}, f32[1,128]{1,0:T(1,128)S(1)}, u32[]{:S(2)}, u32[]{:S(2)}) collective-permute-start(f32[1,128]{1,0:T(1,128)S(1)} %bitcast_add_fusion), channel_id=1, source_target_pairs={{0,2},{1,3},{2,0},{3,1},{4,6},{5,7},{6,4},{7,5},{8,10},{9,11},{10,... | collective-permute-start | bytes 1544 | tf_op jit(solution)/shard_map/ppermute | solution.py:47
  18.2 6.4 %collective-permute-start.17 = (bf16[64,1024]{1,0:T(8,128)(2,1)S(1)}, bf16[64,1024]{1,0:T(8,128)(2,1)S(1)}, u32[]{:S(2)}, u32[]{:S(2)}) collective-permute-start(bf16[64,1024]{1,0:T(8,128)(2,1)S(1)} %get-tuple-element.72.refs_11_), channel_id=1, source_target_pairs={{0,1},{2,0},{4,2},{6,4},{7,6},{5,7},{3,5},{1,3},{8,9},{10,8},{12,1... | collective-permute-start | bytes 393224 | tf_op jit(solution)/shard_map/ppermute | solution.py:42
  19.8 6.4 %collective-permute-start.5 = (bf16[64,1024]{1,0:T(8,128)(2,1)S(1)}, bf16[64,1024]{1,0:T(8,128)(2,1)S(1)}, u32[]{:S(2)}, u32[]{:S(2)}) collective-permute-start(bf16[64,1024]{1,0:T(8,128)(2,1)S(1)} %get-tuple-element.73.refs_4_), channel_id=1, source_target_pairs={{0,2},{2,4},{4,6},{6,7},{7,5},{5,3},{3,1},{1,0},{8,10},{10,12},{12... | collective-permute-start | bytes 393224 | tf_op jit(solution)/shard_map/ppermute | solution.py:42
  20.4 11.2 %collective-permute-start.14 = (bf16[64,1024]{1,0:T(8,128)(2,1)S(1)}, bf16[64,1024]{1,0:T(8,128)(2,1)S(1)}, u32[]{:S(2)}, u32[]{:S(2)}) collective-permute-start(bf16[64,1024]{1,0:T(8,128)(2,1)S(1)} %get-tuple-element.72.refs_11_), channel_id=1, source_target_pairs={{0,2},{2,4},{4,6},{6,7},{7,5},{5,3},{3,1},{1,0},{8,10},{10,12},{12... | collective-permute-start | bytes 393224 | tf_op jit(solution)/shard_map/ppermute | solution.py:42
  21.8 5.7 %collective-permute-start.6 = (bf16[64,1024]{1,0:T(8,128)(2,1)S(1)}, bf16[64,1024]{1,0:T(8,128)(2,1)S(1)}, u32[]{:S(2)}, u32[]{:S(2)}) collective-permute-start(bf16[64,1024]{1,0:T(8,128)(2,1)S(1)} %get-tuple-element.73.refs_4_), channel_id=1, source_target_pairs={{0,1},{2,0},{4,2},{6,4},{7,6},{5,7},{3,5},{1,3},{8,9},{10,8},{12,1... | collective-permute-start | bytes 393224 | tf_op jit(solution)/shard_map/ppermute | solution.py:42
  24.6 7.5 %collective-permute-start.18 = (bf16[64,1024]{1,0:T(8,128)(2,1)S(1)}, bf16[64,1024]{1,0:T(8,128)(2,1)S(1)}, u32[]{:S(2)}, u32[]{:S(2)}) collective-permute-start(bf16[64,1024]{1,0:T(8,128)(2,1)S(1)} %collective-permute-done.17.refs_12_), channel_id=1, source_target_pairs={{0,1},{2,0},{4,2},{6,4},{7,6},{5,7},{3,5},{1,3},{8,9},{10,8},{12,1... | collective-permute-start | bytes 393224 | tf_op jit(solution)/shard_map/ppermute | solution.py:42
  26.2 7.4 %collective-permute-start.8 = (bf16[64,1024]{1,0:T(8,128)(2,1)S(1)}, bf16[64,1024]{1,0:T(8,128)(2,1)S(1)}, u32[]{:S(2)}, u32[]{:S(2)}) collective-permute-start(bf16[64,1024]{1,0:T(8,128)(2,1)S(1)} %collective-permute-done.5.refs_3_), channel_id=1, source_target_pairs={{0,2},{2,4},{4,6},{6,7},{7,5},{5,3},{3,1},{1,0},{8,10},{10,12},{12... | collective-permute-start | bytes 393224 | tf_op jit(solution)/shard_map/ppermute | solution.py:42
  27.6 13.8 %collective-permute-start.7 = (f32[2,128]{1,0:T(2,128)S(1)}, f32[2,128]{1,0:T(2,128)S(1)}, u32[]{:S(2)}, u32[]{:S(2)}) collective-permute-start(f32[2,128]{1,0:T(2,128)S(1)} %pad_maximum_fusion.8), channel_id=1, source_target_pairs={{0,16},{8,24},{16,0},{24,8},{1,17},{9,25},{17,1},{25,9},{2,18},{10... | collective-permute-start | bytes 3080 | tf_op jit(solution)/shard_map/ppermute | solution.py:116
  30.1 7.7 %collective-permute-start.9 = (bf16[64,1024]{1,0:T(8,128)(2,1)S(1)}, bf16[64,1024]{1,0:T(8,128)(2,1)S(1)}, u32[]{:S(2)}, u32[]{:S(2)}) collective-permute-start(bf16[64,1024]{1,0:T(8,128)(2,1)S(1)} %collective-permute-done.6.refs_5_), channel_id=1, source_target_pairs={{0,1},{2,0},{4,2},{6,4},{7,6},{5,7},{3,5},{1,3},{8,9},{10,8},{12,1... | collective-permute-start | bytes 393224 | tf_op jit(solution)/shard_map/ppermute | solution.py:42
  31.6 5.7 %collective-permute-start.15 = (bf16[64,1024]{1,0:T(8,128)(2,1)S(1)}, bf16[64,1024]{1,0:T(8,128)(2,1)S(1)}, u32[]{:S(2)}, u32[]{:S(2)}) collective-permute-start(bf16[64,1024]{1,0:T(8,128)(2,1)S(1)} %collective-permute-done.14.refs_10_), channel_id=1, source_target_pairs={{0,2},{2,4},{4,6},{6,7},{7,5},{5,3},{3,1},{1,0},{8,10},{10,12},{12... | collective-permute-start | bytes 393224 | tf_op jit(solution)/shard_map/ppermute | solution.py:42
  32.1 7.2 %collective-permute-start.19 = (bf16[64,1024]{1,0:T(8,128)(2,1)S(1)}, bf16[64,1024]{1,0:T(8,128)(2,1)S(1)}, u32[]{:S(2)}, u32[]{:S(2)}) collective-permute-start(bf16[64,1024]{1,0:T(8,128)(2,1)S(1)} %collective-permute-done.18.refs_13_), channel_id=1, source_target_pairs={{0,1},{2,0},{4,2},{6,4},{7,6},{5,7},{3,5},{1,3},{8,9},{10,8},{12,1... | collective-permute-start | bytes 393224 | tf_op jit(solution)/shard_map/ppermute | solution.py:42
  33.6 6.5 %collective-permute-start.11 = (bf16[64,1024]{1,0:T(8,128)(2,1)S(1)}, bf16[64,1024]{1,0:T(8,128)(2,1)S(1)}, u32[]{:S(2)}, u32[]{:S(2)}) collective-permute-start(bf16[64,1024]{1,0:T(8,128)(2,1)S(1)} %collective-permute-done.8.refs_2_), channel_id=1, source_target_pairs={{0,2},{2,4},{4,6},{6,7},{7,5},{5,3},{3,1},{1,0},{8,10},{10,12},{12... | collective-permute-start | bytes 393224 | tf_op jit(solution)/shard_map/ppermute | solution.py:42
  37.3 6.9 %collective-permute-start.16 = (bf16[64,1024]{1,0:T(8,128)(2,1)S(1)}, bf16[64,1024]{1,0:T(8,128)(2,1)S(1)}, u32[]{:S(2)}, u32[]{:S(2)}) collective-permute-start(bf16[64,1024]{1,0:T(8,128)(2,1)S(1)} %collective-permute-done.15.refs_9_), channel_id=1, source_target_pairs={{0,2},{2,4},{4,6},{6,7},{7,5},{5,3},{3,1},{1,0},{8,10},{10,12},{12... | collective-permute-start | bytes 393224 | tf_op jit(solution)/shard_map/ppermute | solution.py:42
  37.8 6.4 %collective-permute-start.13 = (bf16[64,1024]{1,0:T(8,128)(2,1)S(1)}, bf16[64,1024]{1,0:T(8,128)(2,1)S(1)}, u32[]{:S(2)}, u32[]{:S(2)}) collective-permute-start(bf16[64,1024]{1,0:T(8,128)(2,1)S(1)} %collective-permute-done.9.refs_6_), channel_id=1, source_target_pairs={{0,1},{2,0},{4,2},{6,4},{7,6},{5,7},{3,5},{1,3},{8,9},{10,8},{12,1... | collective-permute-start | bytes 393224 | tf_op jit(solution)/shard_map/ppermute | solution.py:42
  58.7 14.2 %collective-permute-start.22 = (s16[128,2048]{1,0:T(8,128)(2,1)}, s16[128,2048]{1,0:T(8,128)(2,1)S(1)}, u32[]{:S(2)}, u32[]{:S(2)}) collective-permute-start(s16[128,2048]{1,0:T(8,128)(2,1)} %round-nearest-even_convert_fusion), channel_id=1, source_target_pairs={{0,16},{8,24},{16,0},{24,8},{1,17},{9,25},{17,1},{25,9},{2,18},{10... | collective-permute-start | bytes 1572872 | tf_op jit(solution)/shard_map/ppermute | solution.py:116
  59.7 13.3 %collective-permute-start.23 = (f32[128]{0:T(128)S(1)}, f32[128]{0:T(128)S(1)}, u32[]{:S(2)}, u32[]{:S(2)}) collective-permute-start(f32[128]{0:T(128)S(1)} %get-tuple-element.102), channel_id=1, source_target_pairs={{0,16},{8,24},{16,0},{24,8},{1,17},{9,25},{17,1},{25,9},{2,18},{10... | collective-permute-start | bytes 1544 | tf_op jit(solution)/shard_map/ppermute | solution.py:116
  78.8 5.4 %collective-permute-start.27 = (f32[2,256]{1,0:T(2,128)S(1)}, f32[2,256]{1,0:T(2,128)S(1)}, u32[]{:S(2)}, u32[]{:S(2)}) collective-permute-start(f32[2,256]{1,0:T(2,128)S(1)} %pad_maximum_fusion.7), channel_id=1, source_target_pairs={{0,6},{1,7},{2,4},{3,5},{4,2},{5,3},{6,0},{7,1},{8,14},{9,15},{10,... | collective-permute-start | bytes 6152 | tf_op jit(solution)/shard_map/ppermute | solution.py:47
  86.8 11.2 %collective-permute-start.28 = (bf16[128,2176]{1,0:T(8,128)(2,1)S(1)}, bf16[128,2176]{1,0:T(8,128)(2,1)S(1)}, u32[]{:S(2)}, u32[]{:S(2)}) collective-permute-start(bf16[128,2176]{1,0:T(8,128)(2,1)S(1)} %get-tuple-element.71), channel_id=1, source_target_pairs={{0,16},{8,24},{16,0},{24,8},{1,17},{9,25},{17,1},{25,9},{2,18},{10... | collective-permute-start | bytes 1671176 | tf_op jit(solution)/shard_map/ppermute | solution.py:116
  110.4 30.3 %collective-permute-start.30 = (bf16[2,64,3072]{2,1,0:T(8,128)(2,1)S(1)}, bf16[2,64,3072]{2,1,0:T(8,128)(2,1)S(1)}, u32[]{:S(2)}, u32[]{:S(2)}) collective-permute-start(bf16[2,64,3072]{2,1,0:T(8,128)(2,1)S(1)} %bitcast.55), channel_id=1, source_target_pairs={{0,16},{8,24},{16,0},{24,8},{1,17},{9,25},{17,1},{25,9},{2,18},{10... | collective-permute-start | bytes 2359304 | tf_op jit(solution)/shard_map/ppermute | solution.py:116
  111.1 5.5 %collective-permute-start.32 = (bf16[32,2176]{1,0:T(8,128)(2,1)S(1)}, bf16[32,2176]{1,0:T(8,128)(2,1)S(1)}, u32[]{:S(2)}, u32[]{:S(2)}) collective-permute-start(bf16[32,2176]{1,0:T(8,128)(2,1)S(1)} %get-tuple-element.68), channel_id=1, source_target_pairs={{0,2},{2,4},{4,6},{6,7},{7,5},{5,3},{3,1},{1,0},{8,10},{10,12},{12... | collective-permute-start | bytes 417800 | tf_op jit(solution)/shard_map/ppermute | solution.py:42
  112.8 5.9 %collective-permute-start.46 = (bf16[32,2176]{1,0:T(8,128)(2,1)S(1)}, bf16[32,2176]{1,0:T(8,128)(2,1)S(1)}, u32[]{:S(2)}, u32[]{:S(2)}) collective-permute-start(bf16[32,2176]{1,0:T(8,128)(2,1)S(1)} %get-tuple-element.67), channel_id=1, source_target_pairs={{0,1},{2,0},{4,2},{6,4},{7,6},{5,7},{3,5},{1,3},{8,9},{10,8},{12,1... | collective-permute-start | bytes 417800 | tf_op jit(solution)/shard_map/ppermute | solution.py:42
  116.6 6.0 %collective-permute-start.33 = (bf16[32,2176]{1,0:T(8,128)(2,1)S(1)}, bf16[32,2176]{1,0:T(8,128)(2,1)S(1)}, u32[]{:S(2)}, u32[]{:S(2)}) collective-permute-start(bf16[32,2176]{1,0:T(8,128)(2,1)S(1)} %add_convert_fusion.9), channel_id=1, source_target_pairs={{0,2},{2,4},{4,6},{6,7},{7,5},{5,3},{3,1},{1,0},{8,10},{10,12},{12... | collective-permute-start | bytes 417800 | tf_op jit(solution)/shard_map/ppermute | solution.py:42
  118.3 5.9 %collective-permute-start.34 = (bf16[32,2176]{1,0:T(8,128)(2,1)S(1)}, bf16[32,2176]{1,0:T(8,128)(2,1)S(1)}, u32[]{:S(2)}, u32[]{:S(2)}) collective-permute-start(bf16[32,2176]{1,0:T(8,128)(2,1)S(1)} %get-tuple-element.35), channel_id=1, source_target_pairs={{0,1},{2,0},{4,2},{6,4},{7,6},{5,7},{3,5},{1,3},{8,9},{10,8},{12,1... | collective-permute-start | bytes 417800 | tf_op jit(solution)/shard_map/ppermute | solution.py:42
  118.7 8.4 %collective-permute-start.48 = (bf16[32,2176]{1,0:T(8,128)(2,1)S(1)}, bf16[32,2176]{1,0:T(8,128)(2,1)S(1)}, u32[]{:S(2)}, u32[]{:S(2)}) collective-permute-start(bf16[32,2176]{1,0:T(8,128)(2,1)S(1)} %add_convert_fusion.3), channel_id=1, source_target_pairs={{0,1},{2,0},{4,2},{6,4},{7,6},{5,7},{3,5},{1,3},{8,9},{10,8},{12,1... | collective-permute-start | bytes 417800 | tf_op jit(solution)/shard_map/ppermute | solution.py:42
  120.1 7.1 %collective-permute-start.47 = (bf16[32,2176]{1,0:T(8,128)(2,1)S(1)}, bf16[32,2176]{1,0:T(8,128)(2,1)S(1)}, u32[]{:S(2)}, u32[]{:S(2)}) collective-permute-start(bf16[32,2176]{1,0:T(8,128)(2,1)S(1)} %get-tuple-element.41), channel_id=1, source_target_pairs={{0,2},{2,4},{4,6},{6,7},{7,5},{5,3},{3,1},{1,0},{8,10},{10,12},{12... | collective-permute-start | bytes 417800 | tf_op jit(solution)/shard_map/ppermute | solution.py:42
  124.3 6.0 %collective-permute-start.36 = (bf16[32,2176]{1,0:T(8,128)(2,1)S(1)}, bf16[32,2176]{1,0:T(8,128)(2,1)S(1)}, u32[]{:S(2)}, u32[]{:S(2)}) collective-permute-start(bf16[32,2176]{1,0:T(8,128)(2,1)S(1)} %get-tuple-element.37), channel_id=1, source_target_pairs={{0,1},{2,0},{4,2},{6,4},{7,6},{5,7},{3,5},{1,3},{8,9},{10,8},{12,1... | collective-permute-start | bytes 417800 | tf_op jit(solution)/shard_map/ppermute | solution.py:42
  124.7 5.6 %collective-permute-start.35 = (bf16[32,2176]{1,0:T(8,128)(2,1)S(1)}, bf16[32,2176]{1,0:T(8,128)(2,1)S(1)}, u32[]{:S(2)}, u32[]{:S(2)}) collective-permute-start(bf16[32,2176]{1,0:T(8,128)(2,1)S(1)} %get-tuple-element.36), channel_id=1, source_target_pairs={{0,2},{2,4},{4,6},{6,7},{7,5},{5,3},{3,1},{1,0},{8,10},{10,12},{12... | collective-permute-start | bytes 417800 | tf_op jit(solution)/shard_map/ppermute | solution.py:42
  127.2 6.6 %collective-permute-start.50 = (bf16[32,2176]{1,0:T(8,128)(2,1)S(1)}, bf16[32,2176]{1,0:T(8,128)(2,1)S(1)}, u32[]{:S(2)}, u32[]{:S(2)}) collective-permute-start(bf16[32,2176]{1,0:T(8,128)(2,1)S(1)} %get-tuple-element.44), channel_id=1, source_target_pairs={{0,1},{2,0},{4,2},{6,4},{7,6},{5,7},{3,5},{1,3},{8,9},{10,8},{12,1... | collective-permute-start | bytes 417800 | tf_op jit(solution)/shard_map/ppermute | solution.py:42
  127.6 6.5 %collective-permute-start.49 = (bf16[32,2176]{1,0:T(8,128)(2,1)S(1)}, bf16[32,2176]{1,0:T(8,128)(2,1)S(1)}, u32[]{:S(2)}, u32[]{:S(2)}) collective-permute-start(bf16[32,2176]{1,0:T(8,128)(2,1)S(1)} %get-tuple-element.43), channel_id=1, source_target_pairs={{0,2},{2,4},{4,6},{6,7},{7,5},{5,3},{3,1},{1,0},{8,10},{10,12},{12... | collective-permute-start | bytes 417800 | tf_op jit(solution)/shard_map/ppermute | solution.py:42
  130.3 5.9 %collective-permute-start.38 = (bf16[32,2176]{1,0:T(8,128)(2,1)S(1)}, bf16[32,2176]{1,0:T(8,128)(2,1)S(1)}, u32[]{:S(2)}, u32[]{:S(2)}) collective-permute-start(bf16[32,2176]{1,0:T(8,128)(2,1)S(1)} %get-tuple-element.39), channel_id=1, source_target_pairs={{0,1},{2,0},{4,2},{6,4},{7,6},{5,7},{3,5},{1,3},{8,9},{10,8},{12,1... | collective-permute-start | bytes 417800 | tf_op jit(solution)/shard_map/ppermute | solution.py:42
  131.3 5.1 %collective-permute-start.37 = (bf16[32,2176]{1,0:T(8,128)(2,1)S(1)}, bf16[32,2176]{1,0:T(8,128)(2,1)S(1)}, u32[]{:S(2)}, u32[]{:S(2)}) collective-permute-start(bf16[32,2176]{1,0:T(8,128)(2,1)S(1)} %get-tuple-element.38), channel_id=1, source_target_pairs={{0,2},{2,4},{4,6},{6,7},{7,5},{5,3},{3,1},{1,0},{8,10},{10,12},{12... | collective-permute-start | bytes 417800 | tf_op jit(solution)/shard_map/ppermute | solution.py:42
  134.2 5.1 %collective-permute-start.52 = (bf16[32,2176]{1,0:T(8,128)(2,1)S(1)}, bf16[32,2176]{1,0:T(8,128)(2,1)S(1)}, u32[]{:S(2)}, u32[]{:S(2)}) collective-permute-start(bf16[32,2176]{1,0:T(8,128)(2,1)S(1)} %get-tuple-element.46), channel_id=1, source_target_pairs={{0,1},{2,0},{4,2},{6,4},{7,6},{5,7},{3,5},{1,3},{8,9},{10,8},{12,1... | collective-permute-start | bytes 417800 | tf_op jit(solution)/shard_map/ppermute | solution.py:42
  140.9 24.0 %collective-permute-start.31 = (bf16[2,2,64,3072]{3,2,0,1:T(8,128)(2,1)S(1)}, bf16[2,2,64,3072]{3,2,0,1:T(8,128)(2,1)S(1)}, u32[]{:S(2)}, u32[]{:S(2)}) collective-permute-start(bf16[2,2,64,3072]{3,2,0,1:T(8,128)(2,1)S(1)} %pad_maximum_fusion.1), channel_id=1, source_target_pairs={{0,8},{8,0},{16,24},{24,16},{1,9},{9,1},{17,25},{25,17},{2,10},{10... | collective-permute-start | bytes 4718600 | tf_op jit(solution)/shard_map/ppermute | solution.py:112
  144.2 6.3 %collective-permute-start.56 = (bf16[32,2048]{1,0:T(8,128)(2,1)S(1)}, bf16[32,2048]{1,0:T(8,128)(2,1)S(1)}, u32[]{:S(2)}, u32[]{:S(2)}) collective-permute-start(bf16[32,2048]{1,0:T(8,128)(2,1)S(1)} %get-tuple-element.74.refs_11_), channel_id=1, source_target_pairs={{0,1},{2,0},{4,2},{6,4},{7,6},{5,7},{3,5},{1,3},{8,9},{10,8},{12,1... | collective-permute-start | bytes 393224 | tf_op jit(solution)/shard_map/ppermute | solution.py:42
  144.8 6.3 %collective-permute-start.39 = (bf16[32,2048]{1,0:T(8,128)(2,1)S(1)}, bf16[32,2048]{1,0:T(8,128)(2,1)S(1)}, u32[]{:S(2)}, u32[]{:S(2)}) collective-permute-start(bf16[32,2048]{1,0:T(8,128)(2,1)S(1)} %get-tuple-element.75.refs_4_), channel_id=1, source_target_pairs={{0,2},{2,4},{4,6},{6,7},{7,5},{5,3},{3,1},{1,0},{8,10},{10,12},{12... | collective-permute-start | bytes 393224 | tf_op jit(solution)/shard_map/ppermute | solution.py:42
  146.3 7.4 %collective-permute-start.53 = (bf16[32,2048]{1,0:T(8,128)(2,1)S(1)}, bf16[32,2048]{1,0:T(8,128)(2,1)S(1)}, u32[]{:S(2)}, u32[]{:S(2)}) collective-permute-start(bf16[32,2048]{1,0:T(8,128)(2,1)S(1)} %get-tuple-element.74.refs_11_), channel_id=1, source_target_pairs={{0,2},{2,4},{4,6},{6,7},{7,5},{5,3},{3,1},{1,0},{8,10},{10,12},{12... | collective-permute-start | bytes 393224 | tf_op jit(solution)/shard_map/ppermute | solution.py:42
  146.9 8.3 %collective-permute-start.43 = (bf16[32,2048]{1,0:T(8,128)(2,1)S(1)}, bf16[32,2048]{1,0:T(8,128)(2,1)S(1)}, u32[]{:S(2)}, u32[]{:S(2)}) collective-permute-start(bf16[32,2048]{1,0:T(8,128)(2,1)S(1)} %get-tuple-element.75.refs_4_), channel_id=1, source_target_pairs={{0,1},{2,0},{4,2},{6,4},{7,6},{5,7},{3,5},{1,3},{8,9},{10,8},{12,1... | collective-permute-start | bytes 393224 | tf_op jit(solution)/shard_map/ppermute | solution.py:42
  150.5 5.2 %collective-permute-start.57 = (bf16[32,2048]{1,0:T(8,128)(2,1)S(1)}, bf16[32,2048]{1,0:T(8,128)(2,1)S(1)}, u32[]{:S(2)}, u32[]{:S(2)}) collective-permute-start(bf16[32,2048]{1,0:T(8,128)(2,1)S(1)} %collective-permute-done.56.refs_12_), channel_id=1, source_target_pairs={{0,1},{2,0},{4,2},{6,4},{7,6},{5,7},{3,5},{1,3},{8,9},{10,8},{12,1... | collective-permute-start | bytes 393224 | tf_op jit(solution)/shard_map/ppermute | solution.py:42
  151.2 5.9 %collective-permute-start.40 = (bf16[32,2048]{1,0:T(8,128)(2,1)S(1)}, bf16[32,2048]{1,0:T(8,128)(2,1)S(1)}, u32[]{:S(2)}, u32[]{:S(2)}) collective-permute-start(bf16[32,2048]{1,0:T(8,128)(2,1)S(1)} %collective-permute-done.39.refs_3_), channel_id=1, source_target_pairs={{0,2},{2,4},{4,6},{6,7},{7,5},{5,3},{3,1},{1,0},{8,10},{10,12},{12... | collective-permute-start | bytes 393224 | tf_op jit(solution)/shard_map/ppermute | solution.py:42
  153.7 6.3 %collective-permute-start.54 = (bf16[32,2048]{1,0:T(8,128)(2,1)S(1)}, bf16[32,2048]{1,0:T(8,128)(2,1)S(1)}, u32[]{:S(2)}, u32[]{:S(2)}) collective-permute-start(bf16[32,2048]{1,0:T(8,128)(2,1)S(1)} %collective-permute-done.53.refs_10_), channel_id=1, source_target_pairs={{0,2},{2,4},{4,6},{6,7},{7,5},{5,3},{3,1},{1,0},{8,10},{10,12},{12... | collective-permute-start | bytes 393224 | tf_op jit(solution)/shard_map/ppermute | solution.py:42
  155.1 6.4 %collective-permute-start.44 = (bf16[32,2048]{1,0:T(8,128)(2,1)S(1)}, bf16[32,2048]{1,0:T(8,128)(2,1)S(1)}, u32[]{:S(2)}, u32[]{:S(2)}) collective-permute-start(bf16[32,2048]{1,0:T(8,128)(2,1)S(1)} %collective-permute-done.43.refs_5_), channel_id=1, source_target_pairs={{0,1},{2,0},{4,2},{6,4},{7,6},{5,7},{3,5},{1,3},{8,9},{10,8},{12,1... | collective-permute-start | bytes 393224 | tf_op jit(solution)/shard_map/ppermute | solution.py:42
  155.8 6.6 %collective-permute-start.58 = (bf16[32,2048]{1,0:T(8,128)(2,1)S(1)}, bf16[32,2048]{1,0:T(8,128)(2,1)S(1)}, u32[]{:S(2)}, u32[]{:S(2)}) collective-permute-start(bf16[32,2048]{1,0:T(8,128)(2,1)S(1)} %collective-permute-done.57.refs_13_), channel_id=1, source_target_pairs={{0,1},{2,0},{4,2},{6,4},{7,6},{5,7},{3,5},{1,3},{8,9},{10,8},{12,1... | collective-permute-start | bytes 393224 | tf_op jit(solution)/shard_map/ppermute | solution.py:42
  157.1 6.4 %collective-permute-start.41 = (bf16[32,2048]{1,0:T(8,128)(2,1)S(1)}, bf16[32,2048]{1,0:T(8,128)(2,1)S(1)}, u32[]{:S(2)}, u32[]{:S(2)}) collective-permute-start(bf16[32,2048]{1,0:T(8,128)(2,1)S(1)} %collective-permute-done.40.refs_2_), channel_id=1, source_target_pairs={{0,2},{2,4},{4,6},{6,7},{7,5},{5,3},{3,1},{1,0},{8,10},{10,12},{12... | collective-permute-start | bytes 393224 | tf_op jit(solution)/shard_map/ppermute | solution.py:42
  160.0 6.1 %collective-permute-start.55 = (bf16[32,2048]{1,0:T(8,128)(2,1)S(1)}, bf16[32,2048]{1,0:T(8,128)(2,1)S(1)}, u32[]{:S(2)}, u32[]{:S(2)}) collective-permute-start(bf16[32,2048]{1,0:T(8,128)(2,1)S(1)} %collective-permute-done.54.refs_9_), channel_id=1, source_target_pairs={{0,2},{2,4},{4,6},{6,7},{7,5},{5,3},{3,1},{1,0},{8,10},{10,12},{12... | collective-permute-start | bytes 393224 | tf_op jit(solution)/shard_map/ppermute | solution.py:42
  162.4 5.6 %collective-permute-start.59 = (bf16[32,2048]{1,0:T(8,128)(2,1)S(1)}, bf16[32,2048]{1,0:T(8,128)(2,1)S(1)}, u32[]{:S(2)}, u32[]{:S(2)}) collective-permute-start(bf16[32,2048]{1,0:T(8,128)(2,1)S(1)} %collective-permute-done.58.refs_14_), channel_id=1, source_target_pairs={{0,1},{2,0},{4,2},{6,4},{7,6},{5,7},{3,5},{1,3},{8,9},{10,8},{12,1... | collective-permute-start | bytes 393224 | tf_op jit(solution)/shard_map/ppermute | solution.py:42
  (20 other events, 128.3 us)

commit v12 on v11

--- a/solution.py
+++ b/solution.py
@@ -156,6 +156,26 @@
             transcendentals=0,
         ),
     )(parents.reshape(1, -1), features)
+
+
+def totals_kernel(logits_ref, out_ref):
+    values = logits_ref[...].astype(F32).T
+    top = jnp.max(values, axis=0, keepdims=True)
+    out_ref[0:1, :] = top
+    out_ref[1:2, :] = jnp.sum(jnp.exp(values - top), axis=0, keepdims=True)
+
+
+def row_totals(logits):
+    return pl.pallas_call(
+        totals_kernel,
+        in_specs=[VMEM],
+        out_specs=VMEM,
+        out_shape=jax.ShapeDtypeStruct((2, logits.shape[0]), F32),
+        compiler_params=pltpu.CompilerParams(vmem_limit_bytes=12 * 2**20),
+        cost_estimate=pl.CostEstimate(
+            flops=4 * logits.size, bytes_accessed=2 * logits.size, transcendentals=logits.size
+        ),
+    )(logits)
 
 
 def hold_kernel(weight_ref, held_ref, sems):
@@ -477,8 +497,8 @@
     row_factor = lax.rsqrt(both[:, 0] / model_width + 1e-05)
 
     targets = target_logits.astype(F32)
-    target_top = jnp.max(targets, axis=1)
-    target_total = jnp.sum(jnp.exp(targets - target_top[:, None]), axis=1)
+    target_totals = row_totals(target_logits)
+    target_top = target_totals[0]
 
     def merge_totals(terms):
         top = functools.reduce(jnp.maximum, [x[0] for x in terms])
@@ -508,7 +528,7 @@
     logits = sum([cross(chip_sum(d), d) for d in range(1, groups.chips)], chip_sum(0))
     top = jnp.max(logits, axis=1)
     total = jnp.sum(jnp.exp(logits - top[:, None]), axis=1)
-    mine = jnp.stack([jnp.concatenate([top, target_top]), jnp.concatenate([total, target_total])])
+    mine = jnp.concatenate([jnp.stack([top, total]), target_totals], axis=1)
     met = ring.meet(mine, merge_totals)
     scale = jnp.exp(mine[0] - met[0]) / met[1]
     draft_scale, target_scale = scale[:group_rows], scale[group_rows:]

time: 181 us -> 175 us (0.967)
  local copies, waits for them, and re-layouts: 9.87 us -> 6.47 us
  other arithmetic: 12.5 us -> 10.2 us
    unnamed x16 -> x10, local copies, waits for them, and re-layouts: 6.79 us -> 3.4 us
where the time goes in v12:
time: 175 us; the launch traced here: 174 us
  starting transfers between devices  65.6 us (37%)
  waiting for transfers between devices  63.8 us (36%)
  Pallas kernels  27.3 us (16%)
  other arithmetic  10.2 us (6%)
  local copies, waits for them, and re-layouts  6.47 us (4%)
    ppermute x42, starting transfers between devices, shift(): lax.ppermute(x, 'vocab', [(order[p], order[(p + step) % size]) for p in r...  43.7 us
    ppermute x42, waiting for transfers between devices, shift(): lax.ppermute(x, 'vocab', [(order[p], order[(p + step) % size]) for p in r...  30.7 us
    ppermute x5, waiting for transfers between devices, shift(): lax.ppermute(x, 'dp', [(i, (i + CORES * step) % size) for i in range(size)])  21.7 us
    ppermute x8, starting transfers between devices, partner(): return lax.ppermute(x, 'vocab', [(v, v ^ bit) for v in range(self.size)])  13.9 us
    pallas_call x1, Pallas kernels, outer(): pl.pallas_call(functools.partial(outer_kernel, len(chunks[0]), copies), g...  11.7 us
    pallas_call x1, Pallas kernels, project(): pl.pallas_call(functools.partial(project_kernel, len(blocks[0]), tile), g...  8.06 us
    ppermute x4, waiting for transfers between devices, swap(): return lax.ppermute(x, 'dp', [(i, i ^ 1) for i in range(self.size)])  6.33 us
    ppermute x5, starting transfers between devices, shift(): lax.ppermute(x, 'dp', [(i, (i + CORES * step) % size) for i in range(size)])  6.14 us
  transfers between devices with their start and end apart: 60, of which 36 were waited for; matrix products, arithmetic and copies ran while one was open for 6% of the time, Pallas kernels for 1%

profile of v12, /device:TPU:0, one launch (start us, length us, event | category | flops | bytes accessed | tf_op | source)
XLA Modules:
  0.0 174.5 jit_solution(18403229764238540382)
XLA Ops:
  0.6 1.6 collective-permute-start.4
  3.3 3.0 %collective-permute-start = (f32[1,128]{1,0:T(1,128)S(1)}, f32[1,128]{1,0:T(1,128)S(1)}, u32[]{:S(2)}, u32[]{:S(2)}) collective-permute-start(f32[1,128]{1,0:T(1,128)S(1)} %bitcast.77), channel_id=1, source_target_pairs={{0,1},{1,0},{2,3},{3,2},{4,5},{5,4},{6,7},{7,6},{8,9},{9,8},{10,11... | collective-permute-start | bytes 1544 | tf_op jit(solution)/shard_map/ppermute | solution.py:47
  6.3 1.5 collective-permute-done
  7.9 5.0 %collective-permute-start.3 = (f32[1,128]{1,0:T(1,128)S(1)}, f32[1,128]{1,0:T(1,128)S(1)}, u32[]{:S(2)}, u32[]{:S(2)}) collective-permute-start(f32[1,128]{1,0:T(1,128)S(1)} %bitcast_add_fusion), channel_id=1, source_target_pairs={{0,6},{1,7},{2,4},{3,5},{4,2},{5,3},{6,0},{7,1},{8,14},{9,15},{10,... | collective-permute-start | bytes 1544 | tf_op jit(solution)/shard_map/ppermute | solution.py:47
  14.1 3.4 %copy-done = bf16[2048,2048]{1,0:T(8,128)(2,1)S(1)} copy-done((bf16[2048,2048]{1,0:T(8,128)(2,1)S(1)}, bf16[2048,2048]{1,0:T(8,128)(2,1)}, u32[]{:S(2)}) %copy-start) | copy-done | bytes 8388632
  18.2 1.6 collective-permute-start.17
  20.4 1.5 collective-permute-start.14
  22.4 2.2 %collective-permute-done.17.refs_12_ = bf16[64,1024]{1,0:T(8,128)(2,1)S(1)} collective-permute-done((bf16[64,1024]{1,0:T(8,128)(2,1)S(1)}, bf16[64,1024]{1,0:T(8,128)(2,1)S(1)}, u32[]{:S(2)}, u32[]{:S(2)}) %collective-permute-start.17) | collective-permute-done | bytes 131104 | tf_op jit(solution)/shard_map/ppermute | solution.py:42
  24.6 1.5 collective-permute-start.18
  27.5 2.5 %collective-permute-start.7 = (f32[2,128]{1,0:T(2,128)S(1)}, f32[2,128]{1,0:T(2,128)S(1)}, u32[]{:S(2)}, u32[]{:S(2)}) collective-permute-start(f32[2,128]{1,0:T(2,128)S(1)} %pad_maximum_fusion.8), channel_id=1, source_target_pairs={{0,16},{8,24},{16,0},{24,8},{1,17},{9,25},{17,1},{25,9},{2,18},{10... | collective-permute-start | bytes 3080 | tf_op jit(solution)/shard_map/ppermute | solution.py:116
  30.1 1.5 collective-permute-start.9
  32.1 1.5 collective-permute-start.19
  34.1 3.1 %collective-permute-done.15.refs_9_ = bf16[64,1024]{1,0:T(8,128)(2,1)S(1)} collective-permute-done((bf16[64,1024]{1,0:T(8,128)(2,1)S(1)}, bf16[64,1024]{1,0:T(8,128)(2,1)S(1)}, u32[]{:S(2)}, u32[]{:S(2)}) %collective-permute-start.15) | collective-permute-done | bytes 131104 | tf_op jit(solution)/shard_map/ppermute | solution.py:42
  37.8 1.5 collective-permute-start.13
  42.1 1.4 dynamic_slice.13
  45.0 8.1 %shard_map.97 = (f32[256,2048]{1,0:T(8,128)S(1)}, f32[256,2048]{1,0:T(8,128)S(1)}, bf16[32,2048]{1,0:T(8,128)(2,1)S(1)}, bf16[32,2048]{1,0:T(8,128)(2,1)S(1)}) custom-call(s32[34]{0:T(128)S(1)} %slice_bitcast_fusion.1.index_ref, f32[4,128]{1,0:T(4,128)S(1)} %get-tuple-element.77.factor_ref, f32[1,2048]{1,0:T(1,128)S(1)} %bitcast.58, ...), custom_call_target="tpu_custom_call" | custom-call | flops 4294967296 | bytes 14680064 | tf_op jit(solution)/shard_map/pallas_call | solution.py:249
  53.2 4.1 %collective-permute-done.21 = f32[256,2048]{1,0:T(8,128)S(1)} collective-permute-done((f32[256,2048]{1,0:T(8,128)S(1)}, f32[256,2048]{1,0:T(8,128)S(1)}, u32[]{:S(2)}, u32[]{:S(2)}) %collective-permute-start.21) | collective-permute-done | bytes 2097184 | tf_op jit(solution)/shard_map/ppermute | solution.py:112
  60.6 11.3 %collective-permute-done.23 = f32[128]{0:T(128)S(1)} collective-permute-done((f32[128]{0:T(128)S(1)}, f32[128]{0:T(128)S(1)}, u32[]{:S(2)}, u32[]{:S(2)}) %collective-permute-start.23) | collective-permute-done | bytes 544 | tf_op jit(solution)/shard_map/ppermute | solution.py:116
  74.6 1.6 collective-permute-done.24
  76.3 1.9 %collective-permute-start.27 = (f32[2,256]{1,0:T(2,128)S(1)}, f32[2,256]{1,0:T(2,128)S(1)}, u32[]{:S(2)}, u32[]{:S(2)}) collective-permute-start(f32[2,256]{1,0:T(2,128)S(1)} %pad_maximum_fusion.7), channel_id=1, source_target_pairs={{0,6},{1,7},{2,4},{3,5},{4,2},{5,3},{6,0},{7,1},{8,14},{9,15},{10,... | collective-permute-start | bytes 6152 | tf_op jit(solution)/shard_map/ppermute | solution.py:47
  79.8 1.7 collective-permute-start.25
  81.7 1.6 collective-permute-done.26
  85.1 10.4 %collective-permute-done.28 = bf16[128,2176]{1,0:T(8,128)(2,1)S(1)} collective-permute-done((bf16[128,2176]{1,0:T(8,128)(2,1)S(1)}, bf16[128,2176]{1,0:T(8,128)(2,1)S(1)}, u32[]{:S(2)}, u32[]{:S(2)}) %collective-permute-start.28) | collective-permute-done | bytes 557088 | tf_op jit(solution)/shard_map/ppermute | solution.py:116
  96.3 2.2 %collective-permute-done.29.other_ref = bf16[2,128,2176]{2,1,0:T(8,128)(2,1)S(1)} collective-permute-done((bf16[2,128,2176]{2,1,0:T(8,128)(2,1)S(1)}, bf16[2,128,2176]{2,1,0:T(8,128)(2,1)S(1)}, u32[]{:S(2)}, u32[]{:S(2)}) %collective-permute-start.29) | collective-permute-done | bytes 1114144 | tf_op jit(solution)/shard_map/ppermute | solution.py:112
  98.5 5.9 %shard_map.99 = (f32[256,2176]{1,0:T(8,128)S(1)}, f32[256,2176]{1,0:T(8,128)S(1)}) custom-call(s32[8]{0:T(128)S(1)} %slice_bitcast_fusion.2.index_ref, bf16[2,128,2176]{2,1,0:T(8,128)(2,1)S(1)} %pad_maximum_fusion.2.mine_ref, bf16[2,128,2176]{2,1,0:T(8,128)(2,1)S(1)} %collective-permute-done.29.other_ref, bf16[2048,2048]{1,0:T(8,128)(2,1)S(1)} %shard_map.96.weight_ref), custom_call_target="tpu_custom_call" | custom-call | flops 4294967296 | bytes 14680064 | tf_op jit(solution)/shard_map/pallas_call | solution.py:300
  105.2 1.7 collective-permute-start.32
  107.4 3.3 %collective-permute-done.32 = bf16[32,2176]{1,0:T(8,128)(2,1)S(1)} collective-permute-done((bf16[32,2176]{1,0:T(8,128)(2,1)S(1)}, bf16[32,2176]{1,0:T(8,128)(2,1)S(1)}, u32[]{:S(2)}, u32[]{:S(2)}) %collective-permute-start.32) | collective-permute-done | bytes 139296 | tf_op jit(solution)/shard_map/ppermute | solution.py:42
  110.7 1.7 collective-permute-start.33
  114.9 1.8 %collective-permute-done.33 = bf16[32,2176]{1,0:T(8,128)(2,1)S(1)} collective-permute-done((bf16[32,2176]{1,0:T(8,128)(2,1)S(1)}, bf16[32,2176]{1,0:T(8,128)(2,1)S(1)}, u32[]{:S(2)}, u32[]{:S(2)}) %collective-permute-start.33) | collective-permute-done | bytes 139296 | tf_op jit(solution)/shard_map/ppermute | solution.py:42
  116.7 1.6 collective-permute-done.34
  118.8 1.7 collective-permute-start.35
  121.7 1.8 %collective-permute-start.49 = (bf16[32,2176]{1,0:T(8,128)(2,1)S(1)}, bf16[32,2176]{1,0:T(8,128)(2,1)S(1)}, u32[]{:S(2)}, u32[]{:S(2)}) collective-permute-start(bf16[32,2176]{1,0:T(8,128)(2,1)S(1)} %get-tuple-element.43), channel_id=1, source_target_pairs={{0,2},{2,4},{4,6},{6,7},{7,5},{5,3},{3,1},{1,0},{8,10},{10,12},{12... | collective-permute-start | bytes 417800 | tf_op jit(solution)/shard_map/ppermute | solution.py:42
  126.5 1.4 collective-permute-done.50
  128.3 1.5 collective-permute-start.52
  130.6 2.8 %collective-permute-done.52 = bf16[32,2176]{1,0:T(8,128)(2,1)S(1)} collective-permute-done((bf16[32,2176]{1,0:T(8,128)(2,1)S(1)}, bf16[32,2176]{1,0:T(8,128)(2,1)S(1)}, u32[]{:S(2)}, u32[]{:S(2)}) %collective-permute-start.52) | collective-permute-done | bytes 139296 | tf_op jit(solution)/shard_map/ppermute | solution.py:42
  133.4 1.5 collective-permute-done.51
  135.4 1.4 fusion.21
  136.8 1.4 fusion.20
  139.0 1.4 collective-permute-start.39
  141.0 1.5 collective-permute-start.43
  142.5 2.2 %collective-permute-done.56.refs_12_ = bf16[32,2048]{1,0:T(8,128)(2,1)S(1)} collective-permute-done((bf16[32,2048]{1,0:T(8,128)(2,1)S(1)}, bf16[32,2048]{1,0:T(8,128)(2,1)S(1)}, u32[]{:S(2)}, u32[]{:S(2)}) %collective-permute-start.56) | collective-permute-done | bytes 131104 | tf_op jit(solution)/shard_map/ppermute | solution.py:42
  145.3 1.4 collective-permute-start.40
  147.9 1.4 collective-permute-start.54
  151.3 1.4 collective-permute-start.41
  152.8 1.4 collective-permute-done.54.refs_9_
  154.2 1.5 collective-permute-start.55
  157.6 1.4 collective-permute-start.42
  162.6 11.7 %shard_map.100 = (f32[2048,3072]{1,0:T(8,128)}, bf16[64,2048]{1,0:T(8,128)(2,1)}) custom-call(s32[17]{0:T(128)S(1)} %slice_bitcast_fusion.3.index_ref, bf16[512,3072]{1,0:T(8,128)(2,1)S(1)} %bitcast.57, bf16[32,2048]{1,0:T(8,128)(2,1)S(1)} %collective-permute-done.42.refs_0_, bf16[32,2048]{1,0:T(8,128)(2,1)S(1)} %collective-permute-done.41.refs_1_, ...), custom_call_target="tpu_custom_call" | custom-call | flops 6442450944 | bytes 30408704 | tf_op jit(solution)/shard_map/pallas_call | solution.py:367
  (145 shorter events, 42.4 us)
Async XLA Ops:
  0.6 17.6 %collective-permute-start.4 = (bf16[128,1024]{1,0:T(8,128)(2,1)}, bf16[128,1024]{1,0:T(8,128)(2,1)S(1)}, u32[]{:S(2)}, u32[]{:S(2)}) collective-permute-start(bf16[128,1024]{1,0:T(8,128)(2,1)} %param.8), channel_id=1, source_target_pairs={{0,0},{1,1},{2,8},{3,9},{4,16},{5,17},{6,24},{7,25},{8,4},{9,5},{1... | collective-permute-start | bytes 786440 | tf_op jit(solution)/shard_map/ppermute | solution.py:475
  7.9 10.3 %collective-permute-start.3 = (f32[1,128]{1,0:T(1,128)S(1)}, f32[1,128]{1,0:T(1,128)S(1)}, u32[]{:S(2)}, u32[]{:S(2)}) collective-permute-start(f32[1,128]{1,0:T(1,128)S(1)} %bitcast_add_fusion), channel_id=1, source_target_pairs={{0,6},{1,7},{2,4},{3,5},{4,2},{5,3},{6,0},{7,1},{8,14},{9,15},{10,... | collective-permute-start | bytes 1544 | tf_op jit(solution)/shard_map/ppermute | solution.py:47
  12.9 5.3 %collective-permute-start.2 = (f32[1,128]{1,0:T(1,128)S(1)}, f32[1,128]{1,0:T(1,128)S(1)}, u32[]{:S(2)}, u32[]{:S(2)}) collective-permute-start(f32[1,128]{1,0:T(1,128)S(1)} %bitcast_add_fusion), channel_id=1, source_target_pairs={{0,4},{1,5},{2,6},{3,7},{4,0},{5,1},{6,2},{7,3},{8,12},{9,13},{10,... | collective-permute-start | bytes 1544 | tf_op jit(solution)/shard_map/ppermute | solution.py:47
  12.9 5.3 %collective-permute-start.1 = (f32[1,128]{1,0:T(1,128)S(1)}, f32[1,128]{1,0:T(1,128)S(1)}, u32[]{:S(2)}, u32[]{:S(2)}) collective-permute-start(f32[1,128]{1,0:T(1,128)S(1)} %bitcast_add_fusion), channel_id=1, source_target_pairs={{0,2},{1,3},{2,0},{3,1},{4,6},{5,7},{6,4},{7,5},{8,10},{9,11},{10,... | collective-permute-start | bytes 1544 | tf_op jit(solution)/shard_map/ppermute | solution.py:47
  18.2 6.4 %collective-permute-start.17 = (bf16[64,1024]{1,0:T(8,128)(2,1)S(1)}, bf16[64,1024]{1,0:T(8,128)(2,1)S(1)}, u32[]{:S(2)}, u32[]{:S(2)}) collective-permute-start(bf16[64,1024]{1,0:T(8,128)(2,1)S(1)} %get-tuple-element.72.refs_11_), channel_id=1, source_target_pairs={{0,1},{2,0},{4,2},{6,4},{7,6},{5,7},{3,5},{1,3},{8,9},{10,8},{12,1... | collective-permute-start | bytes 393224 | tf_op jit(solution)/shard_map/ppermute | solution.py:42
  19.8 6.4 %collective-permute-start.5 = (bf16[64,1024]{1,0:T(8,128)(2,1)S(1)}, bf16[64,1024]{1,0:T(8,128)(2,1)S(1)}, u32[]{:S(2)}, u32[]{:S(2)}) collective-permute-start(bf16[64,1024]{1,0:T(8,128)(2,1)S(1)} %get-tuple-element.73.refs_4_), channel_id=1, source_target_pairs={{0,2},{2,4},{4,6},{6,7},{7,5},{5,3},{3,1},{1,0},{8,10},{10,12},{12... | collective-permute-start | bytes 393224 | tf_op jit(solution)/shard_map/ppermute | solution.py:42
  20.4 11.2 %collective-permute-start.14 = (bf16[64,1024]{1,0:T(8,128)(2,1)S(1)}, bf16[64,1024]{1,0:T(8,128)(2,1)S(1)}, u32[]{:S(2)}, u32[]{:S(2)}) collective-permute-start(bf16[64,1024]{1,0:T(8,128)(2,1)S(1)} %get-tuple-element.72.refs_11_), channel_id=1, source_target_pairs={{0,2},{2,4},{4,6},{6,7},{7,5},{5,3},{3,1},{1,0},{8,10},{10,12},{12... | collective-permute-start | bytes 393224 | tf_op jit(solution)/shard_map/ppermute | solution.py:42
  21.8 5.7 %collective-permute-start.6 = (bf16[64,1024]{1,0:T(8,128)(2,1)S(1)}, bf16[64,1024]{1,0:T(8,128)(2,1)S(1)}, u32[]{:S(2)}, u32[]{:S(2)}) collective-permute-start(bf16[64,1024]{1,0:T(8,128)(2,1)S(1)} %get-tuple-element.73.refs_4_), channel_id=1, source_target_pairs={{0,1},{2,0},{4,2},{6,4},{7,6},{5,7},{3,5},{1,3},{8,9},{10,8},{12,1... | collective-permute-start | bytes 393224 | tf_op jit(solution)/shard_map/ppermute | solution.py:42
  24.6 7.5 %collective-permute-start.18 = (bf16[64,1024]{1,0:T(8,128)(2,1)S(1)}, bf16[64,1024]{1,0:T(8,128)(2,1)S(1)}, u32[]{:S(2)}, u32[]{:S(2)}) collective-permute-start(bf16[64,1024]{1,0:T(8,128)(2,1)S(1)} %collective-permute-done.17.refs_12_), channel_id=1, source_target_pairs={{0,1},{2,0},{4,2},{6,4},{7,6},{5,7},{3,5},{1,3},{8,9},{10,8},{12,1... | collective-permute-start | bytes 393224 | tf_op jit(solution)/shard_map/ppermute | solution.py:42
  26.2 7.4 %collective-permute-start.8 = (bf16[64,1024]{1,0:T(8,128)(2,1)S(1)}, bf16[64,1024]{1,0:T(8,128)(2,1)S(1)}, u32[]{:S(2)}, u32[]{:S(2)}) collective-permute-start(bf16[64,1024]{1,0:T(8,128)(2,1)S(1)} %collective-permute-done.5.refs_3_), channel_id=1, source_target_pairs={{0,2},{2,4},{4,6},{6,7},{7,5},{5,3},{3,1},{1,0},{8,10},{10,12},{12... | collective-permute-start | bytes 393224 | tf_op jit(solution)/shard_map/ppermute | solution.py:42
  27.5 13.8 %collective-permute-start.7 = (f32[2,128]{1,0:T(2,128)S(1)}, f32[2,128]{1,0:T(2,128)S(1)}, u32[]{:S(2)}, u32[]{:S(2)}) collective-permute-start(f32[2,128]{1,0:T(2,128)S(1)} %pad_maximum_fusion.8), channel_id=1, source_target_pairs={{0,16},{8,24},{16,0},{24,8},{1,17},{9,25},{17,1},{25,9},{2,18},{10... | collective-permute-start | bytes 3080 | tf_op jit(solution)/shard_map/ppermute | solution.py:116
  30.1 7.7 %collective-permute-start.9 = (bf16[64,1024]{1,0:T(8,128)(2,1)S(1)}, bf16[64,1024]{1,0:T(8,128)(2,1)S(1)}, u32[]{:S(2)}, u32[]{:S(2)}) collective-permute-start(bf16[64,1024]{1,0:T(8,128)(2,1)S(1)} %collective-permute-done.6.refs_5_), channel_id=1, source_target_pairs={{0,1},{2,0},{4,2},{6,4},{7,6},{5,7},{3,5},{1,3},{8,9},{10,8},{12,1... | collective-permute-start | bytes 393224 | tf_op jit(solution)/shard_map/ppermute | solution.py:42
  31.6 5.7 %collective-permute-start.15 = (bf16[64,1024]{1,0:T(8,128)(2,1)S(1)}, bf16[64,1024]{1,0:T(8,128)(2,1)S(1)}, u32[]{:S(2)}, u32[]{:S(2)}) collective-permute-start(bf16[64,1024]{1,0:T(8,128)(2,1)S(1)} %collective-permute-done.14.refs_10_), channel_id=1, source_target_pairs={{0,2},{2,4},{4,6},{6,7},{7,5},{5,3},{3,1},{1,0},{8,10},{10,12},{12... | collective-permute-start | bytes 393224 | tf_op jit(solution)/shard_map/ppermute | solution.py:42
  32.1 7.2 %collective-permute-start.19 = (bf16[64,1024]{1,0:T(8,128)(2,1)S(1)}, bf16[64,1024]{1,0:T(8,128)(2,1)S(1)}, u32[]{:S(2)}, u32[]{:S(2)}) collective-permute-start(bf16[64,1024]{1,0:T(8,128)(2,1)S(1)} %collective-permute-done.18.refs_13_), channel_id=1, source_target_pairs={{0,1},{2,0},{4,2},{6,4},{7,6},{5,7},{3,5},{1,3},{8,9},{10,8},{12,1... | collective-permute-start | bytes 393224 | tf_op jit(solution)/shard_map/ppermute | solution.py:42
  33.6 6.5 %collective-permute-start.11 = (bf16[64,1024]{1,0:T(8,128)(2,1)S(1)}, bf16[64,1024]{1,0:T(8,128)(2,1)S(1)}, u32[]{:S(2)}, u32[]{:S(2)}) collective-permute-start(bf16[64,1024]{1,0:T(8,128)(2,1)S(1)} %collective-permute-done.8.refs_2_), channel_id=1, source_target_pairs={{0,2},{2,4},{4,6},{6,7},{7,5},{5,3},{3,1},{1,0},{8,10},{10,12},{12... | collective-permute-start | bytes 393224 | tf_op jit(solution)/shard_map/ppermute | solution.py:42
  37.3 6.9 %collective-permute-start.16 = (bf16[64,1024]{1,0:T(8,128)(2,1)S(1)}, bf16[64,1024]{1,0:T(8,128)(2,1)S(1)}, u32[]{:S(2)}, u32[]{:S(2)}) collective-permute-start(bf16[64,1024]{1,0:T(8,128)(2,1)S(1)} %collective-permute-done.15.refs_9_), channel_id=1, source_target_pairs={{0,2},{2,4},{4,6},{6,7},{7,5},{5,3},{3,1},{1,0},{8,10},{10,12},{12... | collective-permute-start | bytes 393224 | tf_op jit(solution)/shard_map/ppermute | solution.py:42
  37.8 6.4 %collective-permute-start.13 = (bf16[64,1024]{1,0:T(8,128)(2,1)S(1)}, bf16[64,1024]{1,0:T(8,128)(2,1)S(1)}, u32[]{:S(2)}, u32[]{:S(2)}) collective-permute-start(bf16[64,1024]{1,0:T(8,128)(2,1)S(1)} %collective-permute-done.9.refs_6_), channel_id=1, source_target_pairs={{0,1},{2,0},{4,2},{6,4},{7,6},{5,7},{3,5},{1,3},{8,9},{10,8},{12,1... | collective-permute-start | bytes 393224 | tf_op jit(solution)/shard_map/ppermute | solution.py:42
  57.8 14.1 %collective-permute-start.22 = (s16[128,2048]{1,0:T(8,128)(2,1)S(1)}, s16[128,2048]{1,0:T(8,128)(2,1)S(1)}, u32[]{:S(2)}, u32[]{:S(2)}) collective-permute-start(s16[128,2048]{1,0:T(8,128)(2,1)S(1)} %round-nearest-even_convert_fusion), channel_id=1, source_target_pairs={{0,16},{8,24},{16,0},{24,8},{1,17},{9,25},{17,1},{25,9},{2,18},{10... | collective-permute-start | bytes 1572872 | tf_op jit(solution)/shard_map/ppermute | solution.py:116
  59.3 12.6 %collective-permute-start.23 = (f32[128]{0:T(128)S(1)}, f32[128]{0:T(128)S(1)}, u32[]{:S(2)}, u32[]{:S(2)}) collective-permute-start(f32[128]{0:T(128)S(1)} %get-tuple-element.102), channel_id=1, source_target_pairs={{0,16},{8,24},{16,0},{24,8},{1,17},{9,25},{17,1},{25,9},{2,18},{10... | collective-permute-start | bytes 1544 | tf_op jit(solution)/shard_map/ppermute | solution.py:116
  76.3 5.4 %collective-permute-start.27 = (f32[2,256]{1,0:T(2,128)S(1)}, f32[2,256]{1,0:T(2,128)S(1)}, u32[]{:S(2)}, u32[]{:S(2)}) collective-permute-start(f32[2,256]{1,0:T(2,128)S(1)} %pad_maximum_fusion.7), channel_id=1, source_target_pairs={{0,6},{1,7},{2,4},{3,5},{4,2},{5,3},{6,0},{7,1},{8,14},{9,15},{10,... | collective-permute-start | bytes 6152 | tf_op jit(solution)/shard_map/ppermute | solution.py:47
  84.3 11.3 %collective-permute-start.28 = (bf16[128,2176]{1,0:T(8,128)(2,1)S(1)}, bf16[128,2176]{1,0:T(8,128)(2,1)S(1)}, u32[]{:S(2)}, u32[]{:S(2)}) collective-permute-start(bf16[128,2176]{1,0:T(8,128)(2,1)S(1)} %get-tuple-element.71), channel_id=1, source_target_pairs={{0,16},{8,24},{16,0},{24,8},{1,17},{9,25},{17,1},{25,9},{2,18},{10... | collective-permute-start | bytes 1671176 | tf_op jit(solution)/shard_map/ppermute | solution.py:116
  104.6 30.3 %collective-permute-start.30 = (bf16[2,64,3072]{2,1,0:T(8,128)(2,1)S(1)}, bf16[2,64,3072]{2,1,0:T(8,128)(2,1)S(1)}, u32[]{:S(2)}, u32[]{:S(2)}) collective-permute-start(bf16[2,64,3072]{2,1,0:T(8,128)(2,1)S(1)} %bitcast.54), channel_id=1, source_target_pairs={{0,16},{8,24},{16,0},{24,8},{1,17},{9,25},{17,1},{25,9},{2,18},{10... | collective-permute-start | bytes 2359304 | tf_op jit(solution)/shard_map/ppermute | solution.py:116
  105.2 5.5 %collective-permute-start.32 = (bf16[32,2176]{1,0:T(8,128)(2,1)S(1)}, bf16[32,2176]{1,0:T(8,128)(2,1)S(1)}, u32[]{:S(2)}, u32[]{:S(2)}) collective-permute-start(bf16[32,2176]{1,0:T(8,128)(2,1)S(1)} %get-tuple-element.68), channel_id=1, source_target_pairs={{0,2},{2,4},{4,6},{6,7},{7,5},{5,3},{3,1},{1,0},{8,10},{10,12},{12... | collective-permute-start | bytes 417800 | tf_op jit(solution)/shard_map/ppermute | solution.py:42
  107.0 5.9 %collective-permute-start.46 = (bf16[32,2176]{1,0:T(8,128)(2,1)S(1)}, bf16[32,2176]{1,0:T(8,128)(2,1)S(1)}, u32[]{:S(2)}, u32[]{:S(2)}) collective-permute-start(bf16[32,2176]{1,0:T(8,128)(2,1)S(1)} %get-tuple-element.67), channel_id=1, source_target_pairs={{0,1},{2,0},{4,2},{6,4},{7,6},{5,7},{3,5},{1,3},{8,9},{10,8},{12,1... | collective-permute-start | bytes 417800 | tf_op jit(solution)/shard_map/ppermute | solution.py:42
  110.7 6.0 %collective-permute-start.33 = (bf16[32,2176]{1,0:T(8,128)(2,1)S(1)}, bf16[32,2176]{1,0:T(8,128)(2,1)S(1)}, u32[]{:S(2)}, u32[]{:S(2)}) collective-permute-start(bf16[32,2176]{1,0:T(8,128)(2,1)S(1)} %add_convert_fusion.9), channel_id=1, source_target_pairs={{0,2},{2,4},{4,6},{6,7},{7,5},{5,3},{3,1},{1,0},{8,10},{10,12},{12... | collective-permute-start | bytes 417800 | tf_op jit(solution)/shard_map/ppermute | solution.py:42
  112.5 5.9 %collective-permute-start.34 = (bf16[32,2176]{1,0:T(8,128)(2,1)S(1)}, bf16[32,2176]{1,0:T(8,128)(2,1)S(1)}, u32[]{:S(2)}, u32[]{:S(2)}) collective-permute-start(bf16[32,2176]{1,0:T(8,128)(2,1)S(1)} %get-tuple-element.35), channel_id=1, source_target_pairs={{0,1},{2,0},{4,2},{6,4},{7,6},{5,7},{3,5},{1,3},{8,9},{10,8},{12,1... | collective-permute-start | bytes 417800 | tf_op jit(solution)/shard_map/ppermute | solution.py:42
  112.8 8.5 %collective-permute-start.48 = (bf16[32,2176]{1,0:T(8,128)(2,1)S(1)}, bf16[32,2176]{1,0:T(8,128)(2,1)S(1)}, u32[]{:S(2)}, u32[]{:S(2)}) collective-permute-start(bf16[32,2176]{1,0:T(8,128)(2,1)S(1)} %add_convert_fusion.3), channel_id=1, source_target_pairs={{0,1},{2,0},{4,2},{6,4},{7,6},{5,7},{3,5},{1,3},{8,9},{10,8},{12,1... | collective-permute-start | bytes 417800 | tf_op jit(solution)/shard_map/ppermute | solution.py:42
  114.2 7.1 %collective-permute-start.47 = (bf16[32,2176]{1,0:T(8,128)(2,1)S(1)}, bf16[32,2176]{1,0:T(8,128)(2,1)S(1)}, u32[]{:S(2)}, u32[]{:S(2)}) collective-permute-start(bf16[32,2176]{1,0:T(8,128)(2,1)S(1)} %get-tuple-element.41), channel_id=1, source_target_pairs={{0,2},{2,4},{4,6},{6,7},{7,5},{5,3},{3,1},{1,0},{8,10},{10,12},{12... | collective-permute-start | bytes 417800 | tf_op jit(solution)/shard_map/ppermute | solution.py:42
  118.4 6.0 %collective-permute-start.36 = (bf16[32,2176]{1,0:T(8,128)(2,1)S(1)}, bf16[32,2176]{1,0:T(8,128)(2,1)S(1)}, u32[]{:S(2)}, u32[]{:S(2)}) collective-permute-start(bf16[32,2176]{1,0:T(8,128)(2,1)S(1)} %get-tuple-element.37), channel_id=1, source_target_pairs={{0,1},{2,0},{4,2},{6,4},{7,6},{5,7},{3,5},{1,3},{8,9},{10,8},{12,1... | collective-permute-start | bytes 417800 | tf_op jit(solution)/shard_map/ppermute | solution.py:42
  118.8 5.6 %collective-permute-start.35 = (bf16[32,2176]{1,0:T(8,128)(2,1)S(1)}, bf16[32,2176]{1,0:T(8,128)(2,1)S(1)}, u32[]{:S(2)}, u32[]{:S(2)}) collective-permute-start(bf16[32,2176]{1,0:T(8,128)(2,1)S(1)} %get-tuple-element.36), channel_id=1, source_target_pairs={{0,2},{2,4},{4,6},{6,7},{7,5},{5,3},{3,1},{1,0},{8,10},{10,12},{12... | collective-permute-start | bytes 417800 | tf_op jit(solution)/shard_map/ppermute | solution.py:42
  121.4 6.6 %collective-permute-start.50 = (bf16[32,2176]{1,0:T(8,128)(2,1)S(1)}, bf16[32,2176]{1,0:T(8,128)(2,1)S(1)}, u32[]{:S(2)}, u32[]{:S(2)}) collective-permute-start(bf16[32,2176]{1,0:T(8,128)(2,1)S(1)} %get-tuple-element.44), channel_id=1, source_target_pairs={{0,1},{2,0},{4,2},{6,4},{7,6},{5,7},{3,5},{1,3},{8,9},{10,8},{12,1... | collective-permute-start | bytes 417800 | tf_op jit(solution)/shard_map/ppermute | solution.py:42
  121.7 6.5 %collective-permute-start.49 = (bf16[32,2176]{1,0:T(8,128)(2,1)S(1)}, bf16[32,2176]{1,0:T(8,128)(2,1)S(1)}, u32[]{:S(2)}, u32[]{:S(2)}) collective-permute-start(bf16[32,2176]{1,0:T(8,128)(2,1)S(1)} %get-tuple-element.43), channel_id=1, source_target_pairs={{0,2},{2,4},{4,6},{6,7},{7,5},{5,3},{3,1},{1,0},{8,10},{10,12},{12... | collective-permute-start | bytes 417800 | tf_op jit(solution)/shard_map/ppermute | solution.py:42
  124.4 5.9 %collective-permute-start.38 = (bf16[32,2176]{1,0:T(8,128)(2,1)S(1)}, bf16[32,2176]{1,0:T(8,128)(2,1)S(1)}, u32[]{:S(2)}, u32[]{:S(2)}) collective-permute-start(bf16[32,2176]{1,0:T(8,128)(2,1)S(1)} %get-tuple-element.39), channel_id=1, source_target_pairs={{0,1},{2,0},{4,2},{6,4},{7,6},{5,7},{3,5},{1,3},{8,9},{10,8},{12,1... | collective-permute-start | bytes 417800 | tf_op jit(solution)/shard_map/ppermute | solution.py:42
  128.3 5.1 %collective-permute-start.52 = (bf16[32,2176]{1,0:T(8,128)(2,1)S(1)}, bf16[32,2176]{1,0:T(8,128)(2,1)S(1)}, u32[]{:S(2)}, u32[]{:S(2)}) collective-permute-start(bf16[32,2176]{1,0:T(8,128)(2,1)S(1)} %get-tuple-element.46), channel_id=1, source_target_pairs={{0,1},{2,0},{4,2},{6,4},{7,6},{5,7},{3,5},{1,3},{8,9},{10,8},{12,1... | collective-permute-start | bytes 417800 | tf_op jit(solution)/shard_map/ppermute | solution.py:42
  129.8 5.1 %collective-permute-start.51 = (bf16[32,2176]{1,0:T(8,128)(2,1)S(1)}, bf16[32,2176]{1,0:T(8,128)(2,1)S(1)}, u32[]{:S(2)}, u32[]{:S(2)}) collective-permute-start(bf16[32,2176]{1,0:T(8,128)(2,1)S(1)} %get-tuple-element.45), channel_id=1, source_target_pairs={{0,2},{2,4},{4,6},{6,7},{7,5},{5,3},{3,1},{1,0},{8,10},{10,12},{12... | collective-permute-start | bytes 417800 | tf_op jit(solution)/shard_map/ppermute | solution.py:42
  135.1 24.0 %collective-permute-start.31 = (bf16[2,2,64,3072]{3,2,0,1:T(8,128)(2,1)S(1)}, bf16[2,2,64,3072]{3,2,0,1:T(8,128)(2,1)S(1)}, u32[]{:S(2)}, u32[]{:S(2)}) collective-permute-start(bf16[2,2,64,3072]{3,2,0,1:T(8,128)(2,1)S(1)} %pad_maximum_fusion.1), channel_id=1, source_target_pairs={{0,8},{8,0},{16,24},{24,16},{1,9},{9,1},{17,25},{25,17},{2,10},{10... | collective-permute-start | bytes 4718600 | tf_op jit(solution)/shard_map/ppermute | solution.py:112
  138.4 6.3 %collective-permute-start.56 = (bf16[32,2048]{1,0:T(8,128)(2,1)S(1)}, bf16[32,2048]{1,0:T(8,128)(2,1)S(1)}, u32[]{:S(2)}, u32[]{:S(2)}) collective-permute-start(bf16[32,2048]{1,0:T(8,128)(2,1)S(1)} %get-tuple-element.74.refs_11_), channel_id=1, source_target_pairs={{0,1},{2,0},{4,2},{6,4},{7,6},{5,7},{3,5},{1,3},{8,9},{10,8},{12,1... | collective-permute-start | bytes 393224 | tf_op jit(solution)/shard_map/ppermute | solution.py:42
  139.0 6.3 %collective-permute-start.39 = (bf16[32,2048]{1,0:T(8,128)(2,1)S(1)}, bf16[32,2048]{1,0:T(8,128)(2,1)S(1)}, u32[]{:S(2)}, u32[]{:S(2)}) collective-permute-start(bf16[32,2048]{1,0:T(8,128)(2,1)S(1)} %get-tuple-element.75.refs_4_), channel_id=1, source_target_pairs={{0,2},{2,4},{4,6},{6,7},{7,5},{5,3},{3,1},{1,0},{8,10},{10,12},{12... | collective-permute-start | bytes 393224 | tf_op jit(solution)/shard_map/ppermute | solution.py:42
  140.4 7.4 %collective-permute-start.53 = (bf16[32,2048]{1,0:T(8,128)(2,1)S(1)}, bf16[32,2048]{1,0:T(8,128)(2,1)S(1)}, u32[]{:S(2)}, u32[]{:S(2)}) collective-permute-start(bf16[32,2048]{1,0:T(8,128)(2,1)S(1)} %get-tuple-element.74.refs_11_), channel_id=1, source_target_pairs={{0,2},{2,4},{4,6},{6,7},{7,5},{5,3},{3,1},{1,0},{8,10},{10,12},{12... | collective-permute-start | bytes 393224 | tf_op jit(solution)/shard_map/ppermute | solution.py:42
  141.0 8.3 %collective-permute-start.43 = (bf16[32,2048]{1,0:T(8,128)(2,1)S(1)}, bf16[32,2048]{1,0:T(8,128)(2,1)S(1)}, u32[]{:S(2)}, u32[]{:S(2)}) collective-permute-start(bf16[32,2048]{1,0:T(8,128)(2,1)S(1)} %get-tuple-element.75.refs_4_), channel_id=1, source_target_pairs={{0,1},{2,0},{4,2},{6,4},{7,6},{5,7},{3,5},{1,3},{8,9},{10,8},{12,1... | collective-permute-start | bytes 393224 | tf_op jit(solution)/shard_map/ppermute | solution.py:42
  144.7 5.2 %collective-permute-start.57 = (bf16[32,2048]{1,0:T(8,128)(2,1)S(1)}, bf16[32,2048]{1,0:T(8,128)(2,1)S(1)}, u32[]{:S(2)}, u32[]{:S(2)}) collective-permute-start(bf16[32,2048]{1,0:T(8,128)(2,1)S(1)} %collective-permute-done.56.refs_12_), channel_id=1, source_target_pairs={{0,1},{2,0},{4,2},{6,4},{7,6},{5,7},{3,5},{1,3},{8,9},{10,8},{12,1... | collective-permute-start | bytes 393224 | tf_op jit(solution)/shard_map/ppermute | solution.py:42
  145.3 5.9 %collective-permute-start.40 = (bf16[32,2048]{1,0:T(8,128)(2,1)S(1)}, bf16[32,2048]{1,0:T(8,128)(2,1)S(1)}, u32[]{:S(2)}, u32[]{:S(2)}) collective-permute-start(bf16[32,2048]{1,0:T(8,128)(2,1)S(1)} %collective-permute-done.39.refs_3_), channel_id=1, source_target_pairs={{0,2},{2,4},{4,6},{6,7},{7,5},{5,3},{3,1},{1,0},{8,10},{10,12},{12... | collective-permute-start | bytes 393224 | tf_op jit(solution)/shard_map/ppermute | solution.py:42
  147.9 6.3 %collective-permute-start.54 = (bf16[32,2048]{1,0:T(8,128)(2,1)S(1)}, bf16[32,2048]{1,0:T(8,128)(2,1)S(1)}, u32[]{:S(2)}, u32[]{:S(2)}) collective-permute-start(bf16[32,2048]{1,0:T(8,128)(2,1)S(1)} %collective-permute-done.53.refs_10_), channel_id=1, source_target_pairs={{0,2},{2,4},{4,6},{6,7},{7,5},{5,3},{3,1},{1,0},{8,10},{10,12},{12... | collective-permute-start | bytes 393224 | tf_op jit(solution)/shard_map/ppermute | solution.py:42
  149.3 6.4 %collective-permute-start.44 = (bf16[32,2048]{1,0:T(8,128)(2,1)S(1)}, bf16[32,2048]{1,0:T(8,128)(2,1)S(1)}, u32[]{:S(2)}, u32[]{:S(2)}) collective-permute-start(bf16[32,2048]{1,0:T(8,128)(2,1)S(1)} %collective-permute-done.43.refs_5_), channel_id=1, source_target_pairs={{0,1},{2,0},{4,2},{6,4},{7,6},{5,7},{3,5},{1,3},{8,9},{10,8},{12,1... | collective-permute-start | bytes 393224 | tf_op jit(solution)/shard_map/ppermute | solution.py:42
  149.9 6.6 %collective-permute-start.58 = (bf16[32,2048]{1,0:T(8,128)(2,1)S(1)}, bf16[32,2048]{1,0:T(8,128)(2,1)S(1)}, u32[]{:S(2)}, u32[]{:S(2)}) collective-permute-start(bf16[32,2048]{1,0:T(8,128)(2,1)S(1)} %collective-permute-done.57.refs_13_), channel_id=1, source_target_pairs={{0,1},{2,0},{4,2},{6,4},{7,6},{5,7},{3,5},{1,3},{8,9},{10,8},{12,1... | collective-permute-start | bytes 393224 | tf_op jit(solution)/shard_map/ppermute | solution.py:42
  151.3 6.4 %collective-permute-start.41 = (bf16[32,2048]{1,0:T(8,128)(2,1)S(1)}, bf16[32,2048]{1,0:T(8,128)(2,1)S(1)}, u32[]{:S(2)}, u32[]{:S(2)}) collective-permute-start(bf16[32,2048]{1,0:T(8,128)(2,1)S(1)} %collective-permute-done.40.refs_2_), channel_id=1, source_target_pairs={{0,2},{2,4},{4,6},{6,7},{7,5},{5,3},{3,1},{1,0},{8,10},{10,12},{12... | collective-permute-start | bytes 393224 | tf_op jit(solution)/shard_map/ppermute | solution.py:42
  154.2 6.1 %collective-permute-start.55 = (bf16[32,2048]{1,0:T(8,128)(2,1)S(1)}, bf16[32,2048]{1,0:T(8,128)(2,1)S(1)}, u32[]{:S(2)}, u32[]{:S(2)}) collective-permute-start(bf16[32,2048]{1,0:T(8,128)(2,1)S(1)} %collective-permute-done.54.refs_9_), channel_id=1, source_target_pairs={{0,2},{2,4},{4,6},{6,7},{7,5},{5,3},{3,1},{1,0},{8,10},{10,12},{12... | collective-permute-start | bytes 393224 | tf_op jit(solution)/shard_map/ppermute | solution.py:42
  156.5 5.6 %collective-permute-start.59 = (bf16[32,2048]{1,0:T(8,128)(2,1)S(1)}, bf16[32,2048]{1,0:T(8,128)(2,1)S(1)}, u32[]{:S(2)}, u32[]{:S(2)}) collective-permute-start(bf16[32,2048]{1,0:T(8,128)(2,1)S(1)} %collective-permute-done.58.refs_14_), channel_id=1, source_target_pairs={{0,1},{2,0},{4,2},{6,4},{7,6},{5,7},{3,5},{1,3},{8,9},{10,8},{12,1... | collective-permute-start | bytes 393224 | tf_op jit(solution)/shard_map/ppermute | solution.py:42
  (17 other events, 87.7 us)

commit v13 on v12

--- a/solution.py
+++ b/solution.py
@@ -206,13 +206,13 @@
 
 def project_kernel(count, tile, index_ref, factor_ref, gain_ref, weight_ref, *refs):
     blocks, refs = refs[: CHUNKS * count], refs[CHUNKS * count :]
-    keep_ref, send_ref = refs[:CORES]
-    piece_refs = refs[CORES : CORES + CHUNKS]
-    raw_ref, turned_ref = refs[CORES + CHUNKS :]
+    send_ref, turned_ref = refs[:2]
+    piece_refs = refs[2 : 2 + CHUNKS]
+    raw_ref, other_ref = refs[2 + CHUNKS :]
     rows, width = blocks[0].shape
     group_rows = CHUNKS * rows
+    groups = factor_ref.shape[0]
     piece = piece_refs[0].shape[0]
-    half = keep_ref.shape[0]
     step = pl.program_id(0)
 
     @pl.when(step == 0)
@@ -223,20 +223,29 @@
             column = pl.multiple_of(index_ref[at + count] * width, width)
             raw_ref[pl.ds(start, rows), pl.ds(column, width)] = ref[...]
         slab = min(raw_ref.shape[1], 256)
-        for g in range(factor_ref.shape[0]):
-            group = pl.ds(g * group_rows, group_rows)
+        for g in range(groups):
+            half_ref = turned_ref if g < groups // CORES else other_ref
+            place = pl.ds(g % (groups // CORES) * group_rows, group_rows)
             for first in range(0, raw_ref.shape[1], slab):
                 columns = pl.ds(first, slab)
-                values = raw_ref[group, columns].astype(F32) * gain_ref[:, columns]
-                turned_ref[columns, group] = (values.T * factor_ref[g : g + 1, :]).astype(BF16)
+                values = raw_ref[pl.ds(g * group_rows, group_rows), columns].astype(F32)
+                values = (values * gain_ref[:, columns]).T * factor_ref[g : g + 1, :]
+                half_ref[columns, place] = values.astype(BF16)
         for h, ref in enumerate(piece_refs):
             start = pl.multiple_of(index_ref[2 * CHUNKS * count + h] * piece, piece)
             ref[...] = raw_ref[pl.ds(start, piece), :]
 
     rows = pl.ds(pl.multiple_of(step * tile, tile), tile)
-    logits = jnp.dot(weight_ref[rows, :], turned_ref[...], preferred_element_type=F32).T
-    keep_ref[...] = logits[:half]
-    send_ref[...] = logits[half:]
+    send_ref[...] = jnp.dot(
+        weight_ref[rows, :], other_ref[...], preferred_element_type=F32
+    ).T
+
+
+def project_own_kernel(tile, weight_ref, turned_ref, keep_ref):
+    rows = pl.ds(pl.multiple_of(pl.program_id(0) * tile, tile), tile)
+    keep_ref[...] = jnp.dot(
+        weight_ref[rows, :], turned_ref[...], preferred_element_type=F32
+    ).T
 
 
 def project(index, blocks, factor, gain, weight, piece_rows):
@@ -245,25 +254,34 @@
     half = all_rows // CORES
     tile = min(vocab, 512)
     out = jax.ShapeDtypeStruct((half, vocab), F32)
+    out_spec = pl.BlockSpec((half, tile), lambda n: (0, n))
     piece = jax.ShapeDtypeStruct((piece_rows, depth), BF16)
-    return pl.pallas_call(
+    whole = lambda rows, columns: pl.BlockSpec((rows, columns), lambda n: (0, 0))
+    cost = pl.CostEstimate(
+        flops=2 * half * depth * vocab,
+        bytes_accessed=2 * vocab * depth + half * (4 * depth + 4 * vocab),
+        transcendentals=0,
+    )
+    send, turned, *pieces = pl.pallas_call(
         functools.partial(project_kernel, len(blocks[0]), tile),
         grid=(vocab // tile,),
         in_specs=[SMEM] + [VMEM] * (3 + CHUNKS * len(blocks[0])),
-        out_specs=[pl.BlockSpec((half, tile), lambda n: (0, n))] * CORES
-        + [pl.BlockSpec((piece_rows, depth), lambda n: (0, 0))] * CHUNKS,
-        out_shape=[out] * CORES + [piece] * CHUNKS,
-        scratch_shapes=[
-            pltpu.VMEM((all_rows, depth), BF16),
-            pltpu.VMEM((depth, all_rows), BF16),
-        ],
+        out_specs=[out_spec, whole(depth, half)] + [whole(piece_rows, depth)] * CHUNKS,
+        out_shape=[out, jax.ShapeDtypeStruct((depth, half), BF16)] + [piece] * CHUNKS,
+        scratch_shapes=[pltpu.VMEM((all_rows, depth), BF16), pltpu.VMEM((depth, half), BF16)],
         compiler_params=pltpu.CompilerParams(vmem_limit_bytes=28 * 2**20),
-        cost_estimate=pl.CostEstimate(
-            flops=2 * all_rows * depth * vocab,
-            bytes_accessed=2 * vocab * depth + all_rows * (2 * depth + 4 * vocab),
-            transcendentals=0,
-        ),
+        cost_estimate=cost,
     )(index, factor, gain, weight, *[x for chunk in blocks for x in chunk])
+    keep = pl.pallas_call(
+        functools.partial(project_own_kernel, tile),
+        grid=(vocab // tile,),
+        in_specs=[VMEM, VMEM],
+        out_specs=out_spec,
+        out_shape=out,
+        compiler_params=pltpu.CompilerParams(vmem_limit_bytes=20 * 2**20),
+        cost_estimate=cost,
+    )(weight, turned)
+    return [keep, send] + pieces
 
 
 def back_kernel(piece, tile, index_ref, mine_ref, other_ref, weight_ref, *refs):

time: 175 us -> 172 us (0.983)
  waiting for transfers between devices: 63.8 us -> 60.5 us
    ppermute x4, waiting for transfers between devices: 6.33 us -> 3.04 us  [swap(): return lax.ppermute(x, 'dp', [(i, i ^ 1) for i in range(self.size)])]
    pallas_call x0 -> x1, Pallas kernels: none -> 3.27 us  [project(): pl.pallas_call(functools.partial(project_own_kernel, tile), grid=(vocab /...]
    pallas_call x1, Pallas kernels: 8.06 us -> 5.22 us  [project(): pl.pallas_call(functools.partial(project_kernel, len(blocks[0]), tile), g...]
  transfers between devices with their start and end apart: 60 -> 60, of which waited for: 36 -> 35; matrix products, arithmetic and copies ran while one was open for 6% -> 6% of each run, Pallas kernels for 1% -> 3%
where the time goes in v13:
time: 172 us
  starting transfers between devices  65.8 us (38%)
  waiting for transfers between devices  60.5 us (35%)
  Pallas kernels  27.7 us (16%)
  other arithmetic  10.2 us (6%)
  local copies, waits for them, and re-layouts  6.48 us (4%)
    ppermute x42, starting transfers between devices, shift(): lax.ppermute(x, 'vocab', [(order[p], order[(p + step) % size]) for p in r...  43.9 us
    ppermute x42, waiting for transfers between devices, shift(): lax.ppermute(x, 'vocab', [(order[p], order[(p + step) % size]) for p in r...  30.7 us
    ppermute x5, waiting for transfers between devices, shift(): lax.ppermute(x, 'dp', [(i, (i + CORES * step) % size) for i in range(size)])  21.7 us
    ppermute x8, starting transfers between devices, partner(): return lax.ppermute(x, 'vocab', [(v, v ^ bit) for v in range(self.size)])  13.9 us
    pallas_call x1, Pallas kernels, outer(): pl.pallas_call(functools.partial(outer_kernel, len(chunks[0]), copies), g...  11.7 us
    ppermute x5, starting transfers between devices, shift(): lax.ppermute(x, 'dp', [(i, (i + CORES * step) % size) for i in range(size)])  6.14 us
    pallas_call x1, Pallas kernels, back(): pl.pallas_call(functools.partial(back_kernel, piece_rows, tile), grid=(de...  5.86 us
    pallas_call x1, Pallas kernels, project(): pl.pallas_call(functools.partial(project_kernel, len(blocks[0]), tile), g...  5.22 us
  transfers between devices with their start and end apart: 60, of which 35 were waited for; matrix products, arithmetic and copies ran while one was open for 6% of the time, Pallas kernels for 3%

profile of v13, /device:TPU:0, one launch (start us, length us, event | category | flops | bytes accessed | tf_op | source)
XLA Modules:
  0.0 171.8 jit_solution(9925010294272405768)
XLA Ops:
  0.6 1.6 collective-permute-start.4
  3.3 3.0 %collective-permute-start = (f32[1,128]{1,0:T(1,128)S(1)}, f32[1,128]{1,0:T(1,128)S(1)}, u32[]{:S(2)}, u32[]{:S(2)}) collective-permute-start(f32[1,128]{1,0:T(1,128)S(1)} %bitcast.77), channel_id=1, source_target_pairs={{0,1},{1,0},{2,3},{3,2},{4,5},{5,4},{6,7},{7,6},{8,9},{9,8},{10,11... | collective-permute-start | bytes 1544 | tf_op jit(solution)/shard_map/ppermute | solution.py:47
  6.3 1.5 collective-permute-done
  7.9 5.0 %collective-permute-start.3 = (f32[1,128]{1,0:T(1,128)S(1)}, f32[1,128]{1,0:T(1,128)S(1)}, u32[]{:S(2)}, u32[]{:S(2)}) collective-permute-start(f32[1,128]{1,0:T(1,128)S(1)} %bitcast_add_fusion), channel_id=1, source_target_pairs={{0,6},{1,7},{2,4},{3,5},{4,2},{5,3},{6,0},{7,1},{8,14},{9,15},{10,... | collective-permute-start | bytes 1544 | tf_op jit(solution)/shard_map/ppermute | solution.py:47
  14.1 3.4 %copy-done = bf16[2048,2048]{1,0:T(8,128)(2,1)S(1)} copy-done((bf16[2048,2048]{1,0:T(8,128)(2,1)S(1)}, bf16[2048,2048]{1,0:T(8,128)(2,1)}, u32[]{:S(2)}) %copy-start) | copy-done | bytes 8388632
  18.2 1.6 collective-permute-start.17
  20.4 1.5 collective-permute-start.14
  22.4 2.2 %collective-permute-done.17.refs_12_ = bf16[64,1024]{1,0:T(8,128)(2,1)S(1)} collective-permute-done((bf16[64,1024]{1,0:T(8,128)(2,1)S(1)}, bf16[64,1024]{1,0:T(8,128)(2,1)S(1)}, u32[]{:S(2)}, u32[]{:S(2)}) %collective-permute-start.17) | collective-permute-done | bytes 131104 | tf_op jit(solution)/shard_map/ppermute | solution.py:42
  24.6 1.5 collective-permute-start.18
  27.5 2.5 %collective-permute-start.7 = (f32[2,128]{1,0:T(2,128)S(1)}, f32[2,128]{1,0:T(2,128)S(1)}, u32[]{:S(2)}, u32[]{:S(2)}) collective-permute-start(f32[2,128]{1,0:T(2,128)S(1)} %pad_maximum_fusion.8), channel_id=1, source_target_pairs={{0,16},{8,24},{16,0},{24,8},{1,17},{9,25},{17,1},{25,9},{2,18},{10... | collective-permute-start | bytes 3080 | tf_op jit(solution)/shard_map/ppermute | solution.py:116
  30.1 1.5 collective-permute-start.9
  32.1 1.5 collective-permute-start.19
  34.1 3.1 %collective-permute-done.15.refs_9_ = bf16[64,1024]{1,0:T(8,128)(2,1)S(1)} collective-permute-done((bf16[64,1024]{1,0:T(8,128)(2,1)S(1)}, bf16[64,1024]{1,0:T(8,128)(2,1)S(1)}, u32[]{:S(2)}, u32[]{:S(2)}) %collective-permute-start.15) | collective-permute-done | bytes 131104 | tf_op jit(solution)/shard_map/ppermute | solution.py:42
  37.8 1.5 collective-permute-start.13
  42.1 1.4 dynamic_slice.13
  45.0 5.2 %shard_map.97 = (f32[256,2048]{1,0:T(8,128)S(1)}, bf16[2048,256]{1,0:T(8,128)(2,1)S(1)}, bf16[32,2048]{1,0:T(8,128)(2,1)S(1)}, bf16[32,2048]{1,0:T(8,128)(2,1)S(1)}) custom-call(s32[34]{0:T(128)S(1)} %slice_bitcast_fusion.1.index_ref, f32[4,128]{1,0:T(4,128)S(1)} %get-tuple-element.77.factor_ref, f32[1,2048]{1,0:T(1,128)S(1)} %bitcast.58, ...), custom_call_target="tpu_custom_call" | custom-call | flops 2147483648 | bytes 12582912 | tf_op jit(solution)/shard_map/pallas_call | solution.py:265
  50.3 3.3 %shard_map.98 = f32[256,2048]{1,0:T(8,128)S(1)} custom-call(bf16[2048,2048]{1,0:T(8,128)(2,1)S(1)} %shard_map.96.weight_ref, bf16[2048,256]{1,0:T(8,128)(2,1)S(1)} %get-tuple-element.29.turned_ref), custom_call_target="tpu_custom_call" | custom-call | flops 2147483648 | bytes 12582912 | tf_op jit(solution)/shard_map/pallas_call | solution.py:275
  57.7 11.3 %collective-permute-done.23 = f32[128]{0:T(128)S(1)} collective-permute-done((f32[128]{0:T(128)S(1)}, f32[128]{0:T(128)S(1)}, u32[]{:S(2)}, u32[]{:S(2)}) %collective-permute-start.23) | collective-permute-done | bytes 544 | tf_op jit(solution)/shard_map/ppermute | solution.py:116
  71.7 1.6 collective-permute-done.24
  73.4 1.9 %collective-permute-start.27 = (f32[2,256]{1,0:T(2,128)S(1)}, f32[2,256]{1,0:T(2,128)S(1)}, u32[]{:S(2)}, u32[]{:S(2)}) collective-permute-start(f32[2,256]{1,0:T(2,128)S(1)} %pad_maximum_fusion.7), channel_id=1, source_target_pairs={{0,6},{1,7},{2,4},{3,5},{4,2},{5,3},{6,0},{7,1},{8,14},{9,15},{10,... | collective-permute-start | bytes 6152 | tf_op jit(solution)/shard_map/ppermute | solution.py:47
  76.9 1.7 collective-permute-start.25
  78.9 1.6 collective-permute-done.26
  82.3 10.4 %collective-permute-done.28 = bf16[128,2176]{1,0:T(8,128)(2,1)S(1)} collective-permute-done((bf16[128,2176]{1,0:T(8,128)(2,1)S(1)}, bf16[128,2176]{1,0:T(8,128)(2,1)S(1)}, u32[]{:S(2)}, u32[]{:S(2)}) %collective-permute-start.28) | collective-permute-done | bytes 557088 | tf_op jit(solution)/shard_map/ppermute | solution.py:116
  93.4 2.2 %collective-permute-done.29.other_ref = bf16[2,128,2176]{2,1,0:T(8,128)(2,1)S(1)} collective-permute-done((bf16[2,128,2176]{2,1,0:T(8,128)(2,1)S(1)}, bf16[2,128,2176]{2,1,0:T(8,128)(2,1)S(1)}, u32[]{:S(2)}, u32[]{:S(2)}) %collective-permute-start.29) | collective-permute-done | bytes 1114144 | tf_op jit(solution)/shard_map/ppermute | solution.py:112
  95.6 5.9 %shard_map.100 = (f32[256,2176]{1,0:T(8,128)S(1)}, f32[256,2176]{1,0:T(8,128)S(1)}) custom-call(s32[8]{0:T(128)S(1)} %slice_bitcast_fusion.2.index_ref, bf16[2,128,2176]{2,1,0:T(8,128)(2,1)S(1)} %pad_maximum_fusion.2.mine_ref, bf16[2,128,2176]{2,1,0:T(8,128)(2,1)S(1)} %collective-permute-done.29.other_ref, bf16[2048,2048]{1,0:T(8,128)(2,1)S(1)} %shard_map.96.weight_ref), custom_call_target="tpu_custom_call" | custom-call | flops 4294967296 | bytes 14680064 | tf_op jit(solution)/shard_map/pallas_call | solution.py:318
  102.4 1.7 %collective-permute-start.32 = (bf16[32,2176]{1,0:T(8,128)(2,1)S(1)}, bf16[32,2176]{1,0:T(8,128)(2,1)S(1)}, u32[]{:S(2)}, u32[]{:S(2)}) collective-permute-start(bf16[32,2176]{1,0:T(8,128)(2,1)S(1)} %get-tuple-element.68), channel_id=1, source_target_pairs={{0,2},{2,4},{4,6},{6,7},{7,5},{5,3},{3,1},{1,0},{8,10},{10,12},{12... | collective-permute-start | bytes 417800 | tf_op jit(solution)/shard_map/ppermute | solution.py:42
  104.5 3.3 %collective-permute-done.32 = bf16[32,2176]{1,0:T(8,128)(2,1)S(1)} collective-permute-done((bf16[32,2176]{1,0:T(8,128)(2,1)S(1)}, bf16[32,2176]{1,0:T(8,128)(2,1)S(1)}, u32[]{:S(2)}, u32[]{:S(2)}) %collective-permute-start.32) | collective-permute-done | bytes 139296 | tf_op jit(solution)/shard_map/ppermute | solution.py:42
  107.9 1.7 %collective-permute-start.33 = (bf16[32,2176]{1,0:T(8,128)(2,1)S(1)}, bf16[32,2176]{1,0:T(8,128)(2,1)S(1)}, u32[]{:S(2)}, u32[]{:S(2)}) collective-permute-start(bf16[32,2176]{1,0:T(8,128)(2,1)S(1)} %add_convert_fusion.9), channel_id=1, source_target_pairs={{0,2},{2,4},{4,6},{6,7},{7,5},{5,3},{3,1},{1,0},{8,10},{10,12},{12... | collective-permute-start | bytes 417800 | tf_op jit(solution)/shard_map/ppermute | solution.py:42
  112.1 1.8 %collective-permute-done.33 = bf16[32,2176]{1,0:T(8,128)(2,1)S(1)} collective-permute-done((bf16[32,2176]{1,0:T(8,128)(2,1)S(1)}, bf16[32,2176]{1,0:T(8,128)(2,1)S(1)}, u32[]{:S(2)}, u32[]{:S(2)}) %collective-permute-start.33) | collective-permute-done | bytes 139296 | tf_op jit(solution)/shard_map/ppermute | solution.py:42
  113.9 1.6 collective-permute-done.34
  116.0 1.7 collective-permute-start.35
  118.9 1.8 %collective-permute-start.49 = (bf16[32,2176]{1,0:T(8,128)(2,1)S(1)}, bf16[32,2176]{1,0:T(8,128)(2,1)S(1)}, u32[]{:S(2)}, u32[]{:S(2)}) collective-permute-start(bf16[32,2176]{1,0:T(8,128)(2,1)S(1)} %get-tuple-element.43), channel_id=1, source_target_pairs={{0,2},{2,4},{4,6},{6,7},{7,5},{5,3},{3,1},{1,0},{8,10},{10,12},{12... | collective-permute-start | bytes 417800 | tf_op jit(solution)/shard_map/ppermute | solution.py:42
  123.7 1.4 collective-permute-done.50
  125.4 1.5 collective-permute-start.52
  127.7 2.8 %collective-permute-done.52 = bf16[32,2176]{1,0:T(8,128)(2,1)S(1)} collective-permute-done((bf16[32,2176]{1,0:T(8,128)(2,1)S(1)}, bf16[32,2176]{1,0:T(8,128)(2,1)S(1)}, u32[]{:S(2)}, u32[]{:S(2)}) %collective-permute-start.52) | collective-permute-done | bytes 139296 | tf_op jit(solution)/shard_map/ppermute | solution.py:42
  130.6 1.4 collective-permute-done.51
  132.5 1.4 fusion.21
  133.9 1.4 fusion.20
  136.3 1.4 collective-permute-start.39
  138.4 1.4 collective-permute-start.43
  139.8 2.2 %collective-permute-done.56.refs_12_ = bf16[32,2048]{1,0:T(8,128)(2,1)S(1)} collective-permute-done((bf16[32,2048]{1,0:T(8,128)(2,1)S(1)}, bf16[32,2048]{1,0:T(8,128)(2,1)S(1)}, u32[]{:S(2)}, u32[]{:S(2)}) %collective-permute-start.56) | collective-permute-done | bytes 131104 | tf_op jit(solution)/shard_map/ppermute | solution.py:42
  142.7 1.4 collective-permute-start.40
  145.2 1.4 collective-permute-start.54
  148.6 1.4 collective-permute-start.41
  150.1 1.4 collective-permute-done.54.refs_9_
  151.5 1.6 collective-permute-start.55
  155.0 1.4 collective-permute-start.42
  159.9 11.7 %shard_map.101 = (f32[2048,3072]{1,0:T(8,128)}, bf16[64,2048]{1,0:T(8,128)(2,1)}) custom-call(s32[17]{0:T(128)S(1)} %slice_bitcast_fusion.3.index_ref, bf16[512,3072]{1,0:T(8,128)(2,1)S(1)} %bitcast.57, bf16[32,2048]{1,0:T(8,128)(2,1)S(1)} %collective-permute-done.42.refs_0_, bf16[32,2048]{1,0:T(8,128)(2,1)S(1)} %collective-permute-done.41.refs_1_, ...), custom_call_target="tpu_custom_call" | custom-call | flops 6442450944 | bytes 30408704 | tf_op jit(solution)/shard_map/pallas_call | solution.py:385
  (146 shorter events, 43.4 us)
Async XLA Ops:
  0.6 17.6 %collective-permute-start.4 = (bf16[128,1024]{1,0:T(8,128)(2,1)}, bf16[128,1024]{1,0:T(8,128)(2,1)S(1)}, u32[]{:S(2)}, u32[]{:S(2)}) collective-permute-start(bf16[128,1024]{1,0:T(8,128)(2,1)} %param.8), channel_id=1, source_target_pairs={{0,0},{1,1},{2,8},{3,9},{4,16},{5,17},{6,24},{7,25},{8,4},{9,5},{1... | collective-permute-start | bytes 786440 | tf_op jit(solution)/shard_map/ppermute | solution.py:493
  7.9 10.3 %collective-permute-start.3 = (f32[1,128]{1,0:T(1,128)S(1)}, f32[1,128]{1,0:T(1,128)S(1)}, u32[]{:S(2)}, u32[]{:S(2)}) collective-permute-start(f32[1,128]{1,0:T(1,128)S(1)} %bitcast_add_fusion), channel_id=1, source_target_pairs={{0,6},{1,7},{2,4},{3,5},{4,2},{5,3},{6,0},{7,1},{8,14},{9,15},{10,... | collective-permute-start | bytes 1544 | tf_op jit(solution)/shard_map/ppermute | solution.py:47
  12.9 5.3 %collective-permute-start.2 = (f32[1,128]{1,0:T(1,128)S(1)}, f32[1,128]{1,0:T(1,128)S(1)}, u32[]{:S(2)}, u32[]{:S(2)}) collective-permute-start(f32[1,128]{1,0:T(1,128)S(1)} %bitcast_add_fusion), channel_id=1, source_target_pairs={{0,4},{1,5},{2,6},{3,7},{4,0},{5,1},{6,2},{7,3},{8,12},{9,13},{10,... | collective-permute-start | bytes 1544 | tf_op jit(solution)/shard_map/ppermute | solution.py:47
  12.9 5.3 %collective-permute-start.1 = (f32[1,128]{1,0:T(1,128)S(1)}, f32[1,128]{1,0:T(1,128)S(1)}, u32[]{:S(2)}, u32[]{:S(2)}) collective-permute-start(f32[1,128]{1,0:T(1,128)S(1)} %bitcast_add_fusion), channel_id=1, source_target_pairs={{0,2},{1,3},{2,0},{3,1},{4,6},{5,7},{6,4},{7,5},{8,10},{9,11},{10,... | collective-permute-start | bytes 1544 | tf_op jit(solution)/shard_map/ppermute | solution.py:47
  18.2 6.4 %collective-permute-start.17 = (bf16[64,1024]{1,0:T(8,128)(2,1)S(1)}, bf16[64,1024]{1,0:T(8,128)(2,1)S(1)}, u32[]{:S(2)}, u32[]{:S(2)}) collective-permute-start(bf16[64,1024]{1,0:T(8,128)(2,1)S(1)} %get-tuple-element.72.refs_11_), channel_id=1, source_target_pairs={{0,1},{2,0},{4,2},{6,4},{7,6},{5,7},{3,5},{1,3},{8,9},{10,8},{12,1... | collective-permute-start | bytes 393224 | tf_op jit(solution)/shard_map/ppermute | solution.py:42
  19.8 6.4 %collective-permute-start.5 = (bf16[64,1024]{1,0:T(8,128)(2,1)S(1)}, bf16[64,1024]{1,0:T(8,128)(2,1)S(1)}, u32[]{:S(2)}, u32[]{:S(2)}) collective-permute-start(bf16[64,1024]{1,0:T(8,128)(2,1)S(1)} %get-tuple-element.73.refs_4_), channel_id=1, source_target_pairs={{0,2},{2,4},{4,6},{6,7},{7,5},{5,3},{3,1},{1,0},{8,10},{10,12},{12... | collective-permute-start | bytes 393224 | tf_op jit(solution)/shard_map/ppermute | solution.py:42
  20.4 11.2 %collective-permute-start.14 = (bf16[64,1024]{1,0:T(8,128)(2,1)S(1)}, bf16[64,1024]{1,0:T(8,128)(2,1)S(1)}, u32[]{:S(2)}, u32[]{:S(2)}) collective-permute-start(bf16[64,1024]{1,0:T(8,128)(2,1)S(1)} %get-tuple-element.72.refs_11_), channel_id=1, source_target_pairs={{0,2},{2,4},{4,6},{6,7},{7,5},{5,3},{3,1},{1,0},{8,10},{10,12},{12... | collective-permute-start | bytes 393224 | tf_op jit(solution)/shard_map/ppermute | solution.py:42
  21.8 5.7 %collective-permute-start.6 = (bf16[64,1024]{1,0:T(8,128)(2,1)S(1)}, bf16[64,1024]{1,0:T(8,128)(2,1)S(1)}, u32[]{:S(2)}, u32[]{:S(2)}) collective-permute-start(bf16[64,1024]{1,0:T(8,128)(2,1)S(1)} %get-tuple-element.73.refs_4_), channel_id=1, source_target_pairs={{0,1},{2,0},{4,2},{6,4},{7,6},{5,7},{3,5},{1,3},{8,9},{10,8},{12,1... | collective-permute-start | bytes 393224 | tf_op jit(solution)/shard_map/ppermute | solution.py:42
  24.6 7.5 %collective-permute-start.18 = (bf16[64,1024]{1,0:T(8,128)(2,1)S(1)}, bf16[64,1024]{1,0:T(8,128)(2,1)S(1)}, u32[]{:S(2)}, u32[]{:S(2)}) collective-permute-start(bf16[64,1024]{1,0:T(8,128)(2,1)S(1)} %collective-permute-done.17.refs_12_), channel_id=1, source_target_pairs={{0,1},{2,0},{4,2},{6,4},{7,6},{5,7},{3,5},{1,3},{8,9},{10,8},{12,1... | collective-permute-start | bytes 393224 | tf_op jit(solution)/shard_map/ppermute | solution.py:42
  26.2 7.4 %collective-permute-start.8 = (bf16[64,1024]{1,0:T(8,128)(2,1)S(1)}, bf16[64,1024]{1,0:T(8,128)(2,1)S(1)}, u32[]{:S(2)}, u32[]{:S(2)}) collective-permute-start(bf16[64,1024]{1,0:T(8,128)(2,1)S(1)} %collective-permute-done.5.refs_3_), channel_id=1, source_target_pairs={{0,2},{2,4},{4,6},{6,7},{7,5},{5,3},{3,1},{1,0},{8,10},{10,12},{12... | collective-permute-start | bytes 393224 | tf_op jit(solution)/shard_map/ppermute | solution.py:42
  27.5 13.8 %collective-permute-start.7 = (f32[2,128]{1,0:T(2,128)S(1)}, f32[2,128]{1,0:T(2,128)S(1)}, u32[]{:S(2)}, u32[]{:S(2)}) collective-permute-start(f32[2,128]{1,0:T(2,128)S(1)} %pad_maximum_fusion.8), channel_id=1, source_target_pairs={{0,16},{8,24},{16,0},{24,8},{1,17},{9,25},{17,1},{25,9},{2,18},{10... | collective-permute-start | bytes 3080 | tf_op jit(solution)/shard_map/ppermute | solution.py:116
  30.1 7.7 %collective-permute-start.9 = (bf16[64,1024]{1,0:T(8,128)(2,1)S(1)}, bf16[64,1024]{1,0:T(8,128)(2,1)S(1)}, u32[]{:S(2)}, u32[]{:S(2)}) collective-permute-start(bf16[64,1024]{1,0:T(8,128)(2,1)S(1)} %collective-permute-done.6.refs_5_), channel_id=1, source_target_pairs={{0,1},{2,0},{4,2},{6,4},{7,6},{5,7},{3,5},{1,3},{8,9},{10,8},{12,1... | collective-permute-start | bytes 393224 | tf_op jit(solution)/shard_map/ppermute | solution.py:42
  31.6 5.7 %collective-permute-start.15 = (bf16[64,1024]{1,0:T(8,128)(2,1)S(1)}, bf16[64,1024]{1,0:T(8,128)(2,1)S(1)}, u32[]{:S(2)}, u32[]{:S(2)}) collective-permute-start(bf16[64,1024]{1,0:T(8,128)(2,1)S(1)} %collective-permute-done.14.refs_10_), channel_id=1, source_target_pairs={{0,2},{2,4},{4,6},{6,7},{7,5},{5,3},{3,1},{1,0},{8,10},{10,12},{12... | collective-permute-start | bytes 393224 | tf_op jit(solution)/shard_map/ppermute | solution.py:42
  32.1 7.2 %collective-permute-start.19 = (bf16[64,1024]{1,0:T(8,128)(2,1)S(1)}, bf16[64,1024]{1,0:T(8,128)(2,1)S(1)}, u32[]{:S(2)}, u32[]{:S(2)}) collective-permute-start(bf16[64,1024]{1,0:T(8,128)(2,1)S(1)} %collective-permute-done.18.refs_13_), channel_id=1, source_target_pairs={{0,1},{2,0},{4,2},{6,4},{7,6},{5,7},{3,5},{1,3},{8,9},{10,8},{12,1... | collective-permute-start | bytes 393224 | tf_op jit(solution)/shard_map/ppermute | solution.py:42
  33.6 6.5 %collective-permute-start.11 = (bf16[64,1024]{1,0:T(8,128)(2,1)S(1)}, bf16[64,1024]{1,0:T(8,128)(2,1)S(1)}, u32[]{:S(2)}, u32[]{:S(2)}) collective-permute-start(bf16[64,1024]{1,0:T(8,128)(2,1)S(1)} %collective-permute-done.8.refs_2_), channel_id=1, source_target_pairs={{0,2},{2,4},{4,6},{6,7},{7,5},{5,3},{3,1},{1,0},{8,10},{10,12},{12... | collective-permute-start | bytes 393224 | tf_op jit(solution)/shard_map/ppermute | solution.py:42
  37.3 6.9 %collective-permute-start.16 = (bf16[64,1024]{1,0:T(8,128)(2,1)S(1)}, bf16[64,1024]{1,0:T(8,128)(2,1)S(1)}, u32[]{:S(2)}, u32[]{:S(2)}) collective-permute-start(bf16[64,1024]{1,0:T(8,128)(2,1)S(1)} %collective-permute-done.15.refs_9_), channel_id=1, source_target_pairs={{0,2},{2,4},{4,6},{6,7},{7,5},{5,3},{3,1},{1,0},{8,10},{10,12},{12... | collective-permute-start | bytes 393224 | tf_op jit(solution)/shard_map/ppermute | solution.py:42
  37.8 6.4 %collective-permute-start.13 = (bf16[64,1024]{1,0:T(8,128)(2,1)S(1)}, bf16[64,1024]{1,0:T(8,128)(2,1)S(1)}, u32[]{:S(2)}, u32[]{:S(2)}) collective-permute-start(bf16[64,1024]{1,0:T(8,128)(2,1)S(1)} %collective-permute-done.9.refs_6_), channel_id=1, source_target_pairs={{0,1},{2,0},{4,2},{6,4},{7,6},{5,7},{3,5},{1,3},{8,9},{10,8},{12,1... | collective-permute-start | bytes 393224 | tf_op jit(solution)/shard_map/ppermute | solution.py:42
  55.0 14.1 %collective-permute-start.22 = (s16[128,2048]{1,0:T(8,128)(2,1)S(1)}, s16[128,2048]{1,0:T(8,128)(2,1)S(1)}, u32[]{:S(2)}, u32[]{:S(2)}) collective-permute-start(s16[128,2048]{1,0:T(8,128)(2,1)S(1)} %round-nearest-even_convert_fusion), channel_id=1, source_target_pairs={{0,16},{8,24},{16,0},{24,8},{1,17},{9,25},{17,1},{25,9},{2,18},{10... | collective-permute-start | bytes 1572872 | tf_op jit(solution)/shard_map/ppermute | solution.py:116
  56.5 12.6 %collective-permute-start.23 = (f32[128]{0:T(128)S(1)}, f32[128]{0:T(128)S(1)}, u32[]{:S(2)}, u32[]{:S(2)}) collective-permute-start(f32[128]{0:T(128)S(1)} %get-tuple-element.102), channel_id=1, source_target_pairs={{0,16},{8,24},{16,0},{24,8},{1,17},{9,25},{17,1},{25,9},{2,18},{10... | collective-permute-start | bytes 1544 | tf_op jit(solution)/shard_map/ppermute | solution.py:116
  73.4 5.4 %collective-permute-start.27 = (f32[2,256]{1,0:T(2,128)S(1)}, f32[2,256]{1,0:T(2,128)S(1)}, u32[]{:S(2)}, u32[]{:S(2)}) collective-permute-start(f32[2,256]{1,0:T(2,128)S(1)} %pad_maximum_fusion.7), channel_id=1, source_target_pairs={{0,6},{1,7},{2,4},{3,5},{4,2},{5,3},{6,0},{7,1},{8,14},{9,15},{10,... | collective-permute-start | bytes 6152 | tf_op jit(solution)/shard_map/ppermute | solution.py:47
  81.4 11.3 %collective-permute-start.28 = (bf16[128,2176]{1,0:T(8,128)(2,1)S(1)}, bf16[128,2176]{1,0:T(8,128)(2,1)S(1)}, u32[]{:S(2)}, u32[]{:S(2)}) collective-permute-start(bf16[128,2176]{1,0:T(8,128)(2,1)S(1)} %get-tuple-element.71), channel_id=1, source_target_pairs={{0,16},{8,24},{16,0},{24,8},{1,17},{9,25},{17,1},{25,9},{2,18},{10... | collective-permute-start | bytes 1671176 | tf_op jit(solution)/shard_map/ppermute | solution.py:116
  101.7 30.3 %collective-permute-start.30 = (bf16[2,64,3072]{2,1,0:T(8,128)(2,1)S(1)}, bf16[2,64,3072]{2,1,0:T(8,128)(2,1)S(1)}, u32[]{:S(2)}, u32[]{:S(2)}) collective-permute-start(bf16[2,64,3072]{2,1,0:T(8,128)(2,1)S(1)} %bitcast.54), channel_id=1, source_target_pairs={{0,16},{8,24},{16,0},{24,8},{1,17},{9,25},{17,1},{25,9},{2,18},{10... | collective-permute-start | bytes 2359304 | tf_op jit(solution)/shard_map/ppermute | solution.py:116
  102.4 5.5 %collective-permute-start.32 = (bf16[32,2176]{1,0:T(8,128)(2,1)S(1)}, bf16[32,2176]{1,0:T(8,128)(2,1)S(1)}, u32[]{:S(2)}, u32[]{:S(2)}) collective-permute-start(bf16[32,2176]{1,0:T(8,128)(2,1)S(1)} %get-tuple-element.68), channel_id=1, source_target_pairs={{0,2},{2,4},{4,6},{6,7},{7,5},{5,3},{3,1},{1,0},{8,10},{10,12},{12... | collective-permute-start | bytes 417800 | tf_op jit(solution)/shard_map/ppermute | solution.py:42
  104.1 5.9 %collective-permute-start.46 = (bf16[32,2176]{1,0:T(8,128)(2,1)S(1)}, bf16[32,2176]{1,0:T(8,128)(2,1)S(1)}, u32[]{:S(2)}, u32[]{:S(2)}) collective-permute-start(bf16[32,2176]{1,0:T(8,128)(2,1)S(1)} %get-tuple-element.67), channel_id=1, source_target_pairs={{0,1},{2,0},{4,2},{6,4},{7,6},{5,7},{3,5},{1,3},{8,9},{10,8},{12,1... | collective-permute-start | bytes 417800 | tf_op jit(solution)/shard_map/ppermute | solution.py:42
  107.9 6.0 %collective-permute-start.33 = (bf16[32,2176]{1,0:T(8,128)(2,1)S(1)}, bf16[32,2176]{1,0:T(8,128)(2,1)S(1)}, u32[]{:S(2)}, u32[]{:S(2)}) collective-permute-start(bf16[32,2176]{1,0:T(8,128)(2,1)S(1)} %add_convert_fusion.9), channel_id=1, source_target_pairs={{0,2},{2,4},{4,6},{6,7},{7,5},{5,3},{3,1},{1,0},{8,10},{10,12},{12... | collective-permute-start | bytes 417800 | tf_op jit(solution)/shard_map/ppermute | solution.py:42
  109.6 5.9 %collective-permute-start.34 = (bf16[32,2176]{1,0:T(8,128)(2,1)S(1)}, bf16[32,2176]{1,0:T(8,128)(2,1)S(1)}, u32[]{:S(2)}, u32[]{:S(2)}) collective-permute-start(bf16[32,2176]{1,0:T(8,128)(2,1)S(1)} %get-tuple-element.35), channel_id=1, source_target_pairs={{0,1},{2,0},{4,2},{6,4},{7,6},{5,7},{3,5},{1,3},{8,9},{10,8},{12,1... | collective-permute-start | bytes 417800 | tf_op jit(solution)/shard_map/ppermute | solution.py:42
  110.0 8.4 %collective-permute-start.48 = (bf16[32,2176]{1,0:T(8,128)(2,1)S(1)}, bf16[32,2176]{1,0:T(8,128)(2,1)S(1)}, u32[]{:S(2)}, u32[]{:S(2)}) collective-permute-start(bf16[32,2176]{1,0:T(8,128)(2,1)S(1)} %add_convert_fusion.3), channel_id=1, source_target_pairs={{0,1},{2,0},{4,2},{6,4},{7,6},{5,7},{3,5},{1,3},{8,9},{10,8},{12,1... | collective-permute-start | bytes 417800 | tf_op jit(solution)/shard_map/ppermute | solution.py:42
  111.4 7.1 %collective-permute-start.47 = (bf16[32,2176]{1,0:T(8,128)(2,1)S(1)}, bf16[32,2176]{1,0:T(8,128)(2,1)S(1)}, u32[]{:S(2)}, u32[]{:S(2)}) collective-permute-start(bf16[32,2176]{1,0:T(8,128)(2,1)S(1)} %get-tuple-element.41), channel_id=1, source_target_pairs={{0,2},{2,4},{4,6},{6,7},{7,5},{5,3},{3,1},{1,0},{8,10},{10,12},{12... | collective-permute-start | bytes 417800 | tf_op jit(solution)/shard_map/ppermute | solution.py:42
  115.5 6.0 %collective-permute-start.36 = (bf16[32,2176]{1,0:T(8,128)(2,1)S(1)}, bf16[32,2176]{1,0:T(8,128)(2,1)S(1)}, u32[]{:S(2)}, u32[]{:S(2)}) collective-permute-start(bf16[32,2176]{1,0:T(8,128)(2,1)S(1)} %get-tuple-element.37), channel_id=1, source_target_pairs={{0,1},{2,0},{4,2},{6,4},{7,6},{5,7},{3,5},{1,3},{8,9},{10,8},{12,1... | collective-permute-start | bytes 417800 | tf_op jit(solution)/shard_map/ppermute | solution.py:42
  116.0 5.6 %collective-permute-start.35 = (bf16[32,2176]{1,0:T(8,128)(2,1)S(1)}, bf16[32,2176]{1,0:T(8,128)(2,1)S(1)}, u32[]{:S(2)}, u32[]{:S(2)}) collective-permute-start(bf16[32,2176]{1,0:T(8,128)(2,1)S(1)} %get-tuple-element.36), channel_id=1, source_target_pairs={{0,2},{2,4},{4,6},{6,7},{7,5},{5,3},{3,1},{1,0},{8,10},{10,12},{12... | collective-permute-start | bytes 417800 | tf_op jit(solution)/shard_map/ppermute | solution.py:42
  118.5 6.6 %collective-permute-start.50 = (bf16[32,2176]{1,0:T(8,128)(2,1)S(1)}, bf16[32,2176]{1,0:T(8,128)(2,1)S(1)}, u32[]{:S(2)}, u32[]{:S(2)}) collective-permute-start(bf16[32,2176]{1,0:T(8,128)(2,1)S(1)} %get-tuple-element.44), channel_id=1, source_target_pairs={{0,1},{2,0},{4,2},{6,4},{7,6},{5,7},{3,5},{1,3},{8,9},{10,8},{12,1... | collective-permute-start | bytes 417800 | tf_op jit(solution)/shard_map/ppermute | solution.py:42
  118.9 6.5 %collective-permute-start.49 = (bf16[32,2176]{1,0:T(8,128)(2,1)S(1)}, bf16[32,2176]{1,0:T(8,128)(2,1)S(1)}, u32[]{:S(2)}, u32[]{:S(2)}) collective-permute-start(bf16[32,2176]{1,0:T(8,128)(2,1)S(1)} %get-tuple-element.43), channel_id=1, source_target_pairs={{0,2},{2,4},{4,6},{6,7},{7,5},{5,3},{3,1},{1,0},{8,10},{10,12},{12... | collective-permute-start | bytes 417800 | tf_op jit(solution)/shard_map/ppermute | solution.py:42
  121.6 5.9 %collective-permute-start.38 = (bf16[32,2176]{1,0:T(8,128)(2,1)S(1)}, bf16[32,2176]{1,0:T(8,128)(2,1)S(1)}, u32[]{:S(2)}, u32[]{:S(2)}) collective-permute-start(bf16[32,2176]{1,0:T(8,128)(2,1)S(1)} %get-tuple-element.39), channel_id=1, source_target_pairs={{0,1},{2,0},{4,2},{6,4},{7,6},{5,7},{3,5},{1,3},{8,9},{10,8},{12,1... | collective-permute-start | bytes 417800 | tf_op jit(solution)/shard_map/ppermute | solution.py:42
  122.6 5.1 %collective-permute-start.37 = (bf16[32,2176]{1,0:T(8,128)(2,1)S(1)}, bf16[32,2176]{1,0:T(8,128)(2,1)S(1)}, u32[]{:S(2)}, u32[]{:S(2)}) collective-permute-start(bf16[32,2176]{1,0:T(8,128)(2,1)S(1)} %get-tuple-element.38), channel_id=1, source_target_pairs={{0,2},{2,4},{4,6},{6,7},{7,5},{5,3},{3,1},{1,0},{8,10},{10,12},{12... | collective-permute-start | bytes 417800 | tf_op jit(solution)/shard_map/ppermute | solution.py:42
  125.4 5.1 %collective-permute-start.52 = (bf16[32,2176]{1,0:T(8,128)(2,1)S(1)}, bf16[32,2176]{1,0:T(8,128)(2,1)S(1)}, u32[]{:S(2)}, u32[]{:S(2)}) collective-permute-start(bf16[32,2176]{1,0:T(8,128)(2,1)S(1)} %get-tuple-element.46), channel_id=1, source_target_pairs={{0,1},{2,0},{4,2},{6,4},{7,6},{5,7},{3,5},{1,3},{8,9},{10,8},{12,1... | collective-permute-start | bytes 417800 | tf_op jit(solution)/shard_map/ppermute | solution.py:42
  132.2 24.2 %collective-permute-start.31 = (bf16[2,2,64,3072]{3,2,0,1:T(8,128)(2,1)S(1)}, bf16[2,2,64,3072]{3,2,0,1:T(8,128)(2,1)S(1)}, u32[]{:S(2)}, u32[]{:S(2)}) collective-permute-start(bf16[2,2,64,3072]{3,2,0,1:T(8,128)(2,1)S(1)} %pad_maximum_fusion.1), channel_id=1, source_target_pairs={{0,8},{8,0},{16,24},{24,16},{1,9},{9,1},{17,25},{25,17},{2,10},{10... | collective-permute-start | bytes 4718600 | tf_op jit(solution)/shard_map/ppermute | solution.py:112
  135.5 6.5 %collective-permute-start.56 = (bf16[32,2048]{1,0:T(8,128)(2,1)S(1)}, bf16[32,2048]{1,0:T(8,128)(2,1)S(1)}, u32[]{:S(2)}, u32[]{:S(2)}) collective-permute-start(bf16[32,2048]{1,0:T(8,128)(2,1)S(1)} %get-tuple-element.74.refs_11_), channel_id=1, source_target_pairs={{0,1},{2,0},{4,2},{6,4},{7,6},{5,7},{3,5},{1,3},{8,9},{10,8},{12,1... | collective-permute-start | bytes 393224 | tf_op jit(solution)/shard_map/ppermute | solution.py:42
  136.3 6.3 %collective-permute-start.39 = (bf16[32,2048]{1,0:T(8,128)(2,1)S(1)}, bf16[32,2048]{1,0:T(8,128)(2,1)S(1)}, u32[]{:S(2)}, u32[]{:S(2)}) collective-permute-start(bf16[32,2048]{1,0:T(8,128)(2,1)S(1)} %get-tuple-element.75.refs_4_), channel_id=1, source_target_pairs={{0,2},{2,4},{4,6},{6,7},{7,5},{5,3},{3,1},{1,0},{8,10},{10,12},{12... | collective-permute-start | bytes 393224 | tf_op jit(solution)/shard_map/ppermute | solution.py:42
  137.8 7.4 %collective-permute-start.53 = (bf16[32,2048]{1,0:T(8,128)(2,1)S(1)}, bf16[32,2048]{1,0:T(8,128)(2,1)S(1)}, u32[]{:S(2)}, u32[]{:S(2)}) collective-permute-start(bf16[32,2048]{1,0:T(8,128)(2,1)S(1)} %get-tuple-element.74.refs_11_), channel_id=1, source_target_pairs={{0,2},{2,4},{4,6},{6,7},{7,5},{5,3},{3,1},{1,0},{8,10},{10,12},{12... | collective-permute-start | bytes 393224 | tf_op jit(solution)/shard_map/ppermute | solution.py:42
  138.4 8.3 %collective-permute-start.43 = (bf16[32,2048]{1,0:T(8,128)(2,1)S(1)}, bf16[32,2048]{1,0:T(8,128)(2,1)S(1)}, u32[]{:S(2)}, u32[]{:S(2)}) collective-permute-start(bf16[32,2048]{1,0:T(8,128)(2,1)S(1)} %get-tuple-element.75.refs_4_), channel_id=1, source_target_pairs={{0,1},{2,0},{4,2},{6,4},{7,6},{5,7},{3,5},{1,3},{8,9},{10,8},{12,1... | collective-permute-start | bytes 393224 | tf_op jit(solution)/shard_map/ppermute | solution.py:42
  142.1 5.2 %collective-permute-start.57 = (bf16[32,2048]{1,0:T(8,128)(2,1)S(1)}, bf16[32,2048]{1,0:T(8,128)(2,1)S(1)}, u32[]{:S(2)}, u32[]{:S(2)}) collective-permute-start(bf16[32,2048]{1,0:T(8,128)(2,1)S(1)} %collective-permute-done.56.refs_12_), channel_id=1, source_target_pairs={{0,1},{2,0},{4,2},{6,4},{7,6},{5,7},{3,5},{1,3},{8,9},{10,8},{12,1... | collective-permute-start | bytes 393224 | tf_op jit(solution)/shard_map/ppermute | solution.py:42
  142.7 5.9 %collective-permute-start.40 = (bf16[32,2048]{1,0:T(8,128)(2,1)S(1)}, bf16[32,2048]{1,0:T(8,128)(2,1)S(1)}, u32[]{:S(2)}, u32[]{:S(2)}) collective-permute-start(bf16[32,2048]{1,0:T(8,128)(2,1)S(1)} %collective-permute-done.39.refs_3_), channel_id=1, source_target_pairs={{0,2},{2,4},{4,6},{6,7},{7,5},{5,3},{3,1},{1,0},{8,10},{10,12},{12... | collective-permute-start | bytes 393224 | tf_op jit(solution)/shard_map/ppermute | solution.py:42
  145.2 6.3 %collective-permute-start.54 = (bf16[32,2048]{1,0:T(8,128)(2,1)S(1)}, bf16[32,2048]{1,0:T(8,128)(2,1)S(1)}, u32[]{:S(2)}, u32[]{:S(2)}) collective-permute-start(bf16[32,2048]{1,0:T(8,128)(2,1)S(1)} %collective-permute-done.53.refs_10_), channel_id=1, source_target_pairs={{0,2},{2,4},{4,6},{6,7},{7,5},{5,3},{3,1},{1,0},{8,10},{10,12},{12... | collective-permute-start | bytes 393224 | tf_op jit(solution)/shard_map/ppermute | solution.py:42
  146.6 6.4 %collective-permute-start.44 = (bf16[32,2048]{1,0:T(8,128)(2,1)S(1)}, bf16[32,2048]{1,0:T(8,128)(2,1)S(1)}, u32[]{:S(2)}, u32[]{:S(2)}) collective-permute-start(bf16[32,2048]{1,0:T(8,128)(2,1)S(1)} %collective-permute-done.43.refs_5_), channel_id=1, source_target_pairs={{0,1},{2,0},{4,2},{6,4},{7,6},{5,7},{3,5},{1,3},{8,9},{10,8},{12,1... | collective-permute-start | bytes 393224 | tf_op jit(solution)/shard_map/ppermute | solution.py:42
  147.3 6.6 %collective-permute-start.58 = (bf16[32,2048]{1,0:T(8,128)(2,1)S(1)}, bf16[32,2048]{1,0:T(8,128)(2,1)S(1)}, u32[]{:S(2)}, u32[]{:S(2)}) collective-permute-start(bf16[32,2048]{1,0:T(8,128)(2,1)S(1)} %collective-permute-done.57.refs_13_), channel_id=1, source_target_pairs={{0,1},{2,0},{4,2},{6,4},{7,6},{5,7},{3,5},{1,3},{8,9},{10,8},{12,1... | collective-permute-start | bytes 393224 | tf_op jit(solution)/shard_map/ppermute | solution.py:42
  148.6 6.4 %collective-permute-start.41 = (bf16[32,2048]{1,0:T(8,128)(2,1)S(1)}, bf16[32,2048]{1,0:T(8,128)(2,1)S(1)}, u32[]{:S(2)}, u32[]{:S(2)}) collective-permute-start(bf16[32,2048]{1,0:T(8,128)(2,1)S(1)} %collective-permute-done.40.refs_2_), channel_id=1, source_target_pairs={{0,2},{2,4},{4,6},{6,7},{7,5},{5,3},{3,1},{1,0},{8,10},{10,12},{12... | collective-permute-start | bytes 393224 | tf_op jit(solution)/shard_map/ppermute | solution.py:42
  151.5 6.1 %collective-permute-start.55 = (bf16[32,2048]{1,0:T(8,128)(2,1)S(1)}, bf16[32,2048]{1,0:T(8,128)(2,1)S(1)}, u32[]{:S(2)}, u32[]{:S(2)}) collective-permute-start(bf16[32,2048]{1,0:T(8,128)(2,1)S(1)} %collective-permute-done.54.refs_9_), channel_id=1, source_target_pairs={{0,2},{2,4},{4,6},{6,7},{7,5},{5,3},{3,1},{1,0},{8,10},{10,12},{12... | collective-permute-start | bytes 393224 | tf_op jit(solution)/shard_map/ppermute | solution.py:42
  153.9 5.6 %collective-permute-start.59 = (bf16[32,2048]{1,0:T(8,128)(2,1)S(1)}, bf16[32,2048]{1,0:T(8,128)(2,1)S(1)}, u32[]{:S(2)}, u32[]{:S(2)}) collective-permute-start(bf16[32,2048]{1,0:T(8,128)(2,1)S(1)} %collective-permute-done.58.refs_14_), channel_id=1, source_target_pairs={{0,1},{2,0},{4,2},{6,4},{7,6},{5,7},{3,5},{1,3},{8,9},{10,8},{12,1... | collective-permute-start | bytes 393224 | tf_op jit(solution)/shard_map/ppermute | solution.py:42
  (17 other events, 88.6 us)

commit v14 on v13

--- a/solution.py
+++ b/solution.py
@@ -178,66 +178,52 @@
     )(logits)
 
 
-def hold_kernel(weight_ref, held_ref, sems):
-    tile = weight_ref.shape[0] // sems.shape[0]
-    copies = [
-        pltpu.make_async_copy(
-            weight_ref.at[pl.ds(n * tile, tile), :], held_ref.at[pl.ds(n * tile, tile), :], sems.at[n]
-        )
-        for n in range(sems.shape[0])
-    ]
-    for copy in copies:
-        copy.start()
-    for copy in copies:
-        copy.wait()
-
-
-def hold(weight):
-    return pl.pallas_call(
-        hold_kernel,
-        in_specs=[pl.BlockSpec(memory_space=pltpu.HBM)],
-        out_specs=VMEM,
-        out_shape=jax.ShapeDtypeStruct(weight.shape, weight.dtype),
-        scratch_shapes=[pltpu.SemaphoreType.DMA((4,))],
-        compiler_params=pltpu.CompilerParams(vmem_limit_bytes=12 * 2**20),
-        cost_estimate=pl.CostEstimate(flops=0, bytes_accessed=2 * weight.size, transcendentals=0),
-    )(weight)
-
-
 def project_kernel(count, tile, index_ref, factor_ref, gain_ref, weight_ref, *refs):
     blocks, refs = refs[: CHUNKS * count], refs[CHUNKS * count :]
-    send_ref, turned_ref = refs[:2]
-    piece_refs = refs[2 : 2 + CHUNKS]
-    raw_ref, other_ref = refs[2 + CHUNKS :]
+    send_ref, turned_ref, held_ref = refs[:3]
+    piece_refs = refs[3 : 3 + CHUNKS]
+    raw_ref, other_ref, sems = refs[3 + CHUNKS :]
     rows, width = blocks[0].shape
+    depth = raw_ref.shape[1]
     group_rows = CHUNKS * rows
     groups = factor_ref.shape[0]
     piece = piece_refs[0].shape[0]
     step = pl.program_id(0)
 
+    def fetch(n):
+        tile_rows = pl.ds(pl.multiple_of(n * tile, tile), tile)
+        return pltpu.make_async_copy(
+            weight_ref.at[tile_rows, :], held_ref.at[tile_rows, :], sems.at[n]
+        )
+
     @pl.when(step == 0)
     def _():
+        for n in range(sems.shape[0]):
+            fetch(n).start()
         for k, ref in enumerate(blocks):
             h, at = k // count, k + k // count * count
             start = pl.multiple_of(index_ref[at] * group_rows + h * rows, rows)
             column = pl.multiple_of(index_ref[at + count] * width, width)
             raw_ref[pl.ds(start, rows), pl.ds(column, width)] = ref[...]
-        slab = min(raw_ref.shape[1], 256)
+        slab = min(depth, 256)
+        gain_start = index_ref[2 * CHUNKS * count + CHUNKS] * depth
         for g in range(groups):
             half_ref = turned_ref if g < groups // CORES else other_ref
             place = pl.ds(g % (groups // CORES) * group_rows, group_rows)
-            for first in range(0, raw_ref.shape[1], slab):
+            for first in range(0, depth, slab):
                 columns = pl.ds(first, slab)
+                gain = gain_ref[:, pl.ds(pl.multiple_of(gain_start + first, slab), slab)]
                 values = raw_ref[pl.ds(g * group_rows, group_rows), columns].astype(F32)
-                values = (values * gain_ref[:, columns]).T * factor_ref[g : g + 1, :]
+                values = (values * gain).T * factor_ref[g : g + 1, :]
                 half_ref[columns, place] = values.astype(BF16)
         for h, ref in enumerate(piece_refs):
             start = pl.multiple_of(index_ref[2 * CHUNKS * count + h] * piece, piece)
             ref[...] = raw_ref[pl.ds(start, piece), :]
 
+    fetch(step).wait()
     rows = pl.ds(pl.multiple_of(step * tile, tile), tile)
     send_ref[...] = jnp.dot(
-        weight_ref[rows, :], other_ref[...], preferred_element_type=F32
+        held_ref[rows, :], other_ref[...], preferred_element_type=F32
     ).T
 
 
@@ -262,14 +248,24 @@
         bytes_accessed=2 * vocab * depth + half * (4 * depth + 4 * vocab),
         transcendentals=0,
     )
-    send, turned, *pieces = pl.pallas_call(
+    send, turned, held, *pieces = pl.pallas_call(
         functools.partial(project_kernel, len(blocks[0]), tile),
         grid=(vocab // tile,),
-        in_specs=[SMEM] + [VMEM] * (3 + CHUNKS * len(blocks[0])),
-        out_specs=[out_spec, whole(depth, half)] + [whole(piece_rows, depth)] * CHUNKS,
-        out_shape=[out, jax.ShapeDtypeStruct((depth, half), BF16)] + [piece] * CHUNKS,
-        scratch_shapes=[pltpu.VMEM((all_rows, depth), BF16), pltpu.VMEM((depth, half), BF16)],
-        compiler_params=pltpu.CompilerParams(vmem_limit_bytes=28 * 2**20),
+        in_specs=[SMEM, VMEM, VMEM, pl.BlockSpec(memory_space=pltpu.HBM)]
+        + [VMEM] * (CHUNKS * len(blocks[0])),
+        out_specs=[out_spec, whole(depth, half), VMEM] + [whole(piece_rows, depth)] * CHUNKS,
+        out_shape=[
+            out,
+            jax.ShapeDtypeStruct((depth, half), BF16),
+            jax.ShapeDtypeStruct(weight.shape, BF16),
+        ]
+        + [piece] * CHUNKS,
+        scratch_shapes=[
+            pltpu.VMEM((all_rows, depth), BF16),
+            pltpu.VMEM((depth, half), BF16),
+            pltpu.SemaphoreType.DMA((vocab // tile,)),
+        ],
+        compiler_params=pltpu.CompilerParams(vmem_limit_bytes=36 * 2**20),
         cost_estimate=cost,
     )(index, factor, gain, weight, *[x for chunk in blocks for x in chunk])
     keep = pl.pallas_call(
@@ -280,8 +276,8 @@
         out_shape=out,
         compiler_params=pltpu.CompilerParams(vmem_limit_bytes=20 * 2**20),
         cost_estimate=cost,
-    )(weight, turned)
-    return [keep, send] + pieces
+    )(held, turned)
+    return [keep, send, held] + pieces
 
 
 def back_kernel(piece, tile, index_ref, mine_ref, other_ref, weight_ref, *refs):
@@ -432,6 +428,7 @@
                 start = p * piece_rows
                 start = start // chunk_rows * group_rows + h * chunk_rows + start % chunk_rows
                 place.append(start // piece_rows)
+            place.append(g)
             add("place", place)
             entry = groups.entry(g, v * share_rows // group_rows)
             first = v * share_rows % group_rows
@@ -492,8 +489,6 @@
     ]
     turned = lax.ppermute(hidden, ("dp", "vocab"), turn)
 
-    weight = hold(head_weight)
-
     live_rows = (valid_rows == 1).astype(F32)
     squares = jnp.sum(jnp.square(hidden.astype(F32)), axis=1)[None]
     rounds = ring.meetings(lambda terms: sum(terms[1:], terms[0]))
@@ -501,7 +496,7 @@
     rounds.append(lambda x: jnp.concatenate([x, groups.swap(x)], axis=0))
     for round in rounds[:2]:
         squares = round(squares)
-    turned = after(turned, squares, weight)
+    turned = after(turned, squares)
     late = rounds[2:]
     exchanged = [squares]
 
@@ -528,8 +523,8 @@
     row_weight = 1048576.0 * live_rows / valid_count
     lane = lax.broadcasted_iota(jnp.uint32, (group_rows, LANES), 1)
 
-    keep, send, *pieces = project(
-        index["place"], blocks, row_factor, gain, weight, piece_rows
+    keep, send, weight, *pieces = project(
+        index["place"], blocks, row_factor, norm_gain.reshape(1, -1), head_weight, piece_rows
     )
     other = groups.swap(send)
 
@@ -571,15 +566,18 @@
     def shares(product):
         return lambda t: product[t % parts * piece_rows :][:piece_rows]
 
+    weights, turns = [], []
+    for h in range(CHUNKS):
+        factor = row_factor[:, h * chunk_rows : (h + 1) * chunk_rows]
+        own_factor = lax.dynamic_slice(factor, (own_entry, own_first), (1, piece_rows))[0]
+        weights.append(own_factor[:, None] * gain)
+        turns.append(pieces[h].astype(F32) * (own_factor**2 / model_width)[:, None])
+    weights, turns = lax.optimization_barrier((weights, turns))
+
     grads = []
     for h, summed in enumerate(ring.scatter_sums([shares(x) for x in products])):
-        factor = row_factor[:, h * chunk_rows : (h + 1) * chunk_rows]
-        own_factor = lax.dynamic_slice(factor, (own_entry, own_first), (1, piece_rows))[0]
-        row_dot = jnp.sum(summed[:, slice_width:], axis=1) / own_factor
-        grad_piece = (
-            own_factor[:, None] * gain * summed[:, :slice_width]
-            - pieces[h].astype(F32) * (own_factor**3 * row_dot / model_width)[:, None]
-        ).astype(BF16)
+        dot = jnp.sum(summed[:, slice_width:], axis=1, keepdims=True)
+        grad_piece = (weights[h] * summed[:, :slice_width] - turns[h] * dot).astype(BF16)
         grads.append(ring.gather(grad_piece, h))
 
     grad_joining, grad_share = outer(index["pieces"], chosen, grads, group_rows // slots)

time: 172 us -> 172 us (level)
  waiting for transfers between devices: 60.5 us -> 64.5 us
  local copies, waits for them, and re-layouts: 6.48 us -> 3.1 us
    ppermute x8, waiting for transfers between devices: 5.09 us -> 11.8 us  [partner(): return lax.ppermute(x, 'vocab', [(v, v ^ bit) for v in range(self.size)])]
    ppermute x4, waiting for transfers between devices: 3.04 us -> 0.25 us  [swap(): return lax.ppermute(x, 'dp', [(i, i ^ 1) for i in range(self.size)])]
    unnamed x10, local copies, waits for them, and re-layouts: 3.4 us -> 0.78 us
    ppermute x42, starting transfers between devices: 43.9 us -> 42.1 us  [shift(): lax.ppermute(x, 'vocab', [(order[p], order[(p + step) % size]) for p in r...]
  transfers between devices with their start and end apart: 60 -> 60, of which waited for: 35 -> 34; matrix products, arithmetic and copies ran while one was open for 6% -> 6% of each run, Pallas kernels for 3% -> 2%
where the time goes in v14:
time: 172 us
  waiting for transfers between devices  64.5 us (38%)
  starting transfers between devices  64.1 us (37%)
  Pallas kernels  27.9 us (16%)
  other arithmetic  10.9 us (6%)
  local copies, waits for them, and re-layouts  3.1 us (2%)
    ppermute x42, starting transfers between devices, shift(): lax.ppermute(x, 'vocab', [(order[p], order[(p + step) % size]) for p in r...  42.1 us
    ppermute x42, waiting for transfers between devices, shift(): lax.ppermute(x, 'vocab', [(order[p], order[(p + step) % size]) for p in r...  32 us
    ppermute x5, waiting for transfers between devices, shift(): lax.ppermute(x, 'dp', [(i, (i + CORES * step) % size) for i in range(size)])  20.4 us
    ppermute x8, starting transfers between devices, partner(): return lax.ppermute(x, 'vocab', [(v, v ^ bit) for v in range(self.size)])  14.5 us
    ppermute x8, waiting for transfers between devices, partner(): return lax.ppermute(x, 'vocab', [(v, v ^ bit) for v in range(self.size)])  11.8 us
    pallas_call x1, Pallas kernels, outer(): pl.pallas_call(functools.partial(outer_kernel, len(chunks[0]), copies), g...  11.7 us
    pallas_call x1, Pallas kernels, project(): pl.pallas_call(functools.partial(project_kernel, len(blocks[0]), tile), g...  6.04 us
    pallas_call x1, Pallas kernels, back(): pl.pallas_call(functools.partial(back_kernel, piece_rows, tile), grid=(de...  5.81 us
  transfers between devices with their start and end apart: 60, of which 34 were waited for; matrix products, arithmetic and copies ran while one was open for 6% of the time, Pallas kernels for 2%

profile of v14, /device:TPU:0, one launch (start us, length us, event | category | flops | bytes accessed | tf_op | source)
XLA Modules:
  0.0 171.6 jit_solution(13375501060064266997)
XLA Ops:
  1.7 3.0 %collective-permute-start = (f32[1,128]{1,0:T(1,128)S(1)}, f32[1,128]{1,0:T(1,128)S(1)}, u32[]{:S(2)}, u32[]{:S(2)}) collective-permute-start(f32[1,128]{1,0:T(1,128)S(1)} %bitcast.77), channel_id=1, source_target_pairs={{0,1},{1,0},{2,3},{3,2},{4,5},{5,4},{6,7},{7,6},{8,9},{9,8},{10,11... | collective-permute-start | bytes 1544 | tf_op jit(solution)/shard_map/ppermute | solution.py:47
  4.7 1.6 collective-permute-start.4
  6.3 4.3 %collective-permute-start.3 = (f32[1,128]{1,0:T(1,128)S(1)}, f32[1,128]{1,0:T(1,128)S(1)}, u32[]{:S(2)}, u32[]{:S(2)}) collective-permute-start(f32[1,128]{1,0:T(1,128)S(1)} %bitcast_add_fusion), channel_id=1, source_target_pairs={{0,6},{1,7},{2,4},{3,5},{4,2},{5,3},{6,0},{7,1},{8,14},{9,15},{10,... | collective-permute-start | bytes 1544 | tf_op jit(solution)/shard_map/ppermute | solution.py:47
  11.3 6.3 %collective-permute-done.3 = f32[1,128]{1,0:T(1,128)S(1)} collective-permute-done((f32[1,128]{1,0:T(1,128)S(1)}, f32[1,128]{1,0:T(1,128)S(1)}, u32[]{:S(2)}, u32[]{:S(2)}) %collective-permute-start.3) | collective-permute-done | bytes 544 | tf_op jit(solution)/shard_map/ppermute | solution.py:47
  19.0 1.5 collective-permute-start.5
  20.6 1.9 %collective-permute-start.6 = (bf16[64,1024]{1,0:T(8,128)(2,1)S(1)}, bf16[64,1024]{1,0:T(8,128)(2,1)S(1)}, u32[]{:S(2)}, u32[]{:S(2)}) collective-permute-start(bf16[64,1024]{1,0:T(8,128)(2,1)S(1)} %get-tuple-element.83.refs_4_), channel_id=1, source_target_pairs={{0,1},{2,0},{4,2},{6,4},{7,6},{5,7},{3,5},{1,3},{8,9},{10,8},{12,1... | collective-permute-start | bytes 393224 | tf_op jit(solution)/shard_map/ppermute | solution.py:42
  22.5 2.3 %collective-permute-done.17.refs_12_ = bf16[64,1024]{1,0:T(8,128)(2,1)S(1)} collective-permute-done((bf16[64,1024]{1,0:T(8,128)(2,1)S(1)}, bf16[64,1024]{1,0:T(8,128)(2,1)S(1)}, u32[]{:S(2)}, u32[]{:S(2)}) %collective-permute-start.17) | collective-permute-done | bytes 131104 | tf_op jit(solution)/shard_map/ppermute | solution.py:42
  25.3 1.6 collective-permute-start.8
  27.7 1.3 collective-permute-start.7
  29.2 1.8 %collective-permute-start.15 = (bf16[64,1024]{1,0:T(8,128)(2,1)S(1)}, bf16[64,1024]{1,0:T(8,128)(2,1)S(1)}, u32[]{:S(2)}, u32[]{:S(2)}) collective-permute-start(bf16[64,1024]{1,0:T(8,128)(2,1)S(1)} %collective-permute-done.14.refs_10_), channel_id=1, source_target_pairs={{0,2},{2,4},{4,6},{6,7},{7,5},{5,3},{3,1},{1,0},{8,10},{10,12},{12... | collective-permute-start | bytes 393224 | tf_op jit(solution)/shard_map/ppermute | solution.py:42
  31.5 1.6 collective-permute-start.11
  34.5 1.6 collective-permute-start.16
  36.6 1.6 collective-permute-start.12
  38.7 2.2 %collective-permute-done.16.refs_8_ = bf16[64,1024]{1,0:T(8,128)(2,1)S(1)} collective-permute-done((bf16[64,1024]{1,0:T(8,128)(2,1)S(1)}, bf16[64,1024]{1,0:T(8,128)(2,1)S(1)}, u32[]{:S(2)}, u32[]{:S(2)}) %collective-permute-start.16) | collective-permute-done | bytes 131104 | tf_op jit(solution)/shard_map/ppermute | solution.py:42
  40.9 1.9 %collective-permute-done.20.refs_15_ = bf16[64,1024]{1,0:T(8,128)(2,1)S(1)} collective-permute-done((bf16[64,1024]{1,0:T(8,128)(2,1)S(1)}, bf16[64,1024]{1,0:T(8,128)(2,1)S(1)}, u32[]{:S(2)}, u32[]{:S(2)}) %collective-permute-start.20) | collective-permute-done | bytes 131104 | tf_op jit(solution)/shard_map/ppermute | solution.py:42
  43.5 6.0 %shard_map.96 = (f32[256,2048]{1,0:T(8,128)S(1)}, bf16[2048,256]{1,0:T(8,128)(2,1)S(1)}, bf16[2048,2048]{1,0:T(8,128)(2,1)S(1)}, bf16[32,2048]{1,0:T(8,128)(2,1)S(1)}, bf16[32,2048]{1,0:T(8,128)(2,1)S(1)}) custom-call(s32[35]{0:T(128)S(1)} %slice_bitcast_fusion.1.index_ref, f32[4,128]{1,0:T(4,128)S(1)} %get-tuple-element.87.factor_ref, ...), custom_call_target="tpu_custom_call" | custom-call | flops 2147483648 | bytes 12582912 | tf_op jit(solution)/shard_map/pallas_call | solution.py:251
  50.3 3.3 %shard_map.97 = f32[256,2048]{1,0:T(8,128)S(1)} custom-call(bf16[2048,2048]{1,0:T(8,128)(2,1)S(1)} %get-tuple-element.34.weight_ref, bf16[2048,256]{1,0:T(8,128)(2,1)S(1)} %get-tuple-element.35.turned_ref), custom_call_target="tpu_custom_call" | custom-call | flops 2147483648 | bytes 12582912 | tf_op jit(solution)/shard_map/pallas_call | solution.py:271
  54.3 1.3 collective-permute-start.22
  57.1 11.4 %collective-permute-done.23 = f32[128]{0:T(128)S(1)} collective-permute-done((f32[128]{0:T(128)S(1)}, f32[128]{0:T(128)S(1)}, u32[]{:S(2)}, u32[]{:S(2)}) %collective-permute-start.23) | collective-permute-done | bytes 544 | tf_op jit(solution)/shard_map/ppermute | solution.py:116
  69.3 1.6 collective-permute-start.24
  70.8 1.2 iota_compare_fusion
  72.9 4.3 %collective-permute-start.27 = (f32[2,256]{1,0:T(2,128)S(1)}, f32[2,256]{1,0:T(2,128)S(1)}, u32[]{:S(2)}, u32[]{:S(2)}) collective-permute-start(f32[2,256]{1,0:T(2,128)S(1)} %pad_maximum_fusion.7), channel_id=1, source_target_pairs={{0,6},{1,7},{2,4},{3,5},{4,2},{5,3},{6,0},{7,1},{8,14},{9,15},{10,... | collective-permute-start | bytes 6152 | tf_op jit(solution)/shard_map/ppermute | solution.py:47
  78.8 3.6 %collective-permute-done.26 = f32[2,256]{1,0:T(2,128)S(1)} collective-permute-done((f32[2,256]{1,0:T(2,128)S(1)}, f32[2,256]{1,0:T(2,128)S(1)}, u32[]{:S(2)}, u32[]{:S(2)}) %collective-permute-start.26) | collective-permute-done | bytes 2080 | tf_op jit(solution)/shard_map/ppermute | solution.py:47
  85.8 9.0 %collective-permute-done.28 = bf16[128,2176]{1,0:T(8,128)(2,1)S(1)} collective-permute-done((bf16[128,2176]{1,0:T(8,128)(2,1)S(1)}, bf16[128,2176]{1,0:T(8,128)(2,1)S(1)}, u32[]{:S(2)}, u32[]{:S(2)}) %collective-permute-start.28) | collective-permute-done | bytes 557088 | tf_op jit(solution)/shard_map/ppermute | solution.py:116
  95.0 1.4 multiply_multiply_fusion
  96.3 1.4 multiply_multiply_fusion.1
  97.9 5.8 %shard_map.99 = (f32[256,2176]{1,0:T(8,128)S(1)}, f32[256,2176]{1,0:T(8,128)S(1)}) custom-call(s32[8]{0:T(128)S(1)} %slice_bitcast_fusion.2.index_ref, bf16[2,128,2176]{2,1,0:T(8,128)(2,1)S(1)} %pad_maximum_fusion.2.mine_ref, bf16[2,128,2176]{2,1,0:T(8,128)(2,1)S(1)} %collective-permute-done.29.other_ref, bf16[2048,2048]{1,0:T(8,128)(2,1)S(1)} %get-tuple-element.34.weight_ref), custom_call_target="tpu_custom_call" | custom-call | flops 4294967296 | bytes 14680064 | tf_op jit(solution)/shard_map/pallas_call | solution.py:314
  105.2 2.1 %collective-permute-start.46 = (bf16[32,2176]{1,0:T(8,128)(2,1)S(1)}, bf16[32,2176]{1,0:T(8,128)(2,1)S(1)}, u32[]{:S(2)}, u32[]{:S(2)}) collective-permute-start(bf16[32,2176]{1,0:T(8,128)(2,1)S(1)} %get-tuple-element.77), channel_id=1, source_target_pairs={{0,1},{2,0},{4,2},{6,4},{7,6},{5,7},{3,5},{1,3},{8,9},{10,8},{12,1... | collective-permute-start | bytes 417800 | tf_op jit(solution)/shard_map/ppermute | solution.py:42
  107.3 3.7 %collective-permute-done.32 = bf16[32,2176]{1,0:T(8,128)(2,1)S(1)} collective-permute-done((bf16[32,2176]{1,0:T(8,128)(2,1)S(1)}, bf16[32,2176]{1,0:T(8,128)(2,1)S(1)}, u32[]{:S(2)}, u32[]{:S(2)}) %collective-permute-start.32) | collective-permute-done | bytes 139296 | tf_op jit(solution)/shard_map/ppermute | solution.py:42
  111.3 1.7 %collective-permute-start.34 = (bf16[32,2176]{1,0:T(8,128)(2,1)S(1)}, bf16[32,2176]{1,0:T(8,128)(2,1)S(1)}, u32[]{:S(2)}, u32[]{:S(2)}) collective-permute-start(bf16[32,2176]{1,0:T(8,128)(2,1)S(1)} %get-tuple-element.44), channel_id=1, source_target_pairs={{0,1},{2,0},{4,2},{6,4},{7,6},{5,7},{3,5},{1,3},{8,9},{10,8},{12,1... | collective-permute-start | bytes 417800 | tf_op jit(solution)/shard_map/ppermute | solution.py:42
  113.1 1.4 collective-permute-start.48
  115.2 1.3 collective-permute-done.33
  116.5 1.4 collective-permute-done.34
  118.0 1.5 collective-permute-start.36
  121.0 1.5 collective-permute-start.50
  124.8 1.2 collective-permute-start.38
  128.6 1.4 collective-permute-start.52
  130.7 1.8 %collective-permute-done.37 = bf16[32,2176]{1,0:T(8,128)(2,1)S(1)} collective-permute-done((bf16[32,2176]{1,0:T(8,128)(2,1)S(1)}, bf16[32,2176]{1,0:T(8,128)(2,1)S(1)}, u32[]{:S(2)}, u32[]{:S(2)}) %collective-permute-start.37) | collective-permute-done | bytes 139296 | tf_op jit(solution)/shard_map/ppermute | solution.py:42
  133.7 1.3 collective-permute-done.51
  136.2 1.4 collective-permute-start.43
  139.4 2.3 %collective-permute-done.56.refs_12_ = bf16[32,2048]{1,0:T(8,128)(2,1)S(1)} collective-permute-done((bf16[32,2048]{1,0:T(8,128)(2,1)S(1)}, bf16[32,2048]{1,0:T(8,128)(2,1)S(1)}, u32[]{:S(2)}, u32[]{:S(2)}) %collective-permute-start.56) | collective-permute-done | bytes 131104 | tf_op jit(solution)/shard_map/ppermute | solution.py:42
  142.6 1.9 %collective-permute-done.43.refs_5_ = bf16[32,2048]{1,0:T(8,128)(2,1)S(1)} collective-permute-done((bf16[32,2048]{1,0:T(8,128)(2,1)S(1)}, bf16[32,2048]{1,0:T(8,128)(2,1)S(1)}, u32[]{:S(2)}, u32[]{:S(2)}) %collective-permute-start.43) | collective-permute-done | bytes 131104 | tf_op jit(solution)/shard_map/ppermute | solution.py:42
  147.3 1.5 collective-permute-start.58
  148.9 2.0 %collective-permute-done.44.refs_6_ = bf16[32,2048]{1,0:T(8,128)(2,1)S(1)} collective-permute-done((bf16[32,2048]{1,0:T(8,128)(2,1)S(1)}, bf16[32,2048]{1,0:T(8,128)(2,1)S(1)}, u32[]{:S(2)}, u32[]{:S(2)}) %collective-permute-start.44) | collective-permute-done | bytes 131104 | tf_op jit(solution)/shard_map/ppermute | solution.py:42
  152.9 1.8 %collective-permute-start.42 = (bf16[32,2048]{1,0:T(8,128)(2,1)S(1)}, bf16[32,2048]{1,0:T(8,128)(2,1)S(1)}, u32[]{:S(2)}, u32[]{:S(2)}) collective-permute-start(bf16[32,2048]{1,0:T(8,128)(2,1)S(1)} %collective-permute-done.41.refs_1_), channel_id=1, source_target_pairs={{0,2},{2,4},{4,6},{6,7},{7,5},{5,3},{3,1},{1,0},{8,10},{10,12},{12... | collective-permute-start | bytes 393224 | tf_op jit(solution)/shard_map/ppermute | solution.py:42
  156.8 1.4 collective-permute-done.42.refs_0_
  158.2 1.6 collective-permute-done.59.refs_15_
  159.7 11.7 %shard_map.100 = (f32[2048,3072]{1,0:T(8,128)}, bf16[64,2048]{1,0:T(8,128)(2,1)}) custom-call(s32[17]{0:T(128)S(1)} %slice_bitcast_fusion.3.index_ref, bf16[512,3072]{1,0:T(8,128)(2,1)S(1)} %bitcast.57, bf16[32,2048]{1,0:T(8,128)(2,1)S(1)} %collective-permute-done.42.refs_0_, bf16[32,2048]{1,0:T(8,128)(2,1)S(1)} %collective-permute-done.41.refs_1_, ...), custom_call_target="tpu_custom_call" | custom-call | flops 6442450944 | bytes 30408704 | tf_op jit(solution)/shard_map/pallas_call | solution.py:381
  (148 shorter events, 39.7 us)
Async XLA Ops:
  4.7 13.7 %collective-permute-start.4 = (bf16[128,1024]{1,0:T(8,128)(2,1)}, bf16[128,1024]{1,0:T(8,128)(2,1)S(1)}, u32[]{:S(2)}, u32[]{:S(2)}) collective-permute-start(bf16[128,1024]{1,0:T(8,128)(2,1)} %param.8), channel_id=1, source_target_pairs={{0,0},{1,1},{2,8},{3,9},{4,16},{5,17},{6,24},{7,25},{8,4},{9,5},{1... | collective-permute-start | bytes 786440 | tf_op jit(solution)/shard_map/ppermute | solution.py:490
  6.3 11.3 %collective-permute-start.3 = (f32[1,128]{1,0:T(1,128)S(1)}, f32[1,128]{1,0:T(1,128)S(1)}, u32[]{:S(2)}, u32[]{:S(2)}) collective-permute-start(f32[1,128]{1,0:T(1,128)S(1)} %bitcast_add_fusion), channel_id=1, source_target_pairs={{0,6},{1,7},{2,4},{3,5},{4,2},{5,3},{6,0},{7,1},{8,14},{9,15},{10,... | collective-permute-start | bytes 1544 | tf_op jit(solution)/shard_map/ppermute | solution.py:47
  10.6 7.3 %collective-permute-start.2 = (f32[1,128]{1,0:T(1,128)S(1)}, f32[1,128]{1,0:T(1,128)S(1)}, u32[]{:S(2)}, u32[]{:S(2)}) collective-permute-start(f32[1,128]{1,0:T(1,128)S(1)} %bitcast_add_fusion), channel_id=1, source_target_pairs={{0,4},{1,5},{2,6},{3,7},{4,0},{5,1},{6,2},{7,3},{8,12},{9,13},{10,... | collective-permute-start | bytes 1544 | tf_op jit(solution)/shard_map/ppermute | solution.py:47
  10.7 7.7 %collective-permute-start.1 = (f32[1,128]{1,0:T(1,128)S(1)}, f32[1,128]{1,0:T(1,128)S(1)}, u32[]{:S(2)}, u32[]{:S(2)}) collective-permute-start(f32[1,128]{1,0:T(1,128)S(1)} %bitcast_add_fusion), channel_id=1, source_target_pairs={{0,2},{1,3},{2,0},{3,1},{4,6},{5,7},{6,4},{7,5},{8,10},{9,11},{10,... | collective-permute-start | bytes 1544 | tf_op jit(solution)/shard_map/ppermute | solution.py:47
  18.4 6.4 %collective-permute-start.17 = (bf16[64,1024]{1,0:T(8,128)(2,1)S(1)}, bf16[64,1024]{1,0:T(8,128)(2,1)S(1)}, u32[]{:S(2)}, u32[]{:S(2)}) collective-permute-start(bf16[64,1024]{1,0:T(8,128)(2,1)S(1)} %get-tuple-element.82.refs_11_), channel_id=1, source_target_pairs={{0,1},{2,0},{4,2},{6,4},{7,6},{5,7},{3,5},{1,3},{8,9},{10,8},{12,1... | collective-permute-start | bytes 393224 | tf_op jit(solution)/shard_map/ppermute | solution.py:42
  19.0 6.4 %collective-permute-start.5 = (bf16[64,1024]{1,0:T(8,128)(2,1)S(1)}, bf16[64,1024]{1,0:T(8,128)(2,1)S(1)}, u32[]{:S(2)}, u32[]{:S(2)}) collective-permute-start(bf16[64,1024]{1,0:T(8,128)(2,1)S(1)} %get-tuple-element.83.refs_4_), channel_id=1, source_target_pairs={{0,2},{2,4},{4,6},{6,7},{7,5},{5,3},{3,1},{1,0},{8,10},{10,12},{12... | collective-permute-start | bytes 393224 | tf_op jit(solution)/shard_map/ppermute | solution.py:42
  20.5 8.7 %collective-permute-start.14 = (bf16[64,1024]{1,0:T(8,128)(2,1)S(1)}, bf16[64,1024]{1,0:T(8,128)(2,1)S(1)}, u32[]{:S(2)}, u32[]{:S(2)}) collective-permute-start(bf16[64,1024]{1,0:T(8,128)(2,1)S(1)} %get-tuple-element.82.refs_11_), channel_id=1, source_target_pairs={{0,2},{2,4},{4,6},{6,7},{7,5},{5,3},{3,1},{1,0},{8,10},{10,12},{12... | collective-permute-start | bytes 393224 | tf_op jit(solution)/shard_map/ppermute | solution.py:42
  20.6 7.1 %collective-permute-start.6 = (bf16[64,1024]{1,0:T(8,128)(2,1)S(1)}, bf16[64,1024]{1,0:T(8,128)(2,1)S(1)}, u32[]{:S(2)}, u32[]{:S(2)}) collective-permute-start(bf16[64,1024]{1,0:T(8,128)(2,1)S(1)} %get-tuple-element.83.refs_4_), channel_id=1, source_target_pairs={{0,1},{2,0},{4,2},{6,4},{7,6},{5,7},{3,5},{1,3},{8,9},{10,8},{12,1... | collective-permute-start | bytes 393224 | tf_op jit(solution)/shard_map/ppermute | solution.py:42
  24.9 6.2 %collective-permute-start.18 = (bf16[64,1024]{1,0:T(8,128)(2,1)S(1)}, bf16[64,1024]{1,0:T(8,128)(2,1)S(1)}, u32[]{:S(2)}, u32[]{:S(2)}) collective-permute-start(bf16[64,1024]{1,0:T(8,128)(2,1)S(1)} %collective-permute-done.17.refs_12_), channel_id=1, source_target_pairs={{0,1},{2,0},{4,2},{6,4},{7,6},{5,7},{3,5},{1,3},{8,9},{10,8},{12,1... | collective-permute-start | bytes 393224 | tf_op jit(solution)/shard_map/ppermute | solution.py:42
  25.3 6.1 %collective-permute-start.8 = (bf16[64,1024]{1,0:T(8,128)(2,1)S(1)}, bf16[64,1024]{1,0:T(8,128)(2,1)S(1)}, u32[]{:S(2)}, u32[]{:S(2)}) collective-permute-start(bf16[64,1024]{1,0:T(8,128)(2,1)S(1)} %collective-permute-done.5.refs_3_), channel_id=1, source_target_pairs={{0,2},{2,4},{4,6},{6,7},{7,5},{5,3},{3,1},{1,0},{8,10},{10,12},{12... | collective-permute-start | bytes 393224 | tf_op jit(solution)/shard_map/ppermute | solution.py:42
  27.7 6.1 %collective-permute-start.7 = (f32[2,128]{1,0:T(2,128)S(1)}, f32[2,128]{1,0:T(2,128)S(1)}, u32[]{:S(2)}, u32[]{:S(2)}) collective-permute-start(f32[2,128]{1,0:T(2,128)S(1)} %pad_maximum_fusion.8), channel_id=1, source_target_pairs={{0,16},{8,24},{16,0},{24,8},{1,17},{9,25},{17,1},{25,9},{2,18},{10... | collective-permute-start | bytes 3080 | tf_op jit(solution)/shard_map/ppermute | solution.py:116
  29.2 5.3 %collective-permute-start.15 = (bf16[64,1024]{1,0:T(8,128)(2,1)S(1)}, bf16[64,1024]{1,0:T(8,128)(2,1)S(1)}, u32[]{:S(2)}, u32[]{:S(2)}) collective-permute-start(bf16[64,1024]{1,0:T(8,128)(2,1)S(1)} %collective-permute-done.14.refs_10_), channel_id=1, source_target_pairs={{0,2},{2,4},{4,6},{6,7},{7,5},{5,3},{3,1},{1,0},{8,10},{10,12},{12... | collective-permute-start | bytes 393224 | tf_op jit(solution)/shard_map/ppermute | solution.py:42
  31.5 5.1 %collective-permute-start.11 = (bf16[64,1024]{1,0:T(8,128)(2,1)S(1)}, bf16[64,1024]{1,0:T(8,128)(2,1)S(1)}, u32[]{:S(2)}, u32[]{:S(2)}) collective-permute-start(bf16[64,1024]{1,0:T(8,128)(2,1)S(1)} %collective-permute-done.8.refs_2_), channel_id=1, source_target_pairs={{0,2},{2,4},{4,6},{6,7},{7,5},{5,3},{3,1},{1,0},{8,10},{10,12},{12... | collective-permute-start | bytes 393224 | tf_op jit(solution)/shard_map/ppermute | solution.py:42
  34.1 6.8 %collective-permute-start.13 = (bf16[64,1024]{1,0:T(8,128)(2,1)S(1)}, bf16[64,1024]{1,0:T(8,128)(2,1)S(1)}, u32[]{:S(2)}, u32[]{:S(2)}) collective-permute-start(bf16[64,1024]{1,0:T(8,128)(2,1)S(1)} %collective-permute-done.9.refs_6_), channel_id=1, source_target_pairs={{0,1},{2,0},{4,2},{6,4},{7,6},{5,7},{3,5},{1,3},{8,9},{10,8},{12,1... | collective-permute-start | bytes 393224 | tf_op jit(solution)/shard_map/ppermute | solution.py:42
  34.5 6.4 %collective-permute-start.16 = (bf16[64,1024]{1,0:T(8,128)(2,1)S(1)}, bf16[64,1024]{1,0:T(8,128)(2,1)S(1)}, u32[]{:S(2)}, u32[]{:S(2)}) collective-permute-start(bf16[64,1024]{1,0:T(8,128)(2,1)S(1)} %collective-permute-done.15.refs_9_), channel_id=1, source_target_pairs={{0,2},{2,4},{4,6},{6,7},{7,5},{5,3},{3,1},{1,0},{8,10},{10,12},{12... | collective-permute-start | bytes 393224 | tf_op jit(solution)/shard_map/ppermute | solution.py:42
  36.1 6.7 %collective-permute-start.20 = (bf16[64,1024]{1,0:T(8,128)(2,1)S(1)}, bf16[64,1024]{1,0:T(8,128)(2,1)S(1)}, u32[]{:S(2)}, u32[]{:S(2)}) collective-permute-start(bf16[64,1024]{1,0:T(8,128)(2,1)S(1)} %collective-permute-done.19.refs_14_), channel_id=1, source_target_pairs={{0,1},{2,0},{4,2},{6,4},{7,6},{5,7},{3,5},{1,3},{8,9},{10,8},{12,1... | collective-permute-start | bytes 393224 | tf_op jit(solution)/shard_map/ppermute | solution.py:42
  36.6 6.2 %collective-permute-start.12 = (bf16[64,1024]{1,0:T(8,128)(2,1)S(1)}, bf16[64,1024]{1,0:T(8,128)(2,1)S(1)}, u32[]{:S(2)}, u32[]{:S(2)}) collective-permute-start(bf16[64,1024]{1,0:T(8,128)(2,1)S(1)} %collective-permute-done.11.refs_1_), channel_id=1, source_target_pairs={{0,2},{2,4},{4,6},{6,7},{7,5},{5,3},{3,1},{1,0},{8,10},{10,12},{12... | collective-permute-start | bytes 393224 | tf_op jit(solution)/shard_map/ppermute | solution.py:42
  54.3 14.2 %collective-permute-start.22 = (s16[128,2048]{1,0:T(8,128)(2,1)S(1)}, s16[128,2048]{1,0:T(8,128)(2,1)S(1)}, u32[]{:S(2)}, u32[]{:S(2)}) collective-permute-start(s16[128,2048]{1,0:T(8,128)(2,1)S(1)} %round-nearest-even_convert_fusion), channel_id=1, source_target_pairs={{0,16},{8,24},{16,0},{24,8},{1,17},{9,25},{17,1},{25,9},{2,18},{10... | collective-permute-start | bytes 1572872 | tf_op jit(solution)/shard_map/ppermute | solution.py:116
  55.7 12.8 %collective-permute-start.23 = (f32[128]{0:T(128)S(1)}, f32[128]{0:T(128)S(1)}, u32[]{:S(2)}, u32[]{:S(2)}) collective-permute-start(f32[128]{0:T(128)S(1)} %get-tuple-element.112), channel_id=1, source_target_pairs={{0,16},{8,24},{16,0},{24,8},{1,17},{9,25},{17,1},{25,9},{2,18},{10... | collective-permute-start | bytes 1544 | tf_op jit(solution)/shard_map/ppermute | solution.py:116
  72.9 5.9 %collective-permute-start.27 = (f32[2,256]{1,0:T(2,128)S(1)}, f32[2,256]{1,0:T(2,128)S(1)}, u32[]{:S(2)}, u32[]{:S(2)}) collective-permute-start(f32[2,256]{1,0:T(2,128)S(1)} %pad_maximum_fusion.7), channel_id=1, source_target_pairs={{0,6},{1,7},{2,4},{3,5},{4,2},{5,3},{6,0},{7,1},{8,14},{9,15},{10,... | collective-permute-start | bytes 6152 | tf_op jit(solution)/shard_map/ppermute | solution.py:47
  83.4 11.4 %collective-permute-start.28 = (bf16[128,2176]{1,0:T(8,128)(2,1)S(1)}, bf16[128,2176]{1,0:T(8,128)(2,1)S(1)}, u32[]{:S(2)}, u32[]{:S(2)}) collective-permute-start(bf16[128,2176]{1,0:T(8,128)(2,1)S(1)} %get-tuple-element.81), channel_id=1, source_target_pairs={{0,16},{8,24},{16,0},{24,8},{1,17},{9,25},{17,1},{25,9},{2,18},{10... | collective-permute-start | bytes 1671176 | tf_op jit(solution)/shard_map/ppermute | solution.py:116
  104.0 29.5 %collective-permute-start.30 = (bf16[2,64,3072]{2,1,0:T(8,128)(2,1)S(1)}, bf16[2,64,3072]{2,1,0:T(8,128)(2,1)S(1)}, u32[]{:S(2)}, u32[]{:S(2)}) collective-permute-start(bf16[2,64,3072]{2,1,0:T(8,128)(2,1)S(1)} %bitcast.54), channel_id=1, source_target_pairs={{0,16},{8,24},{16,0},{24,8},{1,17},{9,25},{17,1},{25,9},{2,18},{10... | collective-permute-start | bytes 2359304 | tf_op jit(solution)/shard_map/ppermute | solution.py:116
  105.1 5.8 %collective-permute-start.32 = (bf16[32,2176]{1,0:T(8,128)(2,1)S(1)}, bf16[32,2176]{1,0:T(8,128)(2,1)S(1)}, u32[]{:S(2)}, u32[]{:S(2)}) collective-permute-start(bf16[32,2176]{1,0:T(8,128)(2,1)S(1)} %get-tuple-element.78), channel_id=1, source_target_pairs={{0,2},{2,4},{4,6},{6,7},{7,5},{5,3},{3,1},{1,0},{8,10},{10,12},{12... | collective-permute-start | bytes 417800 | tf_op jit(solution)/shard_map/ppermute | solution.py:42
  105.2 7.9 %collective-permute-start.46 = (bf16[32,2176]{1,0:T(8,128)(2,1)S(1)}, bf16[32,2176]{1,0:T(8,128)(2,1)S(1)}, u32[]{:S(2)}, u32[]{:S(2)}) collective-permute-start(bf16[32,2176]{1,0:T(8,128)(2,1)S(1)} %get-tuple-element.77), channel_id=1, source_target_pairs={{0,1},{2,0},{4,2},{6,4},{7,6},{5,7},{3,5},{1,3},{8,9},{10,8},{12,1... | collective-permute-start | bytes 417800 | tf_op jit(solution)/shard_map/ppermute | solution.py:42
  111.0 5.5 %collective-permute-start.33 = (bf16[32,2176]{1,0:T(8,128)(2,1)S(1)}, bf16[32,2176]{1,0:T(8,128)(2,1)S(1)}, u32[]{:S(2)}, u32[]{:S(2)}) collective-permute-start(bf16[32,2176]{1,0:T(8,128)(2,1)S(1)} %add_convert_fusion.9), channel_id=1, source_target_pairs={{0,2},{2,4},{4,6},{6,7},{7,5},{5,3},{3,1},{1,0},{8,10},{10,12},{12... | collective-permute-start | bytes 417800 | tf_op jit(solution)/shard_map/ppermute | solution.py:42
  111.3 6.6 %collective-permute-start.34 = (bf16[32,2176]{1,0:T(8,128)(2,1)S(1)}, bf16[32,2176]{1,0:T(8,128)(2,1)S(1)}, u32[]{:S(2)}, u32[]{:S(2)}) collective-permute-start(bf16[32,2176]{1,0:T(8,128)(2,1)S(1)} %get-tuple-element.44), channel_id=1, source_target_pairs={{0,1},{2,0},{4,2},{6,4},{7,6},{5,7},{3,5},{1,3},{8,9},{10,8},{12,1... | collective-permute-start | bytes 417800 | tf_op jit(solution)/shard_map/ppermute | solution.py:42
  113.1 7.8 %collective-permute-start.48 = (bf16[32,2176]{1,0:T(8,128)(2,1)S(1)}, bf16[32,2176]{1,0:T(8,128)(2,1)S(1)}, u32[]{:S(2)}, u32[]{:S(2)}) collective-permute-start(bf16[32,2176]{1,0:T(8,128)(2,1)S(1)} %add_convert_fusion.3), channel_id=1, source_target_pairs={{0,1},{2,0},{4,2},{6,4},{7,6},{5,7},{3,5},{1,3},{8,9},{10,8},{12,1... | collective-permute-start | bytes 417800 | tf_op jit(solution)/shard_map/ppermute | solution.py:42
  114.5 6.4 %collective-permute-start.47 = (bf16[32,2176]{1,0:T(8,128)(2,1)S(1)}, bf16[32,2176]{1,0:T(8,128)(2,1)S(1)}, u32[]{:S(2)}, u32[]{:S(2)}) collective-permute-start(bf16[32,2176]{1,0:T(8,128)(2,1)S(1)} %get-tuple-element.51), channel_id=1, source_target_pairs={{0,2},{2,4},{4,6},{6,7},{7,5},{5,3},{3,1},{1,0},{8,10},{10,12},{12... | collective-permute-start | bytes 417800 | tf_op jit(solution)/shard_map/ppermute | solution.py:42
  118.0 5.8 %collective-permute-start.36 = (bf16[32,2176]{1,0:T(8,128)(2,1)S(1)}, bf16[32,2176]{1,0:T(8,128)(2,1)S(1)}, u32[]{:S(2)}, u32[]{:S(2)}) collective-permute-start(bf16[32,2176]{1,0:T(8,128)(2,1)S(1)} %get-tuple-element.46), channel_id=1, source_target_pairs={{0,1},{2,0},{4,2},{6,4},{7,6},{5,7},{3,5},{1,3},{8,9},{10,8},{12,1... | collective-permute-start | bytes 417800 | tf_op jit(solution)/shard_map/ppermute | solution.py:42
  119.5 5.3 %collective-permute-start.35 = (bf16[32,2176]{1,0:T(8,128)(2,1)S(1)}, bf16[32,2176]{1,0:T(8,128)(2,1)S(1)}, u32[]{:S(2)}, u32[]{:S(2)}) collective-permute-start(bf16[32,2176]{1,0:T(8,128)(2,1)S(1)} %get-tuple-element.45), channel_id=1, source_target_pairs={{0,2},{2,4},{4,6},{6,7},{7,5},{5,3},{3,1},{1,0},{8,10},{10,12},{12... | collective-permute-start | bytes 417800 | tf_op jit(solution)/shard_map/ppermute | solution.py:42
  121.0 6.5 %collective-permute-start.50 = (bf16[32,2176]{1,0:T(8,128)(2,1)S(1)}, bf16[32,2176]{1,0:T(8,128)(2,1)S(1)}, u32[]{:S(2)}, u32[]{:S(2)}) collective-permute-start(bf16[32,2176]{1,0:T(8,128)(2,1)S(1)} %get-tuple-element.54), channel_id=1, source_target_pairs={{0,1},{2,0},{4,2},{6,4},{7,6},{5,7},{3,5},{1,3},{8,9},{10,8},{12,1... | collective-permute-start | bytes 417800 | tf_op jit(solution)/shard_map/ppermute | solution.py:42
  122.5 6.0 %collective-permute-start.49 = (bf16[32,2176]{1,0:T(8,128)(2,1)S(1)}, bf16[32,2176]{1,0:T(8,128)(2,1)S(1)}, u32[]{:S(2)}, u32[]{:S(2)}) collective-permute-start(bf16[32,2176]{1,0:T(8,128)(2,1)S(1)} %get-tuple-element.53), channel_id=1, source_target_pairs={{0,2},{2,4},{4,6},{6,7},{7,5},{5,3},{3,1},{1,0},{8,10},{10,12},{12... | collective-permute-start | bytes 417800 | tf_op jit(solution)/shard_map/ppermute | solution.py:42
  124.8 5.9 %collective-permute-start.38 = (bf16[32,2176]{1,0:T(8,128)(2,1)S(1)}, bf16[32,2176]{1,0:T(8,128)(2,1)S(1)}, u32[]{:S(2)}, u32[]{:S(2)}) collective-permute-start(bf16[32,2176]{1,0:T(8,128)(2,1)S(1)} %get-tuple-element.48), channel_id=1, source_target_pairs={{0,1},{2,0},{4,2},{6,4},{7,6},{5,7},{3,5},{1,3},{8,9},{10,8},{12,1... | collective-permute-start | bytes 417800 | tf_op jit(solution)/shard_map/ppermute | solution.py:42
  126.0 6.5 %collective-permute-start.37 = (bf16[32,2176]{1,0:T(8,128)(2,1)S(1)}, bf16[32,2176]{1,0:T(8,128)(2,1)S(1)}, u32[]{:S(2)}, u32[]{:S(2)}) collective-permute-start(bf16[32,2176]{1,0:T(8,128)(2,1)S(1)} %get-tuple-element.47), channel_id=1, source_target_pairs={{0,2},{2,4},{4,6},{6,7},{7,5},{5,3},{3,1},{1,0},{8,10},{10,12},{12... | collective-permute-start | bytes 417800 | tf_op jit(solution)/shard_map/ppermute | solution.py:42
  128.6 5.2 %collective-permute-start.52 = (bf16[32,2176]{1,0:T(8,128)(2,1)S(1)}, bf16[32,2176]{1,0:T(8,128)(2,1)S(1)}, u32[]{:S(2)}, u32[]{:S(2)}) collective-permute-start(bf16[32,2176]{1,0:T(8,128)(2,1)S(1)} %get-tuple-element.56), channel_id=1, source_target_pairs={{0,1},{2,0},{4,2},{6,4},{7,6},{5,7},{3,5},{1,3},{8,9},{10,8},{12,1... | collective-permute-start | bytes 417800 | tf_op jit(solution)/shard_map/ppermute | solution.py:42
  129.9 5.1 %collective-permute-start.51 = (bf16[32,2176]{1,0:T(8,128)(2,1)S(1)}, bf16[32,2176]{1,0:T(8,128)(2,1)S(1)}, u32[]{:S(2)}, u32[]{:S(2)}) collective-permute-start(bf16[32,2176]{1,0:T(8,128)(2,1)S(1)} %get-tuple-element.55), channel_id=1, source_target_pairs={{0,2},{2,4},{4,6},{6,7},{7,5},{5,3},{3,1},{1,0},{8,10},{10,12},{12... | collective-permute-start | bytes 417800 | tf_op jit(solution)/shard_map/ppermute | solution.py:42
  132.7 5.5 %collective-permute-start.39 = (bf16[32,2048]{1,0:T(8,128)(2,1)S(1)}, bf16[32,2048]{1,0:T(8,128)(2,1)S(1)}, u32[]{:S(2)}, u32[]{:S(2)}) collective-permute-start(bf16[32,2048]{1,0:T(8,128)(2,1)S(1)} %fusion.6.refs_4_), channel_id=1, source_target_pairs={{0,2},{2,4},{4,6},{6,7},{7,5},{5,3},{3,1},{1,0},{8,10},{10,12},{12... | collective-permute-start | bytes 393224 | tf_op jit(solution)/shard_map/ppermute | solution.py:42
  133.7 21.3 %collective-permute-start.31 = (bf16[2,2,64,3072]{3,2,0,1:T(8,128)(2,1)S(1)}, bf16[2,2,64,3072]{3,2,0,1:T(8,128)(2,1)S(1)}, u32[]{:S(2)}, u32[]{:S(2)}) collective-permute-start(bf16[2,2,64,3072]{3,2,0,1:T(8,128)(2,1)S(1)} %pad_maximum_fusion.1), channel_id=1, source_target_pairs={{0,8},{8,0},{16,24},{24,16},{1,9},{9,1},{17,25},{25,17},{2,10},{10... | collective-permute-start | bytes 4718600 | tf_op jit(solution)/shard_map/ppermute | solution.py:112
  135.3 6.4 %collective-permute-start.56 = (bf16[32,2048]{1,0:T(8,128)(2,1)S(1)}, bf16[32,2048]{1,0:T(8,128)(2,1)S(1)}, u32[]{:S(2)}, u32[]{:S(2)}) collective-permute-start(bf16[32,2048]{1,0:T(8,128)(2,1)S(1)} %fusion.4.refs_11_), channel_id=1, source_target_pairs={{0,1},{2,0},{4,2},{6,4},{7,6},{5,7},{3,5},{1,3},{8,9},{10,8},{12,1... | collective-permute-start | bytes 393224 | tf_op jit(solution)/shard_map/ppermute | solution.py:42
  136.2 8.3 %collective-permute-start.43 = (bf16[32,2048]{1,0:T(8,128)(2,1)S(1)}, bf16[32,2048]{1,0:T(8,128)(2,1)S(1)}, u32[]{:S(2)}, u32[]{:S(2)}) collective-permute-start(bf16[32,2048]{1,0:T(8,128)(2,1)S(1)} %fusion.6.refs_4_), channel_id=1, source_target_pairs={{0,1},{2,0},{4,2},{6,4},{7,6},{5,7},{3,5},{1,3},{8,9},{10,8},{12,1... | collective-permute-start | bytes 393224 | tf_op jit(solution)/shard_map/ppermute | solution.py:42
  137.6 7.8 %collective-permute-start.53 = (bf16[32,2048]{1,0:T(8,128)(2,1)S(1)}, bf16[32,2048]{1,0:T(8,128)(2,1)S(1)}, u32[]{:S(2)}, u32[]{:S(2)}) collective-permute-start(bf16[32,2048]{1,0:T(8,128)(2,1)S(1)} %fusion.4.refs_11_), channel_id=1, source_target_pairs={{0,2},{2,4},{4,6},{6,7},{7,5},{5,3},{3,1},{1,0},{8,10},{10,12},{12... | collective-permute-start | bytes 393224 | tf_op jit(solution)/shard_map/ppermute | solution.py:42
  138.2 8.3 %collective-permute-start.40 = (bf16[32,2048]{1,0:T(8,128)(2,1)S(1)}, bf16[32,2048]{1,0:T(8,128)(2,1)S(1)}, u32[]{:S(2)}, u32[]{:S(2)}) collective-permute-start(bf16[32,2048]{1,0:T(8,128)(2,1)S(1)} %collective-permute-done.39.refs_3_), channel_id=1, source_target_pairs={{0,2},{2,4},{4,6},{6,7},{7,5},{5,3},{3,1},{1,0},{8,10},{10,12},{12... | collective-permute-start | bytes 393224 | tf_op jit(solution)/shard_map/ppermute | solution.py:42
  141.7 5.6 %collective-permute-start.57 = (bf16[32,2048]{1,0:T(8,128)(2,1)S(1)}, bf16[32,2048]{1,0:T(8,128)(2,1)S(1)}, u32[]{:S(2)}, u32[]{:S(2)}) collective-permute-start(bf16[32,2048]{1,0:T(8,128)(2,1)S(1)} %collective-permute-done.56.refs_12_), channel_id=1, source_target_pairs={{0,1},{2,0},{4,2},{6,4},{7,6},{5,7},{3,5},{1,3},{8,9},{10,8},{12,1... | collective-permute-start | bytes 393224 | tf_op jit(solution)/shard_map/ppermute | solution.py:42
  144.5 6.4 %collective-permute-start.44 = (bf16[32,2048]{1,0:T(8,128)(2,1)S(1)}, bf16[32,2048]{1,0:T(8,128)(2,1)S(1)}, u32[]{:S(2)}, u32[]{:S(2)}) collective-permute-start(bf16[32,2048]{1,0:T(8,128)(2,1)S(1)} %collective-permute-done.43.refs_5_), channel_id=1, source_target_pairs={{0,1},{2,0},{4,2},{6,4},{7,6},{5,7},{3,5},{1,3},{8,9},{10,8},{12,1... | collective-permute-start | bytes 393224 | tf_op jit(solution)/shard_map/ppermute | solution.py:42
  145.4 6.4 %collective-permute-start.54 = (bf16[32,2048]{1,0:T(8,128)(2,1)S(1)}, bf16[32,2048]{1,0:T(8,128)(2,1)S(1)}, u32[]{:S(2)}, u32[]{:S(2)}) collective-permute-start(bf16[32,2048]{1,0:T(8,128)(2,1)S(1)} %collective-permute-done.53.refs_10_), channel_id=1, source_target_pairs={{0,2},{2,4},{4,6},{6,7},{7,5},{5,3},{3,1},{1,0},{8,10},{10,12},{12... | collective-permute-start | bytes 393224 | tf_op jit(solution)/shard_map/ppermute | solution.py:42
  146.5 6.4 %collective-permute-start.41 = (bf16[32,2048]{1,0:T(8,128)(2,1)S(1)}, bf16[32,2048]{1,0:T(8,128)(2,1)S(1)}, u32[]{:S(2)}, u32[]{:S(2)}) collective-permute-start(bf16[32,2048]{1,0:T(8,128)(2,1)S(1)} %collective-permute-done.40.refs_2_), channel_id=1, source_target_pairs={{0,2},{2,4},{4,6},{6,7},{7,5},{5,3},{3,1},{1,0},{8,10},{10,12},{12... | collective-permute-start | bytes 393224 | tf_op jit(solution)/shard_map/ppermute | solution.py:42
  147.3 7.5 %collective-permute-start.58 = (bf16[32,2048]{1,0:T(8,128)(2,1)S(1)}, bf16[32,2048]{1,0:T(8,128)(2,1)S(1)}, u32[]{:S(2)}, u32[]{:S(2)}) collective-permute-start(bf16[32,2048]{1,0:T(8,128)(2,1)S(1)} %collective-permute-done.57.refs_13_), channel_id=1, source_target_pairs={{0,1},{2,0},{4,2},{6,4},{7,6},{5,7},{3,5},{1,3},{8,9},{10,8},{12,1... | collective-permute-start | bytes 393224 | tf_op jit(solution)/shard_map/ppermute | solution.py:42
  152.9 5.2 %collective-permute-start.42 = (bf16[32,2048]{1,0:T(8,128)(2,1)S(1)}, bf16[32,2048]{1,0:T(8,128)(2,1)S(1)}, u32[]{:S(2)}, u32[]{:S(2)}) collective-permute-start(bf16[32,2048]{1,0:T(8,128)(2,1)S(1)} %collective-permute-done.41.refs_1_), channel_id=1, source_target_pairs={{0,2},{2,4},{4,6},{6,7},{7,5},{5,3},{3,1},{1,0},{8,10},{10,12},{12... | collective-permute-start | bytes 393224 | tf_op jit(solution)/shard_map/ppermute | solution.py:42
  (17 other events, 101.2 us)

commit v15 on v14

--- a/solution.py
+++ b/solution.py
@@ -491,13 +491,12 @@
 
     live_rows = (valid_rows == 1).astype(F32)
     squares = jnp.sum(jnp.square(hidden.astype(F32)), axis=1)[None]
-    rounds = ring.meetings(lambda terms: sum(terms[1:], terms[0]))
+    rounds = ring.meetings(lambda terms: sum(terms[1:], terms[0]))[::-1]
     rounds.append(lambda x: groups.gather_chips(jnp.concatenate([x, live_rows[None]])))
     rounds.append(lambda x: jnp.concatenate([x, groups.swap(x)], axis=0))
-    for round in rounds[:2]:
-        squares = round(squares)
+    squares = rounds[0](squares)
     turned = after(turned, squares)
-    late = rounds[2:]
+    late = rounds[1:]
     exchanged = [squares]
 
     def seen(step, arrivals):

time: 172 us -> 174 us (1.012)
  waiting for transfers between devices: 64.5 us -> 67.8 us
  transfers between devices with their start and end apart: 60 -> 60, of which waited for: 34 -> 32; matrix products, arithmetic and copies ran while one was open for 6% -> 6% of each run, Pallas kernels for 2% -> 2%
where the time goes in v15:
time: 174 us
  waiting for transfers between devices  67.8 us (39%)
  starting transfers between devices  62.9 us (36%)
  Pallas kernels  27.9 us (16%)
  other arithmetic  10.9 us (6%)
  local copies, waits for them, and re-layouts  3.11 us (2%)
    ppermute x42, starting transfers between devices, shift(): lax.ppermute(x, 'vocab', [(order[p], order[(p + step) % size]) for p in r...  42.6 us
    ppermute x42, waiting for transfers between devices, shift(): lax.ppermute(x, 'vocab', [(order[p], order[(p + step) % size]) for p in r...  33.3 us
    ppermute x5, waiting for transfers between devices, shift(): lax.ppermute(x, 'dp', [(i, (i + CORES * step) % size) for i in range(size)])  21.4 us
    ppermute x8, starting transfers between devices, partner(): return lax.ppermute(x, 'vocab', [(v, v ^ bit) for v in range(self.size)])  14.1 us
    ppermute x8, waiting for transfers between devices, partner(): return lax.ppermute(x, 'vocab', [(v, v ^ bit) for v in range(self.size)])  12.8 us
    pallas_call x1, Pallas kernels, outer(): pl.pallas_call(functools.partial(outer_kernel, len(chunks[0]), copies), g...  11.7 us
    pallas_call x1, Pallas kernels, project(): pl.pallas_call(functools.partial(project_kernel, len(blocks[0]), tile), g...  6.04 us
    pallas_call x1, Pallas kernels, back(): pl.pallas_call(functools.partial(back_kernel, piece_rows, tile), grid=(de...  5.81 us
  transfers between devices with their start and end apart: 60, of which 32 were waited for; matrix products, arithmetic and copies ran while one was open for 6% of the time, Pallas kernels for 2%

profile of v15, /device:TPU:0, one launch (start us, length us, event | category | flops | bytes accessed | tf_op | source)
XLA Modules:
  0.0 173.7 jit_solution(5790676772799883480)
XLA Ops:
  0.6 1.6 collective-permute-start.3
  3.3 5.7 %collective-permute-start.1 = (f32[1,128]{1,0:T(1,128)S(1)}, f32[1,128]{1,0:T(1,128)S(1)}, u32[]{:S(2)}, u32[]{:S(2)}) collective-permute-start(f32[1,128]{1,0:T(1,128)S(1)} %bitcast.76), channel_id=1, source_target_pairs={{0,4},{1,5},{2,6},{3,7},{4,0},{5,1},{6,2},{7,3},{8,12},{9,13},{10,... | collective-permute-start | bytes 1544 | tf_op jit(solution)/shard_map/ppermute | solution.py:47
  9.9 5.4 %collective-permute-done.1 = f32[1,128]{1,0:T(1,128)S(1)} collective-permute-done((f32[1,128]{1,0:T(1,128)S(1)}, f32[1,128]{1,0:T(1,128)S(1)}, u32[]{:S(2)}, u32[]{:S(2)}) %collective-permute-start.1) | collective-permute-done | bytes 544 | tf_op jit(solution)/shard_map/ppermute | solution.py:47
  15.8 1.6 collective-permute-start.17
  17.4 1.9 %collective-permute-start.4 = (bf16[64,1024]{1,0:T(8,128)(2,1)S(1)}, bf16[64,1024]{1,0:T(8,128)(2,1)S(1)}, u32[]{:S(2)}, u32[]{:S(2)}) collective-permute-start(bf16[64,1024]{1,0:T(8,128)(2,1)S(1)} %get-tuple-element.85.refs_4_), channel_id=1, source_target_pairs={{0,2},{2,4},{4,6},{6,7},{7,5},{5,3},{3,1},{1,0},{8,10},{10,12},{12... | collective-permute-start | bytes 393224 | tf_op jit(solution)/shard_map/ppermute | solution.py:42
  19.9 2.3 %collective-permute-done.17.refs_12_ = bf16[64,1024]{1,0:T(8,128)(2,1)S(1)} collective-permute-done((bf16[64,1024]{1,0:T(8,128)(2,1)S(1)}, bf16[64,1024]{1,0:T(8,128)(2,1)S(1)}, u32[]{:S(2)}, u32[]{:S(2)}) %collective-permute-start.17) | collective-permute-done | bytes 131104 | tf_op jit(solution)/shard_map/ppermute | solution.py:42
  22.2 1.5 collective-permute-start.18
  23.7 1.3 collective-permute-done.5.refs_5_
  25.0 1.5 collective-permute-start.8
  27.7 1.5 collective-permute-start.6
  29.3 2.4 %collective-permute-done.6 = f32[1,128]{1,0:T(1,128)S(1)} collective-permute-done((f32[1,128]{1,0:T(1,128)S(1)}, f32[1,128]{1,0:T(1,128)S(1)}, u32[]{:S(2)}, u32[]{:S(2)}) %collective-permute-start.6) | collective-permute-done | bytes 544 | tf_op jit(solution)/shard_map/ppermute | solution.py:47
  32.7 1.2 collective-permute-start.11
  34.7 1.2 collective-permute-start.19
  37.7 1.2 collective-permute-done.10.refs_1_
  39.7 1.2 collective-permute-start.20
  41.6 3.7 %collective-permute-done.20.refs_15_ = bf16[64,1024]{1,0:T(8,128)(2,1)S(1)} collective-permute-done((bf16[64,1024]{1,0:T(8,128)(2,1)S(1)}, bf16[64,1024]{1,0:T(8,128)(2,1)S(1)}, u32[]{:S(2)}, u32[]{:S(2)}) %collective-permute-start.20) | collective-permute-done | bytes 131104 | tf_op jit(solution)/shard_map/ppermute | solution.py:42
  46.1 6.0 %shard_map.96 = (f32[256,2048]{1,0:T(8,128)S(1)}, bf16[2048,256]{1,0:T(8,128)(2,1)S(1)}, bf16[2048,2048]{1,0:T(8,128)(2,1)S(1)}, bf16[32,2048]{1,0:T(8,128)(2,1)S(1)}, bf16[32,2048]{1,0:T(8,128)(2,1)S(1)}) custom-call(s32[35]{0:T(128)S(1)} %slice_bitcast_fusion.1.index_ref, f32[4,128]{1,0:T(4,128)S(1)} %get-tuple-element.89.factor_ref, ...), custom_call_target="tpu_custom_call" | custom-call | flops 2147483648 | bytes 12582912 | tf_op jit(solution)/shard_map/pallas_call | solution.py:251
  52.9 3.3 %shard_map.97 = f32[256,2048]{1,0:T(8,128)S(1)} custom-call(bf16[2048,2048]{1,0:T(8,128)(2,1)S(1)} %get-tuple-element.36.weight_ref, bf16[2048,256]{1,0:T(8,128)(2,1)S(1)} %get-tuple-element.37.turned_ref), custom_call_target="tpu_custom_call" | custom-call | flops 2147483648 | bytes 12582912 | tf_op jit(solution)/shard_map/pallas_call | solution.py:271
  59.7 11.4 %collective-permute-done.23 = f32[128]{0:T(128)S(1)} collective-permute-done((f32[128]{0:T(128)S(1)}, f32[128]{0:T(128)S(1)}, u32[]{:S(2)}, u32[]{:S(2)}) %collective-permute-start.23) | collective-permute-done | bytes 544 | tf_op jit(solution)/shard_map/ppermute | solution.py:116
  71.8 1.4 collective-permute-start.24
  73.3 1.2 iota_compare_fusion
  75.5 3.6 %collective-permute-start.27 = (f32[2,256]{1,0:T(2,128)S(1)}, f32[2,256]{1,0:T(2,128)S(1)}, u32[]{:S(2)}, u32[]{:S(2)}) collective-permute-start(f32[2,256]{1,0:T(2,128)S(1)} %pad_maximum_fusion.7), channel_id=1, source_target_pairs={{0,6},{1,7},{2,4},{3,5},{4,2},{5,3},{6,0},{7,1},{8,14},{9,15},{10,... | collective-permute-start | bytes 6152 | tf_op jit(solution)/shard_map/ppermute | solution.py:47
  81.0 3.4 %collective-permute-done.26 = f32[2,256]{1,0:T(2,128)S(1)} collective-permute-done((f32[2,256]{1,0:T(2,128)S(1)}, f32[2,256]{1,0:T(2,128)S(1)}, u32[]{:S(2)}, u32[]{:S(2)}) %collective-permute-start.26) | collective-permute-done | bytes 2080 | tf_op jit(solution)/shard_map/ppermute | solution.py:47
  86.9 9.9 %collective-permute-done.28 = bf16[128,2176]{1,0:T(8,128)(2,1)S(1)} collective-permute-done((bf16[128,2176]{1,0:T(8,128)(2,1)S(1)}, bf16[128,2176]{1,0:T(8,128)(2,1)S(1)}, u32[]{:S(2)}, u32[]{:S(2)}) %collective-permute-start.28) | collective-permute-done | bytes 557088 | tf_op jit(solution)/shard_map/ppermute | solution.py:116
  97.0 1.4 multiply_multiply_fusion
  98.4 1.4 multiply_multiply_fusion.1
  99.9 5.8 %shard_map.99 = (f32[256,2176]{1,0:T(8,128)S(1)}, f32[256,2176]{1,0:T(8,128)S(1)}) custom-call(s32[8]{0:T(128)S(1)} %slice_bitcast_fusion.2.index_ref, bf16[2,128,2176]{2,1,0:T(8,128)(2,1)S(1)} %pad_maximum_fusion.2.mine_ref, bf16[2,128,2176]{2,1,0:T(8,128)(2,1)S(1)} %collective-permute-done.29.other_ref, bf16[2048,2048]{1,0:T(8,128)(2,1)S(1)} %get-tuple-element.36.weight_ref), custom_call_target="tpu_custom_call" | custom-call | flops 4294967296 | bytes 14680064 | tf_op jit(solution)/shard_map/pallas_call | solution.py:314
  107.0 2.1 %collective-permute-start.46 = (bf16[32,2176]{1,0:T(8,128)(2,1)S(1)}, bf16[32,2176]{1,0:T(8,128)(2,1)S(1)}, u32[]{:S(2)}, u32[]{:S(2)}) collective-permute-start(bf16[32,2176]{1,0:T(8,128)(2,1)S(1)} %get-tuple-element.79), channel_id=1, source_target_pairs={{0,1},{2,0},{4,2},{6,4},{7,6},{5,7},{3,5},{1,3},{8,9},{10,8},{12,1... | collective-permute-start | bytes 417800 | tf_op jit(solution)/shard_map/ppermute | solution.py:42
  109.1 3.7 %collective-permute-done.32 = bf16[32,2176]{1,0:T(8,128)(2,1)S(1)} collective-permute-done((bf16[32,2176]{1,0:T(8,128)(2,1)S(1)}, bf16[32,2176]{1,0:T(8,128)(2,1)S(1)}, u32[]{:S(2)}, u32[]{:S(2)}) %collective-permute-start.32) | collective-permute-done | bytes 139296 | tf_op jit(solution)/shard_map/ppermute | solution.py:42
  113.2 1.7 %collective-permute-start.34 = (bf16[32,2176]{1,0:T(8,128)(2,1)S(1)}, bf16[32,2176]{1,0:T(8,128)(2,1)S(1)}, u32[]{:S(2)}, u32[]{:S(2)}) collective-permute-start(bf16[32,2176]{1,0:T(8,128)(2,1)S(1)} %get-tuple-element.46), channel_id=1, source_target_pairs={{0,1},{2,0},{4,2},{6,4},{7,6},{5,7},{3,5},{1,3},{8,9},{10,8},{12,1... | collective-permute-start | bytes 417800 | tf_op jit(solution)/shard_map/ppermute | solution.py:42
  114.9 1.2 collective-permute-start.48
  117.0 1.6 collective-permute-done.33
  118.6 1.2 collective-permute-done.34
  119.8 1.5 collective-permute-start.36
  122.8 1.5 collective-permute-start.50
  126.4 1.2 collective-permute-start.38
  130.4 1.2 collective-permute-start.52
  132.4 1.5 collective-permute-done.37
  137.8 1.4 collective-permute-start.43
  141.0 2.4 %collective-permute-done.56.refs_12_ = bf16[32,2048]{1,0:T(8,128)(2,1)S(1)} collective-permute-done((bf16[32,2048]{1,0:T(8,128)(2,1)S(1)}, bf16[32,2048]{1,0:T(8,128)(2,1)S(1)}, u32[]{:S(2)}, u32[]{:S(2)}) %collective-permute-start.56) | collective-permute-done | bytes 131104 | tf_op jit(solution)/shard_map/ppermute | solution.py:42
  144.2 2.0 %collective-permute-done.43.refs_5_ = bf16[32,2048]{1,0:T(8,128)(2,1)S(1)} collective-permute-done((bf16[32,2048]{1,0:T(8,128)(2,1)S(1)}, bf16[32,2048]{1,0:T(8,128)(2,1)S(1)}, u32[]{:S(2)}, u32[]{:S(2)}) %collective-permute-start.43) | collective-permute-done | bytes 131104 | tf_op jit(solution)/shard_map/ppermute | solution.py:42
  147.0 1.2 collective-permute-start.54
  150.3 2.3 %collective-permute-done.44.refs_6_ = bf16[32,2048]{1,0:T(8,128)(2,1)S(1)} collective-permute-done((bf16[32,2048]{1,0:T(8,128)(2,1)S(1)}, bf16[32,2048]{1,0:T(8,128)(2,1)S(1)}, u32[]{:S(2)}, u32[]{:S(2)}) %collective-permute-start.44) | collective-permute-done | bytes 131104 | tf_op jit(solution)/shard_map/ppermute | solution.py:42
  153.3 1.3 collective-permute-start.55
  154.6 2.2 %collective-permute-start.42 = (bf16[32,2048]{1,0:T(8,128)(2,1)S(1)}, bf16[32,2048]{1,0:T(8,128)(2,1)S(1)}, u32[]{:S(2)}, u32[]{:S(2)}) collective-permute-start(bf16[32,2048]{1,0:T(8,128)(2,1)S(1)} %collective-permute-done.41.refs_1_), channel_id=1, source_target_pairs={{0,2},{2,4},{4,6},{6,7},{7,5},{5,3},{3,1},{1,0},{8,10},{10,12},{12... | collective-permute-start | bytes 393224 | tf_op jit(solution)/shard_map/ppermute | solution.py:42
  158.3 1.5 collective-permute-done.42.refs_0_
  159.8 2.0 %collective-permute-done.59.refs_15_ = bf16[32,2048]{1,0:T(8,128)(2,1)S(1)} collective-permute-done((bf16[32,2048]{1,0:T(8,128)(2,1)S(1)}, bf16[32,2048]{1,0:T(8,128)(2,1)S(1)}, u32[]{:S(2)}, u32[]{:S(2)}) %collective-permute-start.59) | collective-permute-done | bytes 131104 | tf_op jit(solution)/shard_map/ppermute | solution.py:42
  161.8 11.7 %shard_map.100 = (f32[2048,3072]{1,0:T(8,128)}, bf16[64,2048]{1,0:T(8,128)(2,1)}) custom-call(s32[17]{0:T(128)S(1)} %slice_bitcast_fusion.3.index_ref, bf16[512,3072]{1,0:T(8,128)(2,1)S(1)} %bitcast.57, bf16[32,2048]{1,0:T(8,128)(2,1)S(1)} %collective-permute-done.42.refs_0_, bf16[32,2048]{1,0:T(8,128)(2,1)S(1)} %collective-permute-done.41.refs_1_, ...), custom_call_target="tpu_custom_call" | custom-call | flops 6442450944 | bytes 30408704 | tf_op jit(solution)/shard_map/pallas_call | solution.py:381
  (148 shorter events, 41.9 us)
Async XLA Ops:
  0.6 15.1 %collective-permute-start.3 = (bf16[128,1024]{1,0:T(8,128)(2,1)}, bf16[128,1024]{1,0:T(8,128)(2,1)S(1)}, u32[]{:S(2)}, u32[]{:S(2)}) collective-permute-start(bf16[128,1024]{1,0:T(8,128)(2,1)} %param.8), channel_id=1, source_target_pairs={{0,0},{1,1},{2,8},{3,9},{4,16},{5,17},{6,24},{7,25},{8,4},{9,5},{1... | collective-permute-start | bytes 786440 | tf_op jit(solution)/shard_map/ppermute | solution.py:490
  3.3 12.0 %collective-permute-start.1 = (f32[1,128]{1,0:T(1,128)S(1)}, f32[1,128]{1,0:T(1,128)S(1)}, u32[]{:S(2)}, u32[]{:S(2)}) collective-permute-start(f32[1,128]{1,0:T(1,128)S(1)} %bitcast.76), channel_id=1, source_target_pairs={{0,4},{1,5},{2,6},{3,7},{4,0},{5,1},{6,2},{7,3},{8,12},{9,13},{10,... | collective-permute-start | bytes 1544 | tf_op jit(solution)/shard_map/ppermute | solution.py:47
  9.0 6.3 %collective-permute-start.2 = (f32[1,128]{1,0:T(1,128)S(1)}, f32[1,128]{1,0:T(1,128)S(1)}, u32[]{:S(2)}, u32[]{:S(2)}) collective-permute-start(f32[1,128]{1,0:T(1,128)S(1)} %bitcast.77), channel_id=1, source_target_pairs={{0,6},{1,7},{2,4},{3,5},{4,2},{5,3},{6,0},{7,1},{8,14},{9,15},{10,... | collective-permute-start | bytes 1544 | tf_op jit(solution)/shard_map/ppermute | solution.py:47
  9.4 6.3 %collective-permute-start = (f32[1,128]{1,0:T(1,128)S(1)}, f32[1,128]{1,0:T(1,128)S(1)}, u32[]{:S(2)}, u32[]{:S(2)}) collective-permute-start(f32[1,128]{1,0:T(1,128)S(1)} %bitcast.78), channel_id=1, source_target_pairs={{0,2},{1,3},{2,0},{3,1},{4,6},{5,7},{6,4},{7,5},{8,10},{9,11},{10,... | collective-permute-start | bytes 1544 | tf_op jit(solution)/shard_map/ppermute | solution.py:47
  15.8 6.4 %collective-permute-start.17 = (bf16[64,1024]{1,0:T(8,128)(2,1)S(1)}, bf16[64,1024]{1,0:T(8,128)(2,1)S(1)}, u32[]{:S(2)}, u32[]{:S(2)}) collective-permute-start(bf16[64,1024]{1,0:T(8,128)(2,1)S(1)} %get-tuple-element.84.refs_11_), channel_id=1, source_target_pairs={{0,1},{2,0},{4,2},{6,4},{7,6},{5,7},{3,5},{1,3},{8,9},{10,8},{12,1... | collective-permute-start | bytes 393224 | tf_op jit(solution)/shard_map/ppermute | solution.py:42
  17.3 7.7 %collective-permute-start.5 = (bf16[64,1024]{1,0:T(8,128)(2,1)S(1)}, bf16[64,1024]{1,0:T(8,128)(2,1)S(1)}, u32[]{:S(2)}, u32[]{:S(2)}) collective-permute-start(bf16[64,1024]{1,0:T(8,128)(2,1)S(1)} %get-tuple-element.85.refs_4_), channel_id=1, source_target_pairs={{0,1},{2,0},{4,2},{6,4},{7,6},{5,7},{3,5},{1,3},{8,9},{10,8},{12,1... | collective-permute-start | bytes 393224 | tf_op jit(solution)/shard_map/ppermute | solution.py:42
  17.4 9.1 %collective-permute-start.4 = (bf16[64,1024]{1,0:T(8,128)(2,1)S(1)}, bf16[64,1024]{1,0:T(8,128)(2,1)S(1)}, u32[]{:S(2)}, u32[]{:S(2)}) collective-permute-start(bf16[64,1024]{1,0:T(8,128)(2,1)S(1)} %get-tuple-element.85.refs_4_), channel_id=1, source_target_pairs={{0,2},{2,4},{4,6},{6,7},{7,5},{5,3},{3,1},{1,0},{8,10},{10,12},{12... | collective-permute-start | bytes 393224 | tf_op jit(solution)/shard_map/ppermute | solution.py:42
  19.4 9.9 %collective-permute-start.14 = (bf16[64,1024]{1,0:T(8,128)(2,1)S(1)}, bf16[64,1024]{1,0:T(8,128)(2,1)S(1)}, u32[]{:S(2)}, u32[]{:S(2)}) collective-permute-start(bf16[64,1024]{1,0:T(8,128)(2,1)S(1)} %get-tuple-element.84.refs_11_), channel_id=1, source_target_pairs={{0,2},{2,4},{4,6},{6,7},{7,5},{5,3},{3,1},{1,0},{8,10},{10,12},{12... | collective-permute-start | bytes 393224 | tf_op jit(solution)/shard_map/ppermute | solution.py:42
  22.2 12.5 %collective-permute-start.18 = (bf16[64,1024]{1,0:T(8,128)(2,1)S(1)}, bf16[64,1024]{1,0:T(8,128)(2,1)S(1)}, u32[]{:S(2)}, u32[]{:S(2)}) collective-permute-start(bf16[64,1024]{1,0:T(8,128)(2,1)S(1)} %collective-permute-done.17.refs_12_), channel_id=1, source_target_pairs={{0,1},{2,0},{4,2},{6,4},{7,6},{5,7},{3,5},{1,3},{8,9},{10,8},{12,1... | collective-permute-start | bytes 393224 | tf_op jit(solution)/shard_map/ppermute | solution.py:42
  25.0 6.6 %collective-permute-start.8 = (bf16[64,1024]{1,0:T(8,128)(2,1)S(1)}, bf16[64,1024]{1,0:T(8,128)(2,1)S(1)}, u32[]{:S(2)}, u32[]{:S(2)}) collective-permute-start(bf16[64,1024]{1,0:T(8,128)(2,1)S(1)} %collective-permute-done.5.refs_5_), channel_id=1, source_target_pairs={{0,1},{2,0},{4,2},{6,4},{7,6},{5,7},{3,5},{1,3},{8,9},{10,8},{12,1... | collective-permute-start | bytes 393224 | tf_op jit(solution)/shard_map/ppermute | solution.py:42
  26.5 5.1 %collective-permute-start.7 = (bf16[64,1024]{1,0:T(8,128)(2,1)S(1)}, bf16[64,1024]{1,0:T(8,128)(2,1)S(1)}, u32[]{:S(2)}, u32[]{:S(2)}) collective-permute-start(bf16[64,1024]{1,0:T(8,128)(2,1)S(1)} %collective-permute-done.4.refs_3_), channel_id=1, source_target_pairs={{0,2},{2,4},{4,6},{6,7},{7,5},{5,3},{3,1},{1,0},{8,10},{10,12},{12... | collective-permute-start | bytes 393224 | tf_op jit(solution)/shard_map/ppermute | solution.py:42
  29.2 7.4 %collective-permute-start.15 = (bf16[64,1024]{1,0:T(8,128)(2,1)S(1)}, bf16[64,1024]{1,0:T(8,128)(2,1)S(1)}, u32[]{:S(2)}, u32[]{:S(2)}) collective-permute-start(bf16[64,1024]{1,0:T(8,128)(2,1)S(1)} %collective-permute-done.14.refs_10_), channel_id=1, source_target_pairs={{0,2},{2,4},{4,6},{6,7},{7,5},{5,3},{3,1},{1,0},{8,10},{10,12},{12... | collective-permute-start | bytes 393224 | tf_op jit(solution)/shard_map/ppermute | solution.py:42
  31.7 5.8 %collective-permute-start.9 = (f32[2,128]{1,0:T(2,128)S(1)}, f32[2,128]{1,0:T(2,128)S(1)}, u32[]{:S(2)}, u32[]{:S(2)}) collective-permute-start(f32[2,128]{1,0:T(2,128)S(1)} %pad_maximum_fusion.8), channel_id=1, source_target_pairs={{0,16},{8,24},{16,0},{24,8},{1,17},{9,25},{17,1},{25,9},{2,18},{10... | collective-permute-start | bytes 3080 | tf_op jit(solution)/shard_map/ppermute | solution.py:116
  34.7 5.0 %collective-permute-start.19 = (bf16[64,1024]{1,0:T(8,128)(2,1)S(1)}, bf16[64,1024]{1,0:T(8,128)(2,1)S(1)}, u32[]{:S(2)}, u32[]{:S(2)}) collective-permute-start(bf16[64,1024]{1,0:T(8,128)(2,1)S(1)} %collective-permute-done.18.refs_13_), channel_id=1, source_target_pairs={{0,1},{2,0},{4,2},{6,4},{7,6},{5,7},{3,5},{1,3},{8,9},{10,8},{12,1... | collective-permute-start | bytes 393224 | tf_op jit(solution)/shard_map/ppermute | solution.py:42
  36.7 5.0 %collective-permute-start.16 = (bf16[64,1024]{1,0:T(8,128)(2,1)S(1)}, bf16[64,1024]{1,0:T(8,128)(2,1)S(1)}, u32[]{:S(2)}, u32[]{:S(2)}) collective-permute-start(bf16[64,1024]{1,0:T(8,128)(2,1)S(1)} %collective-permute-done.15.refs_9_), channel_id=1, source_target_pairs={{0,2},{2,4},{4,6},{6,7},{7,5},{5,3},{3,1},{1,0},{8,10},{10,12},{12... | collective-permute-start | bytes 393224 | tf_op jit(solution)/shard_map/ppermute | solution.py:42
  38.9 6.4 %collective-permute-start.13 = (bf16[64,1024]{1,0:T(8,128)(2,1)S(1)}, bf16[64,1024]{1,0:T(8,128)(2,1)S(1)}, u32[]{:S(2)}, u32[]{:S(2)}) collective-permute-start(bf16[64,1024]{1,0:T(8,128)(2,1)S(1)} %collective-permute-done.10.refs_1_), channel_id=1, source_target_pairs={{0,2},{2,4},{4,6},{6,7},{7,5},{5,3},{3,1},{1,0},{8,10},{10,12},{12... | collective-permute-start | bytes 393224 | tf_op jit(solution)/shard_map/ppermute | solution.py:42
  39.7 5.6 %collective-permute-start.20 = (bf16[64,1024]{1,0:T(8,128)(2,1)S(1)}, bf16[64,1024]{1,0:T(8,128)(2,1)S(1)}, u32[]{:S(2)}, u32[]{:S(2)}) collective-permute-start(bf16[64,1024]{1,0:T(8,128)(2,1)S(1)} %collective-permute-done.19.refs_14_), channel_id=1, source_target_pairs={{0,1},{2,0},{4,2},{6,4},{7,6},{5,7},{3,5},{1,3},{8,9},{10,8},{12,1... | collective-permute-start | bytes 393224 | tf_op jit(solution)/shard_map/ppermute | solution.py:42
  56.8 14.2 %collective-permute-start.22 = (s16[128,2048]{1,0:T(8,128)(2,1)S(1)}, s16[128,2048]{1,0:T(8,128)(2,1)S(1)}, u32[]{:S(2)}, u32[]{:S(2)}) collective-permute-start(s16[128,2048]{1,0:T(8,128)(2,1)S(1)} %round-nearest-even_convert_fusion), channel_id=1, source_target_pairs={{0,16},{8,24},{16,0},{24,8},{1,17},{9,25},{17,1},{25,9},{2,18},{10... | collective-permute-start | bytes 1572872 | tf_op jit(solution)/shard_map/ppermute | solution.py:116
  58.1 13.0 %collective-permute-start.23 = (f32[128]{0:T(128)S(1)}, f32[128]{0:T(128)S(1)}, u32[]{:S(2)}, u32[]{:S(2)}) collective-permute-start(f32[128]{0:T(128)S(1)} %get-tuple-element.114), channel_id=1, source_target_pairs={{0,16},{8,24},{16,0},{24,8},{1,17},{9,25},{17,1},{25,9},{2,18},{10... | collective-permute-start | bytes 1544 | tf_op jit(solution)/shard_map/ppermute | solution.py:116
  75.5 5.4 %collective-permute-start.27 = (f32[2,256]{1,0:T(2,128)S(1)}, f32[2,256]{1,0:T(2,128)S(1)}, u32[]{:S(2)}, u32[]{:S(2)}) collective-permute-start(f32[2,256]{1,0:T(2,128)S(1)} %pad_maximum_fusion.7), channel_id=1, source_target_pairs={{0,6},{1,7},{2,4},{3,5},{4,2},{5,3},{6,0},{7,1},{8,14},{9,15},{10,... | collective-permute-start | bytes 6152 | tf_op jit(solution)/shard_map/ppermute | solution.py:47
  85.3 11.5 %collective-permute-start.28 = (bf16[128,2176]{1,0:T(8,128)(2,1)S(1)}, bf16[128,2176]{1,0:T(8,128)(2,1)S(1)}, u32[]{:S(2)}, u32[]{:S(2)}) collective-permute-start(bf16[128,2176]{1,0:T(8,128)(2,1)S(1)} %get-tuple-element.83), channel_id=1, source_target_pairs={{0,16},{8,24},{16,0},{24,8},{1,17},{9,25},{17,1},{25,9},{2,18},{10... | collective-permute-start | bytes 1671176 | tf_op jit(solution)/shard_map/ppermute | solution.py:116
  106.0 29.3 %collective-permute-start.30 = (bf16[2,64,3072]{2,1,0:T(8,128)(2,1)S(1)}, bf16[2,64,3072]{2,1,0:T(8,128)(2,1)S(1)}, u32[]{:S(2)}, u32[]{:S(2)}) collective-permute-start(bf16[2,64,3072]{2,1,0:T(8,128)(2,1)S(1)} %bitcast.54), channel_id=1, source_target_pairs={{0,16},{8,24},{16,0},{24,8},{1,17},{9,25},{17,1},{25,9},{2,18},{10... | collective-permute-start | bytes 2359304 | tf_op jit(solution)/shard_map/ppermute | solution.py:116
  106.9 5.8 %collective-permute-start.32 = (bf16[32,2176]{1,0:T(8,128)(2,1)S(1)}, bf16[32,2176]{1,0:T(8,128)(2,1)S(1)}, u32[]{:S(2)}, u32[]{:S(2)}) collective-permute-start(bf16[32,2176]{1,0:T(8,128)(2,1)S(1)} %get-tuple-element.80), channel_id=1, source_target_pairs={{0,2},{2,4},{4,6},{6,7},{7,5},{5,3},{3,1},{1,0},{8,10},{10,12},{12... | collective-permute-start | bytes 417800 | tf_op jit(solution)/shard_map/ppermute | solution.py:42
  107.0 7.9 %collective-permute-start.46 = (bf16[32,2176]{1,0:T(8,128)(2,1)S(1)}, bf16[32,2176]{1,0:T(8,128)(2,1)S(1)}, u32[]{:S(2)}, u32[]{:S(2)}) collective-permute-start(bf16[32,2176]{1,0:T(8,128)(2,1)S(1)} %get-tuple-element.79), channel_id=1, source_target_pairs={{0,1},{2,0},{4,2},{6,4},{7,6},{5,7},{3,5},{1,3},{8,9},{10,8},{12,1... | collective-permute-start | bytes 417800 | tf_op jit(solution)/shard_map/ppermute | solution.py:42
  112.8 5.8 %collective-permute-start.33 = (bf16[32,2176]{1,0:T(8,128)(2,1)S(1)}, bf16[32,2176]{1,0:T(8,128)(2,1)S(1)}, u32[]{:S(2)}, u32[]{:S(2)}) collective-permute-start(bf16[32,2176]{1,0:T(8,128)(2,1)S(1)} %add_convert_fusion.9), channel_id=1, source_target_pairs={{0,2},{2,4},{4,6},{6,7},{7,5},{5,3},{3,1},{1,0},{8,10},{10,12},{12... | collective-permute-start | bytes 417800 | tf_op jit(solution)/shard_map/ppermute | solution.py:42
  113.2 6.6 %collective-permute-start.34 = (bf16[32,2176]{1,0:T(8,128)(2,1)S(1)}, bf16[32,2176]{1,0:T(8,128)(2,1)S(1)}, u32[]{:S(2)}, u32[]{:S(2)}) collective-permute-start(bf16[32,2176]{1,0:T(8,128)(2,1)S(1)} %get-tuple-element.46), channel_id=1, source_target_pairs={{0,1},{2,0},{4,2},{6,4},{7,6},{5,7},{3,5},{1,3},{8,9},{10,8},{12,1... | collective-permute-start | bytes 417800 | tf_op jit(solution)/shard_map/ppermute | solution.py:42
  114.9 7.8 %collective-permute-start.48 = (bf16[32,2176]{1,0:T(8,128)(2,1)S(1)}, bf16[32,2176]{1,0:T(8,128)(2,1)S(1)}, u32[]{:S(2)}, u32[]{:S(2)}) collective-permute-start(bf16[32,2176]{1,0:T(8,128)(2,1)S(1)} %add_convert_fusion.3), channel_id=1, source_target_pairs={{0,1},{2,0},{4,2},{6,4},{7,6},{5,7},{3,5},{1,3},{8,9},{10,8},{12,1... | collective-permute-start | bytes 417800 | tf_op jit(solution)/shard_map/ppermute | solution.py:42
  116.1 6.6 %collective-permute-start.47 = (bf16[32,2176]{1,0:T(8,128)(2,1)S(1)}, bf16[32,2176]{1,0:T(8,128)(2,1)S(1)}, u32[]{:S(2)}, u32[]{:S(2)}) collective-permute-start(bf16[32,2176]{1,0:T(8,128)(2,1)S(1)} %get-tuple-element.53), channel_id=1, source_target_pairs={{0,2},{2,4},{4,6},{6,7},{7,5},{5,3},{3,1},{1,0},{8,10},{10,12},{12... | collective-permute-start | bytes 417800 | tf_op jit(solution)/shard_map/ppermute | solution.py:42
  119.8 5.8 %collective-permute-start.36 = (bf16[32,2176]{1,0:T(8,128)(2,1)S(1)}, bf16[32,2176]{1,0:T(8,128)(2,1)S(1)}, u32[]{:S(2)}, u32[]{:S(2)}) collective-permute-start(bf16[32,2176]{1,0:T(8,128)(2,1)S(1)} %get-tuple-element.48), channel_id=1, source_target_pairs={{0,1},{2,0},{4,2},{6,4},{7,6},{5,7},{3,5},{1,3},{8,9},{10,8},{12,1... | collective-permute-start | bytes 417800 | tf_op jit(solution)/shard_map/ppermute | solution.py:42
  121.3 5.1 %collective-permute-start.35 = (bf16[32,2176]{1,0:T(8,128)(2,1)S(1)}, bf16[32,2176]{1,0:T(8,128)(2,1)S(1)}, u32[]{:S(2)}, u32[]{:S(2)}) collective-permute-start(bf16[32,2176]{1,0:T(8,128)(2,1)S(1)} %get-tuple-element.47), channel_id=1, source_target_pairs={{0,2},{2,4},{4,6},{6,7},{7,5},{5,3},{3,1},{1,0},{8,10},{10,12},{12... | collective-permute-start | bytes 417800 | tf_op jit(solution)/shard_map/ppermute | solution.py:42
  122.8 6.6 %collective-permute-start.50 = (bf16[32,2176]{1,0:T(8,128)(2,1)S(1)}, bf16[32,2176]{1,0:T(8,128)(2,1)S(1)}, u32[]{:S(2)}, u32[]{:S(2)}) collective-permute-start(bf16[32,2176]{1,0:T(8,128)(2,1)S(1)} %get-tuple-element.56), channel_id=1, source_target_pairs={{0,1},{2,0},{4,2},{6,4},{7,6},{5,7},{3,5},{1,3},{8,9},{10,8},{12,1... | collective-permute-start | bytes 417800 | tf_op jit(solution)/shard_map/ppermute | solution.py:42
  124.3 6.0 %collective-permute-start.49 = (bf16[32,2176]{1,0:T(8,128)(2,1)S(1)}, bf16[32,2176]{1,0:T(8,128)(2,1)S(1)}, u32[]{:S(2)}, u32[]{:S(2)}) collective-permute-start(bf16[32,2176]{1,0:T(8,128)(2,1)S(1)} %get-tuple-element.55), channel_id=1, source_target_pairs={{0,2},{2,4},{4,6},{6,7},{7,5},{5,3},{3,1},{1,0},{8,10},{10,12},{12... | collective-permute-start | bytes 417800 | tf_op jit(solution)/shard_map/ppermute | solution.py:42
  126.4 6.0 %collective-permute-start.38 = (bf16[32,2176]{1,0:T(8,128)(2,1)S(1)}, bf16[32,2176]{1,0:T(8,128)(2,1)S(1)}, u32[]{:S(2)}, u32[]{:S(2)}) collective-permute-start(bf16[32,2176]{1,0:T(8,128)(2,1)S(1)} %get-tuple-element.50), channel_id=1, source_target_pairs={{0,1},{2,0},{4,2},{6,4},{7,6},{5,7},{3,5},{1,3},{8,9},{10,8},{12,1... | collective-permute-start | bytes 417800 | tf_op jit(solution)/shard_map/ppermute | solution.py:42
  127.6 6.4 %collective-permute-start.37 = (bf16[32,2176]{1,0:T(8,128)(2,1)S(1)}, bf16[32,2176]{1,0:T(8,128)(2,1)S(1)}, u32[]{:S(2)}, u32[]{:S(2)}) collective-permute-start(bf16[32,2176]{1,0:T(8,128)(2,1)S(1)} %get-tuple-element.49), channel_id=1, source_target_pairs={{0,2},{2,4},{4,6},{6,7},{7,5},{5,3},{3,1},{1,0},{8,10},{10,12},{12... | collective-permute-start | bytes 417800 | tf_op jit(solution)/shard_map/ppermute | solution.py:42
  130.4 5.1 %collective-permute-start.52 = (bf16[32,2176]{1,0:T(8,128)(2,1)S(1)}, bf16[32,2176]{1,0:T(8,128)(2,1)S(1)}, u32[]{:S(2)}, u32[]{:S(2)}) collective-permute-start(bf16[32,2176]{1,0:T(8,128)(2,1)S(1)} %get-tuple-element.58), channel_id=1, source_target_pairs={{0,1},{2,0},{4,2},{6,4},{7,6},{5,7},{3,5},{1,3},{8,9},{10,8},{12,1... | collective-permute-start | bytes 417800 | tf_op jit(solution)/shard_map/ppermute | solution.py:42
  131.6 5.1 %collective-permute-start.51 = (bf16[32,2176]{1,0:T(8,128)(2,1)S(1)}, bf16[32,2176]{1,0:T(8,128)(2,1)S(1)}, u32[]{:S(2)}, u32[]{:S(2)}) collective-permute-start(bf16[32,2176]{1,0:T(8,128)(2,1)S(1)} %get-tuple-element.57), channel_id=1, source_target_pairs={{0,2},{2,4},{4,6},{6,7},{7,5},{5,3},{3,1},{1,0},{8,10},{10,12},{12... | collective-permute-start | bytes 417800 | tf_op jit(solution)/shard_map/ppermute | solution.py:42
  134.2 5.6 %collective-permute-start.39 = (bf16[32,2048]{1,0:T(8,128)(2,1)S(1)}, bf16[32,2048]{1,0:T(8,128)(2,1)S(1)}, u32[]{:S(2)}, u32[]{:S(2)}) collective-permute-start(bf16[32,2048]{1,0:T(8,128)(2,1)S(1)} %fusion.6.refs_4_), channel_id=1, source_target_pairs={{0,2},{2,4},{4,6},{6,7},{7,5},{5,3},{3,1},{1,0},{8,10},{10,12},{12... | collective-permute-start | bytes 393224 | tf_op jit(solution)/shard_map/ppermute | solution.py:42
  135.4 21.4 %collective-permute-start.31 = (bf16[2,2,64,3072]{3,2,0,1:T(8,128)(2,1)S(1)}, bf16[2,2,64,3072]{3,2,0,1:T(8,128)(2,1)S(1)}, u32[]{:S(2)}, u32[]{:S(2)}) collective-permute-start(bf16[2,2,64,3072]{3,2,0,1:T(8,128)(2,1)S(1)} %pad_maximum_fusion.1), channel_id=1, source_target_pairs={{0,8},{8,0},{16,24},{24,16},{1,9},{9,1},{17,25},{25,17},{2,10},{10... | collective-permute-start | bytes 4718600 | tf_op jit(solution)/shard_map/ppermute | solution.py:112
  136.9 6.5 %collective-permute-start.56 = (bf16[32,2048]{1,0:T(8,128)(2,1)S(1)}, bf16[32,2048]{1,0:T(8,128)(2,1)S(1)}, u32[]{:S(2)}, u32[]{:S(2)}) collective-permute-start(bf16[32,2048]{1,0:T(8,128)(2,1)S(1)} %fusion.4.refs_11_), channel_id=1, source_target_pairs={{0,1},{2,0},{4,2},{6,4},{7,6},{5,7},{3,5},{1,3},{8,9},{10,8},{12,1... | collective-permute-start | bytes 393224 | tf_op jit(solution)/shard_map/ppermute | solution.py:42
  137.8 8.4 %collective-permute-start.43 = (bf16[32,2048]{1,0:T(8,128)(2,1)S(1)}, bf16[32,2048]{1,0:T(8,128)(2,1)S(1)}, u32[]{:S(2)}, u32[]{:S(2)}) collective-permute-start(bf16[32,2048]{1,0:T(8,128)(2,1)S(1)} %fusion.6.refs_4_), channel_id=1, source_target_pairs={{0,1},{2,0},{4,2},{6,4},{7,6},{5,7},{3,5},{1,3},{8,9},{10,8},{12,1... | collective-permute-start | bytes 393224 | tf_op jit(solution)/shard_map/ppermute | solution.py:42
  139.2 7.8 %collective-permute-start.53 = (bf16[32,2048]{1,0:T(8,128)(2,1)S(1)}, bf16[32,2048]{1,0:T(8,128)(2,1)S(1)}, u32[]{:S(2)}, u32[]{:S(2)}) collective-permute-start(bf16[32,2048]{1,0:T(8,128)(2,1)S(1)} %fusion.4.refs_11_), channel_id=1, source_target_pairs={{0,2},{2,4},{4,6},{6,7},{7,5},{5,3},{3,1},{1,0},{8,10},{10,12},{12... | collective-permute-start | bytes 393224 | tf_op jit(solution)/shard_map/ppermute | solution.py:42
  139.8 8.4 %collective-permute-start.40 = (bf16[32,2048]{1,0:T(8,128)(2,1)S(1)}, bf16[32,2048]{1,0:T(8,128)(2,1)S(1)}, u32[]{:S(2)}, u32[]{:S(2)}) collective-permute-start(bf16[32,2048]{1,0:T(8,128)(2,1)S(1)} %collective-permute-done.39.refs_3_), channel_id=1, source_target_pairs={{0,2},{2,4},{4,6},{6,7},{7,5},{5,3},{3,1},{1,0},{8,10},{10,12},{12... | collective-permute-start | bytes 393224 | tf_op jit(solution)/shard_map/ppermute | solution.py:42
  143.4 5.7 %collective-permute-start.57 = (bf16[32,2048]{1,0:T(8,128)(2,1)S(1)}, bf16[32,2048]{1,0:T(8,128)(2,1)S(1)}, u32[]{:S(2)}, u32[]{:S(2)}) collective-permute-start(bf16[32,2048]{1,0:T(8,128)(2,1)S(1)} %collective-permute-done.56.refs_12_), channel_id=1, source_target_pairs={{0,1},{2,0},{4,2},{6,4},{7,6},{5,7},{3,5},{1,3},{8,9},{10,8},{12,1... | collective-permute-start | bytes 393224 | tf_op jit(solution)/shard_map/ppermute | solution.py:42
  146.2 6.4 %collective-permute-start.44 = (bf16[32,2048]{1,0:T(8,128)(2,1)S(1)}, bf16[32,2048]{1,0:T(8,128)(2,1)S(1)}, u32[]{:S(2)}, u32[]{:S(2)}) collective-permute-start(bf16[32,2048]{1,0:T(8,128)(2,1)S(1)} %collective-permute-done.43.refs_5_), channel_id=1, source_target_pairs={{0,1},{2,0},{4,2},{6,4},{7,6},{5,7},{3,5},{1,3},{8,9},{10,8},{12,1... | collective-permute-start | bytes 393224 | tf_op jit(solution)/shard_map/ppermute | solution.py:42
  147.0 6.3 %collective-permute-start.54 = (bf16[32,2048]{1,0:T(8,128)(2,1)S(1)}, bf16[32,2048]{1,0:T(8,128)(2,1)S(1)}, u32[]{:S(2)}, u32[]{:S(2)}) collective-permute-start(bf16[32,2048]{1,0:T(8,128)(2,1)S(1)} %collective-permute-done.53.refs_10_), channel_id=1, source_target_pairs={{0,2},{2,4},{4,6},{6,7},{7,5},{5,3},{3,1},{1,0},{8,10},{10,12},{12... | collective-permute-start | bytes 393224 | tf_op jit(solution)/shard_map/ppermute | solution.py:42
  148.2 6.4 %collective-permute-start.41 = (bf16[32,2048]{1,0:T(8,128)(2,1)S(1)}, bf16[32,2048]{1,0:T(8,128)(2,1)S(1)}, u32[]{:S(2)}, u32[]{:S(2)}) collective-permute-start(bf16[32,2048]{1,0:T(8,128)(2,1)S(1)} %collective-permute-done.40.refs_2_), channel_id=1, source_target_pairs={{0,2},{2,4},{4,6},{6,7},{7,5},{5,3},{3,1},{1,0},{8,10},{10,12},{12... | collective-permute-start | bytes 393224 | tf_op jit(solution)/shard_map/ppermute | solution.py:42
  149.1 7.7 %collective-permute-start.58 = (bf16[32,2048]{1,0:T(8,128)(2,1)S(1)}, bf16[32,2048]{1,0:T(8,128)(2,1)S(1)}, u32[]{:S(2)}, u32[]{:S(2)}) collective-permute-start(bf16[32,2048]{1,0:T(8,128)(2,1)S(1)} %collective-permute-done.57.refs_13_), channel_id=1, source_target_pairs={{0,1},{2,0},{4,2},{6,4},{7,6},{5,7},{3,5},{1,3},{8,9},{10,8},{12,1... | collective-permute-start | bytes 393224 | tf_op jit(solution)/shard_map/ppermute | solution.py:42
  154.6 5.1 %collective-permute-start.42 = (bf16[32,2048]{1,0:T(8,128)(2,1)S(1)}, bf16[32,2048]{1,0:T(8,128)(2,1)S(1)}, u32[]{:S(2)}, u32[]{:S(2)}) collective-permute-start(bf16[32,2048]{1,0:T(8,128)(2,1)S(1)} %collective-permute-done.41.refs_1_), channel_id=1, source_target_pairs={{0,2},{2,4},{4,6},{6,7},{7,5},{5,3},{3,1},{1,0},{8,10},{10,12},{12... | collective-permute-start | bytes 393224 | tf_op jit(solution)/shard_map/ppermute | solution.py:42
  (17 other events, 94.7 us)

commit v16 on v14

--- a/solution.py
+++ b/solution.py
@@ -375,8 +375,8 @@
 def outer(index, chosen, chunks, share_rows):
     depth = chunks[0][0].shape[1]
     all_rows, joined = chosen.shape
-    tile = min(depth // 4, 256)
-    slots, copies = 3, 4
+    tile = min(depth // 4, 512)
+    slots, copies = 2, 8
     pieces = [x for chunk in chunks for x in chunk]
     return pl.pallas_call(
         functools.partial(outer_kernel, len(chunks[0]), copies),
@@ -395,7 +395,7 @@
             pltpu.VMEM((slots, tile, joined), F32),
             pltpu.SemaphoreType.DMA((slots, copies)),
         ],
-        compiler_params=pltpu.CompilerParams(vmem_limit_bytes=32 * 2**20),
+        compiler_params=pltpu.CompilerParams(vmem_limit_bytes=40 * 2**20),
         cost_estimate=pl.CostEstimate(
             flops=2 * all_rows * depth * joined,
             bytes_accessed=4 * depth * joined + 2 * all_rows * (depth + joined),

time: 172 us -> 173 us (level)
  transfers between devices with their start and end apart: 60 -> 60, of which waited for: 34 -> 35; matrix products, arithmetic and copies ran while one was open for 6% -> 6% of each run, Pallas kernels for 2% -> 2%
where the time goes in v16:
time: 173 us; the launch traced here: 172 us
  waiting for transfers between devices  64.7 us (37%)
  starting transfers between devices  63.9 us (37%)
  Pallas kernels  28.5 us (16%)
  other arithmetic  10.9 us (6%)
  local copies, waits for them, and re-layouts  3.1 us (2%)
    ppermute x42, starting transfers between devices, shift(): lax.ppermute(x, 'vocab', [(order[p], order[(p + step) % size]) for p in r...  41.9 us
    ppermute x42, waiting for transfers between devices, shift(): lax.ppermute(x, 'vocab', [(order[p], order[(p + step) % size]) for p in r...  32.2 us
    ppermute x5, waiting for transfers between devices, shift(): lax.ppermute(x, 'dp', [(i, (i + CORES * step) % size) for i in range(size)])  20.4 us
    ppermute x8, starting transfers between devices, partner(): return lax.ppermute(x, 'vocab', [(v, v ^ bit) for v in range(self.size)])  14.5 us
    pallas_call x1, Pallas kernels, outer(): pl.pallas_call(functools.partial(outer_kernel, len(chunks[0]), copies), g...  12.4 us
    ppermute x8, waiting for transfers between devices, partner(): return lax.ppermute(x, 'vocab', [(v, v ^ bit) for v in range(self.size)])  11.8 us
    pallas_call x1, Pallas kernels, project(): pl.pallas_call(functools.partial(project_kernel, len(blocks[0]), tile), g...  6.04 us
    pallas_call x1, Pallas kernels, back(): pl.pallas_call(functools.partial(back_kernel, piece_rows, tile), grid=(de...  5.81 us
  transfers between devices with their start and end apart: 60, of which 35 were waited for; matrix products, arithmetic and copies ran while one was open for 6% of the time, Pallas kernels for 2%

profile of v16, /device:TPU:0, one launch (start us, length us, event | category | flops | bytes accessed | tf_op | source)
XLA Modules:
  0.0 172.3 jit_solution(5188667603696370414)
XLA Ops:
  1.7 3.0 %collective-permute-start = (f32[1,128]{1,0:T(1,128)S(1)}, f32[1,128]{1,0:T(1,128)S(1)}, u32[]{:S(2)}, u32[]{:S(2)}) collective-permute-start(f32[1,128]{1,0:T(1,128)S(1)} %bitcast.77), channel_id=1, source_target_pairs={{0,1},{1,0},{2,3},{3,2},{4,5},{5,4},{6,7},{7,6},{8,9},{9,8},{10,11... | collective-permute-start | bytes 1544 | tf_op jit(solution)/shard_map/ppermute | solution.py:47
  4.7 1.6 collective-permute-start.4
  6.3 4.3 %collective-permute-start.3 = (f32[1,128]{1,0:T(1,128)S(1)}, f32[1,128]{1,0:T(1,128)S(1)}, u32[]{:S(2)}, u32[]{:S(2)}) collective-permute-start(f32[1,128]{1,0:T(1,128)S(1)} %bitcast_add_fusion), channel_id=1, source_target_pairs={{0,6},{1,7},{2,4},{3,5},{4,2},{5,3},{6,0},{7,1},{8,14},{9,15},{10,... | collective-permute-start | bytes 1544 | tf_op jit(solution)/shard_map/ppermute | solution.py:47
  11.3 6.3 %collective-permute-done.3 = f32[1,128]{1,0:T(1,128)S(1)} collective-permute-done((f32[1,128]{1,0:T(1,128)S(1)}, f32[1,128]{1,0:T(1,128)S(1)}, u32[]{:S(2)}, u32[]{:S(2)}) %collective-permute-start.3) | collective-permute-done | bytes 544 | tf_op jit(solution)/shard_map/ppermute | solution.py:47
  19.0 1.5 collective-permute-start.5
  20.6 1.9 %collective-permute-start.6 = (bf16[64,1024]{1,0:T(8,128)(2,1)S(1)}, bf16[64,1024]{1,0:T(8,128)(2,1)S(1)}, u32[]{:S(2)}, u32[]{:S(2)}) collective-permute-start(bf16[64,1024]{1,0:T(8,128)(2,1)S(1)} %get-tuple-element.83.refs_4_), channel_id=1, source_target_pairs={{0,1},{2,0},{4,2},{6,4},{7,6},{5,7},{3,5},{1,3},{8,9},{10,8},{12,1... | collective-permute-start | bytes 393224 | tf_op jit(solution)/shard_map/ppermute | solution.py:42
  22.5 2.3 %collective-permute-done.17.refs_12_ = bf16[64,1024]{1,0:T(8,128)(2,1)S(1)} collective-permute-done((bf16[64,1024]{1,0:T(8,128)(2,1)S(1)}, bf16[64,1024]{1,0:T(8,128)(2,1)S(1)}, u32[]{:S(2)}, u32[]{:S(2)}) %collective-permute-start.17) | collective-permute-done | bytes 131104 | tf_op jit(solution)/shard_map/ppermute | solution.py:42
  25.3 1.6 collective-permute-start.8
  27.7 1.3 collective-permute-start.7
  29.2 1.8 %collective-permute-start.15 = (bf16[64,1024]{1,0:T(8,128)(2,1)S(1)}, bf16[64,1024]{1,0:T(8,128)(2,1)S(1)}, u32[]{:S(2)}, u32[]{:S(2)}) collective-permute-start(bf16[64,1024]{1,0:T(8,128)(2,1)S(1)} %collective-permute-done.14.refs_10_), channel_id=1, source_target_pairs={{0,2},{2,4},{4,6},{6,7},{7,5},{5,3},{3,1},{1,0},{8,10},{10,12},{12... | collective-permute-start | bytes 393224 | tf_op jit(solution)/shard_map/ppermute | solution.py:42
  31.5 1.6 collective-permute-start.11
  34.5 1.6 collective-permute-start.16
  36.6 1.6 collective-permute-start.12
  38.7 2.2 %collective-permute-done.16.refs_8_ = bf16[64,1024]{1,0:T(8,128)(2,1)S(1)} collective-permute-done((bf16[64,1024]{1,0:T(8,128)(2,1)S(1)}, bf16[64,1024]{1,0:T(8,128)(2,1)S(1)}, u32[]{:S(2)}, u32[]{:S(2)}) %collective-permute-start.16) | collective-permute-done | bytes 131104 | tf_op jit(solution)/shard_map/ppermute | solution.py:42
  40.9 1.9 %collective-permute-done.20.refs_15_ = bf16[64,1024]{1,0:T(8,128)(2,1)S(1)} collective-permute-done((bf16[64,1024]{1,0:T(8,128)(2,1)S(1)}, bf16[64,1024]{1,0:T(8,128)(2,1)S(1)}, u32[]{:S(2)}, u32[]{:S(2)}) %collective-permute-start.20) | collective-permute-done | bytes 131104 | tf_op jit(solution)/shard_map/ppermute | solution.py:42
  43.5 6.0 %shard_map.96 = (f32[256,2048]{1,0:T(8,128)S(1)}, bf16[2048,256]{1,0:T(8,128)(2,1)S(1)}, bf16[2048,2048]{1,0:T(8,128)(2,1)S(1)}, bf16[32,2048]{1,0:T(8,128)(2,1)S(1)}, bf16[32,2048]{1,0:T(8,128)(2,1)S(1)}) custom-call(s32[35]{0:T(128)S(1)} %slice_bitcast_fusion.1.index_ref, f32[4,128]{1,0:T(4,128)S(1)} %get-tuple-element.87.factor_ref, ...), custom_call_target="tpu_custom_call" | custom-call | flops 2147483648 | bytes 12582912 | tf_op jit(solution)/shard_map/pallas_call | solution.py:251
  50.3 3.3 %shard_map.97 = f32[256,2048]{1,0:T(8,128)S(1)} custom-call(bf16[2048,2048]{1,0:T(8,128)(2,1)S(1)} %get-tuple-element.34.weight_ref, bf16[2048,256]{1,0:T(8,128)(2,1)S(1)} %get-tuple-element.35.turned_ref), custom_call_target="tpu_custom_call" | custom-call | flops 2147483648 | bytes 12582912 | tf_op jit(solution)/shard_map/pallas_call | solution.py:271
  54.3 1.3 collective-permute-start.22
  57.1 11.4 %collective-permute-done.23 = f32[128]{0:T(128)S(1)} collective-permute-done((f32[128]{0:T(128)S(1)}, f32[128]{0:T(128)S(1)}, u32[]{:S(2)}, u32[]{:S(2)}) %collective-permute-start.23) | collective-permute-done | bytes 544 | tf_op jit(solution)/shard_map/ppermute | solution.py:116
  69.3 1.6 collective-permute-start.24
  70.8 1.2 iota_compare_fusion
  72.9 4.3 %collective-permute-start.27 = (f32[2,256]{1,0:T(2,128)S(1)}, f32[2,256]{1,0:T(2,128)S(1)}, u32[]{:S(2)}, u32[]{:S(2)}) collective-permute-start(f32[2,256]{1,0:T(2,128)S(1)} %pad_maximum_fusion.7), channel_id=1, source_target_pairs={{0,6},{1,7},{2,4},{3,5},{4,2},{5,3},{6,0},{7,1},{8,14},{9,15},{10,... | collective-permute-start | bytes 6152 | tf_op jit(solution)/shard_map/ppermute | solution.py:47
  78.8 3.6 %collective-permute-done.26 = f32[2,256]{1,0:T(2,128)S(1)} collective-permute-done((f32[2,256]{1,0:T(2,128)S(1)}, f32[2,256]{1,0:T(2,128)S(1)}, u32[]{:S(2)}, u32[]{:S(2)}) %collective-permute-start.26) | collective-permute-done | bytes 2080 | tf_op jit(solution)/shard_map/ppermute | solution.py:47
  85.8 9.0 %collective-permute-done.28 = bf16[128,2176]{1,0:T(8,128)(2,1)S(1)} collective-permute-done((bf16[128,2176]{1,0:T(8,128)(2,1)S(1)}, bf16[128,2176]{1,0:T(8,128)(2,1)S(1)}, u32[]{:S(2)}, u32[]{:S(2)}) %collective-permute-start.28) | collective-permute-done | bytes 557088 | tf_op jit(solution)/shard_map/ppermute | solution.py:116
  95.0 1.4 multiply_multiply_fusion
  96.3 1.4 multiply_multiply_fusion.1
  97.9 5.8 %shard_map.99 = (f32[256,2176]{1,0:T(8,128)S(1)}, f32[256,2176]{1,0:T(8,128)S(1)}) custom-call(s32[8]{0:T(128)S(1)} %slice_bitcast_fusion.2.index_ref, bf16[2,128,2176]{2,1,0:T(8,128)(2,1)S(1)} %pad_maximum_fusion.2.mine_ref, bf16[2,128,2176]{2,1,0:T(8,128)(2,1)S(1)} %collective-permute-done.29.other_ref, bf16[2048,2048]{1,0:T(8,128)(2,1)S(1)} %get-tuple-element.34.weight_ref), custom_call_target="tpu_custom_call" | custom-call | flops 4294967296 | bytes 14680064 | tf_op jit(solution)/shard_map/pallas_call | solution.py:314
  105.2 2.1 %collective-permute-start.46 = (bf16[32,2176]{1,0:T(8,128)(2,1)S(1)}, bf16[32,2176]{1,0:T(8,128)(2,1)S(1)}, u32[]{:S(2)}, u32[]{:S(2)}) collective-permute-start(bf16[32,2176]{1,0:T(8,128)(2,1)S(1)} %get-tuple-element.77), channel_id=1, source_target_pairs={{0,1},{2,0},{4,2},{6,4},{7,6},{5,7},{3,5},{1,3},{8,9},{10,8},{12,1... | collective-permute-start | bytes 417800 | tf_op jit(solution)/shard_map/ppermute | solution.py:42
  107.3 3.7 %collective-permute-done.32 = bf16[32,2176]{1,0:T(8,128)(2,1)S(1)} collective-permute-done((bf16[32,2176]{1,0:T(8,128)(2,1)S(1)}, bf16[32,2176]{1,0:T(8,128)(2,1)S(1)}, u32[]{:S(2)}, u32[]{:S(2)}) %collective-permute-start.32) | collective-permute-done | bytes 139296 | tf_op jit(solution)/shard_map/ppermute | solution.py:42
  111.4 1.7 %collective-permute-start.34 = (bf16[32,2176]{1,0:T(8,128)(2,1)S(1)}, bf16[32,2176]{1,0:T(8,128)(2,1)S(1)}, u32[]{:S(2)}, u32[]{:S(2)}) collective-permute-start(bf16[32,2176]{1,0:T(8,128)(2,1)S(1)} %get-tuple-element.44), channel_id=1, source_target_pairs={{0,1},{2,0},{4,2},{6,4},{7,6},{5,7},{3,5},{1,3},{8,9},{10,8},{12,1... | collective-permute-start | bytes 417800 | tf_op jit(solution)/shard_map/ppermute | solution.py:42
  113.1 1.4 collective-permute-start.48
  115.2 1.3 collective-permute-done.33
  116.5 1.4 collective-permute-done.34
  118.0 1.5 collective-permute-start.36
  121.0 1.5 collective-permute-start.50
  128.6 1.3 collective-permute-start.52
  130.7 1.8 %collective-permute-done.37 = bf16[32,2176]{1,0:T(8,128)(2,1)S(1)} collective-permute-done((bf16[32,2176]{1,0:T(8,128)(2,1)S(1)}, bf16[32,2176]{1,0:T(8,128)(2,1)S(1)}, u32[]{:S(2)}, u32[]{:S(2)}) %collective-permute-start.37) | collective-permute-done | bytes 139296 | tf_op jit(solution)/shard_map/ppermute | solution.py:42
  133.8 1.2 collective-permute-done.51
  136.2 1.4 collective-permute-start.43
  139.4 2.4 %collective-permute-done.56.refs_12_ = bf16[32,2048]{1,0:T(8,128)(2,1)S(1)} collective-permute-done((bf16[32,2048]{1,0:T(8,128)(2,1)S(1)}, bf16[32,2048]{1,0:T(8,128)(2,1)S(1)}, u32[]{:S(2)}, u32[]{:S(2)}) %collective-permute-start.56) | collective-permute-done | bytes 131104 | tf_op jit(solution)/shard_map/ppermute | solution.py:42
  142.6 2.0 %collective-permute-done.43.refs_5_ = bf16[32,2048]{1,0:T(8,128)(2,1)S(1)} collective-permute-done((bf16[32,2048]{1,0:T(8,128)(2,1)S(1)}, bf16[32,2048]{1,0:T(8,128)(2,1)S(1)}, u32[]{:S(2)}, u32[]{:S(2)}) %collective-permute-start.43) | collective-permute-done | bytes 131104 | tf_op jit(solution)/shard_map/ppermute | solution.py:42
  147.4 1.4 collective-permute-start.58
  148.9 2.1 %collective-permute-done.44.refs_6_ = bf16[32,2048]{1,0:T(8,128)(2,1)S(1)} collective-permute-done((bf16[32,2048]{1,0:T(8,128)(2,1)S(1)}, bf16[32,2048]{1,0:T(8,128)(2,1)S(1)}, u32[]{:S(2)}, u32[]{:S(2)}) %collective-permute-start.44) | collective-permute-done | bytes 131104 | tf_op jit(solution)/shard_map/ppermute | solution.py:42
  151.7 1.3 collective-permute-start.55
  153.0 1.8 %collective-permute-start.42 = (bf16[32,2048]{1,0:T(8,128)(2,1)S(1)}, bf16[32,2048]{1,0:T(8,128)(2,1)S(1)}, u32[]{:S(2)}, u32[]{:S(2)}) collective-permute-start(bf16[32,2048]{1,0:T(8,128)(2,1)S(1)} %collective-permute-done.41.refs_1_), channel_id=1, source_target_pairs={{0,2},{2,4},{4,6},{6,7},{7,5},{5,3},{3,1},{1,0},{8,10},{10,12},{12... | collective-permute-start | bytes 393224 | tf_op jit(solution)/shard_map/ppermute | solution.py:42
  156.7 1.4 collective-permute-done.42.refs_0_
  158.1 1.7 collective-permute-done.59.refs_15_
  159.8 12.4 %shard_map.100 = (f32[2048,3072]{1,0:T(8,128)}, bf16[64,2048]{1,0:T(8,128)(2,1)}) custom-call(s32[17]{0:T(128)S(1)} %slice_bitcast_fusion.3.index_ref, bf16[512,3072]{1,0:T(8,128)(2,1)S(1)} %bitcast.57, bf16[32,2048]{1,0:T(8,128)(2,1)S(1)} %collective-permute-done.42.refs_0_, bf16[32,2048]{1,0:T(8,128)(2,1)S(1)} %collective-permute-done.41.refs_1_, ...), custom_call_target="tpu_custom_call" | custom-call | flops 6442450944 | bytes 30408704 | tf_op jit(solution)/shard_map/pallas_call | solution.py:381
  (148 shorter events, 39.7 us)
Async XLA Ops:
  4.7 13.7 %collective-permute-start.4 = (bf16[128,1024]{1,0:T(8,128)(2,1)}, bf16[128,1024]{1,0:T(8,128)(2,1)S(1)}, u32[]{:S(2)}, u32[]{:S(2)}) collective-permute-start(bf16[128,1024]{1,0:T(8,128)(2,1)} %param.8), channel_id=1, source_target_pairs={{0,0},{1,1},{2,8},{3,9},{4,16},{5,17},{6,24},{7,25},{8,4},{9,5},{1... | collective-permute-start | bytes 786440 | tf_op jit(solution)/shard_map/ppermute | solution.py:490
  6.3 11.3 %collective-permute-start.3 = (f32[1,128]{1,0:T(1,128)S(1)}, f32[1,128]{1,0:T(1,128)S(1)}, u32[]{:S(2)}, u32[]{:S(2)}) collective-permute-start(f32[1,128]{1,0:T(1,128)S(1)} %bitcast_add_fusion), channel_id=1, source_target_pairs={{0,6},{1,7},{2,4},{3,5},{4,2},{5,3},{6,0},{7,1},{8,14},{9,15},{10,... | collective-permute-start | bytes 1544 | tf_op jit(solution)/shard_map/ppermute | solution.py:47
  10.6 7.3 %collective-permute-start.2 = (f32[1,128]{1,0:T(1,128)S(1)}, f32[1,128]{1,0:T(1,128)S(1)}, u32[]{:S(2)}, u32[]{:S(2)}) collective-permute-start(f32[1,128]{1,0:T(1,128)S(1)} %bitcast_add_fusion), channel_id=1, source_target_pairs={{0,4},{1,5},{2,6},{3,7},{4,0},{5,1},{6,2},{7,3},{8,12},{9,13},{10,... | collective-permute-start | bytes 1544 | tf_op jit(solution)/shard_map/ppermute | solution.py:47
  10.7 7.7 %collective-permute-start.1 = (f32[1,128]{1,0:T(1,128)S(1)}, f32[1,128]{1,0:T(1,128)S(1)}, u32[]{:S(2)}, u32[]{:S(2)}) collective-permute-start(f32[1,128]{1,0:T(1,128)S(1)} %bitcast_add_fusion), channel_id=1, source_target_pairs={{0,2},{1,3},{2,0},{3,1},{4,6},{5,7},{6,4},{7,5},{8,10},{9,11},{10,... | collective-permute-start | bytes 1544 | tf_op jit(solution)/shard_map/ppermute | solution.py:47
  18.4 6.4 %collective-permute-start.17 = (bf16[64,1024]{1,0:T(8,128)(2,1)S(1)}, bf16[64,1024]{1,0:T(8,128)(2,1)S(1)}, u32[]{:S(2)}, u32[]{:S(2)}) collective-permute-start(bf16[64,1024]{1,0:T(8,128)(2,1)S(1)} %get-tuple-element.82.refs_11_), channel_id=1, source_target_pairs={{0,1},{2,0},{4,2},{6,4},{7,6},{5,7},{3,5},{1,3},{8,9},{10,8},{12,1... | collective-permute-start | bytes 393224 | tf_op jit(solution)/shard_map/ppermute | solution.py:42
  19.0 6.4 %collective-permute-start.5 = (bf16[64,1024]{1,0:T(8,128)(2,1)S(1)}, bf16[64,1024]{1,0:T(8,128)(2,1)S(1)}, u32[]{:S(2)}, u32[]{:S(2)}) collective-permute-start(bf16[64,1024]{1,0:T(8,128)(2,1)S(1)} %get-tuple-element.83.refs_4_), channel_id=1, source_target_pairs={{0,2},{2,4},{4,6},{6,7},{7,5},{5,3},{3,1},{1,0},{8,10},{10,12},{12... | collective-permute-start | bytes 393224 | tf_op jit(solution)/shard_map/ppermute | solution.py:42
  20.5 8.7 %collective-permute-start.14 = (bf16[64,1024]{1,0:T(8,128)(2,1)S(1)}, bf16[64,1024]{1,0:T(8,128)(2,1)S(1)}, u32[]{:S(2)}, u32[]{:S(2)}) collective-permute-start(bf16[64,1024]{1,0:T(8,128)(2,1)S(1)} %get-tuple-element.82.refs_11_), channel_id=1, source_target_pairs={{0,2},{2,4},{4,6},{6,7},{7,5},{5,3},{3,1},{1,0},{8,10},{10,12},{12... | collective-permute-start | bytes 393224 | tf_op jit(solution)/shard_map/ppermute | solution.py:42
  20.6 7.1 %collective-permute-start.6 = (bf16[64,1024]{1,0:T(8,128)(2,1)S(1)}, bf16[64,1024]{1,0:T(8,128)(2,1)S(1)}, u32[]{:S(2)}, u32[]{:S(2)}) collective-permute-start(bf16[64,1024]{1,0:T(8,128)(2,1)S(1)} %get-tuple-element.83.refs_4_), channel_id=1, source_target_pairs={{0,1},{2,0},{4,2},{6,4},{7,6},{5,7},{3,5},{1,3},{8,9},{10,8},{12,1... | collective-permute-start | bytes 393224 | tf_op jit(solution)/shard_map/ppermute | solution.py:42
  24.9 6.2 %collective-permute-start.18 = (bf16[64,1024]{1,0:T(8,128)(2,1)S(1)}, bf16[64,1024]{1,0:T(8,128)(2,1)S(1)}, u32[]{:S(2)}, u32[]{:S(2)}) collective-permute-start(bf16[64,1024]{1,0:T(8,128)(2,1)S(1)} %collective-permute-done.17.refs_12_), channel_id=1, source_target_pairs={{0,1},{2,0},{4,2},{6,4},{7,6},{5,7},{3,5},{1,3},{8,9},{10,8},{12,1... | collective-permute-start | bytes 393224 | tf_op jit(solution)/shard_map/ppermute | solution.py:42
  25.3 6.1 %collective-permute-start.8 = (bf16[64,1024]{1,0:T(8,128)(2,1)S(1)}, bf16[64,1024]{1,0:T(8,128)(2,1)S(1)}, u32[]{:S(2)}, u32[]{:S(2)}) collective-permute-start(bf16[64,1024]{1,0:T(8,128)(2,1)S(1)} %collective-permute-done.5.refs_3_), channel_id=1, source_target_pairs={{0,2},{2,4},{4,6},{6,7},{7,5},{5,3},{3,1},{1,0},{8,10},{10,12},{12... | collective-permute-start | bytes 393224 | tf_op jit(solution)/shard_map/ppermute | solution.py:42
  27.7 6.1 %collective-permute-start.7 = (f32[2,128]{1,0:T(2,128)S(1)}, f32[2,128]{1,0:T(2,128)S(1)}, u32[]{:S(2)}, u32[]{:S(2)}) collective-permute-start(f32[2,128]{1,0:T(2,128)S(1)} %pad_maximum_fusion.8), channel_id=1, source_target_pairs={{0,16},{8,24},{16,0},{24,8},{1,17},{9,25},{17,1},{25,9},{2,18},{10... | collective-permute-start | bytes 3080 | tf_op jit(solution)/shard_map/ppermute | solution.py:116
  29.2 5.3 %collective-permute-start.15 = (bf16[64,1024]{1,0:T(8,128)(2,1)S(1)}, bf16[64,1024]{1,0:T(8,128)(2,1)S(1)}, u32[]{:S(2)}, u32[]{:S(2)}) collective-permute-start(bf16[64,1024]{1,0:T(8,128)(2,1)S(1)} %collective-permute-done.14.refs_10_), channel_id=1, source_target_pairs={{0,2},{2,4},{4,6},{6,7},{7,5},{5,3},{3,1},{1,0},{8,10},{10,12},{12... | collective-permute-start | bytes 393224 | tf_op jit(solution)/shard_map/ppermute | solution.py:42
  31.5 5.1 %collective-permute-start.11 = (bf16[64,1024]{1,0:T(8,128)(2,1)S(1)}, bf16[64,1024]{1,0:T(8,128)(2,1)S(1)}, u32[]{:S(2)}, u32[]{:S(2)}) collective-permute-start(bf16[64,1024]{1,0:T(8,128)(2,1)S(1)} %collective-permute-done.8.refs_2_), channel_id=1, source_target_pairs={{0,2},{2,4},{4,6},{6,7},{7,5},{5,3},{3,1},{1,0},{8,10},{10,12},{12... | collective-permute-start | bytes 393224 | tf_op jit(solution)/shard_map/ppermute | solution.py:42
  34.1 6.8 %collective-permute-start.13 = (bf16[64,1024]{1,0:T(8,128)(2,1)S(1)}, bf16[64,1024]{1,0:T(8,128)(2,1)S(1)}, u32[]{:S(2)}, u32[]{:S(2)}) collective-permute-start(bf16[64,1024]{1,0:T(8,128)(2,1)S(1)} %collective-permute-done.9.refs_6_), channel_id=1, source_target_pairs={{0,1},{2,0},{4,2},{6,4},{7,6},{5,7},{3,5},{1,3},{8,9},{10,8},{12,1... | collective-permute-start | bytes 393224 | tf_op jit(solution)/shard_map/ppermute | solution.py:42
  34.5 6.4 %collective-permute-start.16 = (bf16[64,1024]{1,0:T(8,128)(2,1)S(1)}, bf16[64,1024]{1,0:T(8,128)(2,1)S(1)}, u32[]{:S(2)}, u32[]{:S(2)}) collective-permute-start(bf16[64,1024]{1,0:T(8,128)(2,1)S(1)} %collective-permute-done.15.refs_9_), channel_id=1, source_target_pairs={{0,2},{2,4},{4,6},{6,7},{7,5},{5,3},{3,1},{1,0},{8,10},{10,12},{12... | collective-permute-start | bytes 393224 | tf_op jit(solution)/shard_map/ppermute | solution.py:42
  36.1 6.7 %collective-permute-start.20 = (bf16[64,1024]{1,0:T(8,128)(2,1)S(1)}, bf16[64,1024]{1,0:T(8,128)(2,1)S(1)}, u32[]{:S(2)}, u32[]{:S(2)}) collective-permute-start(bf16[64,1024]{1,0:T(8,128)(2,1)S(1)} %collective-permute-done.19.refs_14_), channel_id=1, source_target_pairs={{0,1},{2,0},{4,2},{6,4},{7,6},{5,7},{3,5},{1,3},{8,9},{10,8},{12,1... | collective-permute-start | bytes 393224 | tf_op jit(solution)/shard_map/ppermute | solution.py:42
  36.6 6.2 %collective-permute-start.12 = (bf16[64,1024]{1,0:T(8,128)(2,1)S(1)}, bf16[64,1024]{1,0:T(8,128)(2,1)S(1)}, u32[]{:S(2)}, u32[]{:S(2)}) collective-permute-start(bf16[64,1024]{1,0:T(8,128)(2,1)S(1)} %collective-permute-done.11.refs_1_), channel_id=1, source_target_pairs={{0,2},{2,4},{4,6},{6,7},{7,5},{5,3},{3,1},{1,0},{8,10},{10,12},{12... | collective-permute-start | bytes 393224 | tf_op jit(solution)/shard_map/ppermute | solution.py:42
  54.3 14.2 %collective-permute-start.22 = (s16[128,2048]{1,0:T(8,128)(2,1)S(1)}, s16[128,2048]{1,0:T(8,128)(2,1)S(1)}, u32[]{:S(2)}, u32[]{:S(2)}) collective-permute-start(s16[128,2048]{1,0:T(8,128)(2,1)S(1)} %round-nearest-even_convert_fusion), channel_id=1, source_target_pairs={{0,16},{8,24},{16,0},{24,8},{1,17},{9,25},{17,1},{25,9},{2,18},{10... | collective-permute-start | bytes 1572872 | tf_op jit(solution)/shard_map/ppermute | solution.py:116
  55.7 12.8 %collective-permute-start.23 = (f32[128]{0:T(128)S(1)}, f32[128]{0:T(128)S(1)}, u32[]{:S(2)}, u32[]{:S(2)}) collective-permute-start(f32[128]{0:T(128)S(1)} %get-tuple-element.112), channel_id=1, source_target_pairs={{0,16},{8,24},{16,0},{24,8},{1,17},{9,25},{17,1},{25,9},{2,18},{10... | collective-permute-start | bytes 1544 | tf_op jit(solution)/shard_map/ppermute | solution.py:116
  72.9 5.9 %collective-permute-start.27 = (f32[2,256]{1,0:T(2,128)S(1)}, f32[2,256]{1,0:T(2,128)S(1)}, u32[]{:S(2)}, u32[]{:S(2)}) collective-permute-start(f32[2,256]{1,0:T(2,128)S(1)} %pad_maximum_fusion.7), channel_id=1, source_target_pairs={{0,6},{1,7},{2,4},{3,5},{4,2},{5,3},{6,0},{7,1},{8,14},{9,15},{10,... | collective-permute-start | bytes 6152 | tf_op jit(solution)/shard_map/ppermute | solution.py:47
  83.4 11.4 %collective-permute-start.28 = (bf16[128,2176]{1,0:T(8,128)(2,1)S(1)}, bf16[128,2176]{1,0:T(8,128)(2,1)S(1)}, u32[]{:S(2)}, u32[]{:S(2)}) collective-permute-start(bf16[128,2176]{1,0:T(8,128)(2,1)S(1)} %get-tuple-element.81), channel_id=1, source_target_pairs={{0,16},{8,24},{16,0},{24,8},{1,17},{9,25},{17,1},{25,9},{2,18},{10... | collective-permute-start | bytes 1671176 | tf_op jit(solution)/shard_map/ppermute | solution.py:116
  104.0 29.6 %collective-permute-start.30 = (bf16[2,64,3072]{2,1,0:T(8,128)(2,1)S(1)}, bf16[2,64,3072]{2,1,0:T(8,128)(2,1)S(1)}, u32[]{:S(2)}, u32[]{:S(2)}) collective-permute-start(bf16[2,64,3072]{2,1,0:T(8,128)(2,1)S(1)} %bitcast.54), channel_id=1, source_target_pairs={{0,16},{8,24},{16,0},{24,8},{1,17},{9,25},{17,1},{25,9},{2,18},{10... | collective-permute-start | bytes 2359304 | tf_op jit(solution)/shard_map/ppermute | solution.py:116
  105.1 5.8 %collective-permute-start.32 = (bf16[32,2176]{1,0:T(8,128)(2,1)S(1)}, bf16[32,2176]{1,0:T(8,128)(2,1)S(1)}, u32[]{:S(2)}, u32[]{:S(2)}) collective-permute-start(bf16[32,2176]{1,0:T(8,128)(2,1)S(1)} %get-tuple-element.78), channel_id=1, source_target_pairs={{0,2},{2,4},{4,6},{6,7},{7,5},{5,3},{3,1},{1,0},{8,10},{10,12},{12... | collective-permute-start | bytes 417800 | tf_op jit(solution)/shard_map/ppermute | solution.py:42
  105.2 7.9 %collective-permute-start.46 = (bf16[32,2176]{1,0:T(8,128)(2,1)S(1)}, bf16[32,2176]{1,0:T(8,128)(2,1)S(1)}, u32[]{:S(2)}, u32[]{:S(2)}) collective-permute-start(bf16[32,2176]{1,0:T(8,128)(2,1)S(1)} %get-tuple-element.77), channel_id=1, source_target_pairs={{0,1},{2,0},{4,2},{6,4},{7,6},{5,7},{3,5},{1,3},{8,9},{10,8},{12,1... | collective-permute-start | bytes 417800 | tf_op jit(solution)/shard_map/ppermute | solution.py:42
  111.0 5.5 %collective-permute-start.33 = (bf16[32,2176]{1,0:T(8,128)(2,1)S(1)}, bf16[32,2176]{1,0:T(8,128)(2,1)S(1)}, u32[]{:S(2)}, u32[]{:S(2)}) collective-permute-start(bf16[32,2176]{1,0:T(8,128)(2,1)S(1)} %add_convert_fusion.9), channel_id=1, source_target_pairs={{0,2},{2,4},{4,6},{6,7},{7,5},{5,3},{3,1},{1,0},{8,10},{10,12},{12... | collective-permute-start | bytes 417800 | tf_op jit(solution)/shard_map/ppermute | solution.py:42
  111.4 6.6 %collective-permute-start.34 = (bf16[32,2176]{1,0:T(8,128)(2,1)S(1)}, bf16[32,2176]{1,0:T(8,128)(2,1)S(1)}, u32[]{:S(2)}, u32[]{:S(2)}) collective-permute-start(bf16[32,2176]{1,0:T(8,128)(2,1)S(1)} %get-tuple-element.44), channel_id=1, source_target_pairs={{0,1},{2,0},{4,2},{6,4},{7,6},{5,7},{3,5},{1,3},{8,9},{10,8},{12,1... | collective-permute-start | bytes 417800 | tf_op jit(solution)/shard_map/ppermute | solution.py:42
  113.1 7.8 %collective-permute-start.48 = (bf16[32,2176]{1,0:T(8,128)(2,1)S(1)}, bf16[32,2176]{1,0:T(8,128)(2,1)S(1)}, u32[]{:S(2)}, u32[]{:S(2)}) collective-permute-start(bf16[32,2176]{1,0:T(8,128)(2,1)S(1)} %add_convert_fusion.3), channel_id=1, source_target_pairs={{0,1},{2,0},{4,2},{6,4},{7,6},{5,7},{3,5},{1,3},{8,9},{10,8},{12,1... | collective-permute-start | bytes 417800 | tf_op jit(solution)/shard_map/ppermute | solution.py:42
  114.5 6.4 %collective-permute-start.47 = (bf16[32,2176]{1,0:T(8,128)(2,1)S(1)}, bf16[32,2176]{1,0:T(8,128)(2,1)S(1)}, u32[]{:S(2)}, u32[]{:S(2)}) collective-permute-start(bf16[32,2176]{1,0:T(8,128)(2,1)S(1)} %get-tuple-element.51), channel_id=1, source_target_pairs={{0,2},{2,4},{4,6},{6,7},{7,5},{5,3},{3,1},{1,0},{8,10},{10,12},{12... | collective-permute-start | bytes 417800 | tf_op jit(solution)/shard_map/ppermute | solution.py:42
  118.0 5.8 %collective-permute-start.36 = (bf16[32,2176]{1,0:T(8,128)(2,1)S(1)}, bf16[32,2176]{1,0:T(8,128)(2,1)S(1)}, u32[]{:S(2)}, u32[]{:S(2)}) collective-permute-start(bf16[32,2176]{1,0:T(8,128)(2,1)S(1)} %get-tuple-element.46), channel_id=1, source_target_pairs={{0,1},{2,0},{4,2},{6,4},{7,6},{5,7},{3,5},{1,3},{8,9},{10,8},{12,1... | collective-permute-start | bytes 417800 | tf_op jit(solution)/shard_map/ppermute | solution.py:42
  119.5 5.3 %collective-permute-start.35 = (bf16[32,2176]{1,0:T(8,128)(2,1)S(1)}, bf16[32,2176]{1,0:T(8,128)(2,1)S(1)}, u32[]{:S(2)}, u32[]{:S(2)}) collective-permute-start(bf16[32,2176]{1,0:T(8,128)(2,1)S(1)} %get-tuple-element.45), channel_id=1, source_target_pairs={{0,2},{2,4},{4,6},{6,7},{7,5},{5,3},{3,1},{1,0},{8,10},{10,12},{12... | collective-permute-start | bytes 417800 | tf_op jit(solution)/shard_map/ppermute | solution.py:42
  121.0 6.5 %collective-permute-start.50 = (bf16[32,2176]{1,0:T(8,128)(2,1)S(1)}, bf16[32,2176]{1,0:T(8,128)(2,1)S(1)}, u32[]{:S(2)}, u32[]{:S(2)}) collective-permute-start(bf16[32,2176]{1,0:T(8,128)(2,1)S(1)} %get-tuple-element.54), channel_id=1, source_target_pairs={{0,1},{2,0},{4,2},{6,4},{7,6},{5,7},{3,5},{1,3},{8,9},{10,8},{12,1... | collective-permute-start | bytes 417800 | tf_op jit(solution)/shard_map/ppermute | solution.py:42
  122.5 6.0 %collective-permute-start.49 = (bf16[32,2176]{1,0:T(8,128)(2,1)S(1)}, bf16[32,2176]{1,0:T(8,128)(2,1)S(1)}, u32[]{:S(2)}, u32[]{:S(2)}) collective-permute-start(bf16[32,2176]{1,0:T(8,128)(2,1)S(1)} %get-tuple-element.53), channel_id=1, source_target_pairs={{0,2},{2,4},{4,6},{6,7},{7,5},{5,3},{3,1},{1,0},{8,10},{10,12},{12... | collective-permute-start | bytes 417800 | tf_op jit(solution)/shard_map/ppermute | solution.py:42
  124.8 5.9 %collective-permute-start.38 = (bf16[32,2176]{1,0:T(8,128)(2,1)S(1)}, bf16[32,2176]{1,0:T(8,128)(2,1)S(1)}, u32[]{:S(2)}, u32[]{:S(2)}) collective-permute-start(bf16[32,2176]{1,0:T(8,128)(2,1)S(1)} %get-tuple-element.48), channel_id=1, source_target_pairs={{0,1},{2,0},{4,2},{6,4},{7,6},{5,7},{3,5},{1,3},{8,9},{10,8},{12,1... | collective-permute-start | bytes 417800 | tf_op jit(solution)/shard_map/ppermute | solution.py:42
  126.0 6.5 %collective-permute-start.37 = (bf16[32,2176]{1,0:T(8,128)(2,1)S(1)}, bf16[32,2176]{1,0:T(8,128)(2,1)S(1)}, u32[]{:S(2)}, u32[]{:S(2)}) collective-permute-start(bf16[32,2176]{1,0:T(8,128)(2,1)S(1)} %get-tuple-element.47), channel_id=1, source_target_pairs={{0,2},{2,4},{4,6},{6,7},{7,5},{5,3},{3,1},{1,0},{8,10},{10,12},{12... | collective-permute-start | bytes 417800 | tf_op jit(solution)/shard_map/ppermute | solution.py:42
  128.6 5.2 %collective-permute-start.52 = (bf16[32,2176]{1,0:T(8,128)(2,1)S(1)}, bf16[32,2176]{1,0:T(8,128)(2,1)S(1)}, u32[]{:S(2)}, u32[]{:S(2)}) collective-permute-start(bf16[32,2176]{1,0:T(8,128)(2,1)S(1)} %get-tuple-element.56), channel_id=1, source_target_pairs={{0,1},{2,0},{4,2},{6,4},{7,6},{5,7},{3,5},{1,3},{8,9},{10,8},{12,1... | collective-permute-start | bytes 417800 | tf_op jit(solution)/shard_map/ppermute | solution.py:42
  129.9 5.1 %collective-permute-start.51 = (bf16[32,2176]{1,0:T(8,128)(2,1)S(1)}, bf16[32,2176]{1,0:T(8,128)(2,1)S(1)}, u32[]{:S(2)}, u32[]{:S(2)}) collective-permute-start(bf16[32,2176]{1,0:T(8,128)(2,1)S(1)} %get-tuple-element.55), channel_id=1, source_target_pairs={{0,2},{2,4},{4,6},{6,7},{7,5},{5,3},{3,1},{1,0},{8,10},{10,12},{12... | collective-permute-start | bytes 417800 | tf_op jit(solution)/shard_map/ppermute | solution.py:42
  132.7 5.5 %collective-permute-start.39 = (bf16[32,2048]{1,0:T(8,128)(2,1)S(1)}, bf16[32,2048]{1,0:T(8,128)(2,1)S(1)}, u32[]{:S(2)}, u32[]{:S(2)}) collective-permute-start(bf16[32,2048]{1,0:T(8,128)(2,1)S(1)} %fusion.6.refs_4_), channel_id=1, source_target_pairs={{0,2},{2,4},{4,6},{6,7},{7,5},{5,3},{3,1},{1,0},{8,10},{10,12},{12... | collective-permute-start | bytes 393224 | tf_op jit(solution)/shard_map/ppermute | solution.py:42
  133.7 21.5 %collective-permute-start.31 = (bf16[2,2,64,3072]{3,2,0,1:T(8,128)(2,1)S(1)}, bf16[2,2,64,3072]{3,2,0,1:T(8,128)(2,1)S(1)}, u32[]{:S(2)}, u32[]{:S(2)}) collective-permute-start(bf16[2,2,64,3072]{3,2,0,1:T(8,128)(2,1)S(1)} %pad_maximum_fusion.1), channel_id=1, source_target_pairs={{0,8},{8,0},{16,24},{24,16},{1,9},{9,1},{17,25},{25,17},{2,10},{10... | collective-permute-start | bytes 4718600 | tf_op jit(solution)/shard_map/ppermute | solution.py:112
  135.3 6.5 %collective-permute-start.56 = (bf16[32,2048]{1,0:T(8,128)(2,1)S(1)}, bf16[32,2048]{1,0:T(8,128)(2,1)S(1)}, u32[]{:S(2)}, u32[]{:S(2)}) collective-permute-start(bf16[32,2048]{1,0:T(8,128)(2,1)S(1)} %fusion.4.refs_11_), channel_id=1, source_target_pairs={{0,1},{2,0},{4,2},{6,4},{7,6},{5,7},{3,5},{1,3},{8,9},{10,8},{12,1... | collective-permute-start | bytes 393224 | tf_op jit(solution)/shard_map/ppermute | solution.py:42
  136.2 8.4 %collective-permute-start.43 = (bf16[32,2048]{1,0:T(8,128)(2,1)S(1)}, bf16[32,2048]{1,0:T(8,128)(2,1)S(1)}, u32[]{:S(2)}, u32[]{:S(2)}) collective-permute-start(bf16[32,2048]{1,0:T(8,128)(2,1)S(1)} %fusion.6.refs_4_), channel_id=1, source_target_pairs={{0,1},{2,0},{4,2},{6,4},{7,6},{5,7},{3,5},{1,3},{8,9},{10,8},{12,1... | collective-permute-start | bytes 393224 | tf_op jit(solution)/shard_map/ppermute | solution.py:42
  137.6 7.8 %collective-permute-start.53 = (bf16[32,2048]{1,0:T(8,128)(2,1)S(1)}, bf16[32,2048]{1,0:T(8,128)(2,1)S(1)}, u32[]{:S(2)}, u32[]{:S(2)}) collective-permute-start(bf16[32,2048]{1,0:T(8,128)(2,1)S(1)} %fusion.4.refs_11_), channel_id=1, source_target_pairs={{0,2},{2,4},{4,6},{6,7},{7,5},{5,3},{3,1},{1,0},{8,10},{10,12},{12... | collective-permute-start | bytes 393224 | tf_op jit(solution)/shard_map/ppermute | solution.py:42
  138.2 8.4 %collective-permute-start.40 = (bf16[32,2048]{1,0:T(8,128)(2,1)S(1)}, bf16[32,2048]{1,0:T(8,128)(2,1)S(1)}, u32[]{:S(2)}, u32[]{:S(2)}) collective-permute-start(bf16[32,2048]{1,0:T(8,128)(2,1)S(1)} %collective-permute-done.39.refs_3_), channel_id=1, source_target_pairs={{0,2},{2,4},{4,6},{6,7},{7,5},{5,3},{3,1},{1,0},{8,10},{10,12},{12... | collective-permute-start | bytes 393224 | tf_op jit(solution)/shard_map/ppermute | solution.py:42
  141.7 5.7 %collective-permute-start.57 = (bf16[32,2048]{1,0:T(8,128)(2,1)S(1)}, bf16[32,2048]{1,0:T(8,128)(2,1)S(1)}, u32[]{:S(2)}, u32[]{:S(2)}) collective-permute-start(bf16[32,2048]{1,0:T(8,128)(2,1)S(1)} %collective-permute-done.56.refs_12_), channel_id=1, source_target_pairs={{0,1},{2,0},{4,2},{6,4},{7,6},{5,7},{3,5},{1,3},{8,9},{10,8},{12,1... | collective-permute-start | bytes 393224 | tf_op jit(solution)/shard_map/ppermute | solution.py:42
  144.5 6.4 %collective-permute-start.44 = (bf16[32,2048]{1,0:T(8,128)(2,1)S(1)}, bf16[32,2048]{1,0:T(8,128)(2,1)S(1)}, u32[]{:S(2)}, u32[]{:S(2)}) collective-permute-start(bf16[32,2048]{1,0:T(8,128)(2,1)S(1)} %collective-permute-done.43.refs_5_), channel_id=1, source_target_pairs={{0,1},{2,0},{4,2},{6,4},{7,6},{5,7},{3,5},{1,3},{8,9},{10,8},{12,1... | collective-permute-start | bytes 393224 | tf_op jit(solution)/shard_map/ppermute | solution.py:42
  145.4 6.4 %collective-permute-start.54 = (bf16[32,2048]{1,0:T(8,128)(2,1)S(1)}, bf16[32,2048]{1,0:T(8,128)(2,1)S(1)}, u32[]{:S(2)}, u32[]{:S(2)}) collective-permute-start(bf16[32,2048]{1,0:T(8,128)(2,1)S(1)} %collective-permute-done.53.refs_10_), channel_id=1, source_target_pairs={{0,2},{2,4},{4,6},{6,7},{7,5},{5,3},{3,1},{1,0},{8,10},{10,12},{12... | collective-permute-start | bytes 393224 | tf_op jit(solution)/shard_map/ppermute | solution.py:42
  146.6 6.4 %collective-permute-start.41 = (bf16[32,2048]{1,0:T(8,128)(2,1)S(1)}, bf16[32,2048]{1,0:T(8,128)(2,1)S(1)}, u32[]{:S(2)}, u32[]{:S(2)}) collective-permute-start(bf16[32,2048]{1,0:T(8,128)(2,1)S(1)} %collective-permute-done.40.refs_2_), channel_id=1, source_target_pairs={{0,2},{2,4},{4,6},{6,7},{7,5},{5,3},{3,1},{1,0},{8,10},{10,12},{12... | collective-permute-start | bytes 393224 | tf_op jit(solution)/shard_map/ppermute | solution.py:42
  147.4 7.4 %collective-permute-start.58 = (bf16[32,2048]{1,0:T(8,128)(2,1)S(1)}, bf16[32,2048]{1,0:T(8,128)(2,1)S(1)}, u32[]{:S(2)}, u32[]{:S(2)}) collective-permute-start(bf16[32,2048]{1,0:T(8,128)(2,1)S(1)} %collective-permute-done.57.refs_13_), channel_id=1, source_target_pairs={{0,1},{2,0},{4,2},{6,4},{7,6},{5,7},{3,5},{1,3},{8,9},{10,8},{12,1... | collective-permute-start | bytes 393224 | tf_op jit(solution)/shard_map/ppermute | solution.py:42
  153.0 5.1 %collective-permute-start.42 = (bf16[32,2048]{1,0:T(8,128)(2,1)S(1)}, bf16[32,2048]{1,0:T(8,128)(2,1)S(1)}, u32[]{:S(2)}, u32[]{:S(2)}) collective-permute-start(bf16[32,2048]{1,0:T(8,128)(2,1)S(1)} %collective-permute-done.41.refs_1_), channel_id=1, source_target_pairs={{0,2},{2,4},{4,6},{6,7},{7,5},{5,3},{3,1},{1,0},{8,10},{10,12},{12... | collective-permute-start | bytes 393224 | tf_op jit(solution)/shard_map/ppermute | solution.py:42
  (17 other events, 101.2 us)
